TPU v7x, 32 devices: a whole 2x2x4 slice. The times are simulated.
32 devices in a mesh: section: 8 (over z, x), tensor: 4 (over y, core).
Axes of the slice: x: 2, y: 2, z: 4, core: 2. Of those that a mesh axis runs over, the one named last changes fastest.
Arguments:
- section_input: bfloat16 [8, 128, 3072], P('section', 'tensor'), may hold values from -6 to 6
- query: bfloat16 [8, 3072, 128], P('section', 'tensor'), may hold values from -100 to 100
- key_stash: bfloat16 [8, 3072, 128], P('section', 'tensor'), may hold values from -4 to 4
- incoming: bfloat16 [8, 128, 3072], P('section', 'tensor'), may hold values from -6 to 6
- version: int32 [8], P('section'), may hold values from 0 to 1
- w_value: bfloat16 [8, 2, 3072, 1536], P('section', None, 'tensor'), may hold values from -0.109375 to 0.109375
- w_out: bfloat16 [8, 2, 3072, 1536], P('section', None, 'tensor'), may hold values from -0.109375 to 0.109375
Outputs:
- input_grad: bfloat16 [8, 128, 3072], P('section', 'tensor')
- grad_value: bfloat16 [8, 3072, 1536], P('section', 'tensor')
- grad_out: bfloat16 [8, 3072, 1536], P('section', 'tensor')
All inputs are finite; a program needn't handle non-finite values.
Results may differ from a plain program's by a relative error of at most 0.018.
Values may be sent and summed in bfloat16 or wider, within the bound.
No kernel may reach another device: no remote copies, remote signals or barrier semaphores. Data moves between devices by JAX's collectives and lax.ppermute only.
A program may use at most 128 MiB of HBM per device.

v0:
```python
import math

import jax
import jax.numpy as jnp
from jax import lax
from jax.sharding import PartitionSpec as P

HEAD_DIM = 96


def from_partner(array, axis, bit):
    return lax.ppermute(array, axis, [(i, i ^ 1 << bit) for i in range(lax.axis_size(axis))])


def shifted(value, axis, steps):
    count = lax.axis_size(axis)
    leading, last = (max(0, -steps), min(count, count - steps))
    return lax.ppermute(value, axis, [(source, source + steps) for source in range(leading, last)])


def contract_rows(left_side, right_side):
    return lax.dot_general(
        left_side, right_side, (((0,), (0,)), ((), ())), preferred_element_type=jnp.float32
    )


def on_device(section_input, query, key_stash, incoming, version, w_value, w_out):
    position = lax.axis_index("section")
    parity = position % 2
    section_parity = position // 2 % 2
    chosen = version[0]
    stacked = jnp.stack([w_value[0], w_out[0]])
    own_halves = lax.dynamic_index_in_dim(stacked, chosen, 1, keepdims=False)
    partner = from_partner(stacked, "section", 0)
    theirs = lax.dynamic_index_in_dim(partner, chosen, 1, keepdims=False)
    left_part = jnp.where(parity == 0, own_halves, theirs)
    right_part = jnp.where(parity == 0, theirs, own_halves)
    weights = jnp.concatenate([left_part, right_part], axis=2)
    value_weight = weights[0]
    out_weight = weights[1]
    local_rows = value_weight.shape[0]
    width = value_weight.shape[1]
    tokens = query.shape[2]
    local_heads = local_rows // HEAD_DIM
    shard_rows = section_input.shape[1]
    full_input = lax.all_gather(section_input[0], "tensor", axis=0, tiled=True)
    values = lax.dot_general(
        value_weight, full_input, (((1,), (1,)), ((), ())), preferred_element_type=jnp.float32
    ).astype(jnp.bfloat16)
    query_heads = query[0].reshape(local_heads, HEAD_DIM, tokens)
    key_heads = key_stash[0].reshape(local_heads, HEAD_DIM, tokens)
    scores = jnp.einsum(
        "hdi,hdj->hij", query_heads, key_heads, preferred_element_type=jnp.float32
    ) * (1.0 / math.sqrt(HEAD_DIM))
    causal = lax.broadcasted_iota(jnp.int32, (tokens, tokens), 1) <= lax.broadcasted_iota(
        jnp.int32, (tokens, tokens), 0
    )
    scores = jnp.where(causal, scores, -jnp.inf)
    row_max = jnp.max(scores, axis=2, keepdims=True)
    expo = jnp.exp(scores - row_max)
    attend = (expo / jnp.sum(expo, axis=2, keepdims=True)).astype(jnp.bfloat16)
    value_heads = values.reshape(local_heads, HEAD_DIM, tokens)
    context = (
        jnp.einsum("hdj,hij->hdi", value_heads, attend, preferred_element_type=jnp.float32)
        .astype(jnp.bfloat16)
        .reshape(local_rows, tokens)
    )
    value_wgrad = jnp.zeros((local_rows, width), jnp.float32)
    out_wgrad = jnp.zeros((local_rows, width), jnp.float32)
    received = incoming[0]
    first_dx = incoming[0]
    input_grad = incoming[0]
    for section_round in range(2):
        if section_round == 0:
            grad_shard = incoming[0]
            active = section_parity == 1
        else:
            grad_shard = received
            active = section_parity == 0
        full_grad = lax.all_gather(grad_shard, "tensor", axis=0, tiled=True)

        def backward_terms(upstream_full):
            context_grad = lax.dot_general(
                out_weight,
                upstream_full,
                (((1,), (1,)), ((), ())),
                preferred_element_type=jnp.float32,
            ).astype(jnp.bfloat16)
            context_heads = context_grad.reshape(local_heads, HEAD_DIM, tokens)
            value_grad = (
                jnp.einsum(
                    "hdi,hij->hdj", context_heads, attend, preferred_element_type=jnp.float32
                )
                .astype(jnp.bfloat16)
                .reshape(local_rows, tokens)
            )
            value_term = jnp.dot(value_grad, full_input, preferred_element_type=jnp.float32)
            out_term = jnp.dot(context, upstream_full, preferred_element_type=jnp.float32)
            return (value_grad, value_term, out_term)

        def skipped(upstream_full):
            return (
                jnp.zeros((local_rows, tokens), jnp.bfloat16),
                jnp.zeros((local_rows, width), jnp.float32),
                jnp.zeros((local_rows, width), jnp.float32),
            )

        value_grad, value_term, out_term = lax.cond(active, backward_terms, skipped, full_grad)
        value_wgrad = value_wgrad + value_term
        out_wgrad = out_wgrad + out_term
        mine_rows = lax.psum_scatter(
            lax.cond(
                active,
                lambda piece_now: contract_rows(piece_now, value_weight),
                lambda piece_now: jnp.zeros(
                    (shard_rows * lax.axis_size("tensor"), width), jnp.float32
                ),
                value_grad,
            ).astype(jnp.bfloat16),
            "tensor",
            scatter_dimension=0,
            tiled=True,
        ).astype(jnp.float32)
        dx_shard = (grad_shard.astype(jnp.float32) + mine_rows).astype(jnp.bfloat16)
        if section_round == 0:
            first_dx = dx_shard
            received = shifted(dx_shard, "section", -2)
        else:
            input_grad = jnp.where(section_parity == 1, first_dx, dx_shard)
    half_width = width // 2
    both_grads = jnp.stack([value_wgrad, out_wgrad])
    kept_half = jnp.where(parity == 0, both_grads[:, :, :half_width], both_grads[:, :, half_width:])
    sent_half = jnp.where(parity == 0, both_grads[:, :, half_width:], both_grads[:, :, :half_width])
    arrived = from_partner(sent_half.astype(jnp.bfloat16), "section", 0).astype(sent_half.dtype)
    summed_grads = (kept_half + arrived).astype(jnp.bfloat16)
    return (input_grad[None], summed_grads[0][None], summed_grads[1][None])


def solution(mesh):
    placed = (
        P("section", "tensor", None),
        P("section", "tensor", None),
        P("section", "tensor", None),
        P("section", "tensor", None),
        P("section"),
        P("section", None, "tensor", None),
        P("section", None, "tensor", None),
    )
    return jax.shard_map(
        on_device,
        mesh=mesh,
        in_specs=placed,
        out_specs=(
            P("section", "tensor", None),
            P("section", "tensor", None),
            P("section", "tensor", None),
        ),
        check_vma=False,
    )
```

profile of v0, /device:TPU:0, one launch (start us, length us, event | category | flops | bytes accessed | tf_op | source)
XLA Modules:
  0.0 451.7 jit_solution(16354145977226301524)
XLA Ops:
  7.3 8.4 %pad_maximum_fusion = bf16[2,2,768,1536]{3,2,0,1:T(8,128)(2,1)} fusion(bf16[1,2,768,1536]{3,2,0,1:T(8,128)(2,1)} %bitcast.61, bf16[1,2,768,1536]{3,2,0,1:T(8,128)(2,1)} %bitcast.63), kind=kLoop, calls=%fused_computation.8 | loop fusion | flops 4718592 | bytes 18874368 | tf_op jit(solution)/shard_map/stack | solution.py:32
  15.6 2.9 collective-permute-start
  19.7 8.6 %all-gather.1 = bf16[1,128,3072]{2,1,0:T(8,128)(2,1)S(1)} all-gather(bf16[1,32,3072]{2,1,0:T(8,128)(2,1)S(1)} %copy-done.13), channel_id=3, replica_groups=mesh['section'=8,'tensor'=4] {'tensor'}, dimensions={1}, use_global_device_ids=true | all-gather | bytes 983040 | tf_op jit(solution)/shard_map/all_gather | solution.py:46
  28.4 8.7 %all-gather = bf16[1,128,3072]{2,1,0:T(8,128)(2,1)S(1)} all-gather(bf16[1,32,3072]{2,1,0:T(8,128)(2,1)S(1)} %copy-done.10), channel_id=2, replica_groups=mesh['section'=8,'tensor'=4] {'tensor'}, dimensions={1}, use_global_device_ids=true | all-gather | bytes 983040 | tf_op jit(solution)/shard_map/all_gather | solution.py:80
  37.1 184.8 %collective-permute-done = bf16[2,2,768,1536]{3,2,0,1:T(8,128)(2,1)} collective-permute-done((bf16[2,2,768,1536]{3,2,0,1:T(8,128)(2,1)}, bf16[2,2,768,1536]{3,2,0,1:T(8,128)(2,1)}, u32[]{:S(2)}, u32[]{:S(2)}) %collective-permute-start) | collective-permute-done | bytes 9437216 | tf_op jit(solution)/shard_map/ppermute | solution.py:12
  221.8 6.8 %select_bitcast_fusion = (bf16[2,768,1536]{2,1,0:T(8,128)(2,1)S(1)}, bf16[2,768,1536]{2,1,0:T(8,128)(2,1)S(1)}) fusion(pred[]{:T(512)S(6)} %eq.17, bf16[2,2,768,1536]{3,2,0,1:T(8,128)(2,1)} %collective-permute-done, s32[]{:T(128)S(6)} %select_n.67, bf16[1,2,768,1536]{3,2,0,1:T(8,128)(2,1)} %bitcast.62, bf16[1,2,768,1536]{3,2,0,1:T(8,128)(2,1)} %bitcast.64), kind=kLoop, calls=%fused_computation.23 | loop fusion | flops 9437184 | bytes 23592964 | tf_op jit(solution)/shard_map/jit(_where)/select_n | solution.py:37
  228.7 1.4 fusion.5
  230.1 1.4 convolution_convert_fusion.5
  232.2 1.4 copy-done.7
  233.6 10.4 %conditional.4 = (bf16[768,128]{1,0:T(8,128)(2,1)}, f32[768,3072]{1,0:T(8,128)}, f32[768,3072]{1,0:T(8,128)}) conditional(s32[]{:T(128)} %convert_element_type.63, () %tuple.37, (bf16[768,3072]{1,0:T(8,128)(2,1)S(1)}, bf16[128,3072]{1,0:T(8,128)(2,1)S(1)}, bf16[8,128,128]{1,2,0:T(8,128)(2,1)S(1)}, bf16[128,3072]{1,0:T(8,128)(2,1)S(1)}, ...), branch_computations={%region_2.3_spmd, %region_3.4_spmd} | conditional | flops 1837301760 | bytes 27197464 | solution.py:108
  234.3 4.9 %broadcast.21.clone = f32[768,3072]{1,0:T(8,128)} broadcast(f32[]{:T(128)} %constant.46.clone), dimensions={} | broadcast | bytes 9437188 | tf_op jit(solution)/shard_map/broadcast.2
  239.2 4.9 %broadcast.21 = f32[768,3072]{1,0:T(8,128)} broadcast(f32[]{:T(128)} %constant.46.clone), dimensions={} | broadcast | bytes 9437188 | tf_op jit(solution)/shard_map/broadcast.2
  245.1 31.1 %reduce-scatter.3.cloned.1.call-done = bf16[32,3072]{1,0:T(8,128)(2,1)} async-done(((bf16[128,3072]{1,0:T(8,128)(2,1)}), bf16[32,3072]{1,0:T(8,128)(2,1)}) %reduce-scatter.3.cloned.1.call-update) | async-done | bytes 196624 | tf_op jit(solution)/shard_map/reduce_scatter | solution.py:111
  278.4 7.2 %collective-permute-done.1 = bf16[32,3072]{1,0:T(8,128)(2,1)S(1)} collective-permute-done((bf16[32,3072]{1,0:T(8,128)(2,1)S(1)}, bf16[32,3072]{1,0:T(8,128)(2,1)S(1)}, u32[]{:S(2)}, u32[]{:S(2)}) %collective-permute-start.1) | collective-permute-done | bytes 196640 | tf_op jit(solution)/shard_map/ppermute | solution.py:18
  285.6 7.6 %all_gather.11 = bf16[128,3072]{1,0:T(8,128)(2,1)S(1)} all-gather(bf16[32,3072]{1,0:T(8,128)(2,1)S(1)} %collective-permute-done.1), channel_id=1, replica_groups=mesh['section'=8,'tensor'=4] {'tensor'}, dimensions={0}, use_global_device_ids=true | all-gather | bytes 983040 | tf_op jit(solution)/shard_map/all_gather | solution.py:80
  293.2 8.4 %conditional.6 = (bf16[768,128]{1,0:T(8,128)(2,1)}, f32[768,3072]{1,0:T(8,128)S(1)}, f32[768,3072]{1,0:T(8,128)S(1)}) conditional(s32[]{:T(128)} %convert_element_type.71, () %tuple.41, (bf16[768,3072]{1,0:T(8,128)(2,1)}, bf16[128,3072]{1,0:T(8,128)(2,1)S(1)}, bf16[8,128,128]{1,2,0:T(8,128)(2,1)S(1)}, bf16[128,3072]{1,0:T(8,128)(2,1)S(1)}, ...), branch_computations={%region_7.8_spmd, %region_8.9_spmd} | conditional | flops 1837301760 | bytes 27197464 | solution.py:108
  293.2 3.7 convolution_convert_fusion.3
  297.9 1.4 fusion.23
  299.3 2.3 fusion.22
  301.6 3.7 copy-done.5
  305.3 2.8 copy-done.6
  308.1 13.2 %add_bitcast_fusion = (f32[1,768,3072]{2,1,0:T(8,128)S(1)}, f32[1,768,3072]{2,1,0:T(8,128)S(1)}) fusion(f32[768,3072]{1,0:T(8,128)} %get-tuple-element.61, f32[768,3072]{1,0:T(8,128)} %copy-done.5, f32[768,3072]{1,0:T(8,128)} %get-tuple-element.59, f32[768,3072]{1,0:T(8,128)} %copy-done.6), kind=kLoop, calls=%fused_computation.16 | loop fusion | flops 4718592 | bytes 56623104 | tf_op jit(solution)/shard_map/stack | solution.py:131
  321.3 4.4 select_convert_fusion
  326.5 2.6 copy-done.3
  329.1 1.5 collective-permute-start.2
  330.7 3.3 conditional.7
  330.7 3.3 fusion.19
  334.8 22.5 %reduce-scatter.5.cloned.1.call-done = bf16[32,3072]{1,0:T(8,128)(2,1)} async-done(((bf16[128,3072]{1,0:T(8,128)(2,1)}), bf16[32,3072]{1,0:T(8,128)(2,1)}) %reduce-scatter.5.cloned.1.call-update) | async-done | bytes 196624 | tf_op jit(solution)/shard_map/reduce_scatter | solution.py:111
  357.3 1.7 fusion.11
  359.0 74.5 %collective-permute-done.2 = bf16[2,768,1536]{2,1,0:T(8,128)(2,1)} collective-permute-done((bf16[2,768,1536]{2,1,0:T(8,128)(2,1)}, bf16[2,768,1536]{2,1,0:T(8,128)(2,1)}, u32[]{:S(2)}, u32[]{:S(2)}) %collective-permute-start.2) | collective-permute-done | bytes 4718624 | tf_op jit(solution)/shard_map/ppermute | solution.py:12
  433.5 8.9 %add_convert_fusion = bf16[2,768,1536]{2,1,0:T(8,128)(2,1)S(1)} fusion(bf16[2,768,1536]{2,1,0:T(8,128)(2,1)} %collective-permute-done.2, pred[]{:T(512)S(6)} %eq.17, f32[1,768,3072]{2,1,0:T(8,128)} %copy-done.2, f32[1,768,3072]{2,1,0:T(8,128)} %copy-done.3), kind=kLoop, calls=%fused_computation.14 | loop fusion | flops 14155776 | bytes 28311552 | tf_op jit(solution)/shard_map/convert_element_type | solution.py:135
  442.4 2.5 fusion.16
  (40 shorter events, 8.0 us)
Async XLA Ops:
  7.2 12.1 %copy-start = (bf16[1,768,128]{2,1,0:T(8,128)(2,1)S(1)}, bf16[1,768,128]{2,1,0:T(8,128)(2,1)}, u32[]{:S(2)}) copy-start(bf16[1,768,128]{2,1,0:T(8,128)(2,1)} %param.16) | copy-start | bytes 589828
  7.2 269.0 %reduce-scatter.3.cloned.1.call-start = ((), (), s32[]{:S(2)}) async-start(), calls=%async_computation.2 | async-start | bytes 983040 | tf_op jit(solution)/shard_map/reduce_scatter | solution.py:111
  7.2 12.0 %copy-start.14 = (bf16[1,768,128]{2,1,0:T(8,128)(2,1)S(1)}, bf16[1,768,128]{2,1,0:T(8,128)(2,1)}, u32[]{:S(2)}) copy-start(bf16[1,768,128]{2,1,0:T(8,128)(2,1)} %param.17) | copy-start | bytes 589828
  7.2 12.5 %copy-start.13 = (bf16[1,32,3072]{2,1,0:T(8,128)(2,1)S(1)}, bf16[1,32,3072]{2,1,0:T(8,128)(2,1)}, u32[]{:S(2)}) copy-start(bf16[1,32,3072]{2,1,0:T(8,128)(2,1)} %param.15) | copy-start | bytes 589828
  7.2 21.1 %copy-start.10 = (bf16[1,32,3072]{2,1,0:T(8,128)(2,1)S(1)}, bf16[1,32,3072]{2,1,0:T(8,128)(2,1)}, u32[]{:S(2)}) copy-start(bf16[1,32,3072]{2,1,0:T(8,128)(2,1)} %param.18) | copy-start | bytes 589828
  15.6 206.2 %collective-permute-start = (bf16[2,2,768,1536]{3,2,0,1:T(8,128)(2,1)}, bf16[2,2,768,1536]{3,2,0,1:T(8,128)(2,1)}, u32[]{:S(2)}, u32[]{:S(2)}) collective-permute-start(bf16[2,2,768,1536]{3,2,0,1:T(8,128)(2,1)} %pad_maximum_fusion), channel_id=1, source_target_pairs={{0,4},{4,0},{8,12},{12,8},{16,20},{20,16},{24,28},{28,24},{1,5},{5... | collective-permute-start | bytes 28311560 | tf_op jit(solution)/shard_map/ppermute | solution.py:12
  230.0 2.1 copy-start.4
  230.1 3.5 copy-start.7
  244.1 0.9 copy-start.8
  245.0 112.3 %reduce-scatter.5.cloned.1.call-start = ((), (), s32[]{:S(2)}) async-start(), calls=%async_computation.3 | async-start | bytes 983040 | tf_op jit(solution)/shard_map/reduce_scatter | solution.py:111
  277.1 8.5 %collective-permute-start.1 = (bf16[32,3072]{1,0:T(8,128)(2,1)S(1)}, bf16[32,3072]{1,0:T(8,128)(2,1)S(1)}, u32[]{:S(2)}, u32[]{:S(2)}) collective-permute-start(bf16[32,3072]{1,0:T(8,128)(2,1)S(1)} %fusion.9), channel_id=1, source_target_pairs={{8,0},{12,4},{16,8},{20,12},{24,16},{28,20},{9,1},{13,5},{17,9},{2... | collective-permute-start | bytes 589832 | tf_op jit(solution)/shard_map/ppermute | solution.py:18
  285.6 7.6 %copy-start.11 = (bf16[32,3072]{1,0:T(8,128)(2,1)}, bf16[32,3072]{1,0:T(8,128)(2,1)S(1)}, u32[]{:S(2)}) copy-start(bf16[32,3072]{1,0:T(8,128)(2,1)S(1)} %collective-permute-done.1) | copy-start | bytes 589828
  301.6 3.7 copy-start.5
  301.6 6.4 %copy-start.6 = (f32[768,3072]{1,0:T(8,128)}, f32[768,3072]{1,0:T(8,128)S(1)}, u32[]{:S(2)}) copy-start(f32[768,3072]{1,0:T(8,128)S(1)} %get-tuple-element.60) | copy-start | bytes 28311556
  321.2 5.3 %copy-start.2 = (f32[1,768,3072]{2,1,0:T(8,128)}, f32[1,768,3072]{2,1,0:T(8,128)S(1)}, u32[]{:S(2)}) copy-start(f32[1,768,3072]{2,1,0:T(8,128)S(1)} %get-tuple-element.81) | copy-start | bytes 28311556
  321.3 7.9 %copy-start.3 = (f32[1,768,3072]{2,1,0:T(8,128)}, f32[1,768,3072]{2,1,0:T(8,128)S(1)}, u32[]{:S(2)}) copy-start(f32[1,768,3072]{2,1,0:T(8,128)S(1)} %get-tuple-element.82) | copy-start | bytes 28311556
  321.3 36.1 %copy-start.12 = (bf16[32,3072]{1,0:T(8,128)(2,1)S(1)}, bf16[32,3072]{1,0:T(8,128)(2,1)}, u32[]{:S(2)}) copy-start(bf16[32,3072]{1,0:T(8,128)(2,1)} %copy-done.11) | copy-start | bytes 589828
  329.1 104.4 %collective-permute-start.2 = (bf16[2,768,1536]{2,1,0:T(8,128)(2,1)}, bf16[2,768,1536]{2,1,0:T(8,128)(2,1)}, u32[]{:S(2)}, u32[]{:S(2)}) collective-permute-start(bf16[2,768,1536]{2,1,0:T(8,128)(2,1)} %select_convert_fusion), channel_id=1, source_target_pairs={{0,4},{4,0},{8,12},{12,8},{16,20},{20,16},{24,28},{28,24},{1,5},{5... | collective-permute-start | bytes 14155784 | tf_op jit(solution)/shard_map/ppermute | solution.py:12
  333.9 0.9 copy-start.9
  433.5 11.4 %copy-start.1 = (bf16[1,768,128]{2,1,0:T(8,128)(2,1)S(1)}, bf16[1,768,128]{2,1,0:T(8,128)(2,1)}, u32[]{:S(2)}) copy-start(bf16[1,768,128]{2,1,0:T(8,128)(2,1)} %param.16) | copy-start | bytes 589828
Sparse Core Ops, SparseCore 0:
  245.1 30.9 reduce-scatter.2
  335.0 22.3 reduce-scatter.4
where the time goes:
time: 452 us
  waiting for transfers between devices  320 us (71%)
  other arithmetic  45.8 us (10%)
  local copies, waits for them, and re-layouts  26.6 us (6%)
  blocking collectives  24.9 us (6%)
  between operations  14.9 us (3%)
  matrix products  13.6 us (3%)
  starting transfers between devices  5.86 us (1%)
    ppermute x2, waiting for transfers between devices, from_partner(): lax.ppermute(array, axis, [(i, i ^ 1 << bit) for i in range(lax.axis_size...  259 us
    reduce_scatter x2, waiting for transfers between devices, on_device(): lax.psum_scatter(lax.cond(active, lambda piece_now: contract_rows(piece_n...  53.6 us
    all_gather x2, blocking collectives, on_device(): full_grad = lax.all_gather(grad_shard, 'tensor', axis=0, tiled=True)  16.3 us
    unnamed x30, local copies, waits for them, and re-layouts  13.6 us
    another operation x1, other arithmetic, on_device(): both_grads = jnp.stack([value_wgrad, out_wgrad])  13.2 us
    another operation x4, local copies, waits for them, and re-layouts  10.5 us
  transfers between devices with their start and end apart: 5, of which 5 were waited for; matrix products, arithmetic and copies ran while one was open for 1% of the time, Pallas kernels for 0%

commit v1 on v0

v1 whole, which is shorter than its diff:
```python
import math

import jax
import jax.numpy as jnp
from jax import lax
from jax.sharding import Mesh, PartitionSpec as P

HEAD_DIM = 96


def swap_half(array):
    return lax.ppermute(array, "half", [(0, 1), (1, 0)])


def nt_dot(left_side, right_side):
    return lax.dot_general(
        left_side, right_side, (((1,), (1,)), ((), ())), preferred_element_type=jnp.float32
    )


def tn_dot(left_side, right_side):
    return lax.dot_general(
        left_side, right_side, (((0,), (0,)), ((), ())), preferred_element_type=jnp.float32
    )


def attention_probs(query, key_stash):
    tokens = query.shape[-1]
    query_heads = query.reshape(-1, HEAD_DIM, tokens)
    key_heads = key_stash.reshape(-1, HEAD_DIM, tokens)
    scores = jnp.einsum(
        "hdi,hdj->hij", query_heads, key_heads, preferred_element_type=jnp.float32
    ) * (1.0 / math.sqrt(HEAD_DIM))
    causal = lax.broadcasted_iota(jnp.int32, (tokens, tokens), 1) <= lax.broadcasted_iota(
        jnp.int32, (tokens, tokens), 0
    )
    scores = jnp.where(causal, scores, -jnp.inf)
    row_max = jnp.max(scores, axis=2, keepdims=True)
    expo = jnp.exp(scores - row_max)
    return (expo / jnp.sum(expo, axis=2, keepdims=True)).astype(jnp.bfloat16)


def on_device(section_input, query, key_stash, incoming, version, w_value, w_out):
    half = lax.axis_index("half")
    odd = lax.axis_index("pair") % 2 == 1
    n_pairs = lax.axis_size("pair")
    n_tensor = lax.axis_size("tensor")
    width = w_value.shape[3]
    rows = w_value.shape[2]
    shard = section_input.shape[1]
    tokens = query.shape[2]

    def own_columns(array):
        return lax.dynamic_slice_in_dim(array, half * width, width, 1)

    def other_columns(array):
        return lax.dynamic_slice_in_dim(array, (1 - half) * width, width, 1)

    first = jnp.where(odd, incoming[0], section_input[0])
    second_own = section_input[0]
    first_pair = jnp.stack([own_columns(first), swap_half(other_columns(first))])
    other_version = swap_half(version)
    stash = jnp.concatenate([query, key_stash])
    stash_other = swap_half(stash)
    input_pair = jnp.stack([own_columns(second_own), swap_half(other_columns(second_own))])

    def chosen(table, which):
        return lax.dynamic_index_in_dim(table[0], which[0], 0, keepdims=False)

    value_weights = [chosen(w_value, version), chosen(w_value, other_version)]
    out_weights = [chosen(w_out, version), chosen(w_out, other_version)]

    probs = attention_probs(
        jnp.concatenate([query[0], stash_other[0]]), jnp.concatenate([key_stash[0], stash_other[1]])
    )
    flipped = jnp.swapaxes(probs, 1, 2)
    mix_first = jnp.where(odd, probs, flipped)
    mix_second = jnp.where(odd, flipped, probs)

    def gathered(pair):
        return lax.all_gather(pair, "tensor", axis=1, tiled=True)

    def mixed(weights, full, mix):
        partial = jnp.stack([nt_dot(weights[0], full[0]), nt_dot(weights[1], full[1])])
        arrived = swap_half(partial.astype(jnp.bfloat16))
        total = (partial + arrived[::-1].astype(jnp.float32)).astype(jnp.bfloat16)
        heads = total.reshape(-1, HEAD_DIM, tokens)
        result = jnp.einsum("hdi,hij->hdj", heads, mix, preferred_element_type=jnp.float32)
        return result.astype(jnp.bfloat16).reshape(2, rows, tokens)

    def scattered(result):
        partial = jnp.stack(
            [tn_dot(result[0], value_weights[0]), tn_dot(result[1], value_weights[1])]
        ).astype(jnp.bfloat16)
        pieces = partial.reshape(2, n_tensor, shard, width)
        arrived = lax.all_to_all(pieces, "tensor", 1, 1, tiled=True)
        return jnp.sum(arrived.astype(jnp.float32), axis=1)

    first_full = gathered(first_pair)
    first_result = mixed(
        [jnp.where(odd, o, v) for v, o in zip(value_weights, out_weights)], first_full, mix_first
    )
    first_dx = (first_pair.astype(jnp.float32) + scattered(first_result)).astype(jnp.bfloat16)
    received = lax.ppermute(
        first_dx, "pair", [(source, source - 1) for source in range(1, n_pairs, 2)]
    )
    second_pair = jnp.where(odd, input_pair, received)
    second_full = gathered(second_pair)
    second_result = mixed(
        [jnp.where(odd, v, o) for v, o in zip(value_weights, out_weights)], second_full, mix_second
    )
    second_dx = (second_pair.astype(jnp.float32) + scattered(second_result)).astype(jnp.bfloat16)

    final_dx = jnp.where(odd, first_dx, second_dx)
    final_other = swap_half(final_dx[1])
    input_grad = jnp.where(
        half == 0,
        jnp.concatenate([final_dx[0], final_other], axis=1),
        jnp.concatenate([final_other, final_dx[0]], axis=1),
    )

    def pair_sum(left_pair, right_pair):
        return (
            jnp.dot(left_pair[0], right_pair[0], preferred_element_type=jnp.float32)
            + jnp.dot(left_pair[1], right_pair[1], preferred_element_type=jnp.float32)
        ).astype(jnp.bfloat16)

    grad_first = pair_sum(first_result, second_full)
    grad_second = pair_sum(second_result, first_full)
    grad_value = jnp.where(odd, grad_first, grad_second)
    grad_out = jnp.where(odd, grad_second, grad_first)
    return (input_grad[None], grad_value[None], grad_out[None])


def solution(mesh):
    sections, tensor = mesh.devices.shape
    split = Mesh(mesh.devices.reshape(sections // 2, 2, tensor), ("pair", "half", "tensor"))
    slots = ("pair", "half")
    by_tokens = P(slots, "tensor", None)
    by_rows = P(slots, None, "tensor", None)
    return jax.shard_map(
        on_device,
        mesh=split,
        in_specs=(by_tokens, by_tokens, by_tokens, by_tokens, P(slots), by_rows, by_rows),
        out_specs=(by_tokens, by_tokens, by_tokens),
        check_vma=False,
    )
```

time: 452 us -> 129 us (0.29)
  waiting for transfers between devices: 320 us -> 28 us
  other arithmetic: 45.8 us -> 9.53 us
  matrix products: 13.6 us -> 38.1 us
  local copies, waits for them, and re-layouts: 26.6 us -> 5.24 us
  between operations: 14.9 us -> 3.74 us
  starting transfers between devices: 5.86 us -> 13 us
  blocking collectives: 24.9 us -> 30.8 us
    ppermute x3 -> x8, waiting for transfers between devices: 266 us -> 22.7 us  [the longest x7 20.5 us: swap_half(): return lax.ppermute(array, 'half', [(0, 1), (1, 0)])]
    reduce_scatter x2 -> x0, waiting for transfers between devices: 53.6 us -> none  [on_device(): lax.psum_scatter(lax.cond(active, lambda piece_now: contract_rows(piece_n...]
    dot_general x7 -> x15, matrix products: 13.2 us -> 38.1 us  [the longest x4 11.3 us: nt_dot(): lax.dot_general(left_side, right_side, (((1,), (1,)), ((), ())), preferre...]
    another operation x2 -> x3, other arithmetic: 21.6 us -> 0.17 us  [the longest x2 0.15 us: scattered(): jnp.stack([tn_dot(result[0], value_weights[0]), tn_dot(result[1], value_w...]
    all_to_all x0 -> x1, blocking collectives: none -> 14.3 us  [scattered(): arrived = lax.all_to_all(pieces, 'tensor', 1, 1, tiled=True)]
    unnamed x30 -> x38, local copies, waits for them, and re-layouts: 13.6 us -> 1.83 us
    convert_element_type x4 -> x5, other arithmetic: 14.3 us -> 2.86 us  [the longest x2 1.67 us: mixed(): arrived = swap_half(partial.astype(jnp.bfloat16))]
    another operation x4 -> x2, local copies, waits for them, and re-layouts: 10.5 us -> 0.99 us  [scattered(): jnp.stack([tn_dot(result[0], value_weights[0]), tn_dot(result[1], value_w...]
  transfers between devices with their start and end apart: 5 -> 9, of which waited for: 5 -> 5; matrix products, arithmetic and copies ran while one was open for 1% -> 20% of each run, Pallas kernels for 0% -> 0%
where the time goes in v1:
time: 129 us; the launch traced here: 128 us
  matrix products  38.1 us (30%)
  blocking collectives  30.8 us (24%)
  waiting for transfers between devices  28 us (22%)
  starting transfers between devices  13 us (10%)
  other arithmetic  9.53 us (7%)
  local copies, waits for them, and re-layouts  5.24 us (4%)
  between operations  3.74 us (3%)
    ppermute x7, waiting for transfers between devices, swap_half(): return lax.ppermute(array, 'half', [(0, 1), (1, 0)])  20.5 us
    all_gather x2, blocking collectives, gathered(): return lax.all_gather(pair, 'tensor', axis=1, tiled=True)  16.5 us
    all_to_all x1, blocking collectives, scattered(): arrived = lax.all_to_all(pieces, 'tensor', 1, 1, tiled=True)  14.3 us
    dot_general x4, matrix products, nt_dot(): lax.dot_general(left_side, right_side, (((1,), (1,)), ((), ())), preferre...  11.3 us
    dot_general x2, matrix products, pair_sum(): jnp.dot(left_pair[1], right_pair[1], preferred_element_type=jnp.float32)  9.25 us
    dot_general x4, matrix products, tn_dot(): lax.dot_general(left_side, right_side, (((0,), (0,)), ((), ())), preferre...  8.88 us
    ppermute x7, starting transfers between devices, swap_half(): return lax.ppermute(array, 'half', [(0, 1), (1, 0)])  7.37 us
    dot_general x2, matrix products, pair_sum(): jnp.dot(left_pair[0], right_pair[0], preferred_element_type=jnp.float32)  6.19 us
  transfers between devices with their start and end apart: 9, of which 5 were waited for; matrix products, arithmetic and copies ran while one was open for 20% of the time, Pallas kernels for 0%

profile of v1, /device:TPU:0, one launch (start us, length us, event | category | flops | bytes accessed | tf_op | source)
XLA Modules:
  0.0 128.4 jit_solution(1166678747074167749)
XLA Ops:
  0.6 3.0 %collective-permute-start.1 = (s32[1]{0:T(128)}, s32[1]{0:T(128)}, u32[]{:S(2)}, u32[]{:S(2)}) collective-permute-start(s32[1]{0:T(128)} %param.11), channel_id=1, source_target_pairs={{0,4},{4,0},{1,5},{5,1},{2,6},{6,2},{3,7},{7,3},{8,12},{12,8},{9,1... | collective-permute-start | bytes 20 | tf_op jit(solution)/shard_map/ppermute | solution.py:12
  3.6 1.0 broadcast_select_fusion
  4.7 1.1 pad_maximum_fusion.4
  5.8 2.0 %collective-permute-start.3 = (bf16[2,768,128]{2,1,0:T(8,128)(2,1)S(1)}, bf16[2,768,128]{2,1,0:T(8,128)(2,1)S(1)}, u32[]{:S(2)}, u32[]{:S(2)}) collective-permute-start(bf16[2,768,128]{2,1,0:T(8,128)(2,1)S(1)} %pad_maximum_fusion.4), channel_id=1, source_target_pairs={{0,4},{4,0},{1,5},{5,1},{2,6},{6,2},{3,7},{7,3},{8,12},{12,8},{9,1... | collective-permute-start | bytes 1179656 | tf_op jit(solution)/shard_map/ppermute | solution.py:12
  11.2 8.6 %all_gather.6 = bf16[2,128,1536]{2,1,0:T(8,128)(2,1)S(1)} all-gather(bf16[2,32,1536]{2,1,0:T(8,128)(2,1)S(1)} %pad_maximum_fusion.7), channel_id=1, replica_groups=mesh['pair'=4,'half'=2,'tensor'=4] {'tensor'}, dimensions={1}, use_global_device_ids=true | all-gather | bytes 983040 | tf_op jit(solution)/shard_map/all_gather | solution.py:81
  19.8 3.5 %fusion.47 = f32[1,768,128]{2,1,0:T(8,128)S(1)} fusion(pred[]{:T(512)S(6)} %eq.9, bf16[1,2,768,1536]{3,2,1,0:T(8,128)(2,1)} %param.13, s32[]{:T(128)S(6)} %select_n.130, bf16[1,2,768,1536]{3,2,1,0:T(8,128)(2,1)} %param.12, bf16[2,128,1536]{2,1,0:T(8,128)(2,1)S(1)} %all_gather.6), kind=kOutput, calls=%fused_computation.50 | convolution fusion | flops 303169536 | bytes 5505029 | tf_op jit(solution)/shard_map/dot_general | solution.py:16
  23.9 2.5 %fusion.44 = f32[1,768,128]{2,1,0:T(8,128)S(1)} fusion(pred[]{:T(512)S(6)} %eq.9, bf16[1,2,768,1536]{3,2,1,0:T(8,128)(2,1)} %param.13, s32[]{:T(128)S(6)} %select_n.127, bf16[1,2,768,1536]{3,2,1,0:T(8,128)(2,1)S(1)} %copy-done, bf16[2,128,1536]{2,1,0:T(8,128)(2,1)S(1)} %all_gather.6), kind=kOutput, calls=%fused_computation.49 | convolution fusion | flops 303169536 | bytes 5505029 | tf_op jit(solution)/shard_map/dot_general | solution.py:16
  29.5 9.3 %collective-permute-done.2 = bf16[2,768,128]{2,1,0:T(8,128)(2,1)} collective-permute-done((bf16[2,768,128]{2,1,0:T(8,128)(2,1)}, bf16[2,768,128]{2,1,0:T(8,128)(2,1)}, u32[]{:S(2)}, u32[]{:S(2)}) %collective-permute-start.2) | collective-permute-done | bytes 393248 | tf_op jit(solution)/shard_map/ppermute | solution.py:12
  38.9 1.1 add_convert_fusion.3
  39.9 1.1 convolution_convert_fusion.5
  41.9 2.3 %fusion.23 = bf16[1,4,32,1536]{3,2,1,0:T(8,128)(2,1)S(1)} fusion(bf16[4,32,768]{2,1,0:T(8,128)(2,1)} %bitcast.165, bf16[1,2,768,1536]{3,2,1,0:T(8,128)(2,1)} %param.12, s32[]{:T(128)S(6)} %select_n.130), kind=kOutput, calls=%fused_computation.29 | convolution fusion | flops 302186496 | bytes 2949124 | tf_op jit(solution)/shard_map/dot_general | solution.py:22
  45.0 2.3 %fusion.20 = bf16[1,4,32,1536]{3,2,1,0:T(8,128)(2,1)S(1)} fusion(bf16[4,32,768]{2,1,0:T(8,128)(2,1)} %bitcast.166, bf16[1,2,768,1536]{3,2,1,0:T(8,128)(2,1)} %param.12, s32[]{:T(128)S(6)} %select_n.127), kind=kOutput, calls=%fused_computation.28 | convolution fusion | flops 302186496 | bytes 2949124 | tf_op jit(solution)/shard_map/dot_general | solution.py:22
  47.5 14.3 %all_to_all.10 = bf16[2,4,32,1536]{3,2,0,1:T(8,128)(2,1)S(1)} all-to-all(bf16[2,4,32,1536]{3,2,0,1:T(8,128)(2,1)S(1)} %copy.18), channel_id=1, replica_groups=mesh['pair'=4,'half'=2,'tensor'=4] {'tensor'}, dimensions={1} | all-to-all | bytes 1572864 | tf_op jit(solution)/shard_map/all_to_all | solution.py:96
  62.0 1.3 %collective-permute-start.5 = (bf16[2,32,1536]{2,1,0:T(8,128)(2,1)S(1)}, bf16[2,32,1536]{2,1,0:T(8,128)(2,1)S(1)}, u32[]{:S(2)}, u32[]{:S(2)}) collective-permute-start(bf16[2,32,1536]{2,1,0:T(8,128)(2,1)S(1)} %add_convert_fusion.5), channel_id=1, source_target_pairs={{8,0},{24,16},{9,1},{25,17},{10,2},{26,18},{11,3},{27,19},{12,4},{... | collective-permute-start | bytes 589832 | tf_op jit(solution)/shard_map/ppermute | solution.py:104
  63.9 4.1 %collective-permute-done.4 = bf16[32,1536]{1,0:T(8,128)(2,1)S(1)} collective-permute-done((bf16[32,1536]{1,0:T(8,128)(2,1)S(1)}, bf16[32,1536]{1,0:T(8,128)(2,1)S(1)}, u32[]{:S(2)}, u32[]{:S(2)}) %collective-permute-start.4) | collective-permute-done | bytes 98336 | tf_op jit(solution)/shard_map/ppermute | solution.py:12
  68.0 2.1 %collective-permute-done.5 = bf16[2,32,1536]{2,1,0:T(8,128)(2,1)S(1)} collective-permute-done((bf16[2,32,1536]{2,1,0:T(8,128)(2,1)S(1)}, bf16[2,32,1536]{2,1,0:T(8,128)(2,1)S(1)}, u32[]{:S(2)}, u32[]{:S(2)}) %collective-permute-start.5) | collective-permute-done | bytes 196640 | tf_op jit(solution)/shard_map/ppermute | solution.py:104
  70.8 7.9 %all_gather.7 = bf16[2,128,1536]{2,1,0:T(8,128)(2,1)S(1)} all-gather(bf16[2,32,1536]{2,1,0:T(8,128)(2,1)S(1)} %maximum_select_fusion), channel_id=1, replica_groups=mesh['pair'=4,'half'=2,'tensor'=4] {'tensor'}, dimensions={1}, use_global_device_ids=true | all-gather | bytes 983040 | tf_op jit(solution)/shard_map/all_gather | solution.py:81
  78.7 2.7 %fusion.53 = f32[1,768,128]{2,1,0:T(8,128)S(1)} fusion(pred[]{:T(512)S(6)} %eq.9, bf16[1,2,768,1536]{3,2,1,0:T(8,128)(2,1)} %param.13, s32[]{:T(128)S(6)} %select_n.130, bf16[1,2,768,1536]{3,2,1,0:T(8,128)(2,1)S(1)} %bitcast.149, bf16[2,128,1536]{2,1,0:T(8,128)(2,1)S(1)} %all_gather.7), kind=kOutput, calls=%fused_computation.52 | convolution fusion | flops 303169536 | bytes 5505029 | tf_op jit(solution)/shard_map/dot_general | solution.py:16
  81.4 2.6 %fusion.50 = f32[1,768,128]{2,1,0:T(8,128)S(1)} fusion(pred[]{:T(512)S(6)} %eq.9, bf16[1,2,768,1536]{3,2,1,0:T(8,128)(2,1)} %param.13, s32[]{:T(128)S(6)} %select_n.127, bf16[1,2,768,1536]{3,2,1,0:T(8,128)(2,1)S(1)} %bitcast.149, bf16[2,128,1536]{2,1,0:T(8,128)(2,1)S(1)} %all_gather.7), kind=kOutput, calls=%fused_computation.51 | convolution fusion | flops 303169536 | bytes 5505029 | tf_op jit(solution)/shard_map/dot_general | solution.py:16
  85.5 4.0 %fusion.68 = f32[768,1536]{1,0:T(8,128)} fusion(bf16[768,128]{1,0:T(8,128)(2,1)S(1)} %bitcast.151, bf16[2,128,1536]{2,1,0:T(8,128)(2,1)} %copy-done.4), kind=kOutput, calls=%fused_computation.84 | convolution fusion | flops 301989888 | bytes 5308416 | tf_op jit(solution)/shard_map/dot_general | solution.py:125
  89.4 7.1 %collective-permute-done.6 = bf16[2,768,128]{2,1,0:T(8,128)(2,1)S(1)} collective-permute-done((bf16[2,768,128]{2,1,0:T(8,128)(2,1)}, bf16[2,768,128]{2,1,0:T(8,128)(2,1)S(1)}, u32[]{:S(2)}, u32[]{:S(2)}) %collective-permute-start.6) | collective-permute-done | bytes 393248 | tf_op jit(solution)/shard_map/ppermute | solution.py:12
  96.6 1.1 convolution_convert_fusion.4
  97.9 2.1 %fusion.29 = bf16[1,4,32,1536]{3,2,1,0:T(8,128)(2,1)S(1)} fusion(bf16[4,32,768]{2,1,0:T(8,128)(2,1)S(1)} %bitcast.163, bf16[1,2,768,1536]{3,2,1,0:T(8,128)(2,1)} %param.12, s32[]{:T(128)S(6)} %select_n.130), kind=kOutput, calls=%fused_computation.31 | convolution fusion | flops 302186496 | bytes 2949124 | tf_op jit(solution)/shard_map/dot_general | solution.py:22
  100.2 2.2 %fusion.26 = bf16[1,4,32,1536]{3,2,1,0:T(8,128)(2,1)S(1)} fusion(bf16[4,32,768]{2,1,0:T(8,128)(2,1)S(1)} %bitcast.164, bf16[1,2,768,1536]{3,2,1,0:T(8,128)(2,1)} %param.12, s32[]{:T(128)S(6)} %select_n.127), kind=kOutput, calls=%fused_computation.30 | convolution fusion | flops 302186496 | bytes 2949124 | tf_op jit(solution)/shard_map/dot_general | solution.py:22
  102.4 0.9 copy.21
  103.4 4.4 %all-to-all-start.1 = ((bf16[2,4,32,1536]{3,2,0,1:T(8,128)(2,1)}), bf16[2,4,32,1536]{3,2,0,1:T(8,128)(2,1)}, u32[]{:S(2)}, u32[]{:S(2)}) async-start(bf16[2,4,32,1536]{3,2,0,1:T(8,128)(2,1)} %copy.21), calls=%async_computation.1 | async-start | bytes 1572864 | tf_op jit(solution)/shard_map/all_to_all | solution.py:96
  107.8 3.3 %add_convert_fusion.1 = bf16[768,1536]{1,0:T(8,128)(2,1)S(1)} fusion(f32[768,1536]{1,0:T(8,128)} %fusion.68, bf16[768,128]{1,0:T(8,128)(2,1)S(1)} %bitcast.157, bf16[2,128,1536]{2,1,0:T(8,128)(2,1)} %copy-done.4), kind=kOutput, calls=%fused_computation.1 | convolution fusion | flops 304349184 | bytes 7667712 | tf_op jit(solution)/shard_map/dot_general | solution.py:124
  111.1 2.9 %fusion.67 = f32[768,1536]{1,0:T(8,128)} fusion(bf16[768,128]{1,0:T(8,128)(2,1)S(1)} %bitcast.155, bf16[2,128,1536]{2,1,0:T(8,128)(2,1)S(1)} %copy-done.2), kind=kOutput, calls=%fused_computation.83 | convolution fusion | flops 301989888 | bytes 5308416 | tf_op jit(solution)/shard_map/dot_general | solution.py:124
  114.0 5.3 %all-to-all-done.1 = bf16[2,4,32,1536]{3,2,0,1:T(8,128)(2,1)} async-done(((bf16[2,4,32,1536]{3,2,0,1:T(8,128)(2,1)}), bf16[2,4,32,1536]{3,2,0,1:T(8,128)(2,1)}, u32[]{:S(2)}, u32[]{:S(2)}) %all-to-all-start.1) | async-done | bytes 786464 | tf_op jit(solution)/shard_map/all_to_all | solution.py:96
  119.3 1.3 %convert_reduce_fusion = f32[2,32,1536]{2,1,0:T(8,128)S(1)} fusion(bf16[2,4,32,1536]{3,2,0,1:T(8,128)(2,1)} %all-to-all-done.1), kind=kLoop, calls=%fused_computation.36 | loop fusion | flops 688128 | bytes 1179648 | tf_op jit(solution)/shard_map/reduce_sum | solution.py:97
  120.6 1.2 fusion.69
  122.4 5.3 %select_bitcast_fusion = (bf16[1,768,1536]{2,1,0:T(8,128)(2,1)}, bf16[1,768,1536]{2,1,0:T(8,128)(2,1)}) fusion(bf16[768,1536]{1,0:T(8,128)(2,1)S(1)} %add_convert_fusion.1, pred[]{:T(512)S(6)} %eq.9, f32[768,1536]{1,0:T(8,128)} %fusion.67, bf16[768,128]{1,0:T(8,128)(2,1)S(1)} %bitcast.153, bf16[2,128,1536]{2,1,0:T(8,128)(2,1)S(1)} %copy-done.3), kind=kOutput, calls=%fused_computation.18 | convolution fusion | flops 306708480 | bytes 12386305 | tf_op jit(solution)/shard_map/dot_general | solution.py:125
  (76 shorter events, 10.9 us)
Async XLA Ops:
  0.6 7.9 %collective-permute-start.1 = (s32[1]{0:T(128)}, s32[1]{0:T(128)}, u32[]{:S(2)}, u32[]{:S(2)}) collective-permute-start(s32[1]{0:T(128)} %param.11), channel_id=1, source_target_pairs={{0,4},{4,0},{1,5},{5,1},{2,6},{6,2},{3,7},{7,3},{8,12},{12,8},{9,1... | collective-permute-start | bytes 20 | tf_op jit(solution)/shard_map/ppermute | solution.py:12
  4.6 6.0 %collective-permute-start = (bf16[32,1536]{1,0:T(8,128)(2,1)S(1)}, bf16[32,1536]{1,0:T(8,128)(2,1)S(1)}, u32[]{:S(2)}, u32[]{:S(2)}) collective-permute-start(bf16[32,1536]{1,0:T(8,128)(2,1)S(1)} %get-tuple-element.16), channel_id=1, source_target_pairs={{0,4},{4,0},{1,5},{5,1},{2,6},{6,2},{3,7},{7,3},{8,12},{12,8},{9,1... | collective-permute-start | bytes 294920 | tf_op jit(solution)/shard_map/ppermute | solution.py:12
  5.8 21.9 %collective-permute-start.3 = (bf16[2,768,128]{2,1,0:T(8,128)(2,1)S(1)}, bf16[2,768,128]{2,1,0:T(8,128)(2,1)S(1)}, u32[]{:S(2)}, u32[]{:S(2)}) collective-permute-start(bf16[2,768,128]{2,1,0:T(8,128)(2,1)S(1)} %pad_maximum_fusion.4), channel_id=1, source_target_pairs={{0,4},{4,0},{1,5},{5,1},{2,6},{6,2},{3,7},{7,3},{8,12},{12,8},{9,1... | collective-permute-start | bytes 1179656 | tf_op jit(solution)/shard_map/ppermute | solution.py:12
  10.6 0.6 copy-start.9
  19.8 3.5 %copy-start.1 = (bf16[2,128,1536]{2,1,0:T(8,128)(2,1)}, bf16[2,128,1536]{2,1,0:T(8,128)(2,1)S(1)}, u32[]{:S(2)}) copy-start(bf16[2,128,1536]{2,1,0:T(8,128)(2,1)S(1)} %all_gather.6) | copy-start | bytes 2359300
  19.8 4.0 %copy-start = (bf16[1,2,768,1536]{3,2,1,0:T(8,128)(2,1)S(1)}, bf16[1,2,768,1536]{3,2,1,0:T(8,128)(2,1)}, u32[]{:S(2)}) copy-start(bf16[1,2,768,1536]{3,2,1,0:T(8,128)(2,1)} %param.12) | copy-start | bytes 14155780
  23.9 3.9 %copy-start.12 = (bf16[1,768,128]{2,1,0:T(8,128)(2,1)S(1)}, bf16[1,768,128]{2,1,0:T(8,128)(2,1)}, u32[]{:S(2)}) copy-start(bf16[1,768,128]{2,1,0:T(8,128)(2,1)} %param.9) | copy-start | bytes 589828
  23.9 3.9 %copy-start.13 = (bf16[1,768,128]{2,1,0:T(8,128)(2,1)S(1)}, bf16[1,768,128]{2,1,0:T(8,128)(2,1)}, u32[]{:S(2)}) copy-start(bf16[1,768,128]{2,1,0:T(8,128)(2,1)} %param.8) | copy-start | bytes 589828
  27.2 11.7 %collective-permute-start.2 = (bf16[2,768,128]{2,1,0:T(8,128)(2,1)}, bf16[2,768,128]{2,1,0:T(8,128)(2,1)}, u32[]{:S(2)}, u32[]{:S(2)}) collective-permute-start(bf16[2,768,128]{2,1,0:T(8,128)(2,1)} %fusion.62), channel_id=1, source_target_pairs={{0,4},{4,0},{1,5},{5,1},{2,6},{6,2},{3,7},{7,3},{8,12},{12,8},{9,1... | collective-permute-start | bytes 1179656 | tf_op jit(solution)/shard_map/ppermute | solution.py:12
  41.9 36.8 %slice-start = ((s8[4718592]{0:T(1024)(128)(4,1)}), s8[524288]{0:T(1024)(128)(4,1)S(1)}, s32[]{:S(2)}) async-start(s8[4718592]{0:T(1024)(128)(4,1)} %bitcast.148), calls=%async_computation.2 | async-start | bytes 1048576
  47.3 31.4 %slice-start.1 = ((s8[4718592]{0:T(1024)(128)(4,1)}), s8[4194304]{0:T(1024)(128)(4,1)S(1)}, s32[]{:S(2)}) async-start(s8[4718592]{0:T(1024)(128)(4,1)} %bitcast.148), calls=%async_computation.3 | async-start | bytes 8388608
  47.4 14.5 %copy-start.10 = (bf16[32,1536]{1,0:T(8,128)(2,1)S(1)}, bf16[32,1536]{1,0:T(8,128)(2,1)}, u32[]{:S(2)}) copy-start(bf16[32,1536]{1,0:T(8,128)(2,1)} %copy-done.9) | copy-start | bytes 294916
  47.4 15.9 %copy-start.14 = (bf16[1,32,3072]{2,1,0:T(8,128)(2,1)S(1)}, bf16[1,32,3072]{2,1,0:T(8,128)(2,1)}, u32[]{:S(2)}) copy-start(bf16[1,32,3072]{2,1,0:T(8,128)(2,1)} %param.7) | copy-start | bytes 589828
  62.0 8.2 %collective-permute-start.5 = (bf16[2,32,1536]{2,1,0:T(8,128)(2,1)S(1)}, bf16[2,32,1536]{2,1,0:T(8,128)(2,1)S(1)}, u32[]{:S(2)}, u32[]{:S(2)}) collective-permute-start(bf16[2,32,1536]{2,1,0:T(8,128)(2,1)S(1)} %add_convert_fusion.5), channel_id=1, source_target_pairs={{8,0},{24,16},{9,1},{25,17},{10,2},{26,18},{11,3},{27,19},{12,4},{... | collective-permute-start | bytes 589832 | tf_op jit(solution)/shard_map/ppermute | solution.py:104
  63.3 6.9 %copy-start.11 = (bf16[1,32,1536]{2,1,0:T(8,128)(2,1)}, bf16[1,32,1536]{2,1,0:T(8,128)(2,1)S(1)}, u32[]{:S(2)}) copy-start(bf16[1,32,1536]{2,1,0:T(8,128)(2,1)S(1)} %get-tuple-element.13) | copy-start | bytes 294916
  63.3 4.7 %collective-permute-start.4 = (bf16[32,1536]{1,0:T(8,128)(2,1)S(1)}, bf16[32,1536]{1,0:T(8,128)(2,1)S(1)}, u32[]{:S(2)}, u32[]{:S(2)}) collective-permute-start(bf16[32,1536]{1,0:T(8,128)(2,1)S(1)} %get-tuple-element.14), channel_id=1, source_target_pairs={{0,4},{4,0},{1,5},{5,1},{2,6},{6,2},{3,7},{7,3},{8,12},{12,8},{9,1... | collective-permute-start | bytes 294920 | tf_op jit(solution)/shard_map/ppermute | solution.py:12
  68.0 2.2 %copy-start.16 = (bf16[32,1536]{1,0:T(8,128)(2,1)}, bf16[32,1536]{1,0:T(8,128)(2,1)S(1)}, u32[]{:S(2)}) copy-start(bf16[32,1536]{1,0:T(8,128)(2,1)S(1)} %collective-permute-done.4) | copy-start | bytes 294916
  70.1 0.7 copy-start.15
  78.7 5.3 %copy-start.4 = (bf16[2,128,1536]{2,1,0:T(8,128)(2,1)}, bf16[2,128,1536]{2,1,0:T(8,128)(2,1)S(1)}, u32[]{:S(2)}) copy-start(bf16[2,128,1536]{2,1,0:T(8,128)(2,1)S(1)} %all_gather.7) | copy-start | bytes 2359300
  81.4 2.6 %copy-start.5 = (f32[1,768,128]{2,1,0:T(8,128)}, f32[1,768,128]{2,1,0:T(8,128)S(1)}, u32[]{:S(2)}) copy-start(f32[1,768,128]{2,1,0:T(8,128)S(1)} %fusion.53) | copy-start | bytes 1179652
  84.0 0.9 copy-start.7
  84.9 11.6 %collective-permute-start.6 = (bf16[2,768,128]{2,1,0:T(8,128)(2,1)}, bf16[2,768,128]{2,1,0:T(8,128)(2,1)S(1)}, u32[]{:S(2)}, u32[]{:S(2)}) collective-permute-start(bf16[2,768,128]{2,1,0:T(8,128)(2,1)} %fusion.61), channel_id=1, source_target_pairs={{0,4},{4,0},{1,5},{5,1},{2,6},{6,2},{3,7},{7,3},{8,12},{12,8},{9,1... | collective-permute-start | bytes 1179656 | tf_op jit(solution)/shard_map/ppermute | solution.py:12
  85.5 11.1 %copy-start.6 = (f32[1,768,128]{2,1,0:T(8,128)S(1)}, f32[1,768,128]{2,1,0:T(8,128)}, u32[]{:S(2)}) copy-start(f32[1,768,128]{2,1,0:T(8,128)} %copy-done.5) | copy-start | bytes 1179652
  85.5 11.1 %copy-start.8 = (f32[1,768,128]{2,1,0:T(8,128)S(1)}, f32[1,768,128]{2,1,0:T(8,128)}, u32[]{:S(2)}) copy-start(f32[1,768,128]{2,1,0:T(8,128)} %copy-done.7) | copy-start | bytes 1179652
  103.4 15.9 %all-to-all-start.1 = ((bf16[2,4,32,1536]{3,2,0,1:T(8,128)(2,1)}), bf16[2,4,32,1536]{3,2,0,1:T(8,128)(2,1)}, u32[]{:S(2)}, u32[]{:S(2)}) async-start(bf16[2,4,32,1536]{3,2,0,1:T(8,128)(2,1)} %copy.21), calls=%async_computation.1 | async-start | bytes 1572864 | tf_op jit(solution)/shard_map/all_to_all | solution.py:96
  107.7 3.3 %copy-start.2 = (bf16[2,128,1536]{2,1,0:T(8,128)(2,1)S(1)}, bf16[2,128,1536]{2,1,0:T(8,128)(2,1)}, u32[]{:S(2)}) copy-start(bf16[2,128,1536]{2,1,0:T(8,128)(2,1)} %copy-done.1) | copy-start | bytes 2359300
  119.3 3.1 %copy-start.3 = (bf16[2,128,1536]{2,1,0:T(8,128)(2,1)S(1)}, bf16[2,128,1536]{2,1,0:T(8,128)(2,1)}, u32[]{:S(2)}) copy-start(bf16[2,128,1536]{2,1,0:T(8,128)(2,1)} %copy-done.1) | copy-start | bytes 2359300
  121.8 5.9 %collective-permute-start.7 = (bf16[32,1536]{1,0:T(8,128)(2,1)S(1)}, bf16[32,1536]{1,0:T(8,128)(2,1)S(1)}, u32[]{:S(2)}, u32[]{:S(2)}) collective-permute-start(bf16[32,1536]{1,0:T(8,128)(2,1)S(1)} %get-tuple-element.12), channel_id=1, source_target_pairs={{0,4},{4,0},{1,5},{5,1},{2,6},{6,2},{3,7},{7,3},{8,12},{12,8},{9,1... | collective-permute-start | bytes 294920 | tf_op jit(solution)/shard_map/ppermute | solution.py:12

commit v2 on v1

v2 whole, which is shorter than its diff:
```python
import functools
import math

import jax
import jax.numpy as jnp
from jax import lax
from jax.experimental import pallas as pl
from jax.experimental.pallas import tpu as pltpu
from jax.sharding import Mesh, PartitionSpec as P

HEAD_DIM = 96
CHUNKS = 4
VMEM_BYTES = 32 * 2**20
NN = (((1,), (0,)), ((), ()))
NT = (((1,), (1,)), ((), ()))
TN = (((0,), (0,)), ((), ()))


def matmul(left_side, right_side, dims):
    return lax.dot_general(left_side, right_side, dims, preferred_element_type=jnp.float32)


def in_vmem():
    return pl.BlockSpec(memory_space=pltpu.VMEM)


def in_smem():
    return pl.BlockSpec(memory_space=pltpu.SMEM)


def in_place():
    return pl.BlockSpec(memory_space=pl.ANY)


def project_kernel(pick_ref, value_ref, out_ref, tokens_ref, partial_ref, held, sems):
    version = pick_ref[1]
    step = held.shape[0] // CHUNKS

    def copy(table_ref, chunk):
        rows = pl.ds(chunk * step, step)
        return pltpu.make_async_copy(table_ref.at[0, version, rows], held.at[rows], sems.at[chunk])

    @pl.when(pick_ref[0] == 1)
    def _():
        for chunk in range(CHUNKS):
            copy(out_ref, chunk).start()

    @pl.when(pick_ref[0] == 0)
    def _():
        for chunk in range(CHUNKS):
            copy(value_ref, chunk).start()

    for chunk in range(CHUNKS):
        copy(value_ref, chunk).wait()
        rows = pl.ds(chunk * step, step)
        partial_ref[rows, :] = matmul(held[rows, :], tokens_ref[...], NT).astype(jnp.bfloat16)


def project(use_out, version, w_value, w_out, tokens):
    rows, width = w_value.shape[2:]
    return pl.pallas_call(
        project_kernel,
        out_shape=jax.ShapeDtypeStruct((rows, tokens.shape[0]), jnp.bfloat16),
        in_specs=[in_smem(), in_place(), in_place(), in_vmem()],
        out_specs=in_vmem(),
        scratch_shapes=[
            pltpu.VMEM((rows, width), jnp.bfloat16),
            pltpu.SemaphoreType.DMA((CHUNKS,)),
        ],
        compiler_params=pltpu.CompilerParams(vmem_limit_bytes=VMEM_BYTES),
        cost_estimate=pl.CostEstimate(
            flops=2 * rows * width * tokens.shape[0],
            bytes_accessed=2 * rows * width,
            transcendentals=0,
        ),
        name="project",
    )(jnp.stack([use_out, version]), w_value, w_out, tokens)


def mix_kernel(
    outer, pick_ref, value_ref, mine_ref, arrived_ref, probs_ref, result_ref, keep_ref, send_ref, held, sems
):
    version = pick_ref[1]
    width = held.shape[1]
    step = width // CHUNKS

    def copy(chunk):
        columns = pl.ds(chunk * step, step)
        return pltpu.make_async_copy(
            value_ref.at[0, version, :, columns], held.at[:, columns], sems.at[chunk]
        )

    for chunk in range(CHUNKS):
        copy(chunk).start()

    def heads(dims):
        for head in range(probs_ref.shape[0]):
            rows = pl.ds(head * HEAD_DIM, HEAD_DIM)
            total = mine_ref[rows, :].astype(jnp.float32) + arrived_ref[rows, :].astype(jnp.float32)
            mixed = matmul(total.astype(jnp.bfloat16), probs_ref[head], dims)
            result_ref[rows, :] = mixed.astype(jnp.bfloat16)

    @pl.when(pick_ref[0] == 1)
    def _():
        heads(NN)

    @pl.when(pick_ref[0] == 0)
    def _():
        heads(NT)

    flipped = result_ref[...].T
    second_core = pick_ref[2] == 1
    shard = flipped.shape[0] // (2 * outer)
    for chunk in range(CHUNKS):
        copy(chunk).wait()
        columns = pl.ds(chunk * step, step)
        partial = matmul(flipped, held[:, columns], NN)
        for index in range(outer):
            low = partial[2 * index * shard : (2 * index + 1) * shard]
            high = partial[(2 * index + 1) * shard : (2 * index + 2) * shard]
            rows = pl.ds(index * shard, shard)
            keep_ref[rows, columns] = jnp.where(second_core, high, low).astype(jnp.bfloat16)
            send_ref[rows, columns] = jnp.where(second_core, low, high).astype(jnp.bfloat16)


def mix(natural, version, core, w_value, mine, arrived, probs, outer):
    rows, width = w_value.shape[2:]
    tokens = mine.shape[1]
    half = jax.ShapeDtypeStruct((tokens // 2, width), jnp.bfloat16)
    return pl.pallas_call(
        functools.partial(mix_kernel, outer),
        out_shape=(jax.ShapeDtypeStruct((rows, tokens), jnp.bfloat16), half, half),
        in_specs=[in_smem(), in_place(), in_vmem(), in_vmem(), in_vmem()],
        out_specs=(in_vmem(), in_vmem(), in_vmem()),
        scratch_shapes=[
            pltpu.VMEM((rows, width), jnp.bfloat16),
            pltpu.SemaphoreType.DMA((CHUNKS,)),
        ],
        compiler_params=pltpu.CompilerParams(vmem_limit_bytes=VMEM_BYTES),
        cost_estimate=pl.CostEstimate(
            flops=2 * rows * (width + tokens) * tokens,
            bytes_accessed=2 * rows * width,
            transcendentals=0,
        ),
        name="mix",
    )(jnp.stack([natural, version, core]), w_value, mine, arrived, probs)


def weight_grad_kernel(odd_ref, a0, a1, b0, b1, first0, first1, second0, second1, value_ref, out_ref):
    odd = odd_ref[0] == 1
    left_first = jnp.concatenate([a0[...], a1[...]], axis=1)
    left_second = jnp.concatenate([b0[...], b1[...]], axis=1)
    right_second = jnp.concatenate([second0[...], second1[...]], axis=0)
    right_first = jnp.concatenate([first0[...], first1[...]], axis=0)
    grad_first = matmul(left_first, right_second, NN)
    grad_second = matmul(left_second, right_first, NN)
    value_ref[0] = jnp.where(odd, grad_first, grad_second).astype(jnp.bfloat16)
    out_ref[0] = jnp.where(odd, grad_second, grad_first).astype(jnp.bfloat16)


def weight_grads(odd, first_results, second_results, first_full, second_full):
    rows, tokens = first_results[0].shape
    width = first_full[0].shape[1]
    step = rows // CHUNKS
    grad = jax.ShapeDtypeStruct((1, rows, width), jnp.bfloat16)
    left = pl.BlockSpec((step, tokens), lambda i: (i, 0))
    right = pl.BlockSpec((tokens, width), lambda i: (0, 0))
    wide = pl.BlockSpec((1, step, width), lambda i: (0, i, 0))
    return pl.pallas_call(
        weight_grad_kernel,
        grid=(CHUNKS,),
        out_shape=(grad, grad),
        in_specs=[in_smem()] + [left] * 4 + [right] * 4,
        out_specs=(wide, wide),
        compiler_params=pltpu.CompilerParams(vmem_limit_bytes=VMEM_BYTES),
        cost_estimate=pl.CostEstimate(
            flops=8 * rows * width * tokens, bytes_accessed=4 * rows * width, transcendentals=0
        ),
        name="weight_grads",
    )(odd[None], *first_results, *second_results, *first_full, *second_full)


def attention_probs(query, key_stash):
    tokens = query.shape[-1]
    query_heads = query.reshape(-1, HEAD_DIM, tokens)
    key_heads = key_stash.reshape(-1, HEAD_DIM, tokens)
    scores = jnp.einsum(
        "hdi,hdj->hij", query_heads, key_heads, preferred_element_type=jnp.float32
    ) * (1.0 / math.sqrt(HEAD_DIM))
    causal = lax.broadcasted_iota(jnp.int32, (tokens, tokens), 1) <= lax.broadcasted_iota(
        jnp.int32, (tokens, tokens), 0
    )
    scores = jnp.where(causal, scores, -jnp.inf)
    row_max = jnp.max(scores, axis=2, keepdims=True)
    expo = jnp.exp(scores - row_max)
    return (expo / jnp.sum(expo, axis=2, keepdims=True)).astype(jnp.bfloat16)


def on_device(section_input, query, key_stash, incoming, version, w_value, w_out):
    half = lax.axis_index("half")
    odd_flag = lax.axis_index("pair") % 2
    odd = odd_flag == 1
    place = lax.axis_index("tensor")
    core, row = place % 2, place // 2
    n_pairs = lax.axis_size("pair")
    n_tensor = lax.axis_size("tensor")
    outer = n_tensor // 2
    width = w_value.shape[3]
    shard = section_input.shape[1]

    def swap_half(array):
        return lax.ppermute(array, "half", [(0, 1), (1, 0)])

    def swap_core(array):
        return lax.ppermute(array, "tensor", [(i, i ^ 1) for i in range(n_tensor)])

    def to_row(array, delta):
        return lax.ppermute(array, "tensor", [(i, i ^ (2 * delta)) for i in range(n_tensor)])

    def to_other_half(array, delta):
        pairs = [
            (h * n_tensor + i, (1 - h) * n_tensor + (i ^ (2 * delta)))
            for h in range(2)
            for i in range(n_tensor)
        ]
        return lax.ppermute(array, ("half", "tensor"), pairs)

    def to_section_below(array, delta):
        pairs = [
            (p * n_tensor + i, (p - 1) * n_tensor + (i ^ (2 * delta)))
            for p in range(1, n_pairs, 2)
            for i in range(n_tensor)
        ]
        return lax.ppermute(array, ("pair", "tensor"), pairs)

    def own_columns(array):
        return lax.dynamic_slice_in_dim(array, half * width, width, 1)

    def other_columns(array):
        return lax.dynamic_slice_in_dim(array, (1 - half) * width, width, 1)

    def gathered(piece):
        return lax.all_gather(piece, "tensor", axis=0, tiled=True)

    def pieces(keep, arrived, addend):
        pair = (keep.astype(jnp.float32) + arrived.astype(jnp.float32)).reshape(outer, shard, width)
        taken = [lax.dynamic_index_in_dim(pair, row ^ d, 0, keepdims=False) for d in range(outer)]
        taken[0] = taken[0] + addend.astype(jnp.float32)
        return [piece.astype(jnp.bfloat16) for piece in taken]

    def added(parts):
        total = parts[0].astype(jnp.float32)
        for part in parts[1:]:
            total = total + part.astype(jnp.float32)
        return total.astype(jnp.bfloat16)

    first = jnp.where(odd, incoming[0], section_input[0])
    first_piece = [own_columns(first), swap_half(other_columns(first))]
    versions = [version[0], swap_half(version)[0]]
    stash = jnp.concatenate([query, key_stash])
    stash_other = swap_half(stash)
    input_piece = [own_columns(section_input[0]), swap_half(other_columns(section_input[0]))]

    first_full = [gathered(first_piece[0]), gathered(first_piece[1])]
    partial = [None, None]
    for m in (1, 0):
        partial[m] = project(odd_flag, versions[m], w_value, w_out, first_full[m])
    arrived = [swap_half(partial[1]), swap_half(partial[0])]
    probs = [attention_probs(query[0], key_stash[0]), attention_probs(stash_other[0], stash_other[1])]
    first_result, keep, send = [None, None], [None, None], [None, None]
    first_sent, second_piece, second_full = [None, None], [None, None], [None, None]
    for m in range(2):
        first_result[m], keep[m], send[m] = mix(
            odd_flag, versions[m], core, w_value, partial[m], arrived[m], probs[m], outer
        )
    for m in range(2):
        first_sent[m] = pieces(keep[m], swap_core(send[m]), first_piece[m])
        received = added([to_section_below(part, d) for d, part in enumerate(first_sent[m])])
        second_piece[m] = jnp.where(odd, input_piece[m], received)
    for m in range(2):
        second_full[m] = gathered(second_piece[m])
        partial[m] = project(1 - odd_flag, versions[m], w_value, w_out, second_full[m])
    arrived = [swap_half(partial[1]), swap_half(partial[0])]
    second_result, last_sent = [None, None], [None, None]
    for m in (1, 0):
        second_result[m], keep[m], send[m] = mix(
            1 - odd_flag, versions[m], core, w_value, partial[m], arrived[m], probs[m], outer
        )
    for m in (1, 0):
        second_sent = pieces(keep[m], swap_core(send[m]), second_piece[m])
        last_sent[m] = [jnp.where(odd, f, s) for f, s in zip(first_sent[m], second_sent)]
    other_grad = added([to_other_half(part, d) for d, part in enumerate(last_sent[1])])
    own_grad = added(
        [last_sent[0][0]] + [to_row(part, d + 1) for d, part in enumerate(last_sent[0][1:])]
    )
    input_grad = jnp.where(
        half == 0,
        jnp.concatenate([own_grad, other_grad], axis=1),
        jnp.concatenate([other_grad, own_grad], axis=1),
    )
    grad_value, grad_out = weight_grads(
        odd_flag, first_result, second_result, first_full, second_full
    )
    return (input_grad[None], grad_value, grad_out)


def solution(mesh):
    sections, tensor = mesh.devices.shape
    split = Mesh(mesh.devices.reshape(sections // 2, 2, tensor), ("pair", "half", "tensor"))
    slots = ("pair", "half")
    by_tokens = P(slots, "tensor", None)
    by_rows = P(slots, None, "tensor", None)
    return jax.shard_map(
        on_device,
        mesh=split,
        in_specs=(by_tokens, by_tokens, by_tokens, by_tokens, P(slots), by_rows, by_rows),
        out_specs=(by_tokens, by_tokens, by_tokens),
        check_vma=False,
    )
```

time: 129 us -> 119 us (0.922)
  matrix products: 38.1 us -> 2.07 us
  Pallas kernels: 0 us -> 25 us
  local copies, waits for them, and re-layouts: 5.24 us -> 20.4 us
  waiting for transfers between devices: 28 us -> 16.2 us
  starting transfers between devices: 13 us -> 19.5 us
  blocking collectives: 30.8 us -> 25.1 us
  between operations: 3.74 us -> 1.67 us
    dot_general x15 -> x0, matrix products: 38.1 us -> none  [the longest x4 11.3 us: nt_dot(): lax.dot_general(left_side, right_side, (((1,), (1,)), ((), ())), preferre...]
    pallas_call x0 -> x9, Pallas kernels: none -> 25 us  [the longest x4 11.5 us: project(): pl.pallas_call(project_kernel, out_shape=jax.ShapeDtypeStruct((rows, toke...]
    unnamed x38 -> x40, local copies, waits for them, and re-layouts: 1.83 us -> 17.1 us
    all_to_all x1 -> x0, blocking collectives: 14.3 us -> none  [scattered(): arrived = lax.all_to_all(pieces, 'tensor', 1, 1, tiled=True)]
    ppermute x7 -> x8, waiting for transfers between devices: 20.5 us -> 6.29 us  [swap_half(): return lax.ppermute(array, 'half', [(0, 1), (1, 0)])]
    all_gather x2 -> x4, blocking collectives: 16.5 us -> 25.1 us  [gathered(): return lax.all_gather(piece, 'tensor', axis=0, tiled=True)]
    ppermute x1 -> x11, starting transfers between devices: 1.29 us -> 9.55 us  [the longest x4 5.17 us: to_section_below(): return lax.ppermute(array, ('pair', 'tensor'), pairs)]
    ppermute x1 -> x11, waiting for transfers between devices: 2.13 us -> 9.87 us  [the longest x4 4.81 us: to_section_below(): return lax.ppermute(array, ('pair', 'tensor'), pairs)]
  transfers between devices with their start and end apart: 9 -> 19, of which waited for: 5 -> 7; matrix products, arithmetic and copies ran while one was open for 20% -> 11% of each run, Pallas kernels for 0% -> 21%
where the time goes in v2:
time: 119 us
  blocking collectives  25.1 us (21%)
  Pallas kernels  25 us (21%)
  local copies, waits for them, and re-layouts  20.4 us (17%)
  starting transfers between devices  19.5 us (16%)
  waiting for transfers between devices  16.2 us (14%)
  other arithmetic  8.81 us (7%)
  matrix products  2.07 us (2%)
  between operations  1.67 us (1%)
    all_gather x4, blocking collectives, gathered(): return lax.all_gather(piece, 'tensor', axis=0, tiled=True)  25.1 us
    unnamed x40, local copies, waits for them, and re-layouts  17.1 us
    pallas_call x4, Pallas kernels, project(): pl.pallas_call(project_kernel, out_shape=jax.ShapeDtypeStruct((rows, toke...  11.5 us
    ppermute x8, starting transfers between devices, swap_half(): return lax.ppermute(array, 'half', [(0, 1), (1, 0)])  9.95 us
    pallas_call x4, Pallas kernels, mix(): pl.pallas_call(functools.partial(mix_kernel, outer), out_shape=(jax.Shape...  9.94 us
    ppermute x8, waiting for transfers between devices, swap_half(): return lax.ppermute(array, 'half', [(0, 1), (1, 0)])  6.29 us
    ppermute x4, starting transfers between devices, to_section_below(): return lax.ppermute(array, ('pair', 'tensor'), pairs)  5.17 us
    ppermute x4, waiting for transfers between devices, to_section_below(): return lax.ppermute(array, ('pair', 'tensor'), pairs)  4.81 us
  transfers between devices with their start and end apart: 19, of which 7 were waited for; matrix products, arithmetic and copies ran while one was open for 11% of the time, Pallas kernels for 21%

profile of v2, /device:TPU:0, one launch (start us, length us, event | category | flops | bytes accessed | tf_op | source)
XLA Modules:
  0.0 118.6 jit_solution(2105837179728289082)
XLA Ops:
  0.6 3.0 %collective-permute-start = (s32[1]{0:T(128)}, s32[1]{0:T(128)}, u32[]{:S(2)}, u32[]{:S(2)}) collective-permute-start(s32[1]{0:T(128)} %param.11), channel_id=1, source_target_pairs={{0,4},{4,0},{1,5},{5,1},{2,6},{6,2},{3,7},{7,3},{8,12},{12,8},{9,1... | collective-permute-start | bytes 20 | tf_op jit(solution)/shard_map/ppermute | solution.py:212
  3.6 1.5 %dynamic-slice_bitcast_fusion = bf16[32,1536]{1,0:T(8,128)(2,1)} fusion(bf16[1,32,3072]{2,1,0:T(8,128)(2,1)} %param.7, s32[]{:T(128)S(6)} %select_n.100), kind=kLoop, calls=%fused_computation.51 | loop fusion | bytes 196612 | tf_op jit(solution)/shard_map/dynamic_slice | solution.py:240
  6.2 2.1 %collective-permute-start.1 = (bf16[32,1536]{1,0:T(8,128)(2,1)S(1)}, bf16[32,1536]{1,0:T(8,128)(2,1)S(1)}, u32[]{:S(2)}, u32[]{:S(2)}) collective-permute-start(bf16[32,1536]{1,0:T(8,128)(2,1)S(1)} %get-tuple-element.36), channel_id=1, source_target_pairs={{0,4},{4,0},{1,5},{5,1},{2,6},{6,2},{3,7},{7,3},{8,12},{12,8},{9,1... | collective-permute-start | bytes 294920 | tf_op jit(solution)/shard_map/ppermute | solution.py:212
  8.9 6.5 %all-gather = bf16[1,128,1536]{2,1,0:T(8,128)(2,1)S(1)} all-gather(bf16[1,32,1536]{2,1,0:T(8,128)(2,1)S(1)} %get-tuple-element.35), channel_id=2, replica_groups=mesh['pair'=4,'half'=2,'tensor'=4] {'tensor'}, dimensions={1}, use_global_device_ids=true | all-gather | bytes 491520 | tf_op jit(solution)/shard_map/all_gather | solution.py:243
  15.5 2.3 %copy-done = bf16[1,2,768,1536]{3,2,1,0:T(8,128)(2,1)S(1)} copy-done((bf16[1,2,768,1536]{3,2,1,0:T(8,128)(2,1)S(1)}, bf16[1,2,768,1536]{3,2,1,0:T(8,128)(2,1)}, u32[]{:S(2)}) %copy-start) | copy-done | bytes 4718616
  17.8 2.3 %copy-done.4 = bf16[1,2,768,1536]{3,2,1,0:T(8,128)(2,1)S(1)} copy-done((bf16[1,2,768,1536]{3,2,1,0:T(8,128)(2,1)S(1)}, bf16[1,2,768,1536]{3,2,1,0:T(8,128)(2,1)}, u32[]{:S(2)}) %copy-start.4) | copy-done | bytes 4718616
  20.1 2.9 %project.4.mine_ref = bf16[768,128]{1,0:T(8,128)(2,1)S(1)} custom-call(s32[2]{0:T(128)S(1)} %pad_add_fusion.1.pick_ref, bf16[1,2,768,1536]{3,2,1,0:T(8,128)(2,1)S(1)} %copy-done, bf16[1,2,768,1536]{3,2,1,0:T(8,128)(2,1)S(1)} %copy-done.4, bf16[128,1536]{1,0:T(8,128)(2,1)S(1)} %bitcast.64), custom_call_target="tpu_custom_call" | custom-call | flops 301989888 | bytes 2359296 | tf_op jit(solution)/shard_map/project/pallas_call | solution.py:61
  27.4 6.1 %all_gather.13.tokens_ref.first1 = bf16[128,1536]{1,0:T(8,128)(2,1)S(1)} all-gather(bf16[32,1536]{1,0:T(8,128)(2,1)S(1)} %collective-permute-done.1), channel_id=1, replica_groups=mesh['pair'=4,'half'=2,'tensor'=4] {'tensor'}, dimensions={0}, use_global_device_ids=true | all-gather | bytes 491520 | tf_op jit(solution)/shard_map/all_gather | solution.py:243
  33.5 2.3 %copy-done.1 = bf16[1,2,768,1536]{3,2,1,0:T(8,128)(2,1)S(1)} copy-done((bf16[1,2,768,1536]{3,2,1,0:T(8,128)(2,1)S(1)}, bf16[1,2,768,1536]{3,2,1,0:T(8,128)(2,1)}, u32[]{:S(2)}) %copy-start.1) | copy-done | bytes 4718616
  35.8 2.3 %copy-done.5 = bf16[1,2,768,1536]{3,2,1,0:T(8,128)(2,1)S(1)} copy-done((bf16[1,2,768,1536]{3,2,1,0:T(8,128)(2,1)S(1)}, bf16[1,2,768,1536]{3,2,1,0:T(8,128)(2,1)}, u32[]{:S(2)}) %copy-start.5) | copy-done | bytes 4718616
  38.2 2.9 %project.5.mine_ref = bf16[768,128]{1,0:T(8,128)(2,1)S(1)} custom-call(s32[2]{0:T(128)S(1)} %pad_add_fusion.2.pick_ref, bf16[1,2,768,1536]{3,2,1,0:T(8,128)(2,1)S(1)} %copy-done.1, bf16[1,2,768,1536]{3,2,1,0:T(8,128)(2,1)S(1)} %copy-done.5, bf16[128,1536]{1,0:T(8,128)(2,1)S(1)} %all_gather.13.tokens_ref.first1), custom_call_target="tpu_custom_call" | custom-call | flops 301989888 | bytes 2359296 | tf_op jit(solution)/shard_map/project/pallas_call | solution.py:61
  43.0 5.2 %collective-permute-done.2.arrived_ref = bf16[768,128]{1,0:T(8,128)(2,1)S(1)} collective-permute-done((bf16[768,128]{1,0:T(8,128)(2,1)S(1)}, bf16[768,128]{1,0:T(8,128)(2,1)S(1)}, u32[]{:S(2)}, u32[]{:S(2)}) %collective-permute-start.2) | collective-permute-done | bytes 196640 | tf_op jit(solution)/shard_map/ppermute | solution.py:212
  48.3 2.3 %mix.4 = (bf16[768,128]{1,0:T(8,128)(2,1)S(1)}, bf16[64,1536]{1,0:T(8,128)(2,1)S(1)}, bf16[64,1536]{1,0:T(8,128)(2,1)S(1)}) custom-call(s32[3]{0:T(128)S(1)} %add_add_fusion.pick_ref, bf16[1,2,768,1536]{3,2,1,0:T(8,128)(2,1)S(1)} %bitcast.63, bf16[768,128]{1,0:T(8,128)(2,1)S(1)} %project.4.mine_ref, bf16[768,128]{1,0:T(8,128)(2,1)S(1)} %collective-permute-done.2.arrived_ref, ...), custom_call_target="tpu_custom_call" | custom-call | flops 327155712 | bytes 2359296 | tf_op jit(solution)/shard_map/mix/pallas_call | solution.py:130
  50.7 1.7 %fusion.32 = (bf16[1,768,128]{2,1,0:T(8,128)(2,1)S(1)}, bf16[1,768,128]{2,1,0:T(8,128)(2,1)}) fusion(bf16[2,768,128]{2,1,0:T(8,128)(2,1)} %collective-permute-done.8), kind=kLoop, calls=%fused_computation.65 | loop fusion | bytes 786432 | tf_op jit(solution)/shard_map/slice | solution.py:269
  52.4 1.5 %fusion.12.probs_ref = bf16[8,128,128]{2,1,0:T(8,128)(2,1)S(1)} fusion(bf16[8,96,128]{2,1,0:T(8,128)(2,1)} %bitcast.78, bf16[8,96,128]{2,1,0:T(8,128)(2,1)S(1)} %bitcast.77, pred[128,128]{1,0:T(8,128)(4,1)S(1)} %iota_compare_fusion), kind=kOutput, calls=%fused_computation.14 | convolution fusion | flops 25823488 | bytes 671744 | tf_op jit(solution)/shard_map/div | solution.py:196
  54.0 2.3 %copy-done.2 = bf16[1,2,768,1536]{3,2,1,0:T(8,128)(2,1)S(1)} copy-done((bf16[1,2,768,1536]{3,2,1,0:T(8,128)(2,1)S(1)}, bf16[1,2,768,1536]{3,2,1,0:T(8,128)(2,1)}, u32[]{:S(2)}) %copy-start.2) | copy-done | bytes 4718616
  56.3 2.3 %mix.5 = (bf16[768,128]{1,0:T(8,128)(2,1)S(1)}, bf16[64,1536]{1,0:T(8,128)(2,1)S(1)}, bf16[64,1536]{1,0:T(8,128)(2,1)S(1)}) custom-call(s32[3]{0:T(128)S(1)} %add_add_fusion.2.pick_ref, bf16[1,2,768,1536]{3,2,1,0:T(8,128)(2,1)S(1)} %copy-done.2, bf16[768,128]{1,0:T(8,128)(2,1)S(1)} %project.5.mine_ref, ...), custom_call_target="tpu_custom_call" | custom-call | flops 327155712 | bytes 2359296 | tf_op jit(solution)/shard_map/mix/pallas_call | solution.py:130
  64.6 3.0 %collective-permute-done.5 = bf16[32,1536]{1,0:T(8,128)(2,1)S(1)} collective-permute-done((bf16[32,1536]{1,0:T(8,128)(2,1)S(1)}, bf16[32,1536]{1,0:T(8,128)(2,1)S(1)}, u32[]{:S(2)}, u32[]{:S(2)}) %collective-permute-start.5) | collective-permute-done | bytes 98336 | tf_op jit(solution)/shard_map/ppermute | solution.py:234
  67.6 1.8 %collective-permute-done.4 = bf16[32,1536]{1,0:T(8,128)(2,1)S(1)} collective-permute-done((bf16[32,1536]{1,0:T(8,128)(2,1)S(1)}, bf16[32,1536]{1,0:T(8,128)(2,1)S(1)}, u32[]{:S(2)}, u32[]{:S(2)}) %collective-permute-start.4) | collective-permute-done | bytes 98336 | tf_op jit(solution)/shard_map/ppermute | solution.py:234
  69.5 6.1 %all_gather.14.tokens_ref.second0 = bf16[128,1536]{1,0:T(8,128)(2,1)S(1)} all-gather(bf16[32,1536]{1,0:T(8,128)(2,1)S(1)} %fusion.18), channel_id=1, replica_groups=mesh['pair'=4,'half'=2,'tensor'=4] {'tensor'}, dimensions={0}, use_global_device_ids=true | all-gather | bytes 491520 | tf_op jit(solution)/shard_map/all_gather | solution.py:243
  75.6 2.3 %copy-done.6 = bf16[1,2,768,1536]{3,2,1,0:T(8,128)(2,1)S(1)} copy-done((bf16[1,2,768,1536]{3,2,1,0:T(8,128)(2,1)S(1)}, bf16[1,2,768,1536]{3,2,1,0:T(8,128)(2,1)}, u32[]{:S(2)}) %copy-start.6) | copy-done | bytes 4718616
  78.0 2.9 %project.6.mine_ref = bf16[768,128]{1,0:T(8,128)(2,1)S(1)} custom-call(s32[2]{0:T(128)S(1)} %pad_add_fusion.pick_ref, bf16[1,2,768,1536]{3,2,1,0:T(8,128)(2,1)S(1)} %copy-done.2, bf16[1,2,768,1536]{3,2,1,0:T(8,128)(2,1)S(1)} %copy-done.6, bf16[128,1536]{1,0:T(8,128)(2,1)S(1)} %all_gather.14.tokens_ref.second0), custom_call_target="tpu_custom_call" | custom-call | flops 301989888 | bytes 2359296 | tf_op jit(solution)/shard_map/project/pallas_call | solution.py:61
  81.6 6.3 %all_gather.15.tokens_ref.second1 = bf16[128,1536]{1,0:T(8,128)(2,1)S(1)} all-gather(bf16[32,1536]{1,0:T(8,128)(2,1)S(1)} %fusion.20), channel_id=1, replica_groups=mesh['pair'=4,'half'=2,'tensor'=4] {'tensor'}, dimensions={0}, use_global_device_ids=true | all-gather | bytes 491520 | tf_op jit(solution)/shard_map/all_gather | solution.py:243
  87.9 2.9 %project.7.mine_ref = bf16[768,128]{1,0:T(8,128)(2,1)S(1)} custom-call(s32[2]{0:T(128)S(1)} %pad_add_fusion.3.pick_ref, bf16[1,2,768,1536]{3,2,1,0:T(8,128)(2,1)S(1)} %copy-done.2, bf16[1,2,768,1536]{3,2,1,0:T(8,128)(2,1)S(1)} %copy-done.6, bf16[128,1536]{1,0:T(8,128)(2,1)S(1)} %all_gather.15.tokens_ref.second1), custom_call_target="tpu_custom_call" | custom-call | flops 301989888 | bytes 2359296 | tf_op jit(solution)/shard_map/project/pallas_call | solution.py:61
  90.8 1.6 %collective-permute-start.12 = (bf16[768,128]{1,0:T(8,128)(2,1)S(1)}, bf16[768,128]{1,0:T(8,128)(2,1)S(1)}, u32[]{:S(2)}, u32[]{:S(2)}) collective-permute-start(bf16[768,128]{1,0:T(8,128)(2,1)S(1)} %project.7.mine_ref), channel_id=1, source_target_pairs={{0,4},{4,0},{1,5},{5,1},{2,6},{6,2},{3,7},{7,3},{8,12},{12,8},{9,1... | collective-permute-start | bytes 589832 | tf_op jit(solution)/shard_map/ppermute | solution.py:212
  93.0 3.1 %mix.7 = (bf16[768,128]{1,0:T(8,128)(2,1)S(1)}, bf16[64,1536]{1,0:T(8,128)(2,1)S(1)}, bf16[64,1536]{1,0:T(8,128)(2,1)}) custom-call(s32[3]{0:T(128)S(1)} %add_add_fusion.3.pick_ref, bf16[1,2,768,1536]{3,2,1,0:T(8,128)(2,1)S(1)} %copy-done.2, bf16[768,128]{1,0:T(8,128)(2,1)S(1)} %project.7.mine_ref, bf16[768,128]{1,0:T(8,128)(2,1)S(1)} %collective-permute-done.15.arrived_ref, ...), custom_call_target="tpu_custom_call" | custom-call | flops 327155712 | bytes 2359296 | tf_op jit(solution)/shard_map/mix/pallas_call | solution.py:130
  98.0 2.3 %copy-done.3 = bf16[1,2,768,1536]{3,2,1,0:T(8,128)(2,1)S(1)} copy-done((bf16[1,2,768,1536]{3,2,1,0:T(8,128)(2,1)S(1)}, bf16[1,2,768,1536]{3,2,1,0:T(8,128)(2,1)}, u32[]{:S(2)}) %copy-start.3) | copy-done | bytes 4718616
  100.3 2.2 %mix.6 = (bf16[768,128]{1,0:T(8,128)(2,1)S(1)}, bf16[64,1536]{1,0:T(8,128)(2,1)S(1)}, bf16[64,1536]{1,0:T(8,128)(2,1)S(1)}) custom-call(s32[3]{0:T(128)S(1)} %add_add_fusion.1.pick_ref, bf16[1,2,768,1536]{3,2,1,0:T(8,128)(2,1)S(1)} %copy-done.3, bf16[768,128]{1,0:T(8,128)(2,1)S(1)} %project.6.mine_ref, ...), custom_call_target="tpu_custom_call" | custom-call | flops 327155712 | bytes 2359296 | tf_op jit(solution)/shard_map/mix/pallas_call | solution.py:130
  102.7 3.5 %weight_grads.1 = (bf16[1,768,1536]{2,1,0:T(8,128)(2,1)}, bf16[1,768,1536]{2,1,0:T(8,128)(2,1)}) custom-call(s32[1]{0:T(128)} %bitcast.odd_ref, bf16[768,128]{1,0:T(8,128)(2,1)S(1)} %get-tuple-element.25.a0, bf16[768,128]{1,0:T(8,128)(2,1)S(1)} %get-tuple-element.26.a1, bf16[768,128]{1,0:T(8,128)(2,1)S(1)} %get-tuple-element.27.b0, ...), custom_call_target="tpu_custom_call" | custom-call | flops 1207959552 | bytes 4718592 | tf_op jit(solution)/shard_map/weight_grads/pallas_call | solution.py:169
  108.1 1.6 %collective-permute-start.17 = (bf16[32,1536]{1,0:T(8,128)(2,1)S(1)}, bf16[32,1536]{1,0:T(8,128)(2,1)S(1)}, u32[]{:S(2)}, u32[]{:S(2)}) collective-permute-start(bf16[32,1536]{1,0:T(8,128)(2,1)S(1)} %get-tuple-element.31), channel_id=1, source_target_pairs={{0,4},{1,5},{2,6},{3,7},{4,0},{5,1},{6,2},{7,3},{8,12},{9,13},{10,... | collective-permute-start | bytes 294920 | tf_op jit(solution)/shard_map/ppermute | solution.py:226
  113.8 2.1 %collective-permute-done.18 = bf16[32,1536]{1,0:T(8,128)(2,1)S(1)} collective-permute-done((bf16[32,1536]{1,0:T(8,128)(2,1)S(1)}, bf16[32,1536]{1,0:T(8,128)(2,1)S(1)}, u32[]{:S(2)}, u32[]{:S(2)}) %collective-permute-start.18) | collective-permute-done | bytes 98336 | tf_op jit(solution)/shard_map/ppermute | solution.py:226
  115.9 2.0 %collective-permute-done.14 = bf16[32,1536]{1,0:T(8,128)(2,1)S(1)} collective-permute-done((bf16[32,1536]{1,0:T(8,128)(2,1)S(1)}, bf16[32,1536]{1,0:T(8,128)(2,1)S(1)}, u32[]{:S(2)}, u32[]{:S(2)}) %collective-permute-start.14) | collective-permute-done | bytes 98336 | tf_op jit(solution)/shard_map/ppermute | solution.py:218
  (91 shorter events, 23.6 us)
Async XLA Ops:
  0.6 26.0 %collective-permute-start = (s32[1]{0:T(128)}, s32[1]{0:T(128)}, u32[]{:S(2)}, u32[]{:S(2)}) collective-permute-start(s32[1]{0:T(128)} %param.11), channel_id=1, source_target_pairs={{0,4},{4,0},{1,5},{5,1},{2,6},{6,2},{3,7},{7,3},{8,12},{12,8},{9,1... | collective-permute-start | bytes 20 | tf_op jit(solution)/shard_map/ppermute | solution.py:212
  5.2 76.3 %collective-permute-start.6 = (bf16[32,1536]{1,0:T(8,128)(2,1)}, bf16[32,1536]{1,0:T(8,128)(2,1)}, u32[]{:S(2)}, u32[]{:S(2)}) collective-permute-start(bf16[32,1536]{1,0:T(8,128)(2,1)} %dynamic-slice_bitcast_fusion), channel_id=1, source_target_pairs={{0,4},{4,0},{1,5},{5,1},{2,6},{6,2},{3,7},{7,3},{8,12},{12,8},{9,1... | collective-permute-start | bytes 294920 | tf_op jit(solution)/shard_map/ppermute | solution.py:212
  6.2 21.2 %collective-permute-start.1 = (bf16[32,1536]{1,0:T(8,128)(2,1)S(1)}, bf16[32,1536]{1,0:T(8,128)(2,1)S(1)}, u32[]{:S(2)}, u32[]{:S(2)}) collective-permute-start(bf16[32,1536]{1,0:T(8,128)(2,1)S(1)} %get-tuple-element.36), channel_id=1, source_target_pairs={{0,4},{4,0},{1,5},{5,1},{2,6},{6,2},{3,7},{7,3},{8,12},{12,8},{9,1... | collective-permute-start | bytes 294920 | tf_op jit(solution)/shard_map/ppermute | solution.py:212
  20.1 3.5 %copy-start.16 = (bf16[1,768,128]{2,1,0:T(8,128)(2,1)S(1)}, bf16[1,768,128]{2,1,0:T(8,128)(2,1)}, u32[]{:S(2)}) copy-start(bf16[1,768,128]{2,1,0:T(8,128)(2,1)} %param.9) | copy-start | bytes 589828
  20.1 3.5 %copy-start.17 = (bf16[1,768,128]{2,1,0:T(8,128)(2,1)S(1)}, bf16[1,768,128]{2,1,0:T(8,128)(2,1)}, u32[]{:S(2)}) copy-start(bf16[1,768,128]{2,1,0:T(8,128)(2,1)} %param.8) | copy-start | bytes 589828
  23.0 30.9 %collective-permute-start.7 = (bf16[768,128]{1,0:T(8,128)(2,1)S(1)}, bf16[768,128]{1,0:T(8,128)(2,1)S(1)}, u32[]{:S(2)}, u32[]{:S(2)}) collective-permute-start(bf16[768,128]{1,0:T(8,128)(2,1)S(1)} %project.4.mine_ref), channel_id=1, source_target_pairs={{0,4},{4,0},{1,5},{5,1},{2,6},{6,2},{3,7},{7,3},{8,12},{12,8},{9,1... | collective-permute-start | bytes 589832 | tf_op jit(solution)/shard_map/ppermute | solution.py:212
  24.4 26.3 %collective-permute-start.8 = (bf16[2,768,128]{2,1,0:T(8,128)(2,1)}, bf16[2,768,128]{2,1,0:T(8,128)(2,1)}, u32[]{:S(2)}, u32[]{:S(2)}) collective-permute-start(bf16[2,768,128]{2,1,0:T(8,128)(2,1)} %pad_maximum_fusion), channel_id=1, source_target_pairs={{0,4},{4,0},{1,5},{5,1},{2,6},{6,2},{3,7},{7,3},{8,12},{12,8},{9,1... | collective-permute-start | bytes 1179656 | tf_op jit(solution)/shard_map/ppermute | solution.py:212
  26.1 22.2 %slice-start = ((s8[4718592]{0:T(1024)(128)(4,1)}), s8[524288]{0:T(1024)(128)(4,1)S(1)}, s32[]{:S(2)}) async-start(s8[4718592]{0:T(1024)(128)(4,1)} %bitcast.62), calls=%async_computation | async-start | bytes 1048576
  38.2 10.1 %slice-start.1 = ((s8[4718592]{0:T(1024)(128)(4,1)}), s8[4194304]{0:T(1024)(128)(4,1)S(1)}, s32[]{:S(2)}) async-start(s8[4718592]{0:T(1024)(128)(4,1)} %bitcast.62), calls=%async_computation.1 | async-start | bytes 8388608
  41.1 7.2 %collective-permute-start.2 = (bf16[768,128]{1,0:T(8,128)(2,1)S(1)}, bf16[768,128]{1,0:T(8,128)(2,1)S(1)}, u32[]{:S(2)}, u32[]{:S(2)}) collective-permute-start(bf16[768,128]{1,0:T(8,128)(2,1)S(1)} %project.5.mine_ref), channel_id=1, source_target_pairs={{0,4},{4,0},{1,5},{5,1},{2,6},{6,2},{3,7},{7,3},{8,12},{12,8},{9,1... | collective-permute-start | bytes 589832 | tf_op jit(solution)/shard_map/ppermute | solution.py:212
  50.6 8.6 %collective-permute-start.3 = (bf16[64,1536]{1,0:T(8,128)(2,1)S(1)}, bf16[64,1536]{1,0:T(8,128)(2,1)S(1)}, u32[]{:S(2)}, u32[]{:S(2)}) collective-permute-start(bf16[64,1536]{1,0:T(8,128)(2,1)S(1)} %get-tuple-element.18), channel_id=1, source_target_pairs={{0,1},{1,0},{2,3},{3,2},{4,5},{5,4},{6,7},{7,6},{8,9},{9,8},{10,11... | collective-permute-start | bytes 589832 | tf_op jit(solution)/shard_map/ppermute | solution.py:215
  52.4 17.0 %copy-start.11 = (bf16[1,32,3072]{2,1,0:T(8,128)(2,1)S(1)}, bf16[1,32,3072]{2,1,0:T(8,128)(2,1)}, u32[]{:S(2)}) copy-start(bf16[1,32,3072]{2,1,0:T(8,128)(2,1)} %param.7) | copy-start | bytes 589828
  54.0 2.3 %copy-start.2 = (bf16[1,2,768,1536]{3,2,1,0:T(8,128)(2,1)S(1)}, bf16[1,2,768,1536]{3,2,1,0:T(8,128)(2,1)}, u32[]{:S(2)}) copy-start(bf16[1,2,768,1536]{3,2,1,0:T(8,128)(2,1)} %value_ref.15) | copy-start | bytes 14155780
  58.6 3.3 %collective-permute-start.9 = (bf16[64,1536]{1,0:T(8,128)(2,1)S(1)}, bf16[64,1536]{1,0:T(8,128)(2,1)S(1)}, u32[]{:S(2)}, u32[]{:S(2)}) collective-permute-start(bf16[64,1536]{1,0:T(8,128)(2,1)S(1)} %get-tuple-element.20), channel_id=1, source_target_pairs={{0,1},{1,0},{2,3},{3,2},{4,5},{5,4},{6,7},{7,6},{8,9},{9,8},{10,11... | collective-permute-start | bytes 589832 | tf_op jit(solution)/shard_map/ppermute | solution.py:215
  59.2 10.3 %copy-start.9 = (f32[64,1536]{1,0:T(8,128)}, f32[64,1536]{1,0:T(8,128)S(1)}, u32[]{:S(2)}) copy-start(f32[64,1536]{1,0:T(8,128)S(1)} %convert_add_fusion.3) | copy-start | bytes 1179652
  59.3 21.6 %copy-start.12 = (bf16[32,1536]{1,0:T(8,128)(2,1)}, bf16[32,1536]{1,0:T(8,128)(2,1)S(1)}, u32[]{:S(2)}) copy-start(bf16[32,1536]{1,0:T(8,128)(2,1)S(1)} %fusion.27) | copy-start | bytes 294916
  59.3 8.3 %collective-permute-start.5 = (bf16[32,1536]{1,0:T(8,128)(2,1)S(1)}, bf16[32,1536]{1,0:T(8,128)(2,1)S(1)}, u32[]{:S(2)}, u32[]{:S(2)}) collective-permute-start(bf16[32,1536]{1,0:T(8,128)(2,1)S(1)} %fusion.17), channel_id=1, source_target_pairs={{8,2},{9,3},{10,0},{11,1},{24,18},{25,19},{26,16},{27,17},{12,6},{... | collective-permute-start | bytes 294920 | tf_op jit(solution)/shard_map/ppermute | solution.py:234
  60.6 8.8 %collective-permute-start.4 = (bf16[32,1536]{1,0:T(8,128)(2,1)S(1)}, bf16[32,1536]{1,0:T(8,128)(2,1)S(1)}, u32[]{:S(2)}, u32[]{:S(2)}) collective-permute-start(bf16[32,1536]{1,0:T(8,128)(2,1)S(1)} %fusion.27), channel_id=1, source_target_pairs={{8,0},{9,1},{10,2},{11,3},{24,16},{25,17},{26,18},{27,19},{12,4},{... | collective-permute-start | bytes 294920 | tf_op jit(solution)/shard_map/ppermute | solution.py:234
  62.0 18.9 %copy-start.10 = (f32[64,1536]{1,0:T(8,128)}, f32[64,1536]{1,0:T(8,128)S(1)}, u32[]{:S(2)}) copy-start(f32[64,1536]{1,0:T(8,128)S(1)} %convert_add_fusion.2) | copy-start | bytes 1179652
  62.0 19.5 %collective-permute-start.11 = (bf16[32,1536]{1,0:T(8,128)(2,1)S(1)}, bf16[32,1536]{1,0:T(8,128)(2,1)S(1)}, u32[]{:S(2)}, u32[]{:S(2)}) collective-permute-start(bf16[32,1536]{1,0:T(8,128)(2,1)S(1)} %fusion.19), channel_id=1, source_target_pairs={{8,2},{9,3},{10,0},{11,1},{24,18},{25,19},{26,16},{27,17},{12,6},{... | collective-permute-start | bytes 294920 | tf_op jit(solution)/shard_map/ppermute | solution.py:234
  63.3 17.6 %copy-start.14 = (bf16[32,1536]{1,0:T(8,128)(2,1)}, bf16[32,1536]{1,0:T(8,128)(2,1)S(1)}, u32[]{:S(2)}) copy-start(bf16[32,1536]{1,0:T(8,128)(2,1)S(1)} %fusion.16) | copy-start | bytes 294916
  63.3 18.2 %collective-permute-start.10 = (bf16[32,1536]{1,0:T(8,128)(2,1)S(1)}, bf16[32,1536]{1,0:T(8,128)(2,1)S(1)}, u32[]{:S(2)}, u32[]{:S(2)}) collective-permute-start(bf16[32,1536]{1,0:T(8,128)(2,1)S(1)} %fusion.16), channel_id=1, source_target_pairs={{8,0},{9,1},{10,2},{11,3},{24,16},{25,17},{26,18},{27,19},{12,4},{... | collective-permute-start | bytes 294920 | tf_op jit(solution)/shard_map/ppermute | solution.py:234
  80.9 12.1 %collective-permute-start.15 = (bf16[768,128]{1,0:T(8,128)(2,1)S(1)}, bf16[768,128]{1,0:T(8,128)(2,1)S(1)}, u32[]{:S(2)}, u32[]{:S(2)}) collective-permute-start(bf16[768,128]{1,0:T(8,128)(2,1)S(1)} %project.6.mine_ref), channel_id=1, source_target_pairs={{0,4},{4,0},{1,5},{5,1},{2,6},{6,2},{3,7},{7,3},{8,12},{12,8},{9,1... | collective-permute-start | bytes 589832 | tf_op jit(solution)/shard_map/ppermute | solution.py:212
  90.8 7.2 %collective-permute-start.12 = (bf16[768,128]{1,0:T(8,128)(2,1)S(1)}, bf16[768,128]{1,0:T(8,128)(2,1)S(1)}, u32[]{:S(2)}, u32[]{:S(2)}) collective-permute-start(bf16[768,128]{1,0:T(8,128)(2,1)S(1)} %project.7.mine_ref), channel_id=1, source_target_pairs={{0,4},{4,0},{1,5},{5,1},{2,6},{6,2},{3,7},{7,3},{8,12},{12,8},{9,1... | collective-permute-start | bytes 589832 | tf_op jit(solution)/shard_map/ppermute | solution.py:212
  96.8 9.4 %collective-permute-start.16 = (bf16[64,1536]{1,0:T(8,128)(2,1)}, bf16[64,1536]{1,0:T(8,128)(2,1)}, u32[]{:S(2)}, u32[]{:S(2)}) collective-permute-start(bf16[64,1536]{1,0:T(8,128)(2,1)} %get-tuple-element.24), channel_id=1, source_target_pairs={{0,1},{1,0},{2,3},{3,2},{4,5},{5,4},{6,7},{7,6},{8,9},{9,8},{10,11... | collective-permute-start | bytes 589832 | tf_op jit(solution)/shard_map/ppermute | solution.py:215
  98.0 2.3 %copy-start.3 = (bf16[1,2,768,1536]{3,2,1,0:T(8,128)(2,1)S(1)}, bf16[1,2,768,1536]{3,2,1,0:T(8,128)(2,1)}, u32[]{:S(2)}) copy-start(bf16[1,2,768,1536]{3,2,1,0:T(8,128)(2,1)} %value_ref.15) | copy-start | bytes 14155780
  100.3 6.8 %copy-start.15 = (bf16[32,1536]{1,0:T(8,128)(2,1)S(1)}, bf16[32,1536]{1,0:T(8,128)(2,1)}, u32[]{:S(2)}) copy-start(bf16[32,1536]{1,0:T(8,128)(2,1)} %copy-done.14) | copy-start | bytes 294916
  102.6 15.3 %copy-start.13 = (bf16[32,1536]{1,0:T(8,128)(2,1)S(1)}, bf16[32,1536]{1,0:T(8,128)(2,1)}, u32[]{:S(2)}) copy-start(bf16[32,1536]{1,0:T(8,128)(2,1)} %copy-done.12) | copy-start | bytes 294916
  102.6 8.0 %collective-permute-start.13 = (bf16[64,1536]{1,0:T(8,128)(2,1)S(1)}, bf16[64,1536]{1,0:T(8,128)(2,1)S(1)}, u32[]{:S(2)}, u32[]{:S(2)}) collective-permute-start(bf16[64,1536]{1,0:T(8,128)(2,1)S(1)} %get-tuple-element.22), channel_id=1, source_target_pairs={{0,1},{1,0},{2,3},{3,2},{4,5},{5,4},{6,7},{7,6},{8,9},{9,8},{10,11... | collective-permute-start | bytes 589832 | tf_op jit(solution)/shard_map/ppermute | solution.py:215
  108.1 5.7 %collective-permute-start.17 = (bf16[32,1536]{1,0:T(8,128)(2,1)S(1)}, bf16[32,1536]{1,0:T(8,128)(2,1)S(1)}, u32[]{:S(2)}, u32[]{:S(2)}) collective-permute-start(bf16[32,1536]{1,0:T(8,128)(2,1)S(1)} %get-tuple-element.31), channel_id=1, source_target_pairs={{0,4},{1,5},{2,6},{3,7},{4,0},{5,1},{6,2},{7,3},{8,12},{9,13},{10,... | collective-permute-start | bytes 294920 | tf_op jit(solution)/shard_map/ppermute | solution.py:226
  109.7 6.2 %collective-permute-start.18 = (bf16[32,1536]{1,0:T(8,128)(2,1)S(1)}, bf16[32,1536]{1,0:T(8,128)(2,1)S(1)}, u32[]{:S(2)}, u32[]{:S(2)}) collective-permute-start(bf16[32,1536]{1,0:T(8,128)(2,1)S(1)} %get-tuple-element.32), channel_id=1, source_target_pairs={{0,6},{1,7},{2,4},{3,5},{4,2},{5,3},{6,0},{7,1},{8,14},{9,15},{10,... | collective-permute-start | bytes 294920 | tf_op jit(solution)/shard_map/ppermute | solution.py:226
  111.5 6.3 %collective-permute-start.14 = (bf16[32,1536]{1,0:T(8,128)(2,1)S(1)}, bf16[32,1536]{1,0:T(8,128)(2,1)S(1)}, u32[]{:S(2)}, u32[]{:S(2)}) collective-permute-start(bf16[32,1536]{1,0:T(8,128)(2,1)S(1)} %fusion.22), channel_id=1, source_target_pairs={{0,2},{1,3},{2,0},{3,1},{4,6},{5,7},{6,4},{7,5},{8,10},{9,11},{10,... | collective-permute-start | bytes 294920 | tf_op jit(solution)/shard_map/ppermute | solution.py:218
  (7 other events, 14.7 us)

commit v3 on v2

v3 whole, which is shorter than its diff:
```python
import functools
import math

import jax
import jax.numpy as jnp
from jax import lax
from jax.experimental import pallas as pl
from jax.experimental.pallas import tpu as pltpu
from jax.sharding import Mesh, PartitionSpec as P

HEAD_DIM = 96
CHUNKS = 4
VMEM_BYTES = 8 * 2**20
GRAD_VMEM_BYTES = 16 * 2**20
PREPARE_VMEM_BYTES = 50 * 2**20
ODD, EVEN, OWN, OTHER, CORE, ROW, HALF = range(7)
NN = (((1,), (0,)), ((), ()))
NT = (((1,), (1,)), ((), ()))
TN = (((0,), (0,)), ((), ()))


def matmul(left_side, right_side, dims):
    return lax.dot_general(left_side, right_side, dims, preferred_element_type=jnp.float32)


def in_vmem():
    return pl.BlockSpec(memory_space=pltpu.VMEM)


def in_smem():
    return pl.BlockSpec(memory_space=pltpu.SMEM)


def in_hbm():
    return pl.BlockSpec(memory_space=pltpu.HBM)


def project_kernel(use_out, micro, index, facts_ref, value_ref, out_ref, tokens_ref, partial_ref):
    version = facts_ref[micro]
    flipped = tokens_ref[index].T

    def rows_of(table_ref):
        partial = matmul(table_ref[0, version], flipped, NN)
        partial_ref[...] = partial.astype(jnp.bfloat16)

    pl.when(facts_ref[use_out] == 1)(lambda: rows_of(out_ref))
    pl.when(facts_ref[use_out] == 0)(lambda: rows_of(value_ref))


def project(use_out, micro, index, facts, w_value, w_out, tokens):
    rows, width = w_value.shape[2:]
    return pl.pallas_call(
        functools.partial(project_kernel, use_out, micro, index),
        out_shape=jax.ShapeDtypeStruct((rows, tokens.shape[1]), jnp.bfloat16),
        in_specs=[in_smem(), in_vmem(), in_vmem(), in_vmem()],
        out_specs=in_vmem(),
        compiler_params=pltpu.CompilerParams(vmem_limit_bytes=VMEM_BYTES),
        cost_estimate=pl.CostEstimate(
            flops=2 * rows * width * tokens.shape[1],
            bytes_accessed=2 * rows * width,
            transcendentals=0,
        ),
        name="project",
    )(facts, w_value, w_out, tokens)


def mix_kernel(
    outer, natural, micro, facts_ref, value_ref, mine_ref, arrived_ref, probs_ref, result_ref, keep_ref, send_ref
):
    version = facts_ref[micro]
    width = value_ref.shape[3]
    step = width // CHUNKS

    def heads(dims):
        for head in range(probs_ref.shape[0]):
            rows = pl.ds(head * HEAD_DIM, HEAD_DIM)
            total = mine_ref[rows, :].astype(jnp.float32) + arrived_ref[rows, :].astype(jnp.float32)
            mixed = matmul(total.astype(jnp.bfloat16), probs_ref[head], dims)
            result_ref[rows, :] = mixed.astype(jnp.bfloat16)

    pl.when(facts_ref[natural] == 1)(lambda: heads(NN))
    pl.when(facts_ref[natural] == 0)(lambda: heads(NT))

    flipped = result_ref[...].T
    second_core = facts_ref[CORE] == 1
    shard = flipped.shape[0] // (2 * outer)
    for chunk in range(CHUNKS):
        columns = pl.ds(chunk * step, step)
        partial = matmul(flipped, value_ref[0, version, :, columns], NN)
        for index in range(outer):
            low = partial[2 * index * shard : (2 * index + 1) * shard]
            high = partial[(2 * index + 1) * shard : (2 * index + 2) * shard]
            keep_ref[index, :, columns] = jnp.where(second_core, high, low).astype(jnp.bfloat16)
            send_ref[index, :, columns] = jnp.where(second_core, low, high).astype(jnp.bfloat16)


def mix(natural, micro, facts, w_value, mine, arrived, probs, outer):
    rows, width = w_value.shape[2:]
    tokens = mine.shape[1]
    half = jax.ShapeDtypeStruct((outer, tokens // (2 * outer), width), jnp.bfloat16)
    return pl.pallas_call(
        functools.partial(mix_kernel, outer, natural, micro),
        out_shape=(jax.ShapeDtypeStruct((rows, tokens), jnp.bfloat16), half, half),
        in_specs=[in_smem(), in_vmem(), in_vmem(), in_vmem(), in_vmem()],
        out_specs=(in_vmem(), in_vmem(), in_vmem()),
        compiler_params=pltpu.CompilerParams(vmem_limit_bytes=VMEM_BYTES),
        cost_estimate=pl.CostEstimate(
            flops=2 * rows * (width + tokens) * tokens,
            bytes_accessed=2 * rows * width,
            transcendentals=0,
        ),
        name="mix",
    )(facts, w_value, mine, arrived, probs)


def combine_kernel(outer, last, facts_ref, keep_ref, arrived_ref, addend_ref, *refs):
    first_refs, sent_refs = refs[:-outer], refs[-outer:]
    for delta in range(outer):
        spot = facts_ref[ROW] ^ delta
        total = keep_ref[spot].astype(jnp.float32) + arrived_ref[spot].astype(jnp.float32)
        if delta == 0:
            total = total + addend_ref[...].astype(jnp.float32)
        total = total.astype(jnp.bfloat16)
        if last:
            total = jnp.where(facts_ref[ODD] == 1, first_refs[delta][...], total)
        sent_refs[delta][...] = total


def combine(facts, keep, arrived, addend, first_sent=()):
    outer, shard, width = keep.shape
    piece = jax.ShapeDtypeStruct((shard, width), jnp.bfloat16)
    return pl.pallas_call(
        functools.partial(combine_kernel, outer, len(first_sent) > 0),
        out_shape=(piece,) * outer,
        in_specs=[in_smem()] + [in_vmem()] * (3 + len(first_sent)),
        out_specs=(in_vmem(),) * outer,
        compiler_params=pltpu.CompilerParams(vmem_limit_bytes=VMEM_BYTES),
        cost_estimate=pl.CostEstimate(
            flops=2 * outer * shard * width,
            bytes_accessed=6 * outer * shard * width,
            transcendentals=0,
        ),
        name="combine",
    )(facts, keep, arrived, addend, *first_sent)


def assemble_kernel(n_own, facts_ref, *refs):
    grad_ref = refs[-1]
    width = refs[0].shape[1]

    def total(parts):
        value = parts[0][...].astype(jnp.float32)
        for part in parts[1:]:
            value = value + part[...].astype(jnp.float32)
        return value.astype(jnp.bfloat16)

    half = facts_ref[HALF]
    own = pl.ds(pl.multiple_of(half * width, width), width)
    other = pl.ds(pl.multiple_of((1 - half) * width, width), width)
    grad_ref[0, :, other] = total(refs[n_own:-1])
    grad_ref[0, :, own] = total(refs[:n_own])


def assemble(facts, own_parts, other_parts):
    shard, width = own_parts[0].shape
    return pl.pallas_call(
        functools.partial(assemble_kernel, len(own_parts)),
        out_shape=jax.ShapeDtypeStruct((1, shard, 2 * width), jnp.bfloat16),
        in_specs=[in_smem()] + [in_vmem()] * (len(own_parts) + len(other_parts)),
        out_specs=in_vmem(),
        compiler_params=pltpu.CompilerParams(vmem_limit_bytes=VMEM_BYTES),
        name="assemble",
    )(facts, *own_parts, *other_parts)


def weight_grad_kernel(facts_ref, a0, a1, b0, b1, first, second0, second1, value_ref, out_ref):
    odd = facts_ref[ODD] == 1
    tokens = a0.shape[1]
    left_first = jnp.concatenate([a0[...], a1[...]], axis=1)
    left_second = jnp.concatenate([b0[...], b1[...]], axis=1)
    right_second = jnp.concatenate([second0[0], second1[0]], axis=0)
    right_first = first[...].reshape(2 * tokens, first.shape[2])
    grad_first = matmul(left_first, right_second, NN)
    grad_second = matmul(left_second, right_first, NN)
    value_ref[0] = jnp.where(odd, grad_first, grad_second).astype(jnp.bfloat16)
    out_ref[0] = jnp.where(odd, grad_second, grad_first).astype(jnp.bfloat16)


def weight_grads(facts, first_results, second_results, first_full, second_full):
    rows, tokens = first_results[0].shape
    width = first_full.shape[2]
    step = rows // CHUNKS
    grad = jax.ShapeDtypeStruct((1, rows, width), jnp.bfloat16)
    left = pl.BlockSpec((step, tokens), lambda i: (i, 0))
    both = pl.BlockSpec((2, tokens, width), lambda i: (0, 0, 0))
    right = pl.BlockSpec((1, tokens, width), lambda i: (0, 0, 0))
    wide = pl.BlockSpec((1, step, width), lambda i: (0, i, 0))
    return pl.pallas_call(
        weight_grad_kernel,
        grid=(CHUNKS,),
        out_shape=(grad, grad),
        in_specs=[in_smem()] + [left] * 4 + [both, right, right],
        out_specs=(wide, wide),
        compiler_params=pltpu.CompilerParams(vmem_limit_bytes=GRAD_VMEM_BYTES),
        cost_estimate=pl.CostEstimate(
            flops=8 * rows * width * tokens, bytes_accessed=4 * rows * width, transcendentals=0
        ),
        name="weight_grads",
    )(facts, *first_results, *second_results, first_full, *second_full)


def prepare_kernel(query_ref, key_ref, value_ref, out_ref, probs_ref, value_held, out_held, sems):
    copies = [
        pltpu.make_async_copy(value_ref, value_held, sems.at[0]),
        pltpu.make_async_copy(out_ref, out_held, sems.at[1]),
    ]
    for copy in copies:
        copy.start()
    tokens = query_ref.shape[2]
    causal = lax.broadcasted_iota(jnp.int32, (tokens, tokens), 1) <= lax.broadcasted_iota(
        jnp.int32, (tokens, tokens), 0
    )
    for head in range(probs_ref.shape[0]):
        rows = pl.ds(head * HEAD_DIM, HEAD_DIM)
        scores = matmul(query_ref[0, rows, :], key_ref[0, rows, :], TN)
        scores = jnp.where(causal, scores * (1.0 / math.sqrt(HEAD_DIM)), -jnp.inf)
        expo = jnp.exp(scores - jnp.max(scores, axis=1, keepdims=True))
        probs_ref[head] = (expo / jnp.sum(expo, axis=1, keepdims=True)).astype(jnp.bfloat16)
    for copy in copies:
        copy.wait()


def prepare(query, key_stash, w_value, w_out):
    rows, tokens = query.shape[1:]
    heads = rows // HEAD_DIM
    table = jax.ShapeDtypeStruct(w_value.shape, jnp.bfloat16)
    return pl.pallas_call(
        prepare_kernel,
        out_shape=(jax.ShapeDtypeStruct((heads, tokens, tokens), jnp.bfloat16), table, table),
        in_specs=[in_vmem(), in_vmem(), in_hbm(), in_hbm()],
        out_specs=(in_vmem(), in_vmem(), in_vmem()),
        scratch_shapes=[pltpu.SemaphoreType.DMA((2,))],
        compiler_params=pltpu.CompilerParams(vmem_limit_bytes=PREPARE_VMEM_BYTES),
        cost_estimate=pl.CostEstimate(
            flops=2 * rows * tokens * tokens,
            bytes_accessed=4 * w_value.size,
            transcendentals=heads * tokens * tokens,
        ),
        name="prepare",
    )(query, key_stash, w_value, w_out)


def on_device(section_input, query, key_stash, incoming, version, w_value, w_out):
    half = lax.axis_index("half")
    odd_flag = lax.axis_index("pair") % 2
    odd = odd_flag == 1
    place = lax.axis_index("tensor")
    core, row = place % 2, place // 2
    n_pairs = lax.axis_size("pair")
    n_tensor = lax.axis_size("tensor")
    outer = n_tensor // 2
    width = w_value.shape[3]
    shard = section_input.shape[1]

    def swap_half(array):
        return lax.ppermute(array, "half", [(0, 1), (1, 0)])

    def swap_core(array):
        return lax.ppermute(array, "tensor", [(i, i ^ 1) for i in range(n_tensor)])

    def to_row(array, delta):
        return lax.ppermute(array, "tensor", [(i, i ^ (2 * delta)) for i in range(n_tensor)])

    def to_other_half(array, delta):
        pairs = [
            (h * n_tensor + i, (1 - h) * n_tensor + (i ^ (2 * delta)))
            for h in range(2)
            for i in range(n_tensor)
        ]
        return lax.ppermute(array, ("half", "tensor"), pairs)

    def to_section_below(array, delta):
        pairs = [
            (p * n_tensor + i, (p - 1) * n_tensor + (i ^ (2 * delta)))
            for p in range(1, n_pairs, 2)
            for i in range(n_tensor)
        ]
        return lax.ppermute(array, ("pair", "tensor"), pairs)

    def own_columns(array):
        return lax.dynamic_slice_in_dim(array, half * width, width, 1)

    def other_columns(array):
        return lax.dynamic_slice_in_dim(array, (1 - half) * width, width, 1)

    def gathered(pieces):
        return lax.all_gather(jnp.stack(pieces), "tensor", axis=1, tiled=True)

    micros = (OWN, OTHER)
    first = jnp.where(odd, incoming[0], section_input[0])
    first_piece = [own_columns(first), swap_half(other_columns(first))]
    other_version = swap_half(version)[0]
    facts = jnp.stack([odd_flag, 1 - odd_flag, version[0], other_version, core, row, half])
    own_probs, w_value, w_out = prepare(query, key_stash, w_value, w_out)
    probs = [own_probs, swap_half(own_probs)]

    first_full = gathered(first_piece)
    partial = [None, None]
    for m in (1, 0):
        partial[m] = project(ODD, micros[m], m, facts, w_value, w_out, first_full)
    arrived = [swap_half(partial[1]), swap_half(partial[0])]
    later_input, _ = lax.optimization_barrier((section_input[0], partial[0]))
    input_piece = [own_columns(later_input), swap_half(other_columns(later_input))]
    first_result, first_sent = [None, None], [None, None]
    second_piece, second_full = [None, None], [None, None]
    for m in range(2):
        first_result[m], keep, send = mix(
            ODD, micros[m], facts, w_value, partial[m], arrived[m], probs[m], outer
        )
        first_sent[m] = combine(facts, keep, swap_core(send), first_piece[m])
        received = [to_section_below(part, d) for d, part in enumerate(first_sent[m])]
        total = sum(part.astype(jnp.float32) for part in received).astype(jnp.bfloat16)
        second_piece[m] = jnp.where(odd, input_piece[m], total)
    for m in range(2):
        second_full[m] = gathered([second_piece[m]])
        partial[m] = project(EVEN, micros[m], 0, facts, w_value, w_out, second_full[m])
    arrived = [swap_half(partial[1]), swap_half(partial[0])]
    second_result, last_sent = [None, None], [None, None]
    for m in (1, 0):
        second_result[m], keep, send = mix(
            EVEN, micros[m], facts, w_value, partial[m], arrived[m], probs[m], outer
        )
        last_sent[m] = combine(facts, keep, swap_core(send), second_piece[m], first_sent[m])
    other_parts = [to_other_half(part, d) for d, part in enumerate(last_sent[1])]
    own_parts = [last_sent[0][0]] + [to_row(part, d + 1) for d, part in enumerate(last_sent[0][1:])]
    second_result, _ = lax.optimization_barrier((second_result, last_sent))
    grad_value, grad_out = weight_grads(
        facts, first_result, second_result, first_full, second_full
    )
    own_parts, other_parts, _ = lax.optimization_barrier((own_parts, other_parts, grad_value))
    input_grad = assemble(facts, own_parts, other_parts)
    return (input_grad, grad_value, grad_out)


def solution(mesh):
    sections, tensor = mesh.devices.shape
    split = Mesh(mesh.devices.reshape(sections // 2, 2, tensor), ("pair", "half", "tensor"))
    slots = ("pair", "half")
    by_tokens = P(slots, "tensor", None)
    by_rows = P(slots, None, "tensor", None)
    return jax.shard_map(
        on_device,
        mesh=split,
        in_specs=(by_tokens, by_tokens, by_tokens, by_tokens, P(slots), by_rows, by_rows),
        out_specs=(by_tokens, by_tokens, by_tokens),
        check_vma=False,
    )
```

time: 119 us -> 98 us (0.82)
  local copies, waits for them, and re-layouts: 20.4 us -> 7.26 us
  other arithmetic: 8.81 us -> 1.15 us
  waiting for transfers between devices: 16.2 us -> 19.8 us
  blocking collectives: 25.1 us -> 22 us
  matrix products: 2.07 us -> 0 us
  Pallas kernels: 25 us -> 26.3 us
    unnamed x40 -> x18, local copies, waits for them, and re-layouts: 17.1 us -> 6.54 us
    ppermute x8, waiting for transfers between devices: 6.29 us -> 14.6 us  [swap_half(): return lax.ppermute(array, 'half', [(0, 1), (1, 0)])]
    all_gather x4 -> x3, blocking collectives: 25.1 us -> 22 us  [gathered(): return lax.all_gather(jnp.stack(pieces), 'tensor', axis=1, tiled=True)]
    ppermute x2, waiting for transfers between devices: 3.09 us -> 0.01 us  [to_other_half(): return lax.ppermute(array, ('half', 'tensor'), pairs)]
    another operation x8 -> x1, other arithmetic: 3.08 us -> 0.02 us  [gathered(): return lax.all_gather(jnp.stack(pieces), 'tensor', axis=1, tiled=True)]
    select_n x5 -> x1, other arithmetic: 2.77 us -> 0.04 us  [on_device(): second_piece[m] = jnp.where(odd, input_piece[m], total)]
    div x2 -> x0, matrix products: 2.07 us -> none  [attention_probs(): return (expo / jnp.sum(expo, axis=2, keepdims=True)).astype(jnp.bfloat16)]
    slice x1 -> x0, local copies, waits for them, and re-layouts: 1.73 us -> none  [on_device(): stash_other[1]]
  transfers between devices with their start and end apart: 19 -> 19, of which waited for: 7 -> 7; matrix products, arithmetic and copies ran while one was open for 11% -> 1% of each run, Pallas kernels for 21% -> 24%
where the time goes in v3:
time: 98 us; the launch traced here: 97.6 us
  Pallas kernels  26.3 us (27%)
  blocking collectives  22 us (22%)
  waiting for transfers between devices  19.8 us (20%)
  starting transfers between devices  19.6 us (20%)
  local copies, waits for them, and re-layouts  7.26 us (7%)
  between operations  1.6 us (2%)
  other arithmetic  1.15 us (1%)
    all_gather x3, blocking collectives, gathered(): return lax.all_gather(jnp.stack(pieces), 'tensor', axis=1, tiled=True)  22 us
    ppermute x8, waiting for transfers between devices, swap_half(): return lax.ppermute(array, 'half', [(0, 1), (1, 0)])  14.6 us
    ppermute x8, starting transfers between devices, swap_half(): return lax.ppermute(array, 'half', [(0, 1), (1, 0)])  10.4 us
    pallas_call x1, Pallas kernels, prepare(): pl.pallas_call(prepare_kernel, out_shape=(jax.ShapeDtypeStruct((heads, to...  7.47 us
    unnamed x18, local copies, waits for them, and re-layouts  6.54 us
    pallas_call x4, Pallas kernels, mix(): pl.pallas_call(functools.partial(mix_kernel, outer, natural, micro), out_...  5.7 us
    pallas_call x4, Pallas kernels, project(): pl.pallas_call(functools.partial(project_kernel, use_out, micro, index),...  5.34 us
    ppermute x4, starting transfers between devices, to_section_below(): return lax.ppermute(array, ('pair', 'tensor'), pairs)  5.17 us
  transfers between devices with their start and end apart: 19, of which 7 were waited for; matrix products, arithmetic and copies ran while one was open for 1% of the time, Pallas kernels for 24%

profile of v3, /device:TPU:0, one launch (start us, length us, event | category | flops | bytes accessed | tf_op | source)
XLA Modules:
  0.0 97.6 jit_solution(2678026307060666263)
XLA Ops:
  1.7 3.0 %collective-permute-start.1 = (bf16[32,1536]{1,0:T(8,128)(2,1)S(1)}, bf16[32,1536]{1,0:T(8,128)(2,1)S(1)}, u32[]{:S(2)}, u32[]{:S(2)}) collective-permute-start(bf16[32,1536]{1,0:T(8,128)(2,1)S(1)} %get-tuple-element.70), channel_id=1, source_target_pairs={{0,4},{4,0},{1,5},{5,1},{2,6},{6,2},{3,7},{7,3},{8,12},{12,8},{9,1... | collective-permute-start | bytes 294920 | tf_op jit(solution)/shard_map/ppermute | solution.py:266
  7.4 7.5 %prepare.1 = (bf16[8,128,128]{2,1,0:T(8,128)(2,1)S(1)}, bf16[1,2,768,1536]{3,2,1,0:T(8,128)(2,1)}, bf16[1,2,768,1536]{3,2,1,0:T(8,128)(2,1)}) custom-call(bf16[1,768,128]{2,1,0:T(8,128)(2,1)S(1)} %copy-done.2, bf16[1,768,128]{2,1,0:T(8,128)(2,1)S(1)} %copy-done.3, bf16[1,2,768,1536]{3,2,1,0:T(8,128)(2,1)} %value_ref.1, bf16[1,2,768,1536]{3,2,1,0:T(8,128)(2,1)} %out_ref.1), custom_call_target="tpu_custom_call" | custom-call | flops 25165824 | bytes 9437184 | tf_op jit(solution)/shard_map/prepare/pallas_call | solution.py:237
  15.6 9.1 %all_gather.9.tokens_ref.first = bf16[2,128,1536]{2,1,0:T(8,128)(2,1)S(1)} all-gather(bf16[2,32,1536]{2,1,0:T(8,128)(2,1)S(1)} %pad_maximum_fusion), channel_id=1, replica_groups=mesh['pair'=4,'half'=2,'tensor'=4] {'tensor'}, dimensions={1}, use_global_device_ids=true | all-gather | bytes 983040 | tf_op jit(solution)/shard_map/all_gather | solution.py:297
  24.7 2.3 %copy-done = bf16[1,2,768,1536]{3,2,1,0:T(8,128)(2,1)S(1)} copy-done((bf16[1,2,768,1536]{3,2,1,0:T(8,128)(2,1)S(1)}, bf16[1,2,768,1536]{3,2,1,0:T(8,128)(2,1)}, u32[]{:S(2)}) %copy-start) | copy-done | bytes 4718616
  27.0 2.3 %copy-done.1 = bf16[1,2,768,1536]{3,2,1,0:T(8,128)(2,1)S(1)} copy-done((bf16[1,2,768,1536]{3,2,1,0:T(8,128)(2,1)S(1)}, bf16[1,2,768,1536]{3,2,1,0:T(8,128)(2,1)}, u32[]{:S(2)}) %copy-start.1) | copy-done | bytes 4718616
  29.3 1.3 %project.5.mine_ref = bf16[768,128]{1,0:T(8,128)(2,1)S(1)} custom-call(s32[7]{0:T(128)S(1)} %stack.38.facts_ref, bf16[1,2,768,1536]{3,2,1,0:T(8,128)(2,1)S(1)} %copy-done, bf16[1,2,768,1536]{3,2,1,0:T(8,128)(2,1)S(1)} %copy-done.1, bf16[2,128,1536]{2,1,0:T(8,128)(2,1)S(1)} %all_gather.9.tokens_ref.first), custom_call_target="tpu_custom_call" | custom-call | flops 301989888 | bytes 2359296 | tf_op jit(solution)/shard_map/project/pallas_call | solution.py:52
  30.7 1.6 %collective-permute-start.2 = (bf16[768,128]{1,0:T(8,128)(2,1)S(1)}, bf16[768,128]{1,0:T(8,128)(2,1)S(1)}, u32[]{:S(2)}, u32[]{:S(2)}) collective-permute-start(bf16[768,128]{1,0:T(8,128)(2,1)S(1)} %project.5.mine_ref), channel_id=1, source_target_pairs={{0,4},{4,0},{1,5},{5,1},{2,6},{6,2},{3,7},{7,3},{8,12},{12,8},{9,1... | collective-permute-start | bytes 589832 | tf_op jit(solution)/shard_map/ppermute | solution.py:266
  32.8 1.3 %project.4.mine_ref = bf16[768,128]{1,0:T(8,128)(2,1)S(1)} custom-call(s32[7]{0:T(128)S(1)} %stack.38.facts_ref, bf16[1,2,768,1536]{3,2,1,0:T(8,128)(2,1)S(1)} %copy-done, bf16[1,2,768,1536]{3,2,1,0:T(8,128)(2,1)S(1)} %copy-done.1, bf16[2,128,1536]{2,1,0:T(8,128)(2,1)S(1)} %all_gather.9.tokens_ref.first), custom_call_target="tpu_custom_call" | custom-call | flops 301989888 | bytes 2359296 | tf_op jit(solution)/shard_map/project/pallas_call | solution.py:52
  34.1 1.5 %collective-permute-start.7 = (bf16[768,128]{1,0:T(8,128)(2,1)S(1)}, bf16[768,128]{1,0:T(8,128)(2,1)S(1)}, u32[]{:S(2)}, u32[]{:S(2)}) collective-permute-start(bf16[768,128]{1,0:T(8,128)(2,1)S(1)} %project.4.mine_ref), channel_id=1, source_target_pairs={{0,4},{4,0},{1,5},{5,1},{2,6},{6,2},{3,7},{7,3},{8,12},{12,8},{9,1... | collective-permute-start | bytes 589832 | tf_op jit(solution)/shard_map/ppermute | solution.py:266
  35.7 2.8 %collective-permute-done.2.arrived_ref = bf16[768,128]{1,0:T(8,128)(2,1)S(1)} collective-permute-done((bf16[768,128]{1,0:T(8,128)(2,1)S(1)}, bf16[768,128]{1,0:T(8,128)(2,1)S(1)}, u32[]{:S(2)}, u32[]{:S(2)}) %collective-permute-start.2) | collective-permute-done | bytes 196640 | tf_op jit(solution)/shard_map/ppermute | solution.py:266
  38.5 1.5 %mix.4 = (bf16[768,128]{1,0:T(8,128)(2,1)S(1)}, bf16[2,32,1536]{2,1,0:T(8,128)(2,1)S(1)}, bf16[2,32,1536]{2,1,0:T(8,128)(2,1)S(1)}) custom-call(s32[7]{0:T(128)S(1)} %stack.38.facts_ref, bf16[1,2,768,1536]{3,2,1,0:T(8,128)(2,1)S(1)} %bitcast.14, bf16[768,128]{1,0:T(8,128)(2,1)S(1)} %project.4.mine_ref, ...), custom_call_target="tpu_custom_call" | custom-call | flops 327155712 | bytes 2359296 | tf_op jit(solution)/shard_map/mix/pallas_call | solution.py:101
  40.0 4.1 %collective-permute-done.8.probs_ref = bf16[8,128,128]{2,1,0:T(8,128)(2,1)S(1)} collective-permute-done((bf16[8,128,128]{2,1,0:T(8,128)(2,1)S(1)}, bf16[8,128,128]{2,1,0:T(8,128)(2,1)S(1)}, u32[]{:S(2)}, u32[]{:S(2)}) %collective-permute-start.8) | collective-permute-done | bytes 262176 | tf_op jit(solution)/shard_map/ppermute | solution.py:266
  44.1 3.6 %collective-permute-done.7.arrived_ref = bf16[768,128]{1,0:T(8,128)(2,1)S(1)} collective-permute-done((bf16[768,128]{1,0:T(8,128)(2,1)S(1)}, bf16[768,128]{1,0:T(8,128)(2,1)S(1)}, u32[]{:S(2)}, u32[]{:S(2)}) %collective-permute-start.7) | collective-permute-done | bytes 196640 | tf_op jit(solution)/shard_map/ppermute | solution.py:266
  47.7 1.5 %mix.5 = (bf16[768,128]{1,0:T(8,128)(2,1)S(1)}, bf16[2,32,1536]{2,1,0:T(8,128)(2,1)S(1)}, bf16[2,32,1536]{2,1,0:T(8,128)(2,1)S(1)}) custom-call(s32[7]{0:T(128)S(1)} %stack.38.facts_ref, bf16[1,2,768,1536]{3,2,1,0:T(8,128)(2,1)S(1)} %bitcast.14, bf16[768,128]{1,0:T(8,128)(2,1)S(1)} %project.5.mine_ref, ...), custom_call_target="tpu_custom_call" | custom-call | flops 327155712 | bytes 2359296 | tf_op jit(solution)/shard_map/mix/pallas_call | solution.py:101
  49.9 1.3 %collective-permute-start.4 = (bf16[32,1536]{1,0:T(8,128)(2,1)S(1)}, bf16[32,1536]{1,0:T(8,128)(2,1)S(1)}, u32[]{:S(2)}, u32[]{:S(2)}) collective-permute-start(bf16[32,1536]{1,0:T(8,128)(2,1)S(1)} %get-tuple-element.41.refs_0_), channel_id=1, source_target_pairs={{8,0},{9,1},{10,2},{11,3},{24,16},{25,17},{26,18},{27,19},{12,4},{... | collective-permute-start | bytes 294920 | tf_op jit(solution)/shard_map/ppermute | solution.py:288
  51.2 1.3 %collective-permute-start.5 = (bf16[32,1536]{1,0:T(8,128)(2,1)S(1)}, bf16[32,1536]{1,0:T(8,128)(2,1)S(1)}, u32[]{:S(2)}, u32[]{:S(2)}) collective-permute-start(bf16[32,1536]{1,0:T(8,128)(2,1)S(1)} %get-tuple-element.42.refs_1_), channel_id=1, source_target_pairs={{8,2},{9,3},{10,0},{11,1},{24,18},{25,19},{26,16},{27,17},{12,6},{... | collective-permute-start | bytes 294920 | tf_op jit(solution)/shard_map/ppermute | solution.py:288
  53.1 1.3 %collective-permute-start.10 = (bf16[32,1536]{1,0:T(8,128)(2,1)S(1)}, bf16[32,1536]{1,0:T(8,128)(2,1)S(1)}, u32[]{:S(2)}, u32[]{:S(2)}) collective-permute-start(bf16[32,1536]{1,0:T(8,128)(2,1)S(1)} %get-tuple-element.45.refs_0_), channel_id=1, source_target_pairs={{8,0},{9,1},{10,2},{11,3},{24,16},{25,17},{26,18},{27,19},{12,4},{... | collective-permute-start | bytes 294920 | tf_op jit(solution)/shard_map/ppermute | solution.py:288
  54.4 1.3 %collective-permute-start.11 = (bf16[32,1536]{1,0:T(8,128)(2,1)S(1)}, bf16[32,1536]{1,0:T(8,128)(2,1)S(1)}, u32[]{:S(2)}, u32[]{:S(2)}) collective-permute-start(bf16[32,1536]{1,0:T(8,128)(2,1)S(1)} %get-tuple-element.46.refs_1_), channel_id=1, source_target_pairs={{8,2},{9,3},{10,0},{11,1},{24,18},{25,19},{26,16},{27,17},{12,6},{... | collective-permute-start | bytes 294920 | tf_op jit(solution)/shard_map/ppermute | solution.py:288
  55.7 1.7 %collective-permute-done.4 = bf16[32,1536]{1,0:T(8,128)(2,1)S(1)} collective-permute-done((bf16[32,1536]{1,0:T(8,128)(2,1)S(1)}, bf16[32,1536]{1,0:T(8,128)(2,1)S(1)}, u32[]{:S(2)}, u32[]{:S(2)}) %collective-permute-start.4) | collective-permute-done | bytes 98336 | tf_op jit(solution)/shard_map/ppermute | solution.py:288
  57.4 1.9 %collective-permute-done.5 = bf16[32,1536]{1,0:T(8,128)(2,1)S(1)} collective-permute-done((bf16[32,1536]{1,0:T(8,128)(2,1)S(1)}, bf16[32,1536]{1,0:T(8,128)(2,1)S(1)}, u32[]{:S(2)}, u32[]{:S(2)}) %collective-permute-start.5) | collective-permute-done | bytes 98336 | tf_op jit(solution)/shard_map/ppermute | solution.py:288
  59.4 1.6 %collective-permute-start.6 = (bf16[32,1536]{1,0:T(8,128)(2,1)S(1)}, bf16[32,1536]{1,0:T(8,128)(2,1)S(1)}, u32[]{:S(2)}, u32[]{:S(2)}) collective-permute-start(bf16[32,1536]{1,0:T(8,128)(2,1)S(1)} %get-tuple-element.67), channel_id=1, source_target_pairs={{0,4},{4,0},{1,5},{5,1},{2,6},{6,2},{3,7},{7,3},{8,12},{12,8},{9,1... | collective-permute-start | bytes 294920 | tf_op jit(solution)/shard_map/ppermute | solution.py:266
  60.9 6.6 %all-gather = bf16[128,1536]{1,0:T(8,128)(2,1)S(1)} all-gather(bf16[32,1536]{1,0:T(8,128)(2,1)S(1)} %get-tuple-element.68.addend_ref), channel_id=2, replica_groups=mesh['pair'=4,'half'=2,'tensor'=4] {'tensor'}, dimensions={0}, use_global_device_ids=true | all-gather | bytes 491520 | tf_op jit(solution)/shard_map/all_gather | solution.py:297
  67.5 1.3 %project.6.mine_ref = bf16[768,128]{1,0:T(8,128)(2,1)S(1)} custom-call(s32[7]{0:T(128)S(1)} %stack.38.facts_ref, bf16[1,2,768,1536]{3,2,1,0:T(8,128)(2,1)S(1)} %bitcast.14, bf16[1,2,768,1536]{3,2,1,0:T(8,128)(2,1)S(1)} %bitcast.16, bf16[1,128,1536]{2,1,0:T(8,128)(2,1)S(1)} %bitcast.17), custom_call_target="tpu_custom_call" | custom-call | flops 301989888 | bytes 2359296 | tf_op jit(solution)/shard_map/project/pallas_call | solution.py:52
  69.5 6.3 %all-gather.1 = bf16[128,1536]{1,0:T(8,128)(2,1)S(1)} all-gather(bf16[32,1536]{1,0:T(8,128)(2,1)S(1)} %fusion.1.addend_ref), channel_id=3, replica_groups=mesh['pair'=4,'half'=2,'tensor'=4] {'tensor'}, dimensions={0}, use_global_device_ids=true | all-gather | bytes 491520 | tf_op jit(solution)/shard_map/all_gather | solution.py:297
  75.8 1.3 %project.7.mine_ref = bf16[768,128]{1,0:T(8,128)(2,1)S(1)} custom-call(s32[7]{0:T(128)S(1)} %stack.38.facts_ref, bf16[1,2,768,1536]{3,2,1,0:T(8,128)(2,1)S(1)} %bitcast.14, bf16[1,2,768,1536]{3,2,1,0:T(8,128)(2,1)S(1)} %bitcast.16, bf16[1,128,1536]{2,1,0:T(8,128)(2,1)S(1)} %bitcast.19), custom_call_target="tpu_custom_call" | custom-call | flops 301989888 | bytes 2359296 | tf_op jit(solution)/shard_map/project/pallas_call | solution.py:52
  77.2 1.5 %collective-permute-start.12 = (bf16[768,128]{1,0:T(8,128)(2,1)S(1)}, bf16[768,128]{1,0:T(8,128)(2,1)S(1)}, u32[]{:S(2)}, u32[]{:S(2)}) collective-permute-start(bf16[768,128]{1,0:T(8,128)(2,1)S(1)} %project.7.mine_ref), channel_id=1, source_target_pairs={{0,4},{4,0},{1,5},{5,1},{2,6},{6,2},{3,7},{7,3},{8,12},{12,8},{9,1... | collective-permute-start | bytes 589832 | tf_op jit(solution)/shard_map/ppermute | solution.py:266
  78.7 1.4 %mix.7 = (bf16[768,128]{1,0:T(8,128)(2,1)S(1)}, bf16[2,32,1536]{2,1,0:T(8,128)(2,1)S(1)}, bf16[2,32,1536]{2,1,0:T(8,128)(2,1)S(1)}) custom-call(s32[7]{0:T(128)S(1)} %stack.38.facts_ref, bf16[1,2,768,1536]{3,2,1,0:T(8,128)(2,1)S(1)} %bitcast.14, bf16[768,128]{1,0:T(8,128)(2,1)S(1)} %project.7.mine_ref, ...), custom_call_target="tpu_custom_call" | custom-call | flops 327155712 | bytes 2359296 | tf_op jit(solution)/shard_map/mix/pallas_call | solution.py:101
  80.2 4.1 %collective-permute-done.12.arrived_ref = bf16[768,128]{1,0:T(8,128)(2,1)S(1)} collective-permute-done((bf16[768,128]{1,0:T(8,128)(2,1)S(1)}, bf16[768,128]{1,0:T(8,128)(2,1)S(1)}, u32[]{:S(2)}, u32[]{:S(2)}) %collective-permute-start.12) | collective-permute-done | bytes 196640 | tf_op jit(solution)/shard_map/ppermute | solution.py:266
  84.4 1.4 %mix.6 = (bf16[768,128]{1,0:T(8,128)(2,1)S(1)}, bf16[2,32,1536]{2,1,0:T(8,128)(2,1)S(1)}, bf16[2,32,1536]{2,1,0:T(8,128)(2,1)S(1)}) custom-call(s32[7]{0:T(128)S(1)} %stack.38.facts_ref, bf16[1,2,768,1536]{3,2,1,0:T(8,128)(2,1)S(1)} %bitcast.14, bf16[768,128]{1,0:T(8,128)(2,1)S(1)} %project.6.mine_ref, ...), custom_call_target="tpu_custom_call" | custom-call | flops 327155712 | bytes 2359296 | tf_op jit(solution)/shard_map/mix/pallas_call | solution.py:101
  86.5 1.5 %collective-permute-start.17 = (bf16[32,1536]{1,0:T(8,128)(2,1)S(1)}, bf16[32,1536]{1,0:T(8,128)(2,1)S(1)}, u32[]{:S(2)}, u32[]{:S(2)}) collective-permute-start(bf16[32,1536]{1,0:T(8,128)(2,1)S(1)} %get-tuple-element.53), channel_id=1, source_target_pairs={{0,4},{1,5},{2,6},{3,7},{4,0},{5,1},{6,2},{7,3},{8,12},{9,13},{10,... | collective-permute-start | bytes 294920 | tf_op jit(solution)/shard_map/ppermute | solution.py:280
  90.7 4.1 %weight_grads.1 = (bf16[1,768,1536]{2,1,0:T(8,128)(2,1)}, bf16[1,768,1536]{2,1,0:T(8,128)(2,1)}) custom-call(s32[7]{0:T(128)S(1)} %stack.38.facts_ref, bf16[768,128]{1,0:T(8,128)(2,1)S(1)} %get-tuple-element.55.a0, bf16[768,128]{1,0:T(8,128)(2,1)S(1)} %get-tuple-element.56.a1, bf16[768,128]{1,0:T(8,128)(2,1)S(1)} %get-tuple-element.59.b0, ...), custom_call_target="tpu_custom_call" | custom-call | flops 1207959552 | bytes 4718592 | tf_op jit(solution)/shard_map/weight_grads/pallas_call | solution.py:198
  94.8 1.6 %collective-permute-done.14.refs_1_ = bf16[32,1536]{1,0:T(8,128)(2,1)S(1)} collective-permute-done((bf16[32,1536]{1,0:T(8,128)(2,1)S(1)}, bf16[32,1536]{1,0:T(8,128)(2,1)S(1)}, u32[]{:S(2)}, u32[]{:S(2)}) %collective-permute-start.14) | collective-permute-done | bytes 98336 | tf_op jit(solution)/shard_map/ppermute | solution.py:272
  (50 shorter events, 11.1 us)
Async XLA Ops:
  1.7 13.8 %collective-permute-start.1 = (bf16[32,1536]{1,0:T(8,128)(2,1)S(1)}, bf16[32,1536]{1,0:T(8,128)(2,1)S(1)}, u32[]{:S(2)}, u32[]{:S(2)}) collective-permute-start(bf16[32,1536]{1,0:T(8,128)(2,1)S(1)} %get-tuple-element.70), channel_id=1, source_target_pairs={{0,4},{4,0},{1,5},{5,1},{2,6},{6,2},{3,7},{7,3},{8,12},{12,8},{9,1... | collective-permute-start | bytes 294920 | tf_op jit(solution)/shard_map/ppermute | solution.py:266
  4.7 10.1 %collective-permute-start = (s32[1]{0:T(128)}, s32[1]{0:T(128)}, u32[]{:S(2)}, u32[]{:S(2)}) collective-permute-start(s32[1]{0:T(128)} %param.11), channel_id=1, source_target_pairs={{0,4},{4,0},{1,5},{5,1},{2,6},{6,2},{3,7},{7,3},{8,12},{12,8},{9,1... | collective-permute-start | bytes 20 | tf_op jit(solution)/shard_map/ppermute | solution.py:266
  5.5 0.9 copy-start.2
  6.4 0.9 copy-start.3
  24.7 2.3 %copy-start = (bf16[1,2,768,1536]{3,2,1,0:T(8,128)(2,1)S(1)}, bf16[1,2,768,1536]{3,2,1,0:T(8,128)(2,1)}, u32[]{:S(2)}) copy-start(bf16[1,2,768,1536]{3,2,1,0:T(8,128)(2,1)} %get-tuple-element.35.value_ref) | copy-start | bytes 14155780
  27.0 2.3 %copy-start.1 = (bf16[1,2,768,1536]{3,2,1,0:T(8,128)(2,1)S(1)}, bf16[1,2,768,1536]{3,2,1,0:T(8,128)(2,1)}, u32[]{:S(2)}) copy-start(bf16[1,2,768,1536]{3,2,1,0:T(8,128)(2,1)} %get-tuple-element.36.out_ref) | copy-start | bytes 14155780
  30.7 7.8 %collective-permute-start.2 = (bf16[768,128]{1,0:T(8,128)(2,1)S(1)}, bf16[768,128]{1,0:T(8,128)(2,1)S(1)}, u32[]{:S(2)}, u32[]{:S(2)}) collective-permute-start(bf16[768,128]{1,0:T(8,128)(2,1)S(1)} %project.5.mine_ref), channel_id=1, source_target_pairs={{0,4},{4,0},{1,5},{5,1},{2,6},{6,2},{3,7},{7,3},{8,12},{12,8},{9,1... | collective-permute-start | bytes 589832 | tf_op jit(solution)/shard_map/ppermute | solution.py:266
  32.2 6.2 %slice-start = ((s8[4718592]{0:T(1024)(128)(4,1)}), s8[4194304]{0:T(1024)(128)(4,1)S(1)}, s32[]{:S(2)}) async-start(s8[4718592]{0:T(1024)(128)(4,1)} %bitcast.13), calls=%async_computation | async-start | bytes 8388608
  32.2 6.2 %slice-start.1 = ((s8[4718592]{0:T(1024)(128)(4,1)}), s8[524288]{0:T(1024)(128)(4,1)S(1)}, s32[]{:S(2)}) async-start(s8[4718592]{0:T(1024)(128)(4,1)} %bitcast.13), calls=%async_computation.1 | async-start | bytes 1048576
  32.2 11.8 %collective-permute-start.8 = (bf16[8,128,128]{2,1,0:T(8,128)(2,1)S(1)}, bf16[8,128,128]{2,1,0:T(8,128)(2,1)S(1)}, u32[]{:S(2)}, u32[]{:S(2)}) collective-permute-start(bf16[8,128,128]{2,1,0:T(8,128)(2,1)S(1)} %get-tuple-element.38.probs_ref), channel_id=1, source_target_pairs={{0,4},{4,0},{1,5},{5,1},{2,6},{6,2},{3,7},{7,3},{8,12},{12,8},{9,1... | collective-permute-start | bytes 786440 | tf_op jit(solution)/shard_map/ppermute | solution.py:266
  32.8 34.7 %slice-start.2 = ((s8[4718592]{0:T(1024)(128)(4,1)}), s8[4194304]{0:T(1024)(128)(4,1)S(1)}, s32[]{:S(2)}) async-start(s8[4718592]{0:T(1024)(128)(4,1)} %bitcast.15), calls=%async_computation.2 | async-start | bytes 8388608
  34.1 25.2 %copy-start.4 = (bf16[1,32,3072]{2,1,0:T(8,128)(2,1)S(1)}, bf16[1,32,3072]{2,1,0:T(8,128)(2,1)}, u32[]{:S(2)}) copy-start(bf16[1,32,3072]{2,1,0:T(8,128)(2,1)} %param.7) | copy-start | bytes 589828
  34.1 33.4 %slice-start.3 = ((s8[4718592]{0:T(1024)(128)(4,1)}), s8[524288]{0:T(1024)(128)(4,1)S(1)}, s32[]{:S(2)}) async-start(s8[4718592]{0:T(1024)(128)(4,1)} %bitcast.15), calls=%async_computation.3 | async-start | bytes 1048576
  34.1 13.6 %collective-permute-start.7 = (bf16[768,128]{1,0:T(8,128)(2,1)S(1)}, bf16[768,128]{1,0:T(8,128)(2,1)S(1)}, u32[]{:S(2)}, u32[]{:S(2)}) collective-permute-start(bf16[768,128]{1,0:T(8,128)(2,1)S(1)} %project.4.mine_ref), channel_id=1, source_target_pairs={{0,4},{4,0},{1,5},{5,1},{2,6},{6,2},{3,7},{7,3},{8,12},{12,8},{9,1... | collective-permute-start | bytes 589832 | tf_op jit(solution)/shard_map/ppermute | solution.py:266
  39.9 9.3 %collective-permute-start.3 = (bf16[2,32,1536]{2,1,0:T(8,128)(2,1)S(1)}, bf16[2,32,1536]{2,1,0:T(8,128)(2,1)S(1)}, u32[]{:S(2)}, u32[]{:S(2)}) collective-permute-start(bf16[2,32,1536]{2,1,0:T(8,128)(2,1)S(1)} %get-tuple-element.40), channel_id=1, source_target_pairs={{0,1},{1,0},{2,3},{3,2},{4,5},{5,4},{6,7},{7,6},{8,9},{9,8},{10,11... | collective-permute-start | bytes 589832 | tf_op jit(solution)/shard_map/ppermute | solution.py:269
  49.2 3.3 %collective-permute-start.9 = (bf16[2,32,1536]{2,1,0:T(8,128)(2,1)S(1)}, bf16[2,32,1536]{2,1,0:T(8,128)(2,1)S(1)}, u32[]{:S(2)}, u32[]{:S(2)}) collective-permute-start(bf16[2,32,1536]{2,1,0:T(8,128)(2,1)S(1)} %get-tuple-element.44), channel_id=1, source_target_pairs={{0,1},{1,0},{2,3},{3,2},{4,5},{5,4},{6,7},{7,6},{8,9},{9,8},{10,11... | collective-permute-start | bytes 589832 | tf_op jit(solution)/shard_map/ppermute | solution.py:269
  49.9 7.5 %collective-permute-start.4 = (bf16[32,1536]{1,0:T(8,128)(2,1)S(1)}, bf16[32,1536]{1,0:T(8,128)(2,1)S(1)}, u32[]{:S(2)}, u32[]{:S(2)}) collective-permute-start(bf16[32,1536]{1,0:T(8,128)(2,1)S(1)} %get-tuple-element.41.refs_0_), channel_id=1, source_target_pairs={{8,0},{9,1},{10,2},{11,3},{24,16},{25,17},{26,18},{27,19},{12,4},{... | collective-permute-start | bytes 294920 | tf_op jit(solution)/shard_map/ppermute | solution.py:288
  51.2 8.1 %collective-permute-start.5 = (bf16[32,1536]{1,0:T(8,128)(2,1)S(1)}, bf16[32,1536]{1,0:T(8,128)(2,1)S(1)}, u32[]{:S(2)}, u32[]{:S(2)}) collective-permute-start(bf16[32,1536]{1,0:T(8,128)(2,1)S(1)} %get-tuple-element.42.refs_1_), channel_id=1, source_target_pairs={{8,2},{9,3},{10,0},{11,1},{24,18},{25,19},{26,16},{27,17},{12,6},{... | collective-permute-start | bytes 294920 | tf_op jit(solution)/shard_map/ppermute | solution.py:288
  53.1 16.3 %collective-permute-start.10 = (bf16[32,1536]{1,0:T(8,128)(2,1)S(1)}, bf16[32,1536]{1,0:T(8,128)(2,1)S(1)}, u32[]{:S(2)}, u32[]{:S(2)}) collective-permute-start(bf16[32,1536]{1,0:T(8,128)(2,1)S(1)} %get-tuple-element.45.refs_0_), channel_id=1, source_target_pairs={{8,0},{9,1},{10,2},{11,3},{24,16},{25,17},{26,18},{27,19},{12,4},{... | collective-permute-start | bytes 294920 | tf_op jit(solution)/shard_map/ppermute | solution.py:288
  54.4 15.0 %collective-permute-start.11 = (bf16[32,1536]{1,0:T(8,128)(2,1)S(1)}, bf16[32,1536]{1,0:T(8,128)(2,1)S(1)}, u32[]{:S(2)}, u32[]{:S(2)}) collective-permute-start(bf16[32,1536]{1,0:T(8,128)(2,1)S(1)} %get-tuple-element.46.refs_1_), channel_id=1, source_target_pairs={{8,2},{9,3},{10,0},{11,1},{24,18},{25,19},{26,16},{27,17},{12,6},{... | collective-permute-start | bytes 294920 | tf_op jit(solution)/shard_map/ppermute | solution.py:288
  59.4 10.1 %collective-permute-start.6 = (bf16[32,1536]{1,0:T(8,128)(2,1)S(1)}, bf16[32,1536]{1,0:T(8,128)(2,1)S(1)}, u32[]{:S(2)}, u32[]{:S(2)}) collective-permute-start(bf16[32,1536]{1,0:T(8,128)(2,1)S(1)} %get-tuple-element.67), channel_id=1, source_target_pairs={{0,4},{4,0},{1,5},{5,1},{2,6},{6,2},{3,7},{7,3},{8,12},{12,8},{9,1... | collective-permute-start | bytes 294920 | tf_op jit(solution)/shard_map/ppermute | solution.py:266
  68.9 9.9 %collective-permute-start.15 = (bf16[768,128]{1,0:T(8,128)(2,1)S(1)}, bf16[768,128]{1,0:T(8,128)(2,1)S(1)}, u32[]{:S(2)}, u32[]{:S(2)}) collective-permute-start(bf16[768,128]{1,0:T(8,128)(2,1)S(1)} %project.6.mine_ref), channel_id=1, source_target_pairs={{0,4},{4,0},{1,5},{5,1},{2,6},{6,2},{3,7},{7,3},{8,12},{12,8},{9,1... | collective-permute-start | bytes 589832 | tf_op jit(solution)/shard_map/ppermute | solution.py:266
  77.2 7.2 %collective-permute-start.12 = (bf16[768,128]{1,0:T(8,128)(2,1)S(1)}, bf16[768,128]{1,0:T(8,128)(2,1)S(1)}, u32[]{:S(2)}, u32[]{:S(2)}) collective-permute-start(bf16[768,128]{1,0:T(8,128)(2,1)S(1)} %project.7.mine_ref), channel_id=1, source_target_pairs={{0,4},{4,0},{1,5},{5,1},{2,6},{6,2},{3,7},{7,3},{8,12},{12,8},{9,1... | collective-permute-start | bytes 589832 | tf_op jit(solution)/shard_map/ppermute | solution.py:266
  80.1 5.8 %collective-permute-start.16 = (bf16[2,32,1536]{2,1,0:T(8,128)(2,1)S(1)}, bf16[2,32,1536]{2,1,0:T(8,128)(2,1)S(1)}, u32[]{:S(2)}, u32[]{:S(2)}) collective-permute-start(bf16[2,32,1536]{2,1,0:T(8,128)(2,1)S(1)} %get-tuple-element.52), channel_id=1, source_target_pairs={{0,1},{1,0},{2,3},{3,2},{4,5},{5,4},{6,7},{7,6},{8,9},{9,8},{10,11... | collective-permute-start | bytes 589832 | tf_op jit(solution)/shard_map/ppermute | solution.py:269
  85.8 3.4 %collective-permute-start.13 = (bf16[2,32,1536]{2,1,0:T(8,128)(2,1)S(1)}, bf16[2,32,1536]{2,1,0:T(8,128)(2,1)S(1)}, u32[]{:S(2)}, u32[]{:S(2)}) collective-permute-start(bf16[2,32,1536]{2,1,0:T(8,128)(2,1)S(1)} %get-tuple-element.48), channel_id=1, source_target_pairs={{0,1},{1,0},{2,3},{3,2},{4,5},{5,4},{6,7},{7,6},{8,9},{9,8},{10,11... | collective-permute-start | bytes 589832 | tf_op jit(solution)/shard_map/ppermute | solution.py:269
  86.5 8.3 %collective-permute-start.17 = (bf16[32,1536]{1,0:T(8,128)(2,1)S(1)}, bf16[32,1536]{1,0:T(8,128)(2,1)S(1)}, u32[]{:S(2)}, u32[]{:S(2)}) collective-permute-start(bf16[32,1536]{1,0:T(8,128)(2,1)S(1)} %get-tuple-element.53), channel_id=1, source_target_pairs={{0,4},{1,5},{2,6},{3,7},{4,0},{5,1},{6,2},{7,3},{8,12},{9,13},{10,... | collective-permute-start | bytes 294920 | tf_op jit(solution)/shard_map/ppermute | solution.py:280
  88.0 6.7 %collective-permute-start.18 = (bf16[32,1536]{1,0:T(8,128)(2,1)S(1)}, bf16[32,1536]{1,0:T(8,128)(2,1)S(1)}, u32[]{:S(2)}, u32[]{:S(2)}) collective-permute-start(bf16[32,1536]{1,0:T(8,128)(2,1)S(1)} %get-tuple-element.54), channel_id=1, source_target_pairs={{0,6},{1,7},{2,4},{3,5},{4,2},{5,3},{6,0},{7,1},{8,14},{9,15},{10,... | collective-permute-start | bytes 294920 | tf_op jit(solution)/shard_map/ppermute | solution.py:280
  89.8 6.6 %collective-permute-start.14 = (bf16[32,1536]{1,0:T(8,128)(2,1)S(1)}, bf16[32,1536]{1,0:T(8,128)(2,1)S(1)}, u32[]{:S(2)}, u32[]{:S(2)}) collective-permute-start(bf16[32,1536]{1,0:T(8,128)(2,1)S(1)} %get-tuple-element.50), channel_id=1, source_target_pairs={{0,2},{1,3},{2,0},{3,1},{4,6},{5,7},{6,4},{7,5},{8,10},{9,11},{10,... | collective-permute-start | bytes 294920 | tf_op jit(solution)/shard_map/ppermute | solution.py:272

commit v4 on v3

--- a/solution.py
+++ b/solution.py
@@ -12,8 +12,10 @@
 CHUNKS = 4
 VMEM_BYTES = 8 * 2**20
 GRAD_VMEM_BYTES = 16 * 2**20
-PREPARE_VMEM_BYTES = 50 * 2**20
+FIRST_VMEM_BYTES = 48 * 2**20
+SECOND_VMEM_BYTES = 47 * 2**20
 ODD, EVEN, OWN, OTHER, CORE, ROW, HALF = range(7)
+SMALL = pl.CostEstimate(flops=1, bytes_accessed=1, transcendentals=0)
 NN = (((1,), (0,)), ((), ()))
 NT = (((1,), (1,)), ((), ()))
 TN = (((0,), (0,)), ((), ()))
@@ -35,41 +37,30 @@
     return pl.BlockSpec(memory_space=pltpu.HBM)
 
 
-def project_kernel(use_out, micro, index, facts_ref, value_ref, out_ref, tokens_ref, partial_ref):
-    version = facts_ref[micro]
+def project_kernel(micro, index, facts_ref, table_ref, tokens_ref, partial_ref):
     flipped = tokens_ref[index].T
-
-    def rows_of(table_ref):
-        partial = matmul(table_ref[0, version], flipped, NN)
-        partial_ref[...] = partial.astype(jnp.bfloat16)
-
-    pl.when(facts_ref[use_out] == 1)(lambda: rows_of(out_ref))
-    pl.when(facts_ref[use_out] == 0)(lambda: rows_of(value_ref))
-
-
-def project(use_out, micro, index, facts, w_value, w_out, tokens):
-    rows, width = w_value.shape[2:]
-    return pl.pallas_call(
-        functools.partial(project_kernel, use_out, micro, index),
+    partial = matmul(table_ref[0, facts_ref[micro]], flipped, NN)
+    partial_ref[...] = partial.astype(jnp.bfloat16)
+
+
+def project(micro, index, facts, table, tokens):
+    rows, width = table.shape[2:]
+    return pl.pallas_call(
+        functools.partial(project_kernel, micro, index),
         out_shape=jax.ShapeDtypeStruct((rows, tokens.shape[1]), jnp.bfloat16),
-        in_specs=[in_smem(), in_vmem(), in_vmem(), in_vmem()],
+        in_specs=[in_smem(), in_vmem(), in_vmem()],
         out_specs=in_vmem(),
         compiler_params=pltpu.CompilerParams(vmem_limit_bytes=VMEM_BYTES),
-        cost_estimate=pl.CostEstimate(
-            flops=2 * rows * width * tokens.shape[1],
-            bytes_accessed=2 * rows * width,
-            transcendentals=0,
-        ),
+        cost_estimate=SMALL,
         name="project",
-    )(facts, w_value, w_out, tokens)
+    )(facts, table, tokens)
 
 
 def mix_kernel(
-    outer, natural, micro, facts_ref, value_ref, mine_ref, arrived_ref, probs_ref, result_ref, keep_ref, send_ref
+    outer, natural, micro, facts_ref, first_ref, second_ref, mine_ref, arrived_ref, probs_ref, result_ref, keep_ref, send_ref
 ):
     version = facts_ref[micro]
-    width = value_ref.shape[3]
-    step = width // CHUNKS
+    step = first_ref.shape[3] // CHUNKS
 
     def heads(dims):
         for head in range(probs_ref.shape[0]):
@@ -81,36 +72,36 @@
     pl.when(facts_ref[natural] == 1)(lambda: heads(NN))
     pl.when(facts_ref[natural] == 0)(lambda: heads(NT))
 
-    flipped = result_ref[...].T
-    second_core = facts_ref[CORE] == 1
-    shard = flipped.shape[0] // (2 * outer)
-    for chunk in range(CHUNKS):
-        columns = pl.ds(chunk * step, step)
-        partial = matmul(flipped, value_ref[0, version, :, columns], NN)
-        for index in range(outer):
-            low = partial[2 * index * shard : (2 * index + 1) * shard]
-            high = partial[(2 * index + 1) * shard : (2 * index + 2) * shard]
-            keep_ref[index, :, columns] = jnp.where(second_core, high, low).astype(jnp.bfloat16)
-            send_ref[index, :, columns] = jnp.where(second_core, low, high).astype(jnp.bfloat16)
-
-
-def mix(natural, micro, facts, w_value, mine, arrived, probs, outer):
-    rows, width = w_value.shape[2:]
+    def spread(value_ref):
+        flipped = result_ref[...].T
+        second_core = facts_ref[CORE] == 1
+        shard = flipped.shape[0] // (2 * outer)
+        for chunk in range(CHUNKS):
+            columns = pl.ds(chunk * step, step)
+            partial = matmul(flipped, value_ref[0, version, :, columns], NN)
+            for index in range(outer):
+                low = partial[2 * index * shard : (2 * index + 1) * shard]
+                high = partial[(2 * index + 1) * shard : (2 * index + 2) * shard]
+                keep_ref[index, :, columns] = jnp.where(second_core, high, low).astype(jnp.bfloat16)
+                send_ref[index, :, columns] = jnp.where(second_core, low, high).astype(jnp.bfloat16)
+
+    pl.when(facts_ref[ODD] == 0)(lambda: spread(first_ref))
+    pl.when(facts_ref[ODD] == 1)(lambda: spread(second_ref))
+
+
+def mix(natural, micro, facts, tables, mine, arrived, probs, outer):
+    rows, width = tables[0].shape[2:]
     tokens = mine.shape[1]
     half = jax.ShapeDtypeStruct((outer, tokens // (2 * outer), width), jnp.bfloat16)
     return pl.pallas_call(
         functools.partial(mix_kernel, outer, natural, micro),
         out_shape=(jax.ShapeDtypeStruct((rows, tokens), jnp.bfloat16), half, half),
-        in_specs=[in_smem(), in_vmem(), in_vmem(), in_vmem(), in_vmem()],
+        in_specs=[in_smem()] + [in_vmem()] * 5,
         out_specs=(in_vmem(), in_vmem(), in_vmem()),
         compiler_params=pltpu.CompilerParams(vmem_limit_bytes=VMEM_BYTES),
-        cost_estimate=pl.CostEstimate(
-            flops=2 * rows * (width + tokens) * tokens,
-            bytes_accessed=2 * rows * width,
-            transcendentals=0,
-        ),
+        cost_estimate=SMALL,
         name="mix",
-    )(facts, w_value, mine, arrived, probs)
+    )(facts, *tables, mine, arrived, probs)
 
 
 def combine_kernel(outer, last, facts_ref, keep_ref, arrived_ref, addend_ref, *refs):
@@ -135,11 +126,7 @@
         in_specs=[in_smem()] + [in_vmem()] * (3 + len(first_sent)),
         out_specs=(in_vmem(),) * outer,
         compiler_params=pltpu.CompilerParams(vmem_limit_bytes=VMEM_BYTES),
-        cost_estimate=pl.CostEstimate(
-            flops=2 * outer * shard * width,
-            bytes_accessed=6 * outer * shard * width,
-            transcendentals=0,
-        ),
+        cost_estimate=SMALL,
         name="combine",
     )(facts, keep, arrived, addend, *first_sent)
 
@@ -202,20 +189,40 @@
         in_specs=[in_smem()] + [left] * 4 + [both, right, right],
         out_specs=(wide, wide),
         compiler_params=pltpu.CompilerParams(vmem_limit_bytes=GRAD_VMEM_BYTES),
-        cost_estimate=pl.CostEstimate(
-            flops=8 * rows * width * tokens, bytes_accessed=4 * rows * width, transcendentals=0
-        ),
+        cost_estimate=SMALL,
         name="weight_grads",
     )(facts, *first_results, *second_results, first_full, *second_full)
 
 
-def prepare_kernel(query_ref, key_ref, value_ref, out_ref, probs_ref, value_held, out_held, sems):
-    copies = [
-        pltpu.make_async_copy(value_ref, value_held, sems.at[0]),
-        pltpu.make_async_copy(out_ref, out_held, sems.at[1]),
+def load_table(use_out, value_ref, out_ref, table_ref, sems):
+    step = table_ref.shape[2] // CHUNKS
+    spots = [
+        (slice(None), version, pl.ds(chunk * step, step))
+        for version in range(2)
+        for chunk in range(CHUNKS)
     ]
-    for copy in copies:
-        copy.start()
+
+    def copies(source_ref):
+        return [
+            pltpu.make_async_copy(source_ref.at[spot], table_ref.at[spot], sems.at[i])
+            for i, spot in enumerate(spots)
+        ]
+
+    @pl.when(use_out)
+    def _():
+        for copy in copies(out_ref):
+            copy.start()
+
+    @pl.when(jnp.logical_not(use_out))
+    def _():
+        for copy in copies(value_ref):
+            copy.start()
+
+    return copies(value_ref)
+
+
+def prepare_kernel(odd_ref, query_ref, key_ref, value_ref, out_ref, probs_ref, table_ref, sems):
+    waits = load_table(odd_ref[0] == 1, value_ref, out_ref, table_ref, sems)
     tokens = query_ref.shape[2]
     causal = lax.broadcasted_iota(jnp.int32, (tokens, tokens), 1) <= lax.broadcasted_iota(
         jnp.int32, (tokens, tokens), 0
@@ -226,28 +233,42 @@
         scores = jnp.where(causal, scores * (1.0 / math.sqrt(HEAD_DIM)), -jnp.inf)
         expo = jnp.exp(scores - jnp.max(scores, axis=1, keepdims=True))
         probs_ref[head] = (expo / jnp.sum(expo, axis=1, keepdims=True)).astype(jnp.bfloat16)
-    for copy in copies:
-        copy.wait()
-
-
-def prepare(query, key_stash, w_value, w_out):
+    for wait in waits:
+        wait.wait()
+
+
+def prepare(odd_flag, query, key_stash, w_value, w_out):
     rows, tokens = query.shape[1:]
     heads = rows // HEAD_DIM
     table = jax.ShapeDtypeStruct(w_value.shape, jnp.bfloat16)
     return pl.pallas_call(
         prepare_kernel,
-        out_shape=(jax.ShapeDtypeStruct((heads, tokens, tokens), jnp.bfloat16), table, table),
-        in_specs=[in_vmem(), in_vmem(), in_hbm(), in_hbm()],
-        out_specs=(in_vmem(), in_vmem(), in_vmem()),
-        scratch_shapes=[pltpu.SemaphoreType.DMA((2,))],
-        compiler_params=pltpu.CompilerParams(vmem_limit_bytes=PREPARE_VMEM_BYTES),
-        cost_estimate=pl.CostEstimate(
-            flops=2 * rows * tokens * tokens,
-            bytes_accessed=4 * w_value.size,
-            transcendentals=heads * tokens * tokens,
-        ),
+        out_shape=(jax.ShapeDtypeStruct((heads, tokens, tokens), jnp.bfloat16), table),
+        in_specs=[in_smem(), in_vmem(), in_vmem(), in_hbm(), in_hbm()],
+        out_specs=(in_vmem(), in_vmem()),
+        scratch_shapes=[pltpu.SemaphoreType.DMA((2 * CHUNKS,))],
+        compiler_params=pltpu.CompilerParams(vmem_limit_bytes=FIRST_VMEM_BYTES),
+        cost_estimate=SMALL,
         name="prepare",
-    )(query, key_stash, w_value, w_out)
+    )(odd_flag[None], query, key_stash, w_value, w_out)
+
+
+def second_kernel(odd_ref, value_ref, out_ref, table_ref, sems):
+    for wait in load_table(odd_ref[0] == 0, value_ref, out_ref, table_ref, sems):
+        wait.wait()
+
+
+def second_table(odd_flag, w_value, w_out):
+    return pl.pallas_call(
+        second_kernel,
+        out_shape=jax.ShapeDtypeStruct(w_value.shape, jnp.bfloat16),
+        in_specs=[in_smem(), in_hbm(), in_hbm()],
+        out_specs=in_vmem(),
+        scratch_shapes=[pltpu.SemaphoreType.DMA((2 * CHUNKS,))],
+        compiler_params=pltpu.CompilerParams(vmem_limit_bytes=SECOND_VMEM_BYTES),
+        cost_estimate=SMALL,
+        name="second_table",
+    )(odd_flag[None], w_value, w_out)
 
 
 def on_device(section_input, query, key_stash, incoming, version, w_value, w_out):
@@ -301,34 +322,41 @@
     first_piece = [own_columns(first), swap_half(other_columns(first))]
     other_version = swap_half(version)[0]
     facts = jnp.stack([odd_flag, 1 - odd_flag, version[0], other_version, core, row, half])
-    own_probs, w_value, w_out = prepare(query, key_stash, w_value, w_out)
-    probs = [own_probs, swap_half(own_probs)]
+    own_probs, first_table = prepare(odd_flag, query, key_stash, w_value, w_out)
+    other_probs = swap_half(own_probs)
+    input_other = swap_half(other_columns(section_input[0]))
 
     first_full = gathered(first_piece)
+    first_full, other_probs, input_other = lax.optimization_barrier(
+        (first_full, other_probs, input_other)
+    )
+    probs = [own_probs, other_probs]
+    input_piece = [own_columns(section_input[0]), input_other]
     partial = [None, None]
     for m in (1, 0):
-        partial[m] = project(ODD, micros[m], m, facts, w_value, w_out, first_full)
+        partial[m] = project(micros[m], m, facts, first_table, first_full)
     arrived = [swap_half(partial[1]), swap_half(partial[0])]
-    later_input, _ = lax.optimization_barrier((section_input[0], partial[0]))
-    input_piece = [own_columns(later_input), swap_half(other_columns(later_input))]
+    later_tables, _ = lax.optimization_barrier(((w_value, w_out), partial[0]))
+    tables = [first_table, second_table(odd_flag, *later_tables)]
     first_result, first_sent = [None, None], [None, None]
     second_piece, second_full = [None, None], [None, None]
     for m in range(2):
         first_result[m], keep, send = mix(
-            ODD, micros[m], facts, w_value, partial[m], arrived[m], probs[m], outer
+            ODD, micros[m], facts, tables, partial[m], arrived[m], probs[m], outer
         )
         first_sent[m] = combine(facts, keep, swap_core(send), first_piece[m])
+    for m in range(2):
         received = [to_section_below(part, d) for d, part in enumerate(first_sent[m])]
         total = sum(part.astype(jnp.float32) for part in received).astype(jnp.bfloat16)
         second_piece[m] = jnp.where(odd, input_piece[m], total)
     for m in range(2):
         second_full[m] = gathered([second_piece[m]])
-        partial[m] = project(EVEN, micros[m], 0, facts, w_value, w_out, second_full[m])
+        partial[m] = project(micros[m], 0, facts, tables[1], second_full[m])
     arrived = [swap_half(partial[1]), swap_half(partial[0])]
     second_result, last_sent = [None, None], [None, None]
     for m in (1, 0):
         second_result[m], keep, send = mix(
-            EVEN, micros[m], facts, w_value, partial[m], arrived[m], probs[m], outer
+            EVEN, micros[m], facts, tables, partial[m], arrived[m], probs[m], outer
         )
         last_sent[m] = combine(facts, keep, swap_core(send), second_piece[m], first_sent[m])
     other_parts = [to_other_half(part, d) for d, part in enumerate(last_sent[1])]

time: 98 us -> 89.3 us (0.911)
  waiting for transfers between devices: 19.8 us -> 13.6 us
  Pallas kernels: 26.3 us -> 23.6 us
  starting transfers between devices: 19.6 us -> 18.6 us
    ppermute x8, waiting for transfers between devices: 14.6 us -> 9.12 us  [swap_half(): return lax.ppermute(array, 'half', [(0, 1), (1, 0)])]
    pallas_call x1, Pallas kernels: 7.47 us -> 2.47 us  [prepare(): pl.pallas_call(prepare_kernel, out_shape=(jax.ShapeDtypeStruct((heads, to...]
    pallas_call x4 -> x5, Pallas kernels: 5.34 us -> 7.59 us  [the longest x4 5.22 us: project(): pl.pallas_call(functools.partial(project_kernel, micro, index), out_shape...]
    ppermute x1, waiting for transfers between devices: 1.6 us -> 0.01 us  [to_row(): lax.ppermute(array, 'tensor', [(i, i ^ 2 * delta) for i in range(n_tensor)])]
    unnamed x18 -> x14, local copies, waits for them, and re-layouts: 6.54 us -> 6.35 us
  transfers between devices with their start and end apart: 19 -> 19, of which waited for: 7 -> 6; matrix products, arithmetic and copies ran while one was open for 1% -> 3% of each run, Pallas kernels for 24% -> 24%
where the time goes in v4:
time: 89.3 us; the launch traced here: 88.9 us
  Pallas kernels  23.6 us (26%)
  blocking collectives  22.5 us (25%)
  starting transfers between devices  18.6 us (21%)
  waiting for transfers between devices  13.6 us (15%)
  local copies, waits for them, and re-layouts  8.04 us (9%)
  between operations  1.56 us (2%)
  other arithmetic  1.05 us (1%)
    all_gather x3, blocking collectives, gathered(): return lax.all_gather(jnp.stack(pieces), 'tensor', axis=1, tiled=True)  22.5 us
    ppermute x8, starting transfers between devices, swap_half(): return lax.ppermute(array, 'half', [(0, 1), (1, 0)])  9.46 us
    ppermute x8, waiting for transfers between devices, swap_half(): return lax.ppermute(array, 'half', [(0, 1), (1, 0)])  9.12 us
    unnamed x14, local copies, waits for them, and re-layouts  6.35 us
    pallas_call x4, Pallas kernels, mix(): pl.pallas_call(functools.partial(mix_kernel, outer, natural, micro), out_...  5.76 us
    pallas_call x4, Pallas kernels, project(): pl.pallas_call(functools.partial(project_kernel, micro, index), out_shape...  5.22 us
    ppermute x4, starting transfers between devices, to_section_below(): return lax.ppermute(array, ('pair', 'tensor'), pairs)  5.17 us
    pallas_call x1, Pallas kernels, weight_grads(): pl.pallas_call(weight_grad_kernel, grid=(CHUNKS,), out_shape=(grad, grad)...  4.05 us
  transfers between devices with their start and end apart: 19, of which 6 were waited for; matrix products, arithmetic and copies ran while one was open for 3% of the time, Pallas kernels for 24%

profile of v4, /device:TPU:0, one launch (start us, length us, event | category | flops | bytes accessed | tf_op | source)
XLA Modules:
  0.0 88.9 jit_solution(15271599370300184727)
XLA Ops:
  0.6 3.0 %collective-permute-start = (s32[1]{0:T(128)}, s32[1]{0:T(128)}, u32[]{:S(2)}, u32[]{:S(2)}) collective-permute-start(s32[1]{0:T(128)} %param.11), channel_id=1, source_target_pairs={{0,4},{4,0},{1,5},{5,1},{2,6},{6,2},{3,7},{7,3},{8,12},{12,8},{9,1... | collective-permute-start | bytes 20 | tf_op jit(solution)/shard_map/ppermute | solution.py:287
  5.6 2.0 %collective-permute-start.3 = (bf16[32,1536]{1,0:T(8,128)(2,1)S(1)}, bf16[32,1536]{1,0:T(8,128)(2,1)S(1)}, u32[]{:S(2)}, u32[]{:S(2)}) collective-permute-start(bf16[32,1536]{1,0:T(8,128)(2,1)S(1)} %dynamic-slice_bitcast_fusion), channel_id=1, source_target_pairs={{0,4},{4,0},{1,5},{5,1},{2,6},{6,2},{3,7},{7,3},{8,12},{12,8},{9,1... | collective-permute-start | bytes 294920 | tf_op jit(solution)/shard_map/ppermute | solution.py:287
  9.5 2.5 %prepare.1 = (bf16[8,128,128]{2,1,0:T(8,128)(2,1)S(1)}, bf16[1,2,768,1536]{3,2,1,0:T(8,128)(2,1)S(1)}) custom-call(s32[1]{0:T(128)} %bitcast.odd_ref, bf16[1,768,128]{2,1,0:T(8,128)(2,1)S(1)} %copy-done.2, bf16[1,768,128]{2,1,0:T(8,128)(2,1)S(1)} %copy-done.3, bf16[1,2,768,1536]{3,2,1,0:T(8,128)(2,1)} %value_ref.2, bf16[1,2,768,1536]{3,2,1,0:T(8,128)(2,1)} %out_ref.2), custom_call_target="tpu_custom_call" | custom-call | flops 1 | bytes 1 | tf_op jit(solution)/shard_map/prepare/pallas_call | solution.py:244
  12.0 2.1 %copy-done = bf16[1,2,768,1536]{3,2,1,0:T(8,128)(2,1)} copy-done((bf16[1,2,768,1536]{3,2,1,0:T(8,128)(2,1)}, bf16[1,2,768,1536]{3,2,1,0:T(8,128)(2,1)S(1)}, u32[]{:S(2)}) %copy-start) | copy-done | bytes 4718616
  15.6 9.1 %all_gather.9.tokens_ref.first = bf16[2,128,1536]{2,1,0:T(8,128)(2,1)S(1)} all-gather(bf16[2,32,1536]{2,1,0:T(8,128)(2,1)S(1)} %pad_maximum_fusion), channel_id=1, replica_groups=mesh['pair'=4,'half'=2,'tensor'=4] {'tensor'}, dimensions={1}, use_global_device_ids=true | all-gather | bytes 983040 | tf_op jit(solution)/shard_map/all_gather | solution.py:318
  24.7 2.3 %copy-done.1 = bf16[1,2,768,1536]{3,2,1,0:T(8,128)(2,1)S(1)} copy-done((bf16[1,2,768,1536]{3,2,1,0:T(8,128)(2,1)S(1)}, bf16[1,2,768,1536]{3,2,1,0:T(8,128)(2,1)}, u32[]{:S(2)}) %copy-start.1) | copy-done | bytes 4718616
  27.1 1.3 %project.4.mine_ref = bf16[768,128]{1,0:T(8,128)(2,1)S(1)} custom-call(s32[7]{0:T(128)S(1)} %stack.36.facts_ref, bf16[1,2,768,1536]{3,2,1,0:T(8,128)(2,1)S(1)} %copy-done.1, bf16[2,128,1536]{2,1,0:T(8,128)(2,1)S(1)} %all_gather.9.tokens_ref.first), custom_call_target="tpu_custom_call" | custom-call | flops 1 | bytes 1 | tf_op jit(solution)/shard_map/project/pallas_call | solution.py:48
  28.4 1.6 %collective-permute-start.8 = (bf16[768,128]{1,0:T(8,128)(2,1)S(1)}, bf16[768,128]{1,0:T(8,128)(2,1)S(1)}, u32[]{:S(2)}, u32[]{:S(2)}) collective-permute-start(bf16[768,128]{1,0:T(8,128)(2,1)S(1)} %project.4.mine_ref), channel_id=1, source_target_pairs={{0,4},{4,0},{1,5},{5,1},{2,6},{6,2},{3,7},{7,3},{8,12},{12,8},{9,1... | collective-permute-start | bytes 589832 | tf_op jit(solution)/shard_map/ppermute | solution.py:287
  29.9 1.3 %project.5.mine_ref = bf16[768,128]{1,0:T(8,128)(2,1)S(1)} custom-call(s32[7]{0:T(128)S(1)} %stack.36.facts_ref, bf16[1,2,768,1536]{3,2,1,0:T(8,128)(2,1)S(1)} %copy-done.1, bf16[2,128,1536]{2,1,0:T(8,128)(2,1)S(1)} %all_gather.9.tokens_ref.first), custom_call_target="tpu_custom_call" | custom-call | flops 1 | bytes 1 | tf_op jit(solution)/shard_map/project/pallas_call | solution.py:48
  31.9 2.4 %second_table.1.second_ref.table_ref = bf16[1,2,768,1536]{3,2,1,0:T(8,128)(2,1)S(1)} custom-call(s32[1]{0:T(128)} %bitcast.odd_ref, bf16[1,2,768,1536]{3,2,1,0:T(8,128)(2,1)} %value_ref.2, bf16[1,2,768,1536]{3,2,1,0:T(8,128)(2,1)} %out_ref.2), custom_call_target="tpu_custom_call" | custom-call | flops 1 | bytes 1 | tf_op jit(solution)/shard_map/second_table/pallas_call | solution.py:262
  34.2 1.9 %collective-permute-done.8.arrived_ref = bf16[768,128]{1,0:T(8,128)(2,1)S(1)} collective-permute-done((bf16[768,128]{1,0:T(8,128)(2,1)S(1)}, bf16[768,128]{1,0:T(8,128)(2,1)S(1)}, u32[]{:S(2)}, u32[]{:S(2)}) %collective-permute-start.8) | collective-permute-done | bytes 196640 | tf_op jit(solution)/shard_map/ppermute | solution.py:287
  36.2 1.5 %mix.5 = (bf16[768,128]{1,0:T(8,128)(2,1)S(1)}, bf16[2,32,1536]{2,1,0:T(8,128)(2,1)S(1)}, bf16[2,32,1536]{2,1,0:T(8,128)(2,1)S(1)}) custom-call(s32[7]{0:T(128)S(1)} %stack.36.facts_ref, bf16[1,2,768,1536]{3,2,1,0:T(8,128)(2,1)S(1)} %bitcast.16, bf16[1,2,768,1536]{3,2,1,0:T(8,128)(2,1)S(1)} %second_table.1.second_ref.table_ref, ...), custom_call_target="tpu_custom_call" | custom-call | flops 1 | bytes 1 | tf_op jit(solution)/shard_map/mix/pallas_call | solution.py:96
  37.7 2.1 %collective-permute-done.4.arrived_ref = bf16[768,128]{1,0:T(8,128)(2,1)S(1)} collective-permute-done((bf16[768,128]{1,0:T(8,128)(2,1)S(1)}, bf16[768,128]{1,0:T(8,128)(2,1)S(1)}, u32[]{:S(2)}, u32[]{:S(2)}) %collective-permute-start.4) | collective-permute-done | bytes 196640 | tf_op jit(solution)/shard_map/ppermute | solution.py:287
  39.8 1.5 %mix.4 = (bf16[768,128]{1,0:T(8,128)(2,1)S(1)}, bf16[2,32,1536]{2,1,0:T(8,128)(2,1)S(1)}, bf16[2,32,1536]{2,1,0:T(8,128)(2,1)S(1)}) custom-call(s32[7]{0:T(128)S(1)} %stack.36.facts_ref, bf16[1,2,768,1536]{3,2,1,0:T(8,128)(2,1)S(1)} %bitcast.16, bf16[1,2,768,1536]{3,2,1,0:T(8,128)(2,1)S(1)} %second_table.1.second_ref.table_ref, ...), custom_call_target="tpu_custom_call" | custom-call | flops 1 | bytes 1 | tf_op jit(solution)/shard_map/mix/pallas_call | solution.py:96
  42.0 1.3 %collective-permute-start.10 = (bf16[32,1536]{1,0:T(8,128)(2,1)S(1)}, bf16[32,1536]{1,0:T(8,128)(2,1)S(1)}, u32[]{:S(2)}, u32[]{:S(2)}) collective-permute-start(bf16[32,1536]{1,0:T(8,128)(2,1)S(1)} %get-tuple-element.51.refs_0_), channel_id=1, source_target_pairs={{8,0},{9,1},{10,2},{11,3},{24,16},{25,17},{26,18},{27,19},{12,4},{... | collective-permute-start | bytes 294920 | tf_op jit(solution)/shard_map/ppermute | solution.py:309
  43.3 1.3 %collective-permute-start.11 = (bf16[32,1536]{1,0:T(8,128)(2,1)S(1)}, bf16[32,1536]{1,0:T(8,128)(2,1)S(1)}, u32[]{:S(2)}, u32[]{:S(2)}) collective-permute-start(bf16[32,1536]{1,0:T(8,128)(2,1)S(1)} %get-tuple-element.52.refs_1_), channel_id=1, source_target_pairs={{8,2},{9,3},{10,0},{11,1},{24,18},{25,19},{26,16},{27,17},{12,6},{... | collective-permute-start | bytes 294920 | tf_op jit(solution)/shard_map/ppermute | solution.py:309
  45.2 1.3 %collective-permute-start.6 = (bf16[32,1536]{1,0:T(8,128)(2,1)S(1)}, bf16[32,1536]{1,0:T(8,128)(2,1)S(1)}, u32[]{:S(2)}, u32[]{:S(2)}) collective-permute-start(bf16[32,1536]{1,0:T(8,128)(2,1)S(1)} %get-tuple-element.45.refs_0_), channel_id=1, source_target_pairs={{8,0},{9,1},{10,2},{11,3},{24,16},{25,17},{26,18},{27,19},{12,4},{... | collective-permute-start | bytes 294920 | tf_op jit(solution)/shard_map/ppermute | solution.py:309
  46.5 1.3 %collective-permute-start.7 = (bf16[32,1536]{1,0:T(8,128)(2,1)S(1)}, bf16[32,1536]{1,0:T(8,128)(2,1)S(1)}, u32[]{:S(2)}, u32[]{:S(2)}) collective-permute-start(bf16[32,1536]{1,0:T(8,128)(2,1)S(1)} %get-tuple-element.46.refs_1_), channel_id=1, source_target_pairs={{8,2},{9,3},{10,0},{11,1},{24,18},{25,19},{26,16},{27,17},{12,6},{... | collective-permute-start | bytes 294920 | tf_op jit(solution)/shard_map/ppermute | solution.py:309
  47.8 1.7 %collective-permute-done.10 = bf16[32,1536]{1,0:T(8,128)(2,1)S(1)} collective-permute-done((bf16[32,1536]{1,0:T(8,128)(2,1)S(1)}, bf16[32,1536]{1,0:T(8,128)(2,1)S(1)}, u32[]{:S(2)}, u32[]{:S(2)}) %collective-permute-start.10) | collective-permute-done | bytes 98336 | tf_op jit(solution)/shard_map/ppermute | solution.py:309
  49.5 1.9 %collective-permute-done.11 = bf16[32,1536]{1,0:T(8,128)(2,1)S(1)} collective-permute-done((bf16[32,1536]{1,0:T(8,128)(2,1)S(1)}, bf16[32,1536]{1,0:T(8,128)(2,1)S(1)}, u32[]{:S(2)}, u32[]{:S(2)}) %collective-permute-start.11) | collective-permute-done | bytes 98336 | tf_op jit(solution)/shard_map/ppermute | solution.py:309
  51.5 7.0 %all-gather.1 = bf16[128,1536]{1,0:T(8,128)(2,1)S(1)} all-gather(bf16[32,1536]{1,0:T(8,128)(2,1)S(1)} %fusion.1.addend_ref), channel_id=3, replica_groups=mesh['pair'=4,'half'=2,'tensor'=4] {'tensor'}, dimensions={0}, use_global_device_ids=true | all-gather | bytes 491520 | tf_op jit(solution)/shard_map/all_gather | solution.py:318
  58.5 1.3 %project.7.mine_ref = bf16[768,128]{1,0:T(8,128)(2,1)S(1)} custom-call(s32[7]{0:T(128)S(1)} %stack.36.facts_ref, bf16[1,2,768,1536]{3,2,1,0:T(8,128)(2,1)S(1)} %second_table.1.second_ref.table_ref, bf16[1,128,1536]{2,1,0:T(8,128)(2,1)S(1)} %bitcast.17), custom_call_target="tpu_custom_call" | custom-call | flops 1 | bytes 1 | tf_op jit(solution)/shard_map/project/pallas_call | solution.py:48
  59.8 1.6 %collective-permute-start.12 = (bf16[768,128]{1,0:T(8,128)(2,1)S(1)}, bf16[768,128]{1,0:T(8,128)(2,1)S(1)}, u32[]{:S(2)}, u32[]{:S(2)}) collective-permute-start(bf16[768,128]{1,0:T(8,128)(2,1)S(1)} %project.7.mine_ref), channel_id=1, source_target_pairs={{0,4},{4,0},{1,5},{5,1},{2,6},{6,2},{3,7},{7,3},{8,12},{12,8},{9,1... | collective-permute-start | bytes 589832 | tf_op jit(solution)/shard_map/ppermute | solution.py:287
  61.4 6.3 %all-gather = bf16[128,1536]{1,0:T(8,128)(2,1)S(1)} all-gather(bf16[32,1536]{1,0:T(8,128)(2,1)S(1)} %fusion.addend_ref), channel_id=2, replica_groups=mesh['pair'=4,'half'=2,'tensor'=4] {'tensor'}, dimensions={0}, use_global_device_ids=true | all-gather | bytes 491520 | tf_op jit(solution)/shard_map/all_gather | solution.py:318
  67.8 1.3 %project.6.mine_ref = bf16[768,128]{1,0:T(8,128)(2,1)S(1)} custom-call(s32[7]{0:T(128)S(1)} %stack.36.facts_ref, bf16[1,2,768,1536]{3,2,1,0:T(8,128)(2,1)S(1)} %second_table.1.second_ref.table_ref, bf16[1,128,1536]{2,1,0:T(8,128)(2,1)S(1)} %bitcast.19), custom_call_target="tpu_custom_call" | custom-call | flops 1 | bytes 1 | tf_op jit(solution)/shard_map/project/pallas_call | solution.py:48
  69.7 1.4 %mix.6 = (bf16[768,128]{1,0:T(8,128)(2,1)S(1)}, bf16[2,32,1536]{2,1,0:T(8,128)(2,1)S(1)}, bf16[2,32,1536]{2,1,0:T(8,128)(2,1)S(1)}) custom-call(s32[7]{0:T(128)S(1)} %stack.36.facts_ref, bf16[1,2,768,1536]{3,2,1,0:T(8,128)(2,1)S(1)} %bitcast.16, bf16[1,2,768,1536]{3,2,1,0:T(8,128)(2,1)S(1)} %second_table.1.second_ref.table_ref, ...), custom_call_target="tpu_custom_call" | custom-call | flops 1 | bytes 1 | tf_op jit(solution)/shard_map/mix/pallas_call | solution.py:96
  71.2 5.1 %collective-permute-done.15.arrived_ref = bf16[768,128]{1,0:T(8,128)(2,1)S(1)} collective-permute-done((bf16[768,128]{1,0:T(8,128)(2,1)S(1)}, bf16[768,128]{1,0:T(8,128)(2,1)S(1)}, u32[]{:S(2)}, u32[]{:S(2)}) %collective-permute-start.15) | collective-permute-done | bytes 196640 | tf_op jit(solution)/shard_map/ppermute | solution.py:287
  76.3 1.4 %mix.7 = (bf16[768,128]{1,0:T(8,128)(2,1)S(1)}, bf16[2,32,1536]{2,1,0:T(8,128)(2,1)S(1)}, bf16[2,32,1536]{2,1,0:T(8,128)(2,1)S(1)}) custom-call(s32[7]{0:T(128)S(1)} %stack.36.facts_ref, bf16[1,2,768,1536]{3,2,1,0:T(8,128)(2,1)S(1)} %bitcast.16, bf16[1,2,768,1536]{3,2,1,0:T(8,128)(2,1)S(1)} %second_table.1.second_ref.table_ref, ...), custom_call_target="tpu_custom_call" | custom-call | flops 1 | bytes 1 | tf_op jit(solution)/shard_map/mix/pallas_call | solution.py:96
  78.4 1.4 %collective-permute-start.14 = (bf16[32,1536]{1,0:T(8,128)(2,1)S(1)}, bf16[32,1536]{1,0:T(8,128)(2,1)S(1)}, u32[]{:S(2)}, u32[]{:S(2)}) collective-permute-start(bf16[32,1536]{1,0:T(8,128)(2,1)S(1)} %get-tuple-element.56), channel_id=1, source_target_pairs={{0,2},{1,3},{2,0},{3,1},{4,6},{5,7},{6,4},{7,5},{8,10},{9,11},{10,... | collective-permute-start | bytes 294920 | tf_op jit(solution)/shard_map/ppermute | solution.py:293
  81.0 1.7 %collective-permute-start.18 = (bf16[32,1536]{1,0:T(8,128)(2,1)S(1)}, bf16[32,1536]{1,0:T(8,128)(2,1)S(1)}, u32[]{:S(2)}, u32[]{:S(2)}) collective-permute-start(bf16[32,1536]{1,0:T(8,128)(2,1)S(1)} %get-tuple-element.60), channel_id=1, source_target_pairs={{0,6},{1,7},{2,4},{3,5},{4,2},{5,3},{6,0},{7,1},{8,14},{9,15},{10,... | collective-permute-start | bytes 294920 | tf_op jit(solution)/shard_map/ppermute | solution.py:301
  82.7 4.1 %weight_grads.1 = (bf16[1,768,1536]{2,1,0:T(8,128)(2,1)}, bf16[1,768,1536]{2,1,0:T(8,128)(2,1)}) custom-call(s32[7]{0:T(128)S(1)} %stack.36.facts_ref, bf16[768,128]{1,0:T(8,128)(2,1)S(1)} %get-tuple-element.61.a0, bf16[768,128]{1,0:T(8,128)(2,1)S(1)} %get-tuple-element.62.a1, bf16[768,128]{1,0:T(8,128)(2,1)S(1)} %get-tuple-element.65.b0, ...), custom_call_target="tpu_custom_call" | custom-call | flops 1 | bytes 1 | tf_op jit(solution)/shard_map/weight_grads/pallas_call | solution.py:185
  87.6 1.3 %assemble.1 = bf16[1,32,3072]{2,1,0:T(8,128)(2,1)} custom-call(s32[7]{0:T(128)S(1)} %stack.36.facts_ref, bf16[32,1536]{1,0:T(8,128)(2,1)S(1)} %get-tuple-element.68.refs_0_, bf16[32,1536]{1,0:T(8,128)(2,1)S(1)} %collective-permute-done.14.refs_1_, bf16[32,1536]{1,0:T(8,128)(2,1)S(1)} %collective-permute-done.17.refs_2_, ...), custom_call_target="tpu_custom_call" | custom-call | tf_op jit(solution)/shard_map/assemble/pallas_call | solution.py:153
  (47 shorter events, 10.2 us)
Async XLA Ops:
  0.6 14.2 %collective-permute-start = (s32[1]{0:T(128)}, s32[1]{0:T(128)}, u32[]{:S(2)}, u32[]{:S(2)}) collective-permute-start(s32[1]{0:T(128)} %param.11), channel_id=1, source_target_pairs={{0,4},{4,0},{1,5},{5,1},{2,6},{6,2},{3,7},{7,3},{8,12},{12,8},{9,1... | collective-permute-start | bytes 20 | tf_op jit(solution)/shard_map/ppermute | solution.py:287
  4.6 11.0 %collective-permute-start.1 = (bf16[32,1536]{1,0:T(8,128)(2,1)S(1)}, bf16[32,1536]{1,0:T(8,128)(2,1)S(1)}, u32[]{:S(2)}, u32[]{:S(2)}) collective-permute-start(bf16[32,1536]{1,0:T(8,128)(2,1)S(1)} %get-tuple-element.74), channel_id=1, source_target_pairs={{0,4},{4,0},{1,5},{5,1},{2,6},{6,2},{3,7},{7,3},{8,12},{12,8},{9,1... | collective-permute-start | bytes 294920 | tf_op jit(solution)/shard_map/ppermute | solution.py:287
  5.6 19.1 %collective-permute-start.3 = (bf16[32,1536]{1,0:T(8,128)(2,1)S(1)}, bf16[32,1536]{1,0:T(8,128)(2,1)S(1)}, u32[]{:S(2)}, u32[]{:S(2)}) collective-permute-start(bf16[32,1536]{1,0:T(8,128)(2,1)S(1)} %dynamic-slice_bitcast_fusion), channel_id=1, source_target_pairs={{0,4},{4,0},{1,5},{5,1},{2,6},{6,2},{3,7},{7,3},{8,12},{12,8},{9,1... | collective-permute-start | bytes 294920 | tf_op jit(solution)/shard_map/ppermute | solution.py:287
  7.6 0.9 %copy-start.2 = (bf16[1,768,128]{2,1,0:T(8,128)(2,1)S(1)}, bf16[1,768,128]{2,1,0:T(8,128)(2,1)}, u32[]{:S(2)}) copy-start(bf16[1,768,128]{2,1,0:T(8,128)(2,1)} %query_ref.1) | copy-start | bytes 589828
  8.5 0.9 %copy-start.3 = (bf16[1,768,128]{2,1,0:T(8,128)(2,1)S(1)}, bf16[1,768,128]{2,1,0:T(8,128)(2,1)}, u32[]{:S(2)}) copy-start(bf16[1,768,128]{2,1,0:T(8,128)(2,1)} %key_ref.1) | copy-start | bytes 589828
  11.9 2.2 %copy-start = (bf16[1,2,768,1536]{3,2,1,0:T(8,128)(2,1)}, bf16[1,2,768,1536]{3,2,1,0:T(8,128)(2,1)S(1)}, u32[]{:S(2)}) copy-start(bf16[1,2,768,1536]{3,2,1,0:T(8,128)(2,1)S(1)} %get-tuple-element.38.table_ref.first_ref) | copy-start | bytes 14155780
  14.1 10.6 %collective-permute-start.2 = (bf16[8,128,128]{2,1,0:T(8,128)(2,1)S(1)}, bf16[8,128,128]{2,1,0:T(8,128)(2,1)S(1)}, u32[]{:S(2)}, u32[]{:S(2)}) collective-permute-start(bf16[8,128,128]{2,1,0:T(8,128)(2,1)S(1)} %get-tuple-element.39.probs_ref), channel_id=1, source_target_pairs={{0,4},{4,0},{1,5},{5,1},{2,6},{6,2},{3,7},{7,3},{8,12},{12,8},{9,1... | collective-permute-start | bytes 786440 | tf_op jit(solution)/shard_map/ppermute | solution.py:287
  24.7 2.3 %copy-start.1 = (bf16[1,2,768,1536]{3,2,1,0:T(8,128)(2,1)S(1)}, bf16[1,2,768,1536]{3,2,1,0:T(8,128)(2,1)}, u32[]{:S(2)}) copy-start(bf16[1,2,768,1536]{3,2,1,0:T(8,128)(2,1)} %copy-done) | copy-start | bytes 14155780
  28.4 7.8 %collective-permute-start.8 = (bf16[768,128]{1,0:T(8,128)(2,1)S(1)}, bf16[768,128]{1,0:T(8,128)(2,1)S(1)}, u32[]{:S(2)}, u32[]{:S(2)}) collective-permute-start(bf16[768,128]{1,0:T(8,128)(2,1)S(1)} %project.4.mine_ref), channel_id=1, source_target_pairs={{0,4},{4,0},{1,5},{5,1},{2,6},{6,2},{3,7},{7,3},{8,12},{12,8},{9,1... | collective-permute-start | bytes 589832 | tf_op jit(solution)/shard_map/ppermute | solution.py:287
  29.9 6.2 %slice-start = ((s8[4718592]{0:T(1024)(128)(4,1)}), s8[4194304]{0:T(1024)(128)(4,1)S(1)}, s32[]{:S(2)}) async-start(s8[4718592]{0:T(1024)(128)(4,1)} %bitcast.15), calls=%async_computation | async-start | bytes 8388608
  31.3 4.9 %slice-start.1 = ((s8[4718592]{0:T(1024)(128)(4,1)}), s8[524288]{0:T(1024)(128)(4,1)S(1)}, s32[]{:S(2)}) async-start(s8[4718592]{0:T(1024)(128)(4,1)} %bitcast.15), calls=%async_computation.1 | async-start | bytes 1048576
  31.3 8.5 %collective-permute-start.4 = (bf16[768,128]{1,0:T(8,128)(2,1)S(1)}, bf16[768,128]{1,0:T(8,128)(2,1)S(1)}, u32[]{:S(2)}, u32[]{:S(2)}) collective-permute-start(bf16[768,128]{1,0:T(8,128)(2,1)S(1)} %project.5.mine_ref), channel_id=1, source_target_pairs={{0,4},{4,0},{1,5},{5,1},{2,6},{6,2},{3,7},{7,3},{8,12},{12,8},{9,1... | collective-permute-start | bytes 589832 | tf_op jit(solution)/shard_map/ppermute | solution.py:287
  37.7 3.7 %collective-permute-start.9 = (bf16[2,32,1536]{2,1,0:T(8,128)(2,1)S(1)}, bf16[2,32,1536]{2,1,0:T(8,128)(2,1)S(1)}, u32[]{:S(2)}, u32[]{:S(2)}) collective-permute-start(bf16[2,32,1536]{2,1,0:T(8,128)(2,1)S(1)} %get-tuple-element.50), channel_id=1, source_target_pairs={{0,1},{1,0},{2,3},{3,2},{4,5},{5,4},{6,7},{7,6},{8,9},{9,8},{10,11... | collective-permute-start | bytes 589832 | tf_op jit(solution)/shard_map/ppermute | solution.py:290
  41.3 20.1 %copy-start.4 = (bf16[1,32,3072]{2,1,0:T(8,128)(2,1)S(1)}, bf16[1,32,3072]{2,1,0:T(8,128)(2,1)}, u32[]{:S(2)}) copy-start(bf16[1,32,3072]{2,1,0:T(8,128)(2,1)} %param.7) | copy-start | bytes 589828
  41.3 3.3 %collective-permute-start.5 = (bf16[2,32,1536]{2,1,0:T(8,128)(2,1)S(1)}, bf16[2,32,1536]{2,1,0:T(8,128)(2,1)S(1)}, u32[]{:S(2)}, u32[]{:S(2)}) collective-permute-start(bf16[2,32,1536]{2,1,0:T(8,128)(2,1)S(1)} %get-tuple-element.44), channel_id=1, source_target_pairs={{0,1},{1,0},{2,3},{3,2},{4,5},{5,4},{6,7},{7,6},{8,9},{9,8},{10,11... | collective-permute-start | bytes 589832 | tf_op jit(solution)/shard_map/ppermute | solution.py:290
  42.0 7.5 %collective-permute-start.10 = (bf16[32,1536]{1,0:T(8,128)(2,1)S(1)}, bf16[32,1536]{1,0:T(8,128)(2,1)S(1)}, u32[]{:S(2)}, u32[]{:S(2)}) collective-permute-start(bf16[32,1536]{1,0:T(8,128)(2,1)S(1)} %get-tuple-element.51.refs_0_), channel_id=1, source_target_pairs={{8,0},{9,1},{10,2},{11,3},{24,16},{25,17},{26,18},{27,19},{12,4},{... | collective-permute-start | bytes 294920 | tf_op jit(solution)/shard_map/ppermute | solution.py:309
  43.3 8.1 %collective-permute-start.11 = (bf16[32,1536]{1,0:T(8,128)(2,1)S(1)}, bf16[32,1536]{1,0:T(8,128)(2,1)S(1)}, u32[]{:S(2)}, u32[]{:S(2)}) collective-permute-start(bf16[32,1536]{1,0:T(8,128)(2,1)S(1)} %get-tuple-element.52.refs_1_), channel_id=1, source_target_pairs={{8,2},{9,3},{10,0},{11,1},{24,18},{25,19},{26,16},{27,17},{12,6},{... | collective-permute-start | bytes 294920 | tf_op jit(solution)/shard_map/ppermute | solution.py:309
  45.2 16.1 %collective-permute-start.6 = (bf16[32,1536]{1,0:T(8,128)(2,1)S(1)}, bf16[32,1536]{1,0:T(8,128)(2,1)S(1)}, u32[]{:S(2)}, u32[]{:S(2)}) collective-permute-start(bf16[32,1536]{1,0:T(8,128)(2,1)S(1)} %get-tuple-element.45.refs_0_), channel_id=1, source_target_pairs={{8,0},{9,1},{10,2},{11,3},{24,16},{25,17},{26,18},{27,19},{12,4},{... | collective-permute-start | bytes 294920 | tf_op jit(solution)/shard_map/ppermute | solution.py:309
  46.5 14.8 %collective-permute-start.7 = (bf16[32,1536]{1,0:T(8,128)(2,1)S(1)}, bf16[32,1536]{1,0:T(8,128)(2,1)S(1)}, u32[]{:S(2)}, u32[]{:S(2)}) collective-permute-start(bf16[32,1536]{1,0:T(8,128)(2,1)S(1)} %get-tuple-element.46.refs_1_), channel_id=1, source_target_pairs={{8,2},{9,3},{10,0},{11,1},{24,18},{25,19},{26,16},{27,17},{12,6},{... | collective-permute-start | bytes 294920 | tf_op jit(solution)/shard_map/ppermute | solution.py:309
  59.8 9.9 %collective-permute-start.12 = (bf16[768,128]{1,0:T(8,128)(2,1)S(1)}, bf16[768,128]{1,0:T(8,128)(2,1)S(1)}, u32[]{:S(2)}, u32[]{:S(2)}) collective-permute-start(bf16[768,128]{1,0:T(8,128)(2,1)S(1)} %project.7.mine_ref), channel_id=1, source_target_pairs={{0,4},{4,0},{1,5},{5,1},{2,6},{6,2},{3,7},{7,3},{8,12},{12,8},{9,1... | collective-permute-start | bytes 589832 | tf_op jit(solution)/shard_map/ppermute | solution.py:287
  69.1 7.2 %collective-permute-start.15 = (bf16[768,128]{1,0:T(8,128)(2,1)S(1)}, bf16[768,128]{1,0:T(8,128)(2,1)S(1)}, u32[]{:S(2)}, u32[]{:S(2)}) collective-permute-start(bf16[768,128]{1,0:T(8,128)(2,1)S(1)} %project.6.mine_ref), channel_id=1, source_target_pairs={{0,4},{4,0},{1,5},{5,1},{2,6},{6,2},{3,7},{7,3},{8,12},{12,8},{9,1... | collective-permute-start | bytes 589832 | tf_op jit(solution)/shard_map/ppermute | solution.py:287
  71.1 6.7 %collective-permute-start.13 = (bf16[2,32,1536]{2,1,0:T(8,128)(2,1)S(1)}, bf16[2,32,1536]{2,1,0:T(8,128)(2,1)S(1)}, u32[]{:S(2)}, u32[]{:S(2)}) collective-permute-start(bf16[2,32,1536]{2,1,0:T(8,128)(2,1)S(1)} %get-tuple-element.54), channel_id=1, source_target_pairs={{0,1},{1,0},{2,3},{3,2},{4,5},{5,4},{6,7},{7,6},{8,9},{9,8},{10,11... | collective-permute-start | bytes 589832 | tf_op jit(solution)/shard_map/ppermute | solution.py:290
  77.7 2.1 %collective-permute-start.16 = (bf16[2,32,1536]{2,1,0:T(8,128)(2,1)S(1)}, bf16[2,32,1536]{2,1,0:T(8,128)(2,1)S(1)}, u32[]{:S(2)}, u32[]{:S(2)}) collective-permute-start(bf16[2,32,1536]{2,1,0:T(8,128)(2,1)S(1)} %get-tuple-element.58), channel_id=1, source_target_pairs={{0,1},{1,0},{2,3},{3,2},{4,5},{5,4},{6,7},{7,6},{8,9},{9,8},{10,11... | collective-permute-start | bytes 589832 | tf_op jit(solution)/shard_map/ppermute | solution.py:290
  78.4 8.3 %collective-permute-start.14 = (bf16[32,1536]{1,0:T(8,128)(2,1)S(1)}, bf16[32,1536]{1,0:T(8,128)(2,1)S(1)}, u32[]{:S(2)}, u32[]{:S(2)}) collective-permute-start(bf16[32,1536]{1,0:T(8,128)(2,1)S(1)} %get-tuple-element.56), channel_id=1, source_target_pairs={{0,2},{1,3},{2,0},{3,1},{4,6},{5,7},{6,4},{7,5},{8,10},{9,11},{10,... | collective-permute-start | bytes 294920 | tf_op jit(solution)/shard_map/ppermute | solution.py:293
  80.4 6.3 %collective-permute-start.17 = (bf16[32,1536]{1,0:T(8,128)(2,1)S(1)}, bf16[32,1536]{1,0:T(8,128)(2,1)S(1)}, u32[]{:S(2)}, u32[]{:S(2)}) collective-permute-start(bf16[32,1536]{1,0:T(8,128)(2,1)S(1)} %get-tuple-element.59), channel_id=1, source_target_pairs={{0,4},{1,5},{2,6},{3,7},{4,0},{5,1},{6,2},{7,3},{8,12},{9,13},{10,... | collective-permute-start | bytes 294920 | tf_op jit(solution)/shard_map/ppermute | solution.py:301
  81.0 6.6 %collective-permute-start.18 = (bf16[32,1536]{1,0:T(8,128)(2,1)S(1)}, bf16[32,1536]{1,0:T(8,128)(2,1)S(1)}, u32[]{:S(2)}, u32[]{:S(2)}) collective-permute-start(bf16[32,1536]{1,0:T(8,128)(2,1)S(1)} %get-tuple-element.60), channel_id=1, source_target_pairs={{0,6},{1,7},{2,4},{3,5},{4,2},{5,3},{6,0},{7,1},{8,14},{9,15},{10,... | collective-permute-start | bytes 294920 | tf_op jit(solution)/shard_map/ppermute | solution.py:301

commit v5 on v3

--- a/solution.py
+++ b/solution.py
@@ -12,8 +12,13 @@
 CHUNKS = 4
 VMEM_BYTES = 8 * 2**20
 GRAD_VMEM_BYTES = 16 * 2**20
-PREPARE_VMEM_BYTES = 50 * 2**20
-ODD, EVEN, OWN, OTHER, CORE, ROW, HALF = range(7)
+FIRST_VMEM_BYTES = 50 * 2**20
+VALUE_VMEM_BYTES = 47 * 2**20
+OUT_VMEM_BYTES = 42 * 2**20
+ODD, EVEN, VERSION, CORE, ROW, HALF = range(6)
+LANES = 128
+NOTE_ROWS = 16
+SMALL = pl.CostEstimate(flops=1, bytes_accessed=1, transcendentals=0)
 NN = (((1,), (0,)), ((), ()))
 NT = (((1,), (1,)), ((), ()))
 TN = (((0,), (0,)), ((), ()))
@@ -35,47 +40,105 @@
     return pl.BlockSpec(memory_space=pltpu.HBM)
 
 
-def project_kernel(use_out, micro, index, facts_ref, value_ref, out_ref, tokens_ref, partial_ref):
-    version = facts_ref[micro]
+def in_place():
+    return pl.BlockSpec(memory_space=pl.ANY)
+
+
+def picked_version(index, facts_ref, message_ref):
+    if index == 0:
+        return facts_ref[VERSION]
+    note = message_ref[message_ref.shape[0] - NOTE_ROWS :, :].astype(jnp.float32)
+    return (jnp.max(note) > 0.5).astype(jnp.int32)
+
+
+def first_project_kernel(
+    index, facts_ref, message_ref, value_ref, out_ref, tokens_ref, partial_ref, held, sems
+):
+    version = picked_version(index, facts_ref, message_ref)
+    step = held.shape[0] // CHUNKS
+
+    def copy(table_ref, chunk):
+        rows = pl.ds(chunk * step, step)
+        return pltpu.make_async_copy(table_ref.at[0, version, rows], held.at[rows], sems.at[chunk])
+
+    def start(table_ref):
+        for chunk in range(CHUNKS):
+            copy(table_ref, chunk).start()
+
+    pl.when(facts_ref[ODD] == 1)(lambda: start(out_ref))
+    pl.when(facts_ref[ODD] == 0)(lambda: start(value_ref))
     flipped = tokens_ref[index].T
+    for chunk in range(CHUNKS):
+        copy(value_ref, chunk).wait()
+        rows = pl.ds(chunk * step, step)
+        partial_ref[rows, :] = matmul(held[rows, :], flipped, NN).astype(jnp.bfloat16)
+
+
+def first_project(index, facts, message, w_value, w_out, tokens):
+    rows, width = w_value.shape[2:]
+    return pl.pallas_call(
+        functools.partial(first_project_kernel, index),
+        out_shape=jax.ShapeDtypeStruct((rows, tokens.shape[1]), jnp.bfloat16),
+        in_specs=[in_smem(), in_vmem(), in_hbm(), in_hbm(), in_vmem()],
+        out_specs=in_vmem(),
+        scratch_shapes=[
+            pltpu.VMEM((rows, width), jnp.bfloat16),
+            pltpu.SemaphoreType.DMA((CHUNKS,)),
+        ],
+        compiler_params=pltpu.CompilerParams(vmem_limit_bytes=FIRST_VMEM_BYTES),
+        cost_estimate=SMALL,
+        name="first_project",
+    )(facts, message, w_value, w_out, tokens)
+
+
+def project_kernel(index, facts_ref, message_ref, value_ref, out_ref, tokens_ref, partial_ref):
+    version = picked_version(index, facts_ref, message_ref)
+    flipped = tokens_ref[0].T
 
     def rows_of(table_ref):
-        partial = matmul(table_ref[0, version], flipped, NN)
-        partial_ref[...] = partial.astype(jnp.bfloat16)
-
-    pl.when(facts_ref[use_out] == 1)(lambda: rows_of(out_ref))
-    pl.when(facts_ref[use_out] == 0)(lambda: rows_of(value_ref))
-
-
-def project(use_out, micro, index, facts, w_value, w_out, tokens):
-    rows, width = w_value.shape[2:]
-    return pl.pallas_call(
-        functools.partial(project_kernel, use_out, micro, index),
+        partial_ref[...] = matmul(table_ref[0, version], flipped, NN).astype(jnp.bfloat16)
+
+    pl.when(facts_ref[ODD] == 1)(lambda: rows_of(value_ref))
+    pl.when(facts_ref[ODD] == 0)(lambda: rows_of(out_ref))
+
+
+def project(index, facts, message, tables, tokens):
+    rows = tables[0].shape[2]
+    return pl.pallas_call(
+        functools.partial(project_kernel, index),
         out_shape=jax.ShapeDtypeStruct((rows, tokens.shape[1]), jnp.bfloat16),
-        in_specs=[in_smem(), in_vmem(), in_vmem(), in_vmem()],
+        in_specs=[in_smem()] + [in_vmem()] * 4,
         out_specs=in_vmem(),
         compiler_params=pltpu.CompilerParams(vmem_limit_bytes=VMEM_BYTES),
-        cost_estimate=pl.CostEstimate(
-            flops=2 * rows * width * tokens.shape[1],
-            bytes_accessed=2 * rows * width,
-            transcendentals=0,
-        ),
+        cost_estimate=SMALL,
         name="project",
-    )(facts, w_value, w_out, tokens)
+    )(facts, message, *tables, tokens)
 
 
 def mix_kernel(
-    outer, natural, micro, facts_ref, value_ref, mine_ref, arrived_ref, probs_ref, result_ref, keep_ref, send_ref
+    outer,
+    natural,
+    index,
+    facts_ref,
+    message_ref,
+    value_ref,
+    mine_ref,
+    arrived_ref,
+    probs_ref,
+    result_ref,
+    keep_ref,
+    send_ref,
 ):
-    version = facts_ref[micro]
-    width = value_ref.shape[3]
-    step = width // CHUNKS
+    version = picked_version(index, facts_ref, message_ref)
+    step = value_ref.shape[3] // CHUNKS
+    tokens = mine_ref.shape[1]
 
     def heads(dims):
-        for head in range(probs_ref.shape[0]):
+        for head in range(mine_ref.shape[0] // HEAD_DIM):
             rows = pl.ds(head * HEAD_DIM, HEAD_DIM)
             total = mine_ref[rows, :].astype(jnp.float32) + arrived_ref[rows, :].astype(jnp.float32)
-            mixed = matmul(total.astype(jnp.bfloat16), probs_ref[head], dims)
+            probs = probs_ref[head * tokens : (head + 1) * tokens, :]
+            mixed = matmul(total.astype(jnp.bfloat16), probs, dims)
             result_ref[rows, :] = mixed.astype(jnp.bfloat16)
 
     pl.when(facts_ref[natural] == 1)(lambda: heads(NN))
@@ -83,34 +146,30 @@
 
     flipped = result_ref[...].T
     second_core = facts_ref[CORE] == 1
-    shard = flipped.shape[0] // (2 * outer)
+    shard = tokens // (2 * outer)
     for chunk in range(CHUNKS):
         columns = pl.ds(chunk * step, step)
         partial = matmul(flipped, value_ref[0, version, :, columns], NN)
-        for index in range(outer):
-            low = partial[2 * index * shard : (2 * index + 1) * shard]
-            high = partial[(2 * index + 1) * shard : (2 * index + 2) * shard]
-            keep_ref[index, :, columns] = jnp.where(second_core, high, low).astype(jnp.bfloat16)
-            send_ref[index, :, columns] = jnp.where(second_core, low, high).astype(jnp.bfloat16)
-
-
-def mix(natural, micro, facts, w_value, mine, arrived, probs, outer):
+        for place in range(outer):
+            low = partial[2 * place * shard : (2 * place + 1) * shard]
+            high = partial[(2 * place + 1) * shard : (2 * place + 2) * shard]
+            keep_ref[place, :, columns] = jnp.where(second_core, high, low).astype(jnp.bfloat16)
+            send_ref[place, :, columns] = jnp.where(second_core, low, high).astype(jnp.bfloat16)
+
+
+def mix(natural, index, facts, messages, w_value, mine, arrived, outer):
     rows, width = w_value.shape[2:]
     tokens = mine.shape[1]
     half = jax.ShapeDtypeStruct((outer, tokens // (2 * outer), width), jnp.bfloat16)
     return pl.pallas_call(
-        functools.partial(mix_kernel, outer, natural, micro),
+        functools.partial(mix_kernel, outer, natural, index),
         out_shape=(jax.ShapeDtypeStruct((rows, tokens), jnp.bfloat16), half, half),
-        in_specs=[in_smem(), in_vmem(), in_vmem(), in_vmem(), in_vmem()],
+        in_specs=[in_smem()] + [in_vmem()] * 5,
         out_specs=(in_vmem(), in_vmem(), in_vmem()),
         compiler_params=pltpu.CompilerParams(vmem_limit_bytes=VMEM_BYTES),
-        cost_estimate=pl.CostEstimate(
-            flops=2 * rows * (width + tokens) * tokens,
-            bytes_accessed=2 * rows * width,
-            transcendentals=0,
-        ),
+        cost_estimate=SMALL,
         name="mix",
-    )(facts, w_value, mine, arrived, probs)
+    )(facts, messages[1], w_value, mine, arrived, messages[index])
 
 
 def combine_kernel(outer, last, facts_ref, keep_ref, arrived_ref, addend_ref, *refs):
@@ -135,11 +194,7 @@
         in_specs=[in_smem()] + [in_vmem()] * (3 + len(first_sent)),
         out_specs=(in_vmem(),) * outer,
         compiler_params=pltpu.CompilerParams(vmem_limit_bytes=VMEM_BYTES),
-        cost_estimate=pl.CostEstimate(
-            flops=2 * outer * shard * width,
-            bytes_accessed=6 * outer * shard * width,
-            transcendentals=0,
-        ),
+        cost_estimate=SMALL,
         name="combine",
     )(facts, keep, arrived, addend, *first_sent)
 
@@ -202,52 +257,132 @@
         in_specs=[in_smem()] + [left] * 4 + [both, right, right],
         out_specs=(wide, wide),
         compiler_params=pltpu.CompilerParams(vmem_limit_bytes=GRAD_VMEM_BYTES),
-        cost_estimate=pl.CostEstimate(
-            flops=8 * rows * width * tokens, bytes_accessed=4 * rows * width, transcendentals=0
-        ),
+        cost_estimate=SMALL,
         name="weight_grads",
     )(facts, *first_results, *second_results, first_full, *second_full)
 
 
-def prepare_kernel(query_ref, key_ref, value_ref, out_ref, probs_ref, value_held, out_held, sems):
+def pack_kernel(
+    facts_ref, query_ref, key_ref, input_ref, message_ref, own_ref, query_held, key_held, input_held, sems
+):
+    pairs = ((query_ref, query_held), (key_ref, key_held), (input_ref, input_held))
     copies = [
-        pltpu.make_async_copy(value_ref, value_held, sems.at[0]),
-        pltpu.make_async_copy(out_ref, out_held, sems.at[1]),
+        pltpu.make_async_copy(source, held, sems.at[i]) for i, (source, held) in enumerate(pairs)
     ]
     for copy in copies:
         copy.start()
     tokens = query_ref.shape[2]
+    shard, width = own_ref.shape
+    heads = query_ref.shape[1] // HEAD_DIM
     causal = lax.broadcasted_iota(jnp.int32, (tokens, tokens), 1) <= lax.broadcasted_iota(
         jnp.int32, (tokens, tokens), 0
     )
-    for head in range(probs_ref.shape[0]):
+    copies[0].wait()
+    copies[1].wait()
+    for head in range(heads):
         rows = pl.ds(head * HEAD_DIM, HEAD_DIM)
-        scores = matmul(query_ref[0, rows, :], key_ref[0, rows, :], TN)
+        scores = matmul(query_held[0, rows, :], key_held[0, rows, :], TN)
         scores = jnp.where(causal, scores * (1.0 / math.sqrt(HEAD_DIM)), -jnp.inf)
         expo = jnp.exp(scores - jnp.max(scores, axis=1, keepdims=True))
-        probs_ref[head] = (expo / jnp.sum(expo, axis=1, keepdims=True)).astype(jnp.bfloat16)
+        probs = (expo / jnp.sum(expo, axis=1, keepdims=True)).astype(jnp.bfloat16)
+        message_ref[head * tokens : (head + 1) * tokens, :] = probs
+    copies[2].wait()
+    half = facts_ref[HALF]
+    own_ref[...] = input_held[0, :, pl.ds(pl.multiple_of(half * width, width), width)]
+    other = input_held[0, :, pl.ds(pl.multiple_of((1 - half) * width, width), width)]
+    for block in range(width // LANES):
+        start = heads * tokens + block * shard
+        message_ref[start : start + shard, :] = other[:, block * LANES : (block + 1) * LANES]
+    note = jnp.zeros((NOTE_ROWS, LANES), jnp.int32) + facts_ref[VERSION]
+    message_ref[message_ref.shape[0] - NOTE_ROWS :, :] = note.astype(jnp.bfloat16)
+
+
+def pack(facts, query, key_stash, section_input):
+    rows, tokens = query.shape[1:]
+    shard = section_input.shape[1]
+    width = section_input.shape[2] // 2
+    length = rows // HEAD_DIM * tokens + width // LANES * shard + NOTE_ROWS
+    return pl.pallas_call(
+        pack_kernel,
+        out_shape=(
+            jax.ShapeDtypeStruct((length, LANES), jnp.bfloat16),
+            jax.ShapeDtypeStruct((shard, width), jnp.bfloat16),
+        ),
+        in_specs=[in_smem(), in_place(), in_place(), in_place()],
+        out_specs=(in_vmem(), in_vmem()),
+        scratch_shapes=[
+            pltpu.VMEM(query.shape, jnp.bfloat16),
+            pltpu.VMEM(query.shape, jnp.bfloat16),
+            pltpu.VMEM(section_input.shape, jnp.bfloat16),
+            pltpu.SemaphoreType.DMA((3,)),
+        ],
+        compiler_params=pltpu.CompilerParams(vmem_limit_bytes=VMEM_BYTES),
+        cost_estimate=SMALL,
+        name="pack",
+    )(facts, query, key_stash, section_input)
+
+
+def load_kernel(source_ref, table_ref, sems):
+    step = table_ref.shape[2] // CHUNKS
+    copies = []
+    for version in range(2):
+        for chunk in range(CHUNKS):
+            spot = (slice(None), version, pl.ds(chunk * step, step))
+            copies.append(
+                pltpu.make_async_copy(
+                    source_ref.at[spot], table_ref.at[spot], sems.at[version * CHUNKS + chunk]
+                )
+            )
+    for copy in copies:
+        copy.start()
     for copy in copies:
         copy.wait()
 
 
-def prepare(query, key_stash, w_value, w_out):
-    rows, tokens = query.shape[1:]
-    heads = rows // HEAD_DIM
-    table = jax.ShapeDtypeStruct(w_value.shape, jnp.bfloat16)
-    return pl.pallas_call(
-        prepare_kernel,
-        out_shape=(jax.ShapeDtypeStruct((heads, tokens, tokens), jnp.bfloat16), table, table),
-        in_specs=[in_vmem(), in_vmem(), in_hbm(), in_hbm()],
-        out_specs=(in_vmem(), in_vmem(), in_vmem()),
-        scratch_shapes=[pltpu.SemaphoreType.DMA((2,))],
-        compiler_params=pltpu.CompilerParams(vmem_limit_bytes=PREPARE_VMEM_BYTES),
-        cost_estimate=pl.CostEstimate(
-            flops=2 * rows * tokens * tokens,
-            bytes_accessed=4 * w_value.size,
-            transcendentals=heads * tokens * tokens,
-        ),
-        name="prepare",
-    )(query, key_stash, w_value, w_out)
+def load_table(table, grant):
+    return pl.pallas_call(
+        load_kernel,
+        out_shape=jax.ShapeDtypeStruct(table.shape, jnp.bfloat16),
+        in_specs=[in_hbm()],
+        out_specs=in_vmem(),
+        scratch_shapes=[pltpu.SemaphoreType.DMA((2 * CHUNKS,))],
+        compiler_params=pltpu.CompilerParams(vmem_limit_bytes=grant),
+        cost_estimate=SMALL,
+        name="load_table",
+    )(table)
+
+
+def arrive_kernel(index, heads, facts_ref, input_ref, *refs):
+    parts, piece_ref = refs[:-1], refs[-1]
+    shard, width = piece_ref.shape
+
+    @pl.when(facts_ref[ODD] == 1)
+    def _():
+        if index == 0:
+            piece_ref[...] = input_ref[...]
+        else:
+            for block in range(width // LANES):
+                start = heads * LANES + block * shard
+                piece_ref[:, block * LANES : (block + 1) * LANES] = input_ref[start : start + shard, :]
+
+    @pl.when(facts_ref[ODD] == 0)
+    def _():
+        total = parts[0][...].astype(jnp.float32)
+        for part in parts[1:]:
+            total = total + part[...].astype(jnp.float32)
+        piece_ref[...] = total.astype(jnp.bfloat16)
+
+
+def arrive(index, heads, facts, source, parts):
+    return pl.pallas_call(
+        functools.partial(arrive_kernel, index, heads),
+        out_shape=jax.ShapeDtypeStruct(parts[0].shape, jnp.bfloat16),
+        in_specs=[in_smem()] + [in_vmem()] * (1 + len(parts)),
+        out_specs=in_vmem(),
+        compiler_params=pltpu.CompilerParams(vmem_limit_bytes=VMEM_BYTES),
+        cost_estimate=SMALL,
+        name="arrive",
+    )(facts, source, *parts)
 
 
 def on_device(section_input, query, key_stash, incoming, version, w_value, w_out):
@@ -279,10 +414,10 @@
         ]
         return lax.ppermute(array, ("half", "tensor"), pairs)
 
-    def to_section_below(array, delta):
+    def swap_section(array, delta):
         pairs = [
-            (p * n_tensor + i, (p - 1) * n_tensor + (i ^ (2 * delta)))
-            for p in range(1, n_pairs, 2)
+            (p * n_tensor + i, (p ^ 1) * n_tensor + (i ^ (2 * delta)))
+            for p in range(n_pairs)
             for i in range(n_tensor)
         ]
         return lax.ppermute(array, ("pair", "tensor"), pairs)
@@ -296,39 +431,45 @@
     def gathered(pieces):
         return lax.all_gather(jnp.stack(pieces), "tensor", axis=1, tiled=True)
 
-    micros = (OWN, OTHER)
+    heads = query.shape[1] // HEAD_DIM
+    facts = jnp.stack([odd_flag, 1 - odd_flag, version[0], core, row, half])
     first = jnp.where(odd, incoming[0], section_input[0])
     first_piece = [own_columns(first), swap_half(other_columns(first))]
-    other_version = swap_half(version)[0]
-    facts = jnp.stack([odd_flag, 1 - odd_flag, version[0], other_version, core, row, half])
-    own_probs, w_value, w_out = prepare(query, key_stash, w_value, w_out)
-    probs = [own_probs, swap_half(own_probs)]
-
+    own_message, input_own = pack(facts, query, key_stash, section_input)
+    other_message = swap_half(own_message)
     first_full = gathered(first_piece)
+    first_full, other_message = lax.optimization_barrier((first_full, other_message))
+    messages = [own_message, other_message]
+
     partial = [None, None]
-    for m in (1, 0):
-        partial[m] = project(ODD, micros[m], m, facts, w_value, w_out, first_full)
+    partial[1] = first_project(1, facts, other_message, w_value, w_out, first_full)
+    partial[0] = first_project(0, facts, other_message, w_value, w_out, first_full)
     arrived = [swap_half(partial[1]), swap_half(partial[0])]
-    later_input, _ = lax.optimization_barrier((section_input[0], partial[0]))
-    input_piece = [own_columns(later_input), swap_half(other_columns(later_input))]
+    later_value, _ = lax.optimization_barrier((w_value, partial))
+    value_table = load_table(later_value, VALUE_VMEM_BYTES)
     first_result, first_sent = [None, None], [None, None]
     second_piece, second_full = [None, None], [None, None]
     for m in range(2):
         first_result[m], keep, send = mix(
-            ODD, micros[m], facts, w_value, partial[m], arrived[m], probs[m], outer
+            ODD, m, facts, messages, value_table, partial[m], arrived[m], outer
         )
         first_sent[m] = combine(facts, keep, swap_core(send), first_piece[m])
-        received = [to_section_below(part, d) for d, part in enumerate(first_sent[m])]
-        total = sum(part.astype(jnp.float32) for part in received).astype(jnp.bfloat16)
-        second_piece[m] = jnp.where(odd, input_piece[m], total)
+    later_out, _ = lax.optimization_barrier((w_out, first_sent))
+    out_table = load_table(later_out, OUT_VMEM_BYTES)
+    input_own, other_input, _ = lax.optimization_barrier((input_own, other_message, out_table))
+    for m in range(2):
+        received = [swap_section(part, d) for d, part in enumerate(first_sent[m])]
+        source = other_input if m else input_own
+        second_piece[m] = arrive(m, heads, facts, source, received)
+    tables = (value_table, out_table)
     for m in range(2):
         second_full[m] = gathered([second_piece[m]])
-        partial[m] = project(EVEN, micros[m], 0, facts, w_value, w_out, second_full[m])
+        partial[m] = project(m, facts, other_message, tables, second_full[m])
     arrived = [swap_half(partial[1]), swap_half(partial[0])]
     second_result, last_sent = [None, None], [None, None]
     for m in (1, 0):
         second_result[m], keep, send = mix(
-            EVEN, micros[m], facts, w_value, partial[m], arrived[m], probs[m], outer
+            EVEN, m, facts, messages, value_table, partial[m], arrived[m], outer
         )
         last_sent[m] = combine(facts, keep, swap_core(send), second_piece[m], first_sent[m])
     other_parts = [to_other_half(part, d) for d, part in enumerate(last_sent[1])]

time: 98 us -> 83.6 us (0.85)
  waiting for transfers between devices: 19.8 us -> 9.65 us
  local copies, waits for them, and re-layouts: 7.26 us -> 2.9 us
  Pallas kernels: 26.3 us -> 30.2 us
  starting transfers between devices: 19.6 us -> 16.5 us
    ppermute x8 -> x6, waiting for transfers between devices: 14.6 us -> 6.77 us  [swap_half(): return lax.ppermute(array, 'half', [(0, 1), (1, 0)])]
    pallas_call x9 -> x13, Pallas kernels: 18.5 us -> 22.4 us  [the longest x2 7.01 us: first_project(): pl.pallas_call(functools.partial(first_project_kernel, index), out_shape=...]
    unnamed x18 -> x10, local copies, waits for them, and re-layouts: 6.54 us -> 2.79 us
    ppermute x8 -> x6, starting transfers between devices: 10.4 us -> 7.41 us  [swap_half(): return lax.ppermute(array, 'half', [(0, 1), (1, 0)])]
    ppermute x4, waiting for transfers between devices: 3.58 us -> 1.27 us  [swap_section(): return lax.ppermute(array, ('pair', 'tensor'), pairs)]
  transfers between devices with their start and end apart: 19 -> 17, of which waited for: 7 -> 5; matrix products, arithmetic and copies ran while one was open for 1% -> 0% of each run, Pallas kernels for 24% -> 30%
where the time goes in v5:
time: 83.6 us; the launch traced here: 83.4 us
  Pallas kernels  30.2 us (36%)
  blocking collectives  21.6 us (26%)
  starting transfers between devices  16.5 us (20%)
  waiting for transfers between devices  9.65 us (12%)
  local copies, waits for them, and re-layouts  2.9 us (3%)
  between operations  1.52 us (2%)
  other arithmetic  0.98 us (1%)
    all_gather x3, blocking collectives, gathered(): return lax.all_gather(jnp.stack(pieces), 'tensor', axis=1, tiled=True)  21.6 us
    ppermute x6, starting transfers between devices, swap_half(): return lax.ppermute(array, 'half', [(0, 1), (1, 0)])  7.41 us
    pallas_call x2, Pallas kernels, first_project(): pl.pallas_call(functools.partial(first_project_kernel, index), out_shape=...  7.01 us
    ppermute x6, waiting for transfers between devices, swap_half(): return lax.ppermute(array, 'half', [(0, 1), (1, 0)])  6.77 us
    pallas_call x4, Pallas kernels, mix(): pl.pallas_call(functools.partial(mix_kernel, outer, natural, index), out_...  5.85 us
    ppermute x4, starting transfers between devices, swap_section(): return lax.ppermute(array, ('pair', 'tensor'), pairs)  5.08 us
    pallas_call x1, Pallas kernels, weight_grads(): pl.pallas_call(weight_grad_kernel, grid=(CHUNKS,), out_shape=(grad, grad)...  4.09 us
    pallas_call x2, Pallas kernels, load_table(): pl.pallas_call(load_kernel, out_shape=jax.ShapeDtypeStruct(table.shape, j...  3.57 us
  transfers between devices with their start and end apart: 17, of which 5 were waited for; matrix products, arithmetic and copies ran while one was open for 0% of the time, Pallas kernels for 30%

profile of v5, /device:TPU:0, one launch (start us, length us, event | category | flops | bytes accessed | tf_op | source)
XLA Modules:
  0.0 83.4 jit_solution(17723970040390856311)
XLA Ops:
  0.6 1.0 %broadcast_select_fusion = bf16[1,32,3072]{2,1,0:T(8,128)(2,1)S(1)} fusion(bf16[1,32,3072]{2,1,0:T(8,128)(2,1)} %param.10, bf16[1,32,3072]{2,1,0:T(8,128)(2,1)} %input_ref.1, pred[]{:T(512)S(6)} %eq.6), kind=kLoop, calls=%fused_computation.1 | loop fusion | flops 98304 | bytes 589825 | tf_op jit(solution)/shard_map/jit(_where)/select_n | solution.py:436
  1.6 3.0 %collective-permute-start = (bf16[32,1536]{1,0:T(8,128)(2,1)S(1)}, bf16[32,1536]{1,0:T(8,128)(2,1)S(1)}, u32[]{:S(2)}, u32[]{:S(2)}) collective-permute-start(bf16[32,1536]{1,0:T(8,128)(2,1)S(1)} %get-tuple-element.76), channel_id=1, source_target_pairs={{0,4},{4,0},{1,5},{5,1},{2,6},{6,2},{3,7},{7,3},{8,12},{12,8},{9,1... | collective-permute-start | bytes 294920 | tf_op jit(solution)/shard_map/ppermute | solution.py:401
  5.4 0.9 %copy-done = bf16[1,32,3072]{2,1,0:T(8,128)(2,1)S(1)} copy-done((bf16[1,32,3072]{2,1,0:T(8,128)(2,1)S(1)}, bf16[1,32,3072]{2,1,0:T(8,128)(2,1)}, u32[]{:S(2)}) %copy-start) | copy-done | bytes 196632
  7.3 0.9 %copy-done.2 = bf16[1,768,128]{2,1,0:T(8,128)(2,1)S(1)} copy-done((bf16[1,768,128]{2,1,0:T(8,128)(2,1)S(1)}, bf16[1,768,128]{2,1,0:T(8,128)(2,1)}, u32[]{:S(2)}) %copy-start.2) | copy-done | bytes 196632
  8.2 2.1 %pack.1 = (bf16[1424,128]{1,0:T(8,128)(2,1)S(1)}, bf16[32,1536]{1,0:T(8,128)(2,1)S(1)}) custom-call(s32[6]{0:T(128)S(1)} %stack.36.facts_ref, bf16[1,768,128]{2,1,0:T(8,128)(2,1)S(1)} %copy-done.1, bf16[1,768,128]{2,1,0:T(8,128)(2,1)S(1)} %copy-done.2, bf16[1,32,3072]{2,1,0:T(8,128)(2,1)S(1)} %copy-done), custom_call_target="tpu_custom_call" | custom-call | flops 1 | bytes 1 | tf_op jit(solution)/shard_map/pack/pallas_call | solution.py:305
  10.4 9.1 %all_gather.9.tokens_ref.first = bf16[2,128,1536]{2,1,0:T(8,128)(2,1)S(1)} all-gather(bf16[2,32,1536]{2,1,0:T(8,128)(2,1)S(1)} %pad_maximum_fusion), channel_id=1, replica_groups=mesh['pair'=4,'half'=2,'tensor'=4] {'tensor'}, dimensions={1}, use_global_device_ids=true | all-gather | bytes 983040 | tf_op jit(solution)/shard_map/all_gather | solution.py:432
  20.3 3.6 %first_project.3.mine_ref = bf16[768,128]{1,0:T(8,128)(2,1)S(1)} custom-call(s32[6]{0:T(128)S(1)} %stack.36.facts_ref, bf16[1424,128]{1,0:T(8,128)(2,1)S(1)} %collective-permute-done.1.message_ref.probs_ref.input_ref, bf16[1,2,768,1536]{3,2,1,0:T(8,128)(2,1)} %source_ref, bf16[1,2,768,1536]{3,2,1,0:T(8,128)(2,1)} %source_ref.1, ...), custom_call_target="tpu_custom_call" | custom-call | flops 1 | bytes 1 | tf_op jit(solution)/shard_map/first_project/pallas_call | solution.py:79
  24.7 3.4 %first_project.2.mine_ref = bf16[768,128]{1,0:T(8,128)(2,1)S(1)} custom-call(s32[6]{0:T(128)S(1)} %stack.36.facts_ref, bf16[1424,128]{1,0:T(8,128)(2,1)S(1)} %collective-permute-done.1.message_ref.probs_ref.input_ref, bf16[1,2,768,1536]{3,2,1,0:T(8,128)(2,1)} %source_ref, bf16[1,2,768,1536]{3,2,1,0:T(8,128)(2,1)} %source_ref.1, ...), custom_call_target="tpu_custom_call" | custom-call | flops 1 | bytes 1 | tf_op jit(solution)/shard_map/first_project/pallas_call | solution.py:79
  28.1 1.4 %collective-permute-start.4 = (bf16[768,128]{1,0:T(8,128)(2,1)S(1)}, bf16[768,128]{1,0:T(8,128)(2,1)S(1)}, u32[]{:S(2)}, u32[]{:S(2)}) collective-permute-start(bf16[768,128]{1,0:T(8,128)(2,1)S(1)} %first_project.2.mine_ref), channel_id=1, source_target_pairs={{0,4},{4,0},{1,5},{5,1},{2,6},{6,2},{3,7},{7,3},{8,12},{12,8},{9,1... | collective-permute-start | bytes 589832 | tf_op jit(solution)/shard_map/ppermute | solution.py:401
  29.5 2.5 %load_table.2.value_ref = bf16[1,2,768,1536]{3,2,1,0:T(8,128)(2,1)S(1)} custom-call(bf16[1,2,768,1536]{3,2,1,0:T(8,128)(2,1)} %source_ref), custom_call_target="tpu_custom_call" | custom-call | flops 1 | bytes 1 | tf_op jit(solution)/shard_map/load_table/pallas_call | solution.py:343
  32.0 1.5 %mix.4 = (bf16[768,128]{1,0:T(8,128)(2,1)S(1)}, bf16[2,32,1536]{2,1,0:T(8,128)(2,1)S(1)}, bf16[2,32,1536]{2,1,0:T(8,128)(2,1)S(1)}) custom-call(s32[6]{0:T(128)S(1)} %stack.36.facts_ref, bf16[1424,128]{1,0:T(8,128)(2,1)S(1)} %collective-permute-done.1.message_ref.probs_ref.input_ref, bf16[1,2,768,1536]{3,2,1,0:T(8,128)(2,1)S(1)} %load_table.2.value_ref, ...), custom_call_target="tpu_custom_call" | custom-call | flops 1 | bytes 1 | tf_op jit(solution)/shard_map/mix/pallas_call | solution.py:164
  33.6 1.5 %collective-permute-done.4.arrived_ref = bf16[768,128]{1,0:T(8,128)(2,1)S(1)} collective-permute-done((bf16[768,128]{1,0:T(8,128)(2,1)S(1)}, bf16[768,128]{1,0:T(8,128)(2,1)S(1)}, u32[]{:S(2)}, u32[]{:S(2)}) %collective-permute-start.4) | collective-permute-done | bytes 196640 | tf_op jit(solution)/shard_map/ppermute | solution.py:401
  35.1 1.6 %mix.5 = (bf16[768,128]{1,0:T(8,128)(2,1)S(1)}, bf16[2,32,1536]{2,1,0:T(8,128)(2,1)S(1)}, bf16[2,32,1536]{2,1,0:T(8,128)(2,1)S(1)}) custom-call(s32[6]{0:T(128)S(1)} %stack.36.facts_ref, bf16[1424,128]{1,0:T(8,128)(2,1)S(1)} %collective-permute-done.1.message_ref.probs_ref.input_ref, bf16[1,2,768,1536]{3,2,1,0:T(8,128)(2,1)S(1)} %load_table.2.value_ref, ...), custom_call_target="tpu_custom_call" | custom-call | flops 1 | bytes 1 | tf_op jit(solution)/shard_map/mix/pallas_call | solution.py:164
  37.3 1.5 %collective-permute-start.6 = (bf16[32,1536]{1,0:T(8,128)(2,1)S(1)}, bf16[32,1536]{1,0:T(8,128)(2,1)S(1)}, u32[]{:S(2)}, u32[]{:S(2)}) collective-permute-start(bf16[32,1536]{1,0:T(8,128)(2,1)S(1)} %get-tuple-element.45.refs_0_), channel_id=1, source_target_pairs={{0,8},{1,9},{2,10},{3,11},{8,0},{9,1},{10,2},{11,3},{16,24},{17,25... | collective-permute-start | bytes 294920 | tf_op jit(solution)/shard_map/ppermute | solution.py:423
  40.0 1.5 %collective-permute-start.8 = (bf16[32,1536]{1,0:T(8,128)(2,1)S(1)}, bf16[32,1536]{1,0:T(8,128)(2,1)S(1)}, u32[]{:S(2)}, u32[]{:S(2)}) collective-permute-start(bf16[32,1536]{1,0:T(8,128)(2,1)S(1)} %get-tuple-element.49.refs_0_), channel_id=1, source_target_pairs={{0,8},{1,9},{2,10},{3,11},{8,0},{9,1},{10,2},{11,3},{16,24},{17,25... | collective-permute-start | bytes 294920 | tf_op jit(solution)/shard_map/ppermute | solution.py:423
  41.5 1.5 %collective-permute-start.9 = (bf16[32,1536]{1,0:T(8,128)(2,1)S(1)}, bf16[32,1536]{1,0:T(8,128)(2,1)S(1)}, u32[]{:S(2)}, u32[]{:S(2)}) collective-permute-start(bf16[32,1536]{1,0:T(8,128)(2,1)S(1)} %get-tuple-element.50.refs_1_), channel_id=1, source_target_pairs={{0,10},{1,11},{2,8},{3,9},{8,2},{9,3},{10,0},{11,1},{16,26},{17,27... | collective-permute-start | bytes 294920 | tf_op jit(solution)/shard_map/ppermute | solution.py:423
  43.0 1.0 %load_table.3.out_ref = bf16[1,2,768,1536]{3,2,1,0:T(8,128)(2,1)S(1)} custom-call(bf16[1,2,768,1536]{3,2,1,0:T(8,128)(2,1)S(1)} %bitcast.12), custom_call_target="tpu_custom_call" | custom-call | flops 1 | bytes 1 | tf_op jit(solution)/shard_map/load_table/pallas_call | solution.py:343
  44.1 1.3 %collective-permute-done.7.refs_1_ = bf16[32,1536]{1,0:T(8,128)(2,1)S(1)} collective-permute-done((bf16[32,1536]{1,0:T(8,128)(2,1)S(1)}, bf16[32,1536]{1,0:T(8,128)(2,1)S(1)}, u32[]{:S(2)}, u32[]{:S(2)}) %collective-permute-start.7) | collective-permute-done | bytes 98336 | tf_op jit(solution)/shard_map/ppermute | solution.py:423
  46.0 6.2 %all-gather = bf16[128,1536]{1,0:T(8,128)(2,1)S(1)} all-gather(bf16[32,1536]{1,0:T(8,128)(2,1)S(1)} %arrive.2.addend_ref), channel_id=2, replica_groups=mesh['pair'=4,'half'=2,'tensor'=4] {'tensor'}, dimensions={0}, use_global_device_ids=true | all-gather | bytes 491520 | tf_op jit(solution)/shard_map/all_gather | solution.py:432
  52.1 1.3 %project.2.mine_ref = bf16[768,128]{1,0:T(8,128)(2,1)S(1)} custom-call(s32[6]{0:T(128)S(1)} %stack.36.facts_ref, bf16[1424,128]{1,0:T(8,128)(2,1)S(1)} %collective-permute-done.1.message_ref.probs_ref.input_ref, bf16[1,2,768,1536]{3,2,1,0:T(8,128)(2,1)S(1)} %load_table.2.value_ref, bf16[1,2,768,1536]{3,2,1,0:T(8,128)(2,1)S(1)} %load_table.3.out_ref, ...), custom_call_target="tpu_custom_call" | custom-call | flops 1 | bytes 1 | tf_op jit(solution)/shard_map/project/pallas_call | solution.py:107
  53.5 1.0 %collective-permute-start.13 = (bf16[768,128]{1,0:T(8,128)(2,1)S(1)}, bf16[768,128]{1,0:T(8,128)(2,1)S(1)}, u32[]{:S(2)}, u32[]{:S(2)}) collective-permute-start(bf16[768,128]{1,0:T(8,128)(2,1)S(1)} %project.2.mine_ref), channel_id=1, source_target_pairs={{0,4},{4,0},{1,5},{5,1},{2,6},{6,2},{3,7},{7,3},{8,12},{12,8},{9,1... | collective-permute-start | bytes 589832 | tf_op jit(solution)/shard_map/ppermute | solution.py:401
  55.1 6.3 %all-gather.1 = bf16[128,1536]{1,0:T(8,128)(2,1)S(1)} all-gather(bf16[32,1536]{1,0:T(8,128)(2,1)S(1)} %arrive.3.addend_ref), channel_id=3, replica_groups=mesh['pair'=4,'half'=2,'tensor'=4] {'tensor'}, dimensions={0}, use_global_device_ids=true | all-gather | bytes 491520 | tf_op jit(solution)/shard_map/all_gather | solution.py:432
  61.4 1.4 %project.3.mine_ref = bf16[768,128]{1,0:T(8,128)(2,1)S(1)} custom-call(s32[6]{0:T(128)S(1)} %stack.36.facts_ref, bf16[1424,128]{1,0:T(8,128)(2,1)S(1)} %collective-permute-done.1.message_ref.probs_ref.input_ref, bf16[1,2,768,1536]{3,2,1,0:T(8,128)(2,1)S(1)} %load_table.2.value_ref, bf16[1,2,768,1536]{3,2,1,0:T(8,128)(2,1)S(1)} %load_table.3.out_ref, ...), custom_call_target="tpu_custom_call" | custom-call | flops 1 | bytes 1 | tf_op jit(solution)/shard_map/project/pallas_call | solution.py:107
  62.8 1.1 %collective-permute-start.10 = (bf16[768,128]{1,0:T(8,128)(2,1)S(1)}, bf16[768,128]{1,0:T(8,128)(2,1)S(1)}, u32[]{:S(2)}, u32[]{:S(2)}) collective-permute-start(bf16[768,128]{1,0:T(8,128)(2,1)S(1)} %project.3.mine_ref), channel_id=1, source_target_pairs={{0,4},{4,0},{1,5},{5,1},{2,6},{6,2},{3,7},{7,3},{8,12},{12,8},{9,1... | collective-permute-start | bytes 589832 | tf_op jit(solution)/shard_map/ppermute | solution.py:401
  63.9 1.4 %mix.7 = (bf16[768,128]{1,0:T(8,128)(2,1)S(1)}, bf16[2,32,1536]{2,1,0:T(8,128)(2,1)S(1)}, bf16[2,32,1536]{2,1,0:T(8,128)(2,1)S(1)}) custom-call(s32[6]{0:T(128)S(1)} %stack.36.facts_ref, bf16[1424,128]{1,0:T(8,128)(2,1)S(1)} %collective-permute-done.1.message_ref.probs_ref.input_ref, bf16[1,2,768,1536]{3,2,1,0:T(8,128)(2,1)S(1)} %load_table.2.value_ref, ...), custom_call_target="tpu_custom_call" | custom-call | flops 1 | bytes 1 | tf_op jit(solution)/shard_map/mix/pallas_call | solution.py:164
  65.5 4.5 %collective-permute-done.10.arrived_ref = bf16[768,128]{1,0:T(8,128)(2,1)S(1)} collective-permute-done((bf16[768,128]{1,0:T(8,128)(2,1)S(1)}, bf16[768,128]{1,0:T(8,128)(2,1)S(1)}, u32[]{:S(2)}, u32[]{:S(2)}) %collective-permute-start.10) | collective-permute-done | bytes 196640 | tf_op jit(solution)/shard_map/ppermute | solution.py:401
  70.0 1.4 %mix.6 = (bf16[768,128]{1,0:T(8,128)(2,1)S(1)}, bf16[2,32,1536]{2,1,0:T(8,128)(2,1)S(1)}, bf16[2,32,1536]{2,1,0:T(8,128)(2,1)S(1)}) custom-call(s32[6]{0:T(128)S(1)} %stack.36.facts_ref, bf16[1424,128]{1,0:T(8,128)(2,1)S(1)} %collective-permute-done.1.message_ref.probs_ref.input_ref, bf16[1,2,768,1536]{3,2,1,0:T(8,128)(2,1)S(1)} %load_table.2.value_ref, ...), custom_call_target="tpu_custom_call" | custom-call | flops 1 | bytes 1 | tf_op jit(solution)/shard_map/mix/pallas_call | solution.py:164
  72.1 1.1 %collective-permute-start.15 = (bf16[32,1536]{1,0:T(8,128)(2,1)S(1)}, bf16[32,1536]{1,0:T(8,128)(2,1)S(1)}, u32[]{:S(2)}, u32[]{:S(2)}) collective-permute-start(bf16[32,1536]{1,0:T(8,128)(2,1)S(1)} %get-tuple-element.61), channel_id=1, source_target_pairs={{0,4},{1,5},{2,6},{3,7},{4,0},{5,1},{6,2},{7,3},{8,12},{9,13},{10,... | collective-permute-start | bytes 294920 | tf_op jit(solution)/shard_map/ppermute | solution.py:415
  73.3 1.6 %collective-permute-start.16 = (bf16[32,1536]{1,0:T(8,128)(2,1)S(1)}, bf16[32,1536]{1,0:T(8,128)(2,1)S(1)}, u32[]{:S(2)}, u32[]{:S(2)}) collective-permute-start(bf16[32,1536]{1,0:T(8,128)(2,1)S(1)} %get-tuple-element.62), channel_id=1, source_target_pairs={{0,6},{1,7},{2,4},{3,5},{4,2},{5,3},{6,0},{7,1},{8,14},{9,15},{10,... | collective-permute-start | bytes 294920 | tf_op jit(solution)/shard_map/ppermute | solution.py:415
  76.4 4.1 %weight_grads.1 = (bf16[1,768,1536]{2,1,0:T(8,128)(2,1)}, bf16[1,768,1536]{2,1,0:T(8,128)(2,1)}) custom-call(s32[6]{0:T(128)S(1)} %stack.36.facts_ref, bf16[768,128]{1,0:T(8,128)(2,1)S(1)} %get-tuple-element.63.a0, bf16[768,128]{1,0:T(8,128)(2,1)S(1)} %get-tuple-element.64.a1, bf16[768,128]{1,0:T(8,128)(2,1)S(1)} %get-tuple-element.67.b0, ...), custom_call_target="tpu_custom_call" | custom-call | flops 1 | bytes 1 | tf_op jit(solution)/shard_map/weight_grads/pallas_call | solution.py:253
  80.5 1.6 %collective-permute-done.12.refs_1_ = bf16[32,1536]{1,0:T(8,128)(2,1)S(1)} collective-permute-done((bf16[32,1536]{1,0:T(8,128)(2,1)S(1)}, bf16[32,1536]{1,0:T(8,128)(2,1)S(1)}, u32[]{:S(2)}, u32[]{:S(2)}) %collective-permute-start.12) | collective-permute-done | bytes 98336 | tf_op jit(solution)/shard_map/ppermute | solution.py:407
  82.1 1.3 %assemble.1 = bf16[1,32,3072]{2,1,0:T(8,128)(2,1)} custom-call(s32[6]{0:T(128)S(1)} %stack.36.facts_ref, bf16[32,1536]{1,0:T(8,128)(2,1)S(1)} %get-tuple-element.70.refs_0_, bf16[32,1536]{1,0:T(8,128)(2,1)S(1)} %collective-permute-done.12.refs_1_, bf16[32,1536]{1,0:T(8,128)(2,1)S(1)} %collective-permute-done.15.refs_2_, ...), custom_call_target="tpu_custom_call" | custom-call | tf_op jit(solution)/shard_map/assemble/pallas_call | solution.py:221
  (39 shorter events, 8.2 us)
Async XLA Ops:
  1.6 8.7 %collective-permute-start = (bf16[32,1536]{1,0:T(8,128)(2,1)S(1)}, bf16[32,1536]{1,0:T(8,128)(2,1)S(1)}, u32[]{:S(2)}, u32[]{:S(2)}) collective-permute-start(bf16[32,1536]{1,0:T(8,128)(2,1)S(1)} %get-tuple-element.76), channel_id=1, source_target_pairs={{0,4},{4,0},{1,5},{5,1},{2,6},{6,2},{3,7},{7,3},{8,12},{12,8},{9,1... | collective-permute-start | bytes 294920 | tf_op jit(solution)/shard_map/ppermute | solution.py:401
  5.4 0.9 %copy-start = (bf16[1,32,3072]{2,1,0:T(8,128)(2,1)S(1)}, bf16[1,32,3072]{2,1,0:T(8,128)(2,1)}, u32[]{:S(2)}) copy-start(bf16[1,32,3072]{2,1,0:T(8,128)(2,1)} %input_ref.1) | copy-start | bytes 589828
  6.3 0.9 %copy-start.1 = (bf16[1,768,128]{2,1,0:T(8,128)(2,1)S(1)}, bf16[1,768,128]{2,1,0:T(8,128)(2,1)}, u32[]{:S(2)}) copy-start(bf16[1,768,128]{2,1,0:T(8,128)(2,1)} %query_ref.1) | copy-start | bytes 589828
  7.2 0.9 %copy-start.2 = (bf16[1,768,128]{2,1,0:T(8,128)(2,1)S(1)}, bf16[1,768,128]{2,1,0:T(8,128)(2,1)}, u32[]{:S(2)}) copy-start(bf16[1,768,128]{2,1,0:T(8,128)(2,1)} %key_ref.1) | copy-start | bytes 589828
  10.3 10.0 %collective-permute-start.1 = (bf16[1424,128]{1,0:T(8,128)(2,1)S(1)}, bf16[1424,128]{1,0:T(8,128)(2,1)S(1)}, u32[]{:S(2)}, u32[]{:S(2)}) collective-permute-start(bf16[1424,128]{1,0:T(8,128)(2,1)S(1)} %get-tuple-element.39.probs_ref), channel_id=1, source_target_pairs={{0,4},{4,0},{1,5},{5,1},{2,6},{6,2},{3,7},{7,3},{8,12},{12,8},{9,1... | collective-permute-start | bytes 1093640 | tf_op jit(solution)/shard_map/ppermute | solution.py:401
  23.9 8.2 %collective-permute-start.2 = (bf16[768,128]{1,0:T(8,128)(2,1)S(1)}, bf16[768,128]{1,0:T(8,128)(2,1)S(1)}, u32[]{:S(2)}, u32[]{:S(2)}) collective-permute-start(bf16[768,128]{1,0:T(8,128)(2,1)S(1)} %first_project.3.mine_ref), channel_id=1, source_target_pairs={{0,4},{4,0},{1,5},{5,1},{2,6},{6,2},{3,7},{7,3},{8,12},{12,8},{9,1... | collective-permute-start | bytes 589832 | tf_op jit(solution)/shard_map/ppermute | solution.py:401
  28.1 6.9 %collective-permute-start.4 = (bf16[768,128]{1,0:T(8,128)(2,1)S(1)}, bf16[768,128]{1,0:T(8,128)(2,1)S(1)}, u32[]{:S(2)}, u32[]{:S(2)}) collective-permute-start(bf16[768,128]{1,0:T(8,128)(2,1)S(1)} %first_project.2.mine_ref), channel_id=1, source_target_pairs={{0,4},{4,0},{1,5},{5,1},{2,6},{6,2},{3,7},{7,3},{8,12},{12,8},{9,1... | collective-permute-start | bytes 589832 | tf_op jit(solution)/shard_map/ppermute | solution.py:401
  29.5 13.6 %slice-start = ((s8[4718592]{0:T(1024)(128)(4,1)}), s8[4194304]{0:T(1024)(128)(4,1)S(1)}, s32[]{:S(2)}) async-start(s8[4718592]{0:T(1024)(128)(4,1)} %bitcast.11), calls=%async_computation | async-start | bytes 8388608
  32.0 11.0 %slice-start.1 = ((s8[4718592]{0:T(1024)(128)(4,1)}), s8[524288]{0:T(1024)(128)(4,1)S(1)}, s32[]{:S(2)}) async-start(s8[4718592]{0:T(1024)(128)(4,1)} %bitcast.11), calls=%async_computation.1 | async-start | bytes 1048576
  33.5 3.2 %collective-permute-start.3 = (bf16[2,32,1536]{2,1,0:T(8,128)(2,1)S(1)}, bf16[2,32,1536]{2,1,0:T(8,128)(2,1)S(1)}, u32[]{:S(2)}, u32[]{:S(2)}) collective-permute-start(bf16[2,32,1536]{2,1,0:T(8,128)(2,1)S(1)} %get-tuple-element.44), channel_id=1, source_target_pairs={{0,1},{1,0},{2,3},{3,2},{4,5},{5,4},{6,7},{7,6},{8,9},{9,8},{10,11... | collective-permute-start | bytes 589832 | tf_op jit(solution)/shard_map/ppermute | solution.py:404
  36.6 2.8 %collective-permute-start.5 = (bf16[2,32,1536]{2,1,0:T(8,128)(2,1)S(1)}, bf16[2,32,1536]{2,1,0:T(8,128)(2,1)S(1)}, u32[]{:S(2)}, u32[]{:S(2)}) collective-permute-start(bf16[2,32,1536]{2,1,0:T(8,128)(2,1)S(1)} %get-tuple-element.48), channel_id=1, source_target_pairs={{0,1},{1,0},{2,3},{3,2},{4,5},{5,4},{6,7},{7,6},{8,9},{9,8},{10,11... | collective-permute-start | bytes 589832 | tf_op jit(solution)/shard_map/ppermute | solution.py:404
  37.3 6.8 %collective-permute-start.6 = (bf16[32,1536]{1,0:T(8,128)(2,1)S(1)}, bf16[32,1536]{1,0:T(8,128)(2,1)S(1)}, u32[]{:S(2)}, u32[]{:S(2)}) collective-permute-start(bf16[32,1536]{1,0:T(8,128)(2,1)S(1)} %get-tuple-element.45.refs_0_), channel_id=1, source_target_pairs={{0,8},{1,9},{2,10},{3,11},{8,0},{9,1},{10,2},{11,3},{16,24},{17,25... | collective-permute-start | bytes 294920 | tf_op jit(solution)/shard_map/ppermute | solution.py:423
  38.8 6.5 %collective-permute-start.7 = (bf16[32,1536]{1,0:T(8,128)(2,1)S(1)}, bf16[32,1536]{1,0:T(8,128)(2,1)S(1)}, u32[]{:S(2)}, u32[]{:S(2)}) collective-permute-start(bf16[32,1536]{1,0:T(8,128)(2,1)S(1)} %get-tuple-element.46.refs_1_), channel_id=1, source_target_pairs={{0,10},{1,11},{2,8},{3,9},{8,2},{9,3},{10,0},{11,1},{16,26},{17,27... | collective-permute-start | bytes 294920 | tf_op jit(solution)/shard_map/ppermute | solution.py:423
  40.0 14.5 %collective-permute-start.8 = (bf16[32,1536]{1,0:T(8,128)(2,1)S(1)}, bf16[32,1536]{1,0:T(8,128)(2,1)S(1)}, u32[]{:S(2)}, u32[]{:S(2)}) collective-permute-start(bf16[32,1536]{1,0:T(8,128)(2,1)S(1)} %get-tuple-element.49.refs_0_), channel_id=1, source_target_pairs={{0,8},{1,9},{2,10},{3,11},{8,0},{9,1},{10,2},{11,3},{16,24},{17,25... | collective-permute-start | bytes 294920 | tf_op jit(solution)/shard_map/ppermute | solution.py:423
  41.5 13.0 %collective-permute-start.9 = (bf16[32,1536]{1,0:T(8,128)(2,1)S(1)}, bf16[32,1536]{1,0:T(8,128)(2,1)S(1)}, u32[]{:S(2)}, u32[]{:S(2)}) collective-permute-start(bf16[32,1536]{1,0:T(8,128)(2,1)S(1)} %get-tuple-element.50.refs_1_), channel_id=1, source_target_pairs={{0,10},{1,11},{2,8},{3,9},{8,2},{9,3},{10,0},{11,1},{16,26},{17,27... | collective-permute-start | bytes 294920 | tf_op jit(solution)/shard_map/ppermute | solution.py:423
  53.5 10.5 %collective-permute-start.13 = (bf16[768,128]{1,0:T(8,128)(2,1)S(1)}, bf16[768,128]{1,0:T(8,128)(2,1)S(1)}, u32[]{:S(2)}, u32[]{:S(2)}) collective-permute-start(bf16[768,128]{1,0:T(8,128)(2,1)S(1)} %project.2.mine_ref), channel_id=1, source_target_pairs={{0,4},{4,0},{1,5},{5,1},{2,6},{6,2},{3,7},{7,3},{8,12},{12,8},{9,1... | collective-permute-start | bytes 589832 | tf_op jit(solution)/shard_map/ppermute | solution.py:401
  62.8 7.2 %collective-permute-start.10 = (bf16[768,128]{1,0:T(8,128)(2,1)S(1)}, bf16[768,128]{1,0:T(8,128)(2,1)S(1)}, u32[]{:S(2)}, u32[]{:S(2)}) collective-permute-start(bf16[768,128]{1,0:T(8,128)(2,1)S(1)} %project.3.mine_ref), channel_id=1, source_target_pairs={{0,4},{4,0},{1,5},{5,1},{2,6},{6,2},{3,7},{7,3},{8,12},{12,8},{9,1... | collective-permute-start | bytes 589832 | tf_op jit(solution)/shard_map/ppermute | solution.py:401
  65.4 6.1 %collective-permute-start.14 = (bf16[2,32,1536]{2,1,0:T(8,128)(2,1)S(1)}, bf16[2,32,1536]{2,1,0:T(8,128)(2,1)S(1)}, u32[]{:S(2)}, u32[]{:S(2)}) collective-permute-start(bf16[2,32,1536]{2,1,0:T(8,128)(2,1)S(1)} %get-tuple-element.60), channel_id=1, source_target_pairs={{0,1},{1,0},{2,3},{3,2},{4,5},{5,4},{6,7},{7,6},{8,9},{9,8},{10,11... | collective-permute-start | bytes 589832 | tf_op jit(solution)/shard_map/ppermute | solution.py:404
  71.4 3.5 %collective-permute-start.11 = (bf16[2,32,1536]{2,1,0:T(8,128)(2,1)S(1)}, bf16[2,32,1536]{2,1,0:T(8,128)(2,1)S(1)}, u32[]{:S(2)}, u32[]{:S(2)}) collective-permute-start(bf16[2,32,1536]{2,1,0:T(8,128)(2,1)S(1)} %get-tuple-element.56), channel_id=1, source_target_pairs={{0,1},{1,0},{2,3},{3,2},{4,5},{5,4},{6,7},{7,6},{8,9},{9,8},{10,11... | collective-permute-start | bytes 589832 | tf_op jit(solution)/shard_map/ppermute | solution.py:404
  72.1 8.3 %collective-permute-start.15 = (bf16[32,1536]{1,0:T(8,128)(2,1)S(1)}, bf16[32,1536]{1,0:T(8,128)(2,1)S(1)}, u32[]{:S(2)}, u32[]{:S(2)}) collective-permute-start(bf16[32,1536]{1,0:T(8,128)(2,1)S(1)} %get-tuple-element.61), channel_id=1, source_target_pairs={{0,4},{1,5},{2,6},{3,7},{4,0},{5,1},{6,2},{7,3},{8,12},{9,13},{10,... | collective-permute-start | bytes 294920 | tf_op jit(solution)/shard_map/ppermute | solution.py:415
  73.3 7.2 %collective-permute-start.16 = (bf16[32,1536]{1,0:T(8,128)(2,1)S(1)}, bf16[32,1536]{1,0:T(8,128)(2,1)S(1)}, u32[]{:S(2)}, u32[]{:S(2)}) collective-permute-start(bf16[32,1536]{1,0:T(8,128)(2,1)S(1)} %get-tuple-element.62), channel_id=1, source_target_pairs={{0,6},{1,7},{2,4},{3,5},{4,2},{5,3},{6,0},{7,1},{8,14},{9,15},{10,... | collective-permute-start | bytes 294920 | tf_op jit(solution)/shard_map/ppermute | solution.py:415
  75.5 6.6 %collective-permute-start.12 = (bf16[32,1536]{1,0:T(8,128)(2,1)S(1)}, bf16[32,1536]{1,0:T(8,128)(2,1)S(1)}, u32[]{:S(2)}, u32[]{:S(2)}) collective-permute-start(bf16[32,1536]{1,0:T(8,128)(2,1)S(1)} %get-tuple-element.58), channel_id=1, source_target_pairs={{0,2},{1,3},{2,0},{3,1},{4,6},{5,7},{6,4},{7,5},{8,10},{9,11},{10,... | collective-permute-start | bytes 294920 | tf_op jit(solution)/shard_map/ppermute | solution.py:407

commit v6 on v5

--- a/solution.py
+++ b/solution.py
@@ -12,7 +12,7 @@
 CHUNKS = 4
 VMEM_BYTES = 8 * 2**20
 GRAD_VMEM_BYTES = 16 * 2**20
-FIRST_VMEM_BYTES = 50 * 2**20
+FIRST_VMEM_BYTES = 46 * 2**20
 VALUE_VMEM_BYTES = 47 * 2**20
 OUT_VMEM_BYTES = 42 * 2**20
 ODD, EVEN, VERSION, CORE, ROW, HALF = range(6)
@@ -51,55 +51,19 @@
     return (jnp.max(note) > 0.5).astype(jnp.int32)
 
 
-def first_project_kernel(
-    index, facts_ref, message_ref, value_ref, out_ref, tokens_ref, partial_ref, held, sems
-):
+def project_kernel(index, facts_ref, message_ref, *refs):
+    tables, (tokens_ref, partial_ref) = refs[:-2], refs[-2:]
     version = picked_version(index, facts_ref, message_ref)
-    step = held.shape[0] // CHUNKS
-
-    def copy(table_ref, chunk):
-        rows = pl.ds(chunk * step, step)
-        return pltpu.make_async_copy(table_ref.at[0, version, rows], held.at[rows], sems.at[chunk])
-
-    def start(table_ref):
-        for chunk in range(CHUNKS):
-            copy(table_ref, chunk).start()
-
-    pl.when(facts_ref[ODD] == 1)(lambda: start(out_ref))
-    pl.when(facts_ref[ODD] == 0)(lambda: start(value_ref))
     flipped = tokens_ref[index].T
-    for chunk in range(CHUNKS):
-        copy(value_ref, chunk).wait()
-        rows = pl.ds(chunk * step, step)
-        partial_ref[rows, :] = matmul(held[rows, :], flipped, NN).astype(jnp.bfloat16)
-
-
-def first_project(index, facts, message, w_value, w_out, tokens):
-    rows, width = w_value.shape[2:]
-    return pl.pallas_call(
-        functools.partial(first_project_kernel, index),
-        out_shape=jax.ShapeDtypeStruct((rows, tokens.shape[1]), jnp.bfloat16),
-        in_specs=[in_smem(), in_vmem(), in_hbm(), in_hbm(), in_vmem()],
-        out_specs=in_vmem(),
-        scratch_shapes=[
-            pltpu.VMEM((rows, width), jnp.bfloat16),
-            pltpu.SemaphoreType.DMA((CHUNKS,)),
-        ],
-        compiler_params=pltpu.CompilerParams(vmem_limit_bytes=FIRST_VMEM_BYTES),
-        cost_estimate=SMALL,
-        name="first_project",
-    )(facts, message, w_value, w_out, tokens)
-
-
-def project_kernel(index, facts_ref, message_ref, value_ref, out_ref, tokens_ref, partial_ref):
-    version = picked_version(index, facts_ref, message_ref)
-    flipped = tokens_ref[0].T
 
     def rows_of(table_ref):
         partial_ref[...] = matmul(table_ref[0, version], flipped, NN).astype(jnp.bfloat16)
 
-    pl.when(facts_ref[ODD] == 1)(lambda: rows_of(value_ref))
-    pl.when(facts_ref[ODD] == 0)(lambda: rows_of(out_ref))
+    if len(tables) == 1:
+        rows_of(tables[0])
+    else:
+        pl.when(facts_ref[ODD] == 1)(lambda: rows_of(tables[0]))
+        pl.when(facts_ref[ODD] == 0)(lambda: rows_of(tables[1]))
 
 
 def project(index, facts, message, tables, tokens):
@@ -107,7 +71,7 @@
     return pl.pallas_call(
         functools.partial(project_kernel, index),
         out_shape=jax.ShapeDtypeStruct((rows, tokens.shape[1]), jnp.bfloat16),
-        in_specs=[in_smem()] + [in_vmem()] * 4,
+        in_specs=[in_smem()] + [in_vmem()] * (2 + len(tables)),
         out_specs=in_vmem(),
         compiler_params=pltpu.CompilerParams(vmem_limit_bytes=VMEM_BYTES),
         cost_estimate=SMALL,
@@ -172,24 +136,24 @@
     )(facts, messages[1], w_value, mine, arrived, messages[index])
 
 
-def combine_kernel(outer, last, facts_ref, keep_ref, arrived_ref, addend_ref, *refs):
+def combine_kernel(outer, last, index, facts_ref, keep_ref, arrived_ref, addend_ref, *refs):
     first_refs, sent_refs = refs[:-outer], refs[-outer:]
     for delta in range(outer):
         spot = facts_ref[ROW] ^ delta
         total = keep_ref[spot].astype(jnp.float32) + arrived_ref[spot].astype(jnp.float32)
         if delta == 0:
-            total = total + addend_ref[...].astype(jnp.float32)
+            total = total + addend_ref[index].astype(jnp.float32)
         total = total.astype(jnp.bfloat16)
         if last:
             total = jnp.where(facts_ref[ODD] == 1, first_refs[delta][...], total)
         sent_refs[delta][...] = total
 
 
-def combine(facts, keep, arrived, addend, first_sent=()):
+def combine(index, facts, keep, arrived, addend, first_sent=()):
     outer, shard, width = keep.shape
     piece = jax.ShapeDtypeStruct((shard, width), jnp.bfloat16)
     return pl.pallas_call(
-        functools.partial(combine_kernel, outer, len(first_sent) > 0),
+        functools.partial(combine_kernel, outer, len(first_sent) > 0, index),
         out_shape=(piece,) * outer,
         in_specs=[in_smem()] + [in_vmem()] * (3 + len(first_sent)),
         out_specs=(in_vmem(),) * outer,
@@ -228,12 +192,12 @@
     )(facts, *own_parts, *other_parts)
 
 
-def weight_grad_kernel(facts_ref, a0, a1, b0, b1, first, second0, second1, value_ref, out_ref):
+def weight_grad_kernel(facts_ref, a0, a1, b0, b1, first, second, value_ref, out_ref):
     odd = facts_ref[ODD] == 1
     tokens = a0.shape[1]
     left_first = jnp.concatenate([a0[...], a1[...]], axis=1)
     left_second = jnp.concatenate([b0[...], b1[...]], axis=1)
-    right_second = jnp.concatenate([second0[0], second1[0]], axis=0)
+    right_second = second[...].reshape(2 * tokens, second.shape[2])
     right_first = first[...].reshape(2 * tokens, first.shape[2])
     grad_first = matmul(left_first, right_second, NN)
     grad_second = matmul(left_second, right_first, NN)
@@ -248,22 +212,48 @@
     grad = jax.ShapeDtypeStruct((1, rows, width), jnp.bfloat16)
     left = pl.BlockSpec((step, tokens), lambda i: (i, 0))
     both = pl.BlockSpec((2, tokens, width), lambda i: (0, 0, 0))
-    right = pl.BlockSpec((1, tokens, width), lambda i: (0, 0, 0))
     wide = pl.BlockSpec((1, step, width), lambda i: (0, i, 0))
     return pl.pallas_call(
         weight_grad_kernel,
         grid=(CHUNKS,),
         out_shape=(grad, grad),
-        in_specs=[in_smem()] + [left] * 4 + [both, right, right],
+        in_specs=[in_smem()] + [left] * 4 + [both] * 2,
         out_specs=(wide, wide),
         compiler_params=pltpu.CompilerParams(vmem_limit_bytes=GRAD_VMEM_BYTES),
         cost_estimate=SMALL,
         name="weight_grads",
-    )(facts, *first_results, *second_results, first_full, *second_full)
+    )(facts, *first_results, *second_results, first_full, second_full)
+
+
+def load(source_ref, table_ref, sems):
+    step = table_ref.shape[2] // CHUNKS
+    copies = []
+    for version in range(2):
+        for chunk in range(CHUNKS):
+            spot = (slice(None), version, pl.ds(chunk * step, step))
+            copies.append(
+                pltpu.make_async_copy(
+                    source_ref.at[spot], table_ref.at[spot], sems.at[version * CHUNKS + chunk]
+                )
+            )
+    return copies
 
 
 def pack_kernel(
-    facts_ref, query_ref, key_ref, input_ref, message_ref, own_ref, query_held, key_held, input_held, sems
+    facts_ref,
+    query_ref,
+    key_ref,
+    input_ref,
+    value_ref,
+    out_ref,
+    message_ref,
+    own_ref,
+    table_ref,
+    query_held,
+    key_held,
+    input_held,
+    sems,
+    table_sems,
 ):
     pairs = ((query_ref, query_held), (key_ref, key_held), (input_ref, input_held))
     copies = [
@@ -271,6 +261,17 @@
     ]
     for copy in copies:
         copy.start()
+
+    @pl.when(facts_ref[ODD] == 1)
+    def _():
+        for copy in load(out_ref, table_ref, table_sems):
+            copy.start()
+
+    @pl.when(facts_ref[ODD] == 0)
+    def _():
+        for copy in load(value_ref, table_ref, table_sems):
+            copy.start()
+
     tokens = query_ref.shape[2]
     shard, width = own_ref.shape
     heads = query_ref.shape[1] // HEAD_DIM
@@ -295,9 +296,11 @@
         message_ref[start : start + shard, :] = other[:, block * LANES : (block + 1) * LANES]
     note = jnp.zeros((NOTE_ROWS, LANES), jnp.int32) + facts_ref[VERSION]
     message_ref[message_ref.shape[0] - NOTE_ROWS :, :] = note.astype(jnp.bfloat16)
-
-
-def pack(facts, query, key_stash, section_input):
+    for copy in load(value_ref, table_ref, table_sems):
+        copy.wait()
+
+
+def pack(facts, query, key_stash, section_input, w_value, w_out):
     rows, tokens = query.shape[1:]
     shard = section_input.shape[1]
     width = section_input.shape[2] // 2
@@ -307,32 +310,25 @@
         out_shape=(
             jax.ShapeDtypeStruct((length, LANES), jnp.bfloat16),
             jax.ShapeDtypeStruct((shard, width), jnp.bfloat16),
+            jax.ShapeDtypeStruct(w_value.shape, jnp.bfloat16),
         ),
-        in_specs=[in_smem(), in_place(), in_place(), in_place()],
-        out_specs=(in_vmem(), in_vmem()),
+        in_specs=[in_smem(), in_place(), in_place(), in_place(), in_hbm(), in_hbm()],
+        out_specs=(in_vmem(), in_vmem(), in_vmem()),
         scratch_shapes=[
             pltpu.VMEM(query.shape, jnp.bfloat16),
             pltpu.VMEM(query.shape, jnp.bfloat16),
             pltpu.VMEM(section_input.shape, jnp.bfloat16),
             pltpu.SemaphoreType.DMA((3,)),
+            pltpu.SemaphoreType.DMA((2 * CHUNKS,)),
         ],
-        compiler_params=pltpu.CompilerParams(vmem_limit_bytes=VMEM_BYTES),
+        compiler_params=pltpu.CompilerParams(vmem_limit_bytes=FIRST_VMEM_BYTES),
         cost_estimate=SMALL,
         name="pack",
-    )(facts, query, key_stash, section_input)
+    )(facts, query, key_stash, section_input, w_value, w_out)
 
 
 def load_kernel(source_ref, table_ref, sems):
-    step = table_ref.shape[2] // CHUNKS
-    copies = []
-    for version in range(2):
-        for chunk in range(CHUNKS):
-            spot = (slice(None), version, pl.ds(chunk * step, step))
-            copies.append(
-                pltpu.make_async_copy(
-                    source_ref.at[spot], table_ref.at[spot], sems.at[version * CHUNKS + chunk]
-                )
-            )
+    copies = load(source_ref, table_ref, sems)
     for copy in copies:
         copy.start()
     for copy in copies:
@@ -352,37 +348,38 @@
     )(table)
 
 
-def arrive_kernel(index, heads, facts_ref, input_ref, *refs):
-    parts, piece_ref = refs[:-1], refs[-1]
-    shard, width = piece_ref.shape
+def arrive_kernel(outer, facts_ref, own_ref, message_ref, *refs):
+    parts, pair_ref = refs[:-1], refs[-1]
+    shard, width = own_ref.shape
 
     @pl.when(facts_ref[ODD] == 1)
     def _():
-        if index == 0:
-            piece_ref[...] = input_ref[...]
-        else:
-            for block in range(width // LANES):
-                start = heads * LANES + block * shard
-                piece_ref[:, block * LANES : (block + 1) * LANES] = input_ref[start : start + shard, :]
+        pair_ref[0] = own_ref[...]
+        first_row = message_ref.shape[0] - NOTE_ROWS - width // LANES * shard
+        for block in range(width // LANES):
+            start = first_row + block * shard
+            columns = pl.ds(block * LANES, LANES)
+            pair_ref[1, :, columns] = message_ref[start : start + shard, :]
 
     @pl.when(facts_ref[ODD] == 0)
     def _():
-        total = parts[0][...].astype(jnp.float32)
-        for part in parts[1:]:
-            total = total + part[...].astype(jnp.float32)
-        piece_ref[...] = total.astype(jnp.bfloat16)
-
-
-def arrive(index, heads, facts, source, parts):
-    return pl.pallas_call(
-        functools.partial(arrive_kernel, index, heads),
-        out_shape=jax.ShapeDtypeStruct(parts[0].shape, jnp.bfloat16),
-        in_specs=[in_smem()] + [in_vmem()] * (1 + len(parts)),
+        for index in range(2):
+            total = parts[index * outer][...].astype(jnp.float32)
+            for part in parts[index * outer + 1 : (index + 1) * outer]:
+                total = total + part[...].astype(jnp.float32)
+            pair_ref[index] = total.astype(jnp.bfloat16)
+
+
+def arrive(facts, input_own, message, parts):
+    return pl.pallas_call(
+        functools.partial(arrive_kernel, len(parts) // 2),
+        out_shape=jax.ShapeDtypeStruct((2,) + input_own.shape, jnp.bfloat16),
+        in_specs=[in_smem()] + [in_vmem()] * (2 + len(parts)),
         out_specs=in_vmem(),
         compiler_params=pltpu.CompilerParams(vmem_limit_bytes=VMEM_BYTES),
         cost_estimate=SMALL,
         name="arrive",
-    )(facts, source, *parts)
+    )(facts, input_own, message, *parts)
 
 
 def on_device(section_input, query, key_stash, incoming, version, w_value, w_out):
@@ -428,50 +425,47 @@
     def other_columns(array):
         return lax.dynamic_slice_in_dim(array, (1 - half) * width, width, 1)
 
-    def gathered(pieces):
-        return lax.all_gather(jnp.stack(pieces), "tensor", axis=1, tiled=True)
-
-    heads = query.shape[1] // HEAD_DIM
+    def gathered(pair):
+        return lax.all_gather(pair, "tensor", axis=1, tiled=True)
+
     facts = jnp.stack([odd_flag, 1 - odd_flag, version[0], core, row, half])
     first = jnp.where(odd, incoming[0], section_input[0])
-    first_piece = [own_columns(first), swap_half(other_columns(first))]
-    own_message, input_own = pack(facts, query, key_stash, section_input)
+    first_pair = jnp.stack([own_columns(first), swap_half(other_columns(first))])
+    own_message, input_own, first_table = pack(
+        facts, query, key_stash, section_input, w_value, w_out
+    )
     other_message = swap_half(own_message)
-    first_full = gathered(first_piece)
+    first_full = gathered(first_pair)
     first_full, other_message = lax.optimization_barrier((first_full, other_message))
     messages = [own_message, other_message]
 
     partial = [None, None]
-    partial[1] = first_project(1, facts, other_message, w_value, w_out, first_full)
-    partial[0] = first_project(0, facts, other_message, w_value, w_out, first_full)
+    for m in (1, 0):
+        partial[m] = project(m, facts, other_message, (first_table,), first_full)
     arrived = [swap_half(partial[1]), swap_half(partial[0])]
     later_value, _ = lax.optimization_barrier((w_value, partial))
     value_table = load_table(later_value, VALUE_VMEM_BYTES)
     first_result, first_sent = [None, None], [None, None]
-    second_piece, second_full = [None, None], [None, None]
     for m in range(2):
         first_result[m], keep, send = mix(
             ODD, m, facts, messages, value_table, partial[m], arrived[m], outer
         )
-        first_sent[m] = combine(facts, keep, swap_core(send), first_piece[m])
+        first_sent[m] = combine(m, facts, keep, swap_core(send), first_pair)
     later_out, _ = lax.optimization_barrier((w_out, first_sent))
     out_table = load_table(later_out, OUT_VMEM_BYTES)
-    input_own, other_input, _ = lax.optimization_barrier((input_own, other_message, out_table))
+    input_own, _ = lax.optimization_barrier((input_own, out_table))
+    received = [swap_section(part, d) for m in range(2) for d, part in enumerate(first_sent[m])]
+    second_pair = arrive(facts, input_own, other_message, received)
+    second_full = gathered(second_pair)
     for m in range(2):
-        received = [swap_section(part, d) for d, part in enumerate(first_sent[m])]
-        source = other_input if m else input_own
-        second_piece[m] = arrive(m, heads, facts, source, received)
-    tables = (value_table, out_table)
-    for m in range(2):
-        second_full[m] = gathered([second_piece[m]])
-        partial[m] = project(m, facts, other_message, tables, second_full[m])
+        partial[m] = project(m, facts, other_message, (value_table, out_table), second_full)
     arrived = [swap_half(partial[1]), swap_half(partial[0])]
     second_result, last_sent = [None, None], [None, None]
     for m in (1, 0):
         second_result[m], keep, send = mix(
             EVEN, m, facts, messages, value_table, partial[m], arrived[m], outer
         )
-        last_sent[m] = combine(facts, keep, swap_core(send), second_piece[m], first_sent[m])
+        last_sent[m] = combine(m, facts, keep, swap_core(send), second_pair, first_sent[m])
     other_parts = [to_other_half(part, d) for d, part in enumerate(last_sent[1])]
     own_parts = [last_sent[0][0]] + [to_row(part, d + 1) for d, part in enumerate(last_sent[0][1:])]
     second_result, _ = lax.optimization_barrier((second_result, last_sent))

time: 83.6 us -> 82.8 us (level)
  waiting for transfers between devices: 9.65 us -> 16.3 us
  blocking collectives: 21.6 us -> 17.5 us
  Pallas kernels: 30.2 us -> 27 us
    pallas_call x4 -> x1, Pallas kernels: 8.17 us -> 0.6 us  [arrive(): pl.pallas_call(functools.partial(arrive_kernel, len(parts) // 2), out_sha...]
    all_gather x3 -> x2, blocking collectives: 21.6 us -> 17.5 us  [gathered(): return lax.all_gather(pair, 'tensor', axis=1, tiled=True)]
    ppermute x4, waiting for transfers between devices: 1.27 us -> 5.05 us  [swap_section(): return lax.ppermute(array, ('pair', 'tensor'), pairs)]
    ppermute x6, waiting for transfers between devices: 6.77 us -> 10.3 us  [swap_half(): return lax.ppermute(array, 'half', [(0, 1), (1, 0)])]
    pallas_call x2 -> x4, Pallas kernels: 2.76 us -> 5.46 us  [project(): pl.pallas_call(functools.partial(project_kernel, index), out_shape=jax.Sh...]
    pallas_call x1, Pallas kernels: 2.09 us -> 3.71 us  [pack(): pl.pallas_call(pack_kernel, out_shape=(jax.ShapeDtypeStruct((length, LANE...]
    ppermute x1, waiting for transfers between devices: 1.59 us -> 0.01 us  [to_row(): lax.ppermute(array, 'tensor', [(i, i ^ 2 * delta) for i in range(n_tensor)])]
    ppermute x2, waiting for transfers between devices: 0.01 us -> 0.9 us  [to_other_half(): return lax.ppermute(array, ('half', 'tensor'), pairs)]
  transfers between devices with their start and end apart: 17 -> 17, of which waited for: 5 -> 9; matrix products, arithmetic and copies ran while one was open for 0% -> 0% of each run, Pallas kernels for 30% -> 27%
where the time goes in v6:
time: 82.8 us; the launch traced here: 82.5 us
  Pallas kernels  27 us (33%)
  blocking collectives  17.5 us (21%)
  starting transfers between devices  16.4 us (20%)
  waiting for transfers between devices  16.3 us (20%)
  local copies, waits for them, and re-layouts  2.9 us (4%)
  between operations  1.51 us (2%)
  other arithmetic  0.98 us (1%)
    all_gather x2, blocking collectives, gathered(): return lax.all_gather(pair, 'tensor', axis=1, tiled=True)  17.5 us
    ppermute x6, waiting for transfers between devices, swap_half(): return lax.ppermute(array, 'half', [(0, 1), (1, 0)])  10.3 us
    ppermute x6, starting transfers between devices, swap_half(): return lax.ppermute(array, 'half', [(0, 1), (1, 0)])  7.41 us
    pallas_call x4, Pallas kernels, mix(): pl.pallas_call(functools.partial(mix_kernel, outer, natural, index), out_...  5.86 us
    pallas_call x4, Pallas kernels, project(): pl.pallas_call(functools.partial(project_kernel, index), out_shape=jax.Sh...  5.46 us
    ppermute x4, starting transfers between devices, swap_section(): return lax.ppermute(array, ('pair', 'tensor'), pairs)  5.08 us
    ppermute x4, waiting for transfers between devices, swap_section(): return lax.ppermute(array, ('pair', 'tensor'), pairs)  5.05 us
    pallas_call x1, Pallas kernels, weight_grads(): pl.pallas_call(weight_grad_kernel, grid=(CHUNKS,), out_shape=(grad, grad)...  4.08 us
  transfers between devices with their start and end apart: 17, of which 9 were waited for; matrix products, arithmetic and copies ran while one was open for 0% of the time, Pallas kernels for 27%

profile of v6, /device:TPU:0, one launch (start us, length us, event | category | flops | bytes accessed | tf_op | source)
XLA Modules:
  0.0 82.5 jit_solution(12585265760815948226)
XLA Ops:
  0.6 1.0 %broadcast_select_fusion = bf16[1,32,3072]{2,1,0:T(8,128)(2,1)S(1)} fusion(bf16[1,32,3072]{2,1,0:T(8,128)(2,1)} %param.10, bf16[1,32,3072]{2,1,0:T(8,128)(2,1)} %input_ref.1, pred[]{:T(512)S(6)} %eq.6), kind=kLoop, calls=%fused_computation.1 | loop fusion | flops 98304 | bytes 589825 | tf_op jit(solution)/shard_map/jit(_where)/select_n | solution.py:432
  1.6 3.0 %collective-permute-start = (bf16[32,1536]{1,0:T(8,128)(2,1)S(1)}, bf16[32,1536]{1,0:T(8,128)(2,1)S(1)}, u32[]{:S(2)}, u32[]{:S(2)}) collective-permute-start(bf16[32,1536]{1,0:T(8,128)(2,1)S(1)} %get-tuple-element.76), channel_id=1, source_target_pairs={{0,4},{4,0},{1,5},{5,1},{2,6},{6,2},{3,7},{7,3},{8,12},{12,8},{9,1... | collective-permute-start | bytes 294920 | tf_op jit(solution)/shard_map/ppermute | solution.py:398
  8.2 3.7 %pack.1 = (bf16[1424,128]{1,0:T(8,128)(2,1)S(1)}, bf16[32,1536]{1,0:T(8,128)(2,1)S(1)}, bf16[1,2,768,1536]{3,2,1,0:T(8,128)(2,1)S(1)}) custom-call(s32[6]{0:T(128)S(1)} %stack.30.facts_ref, bf16[1,768,128]{2,1,0:T(8,128)(2,1)S(1)} %copy-done.1, bf16[1,768,128]{2,1,0:T(8,128)(2,1)S(1)} %copy-done.2, bf16[1,32,3072]{2,1,0:T(8,128)(2,1)S(1)} %copy-done, ...), custom_call_target="tpu_custom_call" | custom-call | flops 1 | bytes 1 | tf_op jit(solution)/shard_map/pack/pallas_call | solution.py:308
  12.0 9.1 %all_gather.6.refs_1_.first = bf16[2,128,1536]{2,1,0:T(8,128)(2,1)S(1)} all-gather(bf16[2,32,1536]{2,1,0:T(8,128)(2,1)S(1)} %pad_maximum_fusion.addend_ref), channel_id=1, replica_groups=mesh['pair'=4,'half'=2,'tensor'=4] {'tensor'}, dimensions={1}, use_global_device_ids=true | all-gather | bytes 983040 | tf_op jit(solution)/shard_map/all_gather | solution.py:429
  21.9 1.4 %project.5.mine_ref = bf16[768,128]{1,0:T(8,128)(2,1)S(1)} custom-call(s32[6]{0:T(128)S(1)} %stack.30.facts_ref, bf16[1424,128]{1,0:T(8,128)(2,1)S(1)} %collective-permute-done.1.message_ref.probs_ref, bf16[1,2,768,1536]{3,2,1,0:T(8,128)(2,1)S(1)} %get-tuple-element.41.refs_0_, bf16[2,128,1536]{2,1,0:T(8,128)(2,1)S(1)} %all_gather.6.refs_1_.first), custom_call_target="tpu_custom_call" | custom-call | flops 1 | bytes 1 | tf_op jit(solution)/shard_map/project/pallas_call | solution.py:71
  24.1 1.3 %project.4.mine_ref = bf16[768,128]{1,0:T(8,128)(2,1)S(1)} custom-call(s32[6]{0:T(128)S(1)} %stack.30.facts_ref, bf16[1424,128]{1,0:T(8,128)(2,1)S(1)} %collective-permute-done.1.message_ref.probs_ref, bf16[1,2,768,1536]{3,2,1,0:T(8,128)(2,1)S(1)} %get-tuple-element.41.refs_0_, bf16[2,128,1536]{2,1,0:T(8,128)(2,1)S(1)} %all_gather.6.refs_1_.first), custom_call_target="tpu_custom_call" | custom-call | flops 1 | bytes 1 | tf_op jit(solution)/shard_map/project/pallas_call | solution.py:71
  25.4 1.4 %collective-permute-start.4 = (bf16[768,128]{1,0:T(8,128)(2,1)S(1)}, bf16[768,128]{1,0:T(8,128)(2,1)S(1)}, u32[]{:S(2)}, u32[]{:S(2)}) collective-permute-start(bf16[768,128]{1,0:T(8,128)(2,1)S(1)} %project.4.mine_ref), channel_id=1, source_target_pairs={{0,4},{4,0},{1,5},{5,1},{2,6},{6,2},{3,7},{7,3},{8,12},{12,8},{9,1... | collective-permute-start | bytes 589832 | tf_op jit(solution)/shard_map/ppermute | solution.py:398
  26.8 2.5 %load_table.2.value_ref.refs_0_ = bf16[1,2,768,1536]{3,2,1,0:T(8,128)(2,1)S(1)} custom-call(bf16[1,2,768,1536]{3,2,1,0:T(8,128)(2,1)} %source_ref), custom_call_target="tpu_custom_call" | custom-call | flops 1 | bytes 1 | tf_op jit(solution)/shard_map/load_table/pallas_call | solution.py:339
  29.3 1.9 %collective-permute-done.2.arrived_ref = bf16[768,128]{1,0:T(8,128)(2,1)S(1)} collective-permute-done((bf16[768,128]{1,0:T(8,128)(2,1)S(1)}, bf16[768,128]{1,0:T(8,128)(2,1)S(1)}, u32[]{:S(2)}, u32[]{:S(2)}) %collective-permute-start.2) | collective-permute-done | bytes 196640 | tf_op jit(solution)/shard_map/ppermute | solution.py:398
  31.2 1.5 %mix.4 = (bf16[768,128]{1,0:T(8,128)(2,1)S(1)}, bf16[2,32,1536]{2,1,0:T(8,128)(2,1)S(1)}, bf16[2,32,1536]{2,1,0:T(8,128)(2,1)S(1)}) custom-call(s32[6]{0:T(128)S(1)} %stack.30.facts_ref, bf16[1424,128]{1,0:T(8,128)(2,1)S(1)} %collective-permute-done.1.message_ref.probs_ref, bf16[1,2,768,1536]{3,2,1,0:T(8,128)(2,1)S(1)} %load_table.2.value_ref.refs_0_, ...), custom_call_target="tpu_custom_call" | custom-call | flops 1 | bytes 1 | tf_op jit(solution)/shard_map/mix/pallas_call | solution.py:128
  32.8 1.2 %collective-permute-done.4.arrived_ref = bf16[768,128]{1,0:T(8,128)(2,1)S(1)} collective-permute-done((bf16[768,128]{1,0:T(8,128)(2,1)S(1)}, bf16[768,128]{1,0:T(8,128)(2,1)S(1)}, u32[]{:S(2)}, u32[]{:S(2)}) %collective-permute-start.4) | collective-permute-done | bytes 196640 | tf_op jit(solution)/shard_map/ppermute | solution.py:398
  34.0 1.6 %mix.5 = (bf16[768,128]{1,0:T(8,128)(2,1)S(1)}, bf16[2,32,1536]{2,1,0:T(8,128)(2,1)S(1)}, bf16[2,32,1536]{2,1,0:T(8,128)(2,1)S(1)}) custom-call(s32[6]{0:T(128)S(1)} %stack.30.facts_ref, bf16[1424,128]{1,0:T(8,128)(2,1)S(1)} %collective-permute-done.1.message_ref.probs_ref, bf16[1,2,768,1536]{3,2,1,0:T(8,128)(2,1)S(1)} %load_table.2.value_ref.refs_0_, ...), custom_call_target="tpu_custom_call" | custom-call | flops 1 | bytes 1 | tf_op jit(solution)/shard_map/mix/pallas_call | solution.py:128
  36.3 1.5 %collective-permute-start.6 = (bf16[32,1536]{1,0:T(8,128)(2,1)S(1)}, bf16[32,1536]{1,0:T(8,128)(2,1)S(1)}, u32[]{:S(2)}, u32[]{:S(2)}) collective-permute-start(bf16[32,1536]{1,0:T(8,128)(2,1)S(1)} %get-tuple-element.46.refs_0_), channel_id=1, source_target_pairs={{0,8},{1,9},{2,10},{3,11},{8,0},{9,1},{10,2},{11,3},{16,24},{17,25... | collective-permute-start | bytes 294920 | tf_op jit(solution)/shard_map/ppermute | solution.py:420
  39.2 1.5 %collective-permute-start.8 = (bf16[32,1536]{1,0:T(8,128)(2,1)S(1)}, bf16[32,1536]{1,0:T(8,128)(2,1)S(1)}, u32[]{:S(2)}, u32[]{:S(2)}) collective-permute-start(bf16[32,1536]{1,0:T(8,128)(2,1)S(1)} %get-tuple-element.50.refs_0_), channel_id=1, source_target_pairs={{0,8},{1,9},{2,10},{3,11},{8,0},{9,1},{10,2},{11,3},{16,24},{17,25... | collective-permute-start | bytes 294920 | tf_op jit(solution)/shard_map/ppermute | solution.py:420
  40.7 1.3 %collective-permute-start.9 = (bf16[32,1536]{1,0:T(8,128)(2,1)S(1)}, bf16[32,1536]{1,0:T(8,128)(2,1)S(1)}, u32[]{:S(2)}, u32[]{:S(2)}) collective-permute-start(bf16[32,1536]{1,0:T(8,128)(2,1)S(1)} %get-tuple-element.51.refs_1_), channel_id=1, source_target_pairs={{0,10},{1,11},{2,8},{3,9},{8,2},{9,3},{10,0},{11,1},{16,26},{17,27... | collective-permute-start | bytes 294920 | tf_op jit(solution)/shard_map/ppermute | solution.py:420
  42.0 1.0 %load_table.3.refs_1_ = bf16[1,2,768,1536]{3,2,1,0:T(8,128)(2,1)S(1)} custom-call(bf16[1,2,768,1536]{3,2,1,0:T(8,128)(2,1)S(1)} %bitcast.9), custom_call_target="tpu_custom_call" | custom-call | flops 1 | bytes 1 | tf_op jit(solution)/shard_map/load_table/pallas_call | solution.py:339
  43.0 1.3 %collective-permute-done.7.refs_1_ = bf16[32,1536]{1,0:T(8,128)(2,1)S(1)} collective-permute-done((bf16[32,1536]{1,0:T(8,128)(2,1)S(1)}, bf16[32,1536]{1,0:T(8,128)(2,1)S(1)}, u32[]{:S(2)}, u32[]{:S(2)}) %collective-permute-start.7) | collective-permute-done | bytes 98336 | tf_op jit(solution)/shard_map/ppermute | solution.py:420
  44.3 1.8 %collective-permute-done.8.refs_2_ = bf16[32,1536]{1,0:T(8,128)(2,1)S(1)} collective-permute-done((bf16[32,1536]{1,0:T(8,128)(2,1)S(1)}, bf16[32,1536]{1,0:T(8,128)(2,1)S(1)}, u32[]{:S(2)}, u32[]{:S(2)}) %collective-permute-start.8) | collective-permute-done | bytes 98336 | tf_op jit(solution)/shard_map/ppermute | solution.py:420
  46.1 1.9 %collective-permute-done.9.refs_3_ = bf16[32,1536]{1,0:T(8,128)(2,1)S(1)} collective-permute-done((bf16[32,1536]{1,0:T(8,128)(2,1)S(1)}, bf16[32,1536]{1,0:T(8,128)(2,1)S(1)}, u32[]{:S(2)}, u32[]{:S(2)}) %collective-permute-start.9) | collective-permute-done | bytes 98336 | tf_op jit(solution)/shard_map/ppermute | solution.py:420
  48.7 8.3 %all_gather.7.refs_2_.second = bf16[2,128,1536]{2,1,0:T(8,128)(2,1)S(1)} all-gather(bf16[2,32,1536]{2,1,0:T(8,128)(2,1)S(1)} %arrive.1.addend_ref), channel_id=1, replica_groups=mesh['pair'=4,'half'=2,'tensor'=4] {'tensor'}, dimensions={1}, use_global_device_ids=true | all-gather | bytes 983040 | tf_op jit(solution)/shard_map/all_gather | solution.py:429
  57.0 1.4 %project.7.mine_ref = bf16[768,128]{1,0:T(8,128)(2,1)S(1)} custom-call(s32[6]{0:T(128)S(1)} %stack.30.facts_ref, bf16[1424,128]{1,0:T(8,128)(2,1)S(1)} %collective-permute-done.1.message_ref.probs_ref, bf16[1,2,768,1536]{3,2,1,0:T(8,128)(2,1)S(1)} %load_table.2.value_ref.refs_0_, bf16[1,2,768,1536]{3,2,1,0:T(8,128)(2,1)S(1)} %load_table.3.refs_1_, ...), custom_call_target="tpu_custom_call" | custom-call | flops 1 | bytes 1 | tf_op jit(solution)/shard_map/project/pallas_call | solution.py:71
  58.5 1.6 %collective-permute-start.10 = (bf16[768,128]{1,0:T(8,128)(2,1)S(1)}, bf16[768,128]{1,0:T(8,128)(2,1)S(1)}, u32[]{:S(2)}, u32[]{:S(2)}) collective-permute-start(bf16[768,128]{1,0:T(8,128)(2,1)S(1)} %project.7.mine_ref), channel_id=1, source_target_pairs={{0,4},{4,0},{1,5},{5,1},{2,6},{6,2},{3,7},{7,3},{8,12},{12,8},{9,1... | collective-permute-start | bytes 589832 | tf_op jit(solution)/shard_map/ppermute | solution.py:398
  60.0 1.3 %project.6.mine_ref = bf16[768,128]{1,0:T(8,128)(2,1)S(1)} custom-call(s32[6]{0:T(128)S(1)} %stack.30.facts_ref, bf16[1424,128]{1,0:T(8,128)(2,1)S(1)} %collective-permute-done.1.message_ref.probs_ref, bf16[1,2,768,1536]{3,2,1,0:T(8,128)(2,1)S(1)} %load_table.2.value_ref.refs_0_, bf16[1,2,768,1536]{3,2,1,0:T(8,128)(2,1)S(1)} %load_table.3.refs_1_, ...), custom_call_target="tpu_custom_call" | custom-call | flops 1 | bytes 1 | tf_op jit(solution)/shard_map/project/pallas_call | solution.py:71
  61.9 4.3 %collective-permute-done.10.arrived_ref = bf16[768,128]{1,0:T(8,128)(2,1)S(1)} collective-permute-done((bf16[768,128]{1,0:T(8,128)(2,1)S(1)}, bf16[768,128]{1,0:T(8,128)(2,1)S(1)}, u32[]{:S(2)}, u32[]{:S(2)}) %collective-permute-start.10) | collective-permute-done | bytes 196640 | tf_op jit(solution)/shard_map/ppermute | solution.py:398
  66.2 1.4 %mix.6 = (bf16[768,128]{1,0:T(8,128)(2,1)S(1)}, bf16[2,32,1536]{2,1,0:T(8,128)(2,1)S(1)}, bf16[2,32,1536]{2,1,0:T(8,128)(2,1)S(1)}) custom-call(s32[6]{0:T(128)S(1)} %stack.30.facts_ref, bf16[1424,128]{1,0:T(8,128)(2,1)S(1)} %collective-permute-done.1.message_ref.probs_ref, bf16[1,2,768,1536]{3,2,1,0:T(8,128)(2,1)S(1)} %load_table.2.value_ref.refs_0_, ...), custom_call_target="tpu_custom_call" | custom-call | flops 1 | bytes 1 | tf_op jit(solution)/shard_map/mix/pallas_call | solution.py:128
  67.7 2.2 %collective-permute-done.13.arrived_ref = bf16[768,128]{1,0:T(8,128)(2,1)S(1)} collective-permute-done((bf16[768,128]{1,0:T(8,128)(2,1)S(1)}, bf16[768,128]{1,0:T(8,128)(2,1)S(1)}, u32[]{:S(2)}, u32[]{:S(2)}) %collective-permute-start.13) | collective-permute-done | bytes 196640 | tf_op jit(solution)/shard_map/ppermute | solution.py:398
  69.9 1.4 %mix.7 = (bf16[768,128]{1,0:T(8,128)(2,1)S(1)}, bf16[2,32,1536]{2,1,0:T(8,128)(2,1)S(1)}, bf16[2,32,1536]{2,1,0:T(8,128)(2,1)S(1)}) custom-call(s32[6]{0:T(128)S(1)} %stack.30.facts_ref, bf16[1424,128]{1,0:T(8,128)(2,1)S(1)} %collective-permute-done.1.message_ref.probs_ref, bf16[1,2,768,1536]{3,2,1,0:T(8,128)(2,1)S(1)} %load_table.2.value_ref.refs_0_, ...), custom_call_target="tpu_custom_call" | custom-call | flops 1 | bytes 1 | tf_op jit(solution)/shard_map/mix/pallas_call | solution.py:128
  72.0 1.1 %collective-permute-start.12 = (bf16[32,1536]{1,0:T(8,128)(2,1)S(1)}, bf16[32,1536]{1,0:T(8,128)(2,1)S(1)}, u32[]{:S(2)}, u32[]{:S(2)}) collective-permute-start(bf16[32,1536]{1,0:T(8,128)(2,1)S(1)} %get-tuple-element.58), channel_id=1, source_target_pairs={{0,2},{1,3},{2,0},{3,1},{4,6},{5,7},{6,4},{7,5},{8,10},{9,11},{10,... | collective-permute-start | bytes 294920 | tf_op jit(solution)/shard_map/ppermute | solution.py:404
  73.7 1.6 %collective-permute-start.15 = (bf16[32,1536]{1,0:T(8,128)(2,1)S(1)}, bf16[32,1536]{1,0:T(8,128)(2,1)S(1)}, u32[]{:S(2)}, u32[]{:S(2)}) collective-permute-start(bf16[32,1536]{1,0:T(8,128)(2,1)S(1)} %get-tuple-element.61), channel_id=1, source_target_pairs={{0,4},{1,5},{2,6},{3,7},{4,0},{5,1},{6,2},{7,3},{8,12},{9,13},{10,... | collective-permute-start | bytes 294920 | tf_op jit(solution)/shard_map/ppermute | solution.py:412
  75.3 1.0 %collective-permute-start.16 = (bf16[32,1536]{1,0:T(8,128)(2,1)S(1)}, bf16[32,1536]{1,0:T(8,128)(2,1)S(1)}, u32[]{:S(2)}, u32[]{:S(2)}) collective-permute-start(bf16[32,1536]{1,0:T(8,128)(2,1)S(1)} %get-tuple-element.62), channel_id=1, source_target_pairs={{0,6},{1,7},{2,4},{3,5},{4,2},{5,3},{6,0},{7,1},{8,14},{9,15},{10,... | collective-permute-start | bytes 294920 | tf_op jit(solution)/shard_map/ppermute | solution.py:412
  76.3 4.1 %weight_grads.1 = (bf16[1,768,1536]{2,1,0:T(8,128)(2,1)}, bf16[1,768,1536]{2,1,0:T(8,128)(2,1)}) custom-call(s32[6]{0:T(128)S(1)} %stack.30.facts_ref, bf16[768,128]{1,0:T(8,128)(2,1)S(1)} %get-tuple-element.63.a0, bf16[768,128]{1,0:T(8,128)(2,1)S(1)} %get-tuple-element.64.a1, bf16[768,128]{1,0:T(8,128)(2,1)S(1)} %get-tuple-element.67.b0, ...), custom_call_target="tpu_custom_call" | custom-call | flops 1 | bytes 1 | tf_op jit(solution)/shard_map/weight_grads/pallas_call | solution.py:216
  81.3 1.3 %assemble.1 = bf16[1,32,3072]{2,1,0:T(8,128)(2,1)} custom-call(s32[6]{0:T(128)S(1)} %stack.30.facts_ref, bf16[32,1536]{1,0:T(8,128)(2,1)S(1)} %get-tuple-element.70.refs_0_, bf16[32,1536]{1,0:T(8,128)(2,1)S(1)} %collective-permute-done.12.refs_1_, bf16[32,1536]{1,0:T(8,128)(2,1)S(1)} %collective-permute-done.15.refs_2_, ...), custom_call_target="tpu_custom_call" | custom-call | tf_op jit(solution)/shard_map/assemble/pallas_call | solution.py:185
  (37 shorter events, 10.2 us)
Async XLA Ops:
  1.6 10.3 %collective-permute-start = (bf16[32,1536]{1,0:T(8,128)(2,1)S(1)}, bf16[32,1536]{1,0:T(8,128)(2,1)S(1)}, u32[]{:S(2)}, u32[]{:S(2)}) collective-permute-start(bf16[32,1536]{1,0:T(8,128)(2,1)S(1)} %get-tuple-element.76), channel_id=1, source_target_pairs={{0,4},{4,0},{1,5},{5,1},{2,6},{6,2},{3,7},{7,3},{8,12},{12,8},{9,1... | collective-permute-start | bytes 294920 | tf_op jit(solution)/shard_map/ppermute | solution.py:398
  5.4 0.9 %copy-start = (bf16[1,32,3072]{2,1,0:T(8,128)(2,1)S(1)}, bf16[1,32,3072]{2,1,0:T(8,128)(2,1)}, u32[]{:S(2)}) copy-start(bf16[1,32,3072]{2,1,0:T(8,128)(2,1)} %input_ref.1) | copy-start | bytes 589828
  6.3 0.9 %copy-start.1 = (bf16[1,768,128]{2,1,0:T(8,128)(2,1)S(1)}, bf16[1,768,128]{2,1,0:T(8,128)(2,1)}, u32[]{:S(2)}) copy-start(bf16[1,768,128]{2,1,0:T(8,128)(2,1)} %query_ref.1) | copy-start | bytes 589828
  7.2 0.9 %copy-start.2 = (bf16[1,768,128]{2,1,0:T(8,128)(2,1)S(1)}, bf16[1,768,128]{2,1,0:T(8,128)(2,1)}, u32[]{:S(2)}) copy-start(bf16[1,768,128]{2,1,0:T(8,128)(2,1)} %key_ref.1) | copy-start | bytes 589828
  11.9 10.0 %collective-permute-start.1 = (bf16[1424,128]{1,0:T(8,128)(2,1)S(1)}, bf16[1424,128]{1,0:T(8,128)(2,1)S(1)}, u32[]{:S(2)}, u32[]{:S(2)}) collective-permute-start(bf16[1424,128]{1,0:T(8,128)(2,1)S(1)} %get-tuple-element.39.probs_ref), channel_id=1, source_target_pairs={{0,4},{4,0},{1,5},{5,1},{2,6},{6,2},{3,7},{7,3},{8,12},{12,8},{9,1... | collective-permute-start | bytes 1093640 | tf_op jit(solution)/shard_map/ppermute | solution.py:398
  23.3 7.9 %collective-permute-start.2 = (bf16[768,128]{1,0:T(8,128)(2,1)S(1)}, bf16[768,128]{1,0:T(8,128)(2,1)S(1)}, u32[]{:S(2)}, u32[]{:S(2)}) collective-permute-start(bf16[768,128]{1,0:T(8,128)(2,1)S(1)} %project.5.mine_ref), channel_id=1, source_target_pairs={{0,4},{4,0},{1,5},{5,1},{2,6},{6,2},{3,7},{7,3},{8,12},{12,8},{9,1... | collective-permute-start | bytes 589832 | tf_op jit(solution)/shard_map/ppermute | solution.py:398
  25.4 8.6 %collective-permute-start.4 = (bf16[768,128]{1,0:T(8,128)(2,1)S(1)}, bf16[768,128]{1,0:T(8,128)(2,1)S(1)}, u32[]{:S(2)}, u32[]{:S(2)}) collective-permute-start(bf16[768,128]{1,0:T(8,128)(2,1)S(1)} %project.4.mine_ref), channel_id=1, source_target_pairs={{0,4},{4,0},{1,5},{5,1},{2,6},{6,2},{3,7},{7,3},{8,12},{12,8},{9,1... | collective-permute-start | bytes 589832 | tf_op jit(solution)/shard_map/ppermute | solution.py:398
  26.8 15.2 %slice-start = ((s8[4718592]{0:T(1024)(128)(4,1)}), s8[4194304]{0:T(1024)(128)(4,1)S(1)}, s32[]{:S(2)}) async-start(s8[4718592]{0:T(1024)(128)(4,1)} %bitcast.8), calls=%async_computation | async-start | bytes 8388608
  29.3 12.6 %slice-start.1 = ((s8[4718592]{0:T(1024)(128)(4,1)}), s8[524288]{0:T(1024)(128)(4,1)S(1)}, s32[]{:S(2)}) async-start(s8[4718592]{0:T(1024)(128)(4,1)} %bitcast.8), calls=%async_computation.1 | async-start | bytes 1048576
  32.7 3.0 %collective-permute-start.3 = (bf16[2,32,1536]{2,1,0:T(8,128)(2,1)S(1)}, bf16[2,32,1536]{2,1,0:T(8,128)(2,1)S(1)}, u32[]{:S(2)}, u32[]{:S(2)}) collective-permute-start(bf16[2,32,1536]{2,1,0:T(8,128)(2,1)S(1)} %get-tuple-element.45), channel_id=1, source_target_pairs={{0,1},{1,0},{2,3},{3,2},{4,5},{5,4},{6,7},{7,6},{8,9},{9,8},{10,11... | collective-permute-start | bytes 589832 | tf_op jit(solution)/shard_map/ppermute | solution.py:401
  35.6 3.0 %collective-permute-start.5 = (bf16[2,32,1536]{2,1,0:T(8,128)(2,1)S(1)}, bf16[2,32,1536]{2,1,0:T(8,128)(2,1)S(1)}, u32[]{:S(2)}, u32[]{:S(2)}) collective-permute-start(bf16[2,32,1536]{2,1,0:T(8,128)(2,1)S(1)} %get-tuple-element.49), channel_id=1, source_target_pairs={{0,1},{1,0},{2,3},{3,2},{4,5},{5,4},{6,7},{7,6},{8,9},{9,8},{10,11... | collective-permute-start | bytes 589832 | tf_op jit(solution)/shard_map/ppermute | solution.py:401
  36.3 6.8 %collective-permute-start.6 = (bf16[32,1536]{1,0:T(8,128)(2,1)S(1)}, bf16[32,1536]{1,0:T(8,128)(2,1)S(1)}, u32[]{:S(2)}, u32[]{:S(2)}) collective-permute-start(bf16[32,1536]{1,0:T(8,128)(2,1)S(1)} %get-tuple-element.46.refs_0_), channel_id=1, source_target_pairs={{0,8},{1,9},{2,10},{3,11},{8,0},{9,1},{10,2},{11,3},{16,24},{17,25... | collective-permute-start | bytes 294920 | tf_op jit(solution)/shard_map/ppermute | solution.py:420
  37.8 6.5 %collective-permute-start.7 = (bf16[32,1536]{1,0:T(8,128)(2,1)S(1)}, bf16[32,1536]{1,0:T(8,128)(2,1)S(1)}, u32[]{:S(2)}, u32[]{:S(2)}) collective-permute-start(bf16[32,1536]{1,0:T(8,128)(2,1)S(1)} %get-tuple-element.47.refs_1_), channel_id=1, source_target_pairs={{0,10},{1,11},{2,8},{3,9},{8,2},{9,3},{10,0},{11,1},{16,26},{17,27... | collective-permute-start | bytes 294920 | tf_op jit(solution)/shard_map/ppermute | solution.py:420
  39.2 6.9 %collective-permute-start.8 = (bf16[32,1536]{1,0:T(8,128)(2,1)S(1)}, bf16[32,1536]{1,0:T(8,128)(2,1)S(1)}, u32[]{:S(2)}, u32[]{:S(2)}) collective-permute-start(bf16[32,1536]{1,0:T(8,128)(2,1)S(1)} %get-tuple-element.50.refs_0_), channel_id=1, source_target_pairs={{0,8},{1,9},{2,10},{3,11},{8,0},{9,1},{10,2},{11,3},{16,24},{17,25... | collective-permute-start | bytes 294920 | tf_op jit(solution)/shard_map/ppermute | solution.py:420
  40.7 7.4 %collective-permute-start.9 = (bf16[32,1536]{1,0:T(8,128)(2,1)S(1)}, bf16[32,1536]{1,0:T(8,128)(2,1)S(1)}, u32[]{:S(2)}, u32[]{:S(2)}) collective-permute-start(bf16[32,1536]{1,0:T(8,128)(2,1)S(1)} %get-tuple-element.51.refs_1_), channel_id=1, source_target_pairs={{0,10},{1,11},{2,8},{3,9},{8,2},{9,3},{10,0},{11,1},{16,26},{17,27... | collective-permute-start | bytes 294920 | tf_op jit(solution)/shard_map/ppermute | solution.py:420
  58.5 7.8 %collective-permute-start.10 = (bf16[768,128]{1,0:T(8,128)(2,1)S(1)}, bf16[768,128]{1,0:T(8,128)(2,1)S(1)}, u32[]{:S(2)}, u32[]{:S(2)}) collective-permute-start(bf16[768,128]{1,0:T(8,128)(2,1)S(1)} %project.7.mine_ref), channel_id=1, source_target_pairs={{0,4},{4,0},{1,5},{5,1},{2,6},{6,2},{3,7},{7,3},{8,12},{12,8},{9,1... | collective-permute-start | bytes 589832 | tf_op jit(solution)/shard_map/ppermute | solution.py:398
  61.3 8.5 %collective-permute-start.13 = (bf16[768,128]{1,0:T(8,128)(2,1)S(1)}, bf16[768,128]{1,0:T(8,128)(2,1)S(1)}, u32[]{:S(2)}, u32[]{:S(2)}) collective-permute-start(bf16[768,128]{1,0:T(8,128)(2,1)S(1)} %project.6.mine_ref), channel_id=1, source_target_pairs={{0,4},{4,0},{1,5},{5,1},{2,6},{6,2},{3,7},{7,3},{8,12},{12,8},{9,1... | collective-permute-start | bytes 589832 | tf_op jit(solution)/shard_map/ppermute | solution.py:398
  67.6 3.8 %collective-permute-start.11 = (bf16[2,32,1536]{2,1,0:T(8,128)(2,1)S(1)}, bf16[2,32,1536]{2,1,0:T(8,128)(2,1)S(1)}, u32[]{:S(2)}, u32[]{:S(2)}) collective-permute-start(bf16[2,32,1536]{2,1,0:T(8,128)(2,1)S(1)} %get-tuple-element.56), channel_id=1, source_target_pairs={{0,1},{1,0},{2,3},{3,2},{4,5},{5,4},{6,7},{7,6},{8,9},{9,8},{10,11... | collective-permute-start | bytes 589832 | tf_op jit(solution)/shard_map/ppermute | solution.py:401
  71.3 1.8 %collective-permute-start.14 = (bf16[2,32,1536]{2,1,0:T(8,128)(2,1)S(1)}, bf16[2,32,1536]{2,1,0:T(8,128)(2,1)S(1)}, u32[]{:S(2)}, u32[]{:S(2)}) collective-permute-start(bf16[2,32,1536]{2,1,0:T(8,128)(2,1)S(1)} %get-tuple-element.60), channel_id=1, source_target_pairs={{0,1},{1,0},{2,3},{3,2},{4,5},{5,4},{6,7},{7,6},{8,9},{9,8},{10,11... | collective-permute-start | bytes 589832 | tf_op jit(solution)/shard_map/ppermute | solution.py:401
  72.0 8.3 %collective-permute-start.12 = (bf16[32,1536]{1,0:T(8,128)(2,1)S(1)}, bf16[32,1536]{1,0:T(8,128)(2,1)S(1)}, u32[]{:S(2)}, u32[]{:S(2)}) collective-permute-start(bf16[32,1536]{1,0:T(8,128)(2,1)S(1)} %get-tuple-element.58), channel_id=1, source_target_pairs={{0,2},{1,3},{2,0},{3,1},{4,6},{5,7},{6,4},{7,5},{8,10},{9,11},{10,... | collective-permute-start | bytes 294920 | tf_op jit(solution)/shard_map/ppermute | solution.py:404
  73.7 6.6 %collective-permute-start.15 = (bf16[32,1536]{1,0:T(8,128)(2,1)S(1)}, bf16[32,1536]{1,0:T(8,128)(2,1)S(1)}, u32[]{:S(2)}, u32[]{:S(2)}) collective-permute-start(bf16[32,1536]{1,0:T(8,128)(2,1)S(1)} %get-tuple-element.61), channel_id=1, source_target_pairs={{0,4},{1,5},{2,6},{3,7},{4,0},{5,1},{6,2},{7,3},{8,12},{9,13},{10,... | collective-permute-start | bytes 294920 | tf_op jit(solution)/shard_map/ppermute | solution.py:412
  75.3 6.0 %collective-permute-start.16 = (bf16[32,1536]{1,0:T(8,128)(2,1)S(1)}, bf16[32,1536]{1,0:T(8,128)(2,1)S(1)}, u32[]{:S(2)}, u32[]{:S(2)}) collective-permute-start(bf16[32,1536]{1,0:T(8,128)(2,1)S(1)} %get-tuple-element.62), channel_id=1, source_target_pairs={{0,6},{1,7},{2,4},{3,5},{4,2},{5,3},{6,0},{7,1},{8,14},{9,15},{10,... | collective-permute-start | bytes 294920 | tf_op jit(solution)/shard_map/ppermute | solution.py:412

commit v7 on v6

--- a/solution.py
+++ b/solution.py
@@ -44,17 +44,16 @@
     return pl.BlockSpec(memory_space=pl.ANY)
 
 
-def picked_version(index, facts_ref, message_ref):
+def picked_version(index, facts_ref, note_ref):
     if index == 0:
         return facts_ref[VERSION]
-    note = message_ref[message_ref.shape[0] - NOTE_ROWS :, :].astype(jnp.float32)
-    return (jnp.max(note) > 0.5).astype(jnp.int32)
-
-
-def project_kernel(index, facts_ref, message_ref, *refs):
+    return (jnp.max(note_ref[...].astype(jnp.float32)) > 0.5).astype(jnp.int32)
+
+
+def project_kernel(index, spot, facts_ref, note_ref, *refs):
     tables, (tokens_ref, partial_ref) = refs[:-2], refs[-2:]
-    version = picked_version(index, facts_ref, message_ref)
-    flipped = tokens_ref[index].T
+    version = picked_version(index, facts_ref, note_ref)
+    flipped = tokens_ref[spot].T
 
     def rows_of(table_ref):
         partial_ref[...] = matmul(table_ref[0, version], flipped, NN).astype(jnp.bfloat16)
@@ -66,17 +65,17 @@
         pl.when(facts_ref[ODD] == 0)(lambda: rows_of(tables[1]))
 
 
-def project(index, facts, message, tables, tokens):
+def project(index, spot, facts, note, tables, tokens):
     rows = tables[0].shape[2]
     return pl.pallas_call(
-        functools.partial(project_kernel, index),
+        functools.partial(project_kernel, index, spot),
         out_shape=jax.ShapeDtypeStruct((rows, tokens.shape[1]), jnp.bfloat16),
         in_specs=[in_smem()] + [in_vmem()] * (2 + len(tables)),
         out_specs=in_vmem(),
         compiler_params=pltpu.CompilerParams(vmem_limit_bytes=VMEM_BYTES),
         cost_estimate=SMALL,
         name="project",
-    )(facts, message, *tables, tokens)
+    )(facts, note, *tables, tokens)
 
 
 def mix_kernel(
@@ -84,7 +83,7 @@
     natural,
     index,
     facts_ref,
-    message_ref,
+    note_ref,
     value_ref,
     mine_ref,
     arrived_ref,
@@ -93,7 +92,7 @@
     keep_ref,
     send_ref,
 ):
-    version = picked_version(index, facts_ref, message_ref)
+    version = picked_version(index, facts_ref, note_ref)
     step = value_ref.shape[3] // CHUNKS
     tokens = mine_ref.shape[1]
 
@@ -121,7 +120,7 @@
             send_ref[place, :, columns] = jnp.where(second_core, low, high).astype(jnp.bfloat16)
 
 
-def mix(natural, index, facts, messages, w_value, mine, arrived, outer):
+def mix(natural, index, facts, note, message, w_value, mine, arrived, outer):
     rows, width = w_value.shape[2:]
     tokens = mine.shape[1]
     half = jax.ShapeDtypeStruct((outer, tokens // (2 * outer), width), jnp.bfloat16)
@@ -133,7 +132,7 @@
         compiler_params=pltpu.CompilerParams(vmem_limit_bytes=VMEM_BYTES),
         cost_estimate=SMALL,
         name="mix",
-    )(facts, messages[1], w_value, mine, arrived, messages[index])
+    )(facts, note, w_value, mine, arrived, message)
 
 
 def combine_kernel(outer, last, index, facts_ref, keep_ref, arrived_ref, addend_ref, *refs):
@@ -192,12 +191,12 @@
     )(facts, *own_parts, *other_parts)
 
 
-def weight_grad_kernel(facts_ref, a0, a1, b0, b1, first, second, value_ref, out_ref):
+def weight_grad_kernel(facts_ref, a0, a1, b0, b1, first, second0, second1, value_ref, out_ref):
     odd = facts_ref[ODD] == 1
     tokens = a0.shape[1]
     left_first = jnp.concatenate([a0[...], a1[...]], axis=1)
     left_second = jnp.concatenate([b0[...], b1[...]], axis=1)
-    right_second = second[...].reshape(2 * tokens, second.shape[2])
+    right_second = jnp.concatenate([second0[0], second1[0]], axis=0)
     right_first = first[...].reshape(2 * tokens, first.shape[2])
     grad_first = matmul(left_first, right_second, NN)
     grad_second = matmul(left_second, right_first, NN)
@@ -212,17 +211,18 @@
     grad = jax.ShapeDtypeStruct((1, rows, width), jnp.bfloat16)
     left = pl.BlockSpec((step, tokens), lambda i: (i, 0))
     both = pl.BlockSpec((2, tokens, width), lambda i: (0, 0, 0))
+    single = pl.BlockSpec((1, tokens, width), lambda i: (0, 0, 0))
     wide = pl.BlockSpec((1, step, width), lambda i: (0, i, 0))
     return pl.pallas_call(
         weight_grad_kernel,
         grid=(CHUNKS,),
         out_shape=(grad, grad),
-        in_specs=[in_smem()] + [left] * 4 + [both] * 2,
+        in_specs=[in_smem()] + [left] * 4 + [both, single, single],
         out_specs=(wide, wide),
         compiler_params=pltpu.CompilerParams(vmem_limit_bytes=GRAD_VMEM_BYTES),
         cost_estimate=SMALL,
         name="weight_grads",
-    )(facts, *first_results, *second_results, first_full, second_full)
+    )(facts, *first_results, *second_results, first_full, *second_full)
 
 
 def load(source_ref, table_ref, sems):
@@ -240,71 +240,46 @@
 
 
 def pack_kernel(
-    facts_ref,
-    query_ref,
-    key_ref,
-    input_ref,
-    value_ref,
-    out_ref,
-    message_ref,
-    own_ref,
-    table_ref,
-    query_held,
-    key_held,
-    input_held,
-    sems,
-    table_sems,
+    facts_ref, stash_ref, input_ref, value_ref, out_ref, message_ref, own_ref, table_ref, sems
 ):
-    pairs = ((query_ref, query_held), (key_ref, key_held), (input_ref, input_held))
-    copies = [
-        pltpu.make_async_copy(source, held, sems.at[i]) for i, (source, held) in enumerate(pairs)
-    ]
-    for copy in copies:
-        copy.start()
-
     @pl.when(facts_ref[ODD] == 1)
     def _():
-        for copy in load(out_ref, table_ref, table_sems):
+        for copy in load(out_ref, table_ref, sems):
             copy.start()
 
     @pl.when(facts_ref[ODD] == 0)
     def _():
-        for copy in load(value_ref, table_ref, table_sems):
+        for copy in load(value_ref, table_ref, sems):
             copy.start()
 
-    tokens = query_ref.shape[2]
+    tokens = stash_ref.shape[2]
     shard, width = own_ref.shape
-    heads = query_ref.shape[1] // HEAD_DIM
+    heads = stash_ref.shape[1] // HEAD_DIM
     causal = lax.broadcasted_iota(jnp.int32, (tokens, tokens), 1) <= lax.broadcasted_iota(
         jnp.int32, (tokens, tokens), 0
     )
-    copies[0].wait()
-    copies[1].wait()
     for head in range(heads):
         rows = pl.ds(head * HEAD_DIM, HEAD_DIM)
-        scores = matmul(query_held[0, rows, :], key_held[0, rows, :], TN)
+        scores = matmul(stash_ref[0, rows, :], stash_ref[1, rows, :], TN)
         scores = jnp.where(causal, scores * (1.0 / math.sqrt(HEAD_DIM)), -jnp.inf)
         expo = jnp.exp(scores - jnp.max(scores, axis=1, keepdims=True))
         probs = (expo / jnp.sum(expo, axis=1, keepdims=True)).astype(jnp.bfloat16)
         message_ref[head * tokens : (head + 1) * tokens, :] = probs
-    copies[2].wait()
     half = facts_ref[HALF]
-    own_ref[...] = input_held[0, :, pl.ds(pl.multiple_of(half * width, width), width)]
-    other = input_held[0, :, pl.ds(pl.multiple_of((1 - half) * width, width), width)]
+    own_ref[...] = input_ref[1, :, pl.ds(pl.multiple_of(half * width, width), width)]
+    other = input_ref[1, :, pl.ds(pl.multiple_of((1 - half) * width, width), width)]
     for block in range(width // LANES):
         start = heads * tokens + block * shard
         message_ref[start : start + shard, :] = other[:, block * LANES : (block + 1) * LANES]
-    note = jnp.zeros((NOTE_ROWS, LANES), jnp.int32) + facts_ref[VERSION]
-    message_ref[message_ref.shape[0] - NOTE_ROWS :, :] = note.astype(jnp.bfloat16)
-    for copy in load(value_ref, table_ref, table_sems):
+    for copy in load(value_ref, table_ref, sems):
         copy.wait()
 
 
-def pack(facts, query, key_stash, section_input, w_value, w_out):
-    rows, tokens = query.shape[1:]
-    shard = section_input.shape[1]
-    width = section_input.shape[2] // 2
-    length = rows // HEAD_DIM * tokens + width // LANES * shard + NOTE_ROWS
+def pack(facts, stash, inputs, w_value, w_out):
+    rows, tokens = stash.shape[1:]
+    shard = inputs.shape[1]
+    width = inputs.shape[2] // 2
+    length = rows // HEAD_DIM * tokens + width // LANES * shard
     return pl.pallas_call(
         pack_kernel,
         out_shape=(
@@ -312,19 +287,13 @@
             jax.ShapeDtypeStruct((shard, width), jnp.bfloat16),
             jax.ShapeDtypeStruct(w_value.shape, jnp.bfloat16),
         ),
-        in_specs=[in_smem(), in_place(), in_place(), in_place(), in_hbm(), in_hbm()],
+        in_specs=[in_smem(), in_vmem(), in_vmem(), in_hbm(), in_hbm()],
         out_specs=(in_vmem(), in_vmem(), in_vmem()),
-        scratch_shapes=[
-            pltpu.VMEM(query.shape, jnp.bfloat16),
-            pltpu.VMEM(query.shape, jnp.bfloat16),
-            pltpu.VMEM(section_input.shape, jnp.bfloat16),
-            pltpu.SemaphoreType.DMA((3,)),
-            pltpu.SemaphoreType.DMA((2 * CHUNKS,)),
-        ],
+        scratch_shapes=[pltpu.SemaphoreType.DMA((2 * CHUNKS,))],
         compiler_params=pltpu.CompilerParams(vmem_limit_bytes=FIRST_VMEM_BYTES),
         cost_estimate=SMALL,
         name="pack",
-    )(facts, query, key_stash, section_input, w_value, w_out)
+    )(facts, stash, inputs, w_value, w_out)
 
 
 def load_kernel(source_ref, table_ref, sems):
@@ -348,38 +317,39 @@
     )(table)
 
 
-def arrive_kernel(outer, facts_ref, own_ref, message_ref, *refs):
-    parts, pair_ref = refs[:-1], refs[-1]
-    shard, width = own_ref.shape
+def arrive_kernel(index, facts_ref, source_ref, *refs):
+    parts, piece_ref = refs[:-1], refs[-1]
+    shard, width = piece_ref.shape[1:]
 
     @pl.when(facts_ref[ODD] == 1)
     def _():
-        pair_ref[0] = own_ref[...]
-        first_row = message_ref.shape[0] - NOTE_ROWS - width // LANES * shard
-        for block in range(width // LANES):
-            start = first_row + block * shard
-            columns = pl.ds(block * LANES, LANES)
-            pair_ref[1, :, columns] = message_ref[start : start + shard, :]
+        if index == 0:
+            piece_ref[0] = source_ref[...]
+        else:
+            first_row = source_ref.shape[0] - width // LANES * shard
+            for block in range(width // LANES):
+                start = first_row + block * shard
+                columns = pl.ds(block * LANES, LANES)
+                piece_ref[0, :, columns] = source_ref[start : start + shard, :]
 
     @pl.when(facts_ref[ODD] == 0)
     def _():
-        for index in range(2):
-            total = parts[index * outer][...].astype(jnp.float32)
-            for part in parts[index * outer + 1 : (index + 1) * outer]:
-                total = total + part[...].astype(jnp.float32)
-            pair_ref[index] = total.astype(jnp.bfloat16)
-
-
-def arrive(facts, input_own, message, parts):
-    return pl.pallas_call(
-        functools.partial(arrive_kernel, len(parts) // 2),
-        out_shape=jax.ShapeDtypeStruct((2,) + input_own.shape, jnp.bfloat16),
-        in_specs=[in_smem()] + [in_vmem()] * (2 + len(parts)),
+        total = parts[0][...].astype(jnp.float32)
+        for part in parts[1:]:
+            total = total + part[...].astype(jnp.float32)
+        piece_ref[0] = total.astype(jnp.bfloat16)
+
+
+def arrive(index, facts, source, parts):
+    return pl.pallas_call(
+        functools.partial(arrive_kernel, index),
+        out_shape=jax.ShapeDtypeStruct((1,) + parts[0].shape, jnp.bfloat16),
+        in_specs=[in_smem()] + [in_vmem()] * (1 + len(parts)),
         out_specs=in_vmem(),
         compiler_params=pltpu.CompilerParams(vmem_limit_bytes=VMEM_BYTES),
         cost_estimate=SMALL,
         name="arrive",
-    )(facts, input_own, message, *parts)
+    )(facts, source, *parts)
 
 
 def on_device(section_input, query, key_stash, incoming, version, w_value, w_out):
@@ -429,43 +399,52 @@
         return lax.all_gather(pair, "tensor", axis=1, tiled=True)
 
     facts = jnp.stack([odd_flag, 1 - odd_flag, version[0], core, row, half])
-    first = jnp.where(odd, incoming[0], section_input[0])
-    first_pair = jnp.stack([own_columns(first), swap_half(other_columns(first))])
-    own_message, input_own, first_table = pack(
-        facts, query, key_stash, section_input, w_value, w_out
-    )
+    inputs = jnp.stack([jnp.where(odd, incoming[0], section_input[0]), section_input[0]])
+    note = jnp.full((NOTE_ROWS, width), version[0], jnp.int32).astype(jnp.bfloat16)
+    sent_piece = jnp.concatenate([other_columns(inputs[0]), note])
+    other_piece = swap_half(sent_piece)
+    other_note = other_piece[shard:]
+    first_pair = jnp.stack([own_columns(inputs[0]), other_piece[:shard]])
+    stash = jnp.concatenate([query, key_stash])
+    own_message, input_own, first_table = pack(facts, stash, inputs, w_value, w_out)
     other_message = swap_half(own_message)
     first_full = gathered(first_pair)
-    first_full, other_message = lax.optimization_barrier((first_full, other_message))
+    own_full, other_message = lax.optimization_barrier((first_full, other_message))
     messages = [own_message, other_message]
 
     partial = [None, None]
     for m in (1, 0):
-        partial[m] = project(m, facts, other_message, (first_table,), first_full)
+        tokens = first_full if m else own_full
+        partial[m] = project(m, m, facts, other_note, (first_table,), tokens)
     arrived = [swap_half(partial[1]), swap_half(partial[0])]
     later_value, _ = lax.optimization_barrier((w_value, partial))
     value_table = load_table(later_value, VALUE_VMEM_BYTES)
     first_result, first_sent = [None, None], [None, None]
+    second_piece, second_full = [None, None], [None, None]
     for m in range(2):
         first_result[m], keep, send = mix(
-            ODD, m, facts, messages, value_table, partial[m], arrived[m], outer
+            ODD, m, facts, other_note, messages[m], value_table, partial[m], arrived[m], outer
         )
         first_sent[m] = combine(m, facts, keep, swap_core(send), first_pair)
     later_out, _ = lax.optimization_barrier((w_out, first_sent))
     out_table = load_table(later_out, OUT_VMEM_BYTES)
-    input_own, _ = lax.optimization_barrier((input_own, out_table))
-    received = [swap_section(part, d) for m in range(2) for d, part in enumerate(first_sent[m])]
-    second_pair = arrive(facts, input_own, other_message, received)
-    second_full = gathered(second_pair)
+    sources = [input_own, other_message]
+    sources, _ = lax.optimization_barrier((sources, out_table))
     for m in range(2):
-        partial[m] = project(m, facts, other_message, (value_table, out_table), second_full)
+        received = [swap_section(part, d) for d, part in enumerate(first_sent[m])]
+        second_piece[m] = arrive(m, facts, sources[m], received)
+    for m in range(2):
+        second_full[m] = gathered(second_piece[m])
+        partial[m] = project(
+            m, 0, facts, other_note, (value_table, out_table), second_full[m]
+        )
     arrived = [swap_half(partial[1]), swap_half(partial[0])]
     second_result, last_sent = [None, None], [None, None]
     for m in (1, 0):
         second_result[m], keep, send = mix(
-            EVEN, m, facts, messages, value_table, partial[m], arrived[m], outer
+            EVEN, m, facts, other_note, messages[m], value_table, partial[m], arrived[m], outer
         )
-        last_sent[m] = combine(m, facts, keep, swap_core(send), second_pair, first_sent[m])
+        last_sent[m] = combine(0, facts, keep, swap_core(send), second_piece[m], first_sent[m])
     other_parts = [to_other_half(part, d) for d, part in enumerate(last_sent[1])]
     own_parts = [last_sent[0][0]] + [to_row(part, d + 1) for d, part in enumerate(last_sent[0][1:])]
     second_result, _ = lax.optimization_barrier((second_result, last_sent))

time: 82.8 us -> 81.7 us (0.987)
  waiting for transfers between devices: 16.3 us -> 11.8 us
  blocking collectives: 17.5 us -> 21.6 us
  local copies, waits for them, and re-layouts: 2.9 us -> 0.15 us
  other arithmetic: 0.98 us -> 3.01 us
    all_gather x2 -> x3, blocking collectives: 17.5 us -> 21.6 us  [gathered(): return lax.all_gather(pair, 'tensor', axis=1, tiled=True)]
    ppermute x4, waiting for transfers between devices: 5.05 us -> 1.27 us  [swap_section(): return lax.ppermute(array, ('pair', 'tensor'), pairs)]
    unnamed x10 -> x4, local copies, waits for them, and re-layouts: 2.79 us -> 0.01 us
    ppermute x1, waiting for transfers between devices: 0.01 us -> 1.63 us  [to_row(): lax.ppermute(array, 'tensor', [(i, i ^ 2 * delta) for i in range(n_tensor)])]
    ppermute x6, waiting for transfers between devices: 10.3 us -> 8.89 us  [swap_half(): return lax.ppermute(array, 'half', [(0, 1), (1, 0)])]
    concatenate x0 -> x1, other arithmetic: none -> 1.06 us  [on_device(): stash = jnp.concatenate([query, key_stash])]
    another operation x1 -> x2, other arithmetic: 0.02 us -> 0.99 us  [the longest x1 0.96 us: on_device(): jnp.stack([jnp.where(odd, incoming[0], section_input[0]), section_input[0]])]
    ppermute x2, waiting for transfers between devices: 0.9 us -> 0.01 us  [to_other_half(): return lax.ppermute(array, ('half', 'tensor'), pairs)]
  transfers between devices with their start and end apart: 17 -> 17, of which waited for: 9 -> 5; matrix products, arithmetic and copies ran while one was open for 0% -> 3% of each run, Pallas kernels for 27% -> 31%
where the time goes in v7:
time: 81.7 us; the launch traced here: 81.4 us
  Pallas kernels  26.9 us (33%)
  blocking collectives  21.6 us (26%)
  starting transfers between devices  16.4 us (20%)
  waiting for transfers between devices  11.8 us (14%)
  other arithmetic  3.01 us (4%)
  between operations  1.56 us (2%)
    all_gather x3, blocking collectives, gathered(): return lax.all_gather(pair, 'tensor', axis=1, tiled=True)  21.6 us
    ppermute x6, waiting for transfers between devices, swap_half(): return lax.ppermute(array, 'half', [(0, 1), (1, 0)])  8.89 us
    ppermute x6, starting transfers between devices, swap_half(): return lax.ppermute(array, 'half', [(0, 1), (1, 0)])  7.41 us
    pallas_call x4, Pallas kernels, mix(): pl.pallas_call(functools.partial(mix_kernel, outer, natural, index), out_...  5.86 us
    pallas_call x4, Pallas kernels, project(): pl.pallas_call(functools.partial(project_kernel, index, spot), out_shape=...  5.49 us
    ppermute x4, starting transfers between devices, swap_section(): return lax.ppermute(array, ('pair', 'tensor'), pairs)  5.08 us
    pallas_call x1, Pallas kernels, weight_grads(): pl.pallas_call(weight_grad_kernel, grid=(CHUNKS,), out_shape=(grad, grad)...  4.06 us
    pallas_call x2, Pallas kernels, load_table(): pl.pallas_call(load_kernel, out_shape=jax.ShapeDtypeStruct(table.shape, j...  3.57 us
  transfers between devices with their start and end apart: 17, of which 5 were waited for; matrix products, arithmetic and copies ran while one was open for 3% of the time, Pallas kernels for 31%

profile of v7, /device:TPU:0, one launch (start us, length us, event | category | flops | bytes accessed | tf_op | source)
XLA Modules:
  0.0 81.4 jit_solution(787814957274943326)
XLA Ops:
  1.3 1.0 %broadcast_select_fusion = bf16[1,32,3072]{2,1,0:T(8,128)(2,1)S(1)} fusion(bf16[1,32,3072]{2,1,0:T(8,128)(2,1)} %param.10, bf16[1,32,3072]{2,1,0:T(8,128)(2,1)} %param.7, pred[]{:T(512)S(6)} %eq.6), kind=kLoop, calls=%fused_computation.3 | loop fusion | flops 98304 | bytes 589825 | tf_op jit(solution)/shard_map/jit(_where)/select_n | solution.py:402
  2.3 3.0 %collective-permute-start = (bf16[48,1536]{1,0:T(8,128)(2,1)S(1)}, bf16[48,1536]{1,0:T(8,128)(2,1)S(1)}, u32[]{:S(2)}, u32[]{:S(2)}) collective-permute-start(bf16[48,1536]{1,0:T(8,128)(2,1)S(1)} %concatenate.6), channel_id=1, source_target_pairs={{0,4},{4,0},{1,5},{5,1},{2,6},{6,2},{3,7},{7,3},{8,12},{12,8},{9,1... | collective-permute-start | bytes 442376 | tf_op jit(solution)/shard_map/ppermute | solution.py:368
  5.3 1.0 %pad_maximum_fusion.1.input_ref = bf16[2,32,3072]{2,1,0:T(8,128)(2,1)S(1)} fusion(bf16[1,32,3072]{2,1,0:T(8,128)(2,1)} %param.7, bf16[1,32,3072]{2,1,0:T(8,128)(2,1)S(1)} %broadcast_select_fusion), kind=kLoop, calls=%fused_computation.1 | loop fusion | flops 196608 | bytes 786432 | tf_op jit(solution)/shard_map/stack | solution.py:402
  6.4 1.1 %pad_maximum_fusion.stash_ref = bf16[2,768,128]{2,1,0:T(8,128)(2,1)S(1)} fusion(bf16[1,768,128]{2,1,0:T(8,128)(2,1)} %param.9, bf16[1,768,128]{2,1,0:T(8,128)(2,1)} %param.8), kind=kLoop, calls=%fused_computation | loop fusion | flops 196608 | bytes 786432 | tf_op jit(solution)/shard_map/concatenate | solution.py:408
  7.5 3.0 %pack.1 = (bf16[1408,128]{1,0:T(8,128)(2,1)S(1)}, bf16[32,1536]{1,0:T(8,128)(2,1)S(1)}, bf16[1,2,768,1536]{3,2,1,0:T(8,128)(2,1)S(1)}) custom-call(s32[6]{0:T(128)S(1)} %stack.34.facts_ref, bf16[2,768,128]{2,1,0:T(8,128)(2,1)S(1)} %pad_maximum_fusion.stash_ref, bf16[2,32,3072]{2,1,0:T(8,128)(2,1)S(1)} %pad_maximum_fusion.1.input_ref, ...), custom_call_target="tpu_custom_call" | custom-call | flops 1 | bytes 1 | tf_op jit(solution)/shard_map/pack/pallas_call | solution.py:283
  10.6 9.1 %all_gather.9.refs_1_.first = bf16[2,128,1536]{2,1,0:T(8,128)(2,1)S(1)} all-gather(bf16[2,32,1536]{2,1,0:T(8,128)(2,1)S(1)} %pad_maximum_fusion.2.addend_ref), channel_id=1, replica_groups=mesh['pair'=4,'half'=2,'tensor'=4] {'tensor'}, dimensions={1}, use_global_device_ids=true | all-gather | bytes 983040 | tf_op jit(solution)/shard_map/all_gather | solution.py:399
  19.8 1.4 %project.5.mine_ref = bf16[768,128]{1,0:T(8,128)(2,1)S(1)} custom-call(s32[6]{0:T(128)S(1)} %stack.34.facts_ref, bf16[16,1536]{1,0:T(8,128)(2,1)S(1)} %slice.8.note_ref, bf16[1,2,768,1536]{3,2,1,0:T(8,128)(2,1)S(1)} %get-tuple-element.40.refs_0_, bf16[2,128,1536]{2,1,0:T(8,128)(2,1)S(1)} %all_gather.9.refs_1_.first), custom_call_target="tpu_custom_call" | custom-call | flops 1 | bytes 1 | tf_op jit(solution)/shard_map/project/pallas_call | solution.py:70
  21.2 1.6 %collective-permute-start.2 = (bf16[768,128]{1,0:T(8,128)(2,1)S(1)}, bf16[768,128]{1,0:T(8,128)(2,1)S(1)}, u32[]{:S(2)}, u32[]{:S(2)}) collective-permute-start(bf16[768,128]{1,0:T(8,128)(2,1)S(1)} %project.5.mine_ref), channel_id=1, source_target_pairs={{0,4},{4,0},{1,5},{5,1},{2,6},{6,2},{3,7},{7,3},{8,12},{12,8},{9,1... | collective-permute-start | bytes 589832 | tf_op jit(solution)/shard_map/ppermute | solution.py:368
  22.7 1.3 %project.4.mine_ref = bf16[768,128]{1,0:T(8,128)(2,1)S(1)} custom-call(s32[6]{0:T(128)S(1)} %stack.34.facts_ref, bf16[16,1536]{1,0:T(8,128)(2,1)S(1)} %slice.8.note_ref, bf16[1,2,768,1536]{3,2,1,0:T(8,128)(2,1)S(1)} %get-tuple-element.40.refs_0_, bf16[2,128,1536]{2,1,0:T(8,128)(2,1)S(1)} %all_gather.9.refs_1_.first), custom_call_target="tpu_custom_call" | custom-call | flops 1 | bytes 1 | tf_op jit(solution)/shard_map/project/pallas_call | solution.py:70
  24.7 2.5 %load_table.2.value_ref.refs_0_ = bf16[1,2,768,1536]{3,2,1,0:T(8,128)(2,1)S(1)} custom-call(bf16[1,2,768,1536]{3,2,1,0:T(8,128)(2,1)} %source_ref), custom_call_target="tpu_custom_call" | custom-call | flops 1 | bytes 1 | tf_op jit(solution)/shard_map/load_table/pallas_call | solution.py:308
  27.2 1.8 %collective-permute-done.2.arrived_ref = bf16[768,128]{1,0:T(8,128)(2,1)S(1)} collective-permute-done((bf16[768,128]{1,0:T(8,128)(2,1)S(1)}, bf16[768,128]{1,0:T(8,128)(2,1)S(1)}, u32[]{:S(2)}, u32[]{:S(2)}) %collective-permute-start.2) | collective-permute-done | bytes 196640 | tf_op jit(solution)/shard_map/ppermute | solution.py:368
  29.0 1.5 %mix.4 = (bf16[768,128]{1,0:T(8,128)(2,1)S(1)}, bf16[2,32,1536]{2,1,0:T(8,128)(2,1)S(1)}, bf16[2,32,1536]{2,1,0:T(8,128)(2,1)S(1)}) custom-call(s32[6]{0:T(128)S(1)} %stack.34.facts_ref, bf16[16,1536]{1,0:T(8,128)(2,1)S(1)} %slice.8.note_ref, bf16[1,2,768,1536]{3,2,1,0:T(8,128)(2,1)S(1)} %load_table.2.value_ref.refs_0_, ...), custom_call_target="tpu_custom_call" | custom-call | flops 1 | bytes 1 | tf_op jit(solution)/shard_map/mix/pallas_call | solution.py:127
  30.5 2.1 %collective-permute-done.4.arrived_ref = bf16[768,128]{1,0:T(8,128)(2,1)S(1)} collective-permute-done((bf16[768,128]{1,0:T(8,128)(2,1)S(1)}, bf16[768,128]{1,0:T(8,128)(2,1)S(1)}, u32[]{:S(2)}, u32[]{:S(2)}) %collective-permute-start.4) | collective-permute-done | bytes 196640 | tf_op jit(solution)/shard_map/ppermute | solution.py:368
  32.6 1.6 %mix.5 = (bf16[768,128]{1,0:T(8,128)(2,1)S(1)}, bf16[2,32,1536]{2,1,0:T(8,128)(2,1)S(1)}, bf16[2,32,1536]{2,1,0:T(8,128)(2,1)S(1)}) custom-call(s32[6]{0:T(128)S(1)} %stack.34.facts_ref, bf16[16,1536]{1,0:T(8,128)(2,1)S(1)} %slice.8.note_ref, bf16[1,2,768,1536]{3,2,1,0:T(8,128)(2,1)S(1)} %load_table.2.value_ref.refs_0_, ...), custom_call_target="tpu_custom_call" | custom-call | flops 1 | bytes 1 | tf_op jit(solution)/shard_map/mix/pallas_call | solution.py:127
  34.9 1.5 %collective-permute-start.6 = (bf16[32,1536]{1,0:T(8,128)(2,1)S(1)}, bf16[32,1536]{1,0:T(8,128)(2,1)S(1)}, u32[]{:S(2)}, u32[]{:S(2)}) collective-permute-start(bf16[32,1536]{1,0:T(8,128)(2,1)S(1)} %get-tuple-element.46.refs_0_), channel_id=1, source_target_pairs={{0,8},{1,9},{2,10},{3,11},{8,0},{9,1},{10,2},{11,3},{16,24},{17,25... | collective-permute-start | bytes 294920 | tf_op jit(solution)/shard_map/ppermute | solution.py:390
  37.6 1.5 %collective-permute-start.8 = (bf16[32,1536]{1,0:T(8,128)(2,1)S(1)}, bf16[32,1536]{1,0:T(8,128)(2,1)S(1)}, u32[]{:S(2)}, u32[]{:S(2)}) collective-permute-start(bf16[32,1536]{1,0:T(8,128)(2,1)S(1)} %get-tuple-element.51.refs_0_), channel_id=1, source_target_pairs={{0,8},{1,9},{2,10},{3,11},{8,0},{9,1},{10,2},{11,3},{16,24},{17,25... | collective-permute-start | bytes 294920 | tf_op jit(solution)/shard_map/ppermute | solution.py:390
  39.1 1.5 %collective-permute-start.9 = (bf16[32,1536]{1,0:T(8,128)(2,1)S(1)}, bf16[32,1536]{1,0:T(8,128)(2,1)S(1)}, u32[]{:S(2)}, u32[]{:S(2)}) collective-permute-start(bf16[32,1536]{1,0:T(8,128)(2,1)S(1)} %get-tuple-element.52.refs_1_), channel_id=1, source_target_pairs={{0,10},{1,11},{2,8},{3,9},{8,2},{9,3},{10,0},{11,1},{16,26},{17,27... | collective-permute-start | bytes 294920 | tf_op jit(solution)/shard_map/ppermute | solution.py:390
  40.6 1.0 %load_table.3.refs_1_ = bf16[1,2,768,1536]{3,2,1,0:T(8,128)(2,1)S(1)} custom-call(bf16[1,2,768,1536]{3,2,1,0:T(8,128)(2,1)S(1)} %bitcast.11), custom_call_target="tpu_custom_call" | custom-call | flops 1 | bytes 1 | tf_op jit(solution)/shard_map/load_table/pallas_call | solution.py:308
  41.7 1.3 %collective-permute-done.7.refs_1_ = bf16[32,1536]{1,0:T(8,128)(2,1)S(1)} collective-permute-done((bf16[32,1536]{1,0:T(8,128)(2,1)S(1)}, bf16[32,1536]{1,0:T(8,128)(2,1)S(1)}, u32[]{:S(2)}, u32[]{:S(2)}) %collective-permute-start.7) | collective-permute-done | bytes 98336 | tf_op jit(solution)/shard_map/ppermute | solution.py:390
  43.5 6.2 %all_gather.10.refs_2_.second0 = bf16[1,128,1536]{2,1,0:T(8,128)(2,1)S(1)} all-gather(bf16[1,32,1536]{2,1,0:T(8,128)(2,1)S(1)} %arrive.2.addend_ref), channel_id=1, replica_groups=mesh['pair'=4,'half'=2,'tensor'=4] {'tensor'}, dimensions={1}, use_global_device_ids=true | all-gather | bytes 491520 | tf_op jit(solution)/shard_map/all_gather | solution.py:399
  49.7 1.3 %project.6.mine_ref = bf16[768,128]{1,0:T(8,128)(2,1)S(1)} custom-call(s32[6]{0:T(128)S(1)} %stack.34.facts_ref, bf16[16,1536]{1,0:T(8,128)(2,1)S(1)} %slice.8.note_ref, bf16[1,2,768,1536]{3,2,1,0:T(8,128)(2,1)S(1)} %load_table.2.value_ref.refs_0_, bf16[1,2,768,1536]{3,2,1,0:T(8,128)(2,1)S(1)} %load_table.3.refs_1_, ...), custom_call_target="tpu_custom_call" | custom-call | flops 1 | bytes 1 | tf_op jit(solution)/shard_map/project/pallas_call | solution.py:70
  51.0 1.6 %collective-permute-start.13 = (bf16[768,128]{1,0:T(8,128)(2,1)S(1)}, bf16[768,128]{1,0:T(8,128)(2,1)S(1)}, u32[]{:S(2)}, u32[]{:S(2)}) collective-permute-start(bf16[768,128]{1,0:T(8,128)(2,1)S(1)} %project.6.mine_ref), channel_id=1, source_target_pairs={{0,4},{4,0},{1,5},{5,1},{2,6},{6,2},{3,7},{7,3},{8,12},{12,8},{9,1... | collective-permute-start | bytes 589832 | tf_op jit(solution)/shard_map/ppermute | solution.py:368
  53.2 6.3 %all_gather.11.refs_2_.second1 = bf16[1,128,1536]{2,1,0:T(8,128)(2,1)S(1)} all-gather(bf16[1,32,1536]{2,1,0:T(8,128)(2,1)S(1)} %arrive.3.addend_ref), channel_id=1, replica_groups=mesh['pair'=4,'half'=2,'tensor'=4] {'tensor'}, dimensions={1}, use_global_device_ids=true | all-gather | bytes 491520 | tf_op jit(solution)/shard_map/all_gather | solution.py:399
  59.5 1.4 %project.7.mine_ref = bf16[768,128]{1,0:T(8,128)(2,1)S(1)} custom-call(s32[6]{0:T(128)S(1)} %stack.34.facts_ref, bf16[16,1536]{1,0:T(8,128)(2,1)S(1)} %slice.8.note_ref, bf16[1,2,768,1536]{3,2,1,0:T(8,128)(2,1)S(1)} %load_table.2.value_ref.refs_0_, bf16[1,2,768,1536]{3,2,1,0:T(8,128)(2,1)S(1)} %load_table.3.refs_1_, ...), custom_call_target="tpu_custom_call" | custom-call | flops 1 | bytes 1 | tf_op jit(solution)/shard_map/project/pallas_call | solution.py:70
  61.5 1.4 %mix.7 = (bf16[768,128]{1,0:T(8,128)(2,1)S(1)}, bf16[2,32,1536]{2,1,0:T(8,128)(2,1)S(1)}, bf16[2,32,1536]{2,1,0:T(8,128)(2,1)S(1)}) custom-call(s32[6]{0:T(128)S(1)} %stack.34.facts_ref, bf16[16,1536]{1,0:T(8,128)(2,1)S(1)} %slice.8.note_ref, bf16[1,2,768,1536]{3,2,1,0:T(8,128)(2,1)S(1)} %load_table.2.value_ref.refs_0_, ...), custom_call_target="tpu_custom_call" | custom-call | flops 1 | bytes 1 | tf_op jit(solution)/shard_map/mix/pallas_call | solution.py:127
  63.1 5.0 %collective-permute-done.10.arrived_ref = bf16[768,128]{1,0:T(8,128)(2,1)S(1)} collective-permute-done((bf16[768,128]{1,0:T(8,128)(2,1)S(1)}, bf16[768,128]{1,0:T(8,128)(2,1)S(1)}, u32[]{:S(2)}, u32[]{:S(2)}) %collective-permute-start.10) | collective-permute-done | bytes 196640 | tf_op jit(solution)/shard_map/ppermute | solution.py:368
  68.1 1.4 %mix.6 = (bf16[768,128]{1,0:T(8,128)(2,1)S(1)}, bf16[2,32,1536]{2,1,0:T(8,128)(2,1)S(1)}, bf16[2,32,1536]{2,1,0:T(8,128)(2,1)S(1)}) custom-call(s32[6]{0:T(128)S(1)} %stack.34.facts_ref, bf16[16,1536]{1,0:T(8,128)(2,1)S(1)} %slice.8.note_ref, bf16[1,2,768,1536]{3,2,1,0:T(8,128)(2,1)S(1)} %load_table.2.value_ref.refs_0_, ...), custom_call_target="tpu_custom_call" | custom-call | flops 1 | bytes 1 | tf_op jit(solution)/shard_map/mix/pallas_call | solution.py:127
  70.8 2.1 %collective-permute-start.16 = (bf16[32,1536]{1,0:T(8,128)(2,1)S(1)}, bf16[32,1536]{1,0:T(8,128)(2,1)S(1)}, u32[]{:S(2)}, u32[]{:S(2)}) collective-permute-start(bf16[32,1536]{1,0:T(8,128)(2,1)S(1)} %get-tuple-element.64), channel_id=1, source_target_pairs={{0,6},{1,7},{2,4},{3,5},{4,2},{5,3},{6,0},{7,1},{8,14},{9,15},{10,... | collective-permute-start | bytes 294920 | tf_op jit(solution)/shard_map/ppermute | solution.py:382
  73.6 0.9 %collective-permute-start.12 = (bf16[32,1536]{1,0:T(8,128)(2,1)S(1)}, bf16[32,1536]{1,0:T(8,128)(2,1)S(1)}, u32[]{:S(2)}, u32[]{:S(2)}) collective-permute-start(bf16[32,1536]{1,0:T(8,128)(2,1)S(1)} %get-tuple-element.60), channel_id=1, source_target_pairs={{0,2},{1,3},{2,0},{3,1},{4,6},{5,7},{6,4},{7,5},{8,10},{9,11},{10,... | collective-permute-start | bytes 294920 | tf_op jit(solution)/shard_map/ppermute | solution.py:374
  74.5 4.1 %weight_grads.1 = (bf16[1,768,1536]{2,1,0:T(8,128)(2,1)}, bf16[1,768,1536]{2,1,0:T(8,128)(2,1)}) custom-call(s32[6]{0:T(128)S(1)} %stack.34.facts_ref, bf16[768,128]{1,0:T(8,128)(2,1)S(1)} %get-tuple-element.65.a0, bf16[768,128]{1,0:T(8,128)(2,1)S(1)} %get-tuple-element.66.a1, bf16[768,128]{1,0:T(8,128)(2,1)S(1)} %get-tuple-element.69.b0, ...), custom_call_target="tpu_custom_call" | custom-call | flops 1 | bytes 1 | tf_op jit(solution)/shard_map/weight_grads/pallas_call | solution.py:216
  78.5 1.6 %collective-permute-done.12.refs_1_ = bf16[32,1536]{1,0:T(8,128)(2,1)S(1)} collective-permute-done((bf16[32,1536]{1,0:T(8,128)(2,1)S(1)}, bf16[32,1536]{1,0:T(8,128)(2,1)S(1)}, u32[]{:S(2)}, u32[]{:S(2)}) %collective-permute-start.12) | collective-permute-done | bytes 98336 | tf_op jit(solution)/shard_map/ppermute | solution.py:374
  80.2 1.3 %assemble.1 = bf16[1,32,3072]{2,1,0:T(8,128)(2,1)} custom-call(s32[6]{0:T(128)S(1)} %stack.34.facts_ref, bf16[32,1536]{1,0:T(8,128)(2,1)S(1)} %get-tuple-element.72.refs_0_, bf16[32,1536]{1,0:T(8,128)(2,1)S(1)} %collective-permute-done.12.refs_1_, bf16[32,1536]{1,0:T(8,128)(2,1)S(1)} %collective-permute-done.15.refs_2_, ...), custom_call_target="tpu_custom_call" | custom-call | tf_op jit(solution)/shard_map/assemble/pallas_call | solution.py:184
  (38 shorter events, 6.6 us)
Async XLA Ops:
  2.3 8.3 %collective-permute-start = (bf16[48,1536]{1,0:T(8,128)(2,1)S(1)}, bf16[48,1536]{1,0:T(8,128)(2,1)S(1)}, u32[]{:S(2)}, u32[]{:S(2)}) collective-permute-start(bf16[48,1536]{1,0:T(8,128)(2,1)S(1)} %concatenate.6), channel_id=1, source_target_pairs={{0,4},{4,0},{1,5},{5,1},{2,6},{6,2},{3,7},{7,3},{8,12},{12,8},{9,1... | collective-permute-start | bytes 442376 | tf_op jit(solution)/shard_map/ppermute | solution.py:368
  10.5 12.3 %collective-permute-start.1 = (bf16[1408,128]{1,0:T(8,128)(2,1)S(1)}, bf16[1408,128]{1,0:T(8,128)(2,1)S(1)}, u32[]{:S(2)}, u32[]{:S(2)}) collective-permute-start(bf16[1408,128]{1,0:T(8,128)(2,1)S(1)} %get-tuple-element.41.probs_ref), channel_id=1, source_target_pairs={{0,4},{4,0},{1,5},{5,1},{2,6},{6,2},{3,7},{7,3},{8,12},{12,8},{9,1... | collective-permute-start | bytes 1081352 | tf_op jit(solution)/shard_map/ppermute | solution.py:368
  21.2 7.8 %collective-permute-start.2 = (bf16[768,128]{1,0:T(8,128)(2,1)S(1)}, bf16[768,128]{1,0:T(8,128)(2,1)S(1)}, u32[]{:S(2)}, u32[]{:S(2)}) collective-permute-start(bf16[768,128]{1,0:T(8,128)(2,1)S(1)} %project.5.mine_ref), channel_id=1, source_target_pairs={{0,4},{4,0},{1,5},{5,1},{2,6},{6,2},{3,7},{7,3},{8,12},{12,8},{9,1... | collective-permute-start | bytes 589832 | tf_op jit(solution)/shard_map/ppermute | solution.py:368
  24.1 8.6 %collective-permute-start.4 = (bf16[768,128]{1,0:T(8,128)(2,1)S(1)}, bf16[768,128]{1,0:T(8,128)(2,1)S(1)}, u32[]{:S(2)}, u32[]{:S(2)}) collective-permute-start(bf16[768,128]{1,0:T(8,128)(2,1)S(1)} %project.4.mine_ref), channel_id=1, source_target_pairs={{0,4},{4,0},{1,5},{5,1},{2,6},{6,2},{3,7},{7,3},{8,12},{12,8},{9,1... | collective-permute-start | bytes 589832 | tf_op jit(solution)/shard_map/ppermute | solution.py:368
  24.7 15.9 %slice-start = ((s8[4718592]{0:T(1024)(128)(4,1)}), s8[4194304]{0:T(1024)(128)(4,1)S(1)}, s32[]{:S(2)}) async-start(s8[4718592]{0:T(1024)(128)(4,1)} %bitcast.10), calls=%async_computation | async-start | bytes 8388608
  27.2 13.4 %slice-start.1 = ((s8[4718592]{0:T(1024)(128)(4,1)}), s8[524288]{0:T(1024)(128)(4,1)S(1)}, s32[]{:S(2)}) async-start(s8[4718592]{0:T(1024)(128)(4,1)} %bitcast.10), calls=%async_computation.1 | async-start | bytes 1048576
  30.4 3.8 %collective-permute-start.3 = (bf16[2,32,1536]{2,1,0:T(8,128)(2,1)S(1)}, bf16[2,32,1536]{2,1,0:T(8,128)(2,1)S(1)}, u32[]{:S(2)}, u32[]{:S(2)}) collective-permute-start(bf16[2,32,1536]{2,1,0:T(8,128)(2,1)S(1)} %get-tuple-element.45), channel_id=1, source_target_pairs={{0,1},{1,0},{2,3},{3,2},{4,5},{5,4},{6,7},{7,6},{8,9},{9,8},{10,11... | collective-permute-start | bytes 589832 | tf_op jit(solution)/shard_map/ppermute | solution.py:371
  34.2 2.8 %collective-permute-start.5 = (bf16[2,32,1536]{2,1,0:T(8,128)(2,1)S(1)}, bf16[2,32,1536]{2,1,0:T(8,128)(2,1)S(1)}, u32[]{:S(2)}, u32[]{:S(2)}) collective-permute-start(bf16[2,32,1536]{2,1,0:T(8,128)(2,1)S(1)} %get-tuple-element.50), channel_id=1, source_target_pairs={{0,1},{1,0},{2,3},{3,2},{4,5},{5,4},{6,7},{7,6},{8,9},{9,8},{10,11... | collective-permute-start | bytes 589832 | tf_op jit(solution)/shard_map/ppermute | solution.py:371
  34.9 6.8 %collective-permute-start.6 = (bf16[32,1536]{1,0:T(8,128)(2,1)S(1)}, bf16[32,1536]{1,0:T(8,128)(2,1)S(1)}, u32[]{:S(2)}, u32[]{:S(2)}) collective-permute-start(bf16[32,1536]{1,0:T(8,128)(2,1)S(1)} %get-tuple-element.46.refs_0_), channel_id=1, source_target_pairs={{0,8},{1,9},{2,10},{3,11},{8,0},{9,1},{10,2},{11,3},{16,24},{17,25... | collective-permute-start | bytes 294920 | tf_op jit(solution)/shard_map/ppermute | solution.py:390
  36.4 6.5 %collective-permute-start.7 = (bf16[32,1536]{1,0:T(8,128)(2,1)S(1)}, bf16[32,1536]{1,0:T(8,128)(2,1)S(1)}, u32[]{:S(2)}, u32[]{:S(2)}) collective-permute-start(bf16[32,1536]{1,0:T(8,128)(2,1)S(1)} %get-tuple-element.47.refs_1_), channel_id=1, source_target_pairs={{0,10},{1,11},{2,8},{3,9},{8,2},{9,3},{10,0},{11,1},{16,26},{17,27... | collective-permute-start | bytes 294920 | tf_op jit(solution)/shard_map/ppermute | solution.py:390
  37.6 15.0 %collective-permute-start.8 = (bf16[32,1536]{1,0:T(8,128)(2,1)S(1)}, bf16[32,1536]{1,0:T(8,128)(2,1)S(1)}, u32[]{:S(2)}, u32[]{:S(2)}) collective-permute-start(bf16[32,1536]{1,0:T(8,128)(2,1)S(1)} %get-tuple-element.51.refs_0_), channel_id=1, source_target_pairs={{0,8},{1,9},{2,10},{3,11},{8,0},{9,1},{10,2},{11,3},{16,24},{17,25... | collective-permute-start | bytes 294920 | tf_op jit(solution)/shard_map/ppermute | solution.py:390
  39.1 13.5 %collective-permute-start.9 = (bf16[32,1536]{1,0:T(8,128)(2,1)S(1)}, bf16[32,1536]{1,0:T(8,128)(2,1)S(1)}, u32[]{:S(2)}, u32[]{:S(2)}) collective-permute-start(bf16[32,1536]{1,0:T(8,128)(2,1)S(1)} %get-tuple-element.52.refs_1_), channel_id=1, source_target_pairs={{0,10},{1,11},{2,8},{3,9},{8,2},{9,3},{10,0},{11,1},{16,26},{17,27... | collective-permute-start | bytes 294920 | tf_op jit(solution)/shard_map/ppermute | solution.py:390
  51.0 10.5 %collective-permute-start.13 = (bf16[768,128]{1,0:T(8,128)(2,1)S(1)}, bf16[768,128]{1,0:T(8,128)(2,1)S(1)}, u32[]{:S(2)}, u32[]{:S(2)}) collective-permute-start(bf16[768,128]{1,0:T(8,128)(2,1)S(1)} %project.6.mine_ref), channel_id=1, source_target_pairs={{0,4},{4,0},{1,5},{5,1},{2,6},{6,2},{3,7},{7,3},{8,12},{12,8},{9,1... | collective-permute-start | bytes 589832 | tf_op jit(solution)/shard_map/ppermute | solution.py:368
  60.9 7.2 %collective-permute-start.10 = (bf16[768,128]{1,0:T(8,128)(2,1)S(1)}, bf16[768,128]{1,0:T(8,128)(2,1)S(1)}, u32[]{:S(2)}, u32[]{:S(2)}) collective-permute-start(bf16[768,128]{1,0:T(8,128)(2,1)S(1)} %project.7.mine_ref), channel_id=1, source_target_pairs={{0,4},{4,0},{1,5},{5,1},{2,6},{6,2},{3,7},{7,3},{8,12},{12,8},{9,1... | collective-permute-start | bytes 589832 | tf_op jit(solution)/shard_map/ppermute | solution.py:368
  63.0 6.6 %collective-permute-start.14 = (bf16[2,32,1536]{2,1,0:T(8,128)(2,1)S(1)}, bf16[2,32,1536]{2,1,0:T(8,128)(2,1)S(1)}, u32[]{:S(2)}, u32[]{:S(2)}) collective-permute-start(bf16[2,32,1536]{2,1,0:T(8,128)(2,1)S(1)} %get-tuple-element.62), channel_id=1, source_target_pairs={{0,1},{1,0},{2,3},{3,2},{4,5},{5,4},{6,7},{7,6},{8,9},{9,8},{10,11... | collective-permute-start | bytes 589832 | tf_op jit(solution)/shard_map/ppermute | solution.py:371
  69.5 3.5 %collective-permute-start.11 = (bf16[2,32,1536]{2,1,0:T(8,128)(2,1)S(1)}, bf16[2,32,1536]{2,1,0:T(8,128)(2,1)S(1)}, u32[]{:S(2)}, u32[]{:S(2)}) collective-permute-start(bf16[2,32,1536]{2,1,0:T(8,128)(2,1)S(1)} %get-tuple-element.58), channel_id=1, source_target_pairs={{0,1},{1,0},{2,3},{3,2},{4,5},{5,4},{6,7},{7,6},{8,9},{9,8},{10,11... | collective-permute-start | bytes 589832 | tf_op jit(solution)/shard_map/ppermute | solution.py:371
  70.2 8.3 %collective-permute-start.15 = (bf16[32,1536]{1,0:T(8,128)(2,1)S(1)}, bf16[32,1536]{1,0:T(8,128)(2,1)S(1)}, u32[]{:S(2)}, u32[]{:S(2)}) collective-permute-start(bf16[32,1536]{1,0:T(8,128)(2,1)S(1)} %get-tuple-element.63), channel_id=1, source_target_pairs={{0,4},{1,5},{2,6},{3,7},{4,0},{5,1},{6,2},{7,3},{8,12},{9,13},{10,... | collective-permute-start | bytes 294920 | tf_op jit(solution)/shard_map/ppermute | solution.py:382
  70.8 7.7 %collective-permute-start.16 = (bf16[32,1536]{1,0:T(8,128)(2,1)S(1)}, bf16[32,1536]{1,0:T(8,128)(2,1)S(1)}, u32[]{:S(2)}, u32[]{:S(2)}) collective-permute-start(bf16[32,1536]{1,0:T(8,128)(2,1)S(1)} %get-tuple-element.64), channel_id=1, source_target_pairs={{0,6},{1,7},{2,4},{3,5},{4,2},{5,3},{6,0},{7,1},{8,14},{9,15},{10,... | collective-permute-start | bytes 294920 | tf_op jit(solution)/shard_map/ppermute | solution.py:382
  73.6 6.6 %collective-permute-start.12 = (bf16[32,1536]{1,0:T(8,128)(2,1)S(1)}, bf16[32,1536]{1,0:T(8,128)(2,1)S(1)}, u32[]{:S(2)}, u32[]{:S(2)}) collective-permute-start(bf16[32,1536]{1,0:T(8,128)(2,1)S(1)} %get-tuple-element.60), channel_id=1, source_target_pairs={{0,2},{1,3},{2,0},{3,1},{4,6},{5,7},{6,4},{7,5},{8,10},{9,11},{10,... | collective-permute-start | bytes 294920 | tf_op jit(solution)/shard_map/ppermute | solution.py:374

commit v8 on v7

--- a/solution.py
+++ b/solution.py
@@ -50,32 +50,61 @@
     return (jnp.max(note_ref[...].astype(jnp.float32)) > 0.5).astype(jnp.int32)
 
 
-def project_kernel(index, spot, facts_ref, note_ref, *refs):
-    tables, (tokens_ref, partial_ref) = refs[:-2], refs[-2:]
+def first_project_kernel(index, facts_ref, note_ref, table_ref, tokens_ref, partial_ref):
     version = picked_version(index, facts_ref, note_ref)
-    flipped = tokens_ref[spot].T
+    partial = matmul(table_ref[0, version], tokens_ref[index].T, NN)
+    partial_ref[...] = partial.astype(jnp.bfloat16)
+
+
+def first_project(index, facts, note, table, tokens):
+    rows = table.shape[2]
+    return pl.pallas_call(
+        functools.partial(first_project_kernel, index),
+        out_shape=jax.ShapeDtypeStruct((rows, tokens.shape[1]), jnp.bfloat16),
+        in_specs=[in_smem()] + [in_vmem()] * 3,
+        out_specs=in_vmem(),
+        compiler_params=pltpu.CompilerParams(vmem_limit_bytes=VMEM_BYTES),
+        cost_estimate=SMALL,
+        name="first_project",
+    )(facts, note, table, tokens)
+
+
+def project_kernel(
+    index, outer, facts_ref, note_ref, value_ref, out_ref, mine_ref, theirs_ref, partial_ref, full_ref
+):
+    version = picked_version(index, facts_ref, note_ref)
+    first_core = facts_ref[CORE] == 0
+    shard = mine_ref.shape[0] // outer
+    for place in range(outer):
+        mine = mine_ref[place * shard : (place + 1) * shard, :]
+        theirs = theirs_ref[place * shard : (place + 1) * shard, :]
+        start = 2 * place * shard
+        full_ref[start : start + shard, :] = jnp.where(first_core, mine, theirs)
+        full_ref[start + shard : start + 2 * shard, :] = jnp.where(first_core, theirs, mine)
+    flipped = full_ref[...].T
 
     def rows_of(table_ref):
         partial_ref[...] = matmul(table_ref[0, version], flipped, NN).astype(jnp.bfloat16)
 
-    if len(tables) == 1:
-        rows_of(tables[0])
-    else:
-        pl.when(facts_ref[ODD] == 1)(lambda: rows_of(tables[0]))
-        pl.when(facts_ref[ODD] == 0)(lambda: rows_of(tables[1]))
-
-
-def project(index, spot, facts, note, tables, tokens):
+    pl.when(facts_ref[ODD] == 1)(lambda: rows_of(value_ref))
+    pl.when(facts_ref[ODD] == 0)(lambda: rows_of(out_ref))
+
+
+def project(index, outer, facts, note, tables, mine, theirs):
     rows = tables[0].shape[2]
-    return pl.pallas_call(
-        functools.partial(project_kernel, index, spot),
-        out_shape=jax.ShapeDtypeStruct((rows, tokens.shape[1]), jnp.bfloat16),
-        in_specs=[in_smem()] + [in_vmem()] * (2 + len(tables)),
-        out_specs=in_vmem(),
+    tokens, width = 2 * mine.shape[0], mine.shape[1]
+    return pl.pallas_call(
+        functools.partial(project_kernel, index, outer),
+        out_shape=(
+            jax.ShapeDtypeStruct((rows, tokens), jnp.bfloat16),
+            jax.ShapeDtypeStruct((tokens, width), jnp.bfloat16),
+        ),
+        in_specs=[in_smem()] + [in_vmem()] * 5,
+        out_specs=(in_vmem(), in_vmem()),
         compiler_params=pltpu.CompilerParams(vmem_limit_bytes=VMEM_BYTES),
         cost_estimate=SMALL,
         name="project",
-    )(facts, note, *tables, tokens)
+    )(facts, note, *tables, mine, theirs)
 
 
 def mix_kernel(
@@ -141,7 +170,8 @@
         spot = facts_ref[ROW] ^ delta
         total = keep_ref[spot].astype(jnp.float32) + arrived_ref[spot].astype(jnp.float32)
         if delta == 0:
-            total = total + addend_ref[index].astype(jnp.float32)
+            addend = addend_ref[...] if index is None else addend_ref[index]
+            total = total + addend.astype(jnp.float32)
         total = total.astype(jnp.bfloat16)
         if last:
             total = jnp.where(facts_ref[ODD] == 1, first_refs[delta][...], total)
@@ -196,7 +226,7 @@
     tokens = a0.shape[1]
     left_first = jnp.concatenate([a0[...], a1[...]], axis=1)
     left_second = jnp.concatenate([b0[...], b1[...]], axis=1)
-    right_second = jnp.concatenate([second0[0], second1[0]], axis=0)
+    right_second = jnp.concatenate([second0[...], second1[...]], axis=0)
     right_first = first[...].reshape(2 * tokens, first.shape[2])
     grad_first = matmul(left_first, right_second, NN)
     grad_second = matmul(left_second, right_first, NN)
@@ -211,7 +241,7 @@
     grad = jax.ShapeDtypeStruct((1, rows, width), jnp.bfloat16)
     left = pl.BlockSpec((step, tokens), lambda i: (i, 0))
     both = pl.BlockSpec((2, tokens, width), lambda i: (0, 0, 0))
-    single = pl.BlockSpec((1, tokens, width), lambda i: (0, 0, 0))
+    single = pl.BlockSpec((tokens, width), lambda i: (0, 0))
     wide = pl.BlockSpec((1, step, width), lambda i: (0, i, 0))
     return pl.pallas_call(
         weight_grad_kernel,
@@ -319,31 +349,31 @@
 
 def arrive_kernel(index, facts_ref, source_ref, *refs):
     parts, piece_ref = refs[:-1], refs[-1]
-    shard, width = piece_ref.shape[1:]
+    shard, width = piece_ref.shape
 
     @pl.when(facts_ref[ODD] == 1)
     def _():
         if index == 0:
-            piece_ref[0] = source_ref[...]
+            piece_ref[...] = source_ref[...]
         else:
             first_row = source_ref.shape[0] - width // LANES * shard
             for block in range(width // LANES):
                 start = first_row + block * shard
                 columns = pl.ds(block * LANES, LANES)
-                piece_ref[0, :, columns] = source_ref[start : start + shard, :]
+                piece_ref[:, columns] = source_ref[start : start + shard, :]
 
     @pl.when(facts_ref[ODD] == 0)
     def _():
         total = parts[0][...].astype(jnp.float32)
         for part in parts[1:]:
             total = total + part[...].astype(jnp.float32)
-        piece_ref[0] = total.astype(jnp.bfloat16)
+        piece_ref[...] = total.astype(jnp.bfloat16)
 
 
 def arrive(index, facts, source, parts):
     return pl.pallas_call(
         functools.partial(arrive_kernel, index),
-        out_shape=jax.ShapeDtypeStruct((1,) + parts[0].shape, jnp.bfloat16),
+        out_shape=jax.ShapeDtypeStruct(parts[0].shape, jnp.bfloat16),
         in_specs=[in_smem()] + [in_vmem()] * (1 + len(parts)),
         out_specs=in_vmem(),
         compiler_params=pltpu.CompilerParams(vmem_limit_bytes=VMEM_BYTES),
@@ -356,11 +386,10 @@
     half = lax.axis_index("half")
     odd_flag = lax.axis_index("pair") % 2
     odd = odd_flag == 1
-    place = lax.axis_index("tensor")
-    core, row = place % 2, place // 2
+    core, row = lax.axis_index("core"), lax.axis_index("outer")
     n_pairs = lax.axis_size("pair")
-    n_tensor = lax.axis_size("tensor")
-    outer = n_tensor // 2
+    outer = lax.axis_size("outer")
+    n_tensor = 2 * outer
     width = w_value.shape[3]
     shard = section_input.shape[1]
 
@@ -368,10 +397,10 @@
         return lax.ppermute(array, "half", [(0, 1), (1, 0)])
 
     def swap_core(array):
-        return lax.ppermute(array, "tensor", [(i, i ^ 1) for i in range(n_tensor)])
+        return lax.ppermute(array, "core", [(0, 1), (1, 0)])
 
     def to_row(array, delta):
-        return lax.ppermute(array, "tensor", [(i, i ^ (2 * delta)) for i in range(n_tensor)])
+        return lax.ppermute(array, "outer", [(i, i ^ delta) for i in range(outer)])
 
     def to_other_half(array, delta):
         pairs = [
@@ -379,7 +408,7 @@
             for h in range(2)
             for i in range(n_tensor)
         ]
-        return lax.ppermute(array, ("half", "tensor"), pairs)
+        return lax.ppermute(array, ("half", "outer", "core"), pairs)
 
     def swap_section(array, delta):
         pairs = [
@@ -387,7 +416,7 @@
             for p in range(n_pairs)
             for i in range(n_tensor)
         ]
-        return lax.ppermute(array, ("pair", "tensor"), pairs)
+        return lax.ppermute(array, ("pair", "outer", "core"), pairs)
 
     def own_columns(array):
         return lax.dynamic_slice_in_dim(array, half * width, width, 1)
@@ -396,7 +425,7 @@
         return lax.dynamic_slice_in_dim(array, (1 - half) * width, width, 1)
 
     def gathered(pair):
-        return lax.all_gather(pair, "tensor", axis=1, tiled=True)
+        return lax.all_gather(pair, ("outer", "core"), axis=1, tiled=True)
 
     facts = jnp.stack([odd_flag, 1 - odd_flag, version[0], core, row, half])
     inputs = jnp.stack([jnp.where(odd, incoming[0], section_input[0]), section_input[0]])
@@ -415,7 +444,7 @@
     partial = [None, None]
     for m in (1, 0):
         tokens = first_full if m else own_full
-        partial[m] = project(m, m, facts, other_note, (first_table,), tokens)
+        partial[m] = first_project(m, facts, other_note, first_table, tokens)
     arrived = [swap_half(partial[1]), swap_half(partial[0])]
     later_value, _ = lax.optimization_barrier((w_value, partial))
     value_table = load_table(later_value, VALUE_VMEM_BYTES)
@@ -434,9 +463,9 @@
         received = [swap_section(part, d) for d, part in enumerate(first_sent[m])]
         second_piece[m] = arrive(m, facts, sources[m], received)
     for m in range(2):
-        second_full[m] = gathered(second_piece[m])
-        partial[m] = project(
-            m, 0, facts, other_note, (value_table, out_table), second_full[m]
+        mine = lax.all_gather(second_piece[m], "outer", axis=0, tiled=True)
+        partial[m], second_full[m] = project(
+            m, outer, facts, other_note, (value_table, out_table), mine, swap_core(mine)
         )
     arrived = [swap_half(partial[1]), swap_half(partial[0])]
     second_result, last_sent = [None, None], [None, None]
@@ -444,7 +473,7 @@
         second_result[m], keep, send = mix(
             EVEN, m, facts, other_note, messages[m], value_table, partial[m], arrived[m], outer
         )
-        last_sent[m] = combine(0, facts, keep, swap_core(send), second_piece[m], first_sent[m])
+        last_sent[m] = combine(None, facts, keep, swap_core(send), second_piece[m], first_sent[m])
     other_parts = [to_other_half(part, d) for d, part in enumerate(last_sent[1])]
     own_parts = [last_sent[0][0]] + [to_row(part, d + 1) for d, part in enumerate(last_sent[0][1:])]
     second_result, _ = lax.optimization_barrier((second_result, last_sent))
@@ -458,10 +487,12 @@
 
 def solution(mesh):
     sections, tensor = mesh.devices.shape
-    split = Mesh(mesh.devices.reshape(sections // 2, 2, tensor), ("pair", "half", "tensor"))
-    slots = ("pair", "half")
-    by_tokens = P(slots, "tensor", None)
-    by_rows = P(slots, None, "tensor", None)
+    split = Mesh(
+        mesh.devices.reshape(sections // 2, 2, tensor // 2, 2), ("pair", "half", "outer", "core")
+    )
+    slots, places = ("pair", "half"), ("outer", "core")
+    by_tokens = P(slots, places, None)
+    by_rows = P(slots, None, places, None)
     return jax.shard_map(
         on_device,
         mesh=split,

time: 81.7 us -> 81.8 us (level)
  waiting for transfers between devices: 11.8 us -> 13.2 us
  blocking collectives: 21.6 us -> 20.3 us
    ppermute x6, waiting for transfers between devices: 8.89 us -> 10.3 us  [swap_half(): return lax.ppermute(array, 'half', [(0, 1), (1, 0)])]
    all_gather x3, blocking collectives: 21.6 us -> 20.3 us  [the longest x2 11.2 us: on_device(): mine = lax.all_gather(second_piece[m], 'outer', axis=0, tiled=True)]
    ppermute x11 -> x13, starting transfers between devices: 9.04 us -> 8.99 us  [the longest x4 5.08 us: swap_section(): return lax.ppermute(array, ('pair', 'outer', 'core'), pairs)]
    ppermute x11 -> x13, waiting for transfers between devices: 2.92 us -> 2.9 us  [the longest x1 1.59 us: to_row(): return lax.ppermute(array, 'outer', [(i, i ^ delta) for i in range(outer)])]
  transfers between devices with their start and end apart: 17 -> 19, of which waited for: 5 -> 6; matrix products, arithmetic and copies ran while one was open for 3% -> 3% of each run, Pallas kernels for 31% -> 31%
where the time goes in v8:
time: 81.8 us; the launch traced here: 81.5 us
  Pallas kernels  26.9 us (33%)
  blocking collectives  20.3 us (25%)
  starting transfers between devices  16.4 us (20%)
  waiting for transfers between devices  13.2 us (16%)
  other arithmetic  3.01 us (4%)
  between operations  1.56 us (2%)
    all_gather x2, blocking collectives, on_device(): mine = lax.all_gather(second_piece[m], 'outer', axis=0, tiled=True)  11.2 us
    ppermute x6, waiting for transfers between devices, swap_half(): return lax.ppermute(array, 'half', [(0, 1), (1, 0)])  10.3 us
    all_gather x1, blocking collectives, gathered(): return lax.all_gather(pair, ('outer', 'core'), axis=1, tiled=True)  9.14 us
    ppermute x6, starting transfers between devices, swap_half(): return lax.ppermute(array, 'half', [(0, 1), (1, 0)])  7.4 us
    pallas_call x4, Pallas kernels, mix(): pl.pallas_call(functools.partial(mix_kernel, outer, natural, index), out_...  5.87 us
    ppermute x4, starting transfers between devices, swap_section(): return lax.ppermute(array, ('pair', 'outer', 'core'), pairs)  5.08 us
    pallas_call x1, Pallas kernels, weight_grads(): pl.pallas_call(weight_grad_kernel, grid=(CHUNKS,), out_shape=(grad, grad)...  4.06 us
    pallas_call x2, Pallas kernels, load_table(): pl.pallas_call(load_kernel, out_shape=jax.ShapeDtypeStruct(table.shape, j...  3.57 us
  transfers between devices with their start and end apart: 19, of which 6 were waited for; matrix products, arithmetic and copies ran while one was open for 3% of the time, Pallas kernels for 31%

profile of v8, /device:TPU:0, one launch (start us, length us, event | category | flops | bytes accessed | tf_op | source)
XLA Modules:
  0.0 81.5 jit_solution(17080550352439135165)
XLA Ops:
  1.3 1.0 %broadcast_select_fusion = bf16[1,32,3072]{2,1,0:T(8,128)(2,1)S(1)} fusion(bf16[1,32,3072]{2,1,0:T(8,128)(2,1)} %param.10, bf16[1,32,3072]{2,1,0:T(8,128)(2,1)} %param.7, pred[]{:T(512)S(6)} %eq.5), kind=kLoop, calls=%fused_computation.3 | loop fusion | flops 98304 | bytes 589825 | tf_op jit(solution)/shard_map/jit(_where)/select_n | solution.py:431
  2.3 3.0 %collective-permute-start = (bf16[48,1536]{1,0:T(8,128)(2,1)S(1)}, bf16[48,1536]{1,0:T(8,128)(2,1)S(1)}, u32[]{:S(2)}, u32[]{:S(2)}) collective-permute-start(bf16[48,1536]{1,0:T(8,128)(2,1)S(1)} %concatenate.6), channel_id=1, source_target_pairs={{0,4},{4,0},{1,5},{5,1},{2,6},{6,2},{3,7},{7,3},{8,12},{12,8},{9,1... | collective-permute-start | bytes 442376 | tf_op jit(solution)/shard_map/ppermute | solution.py:397
  5.3 1.0 %pad_maximum_fusion.1.input_ref = bf16[2,32,3072]{2,1,0:T(8,128)(2,1)S(1)} fusion(bf16[1,32,3072]{2,1,0:T(8,128)(2,1)} %param.7, bf16[1,32,3072]{2,1,0:T(8,128)(2,1)S(1)} %broadcast_select_fusion), kind=kLoop, calls=%fused_computation.1 | loop fusion | flops 196608 | bytes 786432 | tf_op jit(solution)/shard_map/stack | solution.py:431
  6.4 1.1 %pad_maximum_fusion.stash_ref = bf16[2,768,128]{2,1,0:T(8,128)(2,1)S(1)} fusion(bf16[1,768,128]{2,1,0:T(8,128)(2,1)} %param.9, bf16[1,768,128]{2,1,0:T(8,128)(2,1)} %param.8), kind=kLoop, calls=%fused_computation | loop fusion | flops 196608 | bytes 786432 | tf_op jit(solution)/shard_map/concatenate | solution.py:437
  7.4 3.0 %pack.1 = (bf16[1408,128]{1,0:T(8,128)(2,1)S(1)}, bf16[32,1536]{1,0:T(8,128)(2,1)S(1)}, bf16[1,2,768,1536]{3,2,1,0:T(8,128)(2,1)S(1)}) custom-call(s32[6]{0:T(128)S(1)} %stack.34.facts_ref, bf16[2,768,128]{2,1,0:T(8,128)(2,1)S(1)} %pad_maximum_fusion.stash_ref, bf16[2,32,3072]{2,1,0:T(8,128)(2,1)S(1)} %pad_maximum_fusion.1.input_ref, ...), custom_call_target="tpu_custom_call" | custom-call | flops 1 | bytes 1 | tf_op jit(solution)/shard_map/pack/pallas_call | solution.py:313
  10.6 9.1 %all_gather.9.tokens_ref.first = bf16[2,128,1536]{2,1,0:T(8,128)(2,1)S(1)} all-gather(bf16[2,32,1536]{2,1,0:T(8,128)(2,1)S(1)} %pad_maximum_fusion.2.addend_ref), channel_id=1, replica_groups=mesh['pair'=4,'half'=2,'outer'=2,'core'=2] {'outer','core'}, dimensions={1}, use_global_device_ids=true | all-gather | bytes 983040 | tf_op jit(solution)/shard_map/all_gather | solution.py:428
  19.8 1.4 %first_project.3.mine_ref = bf16[768,128]{1,0:T(8,128)(2,1)S(1)} custom-call(s32[6]{0:T(128)S(1)} %stack.34.facts_ref, bf16[16,1536]{1,0:T(8,128)(2,1)S(1)} %slice.8.note_ref, bf16[1,2,768,1536]{3,2,1,0:T(8,128)(2,1)S(1)} %get-tuple-element.44.table_ref, bf16[2,128,1536]{2,1,0:T(8,128)(2,1)S(1)} %all_gather.9.tokens_ref.first), custom_call_target="tpu_custom_call" | custom-call | flops 1 | bytes 1 | tf_op jit(solution)/shard_map/first_project/pallas_call | solution.py:61
  21.2 1.6 %collective-permute-start.2 = (bf16[768,128]{1,0:T(8,128)(2,1)S(1)}, bf16[768,128]{1,0:T(8,128)(2,1)S(1)}, u32[]{:S(2)}, u32[]{:S(2)}) collective-permute-start(bf16[768,128]{1,0:T(8,128)(2,1)S(1)} %first_project.3.mine_ref), channel_id=1, source_target_pairs={{0,4},{4,0},{1,5},{5,1},{2,6},{6,2},{3,7},{7,3},{8,12},{12,8},{9,1... | collective-permute-start | bytes 589832 | tf_op jit(solution)/shard_map/ppermute | solution.py:397
  22.7 1.3 %first_project.2.mine_ref = bf16[768,128]{1,0:T(8,128)(2,1)S(1)} custom-call(s32[6]{0:T(128)S(1)} %stack.34.facts_ref, bf16[16,1536]{1,0:T(8,128)(2,1)S(1)} %slice.8.note_ref, bf16[1,2,768,1536]{3,2,1,0:T(8,128)(2,1)S(1)} %get-tuple-element.44.table_ref, bf16[2,128,1536]{2,1,0:T(8,128)(2,1)S(1)} %all_gather.9.tokens_ref.first), custom_call_target="tpu_custom_call" | custom-call | flops 1 | bytes 1 | tf_op jit(solution)/shard_map/first_project/pallas_call | solution.py:61
  24.6 2.5 %load_table.2.value_ref = bf16[1,2,768,1536]{3,2,1,0:T(8,128)(2,1)S(1)} custom-call(bf16[1,2,768,1536]{3,2,1,0:T(8,128)(2,1)} %source_ref), custom_call_target="tpu_custom_call" | custom-call | flops 1 | bytes 1 | tf_op jit(solution)/shard_map/load_table/pallas_call | solution.py:338
  27.2 1.8 %collective-permute-done.2.arrived_ref = bf16[768,128]{1,0:T(8,128)(2,1)S(1)} collective-permute-done((bf16[768,128]{1,0:T(8,128)(2,1)S(1)}, bf16[768,128]{1,0:T(8,128)(2,1)S(1)}, u32[]{:S(2)}, u32[]{:S(2)}) %collective-permute-start.2) | collective-permute-done | bytes 196640 | tf_op jit(solution)/shard_map/ppermute | solution.py:397
  29.0 1.5 %mix.4 = (bf16[768,128]{1,0:T(8,128)(2,1)S(1)}, bf16[2,32,1536]{2,1,0:T(8,128)(2,1)S(1)}, bf16[2,32,1536]{2,1,0:T(8,128)(2,1)S(1)}) custom-call(s32[6]{0:T(128)S(1)} %stack.34.facts_ref, bf16[16,1536]{1,0:T(8,128)(2,1)S(1)} %slice.8.note_ref, bf16[1,2,768,1536]{3,2,1,0:T(8,128)(2,1)S(1)} %load_table.2.value_ref, bf16[768,128]{1,0:T(8,128)(2,1)S(1)} %first_project.2.mine_ref, ...), custom_call_target="tpu_custom_call" | custom-call | flops 1 | bytes 1 | tf_op jit(solution)/shard_map/mix/pallas_call | solution.py:156
  30.5 2.1 %collective-permute-done.4.arrived_ref = bf16[768,128]{1,0:T(8,128)(2,1)S(1)} collective-permute-done((bf16[768,128]{1,0:T(8,128)(2,1)S(1)}, bf16[768,128]{1,0:T(8,128)(2,1)S(1)}, u32[]{:S(2)}, u32[]{:S(2)}) %collective-permute-start.4) | collective-permute-done | bytes 196640 | tf_op jit(solution)/shard_map/ppermute | solution.py:397
  32.6 1.6 %mix.5 = (bf16[768,128]{1,0:T(8,128)(2,1)S(1)}, bf16[2,32,1536]{2,1,0:T(8,128)(2,1)S(1)}, bf16[2,32,1536]{2,1,0:T(8,128)(2,1)S(1)}) custom-call(s32[6]{0:T(128)S(1)} %stack.34.facts_ref, bf16[16,1536]{1,0:T(8,128)(2,1)S(1)} %slice.8.note_ref, bf16[1,2,768,1536]{3,2,1,0:T(8,128)(2,1)S(1)} %load_table.2.value_ref, bf16[768,128]{1,0:T(8,128)(2,1)S(1)} %first_project.3.mine_ref, ...), custom_call_target="tpu_custom_call" | custom-call | flops 1 | bytes 1 | tf_op jit(solution)/shard_map/mix/pallas_call | solution.py:156
  34.9 1.5 %collective-permute-start.6 = (bf16[32,1536]{1,0:T(8,128)(2,1)S(1)}, bf16[32,1536]{1,0:T(8,128)(2,1)S(1)}, u32[]{:S(2)}, u32[]{:S(2)}) collective-permute-start(bf16[32,1536]{1,0:T(8,128)(2,1)S(1)} %get-tuple-element.50.refs_0_), channel_id=1, source_target_pairs={{0,8},{1,9},{2,10},{3,11},{8,0},{9,1},{10,2},{11,3},{16,24},{17,25... | collective-permute-start | bytes 294920 | tf_op jit(solution)/shard_map/ppermute | solution.py:419
  37.6 2.4 %collective-permute-start.10 = (bf16[32,1536]{1,0:T(8,128)(2,1)S(1)}, bf16[32,1536]{1,0:T(8,128)(2,1)S(1)}, u32[]{:S(2)}, u32[]{:S(2)}) collective-permute-start(bf16[32,1536]{1,0:T(8,128)(2,1)S(1)} %get-tuple-element.56.refs_1_), channel_id=1, source_target_pairs={{0,10},{1,11},{2,8},{3,9},{8,2},{9,3},{10,0},{11,1},{16,26},{17,27... | collective-permute-start | bytes 294920 | tf_op jit(solution)/shard_map/ppermute | solution.py:419
  40.6 1.0 %load_table.3.out_ref = bf16[1,2,768,1536]{3,2,1,0:T(8,128)(2,1)S(1)} custom-call(bf16[1,2,768,1536]{3,2,1,0:T(8,128)(2,1)S(1)} %bitcast.11), custom_call_target="tpu_custom_call" | custom-call | flops 1 | bytes 1 | tf_op jit(solution)/shard_map/load_table/pallas_call | solution.py:338
  41.6 1.3 %collective-permute-done.7.refs_1_ = bf16[32,1536]{1,0:T(8,128)(2,1)S(1)} collective-permute-done((bf16[32,1536]{1,0:T(8,128)(2,1)S(1)}, bf16[32,1536]{1,0:T(8,128)(2,1)S(1)}, u32[]{:S(2)}, u32[]{:S(2)}) %collective-permute-start.7) | collective-permute-done | bytes 98336 | tf_op jit(solution)/shard_map/ppermute | solution.py:419
  43.5 5.3 %all_gather.10.mine_ref = bf16[64,1536]{1,0:T(8,128)(2,1)S(1)} all-gather(bf16[32,1536]{1,0:T(8,128)(2,1)S(1)} %arrive.2.addend_ref), channel_id=1, replica_groups=mesh['pair'=4,'half'=2,'outer'=2,'core'=2] {'outer'}, dimensions={0}, use_global_device_ids=true | all-gather | bytes 294912 | tf_op jit(solution)/shard_map/all_gather | solution.py:466
  49.4 5.9 %all_gather.11.mine_ref = bf16[64,1536]{1,0:T(8,128)(2,1)S(1)} all-gather(bf16[32,1536]{1,0:T(8,128)(2,1)S(1)} %arrive.3.addend_ref), channel_id=1, replica_groups=mesh['pair'=4,'half'=2,'outer'=2,'core'=2] {'outer'}, dimensions={0}, use_global_device_ids=true | all-gather | bytes 294912 | tf_op jit(solution)/shard_map/all_gather | solution.py:466
  55.3 1.4 %project.2 = (bf16[768,128]{1,0:T(8,128)(2,1)S(1)}, bf16[128,1536]{1,0:T(8,128)(2,1)S(1)}) custom-call(s32[6]{0:T(128)S(1)} %stack.34.facts_ref, bf16[16,1536]{1,0:T(8,128)(2,1)S(1)} %slice.8.note_ref, bf16[1,2,768,1536]{3,2,1,0:T(8,128)(2,1)S(1)} %load_table.2.value_ref, bf16[1,2,768,1536]{3,2,1,0:T(8,128)(2,1)S(1)} %load_table.3.out_ref, ...), custom_call_target="tpu_custom_call" | custom-call | flops 1 | bytes 1 | tf_op jit(solution)/shard_map/project/pallas_call | solution.py:96
  56.6 1.6 %collective-permute-start.15 = (bf16[768,128]{1,0:T(8,128)(2,1)S(1)}, bf16[768,128]{1,0:T(8,128)(2,1)S(1)}, u32[]{:S(2)}, u32[]{:S(2)}) collective-permute-start(bf16[768,128]{1,0:T(8,128)(2,1)S(1)} %get-tuple-element.60.mine_ref), channel_id=1, source_target_pairs={{0,4},{4,0},{1,5},{5,1},{2,6},{6,2},{3,7},{7,3},{8,12},{12,8},{9,1... | collective-permute-start | bytes 589832 | tf_op jit(solution)/shard_map/ppermute | solution.py:397
  58.2 1.4 %project.3 = (bf16[768,128]{1,0:T(8,128)(2,1)S(1)}, bf16[128,1536]{1,0:T(8,128)(2,1)S(1)}) custom-call(s32[6]{0:T(128)S(1)} %stack.34.facts_ref, bf16[16,1536]{1,0:T(8,128)(2,1)S(1)} %slice.8.note_ref, bf16[1,2,768,1536]{3,2,1,0:T(8,128)(2,1)S(1)} %load_table.2.value_ref, bf16[1,2,768,1536]{3,2,1,0:T(8,128)(2,1)S(1)} %load_table.3.out_ref, ...), custom_call_target="tpu_custom_call" | custom-call | flops 1 | bytes 1 | tf_op jit(solution)/shard_map/project/pallas_call | solution.py:96
  60.3 4.2 %collective-permute-done.15.arrived_ref = bf16[768,128]{1,0:T(8,128)(2,1)S(1)} collective-permute-done((bf16[768,128]{1,0:T(8,128)(2,1)S(1)}, bf16[768,128]{1,0:T(8,128)(2,1)S(1)}, u32[]{:S(2)}, u32[]{:S(2)}) %collective-permute-start.15) | collective-permute-done | bytes 196640 | tf_op jit(solution)/shard_map/ppermute | solution.py:397
  64.4 1.4 %mix.7 = (bf16[768,128]{1,0:T(8,128)(2,1)S(1)}, bf16[2,32,1536]{2,1,0:T(8,128)(2,1)S(1)}, bf16[2,32,1536]{2,1,0:T(8,128)(2,1)S(1)}) custom-call(s32[6]{0:T(128)S(1)} %stack.34.facts_ref, bf16[16,1536]{1,0:T(8,128)(2,1)S(1)} %slice.8.note_ref, bf16[1,2,768,1536]{3,2,1,0:T(8,128)(2,1)S(1)} %load_table.2.value_ref, ...), custom_call_target="tpu_custom_call" | custom-call | flops 1 | bytes 1 | tf_op jit(solution)/shard_map/mix/pallas_call | solution.py:156
  65.9 2.3 %collective-permute-done.12.arrived_ref = bf16[768,128]{1,0:T(8,128)(2,1)S(1)} collective-permute-done((bf16[768,128]{1,0:T(8,128)(2,1)S(1)}, bf16[768,128]{1,0:T(8,128)(2,1)S(1)}, u32[]{:S(2)}, u32[]{:S(2)}) %collective-permute-start.12) | collective-permute-done | bytes 196640 | tf_op jit(solution)/shard_map/ppermute | solution.py:397
  68.2 1.4 %mix.6 = (bf16[768,128]{1,0:T(8,128)(2,1)S(1)}, bf16[2,32,1536]{2,1,0:T(8,128)(2,1)S(1)}, bf16[2,32,1536]{2,1,0:T(8,128)(2,1)S(1)}) custom-call(s32[6]{0:T(128)S(1)} %stack.34.facts_ref, bf16[16,1536]{1,0:T(8,128)(2,1)S(1)} %slice.8.note_ref, bf16[1,2,768,1536]{3,2,1,0:T(8,128)(2,1)S(1)} %load_table.2.value_ref, ...), custom_call_target="tpu_custom_call" | custom-call | flops 1 | bytes 1 | tf_op jit(solution)/shard_map/mix/pallas_call | solution.py:156
  70.3 1.6 %collective-permute-start.17 = (bf16[32,1536]{1,0:T(8,128)(2,1)S(1)}, bf16[32,1536]{1,0:T(8,128)(2,1)S(1)}, u32[]{:S(2)}, u32[]{:S(2)}) collective-permute-start(bf16[32,1536]{1,0:T(8,128)(2,1)S(1)} %get-tuple-element.69), channel_id=1, source_target_pairs={{0,4},{1,5},{2,6},{3,7},{4,0},{5,1},{6,2},{7,3},{8,12},{9,13},{10,... | collective-permute-start | bytes 294920 | tf_op jit(solution)/shard_map/ppermute | solution.py:411
  71.9 1.2 %collective-permute-start.18 = (bf16[32,1536]{1,0:T(8,128)(2,1)S(1)}, bf16[32,1536]{1,0:T(8,128)(2,1)S(1)}, u32[]{:S(2)}, u32[]{:S(2)}) collective-permute-start(bf16[32,1536]{1,0:T(8,128)(2,1)S(1)} %get-tuple-element.70), channel_id=1, source_target_pairs={{0,6},{1,7},{2,4},{3,5},{4,2},{5,3},{6,0},{7,1},{8,14},{9,15},{10,... | collective-permute-start | bytes 294920 | tf_op jit(solution)/shard_map/ppermute | solution.py:411
  74.6 4.1 %weight_grads.1 = (bf16[1,768,1536]{2,1,0:T(8,128)(2,1)}, bf16[1,768,1536]{2,1,0:T(8,128)(2,1)}) custom-call(s32[6]{0:T(128)S(1)} %stack.34.facts_ref, bf16[768,128]{1,0:T(8,128)(2,1)S(1)} %get-tuple-element.71.a0, bf16[768,128]{1,0:T(8,128)(2,1)S(1)} %get-tuple-element.72.a1, bf16[768,128]{1,0:T(8,128)(2,1)S(1)} %get-tuple-element.75.b0, ...), custom_call_target="tpu_custom_call" | custom-call | flops 1 | bytes 1 | tf_op jit(solution)/shard_map/weight_grads/pallas_call | solution.py:246
  78.7 1.6 %collective-permute-done.14.refs_1_ = bf16[32,1536]{1,0:T(8,128)(2,1)S(1)} collective-permute-done((bf16[32,1536]{1,0:T(8,128)(2,1)S(1)}, bf16[32,1536]{1,0:T(8,128)(2,1)S(1)}, u32[]{:S(2)}, u32[]{:S(2)}) %collective-permute-start.14) | collective-permute-done | bytes 98336 | tf_op jit(solution)/shard_map/ppermute | solution.py:403
  80.3 1.3 %assemble.1 = bf16[1,32,3072]{2,1,0:T(8,128)(2,1)} custom-call(s32[6]{0:T(128)S(1)} %stack.34.facts_ref, bf16[32,1536]{1,0:T(8,128)(2,1)S(1)} %get-tuple-element.80.refs_0_, bf16[32,1536]{1,0:T(8,128)(2,1)S(1)} %collective-permute-done.14.refs_1_, bf16[32,1536]{1,0:T(8,128)(2,1)S(1)} %collective-permute-done.17.refs_2_, ...), custom_call_target="tpu_custom_call" | custom-call | tf_op jit(solution)/shard_map/assemble/pallas_call | solution.py:214
  (42 shorter events, 7.5 us)
Async XLA Ops:
  2.3 8.2 %collective-permute-start = (bf16[48,1536]{1,0:T(8,128)(2,1)S(1)}, bf16[48,1536]{1,0:T(8,128)(2,1)S(1)}, u32[]{:S(2)}, u32[]{:S(2)}) collective-permute-start(bf16[48,1536]{1,0:T(8,128)(2,1)S(1)} %concatenate.6), channel_id=1, source_target_pairs={{0,4},{4,0},{1,5},{5,1},{2,6},{6,2},{3,7},{7,3},{8,12},{12,8},{9,1... | collective-permute-start | bytes 442376 | tf_op jit(solution)/shard_map/ppermute | solution.py:397
  10.5 12.3 %collective-permute-start.1 = (bf16[1408,128]{1,0:T(8,128)(2,1)S(1)}, bf16[1408,128]{1,0:T(8,128)(2,1)S(1)}, u32[]{:S(2)}, u32[]{:S(2)}) collective-permute-start(bf16[1408,128]{1,0:T(8,128)(2,1)S(1)} %get-tuple-element.45.probs_ref), channel_id=1, source_target_pairs={{0,4},{4,0},{1,5},{5,1},{2,6},{6,2},{3,7},{7,3},{8,12},{12,8},{9,1... | collective-permute-start | bytes 1081352 | tf_op jit(solution)/shard_map/ppermute | solution.py:397
  21.2 7.8 %collective-permute-start.2 = (bf16[768,128]{1,0:T(8,128)(2,1)S(1)}, bf16[768,128]{1,0:T(8,128)(2,1)S(1)}, u32[]{:S(2)}, u32[]{:S(2)}) collective-permute-start(bf16[768,128]{1,0:T(8,128)(2,1)S(1)} %first_project.3.mine_ref), channel_id=1, source_target_pairs={{0,4},{4,0},{1,5},{5,1},{2,6},{6,2},{3,7},{7,3},{8,12},{12,8},{9,1... | collective-permute-start | bytes 589832 | tf_op jit(solution)/shard_map/ppermute | solution.py:397
  24.0 8.6 %collective-permute-start.4 = (bf16[768,128]{1,0:T(8,128)(2,1)S(1)}, bf16[768,128]{1,0:T(8,128)(2,1)S(1)}, u32[]{:S(2)}, u32[]{:S(2)}) collective-permute-start(bf16[768,128]{1,0:T(8,128)(2,1)S(1)} %first_project.2.mine_ref), channel_id=1, source_target_pairs={{0,4},{4,0},{1,5},{5,1},{2,6},{6,2},{3,7},{7,3},{8,12},{12,8},{9,1... | collective-permute-start | bytes 589832 | tf_op jit(solution)/shard_map/ppermute | solution.py:397
  24.6 15.9 %slice-start = ((s8[4718592]{0:T(1024)(128)(4,1)}), s8[4194304]{0:T(1024)(128)(4,1)S(1)}, s32[]{:S(2)}) async-start(s8[4718592]{0:T(1024)(128)(4,1)} %bitcast.10), calls=%async_computation | async-start | bytes 8388608
  27.2 13.4 %slice-start.1 = ((s8[4718592]{0:T(1024)(128)(4,1)}), s8[524288]{0:T(1024)(128)(4,1)S(1)}, s32[]{:S(2)}) async-start(s8[4718592]{0:T(1024)(128)(4,1)} %bitcast.10), calls=%async_computation.1 | async-start | bytes 1048576
  30.4 3.8 %collective-permute-start.3 = (bf16[2,32,1536]{2,1,0:T(8,128)(2,1)S(1)}, bf16[2,32,1536]{2,1,0:T(8,128)(2,1)S(1)}, u32[]{:S(2)}, u32[]{:S(2)}) collective-permute-start(bf16[2,32,1536]{2,1,0:T(8,128)(2,1)S(1)} %get-tuple-element.49), channel_id=1, source_target_pairs={{0,1},{1,0},{2,3},{3,2},{4,5},{5,4},{6,7},{7,6},{8,9},{9,8},{10,11... | collective-permute-start | bytes 589832 | tf_op jit(solution)/shard_map/ppermute | solution.py:400
  34.2 2.8 %collective-permute-start.5 = (bf16[2,32,1536]{2,1,0:T(8,128)(2,1)S(1)}, bf16[2,32,1536]{2,1,0:T(8,128)(2,1)S(1)}, u32[]{:S(2)}, u32[]{:S(2)}) collective-permute-start(bf16[2,32,1536]{2,1,0:T(8,128)(2,1)S(1)} %get-tuple-element.54), channel_id=1, source_target_pairs={{0,1},{1,0},{2,3},{3,2},{4,5},{5,4},{6,7},{7,6},{8,9},{9,8},{10,11... | collective-permute-start | bytes 589832 | tf_op jit(solution)/shard_map/ppermute | solution.py:400
  34.9 6.8 %collective-permute-start.6 = (bf16[32,1536]{1,0:T(8,128)(2,1)S(1)}, bf16[32,1536]{1,0:T(8,128)(2,1)S(1)}, u32[]{:S(2)}, u32[]{:S(2)}) collective-permute-start(bf16[32,1536]{1,0:T(8,128)(2,1)S(1)} %get-tuple-element.50.refs_0_), channel_id=1, source_target_pairs={{0,8},{1,9},{2,10},{3,11},{8,0},{9,1},{10,2},{11,3},{16,24},{17,25... | collective-permute-start | bytes 294920 | tf_op jit(solution)/shard_map/ppermute | solution.py:419
  36.4 6.5 %collective-permute-start.7 = (bf16[32,1536]{1,0:T(8,128)(2,1)S(1)}, bf16[32,1536]{1,0:T(8,128)(2,1)S(1)}, u32[]{:S(2)}, u32[]{:S(2)}) collective-permute-start(bf16[32,1536]{1,0:T(8,128)(2,1)S(1)} %get-tuple-element.51.refs_1_), channel_id=1, source_target_pairs={{0,10},{1,11},{2,8},{3,9},{8,2},{9,3},{10,0},{11,1},{16,26},{17,27... | collective-permute-start | bytes 294920 | tf_op jit(solution)/shard_map/ppermute | solution.py:419
  37.6 11.2 %collective-permute-start.10 = (bf16[32,1536]{1,0:T(8,128)(2,1)S(1)}, bf16[32,1536]{1,0:T(8,128)(2,1)S(1)}, u32[]{:S(2)}, u32[]{:S(2)}) collective-permute-start(bf16[32,1536]{1,0:T(8,128)(2,1)S(1)} %get-tuple-element.56.refs_1_), channel_id=1, source_target_pairs={{0,10},{1,11},{2,8},{3,9},{8,2},{9,3},{10,0},{11,1},{16,26},{17,27... | collective-permute-start | bytes 294920 | tf_op jit(solution)/shard_map/ppermute | solution.py:419
  40.0 8.8 %collective-permute-start.9 = (bf16[32,1536]{1,0:T(8,128)(2,1)S(1)}, bf16[32,1536]{1,0:T(8,128)(2,1)S(1)}, u32[]{:S(2)}, u32[]{:S(2)}) collective-permute-start(bf16[32,1536]{1,0:T(8,128)(2,1)S(1)} %get-tuple-element.55.refs_0_), channel_id=1, source_target_pairs={{0,8},{1,9},{2,10},{3,11},{8,0},{9,1},{10,2},{11,3},{16,24},{17,25... | collective-permute-start | bytes 294920 | tf_op jit(solution)/shard_map/ppermute | solution.py:419
  48.8 6.5 %collective-permute-start.8 = (bf16[64,1536]{1,0:T(8,128)(2,1)S(1)}, bf16[64,1536]{1,0:T(8,128)(2,1)S(1)}, u32[]{:S(2)}, u32[]{:S(2)}) collective-permute-start(bf16[64,1536]{1,0:T(8,128)(2,1)S(1)} %all_gather.10.mine_ref), channel_id=1, source_target_pairs={{0,1},{1,0},{2,3},{3,2},{4,5},{5,4},{6,7},{7,6},{8,9},{9,8},{10,11... | collective-permute-start | bytes 589832 | tf_op jit(solution)/shard_map/ppermute | solution.py:400
  55.3 2.9 %collective-permute-start.11 = (bf16[64,1536]{1,0:T(8,128)(2,1)S(1)}, bf16[64,1536]{1,0:T(8,128)(2,1)S(1)}, u32[]{:S(2)}, u32[]{:S(2)}) collective-permute-start(bf16[64,1536]{1,0:T(8,128)(2,1)S(1)} %all_gather.11.mine_ref), channel_id=1, source_target_pairs={{0,1},{1,0},{2,3},{3,2},{4,5},{5,4},{6,7},{7,6},{8,9},{9,8},{10,11... | collective-permute-start | bytes 589832 | tf_op jit(solution)/shard_map/ppermute | solution.py:400
  56.6 7.8 %collective-permute-start.15 = (bf16[768,128]{1,0:T(8,128)(2,1)S(1)}, bf16[768,128]{1,0:T(8,128)(2,1)S(1)}, u32[]{:S(2)}, u32[]{:S(2)}) collective-permute-start(bf16[768,128]{1,0:T(8,128)(2,1)S(1)} %get-tuple-element.60.mine_ref), channel_id=1, source_target_pairs={{0,4},{4,0},{1,5},{5,1},{2,6},{6,2},{3,7},{7,3},{8,12},{12,8},{9,1... | collective-permute-start | bytes 589832 | tf_op jit(solution)/shard_map/ppermute | solution.py:397
  59.7 8.6 %collective-permute-start.12 = (bf16[768,128]{1,0:T(8,128)(2,1)S(1)}, bf16[768,128]{1,0:T(8,128)(2,1)S(1)}, u32[]{:S(2)}, u32[]{:S(2)}) collective-permute-start(bf16[768,128]{1,0:T(8,128)(2,1)S(1)} %get-tuple-element.62.mine_ref), channel_id=1, source_target_pairs={{0,4},{4,0},{1,5},{5,1},{2,6},{6,2},{3,7},{7,3},{8,12},{12,8},{9,1... | collective-permute-start | bytes 589832 | tf_op jit(solution)/shard_map/ppermute | solution.py:397
  65.9 3.8 %collective-permute-start.16 = (bf16[2,32,1536]{2,1,0:T(8,128)(2,1)S(1)}, bf16[2,32,1536]{2,1,0:T(8,128)(2,1)S(1)}, u32[]{:S(2)}, u32[]{:S(2)}) collective-permute-start(bf16[2,32,1536]{2,1,0:T(8,128)(2,1)S(1)} %get-tuple-element.68), channel_id=1, source_target_pairs={{0,1},{1,0},{2,3},{3,2},{4,5},{5,4},{6,7},{7,6},{8,9},{9,8},{10,11... | collective-permute-start | bytes 589832 | tf_op jit(solution)/shard_map/ppermute | solution.py:400
  69.6 3.4 %collective-permute-start.13 = (bf16[2,32,1536]{2,1,0:T(8,128)(2,1)S(1)}, bf16[2,32,1536]{2,1,0:T(8,128)(2,1)S(1)}, u32[]{:S(2)}, u32[]{:S(2)}) collective-permute-start(bf16[2,32,1536]{2,1,0:T(8,128)(2,1)S(1)} %get-tuple-element.64), channel_id=1, source_target_pairs={{0,1},{1,0},{2,3},{3,2},{4,5},{5,4},{6,7},{7,6},{8,9},{9,8},{10,11... | collective-permute-start | bytes 589832 | tf_op jit(solution)/shard_map/ppermute | solution.py:400
  70.3 8.3 %collective-permute-start.17 = (bf16[32,1536]{1,0:T(8,128)(2,1)S(1)}, bf16[32,1536]{1,0:T(8,128)(2,1)S(1)}, u32[]{:S(2)}, u32[]{:S(2)}) collective-permute-start(bf16[32,1536]{1,0:T(8,128)(2,1)S(1)} %get-tuple-element.69), channel_id=1, source_target_pairs={{0,4},{1,5},{2,6},{3,7},{4,0},{5,1},{6,2},{7,3},{8,12},{9,13},{10,... | collective-permute-start | bytes 294920 | tf_op jit(solution)/shard_map/ppermute | solution.py:411
  71.9 6.8 %collective-permute-start.18 = (bf16[32,1536]{1,0:T(8,128)(2,1)S(1)}, bf16[32,1536]{1,0:T(8,128)(2,1)S(1)}, u32[]{:S(2)}, u32[]{:S(2)}) collective-permute-start(bf16[32,1536]{1,0:T(8,128)(2,1)S(1)} %get-tuple-element.70), channel_id=1, source_target_pairs={{0,6},{1,7},{2,4},{3,5},{4,2},{5,3},{6,0},{7,1},{8,14},{9,15},{10,... | collective-permute-start | bytes 294920 | tf_op jit(solution)/shard_map/ppermute | solution.py:411
  73.7 6.6 %collective-permute-start.14 = (bf16[32,1536]{1,0:T(8,128)(2,1)S(1)}, bf16[32,1536]{1,0:T(8,128)(2,1)S(1)}, u32[]{:S(2)}, u32[]{:S(2)}) collective-permute-start(bf16[32,1536]{1,0:T(8,128)(2,1)S(1)} %get-tuple-element.66), channel_id=1, source_target_pairs={{0,2},{2,0},{1,3},{3,1},{4,6},{6,4},{5,7},{7,5},{8,10},{10,8},{9,1... | collective-permute-start | bytes 294920 | tf_op jit(solution)/shard_map/ppermute | solution.py:403

commit v9 on v8

--- a/solution.py
+++ b/solution.py
@@ -69,18 +69,22 @@
     )(facts, note, table, tokens)
 
 
-def project_kernel(
-    index, outer, facts_ref, note_ref, value_ref, out_ref, mine_ref, theirs_ref, partial_ref, full_ref
-):
+def project_kernel(index, outer, facts_ref, note_ref, value_ref, out_ref, *refs):
+    piece_refs, (partial_ref, full_ref) = refs[:-2], refs[-2:]
     version = picked_version(index, facts_ref, note_ref)
     first_core = facts_ref[CORE] == 0
-    shard = mine_ref.shape[0] // outer
+    shard = piece_refs[0].shape[0]
+    mine = [ref[...] for ref in piece_refs[:outer]]
+    theirs = [ref[...] for ref in piece_refs[outer:]]
     for place in range(outer):
-        mine = mine_ref[place * shard : (place + 1) * shard, :]
-        theirs = theirs_ref[place * shard : (place + 1) * shard, :]
+        offset = facts_ref[ROW] ^ place
+        own, other = mine[0], theirs[0]
+        for delta in range(1, outer):
+            own = jnp.where(offset == delta, mine[delta], own)
+            other = jnp.where(offset == delta, theirs[delta], other)
         start = 2 * place * shard
-        full_ref[start : start + shard, :] = jnp.where(first_core, mine, theirs)
-        full_ref[start + shard : start + 2 * shard, :] = jnp.where(first_core, theirs, mine)
+        full_ref[start : start + shard, :] = jnp.where(first_core, own, other)
+        full_ref[start + shard : start + 2 * shard, :] = jnp.where(first_core, other, own)
     flipped = full_ref[...].T
 
     def rows_of(table_ref):
@@ -90,21 +94,22 @@
     pl.when(facts_ref[ODD] == 0)(lambda: rows_of(out_ref))
 
 
-def project(index, outer, facts, note, tables, mine, theirs):
-    rows = tables[0].shape[2]
-    tokens, width = 2 * mine.shape[0], mine.shape[1]
+def project(index, facts, note, tables, mine, theirs):
+    outer = len(mine)
+    rows, width = tables[0].shape[2:]
+    tokens = 2 * outer * mine[0].shape[0]
     return pl.pallas_call(
         functools.partial(project_kernel, index, outer),
         out_shape=(
             jax.ShapeDtypeStruct((rows, tokens), jnp.bfloat16),
             jax.ShapeDtypeStruct((tokens, width), jnp.bfloat16),
         ),
-        in_specs=[in_smem()] + [in_vmem()] * 5,
+        in_specs=[in_smem()] + [in_vmem()] * (3 + 2 * outer),
         out_specs=(in_vmem(), in_vmem()),
         compiler_params=pltpu.CompilerParams(vmem_limit_bytes=VMEM_BYTES),
         cost_estimate=SMALL,
         name="project",
-    )(facts, note, *tables, mine, theirs)
+    )(facts, note, *tables, *mine, *theirs)
 
 
 def mix_kernel(
@@ -463,9 +468,10 @@
         received = [swap_section(part, d) for d, part in enumerate(first_sent[m])]
         second_piece[m] = arrive(m, facts, sources[m], received)
     for m in range(2):
-        mine = lax.all_gather(second_piece[m], "outer", axis=0, tiled=True)
+        mine = [second_piece[m]] + [to_row(second_piece[m], d) for d in range(1, outer)]
+        theirs = [swap_core(piece) for piece in mine]
         partial[m], second_full[m] = project(
-            m, outer, facts, other_note, (value_table, out_table), mine, swap_core(mine)
+            m, facts, other_note, (value_table, out_table), mine, theirs
         )
     arrived = [swap_half(partial[1]), swap_half(partial[0])]
     second_result, last_sent = [None, None], [None, None]
@@ -473,6 +479,8 @@
         second_result[m], keep, send = mix(
             EVEN, m, facts, other_note, messages[m], value_table, partial[m], arrived[m], outer
         )
+        if m == 0:
+            keep, _ = lax.optimization_barrier((keep, last_sent[1]))
         last_sent[m] = combine(None, facts, keep, swap_core(send), second_piece[m], first_sent[m])
     other_parts = [to_other_half(part, d) for d, part in enumerate(last_sent[1])]
     own_parts = [last_sent[0][0]] + [to_row(part, d + 1) for d, part in enumerate(last_sent[0][1:])]

time: 81.8 us -> 78.6 us (0.961)
  blocking collectives: 20.3 us -> 9.14 us
  waiting for transfers between devices: 13.2 us -> 17.9 us
  starting transfers between devices: 16.4 us -> 19.7 us
    all_gather x2 -> x0, blocking collectives: 11.2 us -> none  [on_device(): mine = lax.all_gather(second_piece[m], 'outer', axis=0, tiled=True)]
    ppermute x1 -> x3, waiting for transfers between devices: 1.59 us -> 4.44 us  [to_row(): return lax.ppermute(array, 'outer', [(i, i ^ delta) for i in range(outer)])]
    ppermute x1 -> x3, starting transfers between devices: 0.91 us -> 3.42 us  [to_row(): return lax.ppermute(array, 'outer', [(i, i ^ delta) for i in range(outer)])]
    ppermute x4, waiting for transfers between devices: 1.28 us -> 3.05 us  [swap_section(): return lax.ppermute(array, ('pair', 'outer', 'core'), pairs)]
  transfers between devices with their start and end apart: 19 -> 23, of which waited for: 6 -> 9; matrix products, arithmetic and copies ran while one was open for 3% -> 3% of each run, Pallas kernels for 31% -> 33%
where the time goes in v9:
time: 78.6 us; the launch traced here: 78.4 us
  Pallas kernels  26.9 us (34%)
  starting transfers between devices  19.7 us (25%)
  waiting for transfers between devices  17.9 us (23%)
  blocking collectives  9.14 us (12%)
  other arithmetic  3.01 us (4%)
  between operations  1.56 us (2%)
    ppermute x6, waiting for transfers between devices, swap_half(): return lax.ppermute(array, 'half', [(0, 1), (1, 0)])  10.3 us
    all_gather x1, blocking collectives, gathered(): return lax.all_gather(pair, ('outer', 'core'), axis=1, tiled=True)  9.14 us
    ppermute x6, starting transfers between devices, swap_half(): return lax.ppermute(array, 'half', [(0, 1), (1, 0)])  7.39 us
    pallas_call x4, Pallas kernels, mix(): pl.pallas_call(functools.partial(mix_kernel, outer, natural, index), out_...  5.87 us
    ppermute x4, starting transfers between devices, swap_section(): return lax.ppermute(array, ('pair', 'outer', 'core'), pairs)  5.08 us
    ppermute x3, waiting for transfers between devices, to_row(): return lax.ppermute(array, 'outer', [(i, i ^ delta) for i in range(outer)])  4.44 us
    pallas_call x1, Pallas kernels, weight_grads(): pl.pallas_call(weight_grad_kernel, grid=(CHUNKS,), out_shape=(grad, grad)...  4.06 us
    pallas_call x2, Pallas kernels, load_table(): pl.pallas_call(load_kernel, out_shape=jax.ShapeDtypeStruct(table.shape, j...  3.57 us
  transfers between devices with their start and end apart: 23, of which 9 were waited for; matrix products, arithmetic and copies ran while one was open for 3% of the time, Pallas kernels for 33%

profile of v9, /device:TPU:0, one launch (start us, length us, event | category | flops | bytes accessed | tf_op | source)
XLA Modules:
  0.0 78.4 jit_solution(15769423701697960966)
XLA Ops:
  2.3 3.0 %collective-permute-start = (bf16[48,1536]{1,0:T(8,128)(2,1)S(1)}, bf16[48,1536]{1,0:T(8,128)(2,1)S(1)}, u32[]{:S(2)}, u32[]{:S(2)}) collective-permute-start(bf16[48,1536]{1,0:T(8,128)(2,1)S(1)} %concatenate.6), channel_id=1, source_target_pairs={{0,4},{4,0},{1,5},{5,1},{2,6},{6,2},{3,7},{7,3},{8,12},{12,8},{9,1... | collective-permute-start | bytes 442376 | tf_op jit(solution)/shard_map/ppermute | solution.py:402
  6.4 1.1 %pad_maximum_fusion.stash_ref = bf16[2,768,128]{2,1,0:T(8,128)(2,1)S(1)} fusion(bf16[1,768,128]{2,1,0:T(8,128)(2,1)} %param.9, bf16[1,768,128]{2,1,0:T(8,128)(2,1)} %param.8), kind=kLoop, calls=%fused_computation | loop fusion | flops 196608 | bytes 786432 | tf_op jit(solution)/shard_map/concatenate | solution.py:442
  7.4 3.0 %pack.1 = (bf16[1408,128]{1,0:T(8,128)(2,1)S(1)}, bf16[32,1536]{1,0:T(8,128)(2,1)S(1)}, bf16[1,2,768,1536]{3,2,1,0:T(8,128)(2,1)S(1)}) custom-call(s32[6]{0:T(128)S(1)} %stack.34.facts_ref, bf16[2,768,128]{2,1,0:T(8,128)(2,1)S(1)} %pad_maximum_fusion.stash_ref, bf16[2,32,3072]{2,1,0:T(8,128)(2,1)S(1)} %pad_maximum_fusion.1.input_ref, ...), custom_call_target="tpu_custom_call" | custom-call | flops 1 | bytes 1 | tf_op jit(solution)/shard_map/pack/pallas_call | solution.py:318
  10.6 9.1 %all_gather.3.tokens_ref.first = bf16[2,128,1536]{2,1,0:T(8,128)(2,1)S(1)} all-gather(bf16[2,32,1536]{2,1,0:T(8,128)(2,1)S(1)} %pad_maximum_fusion.2.addend_ref), channel_id=1, replica_groups=mesh['pair'=4,'half'=2,'outer'=2,'core'=2] {'outer','core'}, dimensions={1}, use_global_device_ids=true | all-gather | bytes 983040 | tf_op jit(solution)/shard_map/all_gather | solution.py:433
  19.8 1.4 %first_project.3.mine_ref = bf16[768,128]{1,0:T(8,128)(2,1)S(1)} custom-call(s32[6]{0:T(128)S(1)} %stack.34.facts_ref, bf16[16,1536]{1,0:T(8,128)(2,1)S(1)} %slice.8.note_ref, bf16[1,2,768,1536]{3,2,1,0:T(8,128)(2,1)S(1)} %get-tuple-element.45.table_ref, bf16[2,128,1536]{2,1,0:T(8,128)(2,1)S(1)} %all_gather.3.tokens_ref.first), custom_call_target="tpu_custom_call" | custom-call | flops 1 | bytes 1 | tf_op jit(solution)/shard_map/first_project/pallas_call | solution.py:61
  21.2 1.6 %collective-permute-start.2 = (bf16[768,128]{1,0:T(8,128)(2,1)S(1)}, bf16[768,128]{1,0:T(8,128)(2,1)S(1)}, u32[]{:S(2)}, u32[]{:S(2)}) collective-permute-start(bf16[768,128]{1,0:T(8,128)(2,1)S(1)} %first_project.3.mine_ref), channel_id=1, source_target_pairs={{0,4},{4,0},{1,5},{5,1},{2,6},{6,2},{3,7},{7,3},{8,12},{12,8},{9,1... | collective-permute-start | bytes 589832 | tf_op jit(solution)/shard_map/ppermute | solution.py:402
  22.7 1.3 %first_project.2.mine_ref = bf16[768,128]{1,0:T(8,128)(2,1)S(1)} custom-call(s32[6]{0:T(128)S(1)} %stack.34.facts_ref, bf16[16,1536]{1,0:T(8,128)(2,1)S(1)} %slice.8.note_ref, bf16[1,2,768,1536]{3,2,1,0:T(8,128)(2,1)S(1)} %get-tuple-element.45.table_ref, bf16[2,128,1536]{2,1,0:T(8,128)(2,1)S(1)} %all_gather.3.tokens_ref.first), custom_call_target="tpu_custom_call" | custom-call | flops 1 | bytes 1 | tf_op jit(solution)/shard_map/first_project/pallas_call | solution.py:61
  24.6 2.5 %load_table.2.value_ref = bf16[1,2,768,1536]{3,2,1,0:T(8,128)(2,1)S(1)} custom-call(bf16[1,2,768,1536]{3,2,1,0:T(8,128)(2,1)} %source_ref), custom_call_target="tpu_custom_call" | custom-call | flops 1 | bytes 1 | tf_op jit(solution)/shard_map/load_table/pallas_call | solution.py:343
  27.2 1.8 %collective-permute-done.2.arrived_ref = bf16[768,128]{1,0:T(8,128)(2,1)S(1)} collective-permute-done((bf16[768,128]{1,0:T(8,128)(2,1)S(1)}, bf16[768,128]{1,0:T(8,128)(2,1)S(1)}, u32[]{:S(2)}, u32[]{:S(2)}) %collective-permute-start.2) | collective-permute-done | bytes 196640 | tf_op jit(solution)/shard_map/ppermute | solution.py:402
  28.9 1.5 %mix.4 = (bf16[768,128]{1,0:T(8,128)(2,1)S(1)}, bf16[2,32,1536]{2,1,0:T(8,128)(2,1)S(1)}, bf16[2,32,1536]{2,1,0:T(8,128)(2,1)S(1)}) custom-call(s32[6]{0:T(128)S(1)} %stack.34.facts_ref, bf16[16,1536]{1,0:T(8,128)(2,1)S(1)} %slice.8.note_ref, bf16[1,2,768,1536]{3,2,1,0:T(8,128)(2,1)S(1)} %load_table.2.value_ref, bf16[768,128]{1,0:T(8,128)(2,1)S(1)} %first_project.2.mine_ref, ...), custom_call_target="tpu_custom_call" | custom-call | flops 1 | bytes 1 | tf_op jit(solution)/shard_map/mix/pallas_call | solution.py:161
  30.5 2.1 %collective-permute-done.4.arrived_ref = bf16[768,128]{1,0:T(8,128)(2,1)S(1)} collective-permute-done((bf16[768,128]{1,0:T(8,128)(2,1)S(1)}, bf16[768,128]{1,0:T(8,128)(2,1)S(1)}, u32[]{:S(2)}, u32[]{:S(2)}) %collective-permute-start.4) | collective-permute-done | bytes 196640 | tf_op jit(solution)/shard_map/ppermute | solution.py:402
  32.6 1.6 %mix.5 = (bf16[768,128]{1,0:T(8,128)(2,1)S(1)}, bf16[2,32,1536]{2,1,0:T(8,128)(2,1)S(1)}, bf16[2,32,1536]{2,1,0:T(8,128)(2,1)S(1)}) custom-call(s32[6]{0:T(128)S(1)} %stack.34.facts_ref, bf16[16,1536]{1,0:T(8,128)(2,1)S(1)} %slice.8.note_ref, bf16[1,2,768,1536]{3,2,1,0:T(8,128)(2,1)S(1)} %load_table.2.value_ref, bf16[768,128]{1,0:T(8,128)(2,1)S(1)} %first_project.3.mine_ref, ...), custom_call_target="tpu_custom_call" | custom-call | flops 1 | bytes 1 | tf_op jit(solution)/shard_map/mix/pallas_call | solution.py:161
  34.9 1.5 %collective-permute-start.6 = (bf16[32,1536]{1,0:T(8,128)(2,1)S(1)}, bf16[32,1536]{1,0:T(8,128)(2,1)S(1)}, u32[]{:S(2)}, u32[]{:S(2)}) collective-permute-start(bf16[32,1536]{1,0:T(8,128)(2,1)S(1)} %get-tuple-element.51.refs_0_), channel_id=1, source_target_pairs={{0,8},{1,9},{2,10},{3,11},{8,0},{9,1},{10,2},{11,3},{16,24},{17,25... | collective-permute-start | bytes 294920 | tf_op jit(solution)/shard_map/ppermute | solution.py:424
  37.6 1.5 %collective-permute-start.11 = (bf16[32,1536]{1,0:T(8,128)(2,1)S(1)}, bf16[32,1536]{1,0:T(8,128)(2,1)S(1)}, u32[]{:S(2)}, u32[]{:S(2)}) collective-permute-start(bf16[32,1536]{1,0:T(8,128)(2,1)S(1)} %get-tuple-element.56.refs_0_), channel_id=1, source_target_pairs={{0,8},{1,9},{2,10},{3,11},{8,0},{9,1},{10,2},{11,3},{16,24},{17,25... | collective-permute-start | bytes 294920 | tf_op jit(solution)/shard_map/ppermute | solution.py:424
  39.1 1.5 %collective-permute-start.12 = (bf16[32,1536]{1,0:T(8,128)(2,1)S(1)}, bf16[32,1536]{1,0:T(8,128)(2,1)S(1)}, u32[]{:S(2)}, u32[]{:S(2)}) collective-permute-start(bf16[32,1536]{1,0:T(8,128)(2,1)S(1)} %get-tuple-element.57.refs_1_), channel_id=1, source_target_pairs={{0,10},{1,11},{2,8},{3,9},{8,2},{9,3},{10,0},{11,1},{16,26},{17,27... | collective-permute-start | bytes 294920 | tf_op jit(solution)/shard_map/ppermute | solution.py:424
  41.6 1.3 %collective-permute-done.7.refs_1_ = bf16[32,1536]{1,0:T(8,128)(2,1)S(1)} collective-permute-done((bf16[32,1536]{1,0:T(8,128)(2,1)S(1)}, bf16[32,1536]{1,0:T(8,128)(2,1)S(1)}, u32[]{:S(2)}, u32[]{:S(2)}) %collective-permute-start.7) | collective-permute-done | bytes 98336 | tf_op jit(solution)/shard_map/ppermute | solution.py:424
  43.5 1.3 %collective-permute-start.8 = (bf16[32,1536]{1,0:T(8,128)(2,1)S(1)}, bf16[32,1536]{1,0:T(8,128)(2,1)S(1)}, u32[]{:S(2)}, u32[]{:S(2)}) collective-permute-start(bf16[32,1536]{1,0:T(8,128)(2,1)S(1)} %arrive.2.refs_0_.addend_ref), channel_id=1, source_target_pairs={{0,2},{2,0},{1,3},{3,1},{4,6},{6,4},{5,7},{7,5},{8,10},{10,8},{9,1... | collective-permute-start | bytes 294920 | tf_op jit(solution)/shard_map/ppermute | solution.py:408
  44.8 1.8 %collective-permute-done.12.refs_1_ = bf16[32,1536]{1,0:T(8,128)(2,1)S(1)} collective-permute-done((bf16[32,1536]{1,0:T(8,128)(2,1)S(1)}, bf16[32,1536]{1,0:T(8,128)(2,1)S(1)}, u32[]{:S(2)}, u32[]{:S(2)}) %collective-permute-start.12) | collective-permute-done | bytes 98336 | tf_op jit(solution)/shard_map/ppermute | solution.py:424
  47.1 1.6 %collective-permute-start.13 = (bf16[32,1536]{1,0:T(8,128)(2,1)S(1)}, bf16[32,1536]{1,0:T(8,128)(2,1)S(1)}, u32[]{:S(2)}, u32[]{:S(2)}) collective-permute-start(bf16[32,1536]{1,0:T(8,128)(2,1)S(1)} %arrive.3.refs_0_.addend_ref), channel_id=1, source_target_pairs={{0,2},{2,0},{1,3},{3,1},{4,6},{6,4},{5,7},{7,5},{8,10},{10,8},{9,1... | collective-permute-start | bytes 294920 | tf_op jit(solution)/shard_map/ppermute | solution.py:408
  49.2 2.6 %collective-permute-done.13.refs_1_ = bf16[32,1536]{1,0:T(8,128)(2,1)S(1)} collective-permute-done((bf16[32,1536]{1,0:T(8,128)(2,1)S(1)}, bf16[32,1536]{1,0:T(8,128)(2,1)S(1)}, u32[]{:S(2)}, u32[]{:S(2)}) %collective-permute-start.13) | collective-permute-done | bytes 98336 | tf_op jit(solution)/shard_map/ppermute | solution.py:408
  51.8 1.4 %project.2 = (bf16[768,128]{1,0:T(8,128)(2,1)S(1)}, bf16[128,1536]{1,0:T(8,128)(2,1)S(1)}) custom-call(s32[6]{0:T(128)S(1)} %stack.34.facts_ref, bf16[16,1536]{1,0:T(8,128)(2,1)S(1)} %slice.8.note_ref, bf16[1,2,768,1536]{3,2,1,0:T(8,128)(2,1)S(1)} %load_table.2.value_ref, bf16[1,2,768,1536]{3,2,1,0:T(8,128)(2,1)S(1)} %load_table.3.out_ref, ...), custom_call_target="tpu_custom_call" | custom-call | flops 1 | bytes 1 | tf_op jit(solution)/shard_map/project/pallas_call | solution.py:101
  53.2 1.6 %collective-permute-start.17 = (bf16[768,128]{1,0:T(8,128)(2,1)S(1)}, bf16[768,128]{1,0:T(8,128)(2,1)S(1)}, u32[]{:S(2)}, u32[]{:S(2)}) collective-permute-start(bf16[768,128]{1,0:T(8,128)(2,1)S(1)} %get-tuple-element.61.mine_ref), channel_id=1, source_target_pairs={{0,4},{4,0},{1,5},{5,1},{2,6},{6,2},{3,7},{7,3},{8,12},{12,8},{9,1... | collective-permute-start | bytes 589832 | tf_op jit(solution)/shard_map/ppermute | solution.py:402
  54.8 1.4 %project.3 = (bf16[768,128]{1,0:T(8,128)(2,1)S(1)}, bf16[128,1536]{1,0:T(8,128)(2,1)S(1)}) custom-call(s32[6]{0:T(128)S(1)} %stack.34.facts_ref, bf16[16,1536]{1,0:T(8,128)(2,1)S(1)} %slice.8.note_ref, bf16[1,2,768,1536]{3,2,1,0:T(8,128)(2,1)S(1)} %load_table.2.value_ref, bf16[1,2,768,1536]{3,2,1,0:T(8,128)(2,1)S(1)} %load_table.3.out_ref, ...), custom_call_target="tpu_custom_call" | custom-call | flops 1 | bytes 1 | tf_op jit(solution)/shard_map/project/pallas_call | solution.py:101
  56.8 4.2 %collective-permute-done.17.arrived_ref = bf16[768,128]{1,0:T(8,128)(2,1)S(1)} collective-permute-done((bf16[768,128]{1,0:T(8,128)(2,1)S(1)}, bf16[768,128]{1,0:T(8,128)(2,1)S(1)}, u32[]{:S(2)}, u32[]{:S(2)}) %collective-permute-start.17) | collective-permute-done | bytes 196640 | tf_op jit(solution)/shard_map/ppermute | solution.py:402
  61.0 1.4 %mix.7 = (bf16[768,128]{1,0:T(8,128)(2,1)S(1)}, bf16[2,32,1536]{2,1,0:T(8,128)(2,1)S(1)}, bf16[2,32,1536]{2,1,0:T(8,128)(2,1)S(1)}) custom-call(s32[6]{0:T(128)S(1)} %stack.34.facts_ref, bf16[16,1536]{1,0:T(8,128)(2,1)S(1)} %slice.8.note_ref, bf16[1,2,768,1536]{3,2,1,0:T(8,128)(2,1)S(1)} %load_table.2.value_ref, ...), custom_call_target="tpu_custom_call" | custom-call | flops 1 | bytes 1 | tf_op jit(solution)/shard_map/mix/pallas_call | solution.py:161
  62.5 2.3 %collective-permute-done.16.arrived_ref = bf16[768,128]{1,0:T(8,128)(2,1)S(1)} collective-permute-done((bf16[768,128]{1,0:T(8,128)(2,1)S(1)}, bf16[768,128]{1,0:T(8,128)(2,1)S(1)}, u32[]{:S(2)}, u32[]{:S(2)}) %collective-permute-start.16) | collective-permute-done | bytes 196640 | tf_op jit(solution)/shard_map/ppermute | solution.py:402
  64.8 1.4 %mix.6 = (bf16[768,128]{1,0:T(8,128)(2,1)S(1)}, bf16[2,32,1536]{2,1,0:T(8,128)(2,1)S(1)}, bf16[2,32,1536]{2,1,0:T(8,128)(2,1)S(1)}) custom-call(s32[6]{0:T(128)S(1)} %stack.34.facts_ref, bf16[16,1536]{1,0:T(8,128)(2,1)S(1)} %slice.8.note_ref, bf16[1,2,768,1536]{3,2,1,0:T(8,128)(2,1)S(1)} %load_table.2.value_ref, ...), custom_call_target="tpu_custom_call" | custom-call | flops 1 | bytes 1 | tf_op jit(solution)/shard_map/mix/pallas_call | solution.py:161
  66.9 1.6 %collective-permute-start.21 = (bf16[32,1536]{1,0:T(8,128)(2,1)S(1)}, bf16[32,1536]{1,0:T(8,128)(2,1)S(1)}, u32[]{:S(2)}, u32[]{:S(2)}) collective-permute-start(bf16[32,1536]{1,0:T(8,128)(2,1)S(1)} %get-tuple-element.67), channel_id=1, source_target_pairs={{0,4},{1,5},{2,6},{3,7},{4,0},{5,1},{6,2},{7,3},{8,12},{9,13},{10,... | collective-permute-start | bytes 294920 | tf_op jit(solution)/shard_map/ppermute | solution.py:416
  68.5 1.5 %collective-permute-start.22 = (bf16[32,1536]{1,0:T(8,128)(2,1)S(1)}, bf16[32,1536]{1,0:T(8,128)(2,1)S(1)}, u32[]{:S(2)}, u32[]{:S(2)}) collective-permute-start(bf16[32,1536]{1,0:T(8,128)(2,1)S(1)} %get-tuple-element.68), channel_id=1, source_target_pairs={{0,6},{1,7},{2,4},{3,5},{4,2},{5,3},{6,0},{7,1},{8,14},{9,15},{10,... | collective-permute-start | bytes 294920 | tf_op jit(solution)/shard_map/ppermute | solution.py:416
  71.1 4.1 %weight_grads.1 = (bf16[1,768,1536]{2,1,0:T(8,128)(2,1)}, bf16[1,768,1536]{2,1,0:T(8,128)(2,1)}) custom-call(s32[6]{0:T(128)S(1)} %stack.34.facts_ref, bf16[768,128]{1,0:T(8,128)(2,1)S(1)} %get-tuple-element.73.a0, bf16[768,128]{1,0:T(8,128)(2,1)S(1)} %get-tuple-element.74.a1, bf16[768,128]{1,0:T(8,128)(2,1)S(1)} %get-tuple-element.77.b0, ...), custom_call_target="tpu_custom_call" | custom-call | flops 1 | bytes 1 | tf_op jit(solution)/shard_map/weight_grads/pallas_call | solution.py:251
  75.3 1.8 %collective-permute-done.20.refs_1_ = bf16[32,1536]{1,0:T(8,128)(2,1)S(1)} collective-permute-done((bf16[32,1536]{1,0:T(8,128)(2,1)S(1)}, bf16[32,1536]{1,0:T(8,128)(2,1)S(1)}, u32[]{:S(2)}, u32[]{:S(2)}) %collective-permute-start.20) | collective-permute-done | bytes 98336 | tf_op jit(solution)/shard_map/ppermute | solution.py:408
  77.1 1.3 %assemble.1 = bf16[1,32,3072]{2,1,0:T(8,128)(2,1)} custom-call(s32[6]{0:T(128)S(1)} %stack.34.facts_ref, bf16[32,1536]{1,0:T(8,128)(2,1)S(1)} %get-tuple-element.82.refs_0_, bf16[32,1536]{1,0:T(8,128)(2,1)S(1)} %collective-permute-done.20.refs_1_, bf16[32,1536]{1,0:T(8,128)(2,1)S(1)} %collective-permute-done.21.refs_2_, ...), custom_call_target="tpu_custom_call" | custom-call | tf_op jit(solution)/shard_map/assemble/pallas_call | solution.py:219
  (48 shorter events, 10.1 us)
Async XLA Ops:
  2.3 8.2 %collective-permute-start = (bf16[48,1536]{1,0:T(8,128)(2,1)S(1)}, bf16[48,1536]{1,0:T(8,128)(2,1)S(1)}, u32[]{:S(2)}, u32[]{:S(2)}) collective-permute-start(bf16[48,1536]{1,0:T(8,128)(2,1)S(1)} %concatenate.6), channel_id=1, source_target_pairs={{0,4},{4,0},{1,5},{5,1},{2,6},{6,2},{3,7},{7,3},{8,12},{12,8},{9,1... | collective-permute-start | bytes 442376 | tf_op jit(solution)/shard_map/ppermute | solution.py:402
  10.5 12.3 %collective-permute-start.1 = (bf16[1408,128]{1,0:T(8,128)(2,1)S(1)}, bf16[1408,128]{1,0:T(8,128)(2,1)S(1)}, u32[]{:S(2)}, u32[]{:S(2)}) collective-permute-start(bf16[1408,128]{1,0:T(8,128)(2,1)S(1)} %get-tuple-element.46.probs_ref), channel_id=1, source_target_pairs={{0,4},{4,0},{1,5},{5,1},{2,6},{6,2},{3,7},{7,3},{8,12},{12,8},{9,1... | collective-permute-start | bytes 1081352 | tf_op jit(solution)/shard_map/ppermute | solution.py:402
  21.2 7.8 %collective-permute-start.2 = (bf16[768,128]{1,0:T(8,128)(2,1)S(1)}, bf16[768,128]{1,0:T(8,128)(2,1)S(1)}, u32[]{:S(2)}, u32[]{:S(2)}) collective-permute-start(bf16[768,128]{1,0:T(8,128)(2,1)S(1)} %first_project.3.mine_ref), channel_id=1, source_target_pairs={{0,4},{4,0},{1,5},{5,1},{2,6},{6,2},{3,7},{7,3},{8,12},{12,8},{9,1... | collective-permute-start | bytes 589832 | tf_op jit(solution)/shard_map/ppermute | solution.py:402
  24.0 8.6 %collective-permute-start.4 = (bf16[768,128]{1,0:T(8,128)(2,1)S(1)}, bf16[768,128]{1,0:T(8,128)(2,1)S(1)}, u32[]{:S(2)}, u32[]{:S(2)}) collective-permute-start(bf16[768,128]{1,0:T(8,128)(2,1)S(1)} %first_project.2.mine_ref), channel_id=1, source_target_pairs={{0,4},{4,0},{1,5},{5,1},{2,6},{6,2},{3,7},{7,3},{8,12},{12,8},{9,1... | collective-permute-start | bytes 589832 | tf_op jit(solution)/shard_map/ppermute | solution.py:402
  24.6 15.9 %slice-start = ((s8[4718592]{0:T(1024)(128)(4,1)}), s8[4194304]{0:T(1024)(128)(4,1)S(1)}, s32[]{:S(2)}) async-start(s8[4718592]{0:T(1024)(128)(4,1)} %bitcast.10), calls=%async_computation | async-start | bytes 8388608
  27.2 13.4 %slice-start.1 = ((s8[4718592]{0:T(1024)(128)(4,1)}), s8[524288]{0:T(1024)(128)(4,1)S(1)}, s32[]{:S(2)}) async-start(s8[4718592]{0:T(1024)(128)(4,1)} %bitcast.10), calls=%async_computation.1 | async-start | bytes 1048576
  30.4 3.8 %collective-permute-start.3 = (bf16[2,32,1536]{2,1,0:T(8,128)(2,1)S(1)}, bf16[2,32,1536]{2,1,0:T(8,128)(2,1)S(1)}, u32[]{:S(2)}, u32[]{:S(2)}) collective-permute-start(bf16[2,32,1536]{2,1,0:T(8,128)(2,1)S(1)} %get-tuple-element.50), channel_id=1, source_target_pairs={{0,1},{1,0},{2,3},{3,2},{4,5},{5,4},{6,7},{7,6},{8,9},{9,8},{10,11... | collective-permute-start | bytes 589832 | tf_op jit(solution)/shard_map/ppermute | solution.py:405
  34.2 2.8 %collective-permute-start.5 = (bf16[2,32,1536]{2,1,0:T(8,128)(2,1)S(1)}, bf16[2,32,1536]{2,1,0:T(8,128)(2,1)S(1)}, u32[]{:S(2)}, u32[]{:S(2)}) collective-permute-start(bf16[2,32,1536]{2,1,0:T(8,128)(2,1)S(1)} %get-tuple-element.55), channel_id=1, source_target_pairs={{0,1},{1,0},{2,3},{3,2},{4,5},{5,4},{6,7},{7,6},{8,9},{9,8},{10,11... | collective-permute-start | bytes 589832 | tf_op jit(solution)/shard_map/ppermute | solution.py:405
  34.9 6.8 %collective-permute-start.6 = (bf16[32,1536]{1,0:T(8,128)(2,1)S(1)}, bf16[32,1536]{1,0:T(8,128)(2,1)S(1)}, u32[]{:S(2)}, u32[]{:S(2)}) collective-permute-start(bf16[32,1536]{1,0:T(8,128)(2,1)S(1)} %get-tuple-element.51.refs_0_), channel_id=1, source_target_pairs={{0,8},{1,9},{2,10},{3,11},{8,0},{9,1},{10,2},{11,3},{16,24},{17,25... | collective-permute-start | bytes 294920 | tf_op jit(solution)/shard_map/ppermute | solution.py:424
  36.4 6.5 %collective-permute-start.7 = (bf16[32,1536]{1,0:T(8,128)(2,1)S(1)}, bf16[32,1536]{1,0:T(8,128)(2,1)S(1)}, u32[]{:S(2)}, u32[]{:S(2)}) collective-permute-start(bf16[32,1536]{1,0:T(8,128)(2,1)S(1)} %get-tuple-element.52.refs_1_), channel_id=1, source_target_pairs={{0,10},{1,11},{2,8},{3,9},{8,2},{9,3},{10,0},{11,1},{16,26},{17,27... | collective-permute-start | bytes 294920 | tf_op jit(solution)/shard_map/ppermute | solution.py:424
  37.6 7.2 %collective-permute-start.11 = (bf16[32,1536]{1,0:T(8,128)(2,1)S(1)}, bf16[32,1536]{1,0:T(8,128)(2,1)S(1)}, u32[]{:S(2)}, u32[]{:S(2)}) collective-permute-start(bf16[32,1536]{1,0:T(8,128)(2,1)S(1)} %get-tuple-element.56.refs_0_), channel_id=1, source_target_pairs={{0,8},{1,9},{2,10},{3,11},{8,0},{9,1},{10,2},{11,3},{16,24},{17,25... | collective-permute-start | bytes 294920 | tf_op jit(solution)/shard_map/ppermute | solution.py:424
  39.1 7.5 %collective-permute-start.12 = (bf16[32,1536]{1,0:T(8,128)(2,1)S(1)}, bf16[32,1536]{1,0:T(8,128)(2,1)S(1)}, u32[]{:S(2)}, u32[]{:S(2)}) collective-permute-start(bf16[32,1536]{1,0:T(8,128)(2,1)S(1)} %get-tuple-element.57.refs_1_), channel_id=1, source_target_pairs={{0,10},{1,11},{2,8},{3,9},{8,2},{9,3},{10,0},{11,1},{16,26},{17,27... | collective-permute-start | bytes 294920 | tf_op jit(solution)/shard_map/ppermute | solution.py:424
  43.5 5.2 %collective-permute-start.8 = (bf16[32,1536]{1,0:T(8,128)(2,1)S(1)}, bf16[32,1536]{1,0:T(8,128)(2,1)S(1)}, u32[]{:S(2)}, u32[]{:S(2)}) collective-permute-start(bf16[32,1536]{1,0:T(8,128)(2,1)S(1)} %arrive.2.refs_0_.addend_ref), channel_id=1, source_target_pairs={{0,2},{2,0},{1,3},{3,1},{4,6},{6,4},{5,7},{7,5},{8,10},{10,8},{9,1... | collective-permute-start | bytes 294920 | tf_op jit(solution)/shard_map/ppermute | solution.py:408
  47.1 4.7 %collective-permute-start.13 = (bf16[32,1536]{1,0:T(8,128)(2,1)S(1)}, bf16[32,1536]{1,0:T(8,128)(2,1)S(1)}, u32[]{:S(2)}, u32[]{:S(2)}) collective-permute-start(bf16[32,1536]{1,0:T(8,128)(2,1)S(1)} %arrive.3.refs_0_.addend_ref), channel_id=1, source_target_pairs={{0,2},{2,0},{1,3},{3,1},{4,6},{6,4},{5,7},{7,5},{8,10},{10,8},{9,1... | collective-permute-start | bytes 294920 | tf_op jit(solution)/shard_map/ppermute | solution.py:408
  48.7 3.1 %collective-permute-start.9 = (bf16[32,1536]{1,0:T(8,128)(2,1)S(1)}, bf16[32,1536]{1,0:T(8,128)(2,1)S(1)}, u32[]{:S(2)}, u32[]{:S(2)}) collective-permute-start(bf16[32,1536]{1,0:T(8,128)(2,1)S(1)} %arrive.2.refs_0_.addend_ref), channel_id=1, source_target_pairs={{0,1},{1,0},{2,3},{3,2},{4,5},{5,4},{6,7},{7,6},{8,9},{9,8},{10,11... | collective-permute-start | bytes 294920 | tf_op jit(solution)/shard_map/ppermute | solution.py:405
  48.7 3.1 %collective-permute-start.10 = (bf16[32,1536]{1,0:T(8,128)(2,1)S(1)}, bf16[32,1536]{1,0:T(8,128)(2,1)S(1)}, u32[]{:S(2)}, u32[]{:S(2)}) collective-permute-start(bf16[32,1536]{1,0:T(8,128)(2,1)S(1)} %collective-permute-done.8.refs_1_), channel_id=1, source_target_pairs={{0,1},{1,0},{2,3},{3,2},{4,5},{5,4},{6,7},{7,6},{8,9},{9,8},{10,11... | collective-permute-start | bytes 294920 | tf_op jit(solution)/shard_map/ppermute | solution.py:405
  49.2 5.6 %collective-permute-start.14 = (bf16[32,1536]{1,0:T(8,128)(2,1)S(1)}, bf16[32,1536]{1,0:T(8,128)(2,1)S(1)}, u32[]{:S(2)}, u32[]{:S(2)}) collective-permute-start(bf16[32,1536]{1,0:T(8,128)(2,1)S(1)} %arrive.3.refs_0_.addend_ref), channel_id=1, source_target_pairs={{0,1},{1,0},{2,3},{3,2},{4,5},{5,4},{6,7},{7,6},{8,9},{9,8},{10,11... | collective-permute-start | bytes 294920 | tf_op jit(solution)/shard_map/ppermute | solution.py:405
  51.8 3.0 %collective-permute-start.15 = (bf16[32,1536]{1,0:T(8,128)(2,1)S(1)}, bf16[32,1536]{1,0:T(8,128)(2,1)S(1)}, u32[]{:S(2)}, u32[]{:S(2)}) collective-permute-start(bf16[32,1536]{1,0:T(8,128)(2,1)S(1)} %collective-permute-done.13.refs_1_), channel_id=1, source_target_pairs={{0,1},{1,0},{2,3},{3,2},{4,5},{5,4},{6,7},{7,6},{8,9},{9,8},{10,11... | collective-permute-start | bytes 294920 | tf_op jit(solution)/shard_map/ppermute | solution.py:405
  53.2 7.8 %collective-permute-start.17 = (bf16[768,128]{1,0:T(8,128)(2,1)S(1)}, bf16[768,128]{1,0:T(8,128)(2,1)S(1)}, u32[]{:S(2)}, u32[]{:S(2)}) collective-permute-start(bf16[768,128]{1,0:T(8,128)(2,1)S(1)} %get-tuple-element.61.mine_ref), channel_id=1, source_target_pairs={{0,4},{4,0},{1,5},{5,1},{2,6},{6,2},{3,7},{7,3},{8,12},{12,8},{9,1... | collective-permute-start | bytes 589832 | tf_op jit(solution)/shard_map/ppermute | solution.py:402
  56.2 8.6 %collective-permute-start.16 = (bf16[768,128]{1,0:T(8,128)(2,1)S(1)}, bf16[768,128]{1,0:T(8,128)(2,1)S(1)}, u32[]{:S(2)}, u32[]{:S(2)}) collective-permute-start(bf16[768,128]{1,0:T(8,128)(2,1)S(1)} %get-tuple-element.63.mine_ref), channel_id=1, source_target_pairs={{0,4},{4,0},{1,5},{5,1},{2,6},{6,2},{3,7},{7,3},{8,12},{12,8},{9,1... | collective-permute-start | bytes 589832 | tf_op jit(solution)/shard_map/ppermute | solution.py:402
  62.4 3.8 %collective-permute-start.18 = (bf16[2,32,1536]{2,1,0:T(8,128)(2,1)S(1)}, bf16[2,32,1536]{2,1,0:T(8,128)(2,1)S(1)}, u32[]{:S(2)}, u32[]{:S(2)}) collective-permute-start(bf16[2,32,1536]{2,1,0:T(8,128)(2,1)S(1)} %get-tuple-element.66), channel_id=1, source_target_pairs={{0,1},{1,0},{2,3},{3,2},{4,5},{5,4},{6,7},{7,6},{8,9},{9,8},{10,11... | collective-permute-start | bytes 589832 | tf_op jit(solution)/shard_map/ppermute | solution.py:405
  66.2 3.7 %collective-permute-start.19 = (bf16[2,32,1536]{2,1,0:T(8,128)(2,1)S(1)}, bf16[2,32,1536]{2,1,0:T(8,128)(2,1)S(1)}, u32[]{:S(2)}, u32[]{:S(2)}) collective-permute-start(bf16[2,32,1536]{2,1,0:T(8,128)(2,1)S(1)} %get-tuple-element.70), channel_id=1, source_target_pairs={{0,1},{1,0},{2,3},{3,2},{4,5},{5,4},{6,7},{7,6},{8,9},{9,8},{10,11... | collective-permute-start | bytes 589832 | tf_op jit(solution)/shard_map/ppermute | solution.py:405
  66.9 8.3 %collective-permute-start.21 = (bf16[32,1536]{1,0:T(8,128)(2,1)S(1)}, bf16[32,1536]{1,0:T(8,128)(2,1)S(1)}, u32[]{:S(2)}, u32[]{:S(2)}) collective-permute-start(bf16[32,1536]{1,0:T(8,128)(2,1)S(1)} %get-tuple-element.67), channel_id=1, source_target_pairs={{0,4},{1,5},{2,6},{3,7},{4,0},{5,1},{6,2},{7,3},{8,12},{9,13},{10,... | collective-permute-start | bytes 294920 | tf_op jit(solution)/shard_map/ppermute | solution.py:416
  68.5 6.8 %collective-permute-start.22 = (bf16[32,1536]{1,0:T(8,128)(2,1)S(1)}, bf16[32,1536]{1,0:T(8,128)(2,1)S(1)}, u32[]{:S(2)}, u32[]{:S(2)}) collective-permute-start(bf16[32,1536]{1,0:T(8,128)(2,1)S(1)} %get-tuple-element.68), channel_id=1, source_target_pairs={{0,6},{1,7},{2,4},{3,5},{4,2},{5,3},{6,0},{7,1},{8,14},{9,15},{10,... | collective-permute-start | bytes 294920 | tf_op jit(solution)/shard_map/ppermute | solution.py:416
  70.5 6.6 %collective-permute-start.20 = (bf16[32,1536]{1,0:T(8,128)(2,1)S(1)}, bf16[32,1536]{1,0:T(8,128)(2,1)S(1)}, u32[]{:S(2)}, u32[]{:S(2)}) collective-permute-start(bf16[32,1536]{1,0:T(8,128)(2,1)S(1)} %get-tuple-element.72), channel_id=1, source_target_pairs={{0,2},{2,0},{1,3},{3,1},{4,6},{6,4},{5,7},{7,5},{8,10},{10,8},{9,1... | collective-permute-start | bytes 294920 | tf_op jit(solution)/shard_map/ppermute | solution.py:408

commit v10 on v9

--- a/solution.py
+++ b/solution.py
@@ -47,35 +47,17 @@
 def picked_version(index, facts_ref, note_ref):
     if index == 0:
         return facts_ref[VERSION]
-    return (jnp.max(note_ref[...].astype(jnp.float32)) > 0.5).astype(jnp.int32)
-
-
-def first_project_kernel(index, facts_ref, note_ref, table_ref, tokens_ref, partial_ref):
-    version = picked_version(index, facts_ref, note_ref)
-    partial = matmul(table_ref[0, version], tokens_ref[index].T, NN)
-    partial_ref[...] = partial.astype(jnp.bfloat16)
-
-
-def first_project(index, facts, note, table, tokens):
-    rows = table.shape[2]
-    return pl.pallas_call(
-        functools.partial(first_project_kernel, index),
-        out_shape=jax.ShapeDtypeStruct((rows, tokens.shape[1]), jnp.bfloat16),
-        in_specs=[in_smem()] + [in_vmem()] * 3,
-        out_specs=in_vmem(),
-        compiler_params=pltpu.CompilerParams(vmem_limit_bytes=VMEM_BYTES),
-        cost_estimate=SMALL,
-        name="first_project",
-    )(facts, note, table, tokens)
-
-
-def project_kernel(index, outer, facts_ref, note_ref, value_ref, out_ref, *refs):
-    piece_refs, (partial_ref, full_ref) = refs[:-2], refs[-2:]
+    note = note_ref[note_ref.shape[0] - NOTE_ROWS :, :]
+    return (jnp.max(note.astype(jnp.float32)) > 0.5).astype(jnp.int32)
+
+
+def project_kernel(index, outer, shard, n_tables, facts_ref, note_ref, *refs):
+    table_refs, piece_refs = refs[:n_tables], refs[n_tables:-2]
+    partial_ref, full_ref = refs[-2:]
     version = picked_version(index, facts_ref, note_ref)
     first_core = facts_ref[CORE] == 0
-    shard = piece_refs[0].shape[0]
-    mine = [ref[...] for ref in piece_refs[:outer]]
-    theirs = [ref[...] for ref in piece_refs[outer:]]
+    mine = [ref[:shard, :] for ref in piece_refs[:outer]]
+    theirs = [ref[:shard, :] for ref in piece_refs[outer:]]
     for place in range(outer):
         offset = facts_ref[ROW] ^ place
         own, other = mine[0], theirs[0]
@@ -90,21 +72,24 @@
     def rows_of(table_ref):
         partial_ref[...] = matmul(table_ref[0, version], flipped, NN).astype(jnp.bfloat16)
 
-    pl.when(facts_ref[ODD] == 1)(lambda: rows_of(value_ref))
-    pl.when(facts_ref[ODD] == 0)(lambda: rows_of(out_ref))
-
-
-def project(index, facts, note, tables, mine, theirs):
+    if n_tables == 1:
+        rows_of(table_refs[0])
+    else:
+        pl.when(facts_ref[ODD] == 1)(lambda: rows_of(table_refs[0]))
+        pl.when(facts_ref[ODD] == 0)(lambda: rows_of(table_refs[1]))
+
+
+def project(index, shard, facts, note, tables, mine, theirs):
     outer = len(mine)
     rows, width = tables[0].shape[2:]
-    tokens = 2 * outer * mine[0].shape[0]
-    return pl.pallas_call(
-        functools.partial(project_kernel, index, outer),
+    tokens = 2 * outer * shard
+    return pl.pallas_call(
+        functools.partial(project_kernel, index, outer, shard, len(tables)),
         out_shape=(
             jax.ShapeDtypeStruct((rows, tokens), jnp.bfloat16),
             jax.ShapeDtypeStruct((tokens, width), jnp.bfloat16),
         ),
-        in_specs=[in_smem()] + [in_vmem()] * (3 + 2 * outer),
+        in_specs=[in_smem()] + [in_vmem()] * (1 + len(tables) + 2 * outer),
         out_specs=(in_vmem(), in_vmem()),
         compiler_params=pltpu.CompilerParams(vmem_limit_bytes=VMEM_BYTES),
         cost_estimate=SMALL,
@@ -169,25 +154,24 @@
     )(facts, note, w_value, mine, arrived, message)
 
 
-def combine_kernel(outer, last, index, facts_ref, keep_ref, arrived_ref, addend_ref, *refs):
+def combine_kernel(outer, last, facts_ref, keep_ref, arrived_ref, addend_ref, *refs):
     first_refs, sent_refs = refs[:-outer], refs[-outer:]
     for delta in range(outer):
         spot = facts_ref[ROW] ^ delta
         total = keep_ref[spot].astype(jnp.float32) + arrived_ref[spot].astype(jnp.float32)
         if delta == 0:
-            addend = addend_ref[...] if index is None else addend_ref[index]
-            total = total + addend.astype(jnp.float32)
+            total = total + addend_ref[: total.shape[0], :].astype(jnp.float32)
         total = total.astype(jnp.bfloat16)
         if last:
             total = jnp.where(facts_ref[ODD] == 1, first_refs[delta][...], total)
         sent_refs[delta][...] = total
 
 
-def combine(index, facts, keep, arrived, addend, first_sent=()):
+def combine(facts, keep, arrived, addend, first_sent=()):
     outer, shard, width = keep.shape
     piece = jax.ShapeDtypeStruct((shard, width), jnp.bfloat16)
     return pl.pallas_call(
-        functools.partial(combine_kernel, outer, len(first_sent) > 0, index),
+        functools.partial(combine_kernel, outer, len(first_sent) > 0),
         out_shape=(piece,) * outer,
         in_specs=[in_smem()] + [in_vmem()] * (3 + len(first_sent)),
         out_specs=(in_vmem(),) * outer,
@@ -226,13 +210,14 @@
     )(facts, *own_parts, *other_parts)
 
 
-def weight_grad_kernel(facts_ref, a0, a1, b0, b1, first, second0, second1, value_ref, out_ref):
+def weight_grad_kernel(
+    facts_ref, a0, a1, b0, b1, first0, first1, second0, second1, value_ref, out_ref
+):
     odd = facts_ref[ODD] == 1
-    tokens = a0.shape[1]
     left_first = jnp.concatenate([a0[...], a1[...]], axis=1)
     left_second = jnp.concatenate([b0[...], b1[...]], axis=1)
     right_second = jnp.concatenate([second0[...], second1[...]], axis=0)
-    right_first = first[...].reshape(2 * tokens, first.shape[2])
+    right_first = jnp.concatenate([first0[...], first1[...]], axis=0)
     grad_first = matmul(left_first, right_second, NN)
     grad_second = matmul(left_second, right_first, NN)
     value_ref[0] = jnp.where(odd, grad_first, grad_second).astype(jnp.bfloat16)
@@ -241,23 +226,22 @@
 
 def weight_grads(facts, first_results, second_results, first_full, second_full):
     rows, tokens = first_results[0].shape
-    width = first_full.shape[2]
+    width = first_full[0].shape[1]
     step = rows // CHUNKS
     grad = jax.ShapeDtypeStruct((1, rows, width), jnp.bfloat16)
     left = pl.BlockSpec((step, tokens), lambda i: (i, 0))
-    both = pl.BlockSpec((2, tokens, width), lambda i: (0, 0, 0))
     single = pl.BlockSpec((tokens, width), lambda i: (0, 0))
     wide = pl.BlockSpec((1, step, width), lambda i: (0, i, 0))
     return pl.pallas_call(
         weight_grad_kernel,
         grid=(CHUNKS,),
         out_shape=(grad, grad),
-        in_specs=[in_smem()] + [left] * 4 + [both, single, single],
+        in_specs=[in_smem()] + [left] * 4 + [single] * 4,
         out_specs=(wide, wide),
         compiler_params=pltpu.CompilerParams(vmem_limit_bytes=GRAD_VMEM_BYTES),
         cost_estimate=SMALL,
         name="weight_grads",
-    )(facts, *first_results, *second_results, first_full, *second_full)
+    )(facts, *first_results, *second_results, *first_full, *second_full)
 
 
 def load(source_ref, table_ref, sems):
@@ -274,61 +258,31 @@
     return copies
 
 
-def pack_kernel(
-    facts_ref, stash_ref, input_ref, value_ref, out_ref, message_ref, own_ref, table_ref, sems
-):
-    @pl.when(facts_ref[ODD] == 1)
-    def _():
-        for copy in load(out_ref, table_ref, sems):
-            copy.start()
-
-    @pl.when(facts_ref[ODD] == 0)
-    def _():
-        for copy in load(value_ref, table_ref, sems):
-            copy.start()
-
+def probs_kernel(stash_ref, probs_ref):
     tokens = stash_ref.shape[2]
-    shard, width = own_ref.shape
-    heads = stash_ref.shape[1] // HEAD_DIM
     causal = lax.broadcasted_iota(jnp.int32, (tokens, tokens), 1) <= lax.broadcasted_iota(
         jnp.int32, (tokens, tokens), 0
     )
-    for head in range(heads):
+    for head in range(stash_ref.shape[1] // HEAD_DIM):
         rows = pl.ds(head * HEAD_DIM, HEAD_DIM)
         scores = matmul(stash_ref[0, rows, :], stash_ref[1, rows, :], TN)
         scores = jnp.where(causal, scores * (1.0 / math.sqrt(HEAD_DIM)), -jnp.inf)
         expo = jnp.exp(scores - jnp.max(scores, axis=1, keepdims=True))
         probs = (expo / jnp.sum(expo, axis=1, keepdims=True)).astype(jnp.bfloat16)
-        message_ref[head * tokens : (head + 1) * tokens, :] = probs
-    half = facts_ref[HALF]
-    own_ref[...] = input_ref[1, :, pl.ds(pl.multiple_of(half * width, width), width)]
-    other = input_ref[1, :, pl.ds(pl.multiple_of((1 - half) * width, width), width)]
-    for block in range(width // LANES):
-        start = heads * tokens + block * shard
-        message_ref[start : start + shard, :] = other[:, block * LANES : (block + 1) * LANES]
-    for copy in load(value_ref, table_ref, sems):
-        copy.wait()
-
-
-def pack(facts, stash, inputs, w_value, w_out):
+        probs_ref[head * tokens : (head + 1) * tokens, :] = probs
+
+
+def attention_probs(stash):
     rows, tokens = stash.shape[1:]
-    shard = inputs.shape[1]
-    width = inputs.shape[2] // 2
-    length = rows // HEAD_DIM * tokens + width // LANES * shard
-    return pl.pallas_call(
-        pack_kernel,
-        out_shape=(
-            jax.ShapeDtypeStruct((length, LANES), jnp.bfloat16),
-            jax.ShapeDtypeStruct((shard, width), jnp.bfloat16),
-            jax.ShapeDtypeStruct(w_value.shape, jnp.bfloat16),
-        ),
-        in_specs=[in_smem(), in_vmem(), in_vmem(), in_hbm(), in_hbm()],
-        out_specs=(in_vmem(), in_vmem(), in_vmem()),
-        scratch_shapes=[pltpu.SemaphoreType.DMA((2 * CHUNKS,))],
-        compiler_params=pltpu.CompilerParams(vmem_limit_bytes=FIRST_VMEM_BYTES),
-        cost_estimate=SMALL,
-        name="pack",
-    )(facts, stash, inputs, w_value, w_out)
+    return pl.pallas_call(
+        probs_kernel,
+        out_shape=jax.ShapeDtypeStruct((rows // HEAD_DIM * tokens, tokens), jnp.bfloat16),
+        in_specs=[in_vmem()],
+        out_specs=in_vmem(),
+        compiler_params=pltpu.CompilerParams(vmem_limit_bytes=VMEM_BYTES),
+        cost_estimate=SMALL,
+        name="probs",
+    )(stash)
 
 
 def load_kernel(source_ref, table_ref, sems):
@@ -339,6 +293,30 @@
         copy.wait()
 
 
+def load_first_kernel(facts_ref, value_ref, out_ref, table_ref, sems):
+    def start(source_ref):
+        for copy in load(source_ref, table_ref, sems):
+            copy.start()
+
+    pl.when(facts_ref[ODD] == 1)(lambda: start(out_ref))
+    pl.when(facts_ref[ODD] == 0)(lambda: start(value_ref))
+    for copy in load(value_ref, table_ref, sems):
+        copy.wait()
+
+
+def load_first(facts, w_value, w_out):
+    return pl.pallas_call(
+        load_first_kernel,
+        out_shape=jax.ShapeDtypeStruct(w_value.shape, jnp.bfloat16),
+        in_specs=[in_smem(), in_hbm(), in_hbm()],
+        out_specs=in_vmem(),
+        scratch_shapes=[pltpu.SemaphoreType.DMA((2 * CHUNKS,))],
+        compiler_params=pltpu.CompilerParams(vmem_limit_bytes=FIRST_VMEM_BYTES),
+        cost_estimate=SMALL,
+        name="load_first",
+    )(facts, w_value, w_out)
+
+
 def load_table(table, grant):
     return pl.pallas_call(
         load_kernel,
@@ -352,20 +330,12 @@
     )(table)
 
 
-def arrive_kernel(index, facts_ref, source_ref, *refs):
+def arrive_kernel(facts_ref, input_ref, *refs):
     parts, piece_ref = refs[:-1], refs[-1]
-    shard, width = piece_ref.shape
 
     @pl.when(facts_ref[ODD] == 1)
     def _():
-        if index == 0:
-            piece_ref[...] = source_ref[...]
-        else:
-            first_row = source_ref.shape[0] - width // LANES * shard
-            for block in range(width // LANES):
-                start = first_row + block * shard
-                columns = pl.ds(block * LANES, LANES)
-                piece_ref[:, columns] = source_ref[start : start + shard, :]
+        piece_ref[...] = input_ref[...]
 
     @pl.when(facts_ref[ODD] == 0)
     def _():
@@ -375,16 +345,16 @@
         piece_ref[...] = total.astype(jnp.bfloat16)
 
 
-def arrive(index, facts, source, parts):
-    return pl.pallas_call(
-        functools.partial(arrive_kernel, index),
+def arrive(facts, input_piece, parts):
+    return pl.pallas_call(
+        arrive_kernel,
         out_shape=jax.ShapeDtypeStruct(parts[0].shape, jnp.bfloat16),
         in_specs=[in_smem()] + [in_vmem()] * (1 + len(parts)),
         out_specs=in_vmem(),
         compiler_params=pltpu.CompilerParams(vmem_limit_bytes=VMEM_BYTES),
         cost_estimate=SMALL,
         name="arrive",
-    )(facts, source, *parts)
+    )(facts, input_piece, *parts)
 
 
 def on_device(section_input, query, key_stash, incoming, version, w_value, w_out):
@@ -429,27 +399,33 @@
     def other_columns(array):
         return lax.dynamic_slice_in_dim(array, (1 - half) * width, width, 1)
 
-    def gathered(pair):
-        return lax.all_gather(pair, ("outer", "core"), axis=1, tiled=True)
+    def spread_rows(piece):
+        return [piece] + [to_row(piece, delta) for delta in range(1, outer)]
 
     facts = jnp.stack([odd_flag, 1 - odd_flag, version[0], core, row, half])
-    inputs = jnp.stack([jnp.where(odd, incoming[0], section_input[0]), section_input[0]])
+    first = jnp.where(odd, incoming[0], section_input[0])
+    own_piece, sent_piece = own_columns(first), other_columns(first)
     note = jnp.full((NOTE_ROWS, width), version[0], jnp.int32).astype(jnp.bfloat16)
-    sent_piece = jnp.concatenate([other_columns(inputs[0]), note])
-    other_piece = swap_half(sent_piece)
-    other_note = other_piece[shard:]
-    first_pair = jnp.stack([own_columns(inputs[0]), other_piece[:shard]])
-    stash = jnp.concatenate([query, key_stash])
-    own_message, input_own, first_table = pack(facts, stash, inputs, w_value, w_out)
-    other_message = swap_half(own_message)
-    first_full = gathered(first_pair)
-    own_full, other_message = lax.optimization_barrier((first_full, other_message))
-    messages = [own_message, other_message]
-
-    partial = [None, None]
+    noted_piece = jnp.concatenate([sent_piece, note])
+    other_note = swap_half(noted_piece)
+    first_piece = [own_piece, other_note[:shard]]
+    first_mine = [spread_rows(piece) for piece in first_piece]
+    own_probs = attention_probs(jnp.concatenate([query, key_stash]))
+    late_value, late_out, _ = lax.optimization_barrier((w_value, w_out, own_probs))
+    first_table = load_first(facts, late_value, late_out)
+    other_probs = swap_half(own_probs)
+    swapped, _ = lax.optimization_barrier((first_mine, first_table))
+    first_theirs = [[swap_core(piece) for piece in pieces] for pieces in swapped]
+
+    probs = [own_probs, other_probs]
+    partial, first_full = [None, None], [None, None]
     for m in (1, 0):
-        tokens = first_full if m else own_full
-        partial[m] = first_project(m, facts, other_note, first_table, tokens)
+        mine = first_mine[m]
+        if m == 0:
+            mine, probs, _ = lax.optimization_barrier((mine, probs, partial[1]))
+        partial[m], first_full[m] = project(
+            m, shard, facts, other_note, (first_table,), mine, first_theirs[m]
+        )
     arrived = [swap_half(partial[1]), swap_half(partial[0])]
     later_value, _ = lax.optimization_barrier((w_value, partial))
     value_table = load_table(later_value, VALUE_VMEM_BYTES)
@@ -457,31 +433,31 @@
     second_piece, second_full = [None, None], [None, None]
     for m in range(2):
         first_result[m], keep, send = mix(
-            ODD, m, facts, other_note, messages[m], value_table, partial[m], arrived[m], outer
+            ODD, m, facts, other_note, probs[m], value_table, partial[m], arrived[m], outer
         )
-        first_sent[m] = combine(m, facts, keep, swap_core(send), first_pair)
+        first_sent[m] = combine(facts, keep, swap_core(send), first_piece[m])
     later_out, _ = lax.optimization_barrier((w_out, first_sent))
     out_table = load_table(later_out, OUT_VMEM_BYTES)
-    sources = [input_own, other_message]
-    sources, _ = lax.optimization_barrier((sources, out_table))
+    later_input, _ = lax.optimization_barrier((section_input[0], out_table))
+    input_piece = [own_columns(later_input), swap_half(other_columns(later_input))]
     for m in range(2):
         received = [swap_section(part, d) for d, part in enumerate(first_sent[m])]
-        second_piece[m] = arrive(m, facts, sources[m], received)
+        second_piece[m] = arrive(facts, input_piece[m], received)
     for m in range(2):
-        mine = [second_piece[m]] + [to_row(second_piece[m], d) for d in range(1, outer)]
+        mine = spread_rows(second_piece[m])
         theirs = [swap_core(piece) for piece in mine]
         partial[m], second_full[m] = project(
-            m, facts, other_note, (value_table, out_table), mine, theirs
+            m, shard, facts, other_note, (value_table, out_table), mine, theirs
         )
     arrived = [swap_half(partial[1]), swap_half(partial[0])]
     second_result, last_sent = [None, None], [None, None]
     for m in (1, 0):
         second_result[m], keep, send = mix(
-            EVEN, m, facts, other_note, messages[m], value_table, partial[m], arrived[m], outer
+            EVEN, m, facts, other_note, probs[m], value_table, partial[m], arrived[m], outer
         )
         if m == 0:
             keep, _ = lax.optimization_barrier((keep, last_sent[1]))
-        last_sent[m] = combine(None, facts, keep, swap_core(send), second_piece[m], first_sent[m])
+        last_sent[m] = combine(facts, keep, swap_core(send), second_piece[m], first_sent[m])
     other_parts = [to_other_half(part, d) for d, part in enumerate(last_sent[1])]
     own_parts = [last_sent[0][0]] + [to_row(part, d + 1) for d, part in enumerate(last_sent[0][1:])]
     second_result, _ = lax.optimization_barrier((second_result, last_sent))

time: 78.6 us -> 75.7 us (0.963)
  blocking collectives: 9.14 us -> 0 us
  starting transfers between devices: 19.7 us -> 25.9 us
  other arithmetic: 3.01 us -> 2.1 us
    all_gather x1 -> x0, blocking collectives: 9.14 us -> none  [gathered(): return lax.all_gather(pair, ('outer', 'core'), axis=1, tiled=True)]
    ppermute x3 -> x5, starting transfers between devices: 3.42 us -> 7.1 us  [to_row(): return lax.ppermute(array, 'outer', [(i, i ^ delta) for i in range(outer)])]
    ppermute x6 -> x7, starting transfers between devices: 7.39 us -> 9.78 us  [swap_half(): return lax.ppermute(array, 'half', [(0, 1), (1, 0)])]
    ppermute x4, waiting for transfers between devices: 3.05 us -> 1.87 us  [swap_section(): return lax.ppermute(array, ('pair', 'outer', 'core'), pairs)]
    ppermute x8 -> x12, starting transfers between devices: 0.8 us -> 1.82 us  [swap_core(): return lax.ppermute(array, 'core', [(0, 1), (1, 0)])]
    another operation x2 -> x0, other arithmetic: 0.99 us -> none  [the longest x1 0.96 us: on_device(): jnp.stack([jnp.where(odd, incoming[0], section_input[0]), section_input[0]])]
    ppermute x2, starting transfers between devices: 3.02 us -> 2.13 us  [to_other_half(): return lax.ppermute(array, ('half', 'outer', 'core'), pairs)]
    pallas_call x7 -> x8, Pallas kernels: 9.71 us -> 10.4 us  [the longest x4 5.56 us: project(): pl.pallas_call(functools.partial(project_kernel, index, outer, shard, len...]
  transfers between devices with their start and end apart: 23 -> 30, of which waited for: 9 -> 12; matrix products, arithmetic and copies ran while one was open for 3% -> 2% of each run, Pallas kernels for 33% -> 35%
where the time goes in v10:
time: 75.7 us; the launch traced here: 75.5 us
  Pallas kernels  27.6 us (36%)
  starting transfers between devices  25.9 us (34%)
  waiting for transfers between devices  18.1 us (24%)
  other arithmetic  2.1 us (3%)
  between operations  1.56 us (2%)
    ppermute x7, waiting for transfers between devices, swap_half(): return lax.ppermute(array, 'half', [(0, 1), (1, 0)])  10.8 us
    ppermute x7, starting transfers between devices, swap_half(): return lax.ppermute(array, 'half', [(0, 1), (1, 0)])  9.78 us
    ppermute x5, starting transfers between devices, to_row(): return lax.ppermute(array, 'outer', [(i, i ^ delta) for i in range(outer)])  7.1 us
    pallas_call x4, Pallas kernels, mix(): pl.pallas_call(functools.partial(mix_kernel, outer, natural, index), out_...  5.89 us
    pallas_call x4, Pallas kernels, project(): pl.pallas_call(functools.partial(project_kernel, index, outer, shard, len...  5.56 us
    ppermute x4, starting transfers between devices, swap_section(): return lax.ppermute(array, ('pair', 'outer', 'core'), pairs)  5.08 us
    ppermute x5, waiting for transfers between devices, to_row(): return lax.ppermute(array, 'outer', [(i, i ^ delta) for i in range(outer)])  4.97 us
    pallas_call x1, Pallas kernels, weight_grads(): pl.pallas_call(weight_grad_kernel, grid=(CHUNKS,), out_shape=(grad, grad)...  4.06 us
  transfers between devices with their start and end apart: 30, of which 12 were waited for; matrix products, arithmetic and copies ran while one was open for 2% of the time, Pallas kernels for 35%

profile of v10, /device:TPU:0, one launch (start us, length us, event | category | flops | bytes accessed | tf_op | source)
XLA Modules:
  0.0 75.5 jit_solution(18060140834788923708)
XLA Ops:
  2.4 3.0 %collective-permute-start = (bf16[48,1536]{1,0:T(8,128)(2,1)S(1)}, bf16[48,1536]{1,0:T(8,128)(2,1)S(1)}, u32[]{:S(2)}, u32[]{:S(2)}) collective-permute-start(bf16[48,1536]{1,0:T(8,128)(2,1)S(1)} %concatenate.6), channel_id=1, source_target_pairs={{0,4},{4,0},{1,5},{5,1},{2,6},{6,2},{3,7},{7,3},{8,12},{12,8},{9,1... | collective-permute-start | bytes 442376 | tf_op jit(solution)/shard_map/ppermute | solution.py:372
  5.4 1.1 %pad_maximum_fusion.stash_ref = bf16[2,768,128]{2,1,0:T(8,128)(2,1)S(1)} fusion(bf16[1,768,128]{2,1,0:T(8,128)(2,1)} %param.9, bf16[1,768,128]{2,1,0:T(8,128)(2,1)} %param.8), kind=kLoop, calls=%fused_computation | loop fusion | flops 196608 | bytes 786432 | tf_op jit(solution)/shard_map/concatenate | solution.py:413
  7.3 2.0 %collective-permute-start.1 = (bf16[32,1536]{1,0:T(8,128)(2,1)S(1)}, bf16[32,1536]{1,0:T(8,128)(2,1)S(1)}, u32[]{:S(2)}, u32[]{:S(2)}) collective-permute-start(bf16[32,1536]{1,0:T(8,128)(2,1)S(1)} %get-tuple-element.60.refs_1_.addend_ref), channel_id=1, source_target_pairs={{0,2},{2,0},{1,3},{3,1},{4,6},{6,4},{5,7},{7,5},{8,10},{10,8},{9,1... | collective-permute-start | bytes 294920 | tf_op jit(solution)/shard_map/ppermute | solution.py:378
  9.7 1.5 %collective-permute-start.3 = (bf16[32,1536]{1,0:T(8,128)(2,1)S(1)}, bf16[32,1536]{1,0:T(8,128)(2,1)S(1)}, u32[]{:S(2)}, u32[]{:S(2)}) collective-permute-start(bf16[32,1536]{1,0:T(8,128)(2,1)S(1)} %slice.4.refs_1_.addend_ref), channel_id=1, source_target_pairs={{0,2},{2,0},{1,3},{3,1},{4,6},{6,4},{5,7},{7,5},{8,10},{10,8},{9,1... | collective-permute-start | bytes 294920 | tf_op jit(solution)/shard_map/ppermute | solution.py:378
  11.2 2.9 %load_first.1.refs_0_ = bf16[1,2,768,1536]{3,2,1,0:T(8,128)(2,1)S(1)} custom-call(s32[6]{0:T(128)S(1)} %stack.23.facts_ref, bf16[1,2,768,1536]{3,2,1,0:T(8,128)(2,1)} %source_ref, bf16[1,2,768,1536]{3,2,1,0:T(8,128)(2,1)} %source_ref.1), custom_call_target="tpu_custom_call" | custom-call | flops 1 | bytes 1 | tf_op jit(solution)/shard_map/load_first/pallas_call | solution.py:308
  15.7 1.4 %project.4 = (bf16[768,128]{1,0:T(8,128)(2,1)S(1)}, bf16[128,1536]{1,0:T(8,128)(2,1)S(1)}) custom-call(s32[6]{0:T(128)S(1)} %stack.23.facts_ref, bf16[48,1536]{1,0:T(8,128)(2,1)S(1)} %collective-permute-done.note_ref, bf16[1,2,768,1536]{3,2,1,0:T(8,128)(2,1)S(1)} %load_first.1.refs_0_, bf16[32,1536]{1,0:T(8,128)(2,1)S(1)} %slice.4.refs_1_.addend_ref, ...), custom_call_target="tpu_custom_call" | custom-call | flops 1 | bytes 1 | tf_op jit(solution)/shard_map/project/pallas_call | solution.py:86
  17.1 2.6 %collective-permute-start.8 = (bf16[768,128]{1,0:T(8,128)(2,1)S(1)}, bf16[768,128]{1,0:T(8,128)(2,1)S(1)}, u32[]{:S(2)}, u32[]{:S(2)}) collective-permute-start(bf16[768,128]{1,0:T(8,128)(2,1)S(1)} %get-tuple-element.57.mine_ref), channel_id=1, source_target_pairs={{0,4},{4,0},{1,5},{5,1},{2,6},{6,2},{3,7},{7,3},{8,12},{12,8},{9,1... | collective-permute-start | bytes 589832 | tf_op jit(solution)/shard_map/ppermute | solution.py:372
  19.8 1.3 %project.5 = (bf16[768,128]{1,0:T(8,128)(2,1)S(1)}, bf16[128,1536]{1,0:T(8,128)(2,1)S(1)}) custom-call(s32[6]{0:T(128)S(1)} %stack.23.facts_ref, bf16[48,1536]{1,0:T(8,128)(2,1)S(1)} %collective-permute-done.note_ref, bf16[1,2,768,1536]{3,2,1,0:T(8,128)(2,1)S(1)} %load_first.1.refs_0_, bf16[32,1536]{1,0:T(8,128)(2,1)S(1)} %get-tuple-element.60.refs_1_.addend_ref, ...), custom_call_target="tpu_custom_call" | custom-call | flops 1 | bytes 1 | tf_op jit(solution)/shard_map/project/pallas_call | solution.py:86
  21.2 2.5 %load_table.2.value_ref.refs_0_ = bf16[1,2,768,1536]{3,2,1,0:T(8,128)(2,1)S(1)} custom-call(bf16[1,2,768,1536]{3,2,1,0:T(8,128)(2,1)} %source_ref), custom_call_target="tpu_custom_call" | custom-call | flops 1 | bytes 1 | tf_op jit(solution)/shard_map/load_table/pallas_call | solution.py:321
  23.8 1.7 %collective-permute-done.8.arrived_ref = bf16[768,128]{1,0:T(8,128)(2,1)S(1)} collective-permute-done((bf16[768,128]{1,0:T(8,128)(2,1)S(1)}, bf16[768,128]{1,0:T(8,128)(2,1)S(1)}, u32[]{:S(2)}, u32[]{:S(2)}) %collective-permute-start.8) | collective-permute-done | bytes 196640 | tf_op jit(solution)/shard_map/ppermute | solution.py:372
  25.5 1.5 %mix.4 = (bf16[768,128]{1,0:T(8,128)(2,1)S(1)}, bf16[2,32,1536]{2,1,0:T(8,128)(2,1)S(1)}, bf16[2,32,1536]{2,1,0:T(8,128)(2,1)S(1)}) custom-call(s32[6]{0:T(128)S(1)} %stack.23.facts_ref, bf16[48,1536]{1,0:T(8,128)(2,1)S(1)} %collective-permute-done.note_ref, bf16[1,2,768,1536]{3,2,1,0:T(8,128)(2,1)S(1)} %load_table.2.value_ref.refs_0_, ...), custom_call_target="tpu_custom_call" | custom-call | flops 1 | bytes 1 | tf_op jit(solution)/shard_map/mix/pallas_call | solution.py:146
  27.1 2.3 %collective-permute-done.10.arrived_ref = bf16[768,128]{1,0:T(8,128)(2,1)S(1)} collective-permute-done((bf16[768,128]{1,0:T(8,128)(2,1)S(1)}, bf16[768,128]{1,0:T(8,128)(2,1)S(1)}, u32[]{:S(2)}, u32[]{:S(2)}) %collective-permute-start.10) | collective-permute-done | bytes 196640 | tf_op jit(solution)/shard_map/ppermute | solution.py:372
  29.4 1.6 %mix.5 = (bf16[768,128]{1,0:T(8,128)(2,1)S(1)}, bf16[2,32,1536]{2,1,0:T(8,128)(2,1)S(1)}, bf16[2,32,1536]{2,1,0:T(8,128)(2,1)S(1)}) custom-call(s32[6]{0:T(128)S(1)} %stack.23.facts_ref, bf16[48,1536]{1,0:T(8,128)(2,1)S(1)} %collective-permute-done.note_ref, bf16[1,2,768,1536]{3,2,1,0:T(8,128)(2,1)S(1)} %load_table.2.value_ref.refs_0_, ...), custom_call_target="tpu_custom_call" | custom-call | flops 1 | bytes 1 | tf_op jit(solution)/shard_map/mix/pallas_call | solution.py:146
  31.7 1.4 %collective-permute-start.12 = (bf16[32,1536]{1,0:T(8,128)(2,1)S(1)}, bf16[32,1536]{1,0:T(8,128)(2,1)S(1)}, u32[]{:S(2)}, u32[]{:S(2)}) collective-permute-start(bf16[32,1536]{1,0:T(8,128)(2,1)S(1)} %get-tuple-element.67.refs_0_), channel_id=1, source_target_pairs={{0,8},{1,9},{2,10},{3,11},{8,0},{9,1},{10,2},{11,3},{16,24},{17,25... | collective-permute-start | bytes 294920 | tf_op jit(solution)/shard_map/ppermute | solution.py:394
  33.1 1.6 %collective-permute-start.13 = (bf16[32,1536]{1,0:T(8,128)(2,1)S(1)}, bf16[32,1536]{1,0:T(8,128)(2,1)S(1)}, u32[]{:S(2)}, u32[]{:S(2)}) collective-permute-start(bf16[32,1536]{1,0:T(8,128)(2,1)S(1)} %get-tuple-element.68.refs_1_), channel_id=1, source_target_pairs={{0,10},{1,11},{2,8},{3,9},{8,2},{9,3},{10,0},{11,1},{16,26},{17,27... | collective-permute-start | bytes 294920 | tf_op jit(solution)/shard_map/ppermute | solution.py:394
  35.2 1.5 %collective-permute-start.18 = (bf16[32,1536]{1,0:T(8,128)(2,1)S(1)}, bf16[32,1536]{1,0:T(8,128)(2,1)S(1)}, u32[]{:S(2)}, u32[]{:S(2)}) collective-permute-start(bf16[32,1536]{1,0:T(8,128)(2,1)S(1)} %get-tuple-element.72.refs_0_), channel_id=1, source_target_pairs={{0,8},{1,9},{2,10},{3,11},{8,0},{9,1},{10,2},{11,3},{16,24},{17,25... | collective-permute-start | bytes 294920 | tf_op jit(solution)/shard_map/ppermute | solution.py:394
  38.5 1.8 %collective-permute-start.17 = (bf16[32,1536]{1,0:T(8,128)(2,1)S(1)}, bf16[32,1536]{1,0:T(8,128)(2,1)S(1)}, u32[]{:S(2)}, u32[]{:S(2)}) collective-permute-start(bf16[32,1536]{1,0:T(8,128)(2,1)S(1)} %get-tuple-element.103), channel_id=1, source_target_pairs={{0,4},{4,0},{1,5},{5,1},{2,6},{6,2},{3,7},{7,3},{8,12},{12,8},{9,1... | collective-permute-start | bytes 294920 | tf_op jit(solution)/shard_map/ppermute | solution.py:372
  40.9 1.5 %collective-permute-start.14 = (bf16[32,1536]{1,0:T(8,128)(2,1)S(1)}, bf16[32,1536]{1,0:T(8,128)(2,1)S(1)}, u32[]{:S(2)}, u32[]{:S(2)}) collective-permute-start(bf16[32,1536]{1,0:T(8,128)(2,1)S(1)} %arrive.2.refs_2_.addend_ref), channel_id=1, source_target_pairs={{0,2},{2,0},{1,3},{3,1},{4,6},{6,4},{5,7},{7,5},{8,10},{10,8},{9,1... | collective-permute-start | bytes 294920 | tf_op jit(solution)/shard_map/ppermute | solution.py:378
  42.4 1.9 %collective-permute-done.19.refs_1_ = bf16[32,1536]{1,0:T(8,128)(2,1)S(1)} collective-permute-done((bf16[32,1536]{1,0:T(8,128)(2,1)S(1)}, bf16[32,1536]{1,0:T(8,128)(2,1)S(1)}, u32[]{:S(2)}, u32[]{:S(2)}) %collective-permute-start.19) | collective-permute-done | bytes 98336 | tf_op jit(solution)/shard_map/ppermute | solution.py:394
  46.7 2.8 %collective-permute-done.20.refs_3_ = bf16[32,1536]{1,0:T(8,128)(2,1)S(1)} collective-permute-done((bf16[32,1536]{1,0:T(8,128)(2,1)S(1)}, bf16[32,1536]{1,0:T(8,128)(2,1)S(1)}, u32[]{:S(2)}, u32[]{:S(2)}) %collective-permute-start.20) | collective-permute-done | bytes 98336 | tf_op jit(solution)/shard_map/ppermute | solution.py:378
  49.5 1.4 %project.6 = (bf16[768,128]{1,0:T(8,128)(2,1)S(1)}, bf16[128,1536]{1,0:T(8,128)(2,1)S(1)}) custom-call(s32[6]{0:T(128)S(1)} %stack.23.facts_ref, bf16[48,1536]{1,0:T(8,128)(2,1)S(1)} %collective-permute-done.note_ref, bf16[1,2,768,1536]{3,2,1,0:T(8,128)(2,1)S(1)} %load_table.2.value_ref.refs_0_, bf16[1,2,768,1536]{3,2,1,0:T(8,128)(2,1)S(1)} %load_table.3.refs_1_, ...), custom_call_target="tpu_custom_call" | custom-call | flops 1 | bytes 1 | tf_op jit(solution)/shard_map/project/pallas_call | solution.py:86
  50.9 1.8 %collective-permute-start.24 = (bf16[768,128]{1,0:T(8,128)(2,1)S(1)}, bf16[768,128]{1,0:T(8,128)(2,1)S(1)}, u32[]{:S(2)}, u32[]{:S(2)}) collective-permute-start(bf16[768,128]{1,0:T(8,128)(2,1)S(1)} %get-tuple-element.76.mine_ref), channel_id=1, source_target_pairs={{0,4},{4,0},{1,5},{5,1},{2,6},{6,2},{3,7},{7,3},{8,12},{12,8},{9,1... | collective-permute-start | bytes 589832 | tf_op jit(solution)/shard_map/ppermute | solution.py:372
  52.7 1.4 %project.7 = (bf16[768,128]{1,0:T(8,128)(2,1)S(1)}, bf16[128,1536]{1,0:T(8,128)(2,1)S(1)}) custom-call(s32[6]{0:T(128)S(1)} %stack.23.facts_ref, bf16[48,1536]{1,0:T(8,128)(2,1)S(1)} %collective-permute-done.note_ref, bf16[1,2,768,1536]{3,2,1,0:T(8,128)(2,1)S(1)} %load_table.2.value_ref.refs_0_, bf16[1,2,768,1536]{3,2,1,0:T(8,128)(2,1)S(1)} %load_table.3.refs_1_, ...), custom_call_target="tpu_custom_call" | custom-call | flops 1 | bytes 1 | tf_op jit(solution)/shard_map/project/pallas_call | solution.py:86
  54.5 4.1 %collective-permute-done.24.arrived_ref = bf16[768,128]{1,0:T(8,128)(2,1)S(1)} collective-permute-done((bf16[768,128]{1,0:T(8,128)(2,1)S(1)}, bf16[768,128]{1,0:T(8,128)(2,1)S(1)}, u32[]{:S(2)}, u32[]{:S(2)}) %collective-permute-start.24) | collective-permute-done | bytes 196640 | tf_op jit(solution)/shard_map/ppermute | solution.py:372
  58.7 1.5 %mix.7 = (bf16[768,128]{1,0:T(8,128)(2,1)S(1)}, bf16[2,32,1536]{2,1,0:T(8,128)(2,1)S(1)}, bf16[2,32,1536]{2,1,0:T(8,128)(2,1)S(1)}) custom-call(s32[6]{0:T(128)S(1)} %stack.23.facts_ref, bf16[48,1536]{1,0:T(8,128)(2,1)S(1)} %collective-permute-done.note_ref, bf16[1,2,768,1536]{3,2,1,0:T(8,128)(2,1)S(1)} %load_table.2.value_ref.refs_0_, ...), custom_call_target="tpu_custom_call" | custom-call | flops 1 | bytes 1 | tf_op jit(solution)/shard_map/mix/pallas_call | solution.py:146
  60.2 2.3 %collective-permute-done.23.arrived_ref = bf16[768,128]{1,0:T(8,128)(2,1)S(1)} collective-permute-done((bf16[768,128]{1,0:T(8,128)(2,1)S(1)}, bf16[768,128]{1,0:T(8,128)(2,1)S(1)}, u32[]{:S(2)}, u32[]{:S(2)}) %collective-permute-start.23) | collective-permute-done | bytes 196640 | tf_op jit(solution)/shard_map/ppermute | solution.py:372
  62.5 1.4 %mix.6 = (bf16[768,128]{1,0:T(8,128)(2,1)S(1)}, bf16[2,32,1536]{2,1,0:T(8,128)(2,1)S(1)}, bf16[2,32,1536]{2,1,0:T(8,128)(2,1)S(1)}) custom-call(s32[6]{0:T(128)S(1)} %stack.23.facts_ref, bf16[48,1536]{1,0:T(8,128)(2,1)S(1)} %collective-permute-done.note_ref, bf16[1,2,768,1536]{3,2,1,0:T(8,128)(2,1)S(1)} %load_table.2.value_ref.refs_0_, ...), custom_call_target="tpu_custom_call" | custom-call | flops 1 | bytes 1 | tf_op jit(solution)/shard_map/mix/pallas_call | solution.py:146
  64.6 1.8 %collective-permute-start.28 = (bf16[32,1536]{1,0:T(8,128)(2,1)S(1)}, bf16[32,1536]{1,0:T(8,128)(2,1)S(1)}, u32[]{:S(2)}, u32[]{:S(2)}) collective-permute-start(bf16[32,1536]{1,0:T(8,128)(2,1)S(1)} %get-tuple-element.81), channel_id=1, source_target_pairs={{0,4},{1,5},{2,6},{3,7},{4,0},{5,1},{6,2},{7,3},{8,12},{9,13},{10,... | collective-permute-start | bytes 294920 | tf_op jit(solution)/shard_map/ppermute | solution.py:386
  67.3 1.5 %collective-permute-start.27 = (bf16[32,1536]{1,0:T(8,128)(2,1)S(1)}, bf16[32,1536]{1,0:T(8,128)(2,1)S(1)}, u32[]{:S(2)}, u32[]{:S(2)}) collective-permute-start(bf16[32,1536]{1,0:T(8,128)(2,1)S(1)} %get-tuple-element.86), channel_id=1, source_target_pairs={{0,2},{2,0},{1,3},{3,1},{4,6},{6,4},{5,7},{7,5},{8,10},{10,8},{9,1... | collective-permute-start | bytes 294920 | tf_op jit(solution)/shard_map/ppermute | solution.py:378
  68.8 4.1 %weight_grads.1 = (bf16[1,768,1536]{2,1,0:T(8,128)(2,1)}, bf16[1,768,1536]{2,1,0:T(8,128)(2,1)}) custom-call(s32[6]{0:T(128)S(1)} %stack.23.facts_ref, bf16[768,128]{1,0:T(8,128)(2,1)S(1)} %get-tuple-element.87.a0, bf16[768,128]{1,0:T(8,128)(2,1)S(1)} %get-tuple-element.88.a1, bf16[768,128]{1,0:T(8,128)(2,1)S(1)} %get-tuple-element.91.b0, ...), custom_call_target="tpu_custom_call" | custom-call | flops 1 | bytes 1 | tf_op jit(solution)/shard_map/weight_grads/pallas_call | solution.py:235
  72.9 1.3 %collective-permute-done.27.refs_1_ = bf16[32,1536]{1,0:T(8,128)(2,1)S(1)} collective-permute-done((bf16[32,1536]{1,0:T(8,128)(2,1)S(1)}, bf16[32,1536]{1,0:T(8,128)(2,1)S(1)}, u32[]{:S(2)}, u32[]{:S(2)}) %collective-permute-start.27) | collective-permute-done | bytes 98336 | tf_op jit(solution)/shard_map/ppermute | solution.py:378
  74.2 1.3 %assemble.1 = bf16[1,32,3072]{2,1,0:T(8,128)(2,1)} custom-call(s32[6]{0:T(128)S(1)} %stack.23.facts_ref, bf16[32,1536]{1,0:T(8,128)(2,1)S(1)} %get-tuple-element.98.refs_0_, bf16[32,1536]{1,0:T(8,128)(2,1)S(1)} %collective-permute-done.27.refs_1_, bf16[32,1536]{1,0:T(8,128)(2,1)S(1)} %collective-permute-done.28.refs_2_, ...), custom_call_target="tpu_custom_call" | custom-call | tf_op jit(solution)/shard_map/assemble/pallas_call | solution.py:203
  (62 shorter events, 12.2 us)
Async XLA Ops:
  2.4 7.3 %collective-permute-start = (bf16[48,1536]{1,0:T(8,128)(2,1)S(1)}, bf16[48,1536]{1,0:T(8,128)(2,1)S(1)}, u32[]{:S(2)}, u32[]{:S(2)}) collective-permute-start(bf16[48,1536]{1,0:T(8,128)(2,1)S(1)} %concatenate.6), channel_id=1, source_target_pairs={{0,4},{4,0},{1,5},{5,1},{2,6},{6,2},{3,7},{7,3},{8,12},{12,8},{9,1... | collective-permute-start | bytes 442376 | tf_op jit(solution)/shard_map/ppermute | solution.py:372
  7.2 12.6 %collective-permute-start.2 = (bf16[1024,128]{1,0:T(8,128)(2,1)S(1)}, bf16[1024,128]{1,0:T(8,128)(2,1)S(1)}, u32[]{:S(2)}, u32[]{:S(2)}) collective-permute-start(bf16[1024,128]{1,0:T(8,128)(2,1)S(1)} %probs.1.probs_ref), channel_id=1, source_target_pairs={{0,4},{4,0},{1,5},{5,1},{2,6},{6,2},{3,7},{7,3},{8,12},{12,8},{9,1... | collective-permute-start | bytes 786440 | tf_op jit(solution)/shard_map/ppermute | solution.py:372
  7.3 6.9 %collective-permute-start.1 = (bf16[32,1536]{1,0:T(8,128)(2,1)S(1)}, bf16[32,1536]{1,0:T(8,128)(2,1)S(1)}, u32[]{:S(2)}, u32[]{:S(2)}) collective-permute-start(bf16[32,1536]{1,0:T(8,128)(2,1)S(1)} %get-tuple-element.60.refs_1_.addend_ref), channel_id=1, source_target_pairs={{0,2},{2,0},{1,3},{3,1},{4,6},{6,4},{5,7},{7,5},{8,10},{10,8},{9,1... | collective-permute-start | bytes 294920 | tf_op jit(solution)/shard_map/ppermute | solution.py:378
  9.7 4.6 %collective-permute-start.3 = (bf16[32,1536]{1,0:T(8,128)(2,1)S(1)}, bf16[32,1536]{1,0:T(8,128)(2,1)S(1)}, u32[]{:S(2)}, u32[]{:S(2)}) collective-permute-start(bf16[32,1536]{1,0:T(8,128)(2,1)S(1)} %slice.4.refs_1_.addend_ref), channel_id=1, source_target_pairs={{0,2},{2,0},{1,3},{3,1},{4,6},{6,4},{5,7},{7,5},{8,10},{10,8},{9,1... | collective-permute-start | bytes 294920 | tf_op jit(solution)/shard_map/ppermute | solution.py:378
  14.3 1.3 %collective-permute-start.4 = (bf16[32,1536]{1,0:T(8,128)(2,1)S(1)}, bf16[32,1536]{1,0:T(8,128)(2,1)S(1)}, u32[]{:S(2)}, u32[]{:S(2)}) collective-permute-start(bf16[32,1536]{1,0:T(8,128)(2,1)S(1)} %slice.4.refs_1_.addend_ref), channel_id=1, source_target_pairs={{0,1},{1,0},{2,3},{3,2},{4,5},{5,4},{6,7},{7,6},{8,9},{9,8},{10,11... | collective-permute-start | bytes 294920 | tf_op jit(solution)/shard_map/ppermute | solution.py:375
  14.3 1.5 %collective-permute-start.5 = (bf16[32,1536]{1,0:T(8,128)(2,1)S(1)}, bf16[32,1536]{1,0:T(8,128)(2,1)S(1)}, u32[]{:S(2)}, u32[]{:S(2)}) collective-permute-start(bf16[32,1536]{1,0:T(8,128)(2,1)S(1)} %collective-permute-done.3.refs_2_), channel_id=1, source_target_pairs={{0,1},{1,0},{2,3},{3,2},{4,5},{5,4},{6,7},{7,6},{8,9},{9,8},{10,11... | collective-permute-start | bytes 294920 | tf_op jit(solution)/shard_map/ppermute | solution.py:375
  14.8 5.0 %collective-permute-start.6 = (bf16[32,1536]{1,0:T(8,128)(2,1)S(1)}, bf16[32,1536]{1,0:T(8,128)(2,1)S(1)}, u32[]{:S(2)}, u32[]{:S(2)}) collective-permute-start(bf16[32,1536]{1,0:T(8,128)(2,1)S(1)} %get-tuple-element.60.refs_1_.addend_ref), channel_id=1, source_target_pairs={{0,1},{1,0},{2,3},{3,2},{4,5},{5,4},{6,7},{7,6},{8,9},{9,8},{10,11... | collective-permute-start | bytes 294920 | tf_op jit(solution)/shard_map/ppermute | solution.py:375
  14.8 5.0 %collective-permute-start.7 = (bf16[32,1536]{1,0:T(8,128)(2,1)S(1)}, bf16[32,1536]{1,0:T(8,128)(2,1)S(1)}, u32[]{:S(2)}, u32[]{:S(2)}) collective-permute-start(bf16[32,1536]{1,0:T(8,128)(2,1)S(1)} %collective-permute-done.1.refs_2_), channel_id=1, source_target_pairs={{0,1},{1,0},{2,3},{3,2},{4,5},{5,4},{6,7},{7,6},{8,9},{9,8},{10,11... | collective-permute-start | bytes 294920 | tf_op jit(solution)/shard_map/ppermute | solution.py:375
  17.1 8.4 %collective-permute-start.8 = (bf16[768,128]{1,0:T(8,128)(2,1)S(1)}, bf16[768,128]{1,0:T(8,128)(2,1)S(1)}, u32[]{:S(2)}, u32[]{:S(2)}) collective-permute-start(bf16[768,128]{1,0:T(8,128)(2,1)S(1)} %get-tuple-element.57.mine_ref), channel_id=1, source_target_pairs={{0,4},{4,0},{1,5},{5,1},{2,6},{6,2},{3,7},{7,3},{8,12},{12,8},{9,1... | collective-permute-start | bytes 589832 | tf_op jit(solution)/shard_map/ppermute | solution.py:372
  21.1 8.3 %collective-permute-start.10 = (bf16[768,128]{1,0:T(8,128)(2,1)S(1)}, bf16[768,128]{1,0:T(8,128)(2,1)S(1)}, u32[]{:S(2)}, u32[]{:S(2)}) collective-permute-start(bf16[768,128]{1,0:T(8,128)(2,1)S(1)} %get-tuple-element.62.mine_ref), channel_id=1, source_target_pairs={{0,4},{4,0},{1,5},{5,1},{2,6},{6,2},{3,7},{7,3},{8,12},{12,8},{9,1... | collective-permute-start | bytes 589832 | tf_op jit(solution)/shard_map/ppermute | solution.py:372
  21.2 16.2 %slice-start = ((s8[4718592]{0:T(1024)(128)(4,1)}), s8[4194304]{0:T(1024)(128)(4,1)S(1)}, s32[]{:S(2)}) async-start(s8[4718592]{0:T(1024)(128)(4,1)} %bitcast.10), calls=%async_computation | async-start | bytes 8388608
  23.8 13.6 %slice-start.1 = ((s8[4718592]{0:T(1024)(128)(4,1)}), s8[524288]{0:T(1024)(128)(4,1)S(1)}, s32[]{:S(2)}) async-start(s8[4718592]{0:T(1024)(128)(4,1)} %bitcast.10), calls=%async_computation.1 | async-start | bytes 1048576
  27.0 4.1 %collective-permute-start.9 = (bf16[2,32,1536]{2,1,0:T(8,128)(2,1)S(1)}, bf16[2,32,1536]{2,1,0:T(8,128)(2,1)S(1)}, u32[]{:S(2)}, u32[]{:S(2)}) collective-permute-start(bf16[2,32,1536]{2,1,0:T(8,128)(2,1)S(1)} %get-tuple-element.66), channel_id=1, source_target_pairs={{0,1},{1,0},{2,3},{3,2},{4,5},{5,4},{6,7},{7,6},{8,9},{9,8},{10,11... | collective-permute-start | bytes 589832 | tf_op jit(solution)/shard_map/ppermute | solution.py:375
  31.0 3.7 %collective-permute-start.11 = (bf16[2,32,1536]{2,1,0:T(8,128)(2,1)S(1)}, bf16[2,32,1536]{2,1,0:T(8,128)(2,1)S(1)}, u32[]{:S(2)}, u32[]{:S(2)}) collective-permute-start(bf16[2,32,1536]{2,1,0:T(8,128)(2,1)S(1)} %get-tuple-element.71), channel_id=1, source_target_pairs={{0,1},{1,0},{2,3},{3,2},{4,5},{5,4},{6,7},{7,6},{8,9},{9,8},{10,11... | collective-permute-start | bytes 589832 | tf_op jit(solution)/shard_map/ppermute | solution.py:375
  31.7 8.6 %collective-permute-start.12 = (bf16[32,1536]{1,0:T(8,128)(2,1)S(1)}, bf16[32,1536]{1,0:T(8,128)(2,1)S(1)}, u32[]{:S(2)}, u32[]{:S(2)}) collective-permute-start(bf16[32,1536]{1,0:T(8,128)(2,1)S(1)} %get-tuple-element.67.refs_0_), channel_id=1, source_target_pairs={{0,8},{1,9},{2,10},{3,11},{8,0},{9,1},{10,2},{11,3},{16,24},{17,25... | collective-permute-start | bytes 294920 | tf_op jit(solution)/shard_map/ppermute | solution.py:394
  33.1 7.2 %collective-permute-start.13 = (bf16[32,1536]{1,0:T(8,128)(2,1)S(1)}, bf16[32,1536]{1,0:T(8,128)(2,1)S(1)}, u32[]{:S(2)}, u32[]{:S(2)}) collective-permute-start(bf16[32,1536]{1,0:T(8,128)(2,1)S(1)} %get-tuple-element.68.refs_1_), channel_id=1, source_target_pairs={{0,10},{1,11},{2,8},{3,9},{8,2},{9,3},{10,0},{11,1},{16,26},{17,27... | collective-permute-start | bytes 294920 | tf_op jit(solution)/shard_map/ppermute | solution.py:394
  35.2 7.1 %collective-permute-start.18 = (bf16[32,1536]{1,0:T(8,128)(2,1)S(1)}, bf16[32,1536]{1,0:T(8,128)(2,1)S(1)}, u32[]{:S(2)}, u32[]{:S(2)}) collective-permute-start(bf16[32,1536]{1,0:T(8,128)(2,1)S(1)} %get-tuple-element.72.refs_0_), channel_id=1, source_target_pairs={{0,8},{1,9},{2,10},{3,11},{8,0},{9,1},{10,2},{11,3},{16,24},{17,25... | collective-permute-start | bytes 294920 | tf_op jit(solution)/shard_map/ppermute | solution.py:394
  36.7 7.5 %collective-permute-start.19 = (bf16[32,1536]{1,0:T(8,128)(2,1)S(1)}, bf16[32,1536]{1,0:T(8,128)(2,1)S(1)}, u32[]{:S(2)}, u32[]{:S(2)}) collective-permute-start(bf16[32,1536]{1,0:T(8,128)(2,1)S(1)} %get-tuple-element.73.refs_1_), channel_id=1, source_target_pairs={{0,10},{1,11},{2,8},{3,9},{8,2},{9,3},{10,0},{11,1},{16,26},{17,27... | collective-permute-start | bytes 294920 | tf_op jit(solution)/shard_map/ppermute | solution.py:394
  38.5 5.7 %collective-permute-start.17 = (bf16[32,1536]{1,0:T(8,128)(2,1)S(1)}, bf16[32,1536]{1,0:T(8,128)(2,1)S(1)}, u32[]{:S(2)}, u32[]{:S(2)}) collective-permute-start(bf16[32,1536]{1,0:T(8,128)(2,1)S(1)} %get-tuple-element.103), channel_id=1, source_target_pairs={{0,4},{4,0},{1,5},{5,1},{2,6},{6,2},{3,7},{7,3},{8,12},{12,8},{9,1... | collective-permute-start | bytes 294920 | tf_op jit(solution)/shard_map/ppermute | solution.py:372
  40.9 5.3 %collective-permute-start.14 = (bf16[32,1536]{1,0:T(8,128)(2,1)S(1)}, bf16[32,1536]{1,0:T(8,128)(2,1)S(1)}, u32[]{:S(2)}, u32[]{:S(2)}) collective-permute-start(bf16[32,1536]{1,0:T(8,128)(2,1)S(1)} %arrive.2.refs_2_.addend_ref), channel_id=1, source_target_pairs={{0,2},{2,0},{1,3},{3,1},{4,6},{6,4},{5,7},{7,5},{8,10},{10,8},{9,1... | collective-permute-start | bytes 294920 | tf_op jit(solution)/shard_map/ppermute | solution.py:378
  44.8 4.7 %collective-permute-start.20 = (bf16[32,1536]{1,0:T(8,128)(2,1)S(1)}, bf16[32,1536]{1,0:T(8,128)(2,1)S(1)}, u32[]{:S(2)}, u32[]{:S(2)}) collective-permute-start(bf16[32,1536]{1,0:T(8,128)(2,1)S(1)} %arrive.3.refs_2_.addend_ref), channel_id=1, source_target_pairs={{0,2},{2,0},{1,3},{3,1},{4,6},{6,4},{5,7},{7,5},{8,10},{10,8},{9,1... | collective-permute-start | bytes 294920 | tf_op jit(solution)/shard_map/ppermute | solution.py:378
  45.4 4.1 %collective-permute-start.15 = (bf16[32,1536]{1,0:T(8,128)(2,1)S(1)}, bf16[32,1536]{1,0:T(8,128)(2,1)S(1)}, u32[]{:S(2)}, u32[]{:S(2)}) collective-permute-start(bf16[32,1536]{1,0:T(8,128)(2,1)S(1)} %arrive.2.refs_2_.addend_ref), channel_id=1, source_target_pairs={{0,1},{1,0},{2,3},{3,2},{4,5},{5,4},{6,7},{7,6},{8,9},{9,8},{10,11... | collective-permute-start | bytes 294920 | tf_op jit(solution)/shard_map/ppermute | solution.py:375
  46.2 3.3 %collective-permute-start.16 = (bf16[32,1536]{1,0:T(8,128)(2,1)S(1)}, bf16[32,1536]{1,0:T(8,128)(2,1)S(1)}, u32[]{:S(2)}, u32[]{:S(2)}) collective-permute-start(bf16[32,1536]{1,0:T(8,128)(2,1)S(1)} %collective-permute-done.14.refs_3_), channel_id=1, source_target_pairs={{0,1},{1,0},{2,3},{3,2},{4,5},{5,4},{6,7},{7,6},{8,9},{9,8},{10,11... | collective-permute-start | bytes 294920 | tf_op jit(solution)/shard_map/ppermute | solution.py:375
  46.2 6.5 %collective-permute-start.21 = (bf16[32,1536]{1,0:T(8,128)(2,1)S(1)}, bf16[32,1536]{1,0:T(8,128)(2,1)S(1)}, u32[]{:S(2)}, u32[]{:S(2)}) collective-permute-start(bf16[32,1536]{1,0:T(8,128)(2,1)S(1)} %arrive.3.refs_2_.addend_ref), channel_id=1, source_target_pairs={{0,1},{1,0},{2,3},{3,2},{4,5},{5,4},{6,7},{7,6},{8,9},{9,8},{10,11... | collective-permute-start | bytes 294920 | tf_op jit(solution)/shard_map/ppermute | solution.py:375
  49.5 3.2 %collective-permute-start.22 = (bf16[32,1536]{1,0:T(8,128)(2,1)S(1)}, bf16[32,1536]{1,0:T(8,128)(2,1)S(1)}, u32[]{:S(2)}, u32[]{:S(2)}) collective-permute-start(bf16[32,1536]{1,0:T(8,128)(2,1)S(1)} %collective-permute-done.20.refs_3_), channel_id=1, source_target_pairs={{0,1},{1,0},{2,3},{3,2},{4,5},{5,4},{6,7},{7,6},{8,9},{9,8},{10,11... | collective-permute-start | bytes 294920 | tf_op jit(solution)/shard_map/ppermute | solution.py:375
  50.9 7.8 %collective-permute-start.24 = (bf16[768,128]{1,0:T(8,128)(2,1)S(1)}, bf16[768,128]{1,0:T(8,128)(2,1)S(1)}, u32[]{:S(2)}, u32[]{:S(2)}) collective-permute-start(bf16[768,128]{1,0:T(8,128)(2,1)S(1)} %get-tuple-element.76.mine_ref), channel_id=1, source_target_pairs={{0,4},{4,0},{1,5},{5,1},{2,6},{6,2},{3,7},{7,3},{8,12},{12,8},{9,1... | collective-permute-start | bytes 589832 | tf_op jit(solution)/shard_map/ppermute | solution.py:372
  54.2 8.3 %collective-permute-start.23 = (bf16[768,128]{1,0:T(8,128)(2,1)S(1)}, bf16[768,128]{1,0:T(8,128)(2,1)S(1)}, u32[]{:S(2)}, u32[]{:S(2)}) collective-permute-start(bf16[768,128]{1,0:T(8,128)(2,1)S(1)} %get-tuple-element.77.mine_ref), channel_id=1, source_target_pairs={{0,4},{4,0},{1,5},{5,1},{2,6},{6,2},{3,7},{7,3},{8,12},{12,8},{9,1... | collective-permute-start | bytes 589832 | tf_op jit(solution)/shard_map/ppermute | solution.py:372
  60.1 3.8 %collective-permute-start.25 = (bf16[2,32,1536]{2,1,0:T(8,128)(2,1)S(1)}, bf16[2,32,1536]{2,1,0:T(8,128)(2,1)S(1)}, u32[]{:S(2)}, u32[]{:S(2)}) collective-permute-start(bf16[2,32,1536]{2,1,0:T(8,128)(2,1)S(1)} %get-tuple-element.80), channel_id=1, source_target_pairs={{0,1},{1,0},{2,3},{3,2},{4,5},{5,4},{6,7},{7,6},{8,9},{9,8},{10,11... | collective-permute-start | bytes 589832 | tf_op jit(solution)/shard_map/ppermute | solution.py:375
  63.9 2.9 %collective-permute-start.26 = (bf16[2,32,1536]{2,1,0:T(8,128)(2,1)S(1)}, bf16[2,32,1536]{2,1,0:T(8,128)(2,1)S(1)}, u32[]{:S(2)}, u32[]{:S(2)}) collective-permute-start(bf16[2,32,1536]{2,1,0:T(8,128)(2,1)S(1)} %get-tuple-element.84), channel_id=1, source_target_pairs={{0,1},{1,0},{2,3},{3,2},{4,5},{5,4},{6,7},{7,6},{8,9},{9,8},{10,11... | collective-permute-start | bytes 589832 | tf_op jit(solution)/shard_map/ppermute | solution.py:375
  64.6 8.3 %collective-permute-start.28 = (bf16[32,1536]{1,0:T(8,128)(2,1)S(1)}, bf16[32,1536]{1,0:T(8,128)(2,1)S(1)}, u32[]{:S(2)}, u32[]{:S(2)}) collective-permute-start(bf16[32,1536]{1,0:T(8,128)(2,1)S(1)} %get-tuple-element.81), channel_id=1, source_target_pairs={{0,4},{1,5},{2,6},{3,7},{4,0},{5,1},{6,2},{7,3},{8,12},{9,13},{10,... | collective-permute-start | bytes 294920 | tf_op jit(solution)/shard_map/ppermute | solution.py:386
  66.4 6.5 %collective-permute-start.29 = (bf16[32,1536]{1,0:T(8,128)(2,1)S(1)}, bf16[32,1536]{1,0:T(8,128)(2,1)S(1)}, u32[]{:S(2)}, u32[]{:S(2)}) collective-permute-start(bf16[32,1536]{1,0:T(8,128)(2,1)S(1)} %get-tuple-element.82), channel_id=1, source_target_pairs={{0,6},{1,7},{2,4},{3,5},{4,2},{5,3},{6,0},{7,1},{8,14},{9,15},{10,... | collective-permute-start | bytes 294920 | tf_op jit(solution)/shard_map/ppermute | solution.py:386
  67.3 6.9 %collective-permute-start.27 = (bf16[32,1536]{1,0:T(8,128)(2,1)S(1)}, bf16[32,1536]{1,0:T(8,128)(2,1)S(1)}, u32[]{:S(2)}, u32[]{:S(2)}) collective-permute-start(bf16[32,1536]{1,0:T(8,128)(2,1)S(1)} %get-tuple-element.86), channel_id=1, source_target_pairs={{0,2},{2,0},{1,3},{3,1},{4,6},{6,4},{5,7},{7,5},{8,10},{10,8},{9,1... | collective-permute-start | bytes 294920 | tf_op jit(solution)/shard_map/ppermute | solution.py:378
  (1 other events, 1.7 us)

commit v11 on v10

--- a/solution.py
+++ b/solution.py
@@ -181,35 +181,6 @@
     )(facts, keep, arrived, addend, *first_sent)
 
 
-def assemble_kernel(n_own, facts_ref, *refs):
-    grad_ref = refs[-1]
-    width = refs[0].shape[1]
-
-    def total(parts):
-        value = parts[0][...].astype(jnp.float32)
-        for part in parts[1:]:
-            value = value + part[...].astype(jnp.float32)
-        return value.astype(jnp.bfloat16)
-
-    half = facts_ref[HALF]
-    own = pl.ds(pl.multiple_of(half * width, width), width)
-    other = pl.ds(pl.multiple_of((1 - half) * width, width), width)
-    grad_ref[0, :, other] = total(refs[n_own:-1])
-    grad_ref[0, :, own] = total(refs[:n_own])
-
-
-def assemble(facts, own_parts, other_parts):
-    shard, width = own_parts[0].shape
-    return pl.pallas_call(
-        functools.partial(assemble_kernel, len(own_parts)),
-        out_shape=jax.ShapeDtypeStruct((1, shard, 2 * width), jnp.bfloat16),
-        in_specs=[in_smem()] + [in_vmem()] * (len(own_parts) + len(other_parts)),
-        out_specs=in_vmem(),
-        compiler_params=pltpu.CompilerParams(vmem_limit_bytes=VMEM_BYTES),
-        name="assemble",
-    )(facts, *own_parts, *other_parts)
-
-
 def weight_grad_kernel(
     facts_ref, a0, a1, b0, b1, first0, first1, second0, second1, value_ref, out_ref
 ):
@@ -330,33 +301,6 @@
     )(table)
 
 
-def arrive_kernel(facts_ref, input_ref, *refs):
-    parts, piece_ref = refs[:-1], refs[-1]
-
-    @pl.when(facts_ref[ODD] == 1)
-    def _():
-        piece_ref[...] = input_ref[...]
-
-    @pl.when(facts_ref[ODD] == 0)
-    def _():
-        total = parts[0][...].astype(jnp.float32)
-        for part in parts[1:]:
-            total = total + part[...].astype(jnp.float32)
-        piece_ref[...] = total.astype(jnp.bfloat16)
-
-
-def arrive(facts, input_piece, parts):
-    return pl.pallas_call(
-        arrive_kernel,
-        out_shape=jax.ShapeDtypeStruct(parts[0].shape, jnp.bfloat16),
-        in_specs=[in_smem()] + [in_vmem()] * (1 + len(parts)),
-        out_specs=in_vmem(),
-        compiler_params=pltpu.CompilerParams(vmem_limit_bytes=VMEM_BYTES),
-        cost_estimate=SMALL,
-        name="arrive",
-    )(facts, input_piece, *parts)
-
-
 def on_device(section_input, query, key_stash, incoming, version, w_value, w_out):
     half = lax.axis_index("half")
     odd_flag = lax.axis_index("pair") % 2
@@ -399,21 +343,29 @@
     def other_columns(array):
         return lax.dynamic_slice_in_dim(array, (1 - half) * width, width, 1)
 
+    def total(parts):
+        value = parts[0].astype(jnp.float32)
+        for part in parts[1:]:
+            value = value + part.astype(jnp.float32)
+        return value
+
     def spread_rows(piece):
         return [piece] + [to_row(piece, delta) for delta in range(1, outer)]
 
     facts = jnp.stack([odd_flag, 1 - odd_flag, version[0], core, row, half])
     first = jnp.where(odd, incoming[0], section_input[0])
     own_piece, sent_piece = own_columns(first), other_columns(first)
-    note = jnp.full((NOTE_ROWS, width), version[0], jnp.int32).astype(jnp.bfloat16)
-    noted_piece = jnp.concatenate([sent_piece, note])
-    other_note = swap_half(noted_piece)
-    first_piece = [own_piece, other_note[:shard]]
-    first_mine = [spread_rows(piece) for piece in first_piece]
+    other_piece = swap_half(sent_piece)
+    first_piece = [own_piece, other_piece]
+    later_own, _ = lax.optimization_barrier((own_piece, other_piece))
+    first_mine = [spread_rows(later_own), spread_rows(other_piece)]
     own_probs = attention_probs(jnp.concatenate([query, key_stash]))
+    note = jnp.full((NOTE_ROWS, LANES), version[0], jnp.int32).astype(jnp.bfloat16)
+    own_probs = jnp.concatenate([own_probs, note])
+    other_probs = swap_half(own_probs)
+    other_note = other_probs
     late_value, late_out, _ = lax.optimization_barrier((w_value, w_out, own_probs))
     first_table = load_first(facts, late_value, late_out)
-    other_probs = swap_half(own_probs)
     swapped, _ = lax.optimization_barrier((first_mine, first_table))
     first_theirs = [[swap_core(piece) for piece in pieces] for pieces in swapped]
 
@@ -442,7 +394,7 @@
     input_piece = [own_columns(later_input), swap_half(other_columns(later_input))]
     for m in range(2):
         received = [swap_section(part, d) for d, part in enumerate(first_sent[m])]
-        second_piece[m] = arrive(facts, input_piece[m], received)
+        second_piece[m] = jnp.where(odd, input_piece[m], total(received).astype(jnp.bfloat16))
     for m in range(2):
         mine = spread_rows(second_piece[m])
         theirs = [swap_core(piece) for piece in mine]
@@ -465,8 +417,13 @@
         facts, first_result, second_result, first_full, second_full
     )
     own_parts, other_parts, _ = lax.optimization_barrier((own_parts, other_parts, grad_value))
-    input_grad = assemble(facts, own_parts, other_parts)
-    return (input_grad, grad_value, grad_out)
+    own_grad = total(own_parts).astype(jnp.bfloat16)
+    other_grad = total(other_parts).astype(jnp.bfloat16)
+    input_grad = jnp.concatenate(
+        [jnp.where(half == 0, own_grad, other_grad), jnp.where(half == 0, other_grad, own_grad)],
+        axis=1,
+    )
+    return (input_grad[None], grad_value, grad_out)
 
 
 def solution(mesh):

time: 75.7 us -> 74.3 us (0.982)
  waiting for transfers between devices: 18.1 us -> 21.2 us
  starting transfers between devices: 25.9 us -> 23.2 us
  Pallas kernels: 27.6 us -> 25.1 us
  other arithmetic: 2.1 us -> 2.94 us
    pallas_call x3 -> x0, Pallas kernels: 2.42 us -> none  [the longest x1 1.26 us: assemble(): pl.pallas_call(functools.partial(assemble_kernel, len(own_parts)), out_sh...]
    ppermute x5, starting transfers between devices: 7.1 us -> 5.02 us  [to_row(): return lax.ppermute(array, 'outer', [(i, i ^ delta) for i in range(outer)])]
    ppermute x4, waiting for transfers between devices: 1.87 us -> 3.2 us  [swap_section(): return lax.ppermute(array, ('pair', 'outer', 'core'), pairs)]
    ppermute x5, waiting for transfers between devices: 4.97 us -> 6.13 us  [to_row(): return lax.ppermute(array, 'outer', [(i, i ^ delta) for i in range(outer)])]
    ppermute x7, starting transfers between devices: 9.78 us -> 8.96 us  [swap_half(): return lax.ppermute(array, 'half', [(0, 1), (1, 0)])]
  transfers between devices with their start and end apart: 30 -> 30, of which waited for: 12 -> 15; matrix products, arithmetic and copies ran while one was open for 2% -> 2% of each run, Pallas kernels for 35% -> 34%
where the time goes in v11:
time: 74.3 us; the launch traced here: 74.2 us
  Pallas kernels  25.1 us (34%)
  starting transfers between devices  23.2 us (31%)
  waiting for transfers between devices  21.2 us (29%)
  other arithmetic  2.94 us (4%)
  between operations  1.54 us (2%)
    ppermute x7, waiting for transfers between devices, swap_half(): return lax.ppermute(array, 'half', [(0, 1), (1, 0)])  11.4 us
    ppermute x7, starting transfers between devices, swap_half(): return lax.ppermute(array, 'half', [(0, 1), (1, 0)])  8.96 us
    ppermute x5, waiting for transfers between devices, to_row(): return lax.ppermute(array, 'outer', [(i, i ^ delta) for i in range(outer)])  6.13 us
    pallas_call x4, Pallas kernels, mix(): pl.pallas_call(functools.partial(mix_kernel, outer, natural, index), out_...  5.85 us
    pallas_call x4, Pallas kernels, project(): pl.pallas_call(functools.partial(project_kernel, index, outer, shard, len...  5.54 us
    ppermute x4, starting transfers between devices, swap_section(): return lax.ppermute(array, ('pair', 'outer', 'core'), pairs)  5.08 us
    ppermute x5, starting transfers between devices, to_row(): return lax.ppermute(array, 'outer', [(i, i ^ delta) for i in range(outer)])  5.02 us
    pallas_call x1, Pallas kernels, weight_grads(): pl.pallas_call(weight_grad_kernel, grid=(CHUNKS,), out_shape=(grad, grad)...  4.04 us
  transfers between devices with their start and end apart: 30, of which 15 were waited for; matrix products, arithmetic and copies ran while one was open for 2% of the time, Pallas kernels for 34%

profile of v11, /device:TPU:0, one launch (start us, length us, event | category | flops | bytes accessed | tf_op | source)
XLA Modules:
  0.0 74.2 jit_solution(16408182814635092200)
XLA Ops:
  0.6 1.0 %bitcast_select_fusion = bf16[32,3072]{1,0:T(8,128)(2,1)S(1)} fusion(bf16[1,32,3072]{2,1,0:T(8,128)(2,1)} %param.10, pred[]{:T(512)S(6)} %eq.10, bf16[1,32,3072]{2,1,0:T(8,128)(2,1)} %param.7), kind=kLoop, calls=%fused_computation.2 | loop fusion | flops 98304 | bytes 589825 | tf_op jit(solution)/shard_map/jit(_where)/select_n | solution.py:356
  1.7 3.0 %collective-permute-start.1 = (bf16[32,1536]{1,0:T(8,128)(2,1)S(1)}, bf16[32,1536]{1,0:T(8,128)(2,1)S(1)}, u32[]{:S(2)}, u32[]{:S(2)}) collective-permute-start(bf16[32,1536]{1,0:T(8,128)(2,1)S(1)} %get-tuple-element.109), channel_id=1, source_target_pairs={{0,4},{4,0},{1,5},{5,1},{2,6},{6,2},{3,7},{7,3},{8,12},{12,8},{9,1... | collective-permute-start | bytes 294920 | tf_op jit(solution)/shard_map/ppermute | solution.py:316
  4.7 1.1 %pad_maximum_fusion.stash_ref = bf16[2,768,128]{2,1,0:T(8,128)(2,1)S(1)} fusion(bf16[1,768,128]{2,1,0:T(8,128)(2,1)} %param.9, bf16[1,768,128]{2,1,0:T(8,128)(2,1)} %param.8), kind=kLoop, calls=%fused_computation | loop fusion | flops 196608 | bytes 786432 | tf_op jit(solution)/shard_map/concatenate | solution.py:362
  7.5 1.9 %collective-permute-start.2 = (bf16[32,1536]{1,0:T(8,128)(2,1)S(1)}, bf16[32,1536]{1,0:T(8,128)(2,1)S(1)}, u32[]{:S(2)}, u32[]{:S(2)}) collective-permute-start(bf16[32,1536]{1,0:T(8,128)(2,1)S(1)} %get-tuple-element.62.refs_1_.addend_ref), channel_id=1, source_target_pairs={{0,2},{2,0},{1,3},{3,1},{4,6},{6,4},{5,7},{7,5},{8,10},{10,8},{9,1... | collective-permute-start | bytes 294920 | tf_op jit(solution)/shard_map/ppermute | solution.py:322
  9.6 2.9 %load_first.1.refs_0_ = bf16[1,2,768,1536]{3,2,1,0:T(8,128)(2,1)S(1)} custom-call(s32[6]{0:T(128)S(1)} %stack.23.facts_ref, bf16[1,2,768,1536]{3,2,1,0:T(8,128)(2,1)} %source_ref, bf16[1,2,768,1536]{3,2,1,0:T(8,128)(2,1)} %source_ref.1), custom_call_target="tpu_custom_call" | custom-call | flops 1 | bytes 1 | tf_op jit(solution)/shard_map/load_first/pallas_call | solution.py:279
  13.0 1.1 %collective-permute-done.3.refs_2_ = bf16[32,1536]{1,0:T(8,128)(2,1)S(1)} collective-permute-done((bf16[32,1536]{1,0:T(8,128)(2,1)S(1)}, bf16[32,1536]{1,0:T(8,128)(2,1)S(1)}, u32[]{:S(2)}, u32[]{:S(2)}) %collective-permute-start.3) | collective-permute-done | bytes 98336 | tf_op jit(solution)/shard_map/ppermute | solution.py:322
  15.5 1.4 %project.4 = (bf16[768,128]{1,0:T(8,128)(2,1)S(1)}, bf16[128,1536]{1,0:T(8,128)(2,1)S(1)}) custom-call(s32[6]{0:T(128)S(1)} %stack.23.facts_ref, bf16[1040,128]{1,0:T(8,128)(2,1)S(1)} %collective-permute-done.note_ref.probs_ref, bf16[1,2,768,1536]{3,2,1,0:T(8,128)(2,1)S(1)} %load_first.1.refs_0_, ...), custom_call_target="tpu_custom_call" | custom-call | flops 1 | bytes 1 | tf_op jit(solution)/shard_map/project/pallas_call | solution.py:86
  16.9 1.6 %collective-permute-start.8 = (bf16[768,128]{1,0:T(8,128)(2,1)S(1)}, bf16[768,128]{1,0:T(8,128)(2,1)S(1)}, u32[]{:S(2)}, u32[]{:S(2)}) collective-permute-start(bf16[768,128]{1,0:T(8,128)(2,1)S(1)} %get-tuple-element.59.mine_ref), channel_id=1, source_target_pairs={{0,4},{4,0},{1,5},{5,1},{2,6},{6,2},{3,7},{7,3},{8,12},{12,8},{9,1... | collective-permute-start | bytes 589832 | tf_op jit(solution)/shard_map/ppermute | solution.py:316
  18.5 1.3 %project.5 = (bf16[768,128]{1,0:T(8,128)(2,1)S(1)}, bf16[128,1536]{1,0:T(8,128)(2,1)S(1)}) custom-call(s32[6]{0:T(128)S(1)} %stack.23.facts_ref, bf16[1040,128]{1,0:T(8,128)(2,1)S(1)} %collective-permute-done.note_ref.probs_ref, bf16[1,2,768,1536]{3,2,1,0:T(8,128)(2,1)S(1)} %load_first.1.refs_0_, bf16[32,1536]{1,0:T(8,128)(2,1)S(1)} %get-tuple-element.62.refs_1_.addend_ref, ...), custom_call_target="tpu_custom_call" | custom-call | flops 1 | bytes 1 | tf_op jit(solution)/shard_map/project/pallas_call | solution.py:86
  20.4 2.5 %load_table.2.value_ref.refs_0_ = bf16[1,2,768,1536]{3,2,1,0:T(8,128)(2,1)S(1)} custom-call(bf16[1,2,768,1536]{3,2,1,0:T(8,128)(2,1)} %source_ref), custom_call_target="tpu_custom_call" | custom-call | flops 1 | bytes 1 | tf_op jit(solution)/shard_map/load_table/pallas_call | solution.py:292
  23.0 1.7 %collective-permute-done.8.arrived_ref = bf16[768,128]{1,0:T(8,128)(2,1)S(1)} collective-permute-done((bf16[768,128]{1,0:T(8,128)(2,1)S(1)}, bf16[768,128]{1,0:T(8,128)(2,1)S(1)}, u32[]{:S(2)}, u32[]{:S(2)}) %collective-permute-start.8) | collective-permute-done | bytes 196640 | tf_op jit(solution)/shard_map/ppermute | solution.py:316
  24.7 1.5 %mix.4 = (bf16[768,128]{1,0:T(8,128)(2,1)S(1)}, bf16[2,32,1536]{2,1,0:T(8,128)(2,1)S(1)}, bf16[2,32,1536]{2,1,0:T(8,128)(2,1)S(1)}) custom-call(s32[6]{0:T(128)S(1)} %stack.23.facts_ref, bf16[1040,128]{1,0:T(8,128)(2,1)S(1)} %collective-permute-done.note_ref.probs_ref, bf16[1,2,768,1536]{3,2,1,0:T(8,128)(2,1)S(1)} %load_table.2.value_ref.refs_0_, ...), custom_call_target="tpu_custom_call" | custom-call | flops 1 | bytes 1 | tf_op jit(solution)/shard_map/mix/pallas_call | solution.py:146
  26.3 2.1 %collective-permute-done.10.arrived_ref = bf16[768,128]{1,0:T(8,128)(2,1)S(1)} collective-permute-done((bf16[768,128]{1,0:T(8,128)(2,1)S(1)}, bf16[768,128]{1,0:T(8,128)(2,1)S(1)}, u32[]{:S(2)}, u32[]{:S(2)}) %collective-permute-start.10) | collective-permute-done | bytes 196640 | tf_op jit(solution)/shard_map/ppermute | solution.py:316
  28.4 1.6 %mix.5 = (bf16[768,128]{1,0:T(8,128)(2,1)S(1)}, bf16[2,32,1536]{2,1,0:T(8,128)(2,1)S(1)}, bf16[2,32,1536]{2,1,0:T(8,128)(2,1)S(1)}) custom-call(s32[6]{0:T(128)S(1)} %stack.23.facts_ref, bf16[1040,128]{1,0:T(8,128)(2,1)S(1)} %collective-permute-done.note_ref.probs_ref, bf16[1,2,768,1536]{3,2,1,0:T(8,128)(2,1)S(1)} %load_table.2.value_ref.refs_0_, ...), custom_call_target="tpu_custom_call" | custom-call | flops 1 | bytes 1 | tf_op jit(solution)/shard_map/mix/pallas_call | solution.py:146
  30.7 1.5 %collective-permute-start.12 = (bf16[32,1536]{1,0:T(8,128)(2,1)S(1)}, bf16[32,1536]{1,0:T(8,128)(2,1)S(1)}, u32[]{:S(2)}, u32[]{:S(2)}) collective-permute-start(bf16[32,1536]{1,0:T(8,128)(2,1)S(1)} %get-tuple-element.69.refs_0_), channel_id=1, source_target_pairs={{0,8},{1,9},{2,10},{3,11},{8,0},{9,1},{10,2},{11,3},{16,24},{17,25... | collective-permute-start | bytes 294920 | tf_op jit(solution)/shard_map/ppermute | solution.py:338
  32.2 1.4 %collective-permute-start.13 = (bf16[32,1536]{1,0:T(8,128)(2,1)S(1)}, bf16[32,1536]{1,0:T(8,128)(2,1)S(1)}, u32[]{:S(2)}, u32[]{:S(2)}) collective-permute-start(bf16[32,1536]{1,0:T(8,128)(2,1)S(1)} %get-tuple-element.70.refs_1_), channel_id=1, source_target_pairs={{0,10},{1,11},{2,8},{3,9},{8,2},{9,3},{10,0},{11,1},{16,26},{17,27... | collective-permute-start | bytes 294920 | tf_op jit(solution)/shard_map/ppermute | solution.py:338
  34.1 1.5 %collective-permute-start.18 = (bf16[32,1536]{1,0:T(8,128)(2,1)S(1)}, bf16[32,1536]{1,0:T(8,128)(2,1)S(1)}, u32[]{:S(2)}, u32[]{:S(2)}) collective-permute-start(bf16[32,1536]{1,0:T(8,128)(2,1)S(1)} %get-tuple-element.74.refs_0_), channel_id=1, source_target_pairs={{0,8},{1,9},{2,10},{3,11},{8,0},{9,1},{10,2},{11,3},{16,24},{17,25... | collective-permute-start | bytes 294920 | tf_op jit(solution)/shard_map/ppermute | solution.py:338
  37.4 1.8 %collective-permute-done.13 = bf16[32,1536]{1,0:T(8,128)(2,1)S(1)} collective-permute-done((bf16[32,1536]{1,0:T(8,128)(2,1)S(1)}, bf16[32,1536]{1,0:T(8,128)(2,1)S(1)}, u32[]{:S(2)}, u32[]{:S(2)}) %collective-permute-start.13) | collective-permute-done | bytes 98336 | tf_op jit(solution)/shard_map/ppermute | solution.py:338
  39.2 1.6 %collective-permute-start.17 = (bf16[32,1536]{1,0:T(8,128)(2,1)S(1)}, bf16[32,1536]{1,0:T(8,128)(2,1)S(1)}, u32[]{:S(2)}, u32[]{:S(2)}) collective-permute-start(bf16[32,1536]{1,0:T(8,128)(2,1)S(1)} %get-tuple-element.107), channel_id=1, source_target_pairs={{0,4},{4,0},{1,5},{5,1},{2,6},{6,2},{3,7},{7,3},{8,12},{12,8},{9,1... | collective-permute-start | bytes 294920 | tf_op jit(solution)/shard_map/ppermute | solution.py:316
  41.6 1.4 %collective-permute-done.19 = bf16[32,1536]{1,0:T(8,128)(2,1)S(1)} collective-permute-done((bf16[32,1536]{1,0:T(8,128)(2,1)S(1)}, bf16[32,1536]{1,0:T(8,128)(2,1)S(1)}, u32[]{:S(2)}, u32[]{:S(2)}) %collective-permute-start.19) | collective-permute-done | bytes 98336 | tf_op jit(solution)/shard_map/ppermute | solution.py:338
  45.9 2.7 %collective-permute-done.20.refs_3_ = bf16[32,1536]{1,0:T(8,128)(2,1)S(1)} collective-permute-done((bf16[32,1536]{1,0:T(8,128)(2,1)S(1)}, bf16[32,1536]{1,0:T(8,128)(2,1)S(1)}, u32[]{:S(2)}, u32[]{:S(2)}) %collective-permute-start.20) | collective-permute-done | bytes 98336 | tf_op jit(solution)/shard_map/ppermute | solution.py:322
  48.7 1.4 %project.6 = (bf16[768,128]{1,0:T(8,128)(2,1)S(1)}, bf16[128,1536]{1,0:T(8,128)(2,1)S(1)}) custom-call(s32[6]{0:T(128)S(1)} %stack.23.facts_ref, bf16[1040,128]{1,0:T(8,128)(2,1)S(1)} %collective-permute-done.note_ref.probs_ref, bf16[1,2,768,1536]{3,2,1,0:T(8,128)(2,1)S(1)} %load_table.2.value_ref.refs_0_, bf16[1,2,768,1536]{3,2,1,0:T(8,128)(2,1)S(1)} %load_table.3.refs_1_, ...), custom_call_target="tpu_custom_call" | custom-call | flops 1 | bytes 1 | tf_op jit(solution)/shard_map/project/pallas_call | solution.py:86
  50.1 1.6 %collective-permute-start.24 = (bf16[768,128]{1,0:T(8,128)(2,1)S(1)}, bf16[768,128]{1,0:T(8,128)(2,1)S(1)}, u32[]{:S(2)}, u32[]{:S(2)}) collective-permute-start(bf16[768,128]{1,0:T(8,128)(2,1)S(1)} %get-tuple-element.78.mine_ref), channel_id=1, source_target_pairs={{0,4},{4,0},{1,5},{5,1},{2,6},{6,2},{3,7},{7,3},{8,12},{12,8},{9,1... | collective-permute-start | bytes 589832 | tf_op jit(solution)/shard_map/ppermute | solution.py:316
  51.6 1.4 %project.7 = (bf16[768,128]{1,0:T(8,128)(2,1)S(1)}, bf16[128,1536]{1,0:T(8,128)(2,1)S(1)}) custom-call(s32[6]{0:T(128)S(1)} %stack.23.facts_ref, bf16[1040,128]{1,0:T(8,128)(2,1)S(1)} %collective-permute-done.note_ref.probs_ref, bf16[1,2,768,1536]{3,2,1,0:T(8,128)(2,1)S(1)} %load_table.2.value_ref.refs_0_, bf16[1,2,768,1536]{3,2,1,0:T(8,128)(2,1)S(1)} %load_table.3.refs_1_, ...), custom_call_target="tpu_custom_call" | custom-call | flops 1 | bytes 1 | tf_op jit(solution)/shard_map/project/pallas_call | solution.py:86
  53.7 4.2 %collective-permute-done.24.arrived_ref = bf16[768,128]{1,0:T(8,128)(2,1)S(1)} collective-permute-done((bf16[768,128]{1,0:T(8,128)(2,1)S(1)}, bf16[768,128]{1,0:T(8,128)(2,1)S(1)}, u32[]{:S(2)}, u32[]{:S(2)}) %collective-permute-start.24) | collective-permute-done | bytes 196640 | tf_op jit(solution)/shard_map/ppermute | solution.py:316
  57.8 1.4 %mix.7 = (bf16[768,128]{1,0:T(8,128)(2,1)S(1)}, bf16[2,32,1536]{2,1,0:T(8,128)(2,1)S(1)}, bf16[2,32,1536]{2,1,0:T(8,128)(2,1)S(1)}) custom-call(s32[6]{0:T(128)S(1)} %stack.23.facts_ref, bf16[1040,128]{1,0:T(8,128)(2,1)S(1)} %collective-permute-done.note_ref.probs_ref, bf16[1,2,768,1536]{3,2,1,0:T(8,128)(2,1)S(1)} %load_table.2.value_ref.refs_0_, ...), custom_call_target="tpu_custom_call" | custom-call | flops 1 | bytes 1 | tf_op jit(solution)/shard_map/mix/pallas_call | solution.py:146
  59.3 2.3 %collective-permute-done.23.arrived_ref = bf16[768,128]{1,0:T(8,128)(2,1)S(1)} collective-permute-done((bf16[768,128]{1,0:T(8,128)(2,1)S(1)}, bf16[768,128]{1,0:T(8,128)(2,1)S(1)}, u32[]{:S(2)}, u32[]{:S(2)}) %collective-permute-start.23) | collective-permute-done | bytes 196640 | tf_op jit(solution)/shard_map/ppermute | solution.py:316
  61.6 1.4 %mix.6 = (bf16[768,128]{1,0:T(8,128)(2,1)S(1)}, bf16[2,32,1536]{2,1,0:T(8,128)(2,1)S(1)}, bf16[2,32,1536]{2,1,0:T(8,128)(2,1)S(1)}) custom-call(s32[6]{0:T(128)S(1)} %stack.23.facts_ref, bf16[1040,128]{1,0:T(8,128)(2,1)S(1)} %collective-permute-done.note_ref.probs_ref, bf16[1,2,768,1536]{3,2,1,0:T(8,128)(2,1)S(1)} %load_table.2.value_ref.refs_0_, ...), custom_call_target="tpu_custom_call" | custom-call | flops 1 | bytes 1 | tf_op jit(solution)/shard_map/mix/pallas_call | solution.py:146
  63.8 1.6 %collective-permute-start.28 = (bf16[32,1536]{1,0:T(8,128)(2,1)S(1)}, bf16[32,1536]{1,0:T(8,128)(2,1)S(1)}, u32[]{:S(2)}, u32[]{:S(2)}) collective-permute-start(bf16[32,1536]{1,0:T(8,128)(2,1)S(1)} %get-tuple-element.83), channel_id=1, source_target_pairs={{0,4},{1,5},{2,6},{3,7},{4,0},{5,1},{6,2},{7,3},{8,12},{9,13},{10,... | collective-permute-start | bytes 294920 | tf_op jit(solution)/shard_map/ppermute | solution.py:330
  66.8 1.3 %collective-permute-start.27 = (bf16[32,1536]{1,0:T(8,128)(2,1)S(1)}, bf16[32,1536]{1,0:T(8,128)(2,1)S(1)}, u32[]{:S(2)}, u32[]{:S(2)}) collective-permute-start(bf16[32,1536]{1,0:T(8,128)(2,1)S(1)} %get-tuple-element.88), channel_id=1, source_target_pairs={{0,2},{2,0},{1,3},{3,1},{4,6},{6,4},{5,7},{7,5},{8,10},{10,8},{9,1... | collective-permute-start | bytes 294920 | tf_op jit(solution)/shard_map/ppermute | solution.py:322
  68.0 4.0 %weight_grads.1 = (bf16[1,768,1536]{2,1,0:T(8,128)(2,1)}, bf16[1,768,1536]{2,1,0:T(8,128)(2,1)}) custom-call(s32[6]{0:T(128)S(1)} %stack.23.facts_ref, bf16[768,128]{1,0:T(8,128)(2,1)S(1)} %get-tuple-element.89.a0, bf16[768,128]{1,0:T(8,128)(2,1)S(1)} %get-tuple-element.90.a1, bf16[768,128]{1,0:T(8,128)(2,1)S(1)} %get-tuple-element.93.b0, ...), custom_call_target="tpu_custom_call" | custom-call | flops 1 | bytes 1 | tf_op jit(solution)/shard_map/weight_grads/pallas_call | solution.py:206
  72.1 1.4 %collective-permute-done.27 = bf16[32,1536]{1,0:T(8,128)(2,1)S(1)} collective-permute-done((bf16[32,1536]{1,0:T(8,128)(2,1)S(1)}, bf16[32,1536]{1,0:T(8,128)(2,1)S(1)}, u32[]{:S(2)}, u32[]{:S(2)}) %collective-permute-start.27) | collective-permute-done | bytes 98336 | tf_op jit(solution)/shard_map/ppermute | solution.py:322
  (61 shorter events, 14.3 us)
Async XLA Ops:
  1.7 5.8 %collective-permute-start.1 = (bf16[32,1536]{1,0:T(8,128)(2,1)S(1)}, bf16[32,1536]{1,0:T(8,128)(2,1)S(1)}, u32[]{:S(2)}, u32[]{:S(2)}) collective-permute-start(bf16[32,1536]{1,0:T(8,128)(2,1)S(1)} %get-tuple-element.109), channel_id=1, source_target_pairs={{0,4},{4,0},{1,5},{5,1},{2,6},{6,2},{3,7},{7,3},{8,12},{12,8},{9,1... | collective-permute-start | bytes 294920 | tf_op jit(solution)/shard_map/ppermute | solution.py:316
  7.2 7.9 %collective-permute-start = (bf16[1040,128]{1,0:T(8,128)(2,1)S(1)}, bf16[1040,128]{1,0:T(8,128)(2,1)S(1)}, u32[]{:S(2)}, u32[]{:S(2)}) collective-permute-start(bf16[1040,128]{1,0:T(8,128)(2,1)S(1)} %concatenate.10.probs_ref), channel_id=1, source_target_pairs={{0,4},{4,0},{1,5},{5,1},{2,6},{6,2},{3,7},{7,3},{8,12},{12,8},{9,1... | collective-permute-start | bytes 798728 | tf_op jit(solution)/shard_map/ppermute | solution.py:316
  7.5 5.5 %collective-permute-start.2 = (bf16[32,1536]{1,0:T(8,128)(2,1)S(1)}, bf16[32,1536]{1,0:T(8,128)(2,1)S(1)}, u32[]{:S(2)}, u32[]{:S(2)}) collective-permute-start(bf16[32,1536]{1,0:T(8,128)(2,1)S(1)} %get-tuple-element.62.refs_1_.addend_ref), channel_id=1, source_target_pairs={{0,2},{2,0},{1,3},{3,1},{4,6},{6,4},{5,7},{7,5},{8,10},{10,8},{9,1... | collective-permute-start | bytes 294920 | tf_op jit(solution)/shard_map/ppermute | solution.py:322
  9.4 4.7 %collective-permute-start.3 = (bf16[32,1536]{1,0:T(8,128)(2,1)S(1)}, bf16[32,1536]{1,0:T(8,128)(2,1)S(1)}, u32[]{:S(2)}, u32[]{:S(2)}) collective-permute-start(bf16[32,1536]{1,0:T(8,128)(2,1)S(1)} %collective-permute-done.1.refs_1_.addend_ref), channel_id=1, source_target_pairs={{0,2},{2,0},{1,3},{3,1},{4,6},{6,4},{5,7},{7,5},{8,10},{10,8},{9,1... | collective-permute-start | bytes 294920 | tf_op jit(solution)/shard_map/ppermute | solution.py:322
  14.1 1.3 %collective-permute-start.4 = (bf16[32,1536]{1,0:T(8,128)(2,1)S(1)}, bf16[32,1536]{1,0:T(8,128)(2,1)S(1)}, u32[]{:S(2)}, u32[]{:S(2)}) collective-permute-start(bf16[32,1536]{1,0:T(8,128)(2,1)S(1)} %collective-permute-done.1.refs_1_.addend_ref), channel_id=1, source_target_pairs={{0,1},{1,0},{2,3},{3,2},{4,5},{5,4},{6,7},{7,6},{8,9},{9,8},{10,11... | collective-permute-start | bytes 294920 | tf_op jit(solution)/shard_map/ppermute | solution.py:319
  14.1 1.5 %collective-permute-start.5 = (bf16[32,1536]{1,0:T(8,128)(2,1)S(1)}, bf16[32,1536]{1,0:T(8,128)(2,1)S(1)}, u32[]{:S(2)}, u32[]{:S(2)}) collective-permute-start(bf16[32,1536]{1,0:T(8,128)(2,1)S(1)} %collective-permute-done.3.refs_2_), channel_id=1, source_target_pairs={{0,1},{1,0},{2,3},{3,2},{4,5},{5,4},{6,7},{7,6},{8,9},{9,8},{10,11... | collective-permute-start | bytes 294920 | tf_op jit(solution)/shard_map/ppermute | solution.py:319
  14.6 3.9 %collective-permute-start.6 = (bf16[32,1536]{1,0:T(8,128)(2,1)S(1)}, bf16[32,1536]{1,0:T(8,128)(2,1)S(1)}, u32[]{:S(2)}, u32[]{:S(2)}) collective-permute-start(bf16[32,1536]{1,0:T(8,128)(2,1)S(1)} %get-tuple-element.62.refs_1_.addend_ref), channel_id=1, source_target_pairs={{0,1},{1,0},{2,3},{3,2},{4,5},{5,4},{6,7},{7,6},{8,9},{9,8},{10,11... | collective-permute-start | bytes 294920 | tf_op jit(solution)/shard_map/ppermute | solution.py:319
  14.6 3.9 %collective-permute-start.7 = (bf16[32,1536]{1,0:T(8,128)(2,1)S(1)}, bf16[32,1536]{1,0:T(8,128)(2,1)S(1)}, u32[]{:S(2)}, u32[]{:S(2)}) collective-permute-start(bf16[32,1536]{1,0:T(8,128)(2,1)S(1)} %collective-permute-done.2.refs_2_), channel_id=1, source_target_pairs={{0,1},{1,0},{2,3},{3,2},{4,5},{5,4},{6,7},{7,6},{8,9},{9,8},{10,11... | collective-permute-start | bytes 294920 | tf_op jit(solution)/shard_map/ppermute | solution.py:319
  16.9 7.8 %collective-permute-start.8 = (bf16[768,128]{1,0:T(8,128)(2,1)S(1)}, bf16[768,128]{1,0:T(8,128)(2,1)S(1)}, u32[]{:S(2)}, u32[]{:S(2)}) collective-permute-start(bf16[768,128]{1,0:T(8,128)(2,1)S(1)} %get-tuple-element.59.mine_ref), channel_id=1, source_target_pairs={{0,4},{4,0},{1,5},{5,1},{2,6},{6,2},{3,7},{7,3},{8,12},{12,8},{9,1... | collective-permute-start | bytes 589832 | tf_op jit(solution)/shard_map/ppermute | solution.py:316
  19.8 8.5 %collective-permute-start.10 = (bf16[768,128]{1,0:T(8,128)(2,1)S(1)}, bf16[768,128]{1,0:T(8,128)(2,1)S(1)}, u32[]{:S(2)}, u32[]{:S(2)}) collective-permute-start(bf16[768,128]{1,0:T(8,128)(2,1)S(1)} %get-tuple-element.64.mine_ref), channel_id=1, source_target_pairs={{0,4},{4,0},{1,5},{5,1},{2,6},{6,2},{3,7},{7,3},{8,12},{12,8},{9,1... | collective-permute-start | bytes 589832 | tf_op jit(solution)/shard_map/ppermute | solution.py:316
  20.4 15.9 %slice-start = ((s8[4718592]{0:T(1024)(128)(4,1)}), s8[4194304]{0:T(1024)(128)(4,1)S(1)}, s32[]{:S(2)}) async-start(s8[4718592]{0:T(1024)(128)(4,1)} %bitcast.12), calls=%async_computation | async-start | bytes 8388608
  23.0 13.4 %slice-start.1 = ((s8[4718592]{0:T(1024)(128)(4,1)}), s8[524288]{0:T(1024)(128)(4,1)S(1)}, s32[]{:S(2)}) async-start(s8[4718592]{0:T(1024)(128)(4,1)} %bitcast.12), calls=%async_computation.1 | async-start | bytes 1048576
  26.2 3.8 %collective-permute-start.9 = (bf16[2,32,1536]{2,1,0:T(8,128)(2,1)S(1)}, bf16[2,32,1536]{2,1,0:T(8,128)(2,1)S(1)}, u32[]{:S(2)}, u32[]{:S(2)}) collective-permute-start(bf16[2,32,1536]{2,1,0:T(8,128)(2,1)S(1)} %get-tuple-element.68), channel_id=1, source_target_pairs={{0,1},{1,0},{2,3},{3,2},{4,5},{5,4},{6,7},{7,6},{8,9},{9,8},{10,11... | collective-permute-start | bytes 589832 | tf_op jit(solution)/shard_map/ppermute | solution.py:319
  30.0 3.6 %collective-permute-start.11 = (bf16[2,32,1536]{2,1,0:T(8,128)(2,1)S(1)}, bf16[2,32,1536]{2,1,0:T(8,128)(2,1)S(1)}, u32[]{:S(2)}, u32[]{:S(2)}) collective-permute-start(bf16[2,32,1536]{2,1,0:T(8,128)(2,1)S(1)} %get-tuple-element.73), channel_id=1, source_target_pairs={{0,1},{1,0},{2,3},{3,2},{4,5},{5,4},{6,7},{7,6},{8,9},{9,8},{10,11... | collective-permute-start | bytes 589832 | tf_op jit(solution)/shard_map/ppermute | solution.py:319
  30.7 6.8 %collective-permute-start.12 = (bf16[32,1536]{1,0:T(8,128)(2,1)S(1)}, bf16[32,1536]{1,0:T(8,128)(2,1)S(1)}, u32[]{:S(2)}, u32[]{:S(2)}) collective-permute-start(bf16[32,1536]{1,0:T(8,128)(2,1)S(1)} %get-tuple-element.69.refs_0_), channel_id=1, source_target_pairs={{0,8},{1,9},{2,10},{3,11},{8,0},{9,1},{10,2},{11,3},{16,24},{17,25... | collective-permute-start | bytes 294920 | tf_op jit(solution)/shard_map/ppermute | solution.py:338
  32.2 7.0 %collective-permute-start.13 = (bf16[32,1536]{1,0:T(8,128)(2,1)S(1)}, bf16[32,1536]{1,0:T(8,128)(2,1)S(1)}, u32[]{:S(2)}, u32[]{:S(2)}) collective-permute-start(bf16[32,1536]{1,0:T(8,128)(2,1)S(1)} %get-tuple-element.70.refs_1_), channel_id=1, source_target_pairs={{0,10},{1,11},{2,8},{3,9},{8,2},{9,3},{10,0},{11,1},{16,26},{17,27... | collective-permute-start | bytes 294920 | tf_op jit(solution)/shard_map/ppermute | solution.py:338
  34.1 7.5 %collective-permute-start.18 = (bf16[32,1536]{1,0:T(8,128)(2,1)S(1)}, bf16[32,1536]{1,0:T(8,128)(2,1)S(1)}, u32[]{:S(2)}, u32[]{:S(2)}) collective-permute-start(bf16[32,1536]{1,0:T(8,128)(2,1)S(1)} %get-tuple-element.74.refs_0_), channel_id=1, source_target_pairs={{0,8},{1,9},{2,10},{3,11},{8,0},{9,1},{10,2},{11,3},{16,24},{17,25... | collective-permute-start | bytes 294920 | tf_op jit(solution)/shard_map/ppermute | solution.py:338
  35.6 7.4 %collective-permute-start.19 = (bf16[32,1536]{1,0:T(8,128)(2,1)S(1)}, bf16[32,1536]{1,0:T(8,128)(2,1)S(1)}, u32[]{:S(2)}, u32[]{:S(2)}) collective-permute-start(bf16[32,1536]{1,0:T(8,128)(2,1)S(1)} %get-tuple-element.75.refs_1_), channel_id=1, source_target_pairs={{0,10},{1,11},{2,8},{3,9},{8,2},{9,3},{10,0},{11,1},{16,26},{17,27... | collective-permute-start | bytes 294920 | tf_op jit(solution)/shard_map/ppermute | solution.py:338
  39.2 4.7 %collective-permute-start.17 = (bf16[32,1536]{1,0:T(8,128)(2,1)S(1)}, bf16[32,1536]{1,0:T(8,128)(2,1)S(1)}, u32[]{:S(2)}, u32[]{:S(2)}) collective-permute-start(bf16[32,1536]{1,0:T(8,128)(2,1)S(1)} %get-tuple-element.107), channel_id=1, source_target_pairs={{0,4},{4,0},{1,5},{5,1},{2,6},{6,2},{3,7},{7,3},{8,12},{12,8},{9,1... | collective-permute-start | bytes 294920 | tf_op jit(solution)/shard_map/ppermute | solution.py:316
  40.8 4.6 %collective-permute-start.14 = (bf16[32,1536]{1,0:T(8,128)(2,1)S(1)}, bf16[32,1536]{1,0:T(8,128)(2,1)S(1)}, u32[]{:S(2)}, u32[]{:S(2)}) collective-permute-start(bf16[32,1536]{1,0:T(8,128)(2,1)S(1)} %get-tuple-element.108.refs_2_.addend_ref), channel_id=1, source_target_pairs={{0,2},{2,0},{1,3},{3,1},{4,6},{6,4},{5,7},{7,5},{8,10},{10,8},{9,1... | collective-permute-start | bytes 294920 | tf_op jit(solution)/shard_map/ppermute | solution.py:322
  44.0 4.7 %collective-permute-start.20 = (bf16[32,1536]{1,0:T(8,128)(2,1)S(1)}, bf16[32,1536]{1,0:T(8,128)(2,1)S(1)}, u32[]{:S(2)}, u32[]{:S(2)}) collective-permute-start(bf16[32,1536]{1,0:T(8,128)(2,1)S(1)} %fusion.1.refs_2_.addend_ref), channel_id=1, source_target_pairs={{0,2},{2,0},{1,3},{3,1},{4,6},{6,4},{5,7},{7,5},{8,10},{10,8},{9,1... | collective-permute-start | bytes 294920 | tf_op jit(solution)/shard_map/ppermute | solution.py:322
  44.9 3.8 %collective-permute-start.15 = (bf16[32,1536]{1,0:T(8,128)(2,1)S(1)}, bf16[32,1536]{1,0:T(8,128)(2,1)S(1)}, u32[]{:S(2)}, u32[]{:S(2)}) collective-permute-start(bf16[32,1536]{1,0:T(8,128)(2,1)S(1)} %get-tuple-element.108.refs_2_.addend_ref), channel_id=1, source_target_pairs={{0,1},{1,0},{2,3},{3,2},{4,5},{5,4},{6,7},{7,6},{8,9},{9,8},{10,11... | collective-permute-start | bytes 294920 | tf_op jit(solution)/shard_map/ppermute | solution.py:319
  45.4 3.2 %collective-permute-start.16 = (bf16[32,1536]{1,0:T(8,128)(2,1)S(1)}, bf16[32,1536]{1,0:T(8,128)(2,1)S(1)}, u32[]{:S(2)}, u32[]{:S(2)}) collective-permute-start(bf16[32,1536]{1,0:T(8,128)(2,1)S(1)} %collective-permute-done.14.refs_3_), channel_id=1, source_target_pairs={{0,1},{1,0},{2,3},{3,2},{4,5},{5,4},{6,7},{7,6},{8,9},{9,8},{10,11... | collective-permute-start | bytes 294920 | tf_op jit(solution)/shard_map/ppermute | solution.py:319
  45.4 6.2 %collective-permute-start.21 = (bf16[32,1536]{1,0:T(8,128)(2,1)S(1)}, bf16[32,1536]{1,0:T(8,128)(2,1)S(1)}, u32[]{:S(2)}, u32[]{:S(2)}) collective-permute-start(bf16[32,1536]{1,0:T(8,128)(2,1)S(1)} %fusion.1.refs_2_.addend_ref), channel_id=1, source_target_pairs={{0,1},{1,0},{2,3},{3,2},{4,5},{5,4},{6,7},{7,6},{8,9},{9,8},{10,11... | collective-permute-start | bytes 294920 | tf_op jit(solution)/shard_map/ppermute | solution.py:319
  48.7 3.0 %collective-permute-start.22 = (bf16[32,1536]{1,0:T(8,128)(2,1)S(1)}, bf16[32,1536]{1,0:T(8,128)(2,1)S(1)}, u32[]{:S(2)}, u32[]{:S(2)}) collective-permute-start(bf16[32,1536]{1,0:T(8,128)(2,1)S(1)} %collective-permute-done.20.refs_3_), channel_id=1, source_target_pairs={{0,1},{1,0},{2,3},{3,2},{4,5},{5,4},{6,7},{7,6},{8,9},{9,8},{10,11... | collective-permute-start | bytes 294920 | tf_op jit(solution)/shard_map/ppermute | solution.py:319
  50.1 7.8 %collective-permute-start.24 = (bf16[768,128]{1,0:T(8,128)(2,1)S(1)}, bf16[768,128]{1,0:T(8,128)(2,1)S(1)}, u32[]{:S(2)}, u32[]{:S(2)}) collective-permute-start(bf16[768,128]{1,0:T(8,128)(2,1)S(1)} %get-tuple-element.78.mine_ref), channel_id=1, source_target_pairs={{0,4},{4,0},{1,5},{5,1},{2,6},{6,2},{3,7},{7,3},{8,12},{12,8},{9,1... | collective-permute-start | bytes 589832 | tf_op jit(solution)/shard_map/ppermute | solution.py:316
  53.1 8.6 %collective-permute-start.23 = (bf16[768,128]{1,0:T(8,128)(2,1)S(1)}, bf16[768,128]{1,0:T(8,128)(2,1)S(1)}, u32[]{:S(2)}, u32[]{:S(2)}) collective-permute-start(bf16[768,128]{1,0:T(8,128)(2,1)S(1)} %get-tuple-element.79.mine_ref), channel_id=1, source_target_pairs={{0,4},{4,0},{1,5},{5,1},{2,6},{6,2},{3,7},{7,3},{8,12},{12,8},{9,1... | collective-permute-start | bytes 589832 | tf_op jit(solution)/shard_map/ppermute | solution.py:316
  59.3 3.9 %collective-permute-start.25 = (bf16[2,32,1536]{2,1,0:T(8,128)(2,1)S(1)}, bf16[2,32,1536]{2,1,0:T(8,128)(2,1)S(1)}, u32[]{:S(2)}, u32[]{:S(2)}) collective-permute-start(bf16[2,32,1536]{2,1,0:T(8,128)(2,1)S(1)} %get-tuple-element.82), channel_id=1, source_target_pairs={{0,1},{1,0},{2,3},{3,2},{4,5},{5,4},{6,7},{7,6},{8,9},{9,8},{10,11... | collective-permute-start | bytes 589832 | tf_op jit(solution)/shard_map/ppermute | solution.py:319
  63.0 3.1 %collective-permute-start.26 = (bf16[2,32,1536]{2,1,0:T(8,128)(2,1)S(1)}, bf16[2,32,1536]{2,1,0:T(8,128)(2,1)S(1)}, u32[]{:S(2)}, u32[]{:S(2)}) collective-permute-start(bf16[2,32,1536]{2,1,0:T(8,128)(2,1)S(1)} %get-tuple-element.86), channel_id=1, source_target_pairs={{0,1},{1,0},{2,3},{3,2},{4,5},{5,4},{6,7},{7,6},{8,9},{9,8},{10,11... | collective-permute-start | bytes 589832 | tf_op jit(solution)/shard_map/ppermute | solution.py:319
  63.8 8.3 %collective-permute-start.28 = (bf16[32,1536]{1,0:T(8,128)(2,1)S(1)}, bf16[32,1536]{1,0:T(8,128)(2,1)S(1)}, u32[]{:S(2)}, u32[]{:S(2)}) collective-permute-start(bf16[32,1536]{1,0:T(8,128)(2,1)S(1)} %get-tuple-element.83), channel_id=1, source_target_pairs={{0,4},{1,5},{2,6},{3,7},{4,0},{5,1},{6,2},{7,3},{8,12},{9,13},{10,... | collective-permute-start | bytes 294920 | tf_op jit(solution)/shard_map/ppermute | solution.py:330
  65.3 6.7 %collective-permute-start.29 = (bf16[32,1536]{1,0:T(8,128)(2,1)S(1)}, bf16[32,1536]{1,0:T(8,128)(2,1)S(1)}, u32[]{:S(2)}, u32[]{:S(2)}) collective-permute-start(bf16[32,1536]{1,0:T(8,128)(2,1)S(1)} %get-tuple-element.84), channel_id=1, source_target_pairs={{0,6},{1,7},{2,4},{3,5},{4,2},{5,3},{6,0},{7,1},{8,14},{9,15},{10,... | collective-permute-start | bytes 294920 | tf_op jit(solution)/shard_map/ppermute | solution.py:330
  66.8 6.7 %collective-permute-start.27 = (bf16[32,1536]{1,0:T(8,128)(2,1)S(1)}, bf16[32,1536]{1,0:T(8,128)(2,1)S(1)}, u32[]{:S(2)}, u32[]{:S(2)}) collective-permute-start(bf16[32,1536]{1,0:T(8,128)(2,1)S(1)} %get-tuple-element.88), channel_id=1, source_target_pairs={{0,2},{2,0},{1,3},{3,1},{4,6},{6,4},{5,7},{7,5},{8,10},{10,8},{9,1... | collective-permute-start | bytes 294920 | tf_op jit(solution)/shard_map/ppermute | solution.py:322
  (1 other events, 3.6 us)

commit v12 on v11

--- a/solution.py
+++ b/solution.py
@@ -366,8 +366,10 @@
     other_note = other_probs
     late_value, late_out, _ = lax.optimization_barrier((w_value, w_out, own_probs))
     first_table = load_first(facts, late_value, late_out)
-    swapped, _ = lax.optimization_barrier((first_mine, first_table))
-    first_theirs = [[swap_core(piece) for piece in pieces] for pieces in swapped]
+    first_theirs = []
+    for pieces in first_mine:
+        later, _ = lax.optimization_barrier((pieces, first_table))
+        first_theirs.append([swap_core(piece) for piece in later])
 
     probs = [own_probs, other_probs]
     partial, first_full = [None, None], [None, None]
@@ -391,7 +393,10 @@
     later_out, _ = lax.optimization_barrier((w_out, first_sent))
     out_table = load_table(later_out, OUT_VMEM_BYTES)
     later_input, _ = lax.optimization_barrier((section_input[0], out_table))
-    input_piece = [own_columns(later_input), swap_half(other_columns(later_input))]
+    input_own, input_sent = lax.optimization_barrier(
+        (own_columns(later_input), other_columns(later_input))
+    )
+    input_piece = [input_own, swap_half(input_sent)]
     for m in range(2):
         received = [swap_section(part, d) for d, part in enumerate(first_sent[m])]
         second_piece[m] = jnp.where(odd, input_piece[m], total(received).astype(jnp.bfloat16))

time: 74.3 us -> 72.6 us (0.977)
  waiting for transfers between devices: 21.2 us -> 19.4 us
    ppermute x5, waiting for transfers between devices: 6.13 us -> 4.55 us  [to_row(): return lax.ppermute(array, 'outer', [(i, i ^ delta) for i in range(outer)])]
    ppermute x7, waiting for transfers between devices: 11.4 us -> 10.4 us  [swap_half(): return lax.ppermute(array, 'half', [(0, 1), (1, 0)])]
where the time goes in v12:
time: 72.6 us; the launch traced here: 72.4 us
  Pallas kernels  25.1 us (35%)
  starting transfers between devices  23.3 us (32%)
  waiting for transfers between devices  19.4 us (27%)
  other arithmetic  2.94 us (4%)
  between operations  1.55 us (2%)
    ppermute x7, waiting for transfers between devices, swap_half(): return lax.ppermute(array, 'half', [(0, 1), (1, 0)])  10.4 us
    ppermute x7, starting transfers between devices, swap_half(): return lax.ppermute(array, 'half', [(0, 1), (1, 0)])  8.95 us
    pallas_call x4, Pallas kernels, mix(): pl.pallas_call(functools.partial(mix_kernel, outer, natural, index), out_...  5.84 us
    pallas_call x4, Pallas kernels, project(): pl.pallas_call(functools.partial(project_kernel, index, outer, shard, len...  5.54 us
    ppermute x4, starting transfers between devices, swap_section(): return lax.ppermute(array, ('pair', 'outer', 'core'), pairs)  5.08 us
    ppermute x5, waiting for transfers between devices, to_row(): return lax.ppermute(array, 'outer', [(i, i ^ delta) for i in range(outer)])  4.55 us
    ppermute x5, starting transfers between devices, to_row(): return lax.ppermute(array, 'outer', [(i, i ^ delta) for i in range(outer)])  4.5 us
    pallas_call x1, Pallas kernels, weight_grads(): pl.pallas_call(weight_grad_kernel, grid=(CHUNKS,), out_shape=(grad, grad)...  4.05 us
  transfers between devices with their start and end apart: 30, of which 15 were waited for; matrix products, arithmetic and copies ran while one was open for 2% of the time, Pallas kernels for 34%

profile of v12, /device:TPU:0, one launch (start us, length us, event | category | flops | bytes accessed | tf_op | source)
XLA Modules:
  0.0 72.4 jit_solution(13054074361568274)
XLA Ops:
  0.6 1.0 %bitcast_select_fusion = bf16[32,3072]{1,0:T(8,128)(2,1)S(1)} fusion(bf16[1,32,3072]{2,1,0:T(8,128)(2,1)} %param.10, pred[]{:T(512)S(6)} %eq.10, bf16[1,32,3072]{2,1,0:T(8,128)(2,1)} %param.7), kind=kLoop, calls=%fused_computation.2 | loop fusion | flops 98304 | bytes 589825 | tf_op jit(solution)/shard_map/jit(_where)/select_n | solution.py:356
  1.7 3.0 %collective-permute-start.1 = (bf16[32,1536]{1,0:T(8,128)(2,1)S(1)}, bf16[32,1536]{1,0:T(8,128)(2,1)S(1)}, u32[]{:S(2)}, u32[]{:S(2)}) collective-permute-start(bf16[32,1536]{1,0:T(8,128)(2,1)S(1)} %get-tuple-element.113), channel_id=1, source_target_pairs={{0,4},{4,0},{1,5},{5,1},{2,6},{6,2},{3,7},{7,3},{8,12},{12,8},{9,1... | collective-permute-start | bytes 294920 | tf_op jit(solution)/shard_map/ppermute | solution.py:316
  4.7 1.1 %pad_maximum_fusion.stash_ref = bf16[2,768,128]{2,1,0:T(8,128)(2,1)S(1)} fusion(bf16[1,768,128]{2,1,0:T(8,128)(2,1)} %param.9, bf16[1,768,128]{2,1,0:T(8,128)(2,1)} %param.8), kind=kLoop, calls=%fused_computation | loop fusion | flops 196608 | bytes 786432 | tf_op jit(solution)/shard_map/concatenate | solution.py:362
  7.5 1.9 %collective-permute-start.3 = (bf16[32,1536]{1,0:T(8,128)(2,1)S(1)}, bf16[32,1536]{1,0:T(8,128)(2,1)S(1)}, u32[]{:S(2)}, u32[]{:S(2)}) collective-permute-start(bf16[32,1536]{1,0:T(8,128)(2,1)S(1)} %collective-permute-done.1.refs_1_.addend_ref), channel_id=1, source_target_pairs={{0,2},{2,0},{1,3},{3,1},{4,6},{6,4},{5,7},{7,5},{8,10},{10,8},{9,1... | collective-permute-start | bytes 294920 | tf_op jit(solution)/shard_map/ppermute | solution.py:322
  9.6 2.9 %load_first.1.refs_0_ = bf16[1,2,768,1536]{3,2,1,0:T(8,128)(2,1)S(1)} custom-call(s32[6]{0:T(128)S(1)} %stack.23.facts_ref, bf16[1,2,768,1536]{3,2,1,0:T(8,128)(2,1)} %source_ref, bf16[1,2,768,1536]{3,2,1,0:T(8,128)(2,1)} %source_ref.1), custom_call_target="tpu_custom_call" | custom-call | flops 1 | bytes 1 | tf_op jit(solution)/shard_map/load_first/pallas_call | solution.py:279
  15.1 1.4 %project.4 = (bf16[768,128]{1,0:T(8,128)(2,1)S(1)}, bf16[128,1536]{1,0:T(8,128)(2,1)S(1)}) custom-call(s32[6]{0:T(128)S(1)} %stack.23.facts_ref, bf16[1040,128]{1,0:T(8,128)(2,1)S(1)} %collective-permute-done.note_ref.probs_ref, bf16[1,2,768,1536]{3,2,1,0:T(8,128)(2,1)S(1)} %load_first.1.refs_0_, ...), custom_call_target="tpu_custom_call" | custom-call | flops 1 | bytes 1 | tf_op jit(solution)/shard_map/project/pallas_call | solution.py:86
  17.6 1.3 %project.5 = (bf16[768,128]{1,0:T(8,128)(2,1)S(1)}, bf16[128,1536]{1,0:T(8,128)(2,1)S(1)}) custom-call(s32[6]{0:T(128)S(1)} %stack.23.facts_ref, bf16[1040,128]{1,0:T(8,128)(2,1)S(1)} %collective-permute-done.note_ref.probs_ref, bf16[1,2,768,1536]{3,2,1,0:T(8,128)(2,1)S(1)} %load_first.1.refs_0_, bf16[32,1536]{1,0:T(8,128)(2,1)S(1)} %get-tuple-element.64.refs_1_.addend_ref, ...), custom_call_target="tpu_custom_call" | custom-call | flops 1 | bytes 1 | tf_op jit(solution)/shard_map/project/pallas_call | solution.py:86
  18.9 1.1 %collective-permute-start.10 = (bf16[768,128]{1,0:T(8,128)(2,1)S(1)}, bf16[768,128]{1,0:T(8,128)(2,1)S(1)}, u32[]{:S(2)}, u32[]{:S(2)}) collective-permute-start(bf16[768,128]{1,0:T(8,128)(2,1)S(1)} %get-tuple-element.66.mine_ref), channel_id=1, source_target_pairs={{0,4},{4,0},{1,5},{5,1},{2,6},{6,2},{3,7},{7,3},{8,12},{12,8},{9,1... | collective-permute-start | bytes 589832 | tf_op jit(solution)/shard_map/ppermute | solution.py:316
  20.0 2.5 %load_table.2.value_ref.refs_0_ = bf16[1,2,768,1536]{3,2,1,0:T(8,128)(2,1)S(1)} custom-call(bf16[1,2,768,1536]{3,2,1,0:T(8,128)(2,1)} %source_ref), custom_call_target="tpu_custom_call" | custom-call | flops 1 | bytes 1 | tf_op jit(solution)/shard_map/load_table/pallas_call | solution.py:292
  22.6 1.8 %collective-permute-done.8.arrived_ref = bf16[768,128]{1,0:T(8,128)(2,1)S(1)} collective-permute-done((bf16[768,128]{1,0:T(8,128)(2,1)S(1)}, bf16[768,128]{1,0:T(8,128)(2,1)S(1)}, u32[]{:S(2)}, u32[]{:S(2)}) %collective-permute-start.8) | collective-permute-done | bytes 196640 | tf_op jit(solution)/shard_map/ppermute | solution.py:316
  24.4 1.5 %mix.4 = (bf16[768,128]{1,0:T(8,128)(2,1)S(1)}, bf16[2,32,1536]{2,1,0:T(8,128)(2,1)S(1)}, bf16[2,32,1536]{2,1,0:T(8,128)(2,1)S(1)}) custom-call(s32[6]{0:T(128)S(1)} %stack.23.facts_ref, bf16[1040,128]{1,0:T(8,128)(2,1)S(1)} %collective-permute-done.note_ref.probs_ref, bf16[1,2,768,1536]{3,2,1,0:T(8,128)(2,1)S(1)} %load_table.2.value_ref.refs_0_, ...), custom_call_target="tpu_custom_call" | custom-call | flops 1 | bytes 1 | tf_op jit(solution)/shard_map/mix/pallas_call | solution.py:146
  26.0 1.4 %collective-permute-done.10.arrived_ref = bf16[768,128]{1,0:T(8,128)(2,1)S(1)} collective-permute-done((bf16[768,128]{1,0:T(8,128)(2,1)S(1)}, bf16[768,128]{1,0:T(8,128)(2,1)S(1)}, u32[]{:S(2)}, u32[]{:S(2)}) %collective-permute-start.10) | collective-permute-done | bytes 196640 | tf_op jit(solution)/shard_map/ppermute | solution.py:316
  27.3 1.6 %mix.5 = (bf16[768,128]{1,0:T(8,128)(2,1)S(1)}, bf16[2,32,1536]{2,1,0:T(8,128)(2,1)S(1)}, bf16[2,32,1536]{2,1,0:T(8,128)(2,1)S(1)}) custom-call(s32[6]{0:T(128)S(1)} %stack.23.facts_ref, bf16[1040,128]{1,0:T(8,128)(2,1)S(1)} %collective-permute-done.note_ref.probs_ref, bf16[1,2,768,1536]{3,2,1,0:T(8,128)(2,1)S(1)} %load_table.2.value_ref.refs_0_, ...), custom_call_target="tpu_custom_call" | custom-call | flops 1 | bytes 1 | tf_op jit(solution)/shard_map/mix/pallas_call | solution.py:146
  29.6 1.5 %collective-permute-start.12 = (bf16[32,1536]{1,0:T(8,128)(2,1)S(1)}, bf16[32,1536]{1,0:T(8,128)(2,1)S(1)}, u32[]{:S(2)}, u32[]{:S(2)}) collective-permute-start(bf16[32,1536]{1,0:T(8,128)(2,1)S(1)} %get-tuple-element.71.refs_0_), channel_id=1, source_target_pairs={{0,8},{1,9},{2,10},{3,11},{8,0},{9,1},{10,2},{11,3},{16,24},{17,25... | collective-permute-start | bytes 294920 | tf_op jit(solution)/shard_map/ppermute | solution.py:338
  31.1 1.5 %collective-permute-start.13 = (bf16[32,1536]{1,0:T(8,128)(2,1)S(1)}, bf16[32,1536]{1,0:T(8,128)(2,1)S(1)}, u32[]{:S(2)}, u32[]{:S(2)}) collective-permute-start(bf16[32,1536]{1,0:T(8,128)(2,1)S(1)} %get-tuple-element.72.refs_1_), channel_id=1, source_target_pairs={{0,10},{1,11},{2,8},{3,9},{8,2},{9,3},{10,0},{11,1},{16,26},{17,27... | collective-permute-start | bytes 294920 | tf_op jit(solution)/shard_map/ppermute | solution.py:338
  33.2 1.5 %collective-permute-start.18 = (bf16[32,1536]{1,0:T(8,128)(2,1)S(1)}, bf16[32,1536]{1,0:T(8,128)(2,1)S(1)}, u32[]{:S(2)}, u32[]{:S(2)}) collective-permute-start(bf16[32,1536]{1,0:T(8,128)(2,1)S(1)} %get-tuple-element.76.refs_0_), channel_id=1, source_target_pairs={{0,8},{1,9},{2,10},{3,11},{8,0},{9,1},{10,2},{11,3},{16,24},{17,25... | collective-permute-start | bytes 294920 | tf_op jit(solution)/shard_map/ppermute | solution.py:338
  35.3 1.0 %load_table.3.refs_1_ = bf16[1,2,768,1536]{3,2,1,0:T(8,128)(2,1)S(1)} custom-call(bf16[1,2,768,1536]{3,2,1,0:T(8,128)(2,1)S(1)} %bitcast.13), custom_call_target="tpu_custom_call" | custom-call | flops 1 | bytes 1 | tf_op jit(solution)/shard_map/load_table/pallas_call | solution.py:292
  36.4 1.6 %collective-permute-start.17 = (bf16[32,1536]{1,0:T(8,128)(2,1)S(1)}, bf16[32,1536]{1,0:T(8,128)(2,1)S(1)}, u32[]{:S(2)}, u32[]{:S(2)}) collective-permute-start(bf16[32,1536]{1,0:T(8,128)(2,1)S(1)} %get-tuple-element.82), channel_id=1, source_target_pairs={{0,4},{4,0},{1,5},{5,1},{2,6},{6,2},{3,7},{7,3},{8,12},{12,8},{9,1... | collective-permute-start | bytes 294920 | tf_op jit(solution)/shard_map/ppermute | solution.py:316
  38.3 1.2 %collective-permute-start.14 = (bf16[32,1536]{1,0:T(8,128)(2,1)S(1)}, bf16[32,1536]{1,0:T(8,128)(2,1)S(1)}, u32[]{:S(2)}, u32[]{:S(2)}) collective-permute-start(bf16[32,1536]{1,0:T(8,128)(2,1)S(1)} %fusion.refs_2_.addend_ref), channel_id=1, source_target_pairs={{0,2},{2,0},{1,3},{3,1},{4,6},{6,4},{5,7},{7,5},{8,10},{10,8},{9,1... | collective-permute-start | bytes 294920 | tf_op jit(solution)/shard_map/ppermute | solution.py:322
  39.8 2.4 %collective-permute-done.19 = bf16[32,1536]{1,0:T(8,128)(2,1)S(1)} collective-permute-done((bf16[32,1536]{1,0:T(8,128)(2,1)S(1)}, bf16[32,1536]{1,0:T(8,128)(2,1)S(1)}, u32[]{:S(2)}, u32[]{:S(2)}) %collective-permute-start.19) | collective-permute-done | bytes 98336 | tf_op jit(solution)/shard_map/ppermute | solution.py:338
  42.9 1.3 %collective-permute-done.14.refs_3_ = bf16[32,1536]{1,0:T(8,128)(2,1)S(1)} collective-permute-done((bf16[32,1536]{1,0:T(8,128)(2,1)S(1)}, bf16[32,1536]{1,0:T(8,128)(2,1)S(1)}, u32[]{:S(2)}, u32[]{:S(2)}) %collective-permute-start.14) | collective-permute-done | bytes 98336 | tf_op jit(solution)/shard_map/ppermute | solution.py:322
  44.7 2.3 %collective-permute-done.20.refs_3_ = bf16[32,1536]{1,0:T(8,128)(2,1)S(1)} collective-permute-done((bf16[32,1536]{1,0:T(8,128)(2,1)S(1)}, bf16[32,1536]{1,0:T(8,128)(2,1)S(1)}, u32[]{:S(2)}, u32[]{:S(2)}) %collective-permute-start.20) | collective-permute-done | bytes 98336 | tf_op jit(solution)/shard_map/ppermute | solution.py:322
  46.9 1.4 %project.6 = (bf16[768,128]{1,0:T(8,128)(2,1)S(1)}, bf16[128,1536]{1,0:T(8,128)(2,1)S(1)}) custom-call(s32[6]{0:T(128)S(1)} %stack.23.facts_ref, bf16[1040,128]{1,0:T(8,128)(2,1)S(1)} %collective-permute-done.note_ref.probs_ref, bf16[1,2,768,1536]{3,2,1,0:T(8,128)(2,1)S(1)} %load_table.2.value_ref.refs_0_, bf16[1,2,768,1536]{3,2,1,0:T(8,128)(2,1)S(1)} %load_table.3.refs_1_, ...), custom_call_target="tpu_custom_call" | custom-call | flops 1 | bytes 1 | tf_op jit(solution)/shard_map/project/pallas_call | solution.py:86
  48.3 1.6 %collective-permute-start.24 = (bf16[768,128]{1,0:T(8,128)(2,1)S(1)}, bf16[768,128]{1,0:T(8,128)(2,1)S(1)}, u32[]{:S(2)}, u32[]{:S(2)}) collective-permute-start(bf16[768,128]{1,0:T(8,128)(2,1)S(1)} %get-tuple-element.81.mine_ref), channel_id=1, source_target_pairs={{0,4},{4,0},{1,5},{5,1},{2,6},{6,2},{3,7},{7,3},{8,12},{12,8},{9,1... | collective-permute-start | bytes 589832 | tf_op jit(solution)/shard_map/ppermute | solution.py:316
  49.9 1.4 %project.7 = (bf16[768,128]{1,0:T(8,128)(2,1)S(1)}, bf16[128,1536]{1,0:T(8,128)(2,1)S(1)}) custom-call(s32[6]{0:T(128)S(1)} %stack.23.facts_ref, bf16[1040,128]{1,0:T(8,128)(2,1)S(1)} %collective-permute-done.note_ref.probs_ref, bf16[1,2,768,1536]{3,2,1,0:T(8,128)(2,1)S(1)} %load_table.2.value_ref.refs_0_, bf16[1,2,768,1536]{3,2,1,0:T(8,128)(2,1)S(1)} %load_table.3.refs_1_, ...), custom_call_target="tpu_custom_call" | custom-call | flops 1 | bytes 1 | tf_op jit(solution)/shard_map/project/pallas_call | solution.py:86
  51.9 4.2 %collective-permute-done.24.arrived_ref = bf16[768,128]{1,0:T(8,128)(2,1)S(1)} collective-permute-done((bf16[768,128]{1,0:T(8,128)(2,1)S(1)}, bf16[768,128]{1,0:T(8,128)(2,1)S(1)}, u32[]{:S(2)}, u32[]{:S(2)}) %collective-permute-start.24) | collective-permute-done | bytes 196640 | tf_op jit(solution)/shard_map/ppermute | solution.py:316
  56.1 1.4 %mix.7 = (bf16[768,128]{1,0:T(8,128)(2,1)S(1)}, bf16[2,32,1536]{2,1,0:T(8,128)(2,1)S(1)}, bf16[2,32,1536]{2,1,0:T(8,128)(2,1)S(1)}) custom-call(s32[6]{0:T(128)S(1)} %stack.23.facts_ref, bf16[1040,128]{1,0:T(8,128)(2,1)S(1)} %collective-permute-done.note_ref.probs_ref, bf16[1,2,768,1536]{3,2,1,0:T(8,128)(2,1)S(1)} %load_table.2.value_ref.refs_0_, ...), custom_call_target="tpu_custom_call" | custom-call | flops 1 | bytes 1 | tf_op jit(solution)/shard_map/mix/pallas_call | solution.py:146
  57.6 2.3 %collective-permute-done.23.arrived_ref = bf16[768,128]{1,0:T(8,128)(2,1)S(1)} collective-permute-done((bf16[768,128]{1,0:T(8,128)(2,1)S(1)}, bf16[768,128]{1,0:T(8,128)(2,1)S(1)}, u32[]{:S(2)}, u32[]{:S(2)}) %collective-permute-start.23) | collective-permute-done | bytes 196640 | tf_op jit(solution)/shard_map/ppermute | solution.py:316
  59.9 1.4 %mix.6 = (bf16[768,128]{1,0:T(8,128)(2,1)S(1)}, bf16[2,32,1536]{2,1,0:T(8,128)(2,1)S(1)}, bf16[2,32,1536]{2,1,0:T(8,128)(2,1)S(1)}) custom-call(s32[6]{0:T(128)S(1)} %stack.23.facts_ref, bf16[1040,128]{1,0:T(8,128)(2,1)S(1)} %collective-permute-done.note_ref.probs_ref, bf16[1,2,768,1536]{3,2,1,0:T(8,128)(2,1)S(1)} %load_table.2.value_ref.refs_0_, ...), custom_call_target="tpu_custom_call" | custom-call | flops 1 | bytes 1 | tf_op jit(solution)/shard_map/mix/pallas_call | solution.py:146
  64.1 1.5 %collective-permute-start.28 = (bf16[32,1536]{1,0:T(8,128)(2,1)S(1)}, bf16[32,1536]{1,0:T(8,128)(2,1)S(1)}, u32[]{:S(2)}, u32[]{:S(2)}) collective-permute-start(bf16[32,1536]{1,0:T(8,128)(2,1)S(1)} %get-tuple-element.87), channel_id=1, source_target_pairs={{0,4},{1,5},{2,6},{3,7},{4,0},{5,1},{6,2},{7,3},{8,12},{9,13},{10,... | collective-permute-start | bytes 294920 | tf_op jit(solution)/shard_map/ppermute | solution.py:330
  65.6 1.4 %collective-permute-start.29 = (bf16[32,1536]{1,0:T(8,128)(2,1)S(1)}, bf16[32,1536]{1,0:T(8,128)(2,1)S(1)}, u32[]{:S(2)}, u32[]{:S(2)}) collective-permute-start(bf16[32,1536]{1,0:T(8,128)(2,1)S(1)} %get-tuple-element.88), channel_id=1, source_target_pairs={{0,6},{1,7},{2,4},{3,5},{4,2},{5,3},{6,0},{7,1},{8,14},{9,15},{10,... | collective-permute-start | bytes 294920 | tf_op jit(solution)/shard_map/ppermute | solution.py:330
  67.0 4.1 %weight_grads.1 = (bf16[1,768,1536]{2,1,0:T(8,128)(2,1)}, bf16[1,768,1536]{2,1,0:T(8,128)(2,1)}) custom-call(s32[6]{0:T(128)S(1)} %stack.23.facts_ref, bf16[768,128]{1,0:T(8,128)(2,1)S(1)} %get-tuple-element.93.a0, bf16[768,128]{1,0:T(8,128)(2,1)S(1)} %get-tuple-element.94.a1, bf16[768,128]{1,0:T(8,128)(2,1)S(1)} %get-tuple-element.97.b0, ...), custom_call_target="tpu_custom_call" | custom-call | flops 1 | bytes 1 | tf_op jit(solution)/shard_map/weight_grads/pallas_call | solution.py:206
  (62 shorter events, 13.5 us)
Async XLA Ops:
  1.7 5.8 %collective-permute-start.1 = (bf16[32,1536]{1,0:T(8,128)(2,1)S(1)}, bf16[32,1536]{1,0:T(8,128)(2,1)S(1)}, u32[]{:S(2)}, u32[]{:S(2)}) collective-permute-start(bf16[32,1536]{1,0:T(8,128)(2,1)S(1)} %get-tuple-element.113), channel_id=1, source_target_pairs={{0,4},{4,0},{1,5},{5,1},{2,6},{6,2},{3,7},{7,3},{8,12},{12,8},{9,1... | collective-permute-start | bytes 294920 | tf_op jit(solution)/shard_map/ppermute | solution.py:316
  7.2 7.9 %collective-permute-start = (bf16[1040,128]{1,0:T(8,128)(2,1)S(1)}, bf16[1040,128]{1,0:T(8,128)(2,1)S(1)}, u32[]{:S(2)}, u32[]{:S(2)}) collective-permute-start(bf16[1040,128]{1,0:T(8,128)(2,1)S(1)} %concatenate.10.probs_ref), channel_id=1, source_target_pairs={{0,4},{4,0},{1,5},{5,1},{2,6},{6,2},{3,7},{7,3},{8,12},{12,8},{9,1... | collective-permute-start | bytes 798728 | tf_op jit(solution)/shard_map/ppermute | solution.py:316
  7.5 5.5 %collective-permute-start.3 = (bf16[32,1536]{1,0:T(8,128)(2,1)S(1)}, bf16[32,1536]{1,0:T(8,128)(2,1)S(1)}, u32[]{:S(2)}, u32[]{:S(2)}) collective-permute-start(bf16[32,1536]{1,0:T(8,128)(2,1)S(1)} %collective-permute-done.1.refs_1_.addend_ref), channel_id=1, source_target_pairs={{0,2},{2,0},{1,3},{3,1},{4,6},{6,4},{5,7},{7,5},{8,10},{10,8},{9,1... | collective-permute-start | bytes 294920 | tf_op jit(solution)/shard_map/ppermute | solution.py:322
  9.4 4.7 %collective-permute-start.2 = (bf16[32,1536]{1,0:T(8,128)(2,1)S(1)}, bf16[32,1536]{1,0:T(8,128)(2,1)S(1)}, u32[]{:S(2)}, u32[]{:S(2)}) collective-permute-start(bf16[32,1536]{1,0:T(8,128)(2,1)S(1)} %get-tuple-element.64.refs_1_.addend_ref), channel_id=1, source_target_pairs={{0,2},{2,0},{1,3},{3,1},{4,6},{6,4},{5,7},{7,5},{8,10},{10,8},{9,1... | collective-permute-start | bytes 294920 | tf_op jit(solution)/shard_map/ppermute | solution.py:322
  13.0 2.1 %collective-permute-start.4 = (bf16[32,1536]{1,0:T(8,128)(2,1)S(1)}, bf16[32,1536]{1,0:T(8,128)(2,1)S(1)}, u32[]{:S(2)}, u32[]{:S(2)}) collective-permute-start(bf16[32,1536]{1,0:T(8,128)(2,1)S(1)} %collective-permute-done.1.refs_1_.addend_ref), channel_id=1, source_target_pairs={{0,1},{1,0},{2,3},{3,2},{4,5},{5,4},{6,7},{7,6},{8,9},{9,8},{10,11... | collective-permute-start | bytes 294920 | tf_op jit(solution)/shard_map/ppermute | solution.py:319
  13.0 2.1 %collective-permute-start.5 = (bf16[32,1536]{1,0:T(8,128)(2,1)S(1)}, bf16[32,1536]{1,0:T(8,128)(2,1)S(1)}, u32[]{:S(2)}, u32[]{:S(2)}) collective-permute-start(bf16[32,1536]{1,0:T(8,128)(2,1)S(1)} %collective-permute-done.3.refs_2_), channel_id=1, source_target_pairs={{0,1},{1,0},{2,3},{3,2},{4,5},{5,4},{6,7},{7,6},{8,9},{9,8},{10,11... | collective-permute-start | bytes 294920 | tf_op jit(solution)/shard_map/ppermute | solution.py:319
  14.1 3.5 %collective-permute-start.6 = (bf16[32,1536]{1,0:T(8,128)(2,1)S(1)}, bf16[32,1536]{1,0:T(8,128)(2,1)S(1)}, u32[]{:S(2)}, u32[]{:S(2)}) collective-permute-start(bf16[32,1536]{1,0:T(8,128)(2,1)S(1)} %get-tuple-element.64.refs_1_.addend_ref), channel_id=1, source_target_pairs={{0,1},{1,0},{2,3},{3,2},{4,5},{5,4},{6,7},{7,6},{8,9},{9,8},{10,11... | collective-permute-start | bytes 294920 | tf_op jit(solution)/shard_map/ppermute | solution.py:319
  14.1 3.5 %collective-permute-start.7 = (bf16[32,1536]{1,0:T(8,128)(2,1)S(1)}, bf16[32,1536]{1,0:T(8,128)(2,1)S(1)}, u32[]{:S(2)}, u32[]{:S(2)}) collective-permute-start(bf16[32,1536]{1,0:T(8,128)(2,1)S(1)} %collective-permute-done.2.refs_2_), channel_id=1, source_target_pairs={{0,1},{1,0},{2,3},{3,2},{4,5},{5,4},{6,7},{7,6},{8,9},{9,8},{10,11... | collective-permute-start | bytes 294920 | tf_op jit(solution)/shard_map/ppermute | solution.py:319
  16.5 7.9 %collective-permute-start.8 = (bf16[768,128]{1,0:T(8,128)(2,1)S(1)}, bf16[768,128]{1,0:T(8,128)(2,1)S(1)}, u32[]{:S(2)}, u32[]{:S(2)}) collective-permute-start(bf16[768,128]{1,0:T(8,128)(2,1)S(1)} %get-tuple-element.61.mine_ref), channel_id=1, source_target_pairs={{0,4},{4,0},{1,5},{5,1},{2,6},{6,2},{3,7},{7,3},{8,12},{12,8},{9,1... | collective-permute-start | bytes 589832 | tf_op jit(solution)/shard_map/ppermute | solution.py:316
  18.9 8.4 %collective-permute-start.10 = (bf16[768,128]{1,0:T(8,128)(2,1)S(1)}, bf16[768,128]{1,0:T(8,128)(2,1)S(1)}, u32[]{:S(2)}, u32[]{:S(2)}) collective-permute-start(bf16[768,128]{1,0:T(8,128)(2,1)S(1)} %get-tuple-element.66.mine_ref), channel_id=1, source_target_pairs={{0,4},{4,0},{1,5},{5,1},{2,6},{6,2},{3,7},{7,3},{8,12},{12,8},{9,1... | collective-permute-start | bytes 589832 | tf_op jit(solution)/shard_map/ppermute | solution.py:316
  20.0 15.3 %slice-start = ((s8[4718592]{0:T(1024)(128)(4,1)}), s8[4194304]{0:T(1024)(128)(4,1)S(1)}, s32[]{:S(2)}) async-start(s8[4718592]{0:T(1024)(128)(4,1)} %bitcast.12), calls=%async_computation | async-start | bytes 8388608
  22.6 12.7 %slice-start.1 = ((s8[4718592]{0:T(1024)(128)(4,1)}), s8[524288]{0:T(1024)(128)(4,1)S(1)}, s32[]{:S(2)}) async-start(s8[4718592]{0:T(1024)(128)(4,1)} %bitcast.12), calls=%async_computation.1 | async-start | bytes 1048576
  25.9 3.1 %collective-permute-start.9 = (bf16[2,32,1536]{2,1,0:T(8,128)(2,1)S(1)}, bf16[2,32,1536]{2,1,0:T(8,128)(2,1)S(1)}, u32[]{:S(2)}, u32[]{:S(2)}) collective-permute-start(bf16[2,32,1536]{2,1,0:T(8,128)(2,1)S(1)} %get-tuple-element.70), channel_id=1, source_target_pairs={{0,1},{1,0},{2,3},{3,2},{4,5},{5,4},{6,7},{7,6},{8,9},{9,8},{10,11... | collective-permute-start | bytes 589832 | tf_op jit(solution)/shard_map/ppermute | solution.py:319
  28.9 3.7 %collective-permute-start.11 = (bf16[2,32,1536]{2,1,0:T(8,128)(2,1)S(1)}, bf16[2,32,1536]{2,1,0:T(8,128)(2,1)S(1)}, u32[]{:S(2)}, u32[]{:S(2)}) collective-permute-start(bf16[2,32,1536]{2,1,0:T(8,128)(2,1)S(1)} %get-tuple-element.75), channel_id=1, source_target_pairs={{0,1},{1,0},{2,3},{3,2},{4,5},{5,4},{6,7},{7,6},{8,9},{9,8},{10,11... | collective-permute-start | bytes 589832 | tf_op jit(solution)/shard_map/ppermute | solution.py:319
  29.6 8.4 %collective-permute-start.12 = (bf16[32,1536]{1,0:T(8,128)(2,1)S(1)}, bf16[32,1536]{1,0:T(8,128)(2,1)S(1)}, u32[]{:S(2)}, u32[]{:S(2)}) collective-permute-start(bf16[32,1536]{1,0:T(8,128)(2,1)S(1)} %get-tuple-element.71.refs_0_), channel_id=1, source_target_pairs={{0,8},{1,9},{2,10},{3,11},{8,0},{9,1},{10,2},{11,3},{16,24},{17,25... | collective-permute-start | bytes 294920 | tf_op jit(solution)/shard_map/ppermute | solution.py:338
  31.1 7.1 %collective-permute-start.13 = (bf16[32,1536]{1,0:T(8,128)(2,1)S(1)}, bf16[32,1536]{1,0:T(8,128)(2,1)S(1)}, u32[]{:S(2)}, u32[]{:S(2)}) collective-permute-start(bf16[32,1536]{1,0:T(8,128)(2,1)S(1)} %get-tuple-element.72.refs_1_), channel_id=1, source_target_pairs={{0,10},{1,11},{2,8},{3,9},{8,2},{9,3},{10,0},{11,1},{16,26},{17,27... | collective-permute-start | bytes 294920 | tf_op jit(solution)/shard_map/ppermute | solution.py:338
  33.2 6.5 %collective-permute-start.18 = (bf16[32,1536]{1,0:T(8,128)(2,1)S(1)}, bf16[32,1536]{1,0:T(8,128)(2,1)S(1)}, u32[]{:S(2)}, u32[]{:S(2)}) collective-permute-start(bf16[32,1536]{1,0:T(8,128)(2,1)S(1)} %get-tuple-element.76.refs_0_), channel_id=1, source_target_pairs={{0,8},{1,9},{2,10},{3,11},{8,0},{9,1},{10,2},{11,3},{16,24},{17,25... | collective-permute-start | bytes 294920 | tf_op jit(solution)/shard_map/ppermute | solution.py:338
  34.7 7.5 %collective-permute-start.19 = (bf16[32,1536]{1,0:T(8,128)(2,1)S(1)}, bf16[32,1536]{1,0:T(8,128)(2,1)S(1)}, u32[]{:S(2)}, u32[]{:S(2)}) collective-permute-start(bf16[32,1536]{1,0:T(8,128)(2,1)S(1)} %get-tuple-element.77.refs_1_), channel_id=1, source_target_pairs={{0,10},{1,11},{2,8},{3,9},{8,2},{9,3},{10,0},{11,1},{16,26},{17,27... | collective-permute-start | bytes 294920 | tf_op jit(solution)/shard_map/ppermute | solution.py:338
  36.4 5.8 %collective-permute-start.17 = (bf16[32,1536]{1,0:T(8,128)(2,1)S(1)}, bf16[32,1536]{1,0:T(8,128)(2,1)S(1)}, u32[]{:S(2)}, u32[]{:S(2)}) collective-permute-start(bf16[32,1536]{1,0:T(8,128)(2,1)S(1)} %get-tuple-element.82), channel_id=1, source_target_pairs={{0,4},{4,0},{1,5},{5,1},{2,6},{6,2},{3,7},{7,3},{8,12},{12,8},{9,1... | collective-permute-start | bytes 294920 | tf_op jit(solution)/shard_map/ppermute | solution.py:316
  38.3 5.8 %collective-permute-start.14 = (bf16[32,1536]{1,0:T(8,128)(2,1)S(1)}, bf16[32,1536]{1,0:T(8,128)(2,1)S(1)}, u32[]{:S(2)}, u32[]{:S(2)}) collective-permute-start(bf16[32,1536]{1,0:T(8,128)(2,1)S(1)} %fusion.refs_2_.addend_ref), channel_id=1, source_target_pairs={{0,2},{2,0},{1,3},{3,1},{4,6},{6,4},{5,7},{7,5},{8,10},{10,8},{9,1... | collective-permute-start | bytes 294920 | tf_op jit(solution)/shard_map/ppermute | solution.py:322
  42.2 4.7 %collective-permute-start.20 = (bf16[32,1536]{1,0:T(8,128)(2,1)S(1)}, bf16[32,1536]{1,0:T(8,128)(2,1)S(1)}, u32[]{:S(2)}, u32[]{:S(2)}) collective-permute-start(bf16[32,1536]{1,0:T(8,128)(2,1)S(1)} %fusion.1.refs_2_.addend_ref), channel_id=1, source_target_pairs={{0,2},{2,0},{1,3},{3,1},{4,6},{6,4},{5,7},{7,5},{8,10},{10,8},{9,1... | collective-permute-start | bytes 294920 | tf_op jit(solution)/shard_map/ppermute | solution.py:322
  42.9 4.1 %collective-permute-start.15 = (bf16[32,1536]{1,0:T(8,128)(2,1)S(1)}, bf16[32,1536]{1,0:T(8,128)(2,1)S(1)}, u32[]{:S(2)}, u32[]{:S(2)}) collective-permute-start(bf16[32,1536]{1,0:T(8,128)(2,1)S(1)} %fusion.refs_2_.addend_ref), channel_id=1, source_target_pairs={{0,1},{1,0},{2,3},{3,2},{4,5},{5,4},{6,7},{7,6},{8,9},{9,8},{10,11... | collective-permute-start | bytes 294920 | tf_op jit(solution)/shard_map/ppermute | solution.py:319
  44.1 2.8 %collective-permute-start.16 = (bf16[32,1536]{1,0:T(8,128)(2,1)S(1)}, bf16[32,1536]{1,0:T(8,128)(2,1)S(1)}, u32[]{:S(2)}, u32[]{:S(2)}) collective-permute-start(bf16[32,1536]{1,0:T(8,128)(2,1)S(1)} %collective-permute-done.14.refs_3_), channel_id=1, source_target_pairs={{0,1},{1,0},{2,3},{3,2},{4,5},{5,4},{6,7},{7,6},{8,9},{9,8},{10,11... | collective-permute-start | bytes 294920 | tf_op jit(solution)/shard_map/ppermute | solution.py:319
  44.2 5.7 %collective-permute-start.21 = (bf16[32,1536]{1,0:T(8,128)(2,1)S(1)}, bf16[32,1536]{1,0:T(8,128)(2,1)S(1)}, u32[]{:S(2)}, u32[]{:S(2)}) collective-permute-start(bf16[32,1536]{1,0:T(8,128)(2,1)S(1)} %fusion.1.refs_2_.addend_ref), channel_id=1, source_target_pairs={{0,1},{1,0},{2,3},{3,2},{4,5},{5,4},{6,7},{7,6},{8,9},{9,8},{10,11... | collective-permute-start | bytes 294920 | tf_op jit(solution)/shard_map/ppermute | solution.py:319
  46.9 3.0 %collective-permute-start.22 = (bf16[32,1536]{1,0:T(8,128)(2,1)S(1)}, bf16[32,1536]{1,0:T(8,128)(2,1)S(1)}, u32[]{:S(2)}, u32[]{:S(2)}) collective-permute-start(bf16[32,1536]{1,0:T(8,128)(2,1)S(1)} %collective-permute-done.20.refs_3_), channel_id=1, source_target_pairs={{0,1},{1,0},{2,3},{3,2},{4,5},{5,4},{6,7},{7,6},{8,9},{9,8},{10,11... | collective-permute-start | bytes 294920 | tf_op jit(solution)/shard_map/ppermute | solution.py:319
  48.3 7.8 %collective-permute-start.24 = (bf16[768,128]{1,0:T(8,128)(2,1)S(1)}, bf16[768,128]{1,0:T(8,128)(2,1)S(1)}, u32[]{:S(2)}, u32[]{:S(2)}) collective-permute-start(bf16[768,128]{1,0:T(8,128)(2,1)S(1)} %get-tuple-element.81.mine_ref), channel_id=1, source_target_pairs={{0,4},{4,0},{1,5},{5,1},{2,6},{6,2},{3,7},{7,3},{8,12},{12,8},{9,1... | collective-permute-start | bytes 589832 | tf_op jit(solution)/shard_map/ppermute | solution.py:316
  51.3 8.6 %collective-permute-start.23 = (bf16[768,128]{1,0:T(8,128)(2,1)S(1)}, bf16[768,128]{1,0:T(8,128)(2,1)S(1)}, u32[]{:S(2)}, u32[]{:S(2)}) collective-permute-start(bf16[768,128]{1,0:T(8,128)(2,1)S(1)} %get-tuple-element.83.mine_ref), channel_id=1, source_target_pairs={{0,4},{4,0},{1,5},{5,1},{2,6},{6,2},{3,7},{7,3},{8,12},{12,8},{9,1... | collective-permute-start | bytes 589832 | tf_op jit(solution)/shard_map/ppermute | solution.py:316
  57.5 3.9 %collective-permute-start.25 = (bf16[2,32,1536]{2,1,0:T(8,128)(2,1)S(1)}, bf16[2,32,1536]{2,1,0:T(8,128)(2,1)S(1)}, u32[]{:S(2)}, u32[]{:S(2)}) collective-permute-start(bf16[2,32,1536]{2,1,0:T(8,128)(2,1)S(1)} %get-tuple-element.86), channel_id=1, source_target_pairs={{0,1},{1,0},{2,3},{3,2},{4,5},{5,4},{6,7},{7,6},{8,9},{9,8},{10,11... | collective-permute-start | bytes 589832 | tf_op jit(solution)/shard_map/ppermute | solution.py:319
  61.3 1.5 %collective-permute-start.26 = (bf16[2,32,1536]{2,1,0:T(8,128)(2,1)S(1)}, bf16[2,32,1536]{2,1,0:T(8,128)(2,1)S(1)}, u32[]{:S(2)}, u32[]{:S(2)}) collective-permute-start(bf16[2,32,1536]{2,1,0:T(8,128)(2,1)S(1)} %get-tuple-element.90), channel_id=1, source_target_pairs={{0,1},{1,0},{2,3},{3,2},{4,5},{5,4},{6,7},{7,6},{8,9},{9,8},{10,11... | collective-permute-start | bytes 589832 | tf_op jit(solution)/shard_map/ppermute | solution.py:319
  63.4 7.6 %collective-permute-start.27 = (bf16[32,1536]{1,0:T(8,128)(2,1)S(1)}, bf16[32,1536]{1,0:T(8,128)(2,1)S(1)}, u32[]{:S(2)}, u32[]{:S(2)}) collective-permute-start(bf16[32,1536]{1,0:T(8,128)(2,1)S(1)} %get-tuple-element.92), channel_id=1, source_target_pairs={{0,2},{2,0},{1,3},{3,1},{4,6},{6,4},{5,7},{7,5},{8,10},{10,8},{9,1... | collective-permute-start | bytes 294920 | tf_op jit(solution)/shard_map/ppermute | solution.py:322
  64.1 7.0 %collective-permute-start.28 = (bf16[32,1536]{1,0:T(8,128)(2,1)S(1)}, bf16[32,1536]{1,0:T(8,128)(2,1)S(1)}, u32[]{:S(2)}, u32[]{:S(2)}) collective-permute-start(bf16[32,1536]{1,0:T(8,128)(2,1)S(1)} %get-tuple-element.87), channel_id=1, source_target_pairs={{0,4},{1,5},{2,6},{3,7},{4,0},{5,1},{6,2},{7,3},{8,12},{9,13},{10,... | collective-permute-start | bytes 294920 | tf_op jit(solution)/shard_map/ppermute | solution.py:330
  65.6 6.1 %collective-permute-start.29 = (bf16[32,1536]{1,0:T(8,128)(2,1)S(1)}, bf16[32,1536]{1,0:T(8,128)(2,1)S(1)}, u32[]{:S(2)}, u32[]{:S(2)}) collective-permute-start(bf16[32,1536]{1,0:T(8,128)(2,1)S(1)} %get-tuple-element.88), channel_id=1, source_target_pairs={{0,6},{1,7},{2,4},{3,5},{4,2},{5,3},{6,0},{7,1},{8,14},{9,15},{10,... | collective-permute-start | bytes 294920 | tf_op jit(solution)/shard_map/ppermute | solution.py:330
  (1 other events, 1.7 us)

commit v13 on v12

--- a/solution.py
+++ b/solution.py
@@ -15,7 +15,6 @@
 FIRST_VMEM_BYTES = 46 * 2**20
 VALUE_VMEM_BYTES = 47 * 2**20
 OUT_VMEM_BYTES = 42 * 2**20
-ODD, EVEN, VERSION, CORE, ROW, HALF = range(6)
 LANES = 128
 NOTE_ROWS = 16
 SMALL = pl.CostEstimate(flops=1, bytes_accessed=1, transcendentals=0)
@@ -32,10 +31,6 @@
     return pl.BlockSpec(memory_space=pltpu.VMEM)
 
 
-def in_smem():
-    return pl.BlockSpec(memory_space=pltpu.SMEM)
-
-
 def in_hbm():
     return pl.BlockSpec(memory_space=pltpu.HBM)
 
@@ -44,22 +39,24 @@
     return pl.BlockSpec(memory_space=pl.ANY)
 
 
-def picked_version(index, facts_ref, note_ref):
-    if index == 0:
-        return facts_ref[VERSION]
-    note = note_ref[note_ref.shape[0] - NOTE_ROWS :, :]
+def is_odd():
+    return (lax.axis_index("pair") & 1) == 1
+
+
+def noted_version(message_ref):
+    note = message_ref[message_ref.shape[0] - NOTE_ROWS :, :]
     return (jnp.max(note.astype(jnp.float32)) > 0.5).astype(jnp.int32)
 
 
-def project_kernel(index, outer, shard, n_tables, facts_ref, note_ref, *refs):
+def project_kernel(outer, shard, n_tables, message_ref, *refs):
     table_refs, piece_refs = refs[:n_tables], refs[n_tables:-2]
     partial_ref, full_ref = refs[-2:]
-    version = picked_version(index, facts_ref, note_ref)
-    first_core = facts_ref[CORE] == 0
+    version = noted_version(message_ref)
+    first_core = lax.axis_index("core") == 0
     mine = [ref[:shard, :] for ref in piece_refs[:outer]]
     theirs = [ref[:shard, :] for ref in piece_refs[outer:]]
     for place in range(outer):
-        offset = facts_ref[ROW] ^ place
+        offset = lax.axis_index("outer") ^ place
         own, other = mine[0], theirs[0]
         for delta in range(1, outer):
             own = jnp.where(offset == delta, mine[delta], own)
@@ -75,43 +72,40 @@
     if n_tables == 1:
         rows_of(table_refs[0])
     else:
-        pl.when(facts_ref[ODD] == 1)(lambda: rows_of(table_refs[0]))
-        pl.when(facts_ref[ODD] == 0)(lambda: rows_of(table_refs[1]))
-
-
-def project(index, shard, facts, note, tables, mine, theirs):
+        pl.when(is_odd())(lambda: rows_of(table_refs[0]))
+        pl.when(jnp.logical_not(is_odd()))(lambda: rows_of(table_refs[1]))
+
+
+def project(shard, message, tables, mine, theirs):
     outer = len(mine)
     rows, width = tables[0].shape[2:]
     tokens = 2 * outer * shard
     return pl.pallas_call(
-        functools.partial(project_kernel, index, outer, shard, len(tables)),
+        functools.partial(project_kernel, outer, shard, len(tables)),
         out_shape=(
             jax.ShapeDtypeStruct((rows, tokens), jnp.bfloat16),
             jax.ShapeDtypeStruct((tokens, width), jnp.bfloat16),
         ),
-        in_specs=[in_smem()] + [in_vmem()] * (1 + len(tables) + 2 * outer),
+        in_specs=[in_vmem()] * (1 + len(tables) + 2 * outer),
         out_specs=(in_vmem(), in_vmem()),
         compiler_params=pltpu.CompilerParams(vmem_limit_bytes=VMEM_BYTES),
         cost_estimate=SMALL,
         name="project",
-    )(facts, note, *tables, *mine, *theirs)
+    )(message, *tables, *mine, *theirs)
 
 
 def mix_kernel(
     outer,
-    natural,
-    index,
-    facts_ref,
-    note_ref,
+    odd_phase,
+    message_ref,
     value_ref,
     mine_ref,
     arrived_ref,
-    probs_ref,
     result_ref,
     keep_ref,
     send_ref,
 ):
-    version = picked_version(index, facts_ref, note_ref)
+    version = noted_version(message_ref)
     step = value_ref.shape[3] // CHUNKS
     tokens = mine_ref.shape[1]
 
@@ -119,15 +113,16 @@
         for head in range(mine_ref.shape[0] // HEAD_DIM):
             rows = pl.ds(head * HEAD_DIM, HEAD_DIM)
             total = mine_ref[rows, :].astype(jnp.float32) + arrived_ref[rows, :].astype(jnp.float32)
-            probs = probs_ref[head * tokens : (head + 1) * tokens, :]
+            probs = message_ref[head * tokens : (head + 1) * tokens, :]
             mixed = matmul(total.astype(jnp.bfloat16), probs, dims)
             result_ref[rows, :] = mixed.astype(jnp.bfloat16)
 
-    pl.when(facts_ref[natural] == 1)(lambda: heads(NN))
-    pl.when(facts_ref[natural] == 0)(lambda: heads(NT))
+    natural = is_odd() == odd_phase
+    pl.when(natural)(lambda: heads(NN))
+    pl.when(jnp.logical_not(natural))(lambda: heads(NT))
 
     flipped = result_ref[...].T
-    second_core = facts_ref[CORE] == 1
+    second_core = lax.axis_index("core") == 1
     shard = tokens // (2 * outer)
     for chunk in range(CHUNKS):
         columns = pl.ds(chunk * step, step)
@@ -139,52 +134,52 @@
             send_ref[place, :, columns] = jnp.where(second_core, low, high).astype(jnp.bfloat16)
 
 
-def mix(natural, index, facts, note, message, w_value, mine, arrived, outer):
+def mix(odd_phase, message, w_value, mine, arrived, outer):
     rows, width = w_value.shape[2:]
     tokens = mine.shape[1]
     half = jax.ShapeDtypeStruct((outer, tokens // (2 * outer), width), jnp.bfloat16)
     return pl.pallas_call(
-        functools.partial(mix_kernel, outer, natural, index),
+        functools.partial(mix_kernel, outer, odd_phase),
         out_shape=(jax.ShapeDtypeStruct((rows, tokens), jnp.bfloat16), half, half),
-        in_specs=[in_smem()] + [in_vmem()] * 5,
+        in_specs=[in_vmem()] * 4,
         out_specs=(in_vmem(), in_vmem(), in_vmem()),
         compiler_params=pltpu.CompilerParams(vmem_limit_bytes=VMEM_BYTES),
         cost_estimate=SMALL,
         name="mix",
-    )(facts, note, w_value, mine, arrived, message)
-
-
-def combine_kernel(outer, last, facts_ref, keep_ref, arrived_ref, addend_ref, *refs):
+    )(message, w_value, mine, arrived)
+
+
+def combine_kernel(outer, last, keep_ref, arrived_ref, addend_ref, *refs):
     first_refs, sent_refs = refs[:-outer], refs[-outer:]
     for delta in range(outer):
-        spot = facts_ref[ROW] ^ delta
+        spot = lax.axis_index("outer") ^ delta
         total = keep_ref[spot].astype(jnp.float32) + arrived_ref[spot].astype(jnp.float32)
         if delta == 0:
             total = total + addend_ref[: total.shape[0], :].astype(jnp.float32)
         total = total.astype(jnp.bfloat16)
         if last:
-            total = jnp.where(facts_ref[ODD] == 1, first_refs[delta][...], total)
+            total = jnp.where(is_odd(), first_refs[delta][...], total)
         sent_refs[delta][...] = total
 
 
-def combine(facts, keep, arrived, addend, first_sent=()):
+def combine(keep, arrived, addend, first_sent=()):
     outer, shard, width = keep.shape
     piece = jax.ShapeDtypeStruct((shard, width), jnp.bfloat16)
     return pl.pallas_call(
         functools.partial(combine_kernel, outer, len(first_sent) > 0),
         out_shape=(piece,) * outer,
-        in_specs=[in_smem()] + [in_vmem()] * (3 + len(first_sent)),
+        in_specs=[in_vmem()] * (3 + len(first_sent)),
         out_specs=(in_vmem(),) * outer,
         compiler_params=pltpu.CompilerParams(vmem_limit_bytes=VMEM_BYTES),
         cost_estimate=SMALL,
         name="combine",
-    )(facts, keep, arrived, addend, *first_sent)
+    )(keep, arrived, addend, *first_sent)
 
 
 def weight_grad_kernel(
-    facts_ref, a0, a1, b0, b1, first0, first1, second0, second1, value_ref, out_ref
+    a0, a1, b0, b1, first0, first1, second0, second1, value_ref, out_ref
 ):
-    odd = facts_ref[ODD] == 1
+    odd = is_odd()
     left_first = jnp.concatenate([a0[...], a1[...]], axis=1)
     left_second = jnp.concatenate([b0[...], b1[...]], axis=1)
     right_second = jnp.concatenate([second0[...], second1[...]], axis=0)
@@ -195,7 +190,7 @@
     out_ref[0] = jnp.where(odd, grad_second, grad_first).astype(jnp.bfloat16)
 
 
-def weight_grads(facts, first_results, second_results, first_full, second_full):
+def weight_grads(first_results, second_results, first_full, second_full):
     rows, tokens = first_results[0].shape
     width = first_full[0].shape[1]
     step = rows // CHUNKS
@@ -207,12 +202,12 @@
         weight_grad_kernel,
         grid=(CHUNKS,),
         out_shape=(grad, grad),
-        in_specs=[in_smem()] + [left] * 4 + [single] * 4,
+        in_specs=[left] * 4 + [single] * 4,
         out_specs=(wide, wide),
         compiler_params=pltpu.CompilerParams(vmem_limit_bytes=GRAD_VMEM_BYTES),
         cost_estimate=SMALL,
         name="weight_grads",
-    )(facts, *first_results, *second_results, *first_full, *second_full)
+    )(*first_results, *second_results, *first_full, *second_full)
 
 
 def load(source_ref, table_ref, sems):
@@ -264,28 +259,28 @@
         copy.wait()
 
 
-def load_first_kernel(facts_ref, value_ref, out_ref, table_ref, sems):
+def load_first_kernel(value_ref, out_ref, table_ref, sems):
     def start(source_ref):
         for copy in load(source_ref, table_ref, sems):
             copy.start()
 
-    pl.when(facts_ref[ODD] == 1)(lambda: start(out_ref))
-    pl.when(facts_ref[ODD] == 0)(lambda: start(value_ref))
+    pl.when(is_odd())(lambda: start(out_ref))
+    pl.when(jnp.logical_not(is_odd()))(lambda: start(value_ref))
     for copy in load(value_ref, table_ref, sems):
         copy.wait()
 
 
-def load_first(facts, w_value, w_out):
+def load_first(w_value, w_out):
     return pl.pallas_call(
         load_first_kernel,
         out_shape=jax.ShapeDtypeStruct(w_value.shape, jnp.bfloat16),
-        in_specs=[in_smem(), in_hbm(), in_hbm()],
+        in_specs=[in_hbm(), in_hbm()],
         out_specs=in_vmem(),
         scratch_shapes=[pltpu.SemaphoreType.DMA((2 * CHUNKS,))],
         compiler_params=pltpu.CompilerParams(vmem_limit_bytes=FIRST_VMEM_BYTES),
         cost_estimate=SMALL,
         name="load_first",
-    )(facts, w_value, w_out)
+    )(w_value, w_out)
 
 
 def load_table(table, grant):
@@ -303,9 +298,7 @@
 
 def on_device(section_input, query, key_stash, incoming, version, w_value, w_out):
     half = lax.axis_index("half")
-    odd_flag = lax.axis_index("pair") % 2
-    odd = odd_flag == 1
-    core, row = lax.axis_index("core"), lax.axis_index("outer")
+    odd = is_odd()
     n_pairs = lax.axis_size("pair")
     outer = lax.axis_size("outer")
     n_tensor = 2 * outer
@@ -352,7 +345,6 @@
     def spread_rows(piece):
         return [piece] + [to_row(piece, delta) for delta in range(1, outer)]
 
-    facts = jnp.stack([odd_flag, 1 - odd_flag, version[0], core, row, half])
     first = jnp.where(odd, incoming[0], section_input[0])
     own_piece, sent_piece = own_columns(first), other_columns(first)
     other_piece = swap_half(sent_piece)
@@ -363,9 +355,8 @@
     note = jnp.full((NOTE_ROWS, LANES), version[0], jnp.int32).astype(jnp.bfloat16)
     own_probs = jnp.concatenate([own_probs, note])
     other_probs = swap_half(own_probs)
-    other_note = other_probs
     late_value, late_out, _ = lax.optimization_barrier((w_value, w_out, own_probs))
-    first_table = load_first(facts, late_value, late_out)
+    first_table = load_first(late_value, late_out)
     first_theirs = []
     for pieces in first_mine:
         later, _ = lax.optimization_barrier((pieces, first_table))
@@ -378,7 +369,7 @@
         if m == 0:
             mine, probs, _ = lax.optimization_barrier((mine, probs, partial[1]))
         partial[m], first_full[m] = project(
-            m, shard, facts, other_note, (first_table,), mine, first_theirs[m]
+            shard, probs[m], (first_table,), mine, first_theirs[m]
         )
     arrived = [swap_half(partial[1]), swap_half(partial[0])]
     later_value, _ = lax.optimization_barrier((w_value, partial))
@@ -387,9 +378,9 @@
     second_piece, second_full = [None, None], [None, None]
     for m in range(2):
         first_result[m], keep, send = mix(
-            ODD, m, facts, other_note, probs[m], value_table, partial[m], arrived[m], outer
+            True, probs[m], value_table, partial[m], arrived[m], outer
         )
-        first_sent[m] = combine(facts, keep, swap_core(send), first_piece[m])
+        first_sent[m] = combine(keep, swap_core(send), first_piece[m])
     later_out, _ = lax.optimization_barrier((w_out, first_sent))
     out_table = load_table(later_out, OUT_VMEM_BYTES)
     later_input, _ = lax.optimization_barrier((section_input[0], out_table))
@@ -404,22 +395,22 @@
         mine = spread_rows(second_piece[m])
         theirs = [swap_core(piece) for piece in mine]
         partial[m], second_full[m] = project(
-            m, shard, facts, other_note, (value_table, out_table), mine, theirs
+            shard, probs[m], (value_table, out_table), mine, theirs
         )
     arrived = [swap_half(partial[1]), swap_half(partial[0])]
     second_result, last_sent = [None, None], [None, None]
     for m in (1, 0):
         second_result[m], keep, send = mix(
-            EVEN, m, facts, other_note, probs[m], value_table, partial[m], arrived[m], outer
+            False, probs[m], value_table, partial[m], arrived[m], outer
         )
         if m == 0:
             keep, _ = lax.optimization_barrier((keep, last_sent[1]))
-        last_sent[m] = combine(facts, keep, swap_core(send), second_piece[m], first_sent[m])
+        last_sent[m] = combine(keep, swap_core(send), second_piece[m], first_sent[m])
     other_parts = [to_other_half(part, d) for d, part in enumerate(last_sent[1])]
     own_parts = [last_sent[0][0]] + [to_row(part, d + 1) for d, part in enumerate(last_sent[0][1:])]
     second_result, _ = lax.optimization_barrier((second_result, last_sent))
     grad_value, grad_out = weight_grads(
-        facts, first_result, second_result, first_full, second_full
+        first_result, second_result, first_full, second_full
     )
     own_parts, other_parts, _ = lax.optimization_barrier((own_parts, other_parts, grad_value))
     own_grad = total(own_parts).astype(jnp.bfloat16)

time: 72.6 us -> 69.3 us (0.955)
  Pallas kernels: 25.1 us -> 17.8 us
  waiting for transfers between devices: 19.4 us -> 23.7 us
    pallas_call x8, Pallas kernels: 11.4 us -> 7.31 us  [the longest x4 3.83 us: mix(): pl.pallas_call(functools.partial(mix_kernel, outer, odd_phase), out_shape...]
    pallas_call x4, Pallas kernels: 2.45 us -> 0.31 us  [combine(): pl.pallas_call(functools.partial(combine_kernel, outer, len(first_sent) >...]
    ppermute x7, waiting for transfers between devices: 10.4 us -> 12.4 us  [swap_half(): return lax.ppermute(array, 'half', [(0, 1), (1, 0)])]
  transfers between devices with their start and end apart: 30 -> 30, of which waited for: 15 -> 15; matrix products, arithmetic and copies ran while one was open for 2% -> 2% of each run, Pallas kernels for 34% -> 26%
where the time goes in v13:
time: 69.3 us; the launch traced here: 69.1 us
  waiting for transfers between devices  23.7 us (34%)
  starting transfers between devices  23.1 us (33%)
  Pallas kernels  17.8 us (26%)
  other arithmetic  2.93 us (4%)
  between operations  1.53 us (2%)
    ppermute x7, waiting for transfers between devices, swap_half(): return lax.ppermute(array, 'half', [(0, 1), (1, 0)])  12.4 us
    ppermute x7, starting transfers between devices, swap_half(): return lax.ppermute(array, 'half', [(0, 1), (1, 0)])  8.95 us
    ppermute x4, starting transfers between devices, swap_section(): return lax.ppermute(array, ('pair', 'outer', 'core'), pairs)  5.08 us
    ppermute x5, waiting for transfers between devices, to_row(): return lax.ppermute(array, 'outer', [(i, i ^ delta) for i in range(outer)])  5.05 us
    ppermute x5, starting transfers between devices, to_row(): return lax.ppermute(array, 'outer', [(i, i ^ delta) for i in range(outer)])  4.45 us
    pallas_call x4, Pallas kernels, mix(): pl.pallas_call(functools.partial(mix_kernel, outer, odd_phase), out_shape...  3.83 us
    ppermute x4, waiting for transfers between devices, swap_section(): return lax.ppermute(array, ('pair', 'outer', 'core'), pairs)  3.68 us
    pallas_call x2, Pallas kernels, load_table(): pl.pallas_call(load_kernel, out_shape=jax.ShapeDtypeStruct(table.shape, j...  3.57 us
  transfers between devices with their start and end apart: 30, of which 15 were waited for; matrix products, arithmetic and copies ran while one was open for 2% of the time, Pallas kernels for 26%

profile of v13, /device:TPU:0, one launch (start us, length us, event | category | flops | bytes accessed | tf_op | source)
XLA Modules:
  0.0 69.1 jit_solution(4050478835182482622)
XLA Ops:
  0.6 1.0 %bitcast_select_fusion = bf16[32,3072]{1,0:T(8,128)(2,1)S(1)} fusion(bf16[1,32,3072]{2,1,0:T(8,128)(2,1)} %param.10, pred[]{:T(512)S(6)} %eq.8, bf16[1,32,3072]{2,1,0:T(8,128)(2,1)} %param.7), kind=kLoop, calls=%fused_computation.2 | loop fusion | flops 98304 | bytes 589825 | tf_op jit(solution)/shard_map/jit(_where)/select_n | solution.py:348
  1.7 3.0 %collective-permute-start = (bf16[32,1536]{1,0:T(8,128)(2,1)S(1)}, bf16[32,1536]{1,0:T(8,128)(2,1)S(1)}, u32[]{:S(2)}, u32[]{:S(2)}) collective-permute-start(bf16[32,1536]{1,0:T(8,128)(2,1)S(1)} %get-tuple-element.113), channel_id=1, source_target_pairs={{0,4},{4,0},{1,5},{5,1},{2,6},{6,2},{3,7},{7,3},{8,12},{12,8},{9,1... | collective-permute-start | bytes 294920 | tf_op jit(solution)/shard_map/ppermute | solution.py:309
  4.7 1.1 %pad_maximum_fusion.stash_ref = bf16[2,768,128]{2,1,0:T(8,128)(2,1)S(1)} fusion(bf16[1,768,128]{2,1,0:T(8,128)(2,1)} %param.9, bf16[1,768,128]{2,1,0:T(8,128)(2,1)} %param.8), kind=kLoop, calls=%fused_computation | loop fusion | flops 196608 | bytes 786432 | tf_op jit(solution)/shard_map/concatenate | solution.py:354
  7.5 1.9 %collective-permute-start.3 = (bf16[32,1536]{1,0:T(8,128)(2,1)S(1)}, bf16[32,1536]{1,0:T(8,128)(2,1)S(1)}, u32[]{:S(2)}, u32[]{:S(2)}) collective-permute-start(bf16[32,1536]{1,0:T(8,128)(2,1)S(1)} %collective-permute-done.refs_1_.addend_ref), channel_id=1, source_target_pairs={{0,2},{2,0},{1,3},{3,1},{4,6},{6,4},{5,7},{7,5},{8,10},{10,8},{9,1... | collective-permute-start | bytes 294920 | tf_op jit(solution)/shard_map/ppermute | solution.py:315
  9.5 2.4 %load_first.1.refs_0_ = bf16[1,2,768,1536]{3,2,1,0:T(8,128)(2,1)S(1)} custom-call(bf16[1,2,768,1536]{3,2,1,0:T(8,128)(2,1)} %source_ref, bf16[1,2,768,1536]{3,2,1,0:T(8,128)(2,1)} %source_ref.1), custom_call_target="tpu_custom_call" | custom-call | flops 1 | bytes 1 | tf_op jit(solution)/shard_map/load_first/pallas_call | solution.py:274
  11.9 1.1 %collective-permute-done.3.refs_2_ = bf16[32,1536]{1,0:T(8,128)(2,1)S(1)} collective-permute-done((bf16[32,1536]{1,0:T(8,128)(2,1)S(1)}, bf16[32,1536]{1,0:T(8,128)(2,1)S(1)}, u32[]{:S(2)}, u32[]{:S(2)}) %collective-permute-start.3) | collective-permute-done | bytes 98336 | tf_op jit(solution)/shard_map/ppermute | solution.py:315
  16.0 1.0 %collective-permute-start.8 = (bf16[768,128]{1,0:T(8,128)(2,1)S(1)}, bf16[768,128]{1,0:T(8,128)(2,1)S(1)}, u32[]{:S(2)}, u32[]{:S(2)}) collective-permute-start(bf16[768,128]{1,0:T(8,128)(2,1)S(1)} %get-tuple-element.61.mine_ref), channel_id=1, source_target_pairs={{0,4},{4,0},{1,5},{5,1},{2,6},{6,2},{3,7},{7,3},{8,12},{12,8},{9,1... | collective-permute-start | bytes 589832 | tf_op jit(solution)/shard_map/ppermute | solution.py:309
  17.9 1.1 %collective-permute-start.10 = (bf16[768,128]{1,0:T(8,128)(2,1)S(1)}, bf16[768,128]{1,0:T(8,128)(2,1)S(1)}, u32[]{:S(2)}, u32[]{:S(2)}) collective-permute-start(bf16[768,128]{1,0:T(8,128)(2,1)S(1)} %get-tuple-element.67.mine_ref), channel_id=1, source_target_pairs={{0,4},{4,0},{1,5},{5,1},{2,6},{6,2},{3,7},{7,3},{8,12},{12,8},{9,1... | collective-permute-start | bytes 589832 | tf_op jit(solution)/shard_map/ppermute | solution.py:309
  19.0 2.5 %load_table.2.value_ref.refs_0_ = bf16[1,2,768,1536]{3,2,1,0:T(8,128)(2,1)S(1)} custom-call(bf16[1,2,768,1536]{3,2,1,0:T(8,128)(2,1)} %source_ref), custom_call_target="tpu_custom_call" | custom-call | flops 1 | bytes 1 | tf_op jit(solution)/shard_map/load_table/pallas_call | solution.py:287
  21.6 2.3 %collective-permute-done.8.arrived_ref = bf16[768,128]{1,0:T(8,128)(2,1)S(1)} collective-permute-done((bf16[768,128]{1,0:T(8,128)(2,1)S(1)}, bf16[768,128]{1,0:T(8,128)(2,1)S(1)}, u32[]{:S(2)}, u32[]{:S(2)}) %collective-permute-start.8) | collective-permute-done | bytes 196640 | tf_op jit(solution)/shard_map/ppermute | solution.py:309
  23.9 1.0 %mix.4 = (bf16[768,128]{1,0:T(8,128)(2,1)S(1)}, bf16[2,32,1536]{2,1,0:T(8,128)(2,1)S(1)}, bf16[2,32,1536]{2,1,0:T(8,128)(2,1)S(1)}) custom-call(bf16[1040,128]{1,0:T(8,128)(2,1)S(1)} %concatenate.10.message_ref, bf16[1,2,768,1536]{3,2,1,0:T(8,128)(2,1)S(1)} %load_table.2.value_ref.refs_0_, bf16[768,128]{1,0:T(8,128)(2,1)S(1)} %get-tuple-element.67.mine_ref, ...), custom_call_target="tpu_custom_call" | custom-call | flops 1 | bytes 1 | tf_op jit(solution)/shard_map/mix/pallas_call | solution.py:141
  25.0 1.8 %collective-permute-done.10.arrived_ref = bf16[768,128]{1,0:T(8,128)(2,1)S(1)} collective-permute-done((bf16[768,128]{1,0:T(8,128)(2,1)S(1)}, bf16[768,128]{1,0:T(8,128)(2,1)S(1)}, u32[]{:S(2)}, u32[]{:S(2)}) %collective-permute-start.10) | collective-permute-done | bytes 196640 | tf_op jit(solution)/shard_map/ppermute | solution.py:309
  26.8 1.0 %mix.5 = (bf16[768,128]{1,0:T(8,128)(2,1)S(1)}, bf16[2,32,1536]{2,1,0:T(8,128)(2,1)S(1)}, bf16[2,32,1536]{2,1,0:T(8,128)(2,1)S(1)}) custom-call(bf16[1040,128]{1,0:T(8,128)(2,1)S(1)} %collective-permute-done.2.message_ref, bf16[1,2,768,1536]{3,2,1,0:T(8,128)(2,1)S(1)} %load_table.2.value_ref.refs_0_, bf16[768,128]{1,0:T(8,128)(2,1)S(1)} %get-tuple-element.61.mine_ref, ...), custom_call_target="tpu_custom_call" | custom-call | flops 1 | bytes 1 | tf_op jit(solution)/shard_map/mix/pallas_call | solution.py:141
  28.0 1.5 %collective-permute-start.12 = (bf16[32,1536]{1,0:T(8,128)(2,1)S(1)}, bf16[32,1536]{1,0:T(8,128)(2,1)S(1)}, u32[]{:S(2)}, u32[]{:S(2)}) collective-permute-start(bf16[32,1536]{1,0:T(8,128)(2,1)S(1)} %get-tuple-element.71.refs_0_), channel_id=1, source_target_pairs={{0,8},{1,9},{2,10},{3,11},{8,0},{9,1},{10,2},{11,3},{16,24},{17,25... | collective-permute-start | bytes 294920 | tf_op jit(solution)/shard_map/ppermute | solution.py:331
  29.5 1.4 %collective-permute-start.13 = (bf16[32,1536]{1,0:T(8,128)(2,1)S(1)}, bf16[32,1536]{1,0:T(8,128)(2,1)S(1)}, u32[]{:S(2)}, u32[]{:S(2)}) collective-permute-start(bf16[32,1536]{1,0:T(8,128)(2,1)S(1)} %get-tuple-element.72.refs_1_), channel_id=1, source_target_pairs={{0,10},{1,11},{2,8},{3,9},{8,2},{9,3},{10,0},{11,1},{16,26},{17,27... | collective-permute-start | bytes 294920 | tf_op jit(solution)/shard_map/ppermute | solution.py:331
  30.9 1.5 %collective-permute-start.18 = (bf16[32,1536]{1,0:T(8,128)(2,1)S(1)}, bf16[32,1536]{1,0:T(8,128)(2,1)S(1)}, u32[]{:S(2)}, u32[]{:S(2)}) collective-permute-start(bf16[32,1536]{1,0:T(8,128)(2,1)S(1)} %get-tuple-element.76.refs_0_), channel_id=1, source_target_pairs={{0,8},{1,9},{2,10},{3,11},{8,0},{9,1},{10,2},{11,3},{16,24},{17,25... | collective-permute-start | bytes 294920 | tf_op jit(solution)/shard_map/ppermute | solution.py:331
  33.2 1.0 %load_table.3.refs_1_ = bf16[1,2,768,1536]{3,2,1,0:T(8,128)(2,1)S(1)} custom-call(bf16[1,2,768,1536]{3,2,1,0:T(8,128)(2,1)S(1)} %bitcast.8), custom_call_target="tpu_custom_call" | custom-call | flops 1 | bytes 1 | tf_op jit(solution)/shard_map/load_table/pallas_call | solution.py:287
  34.2 1.6 %collective-permute-start.17 = (bf16[32,1536]{1,0:T(8,128)(2,1)S(1)}, bf16[32,1536]{1,0:T(8,128)(2,1)S(1)}, u32[]{:S(2)}, u32[]{:S(2)}) collective-permute-start(bf16[32,1536]{1,0:T(8,128)(2,1)S(1)} %get-tuple-element.82), channel_id=1, source_target_pairs={{0,4},{4,0},{1,5},{5,1},{2,6},{6,2},{3,7},{7,3},{8,12},{12,8},{9,1... | collective-permute-start | bytes 294920 | tf_op jit(solution)/shard_map/ppermute | solution.py:309
  36.6 0.9 %collective-permute-start.14 = (bf16[32,1536]{1,0:T(8,128)(2,1)S(1)}, bf16[32,1536]{1,0:T(8,128)(2,1)S(1)}, u32[]{:S(2)}, u32[]{:S(2)}) collective-permute-start(bf16[32,1536]{1,0:T(8,128)(2,1)S(1)} %fusion.refs_2_.addend_ref), channel_id=1, source_target_pairs={{0,2},{2,0},{1,3},{3,1},{4,6},{6,4},{5,7},{7,5},{8,10},{10,8},{9,1... | collective-permute-start | bytes 294920 | tf_op jit(solution)/shard_map/ppermute | solution.py:315
  38.0 2.4 %collective-permute-done.19 = bf16[32,1536]{1,0:T(8,128)(2,1)S(1)} collective-permute-done((bf16[32,1536]{1,0:T(8,128)(2,1)S(1)}, bf16[32,1536]{1,0:T(8,128)(2,1)S(1)}, u32[]{:S(2)}, u32[]{:S(2)}) %collective-permute-start.19) | collective-permute-done | bytes 98336 | tf_op jit(solution)/shard_map/ppermute | solution.py:331
  41.2 1.1 %collective-permute-done.14.refs_3_ = bf16[32,1536]{1,0:T(8,128)(2,1)S(1)} collective-permute-done((bf16[32,1536]{1,0:T(8,128)(2,1)S(1)}, bf16[32,1536]{1,0:T(8,128)(2,1)S(1)}, u32[]{:S(2)}, u32[]{:S(2)}) %collective-permute-start.14) | collective-permute-done | bytes 98336 | tf_op jit(solution)/shard_map/ppermute | solution.py:315
  42.9 2.3 %collective-permute-done.20.refs_3_ = bf16[32,1536]{1,0:T(8,128)(2,1)S(1)} collective-permute-done((bf16[32,1536]{1,0:T(8,128)(2,1)S(1)}, bf16[32,1536]{1,0:T(8,128)(2,1)S(1)}, u32[]{:S(2)}, u32[]{:S(2)}) %collective-permute-start.20) | collective-permute-done | bytes 98336 | tf_op jit(solution)/shard_map/ppermute | solution.py:315
  45.2 0.9 %project.6 = (bf16[768,128]{1,0:T(8,128)(2,1)S(1)}, bf16[128,1536]{1,0:T(8,128)(2,1)S(1)}) custom-call(bf16[1040,128]{1,0:T(8,128)(2,1)S(1)} %concatenate.10.message_ref, bf16[1,2,768,1536]{3,2,1,0:T(8,128)(2,1)S(1)} %load_table.2.value_ref.refs_0_, bf16[1,2,768,1536]{3,2,1,0:T(8,128)(2,1)S(1)} %load_table.3.refs_1_, ...), custom_call_target="tpu_custom_call" | custom-call | flops 1 | bytes 1 | tf_op jit(solution)/shard_map/project/pallas_call | solution.py:83
  46.1 1.6 %collective-permute-start.24 = (bf16[768,128]{1,0:T(8,128)(2,1)S(1)}, bf16[768,128]{1,0:T(8,128)(2,1)S(1)}, u32[]{:S(2)}, u32[]{:S(2)}) collective-permute-start(bf16[768,128]{1,0:T(8,128)(2,1)S(1)} %get-tuple-element.81.mine_ref), channel_id=1, source_target_pairs={{0,4},{4,0},{1,5},{5,1},{2,6},{6,2},{3,7},{7,3},{8,12},{12,8},{9,1... | collective-permute-start | bytes 589832 | tf_op jit(solution)/shard_map/ppermute | solution.py:309
  49.1 4.7 %collective-permute-done.24.arrived_ref = bf16[768,128]{1,0:T(8,128)(2,1)S(1)} collective-permute-done((bf16[768,128]{1,0:T(8,128)(2,1)S(1)}, bf16[768,128]{1,0:T(8,128)(2,1)S(1)}, u32[]{:S(2)}, u32[]{:S(2)}) %collective-permute-start.24) | collective-permute-done | bytes 196640 | tf_op jit(solution)/shard_map/ppermute | solution.py:309
  54.8 2.9 %collective-permute-done.23.arrived_ref = bf16[768,128]{1,0:T(8,128)(2,1)S(1)} collective-permute-done((bf16[768,128]{1,0:T(8,128)(2,1)S(1)}, bf16[768,128]{1,0:T(8,128)(2,1)S(1)}, u32[]{:S(2)}, u32[]{:S(2)}) %collective-permute-start.23) | collective-permute-done | bytes 196640 | tf_op jit(solution)/shard_map/ppermute | solution.py:309
  57.7 0.9 %mix.6 = (bf16[768,128]{1,0:T(8,128)(2,1)S(1)}, bf16[2,32,1536]{2,1,0:T(8,128)(2,1)S(1)}, bf16[2,32,1536]{2,1,0:T(8,128)(2,1)S(1)}) custom-call(bf16[1040,128]{1,0:T(8,128)(2,1)S(1)} %concatenate.10.message_ref, bf16[1,2,768,1536]{3,2,1,0:T(8,128)(2,1)S(1)} %load_table.2.value_ref.refs_0_, bf16[768,128]{1,0:T(8,128)(2,1)S(1)} %get-tuple-element.81.mine_ref, ...), custom_call_target="tpu_custom_call" | custom-call | flops 1 | bytes 1 | tf_op jit(solution)/shard_map/mix/pallas_call | solution.py:141
  58.7 1.3 %collective-permute-done.26.arrived_ref = bf16[2,32,1536]{2,1,0:T(8,128)(2,1)S(1)} collective-permute-done((bf16[2,32,1536]{2,1,0:T(8,128)(2,1)S(1)}, bf16[2,32,1536]{2,1,0:T(8,128)(2,1)S(1)}, u32[]{:S(2)}, u32[]{:S(2)}) %collective-permute-start.26) | collective-permute-done | bytes 196640 | tf_op jit(solution)/shard_map/ppermute | solution.py:312
  60.9 1.5 %collective-permute-start.28 = (bf16[32,1536]{1,0:T(8,128)(2,1)S(1)}, bf16[32,1536]{1,0:T(8,128)(2,1)S(1)}, u32[]{:S(2)}, u32[]{:S(2)}) collective-permute-start(bf16[32,1536]{1,0:T(8,128)(2,1)S(1)} %get-tuple-element.87), channel_id=1, source_target_pairs={{0,4},{1,5},{2,6},{3,7},{4,0},{5,1},{6,2},{7,3},{8,12},{9,13},{10,... | collective-permute-start | bytes 294920 | tf_op jit(solution)/shard_map/ppermute | solution.py:323
  62.4 1.3 %collective-permute-start.29 = (bf16[32,1536]{1,0:T(8,128)(2,1)S(1)}, bf16[32,1536]{1,0:T(8,128)(2,1)S(1)}, u32[]{:S(2)}, u32[]{:S(2)}) collective-permute-start(bf16[32,1536]{1,0:T(8,128)(2,1)S(1)} %get-tuple-element.88), channel_id=1, source_target_pairs={{0,6},{1,7},{2,4},{3,5},{4,2},{5,3},{6,0},{7,1},{8,14},{9,15},{10,... | collective-permute-start | bytes 294920 | tf_op jit(solution)/shard_map/ppermute | solution.py:323
  63.7 3.5 %weight_grads.1 = (bf16[1,768,1536]{2,1,0:T(8,128)(2,1)}, bf16[1,768,1536]{2,1,0:T(8,128)(2,1)}) custom-call(bf16[768,128]{1,0:T(8,128)(2,1)S(1)} %get-tuple-element.93.a0, bf16[768,128]{1,0:T(8,128)(2,1)S(1)} %get-tuple-element.94.a1, bf16[768,128]{1,0:T(8,128)(2,1)S(1)} %get-tuple-element.97.b0, bf16[768,128]{1,0:T(8,128)(2,1)S(1)} %get-tuple-element.98.b1, ...), custom_call_target="tpu_custom_call" | custom-call | flops 1 | bytes 1 | tf_op jit(solution)/shard_map/weight_grads/pallas_call | solution.py:201
  67.2 1.2 %collective-permute-done.29 = bf16[32,1536]{1,0:T(8,128)(2,1)S(1)} collective-permute-done((bf16[32,1536]{1,0:T(8,128)(2,1)S(1)}, bf16[32,1536]{1,0:T(8,128)(2,1)S(1)}, u32[]{:S(2)}, u32[]{:S(2)}) %collective-permute-start.29) | collective-permute-done | bytes 98336 | tf_op jit(solution)/shard_map/ppermute | solution.py:323
  (61 shorter events, 12.9 us)
Async XLA Ops:
  1.7 5.8 %collective-permute-start = (bf16[32,1536]{1,0:T(8,128)(2,1)S(1)}, bf16[32,1536]{1,0:T(8,128)(2,1)S(1)}, u32[]{:S(2)}, u32[]{:S(2)}) collective-permute-start(bf16[32,1536]{1,0:T(8,128)(2,1)S(1)} %get-tuple-element.113), channel_id=1, source_target_pairs={{0,4},{4,0},{1,5},{5,1},{2,6},{6,2},{3,7},{7,3},{8,12},{12,8},{9,1... | collective-permute-start | bytes 294920 | tf_op jit(solution)/shard_map/ppermute | solution.py:309
  7.2 7.9 %collective-permute-start.2 = (bf16[1040,128]{1,0:T(8,128)(2,1)S(1)}, bf16[1040,128]{1,0:T(8,128)(2,1)S(1)}, u32[]{:S(2)}, u32[]{:S(2)}) collective-permute-start(bf16[1040,128]{1,0:T(8,128)(2,1)S(1)} %concatenate.10.message_ref), channel_id=1, source_target_pairs={{0,4},{4,0},{1,5},{5,1},{2,6},{6,2},{3,7},{7,3},{8,12},{12,8},{9,1... | collective-permute-start | bytes 798728 | tf_op jit(solution)/shard_map/ppermute | solution.py:309
  7.5 5.5 %collective-permute-start.3 = (bf16[32,1536]{1,0:T(8,128)(2,1)S(1)}, bf16[32,1536]{1,0:T(8,128)(2,1)S(1)}, u32[]{:S(2)}, u32[]{:S(2)}) collective-permute-start(bf16[32,1536]{1,0:T(8,128)(2,1)S(1)} %collective-permute-done.refs_1_.addend_ref), channel_id=1, source_target_pairs={{0,2},{2,0},{1,3},{3,1},{4,6},{6,4},{5,7},{7,5},{8,10},{10,8},{9,1... | collective-permute-start | bytes 294920 | tf_op jit(solution)/shard_map/ppermute | solution.py:315
  9.4 4.7 %collective-permute-start.1 = (bf16[32,1536]{1,0:T(8,128)(2,1)S(1)}, bf16[32,1536]{1,0:T(8,128)(2,1)S(1)}, u32[]{:S(2)}, u32[]{:S(2)}) collective-permute-start(bf16[32,1536]{1,0:T(8,128)(2,1)S(1)} %get-tuple-element.65.refs_1_.addend_ref), channel_id=1, source_target_pairs={{0,2},{2,0},{1,3},{3,1},{4,6},{6,4},{5,7},{7,5},{8,10},{10,8},{9,1... | collective-permute-start | bytes 294920 | tf_op jit(solution)/shard_map/ppermute | solution.py:315
  13.0 2.1 %collective-permute-start.4 = (bf16[32,1536]{1,0:T(8,128)(2,1)S(1)}, bf16[32,1536]{1,0:T(8,128)(2,1)S(1)}, u32[]{:S(2)}, u32[]{:S(2)}) collective-permute-start(bf16[32,1536]{1,0:T(8,128)(2,1)S(1)} %collective-permute-done.refs_1_.addend_ref), channel_id=1, source_target_pairs={{0,1},{1,0},{2,3},{3,2},{4,5},{5,4},{6,7},{7,6},{8,9},{9,8},{10,11... | collective-permute-start | bytes 294920 | tf_op jit(solution)/shard_map/ppermute | solution.py:312
  13.0 2.1 %collective-permute-start.5 = (bf16[32,1536]{1,0:T(8,128)(2,1)S(1)}, bf16[32,1536]{1,0:T(8,128)(2,1)S(1)}, u32[]{:S(2)}, u32[]{:S(2)}) collective-permute-start(bf16[32,1536]{1,0:T(8,128)(2,1)S(1)} %collective-permute-done.3.refs_2_), channel_id=1, source_target_pairs={{0,1},{1,0},{2,3},{3,2},{4,5},{5,4},{6,7},{7,6},{8,9},{9,8},{10,11... | collective-permute-start | bytes 294920 | tf_op jit(solution)/shard_map/ppermute | solution.py:312
  14.1 2.9 %collective-permute-start.6 = (bf16[32,1536]{1,0:T(8,128)(2,1)S(1)}, bf16[32,1536]{1,0:T(8,128)(2,1)S(1)}, u32[]{:S(2)}, u32[]{:S(2)}) collective-permute-start(bf16[32,1536]{1,0:T(8,128)(2,1)S(1)} %get-tuple-element.65.refs_1_.addend_ref), channel_id=1, source_target_pairs={{0,1},{1,0},{2,3},{3,2},{4,5},{5,4},{6,7},{7,6},{8,9},{9,8},{10,11... | collective-permute-start | bytes 294920 | tf_op jit(solution)/shard_map/ppermute | solution.py:312
  14.1 2.9 %collective-permute-start.7 = (bf16[32,1536]{1,0:T(8,128)(2,1)S(1)}, bf16[32,1536]{1,0:T(8,128)(2,1)S(1)}, u32[]{:S(2)}, u32[]{:S(2)}) collective-permute-start(bf16[32,1536]{1,0:T(8,128)(2,1)S(1)} %collective-permute-done.1.refs_2_), channel_id=1, source_target_pairs={{0,1},{1,0},{2,3},{3,2},{4,5},{5,4},{6,7},{7,6},{8,9},{9,8},{10,11... | collective-permute-start | bytes 294920 | tf_op jit(solution)/shard_map/ppermute | solution.py:312
  16.0 7.9 %collective-permute-start.8 = (bf16[768,128]{1,0:T(8,128)(2,1)S(1)}, bf16[768,128]{1,0:T(8,128)(2,1)S(1)}, u32[]{:S(2)}, u32[]{:S(2)}) collective-permute-start(bf16[768,128]{1,0:T(8,128)(2,1)S(1)} %get-tuple-element.61.mine_ref), channel_id=1, source_target_pairs={{0,4},{4,0},{1,5},{5,1},{2,6},{6,2},{3,7},{7,3},{8,12},{12,8},{9,1... | collective-permute-start | bytes 589832 | tf_op jit(solution)/shard_map/ppermute | solution.py:309
  17.9 8.9 %collective-permute-start.10 = (bf16[768,128]{1,0:T(8,128)(2,1)S(1)}, bf16[768,128]{1,0:T(8,128)(2,1)S(1)}, u32[]{:S(2)}, u32[]{:S(2)}) collective-permute-start(bf16[768,128]{1,0:T(8,128)(2,1)S(1)} %get-tuple-element.67.mine_ref), channel_id=1, source_target_pairs={{0,4},{4,0},{1,5},{5,1},{2,6},{6,2},{3,7},{7,3},{8,12},{12,8},{9,1... | collective-permute-start | bytes 589832 | tf_op jit(solution)/shard_map/ppermute | solution.py:309
  19.0 14.1 %slice-start = ((s8[4718592]{0:T(1024)(128)(4,1)}), s8[4194304]{0:T(1024)(128)(4,1)S(1)}, s32[]{:S(2)}) async-start(s8[4718592]{0:T(1024)(128)(4,1)} %bitcast.7), calls=%async_computation | async-start | bytes 8388608
  21.6 11.6 %slice-start.1 = ((s8[4718592]{0:T(1024)(128)(4,1)}), s8[524288]{0:T(1024)(128)(4,1)S(1)}, s32[]{:S(2)}) async-start(s8[4718592]{0:T(1024)(128)(4,1)} %bitcast.7), calls=%async_computation.1 | async-start | bytes 1048576
  24.9 3.0 %collective-permute-start.9 = (bf16[2,32,1536]{2,1,0:T(8,128)(2,1)S(1)}, bf16[2,32,1536]{2,1,0:T(8,128)(2,1)S(1)}, u32[]{:S(2)}, u32[]{:S(2)}) collective-permute-start(bf16[2,32,1536]{2,1,0:T(8,128)(2,1)S(1)} %get-tuple-element.70), channel_id=1, source_target_pairs={{0,1},{1,0},{2,3},{3,2},{4,5},{5,4},{6,7},{7,6},{8,9},{9,8},{10,11... | collective-permute-start | bytes 589832 | tf_op jit(solution)/shard_map/ppermute | solution.py:312
  27.8 3.0 %collective-permute-start.11 = (bf16[2,32,1536]{2,1,0:T(8,128)(2,1)S(1)}, bf16[2,32,1536]{2,1,0:T(8,128)(2,1)S(1)}, u32[]{:S(2)}, u32[]{:S(2)}) collective-permute-start(bf16[2,32,1536]{2,1,0:T(8,128)(2,1)S(1)} %get-tuple-element.75), channel_id=1, source_target_pairs={{0,1},{1,0},{2,3},{3,2},{4,5},{5,4},{6,7},{7,6},{8,9},{9,8},{10,11... | collective-permute-start | bytes 589832 | tf_op jit(solution)/shard_map/ppermute | solution.py:312
  28.0 7.8 %collective-permute-start.12 = (bf16[32,1536]{1,0:T(8,128)(2,1)S(1)}, bf16[32,1536]{1,0:T(8,128)(2,1)S(1)}, u32[]{:S(2)}, u32[]{:S(2)}) collective-permute-start(bf16[32,1536]{1,0:T(8,128)(2,1)S(1)} %get-tuple-element.71.refs_0_), channel_id=1, source_target_pairs={{0,8},{1,9},{2,10},{3,11},{8,0},{9,1},{10,2},{11,3},{16,24},{17,25... | collective-permute-start | bytes 294920 | tf_op jit(solution)/shard_map/ppermute | solution.py:331
  29.5 7.0 %collective-permute-start.13 = (bf16[32,1536]{1,0:T(8,128)(2,1)S(1)}, bf16[32,1536]{1,0:T(8,128)(2,1)S(1)}, u32[]{:S(2)}, u32[]{:S(2)}) collective-permute-start(bf16[32,1536]{1,0:T(8,128)(2,1)S(1)} %get-tuple-element.72.refs_1_), channel_id=1, source_target_pairs={{0,10},{1,11},{2,8},{3,9},{8,2},{9,3},{10,0},{11,1},{16,26},{17,27... | collective-permute-start | bytes 294920 | tf_op jit(solution)/shard_map/ppermute | solution.py:331
  30.9 7.1 %collective-permute-start.18 = (bf16[32,1536]{1,0:T(8,128)(2,1)S(1)}, bf16[32,1536]{1,0:T(8,128)(2,1)S(1)}, u32[]{:S(2)}, u32[]{:S(2)}) collective-permute-start(bf16[32,1536]{1,0:T(8,128)(2,1)S(1)} %get-tuple-element.76.refs_0_), channel_id=1, source_target_pairs={{0,8},{1,9},{2,10},{3,11},{8,0},{9,1},{10,2},{11,3},{16,24},{17,25... | collective-permute-start | bytes 294920 | tf_op jit(solution)/shard_map/ppermute | solution.py:331
  32.4 8.0 %collective-permute-start.19 = (bf16[32,1536]{1,0:T(8,128)(2,1)S(1)}, bf16[32,1536]{1,0:T(8,128)(2,1)S(1)}, u32[]{:S(2)}, u32[]{:S(2)}) collective-permute-start(bf16[32,1536]{1,0:T(8,128)(2,1)S(1)} %get-tuple-element.77.refs_1_), channel_id=1, source_target_pairs={{0,10},{1,11},{2,8},{3,9},{8,2},{9,3},{10,0},{11,1},{16,26},{17,27... | collective-permute-start | bytes 294920 | tf_op jit(solution)/shard_map/ppermute | solution.py:331
  34.2 6.2 %collective-permute-start.17 = (bf16[32,1536]{1,0:T(8,128)(2,1)S(1)}, bf16[32,1536]{1,0:T(8,128)(2,1)S(1)}, u32[]{:S(2)}, u32[]{:S(2)}) collective-permute-start(bf16[32,1536]{1,0:T(8,128)(2,1)S(1)} %get-tuple-element.82), channel_id=1, source_target_pairs={{0,4},{4,0},{1,5},{5,1},{2,6},{6,2},{3,7},{7,3},{8,12},{12,8},{9,1... | collective-permute-start | bytes 294920 | tf_op jit(solution)/shard_map/ppermute | solution.py:309
  36.6 5.8 %collective-permute-start.14 = (bf16[32,1536]{1,0:T(8,128)(2,1)S(1)}, bf16[32,1536]{1,0:T(8,128)(2,1)S(1)}, u32[]{:S(2)}, u32[]{:S(2)}) collective-permute-start(bf16[32,1536]{1,0:T(8,128)(2,1)S(1)} %fusion.refs_2_.addend_ref), channel_id=1, source_target_pairs={{0,2},{2,0},{1,3},{3,1},{4,6},{6,4},{5,7},{7,5},{8,10},{10,8},{9,1... | collective-permute-start | bytes 294920 | tf_op jit(solution)/shard_map/ppermute | solution.py:315
  40.5 4.7 %collective-permute-start.20 = (bf16[32,1536]{1,0:T(8,128)(2,1)S(1)}, bf16[32,1536]{1,0:T(8,128)(2,1)S(1)}, u32[]{:S(2)}, u32[]{:S(2)}) collective-permute-start(bf16[32,1536]{1,0:T(8,128)(2,1)S(1)} %fusion.1.refs_2_.addend_ref), channel_id=1, source_target_pairs={{0,2},{2,0},{1,3},{3,1},{4,6},{6,4},{5,7},{7,5},{8,10},{10,8},{9,1... | collective-permute-start | bytes 294920 | tf_op jit(solution)/shard_map/ppermute | solution.py:315
  41.2 3.9 %collective-permute-start.15 = (bf16[32,1536]{1,0:T(8,128)(2,1)S(1)}, bf16[32,1536]{1,0:T(8,128)(2,1)S(1)}, u32[]{:S(2)}, u32[]{:S(2)}) collective-permute-start(bf16[32,1536]{1,0:T(8,128)(2,1)S(1)} %fusion.refs_2_.addend_ref), channel_id=1, source_target_pairs={{0,1},{1,0},{2,3},{3,2},{4,5},{5,4},{6,7},{7,6},{8,9},{9,8},{10,11... | collective-permute-start | bytes 294920 | tf_op jit(solution)/shard_map/ppermute | solution.py:312
  42.4 2.8 %collective-permute-start.16 = (bf16[32,1536]{1,0:T(8,128)(2,1)S(1)}, bf16[32,1536]{1,0:T(8,128)(2,1)S(1)}, u32[]{:S(2)}, u32[]{:S(2)}) collective-permute-start(bf16[32,1536]{1,0:T(8,128)(2,1)S(1)} %collective-permute-done.14.refs_3_), channel_id=1, source_target_pairs={{0,1},{1,0},{2,3},{3,2},{4,5},{5,4},{6,7},{7,6},{8,9},{9,8},{10,11... | collective-permute-start | bytes 294920 | tf_op jit(solution)/shard_map/ppermute | solution.py:312
  42.4 5.3 %collective-permute-start.21 = (bf16[32,1536]{1,0:T(8,128)(2,1)S(1)}, bf16[32,1536]{1,0:T(8,128)(2,1)S(1)}, u32[]{:S(2)}, u32[]{:S(2)}) collective-permute-start(bf16[32,1536]{1,0:T(8,128)(2,1)S(1)} %fusion.1.refs_2_.addend_ref), channel_id=1, source_target_pairs={{0,1},{1,0},{2,3},{3,2},{4,5},{5,4},{6,7},{7,6},{8,9},{9,8},{10,11... | collective-permute-start | bytes 294920 | tf_op jit(solution)/shard_map/ppermute | solution.py:312
  45.2 2.5 %collective-permute-start.22 = (bf16[32,1536]{1,0:T(8,128)(2,1)S(1)}, bf16[32,1536]{1,0:T(8,128)(2,1)S(1)}, u32[]{:S(2)}, u32[]{:S(2)}) collective-permute-start(bf16[32,1536]{1,0:T(8,128)(2,1)S(1)} %collective-permute-done.20.refs_3_), channel_id=1, source_target_pairs={{0,1},{1,0},{2,3},{3,2},{4,5},{5,4},{6,7},{7,6},{8,9},{9,8},{10,11... | collective-permute-start | bytes 294920 | tf_op jit(solution)/shard_map/ppermute | solution.py:312
  46.1 7.8 %collective-permute-start.24 = (bf16[768,128]{1,0:T(8,128)(2,1)S(1)}, bf16[768,128]{1,0:T(8,128)(2,1)S(1)}, u32[]{:S(2)}, u32[]{:S(2)}) collective-permute-start(bf16[768,128]{1,0:T(8,128)(2,1)S(1)} %get-tuple-element.81.mine_ref), channel_id=1, source_target_pairs={{0,4},{4,0},{1,5},{5,1},{2,6},{6,2},{3,7},{7,3},{8,12},{12,8},{9,1... | collective-permute-start | bytes 589832 | tf_op jit(solution)/shard_map/ppermute | solution.py:309
  48.5 9.1 %collective-permute-start.23 = (bf16[768,128]{1,0:T(8,128)(2,1)S(1)}, bf16[768,128]{1,0:T(8,128)(2,1)S(1)}, u32[]{:S(2)}, u32[]{:S(2)}) collective-permute-start(bf16[768,128]{1,0:T(8,128)(2,1)S(1)} %get-tuple-element.83.mine_ref), channel_id=1, source_target_pairs={{0,4},{4,0},{1,5},{5,1},{2,6},{6,2},{3,7},{7,3},{8,12},{12,8},{9,1... | collective-permute-start | bytes 589832 | tf_op jit(solution)/shard_map/ppermute | solution.py:309
  54.7 3.9 %collective-permute-start.25 = (bf16[2,32,1536]{2,1,0:T(8,128)(2,1)S(1)}, bf16[2,32,1536]{2,1,0:T(8,128)(2,1)S(1)}, u32[]{:S(2)}, u32[]{:S(2)}) collective-permute-start(bf16[2,32,1536]{2,1,0:T(8,128)(2,1)S(1)} %get-tuple-element.86), channel_id=1, source_target_pairs={{0,1},{1,0},{2,3},{3,2},{4,5},{5,4},{6,7},{7,6},{8,9},{9,8},{10,11... | collective-permute-start | bytes 589832 | tf_op jit(solution)/shard_map/ppermute | solution.py:312
  58.5 1.5 %collective-permute-start.26 = (bf16[2,32,1536]{2,1,0:T(8,128)(2,1)S(1)}, bf16[2,32,1536]{2,1,0:T(8,128)(2,1)S(1)}, u32[]{:S(2)}, u32[]{:S(2)}) collective-permute-start(bf16[2,32,1536]{2,1,0:T(8,128)(2,1)S(1)} %get-tuple-element.90), channel_id=1, source_target_pairs={{0,1},{1,0},{2,3},{3,2},{4,5},{5,4},{6,7},{7,6},{8,9},{9,8},{10,11... | collective-permute-start | bytes 589832 | tf_op jit(solution)/shard_map/ppermute | solution.py:312
  60.1 7.0 %collective-permute-start.27 = (bf16[32,1536]{1,0:T(8,128)(2,1)S(1)}, bf16[32,1536]{1,0:T(8,128)(2,1)S(1)}, u32[]{:S(2)}, u32[]{:S(2)}) collective-permute-start(bf16[32,1536]{1,0:T(8,128)(2,1)S(1)} %get-tuple-element.92), channel_id=1, source_target_pairs={{0,2},{2,0},{1,3},{3,1},{4,6},{6,4},{5,7},{7,5},{8,10},{10,8},{9,1... | collective-permute-start | bytes 294920 | tf_op jit(solution)/shard_map/ppermute | solution.py:315
  60.9 6.3 %collective-permute-start.28 = (bf16[32,1536]{1,0:T(8,128)(2,1)S(1)}, bf16[32,1536]{1,0:T(8,128)(2,1)S(1)}, u32[]{:S(2)}, u32[]{:S(2)}) collective-permute-start(bf16[32,1536]{1,0:T(8,128)(2,1)S(1)} %get-tuple-element.87), channel_id=1, source_target_pairs={{0,4},{1,5},{2,6},{3,7},{4,0},{5,1},{6,2},{7,3},{8,12},{9,13},{10,... | collective-permute-start | bytes 294920 | tf_op jit(solution)/shard_map/ppermute | solution.py:323
  62.4 6.0 %collective-permute-start.29 = (bf16[32,1536]{1,0:T(8,128)(2,1)S(1)}, bf16[32,1536]{1,0:T(8,128)(2,1)S(1)}, u32[]{:S(2)}, u32[]{:S(2)}) collective-permute-start(bf16[32,1536]{1,0:T(8,128)(2,1)S(1)} %get-tuple-element.88), channel_id=1, source_target_pairs={{0,6},{1,7},{2,4},{3,5},{4,2},{5,3},{6,0},{7,1},{8,14},{9,15},{10,... | collective-permute-start | bytes 294920 | tf_op jit(solution)/shard_map/ppermute | solution.py:323
  (1 other events, 1.8 us)

commit v14 on v13

--- a/solution.py
+++ b/solution.py
@@ -412,9 +412,9 @@
     grad_value, grad_out = weight_grads(
         first_result, second_result, first_full, second_full
     )
-    own_parts, other_parts, _ = lax.optimization_barrier((own_parts, other_parts, grad_value))
+    other_grad = lax.optimization_barrier(total(other_parts).astype(jnp.bfloat16))
+    own_parts, _ = lax.optimization_barrier((own_parts, grad_value))
     own_grad = total(own_parts).astype(jnp.bfloat16)
-    other_grad = total(other_parts).astype(jnp.bfloat16)
     input_grad = jnp.concatenate(
         [jnp.where(half == 0, own_grad, other_grad), jnp.where(half == 0, other_grad, own_grad)],
         axis=1,

time: 69.3 us -> 68.8 us (level)
  waiting for transfers between devices: 23.7 us -> 22.2 us
  other arithmetic: 2.93 us -> 3.84 us
    ppermute x12, waiting for transfers between devices: 1.35 us -> 0.03 us  [swap_core(): return lax.ppermute(array, 'core', [(0, 1), (1, 0)])]
    convert_element_type x0 -> x1, other arithmetic: none -> 0.92 us  [on_device(): total(other_parts).astype(jnp.bfloat16)]
    ppermute x2, waiting for transfers between devices: 1.2 us -> 0.5 us  [to_other_half(): return lax.ppermute(array, ('half', 'outer', 'core'), pairs)]
  transfers between devices with their start and end apart: 30 -> 30, of which waited for: 15 -> 15; matrix products, arithmetic and copies ran while one was open for 2% -> 3% of each run, Pallas kernels for 26% -> 26%
where the time goes in v14:
time: 68.8 us; the launch traced here: 68.6 us
  starting transfers between devices  23.2 us (34%)
  waiting for transfers between devices  22.2 us (32%)
  Pallas kernels  17.8 us (26%)
  other arithmetic  3.84 us (6%)
  between operations  1.54 us (2%)
    ppermute x7, waiting for transfers between devices, swap_half(): return lax.ppermute(array, 'half', [(0, 1), (1, 0)])  12.4 us
    ppermute x7, starting transfers between devices, swap_half(): return lax.ppermute(array, 'half', [(0, 1), (1, 0)])  8.97 us
    ppermute x5, waiting for transfers between devices, to_row(): return lax.ppermute(array, 'outer', [(i, i ^ delta) for i in range(outer)])  5.52 us
    ppermute x4, starting transfers between devices, swap_section(): return lax.ppermute(array, ('pair', 'outer', 'core'), pairs)  5.08 us
    ppermute x5, starting transfers between devices, to_row(): return lax.ppermute(array, 'outer', [(i, i ^ delta) for i in range(outer)])  5.08 us
    pallas_call x4, Pallas kernels, mix(): pl.pallas_call(functools.partial(mix_kernel, outer, odd_phase), out_shape...  3.84 us
    ppermute x4, waiting for transfers between devices, swap_section(): return lax.ppermute(array, ('pair', 'outer', 'core'), pairs)  3.69 us
    pallas_call x2, Pallas kernels, load_table(): pl.pallas_call(load_kernel, out_shape=jax.ShapeDtypeStruct(table.shape, j...  3.57 us
  transfers between devices with their start and end apart: 30, of which 15 were waited for; matrix products, arithmetic and copies ran while one was open for 3% of the time, Pallas kernels for 26%

profile of v14, /device:TPU:0, one launch (start us, length us, event | category | flops | bytes accessed | tf_op | source)
XLA Modules:
  0.0 68.6 jit_solution(13819721562118589745)
XLA Ops:
  0.6 1.0 %bitcast_select_fusion = bf16[32,3072]{1,0:T(8,128)(2,1)S(1)} fusion(bf16[1,32,3072]{2,1,0:T(8,128)(2,1)} %param.10, pred[]{:T(512)S(6)} %eq.8, bf16[1,32,3072]{2,1,0:T(8,128)(2,1)} %param.7), kind=kLoop, calls=%fused_computation.2 | loop fusion | flops 98304 | bytes 589825 | tf_op jit(solution)/shard_map/jit(_where)/select_n | solution.py:348
  1.7 3.0 %collective-permute-start = (bf16[32,1536]{1,0:T(8,128)(2,1)S(1)}, bf16[32,1536]{1,0:T(8,128)(2,1)S(1)}, u32[]{:S(2)}, u32[]{:S(2)}) collective-permute-start(bf16[32,1536]{1,0:T(8,128)(2,1)S(1)} %get-tuple-element.109), channel_id=1, source_target_pairs={{0,4},{4,0},{1,5},{5,1},{2,6},{6,2},{3,7},{7,3},{8,12},{12,8},{9,1... | collective-permute-start | bytes 294920 | tf_op jit(solution)/shard_map/ppermute | solution.py:309
  4.7 1.1 %pad_maximum_fusion.stash_ref = bf16[2,768,128]{2,1,0:T(8,128)(2,1)S(1)} fusion(bf16[1,768,128]{2,1,0:T(8,128)(2,1)} %param.9, bf16[1,768,128]{2,1,0:T(8,128)(2,1)} %param.8), kind=kLoop, calls=%fused_computation | loop fusion | flops 196608 | bytes 786432 | tf_op jit(solution)/shard_map/concatenate | solution.py:354
  7.5 1.9 %collective-permute-start.3 = (bf16[32,1536]{1,0:T(8,128)(2,1)S(1)}, bf16[32,1536]{1,0:T(8,128)(2,1)S(1)}, u32[]{:S(2)}, u32[]{:S(2)}) collective-permute-start(bf16[32,1536]{1,0:T(8,128)(2,1)S(1)} %collective-permute-done.refs_1_.addend_ref), channel_id=1, source_target_pairs={{0,2},{2,0},{1,3},{3,1},{4,6},{6,4},{5,7},{7,5},{8,10},{10,8},{9,1... | collective-permute-start | bytes 294920 | tf_op jit(solution)/shard_map/ppermute | solution.py:315
  9.5 2.4 %load_first.1.refs_0_ = bf16[1,2,768,1536]{3,2,1,0:T(8,128)(2,1)S(1)} custom-call(bf16[1,2,768,1536]{3,2,1,0:T(8,128)(2,1)} %source_ref, bf16[1,2,768,1536]{3,2,1,0:T(8,128)(2,1)} %source_ref.1), custom_call_target="tpu_custom_call" | custom-call | flops 1 | bytes 1 | tf_op jit(solution)/shard_map/load_first/pallas_call | solution.py:274
  11.9 1.1 %collective-permute-done.3.refs_2_ = bf16[32,1536]{1,0:T(8,128)(2,1)S(1)} collective-permute-done((bf16[32,1536]{1,0:T(8,128)(2,1)S(1)}, bf16[32,1536]{1,0:T(8,128)(2,1)S(1)}, u32[]{:S(2)}, u32[]{:S(2)}) %collective-permute-start.3) | collective-permute-done | bytes 98336 | tf_op jit(solution)/shard_map/ppermute | solution.py:315
  16.0 1.0 %collective-permute-start.8 = (bf16[768,128]{1,0:T(8,128)(2,1)S(1)}, bf16[768,128]{1,0:T(8,128)(2,1)S(1)}, u32[]{:S(2)}, u32[]{:S(2)}) collective-permute-start(bf16[768,128]{1,0:T(8,128)(2,1)S(1)} %get-tuple-element.59.mine_ref), channel_id=1, source_target_pairs={{0,4},{4,0},{1,5},{5,1},{2,6},{6,2},{3,7},{7,3},{8,12},{12,8},{9,1... | collective-permute-start | bytes 589832 | tf_op jit(solution)/shard_map/ppermute | solution.py:309
  17.9 1.1 %collective-permute-start.10 = (bf16[768,128]{1,0:T(8,128)(2,1)S(1)}, bf16[768,128]{1,0:T(8,128)(2,1)S(1)}, u32[]{:S(2)}, u32[]{:S(2)}) collective-permute-start(bf16[768,128]{1,0:T(8,128)(2,1)S(1)} %get-tuple-element.65.mine_ref), channel_id=1, source_target_pairs={{0,4},{4,0},{1,5},{5,1},{2,6},{6,2},{3,7},{7,3},{8,12},{12,8},{9,1... | collective-permute-start | bytes 589832 | tf_op jit(solution)/shard_map/ppermute | solution.py:309
  19.0 2.5 %load_table.2.value_ref.refs_0_ = bf16[1,2,768,1536]{3,2,1,0:T(8,128)(2,1)S(1)} custom-call(bf16[1,2,768,1536]{3,2,1,0:T(8,128)(2,1)} %source_ref), custom_call_target="tpu_custom_call" | custom-call | flops 1 | bytes 1 | tf_op jit(solution)/shard_map/load_table/pallas_call | solution.py:287
  21.6 2.3 %collective-permute-done.8.arrived_ref = bf16[768,128]{1,0:T(8,128)(2,1)S(1)} collective-permute-done((bf16[768,128]{1,0:T(8,128)(2,1)S(1)}, bf16[768,128]{1,0:T(8,128)(2,1)S(1)}, u32[]{:S(2)}, u32[]{:S(2)}) %collective-permute-start.8) | collective-permute-done | bytes 196640 | tf_op jit(solution)/shard_map/ppermute | solution.py:309
  23.9 1.0 %mix.4 = (bf16[768,128]{1,0:T(8,128)(2,1)S(1)}, bf16[2,32,1536]{2,1,0:T(8,128)(2,1)S(1)}, bf16[2,32,1536]{2,1,0:T(8,128)(2,1)S(1)}) custom-call(bf16[1040,128]{1,0:T(8,128)(2,1)S(1)} %concatenate.10.message_ref, bf16[1,2,768,1536]{3,2,1,0:T(8,128)(2,1)S(1)} %load_table.2.value_ref.refs_0_, bf16[768,128]{1,0:T(8,128)(2,1)S(1)} %get-tuple-element.65.mine_ref, ...), custom_call_target="tpu_custom_call" | custom-call | flops 1 | bytes 1 | tf_op jit(solution)/shard_map/mix/pallas_call | solution.py:141
  25.0 1.8 %collective-permute-done.10.arrived_ref = bf16[768,128]{1,0:T(8,128)(2,1)S(1)} collective-permute-done((bf16[768,128]{1,0:T(8,128)(2,1)S(1)}, bf16[768,128]{1,0:T(8,128)(2,1)S(1)}, u32[]{:S(2)}, u32[]{:S(2)}) %collective-permute-start.10) | collective-permute-done | bytes 196640 | tf_op jit(solution)/shard_map/ppermute | solution.py:309
  26.8 1.0 %mix.5 = (bf16[768,128]{1,0:T(8,128)(2,1)S(1)}, bf16[2,32,1536]{2,1,0:T(8,128)(2,1)S(1)}, bf16[2,32,1536]{2,1,0:T(8,128)(2,1)S(1)}) custom-call(bf16[1040,128]{1,0:T(8,128)(2,1)S(1)} %collective-permute-done.2.message_ref, bf16[1,2,768,1536]{3,2,1,0:T(8,128)(2,1)S(1)} %load_table.2.value_ref.refs_0_, bf16[768,128]{1,0:T(8,128)(2,1)S(1)} %get-tuple-element.59.mine_ref, ...), custom_call_target="tpu_custom_call" | custom-call | flops 1 | bytes 1 | tf_op jit(solution)/shard_map/mix/pallas_call | solution.py:141
  28.0 1.5 %collective-permute-start.12 = (bf16[32,1536]{1,0:T(8,128)(2,1)S(1)}, bf16[32,1536]{1,0:T(8,128)(2,1)S(1)}, u32[]{:S(2)}, u32[]{:S(2)}) collective-permute-start(bf16[32,1536]{1,0:T(8,128)(2,1)S(1)} %get-tuple-element.69.refs_0_), channel_id=1, source_target_pairs={{0,8},{1,9},{2,10},{3,11},{8,0},{9,1},{10,2},{11,3},{16,24},{17,25... | collective-permute-start | bytes 294920 | tf_op jit(solution)/shard_map/ppermute | solution.py:331
  29.5 1.4 %collective-permute-start.13 = (bf16[32,1536]{1,0:T(8,128)(2,1)S(1)}, bf16[32,1536]{1,0:T(8,128)(2,1)S(1)}, u32[]{:S(2)}, u32[]{:S(2)}) collective-permute-start(bf16[32,1536]{1,0:T(8,128)(2,1)S(1)} %get-tuple-element.70.refs_1_), channel_id=1, source_target_pairs={{0,10},{1,11},{2,8},{3,9},{8,2},{9,3},{10,0},{11,1},{16,26},{17,27... | collective-permute-start | bytes 294920 | tf_op jit(solution)/shard_map/ppermute | solution.py:331
  30.9 1.5 %collective-permute-start.18 = (bf16[32,1536]{1,0:T(8,128)(2,1)S(1)}, bf16[32,1536]{1,0:T(8,128)(2,1)S(1)}, u32[]{:S(2)}, u32[]{:S(2)}) collective-permute-start(bf16[32,1536]{1,0:T(8,128)(2,1)S(1)} %get-tuple-element.74.refs_0_), channel_id=1, source_target_pairs={{0,8},{1,9},{2,10},{3,11},{8,0},{9,1},{10,2},{11,3},{16,24},{17,25... | collective-permute-start | bytes 294920 | tf_op jit(solution)/shard_map/ppermute | solution.py:331
  33.2 1.0 %load_table.3.refs_1_ = bf16[1,2,768,1536]{3,2,1,0:T(8,128)(2,1)S(1)} custom-call(bf16[1,2,768,1536]{3,2,1,0:T(8,128)(2,1)S(1)} %bitcast.8), custom_call_target="tpu_custom_call" | custom-call | flops 1 | bytes 1 | tf_op jit(solution)/shard_map/load_table/pallas_call | solution.py:287
  34.2 1.6 %collective-permute-start.17 = (bf16[32,1536]{1,0:T(8,128)(2,1)S(1)}, bf16[32,1536]{1,0:T(8,128)(2,1)S(1)}, u32[]{:S(2)}, u32[]{:S(2)}) collective-permute-start(bf16[32,1536]{1,0:T(8,128)(2,1)S(1)} %get-tuple-element.80), channel_id=1, source_target_pairs={{0,4},{4,0},{1,5},{5,1},{2,6},{6,2},{3,7},{7,3},{8,12},{12,8},{9,1... | collective-permute-start | bytes 294920 | tf_op jit(solution)/shard_map/ppermute | solution.py:309
  36.6 0.9 %collective-permute-start.14 = (bf16[32,1536]{1,0:T(8,128)(2,1)S(1)}, bf16[32,1536]{1,0:T(8,128)(2,1)S(1)}, u32[]{:S(2)}, u32[]{:S(2)}) collective-permute-start(bf16[32,1536]{1,0:T(8,128)(2,1)S(1)} %fusion.refs_2_.addend_ref), channel_id=1, source_target_pairs={{0,2},{2,0},{1,3},{3,1},{4,6},{6,4},{5,7},{7,5},{8,10},{10,8},{9,1... | collective-permute-start | bytes 294920 | tf_op jit(solution)/shard_map/ppermute | solution.py:315
  38.0 2.4 %collective-permute-done.19 = bf16[32,1536]{1,0:T(8,128)(2,1)S(1)} collective-permute-done((bf16[32,1536]{1,0:T(8,128)(2,1)S(1)}, bf16[32,1536]{1,0:T(8,128)(2,1)S(1)}, u32[]{:S(2)}, u32[]{:S(2)}) %collective-permute-start.19) | collective-permute-done | bytes 98336 | tf_op jit(solution)/shard_map/ppermute | solution.py:331
  41.2 1.1 %collective-permute-done.14.refs_3_ = bf16[32,1536]{1,0:T(8,128)(2,1)S(1)} collective-permute-done((bf16[32,1536]{1,0:T(8,128)(2,1)S(1)}, bf16[32,1536]{1,0:T(8,128)(2,1)S(1)}, u32[]{:S(2)}, u32[]{:S(2)}) %collective-permute-start.14) | collective-permute-done | bytes 98336 | tf_op jit(solution)/shard_map/ppermute | solution.py:315
  42.9 2.3 %collective-permute-done.20.refs_3_ = bf16[32,1536]{1,0:T(8,128)(2,1)S(1)} collective-permute-done((bf16[32,1536]{1,0:T(8,128)(2,1)S(1)}, bf16[32,1536]{1,0:T(8,128)(2,1)S(1)}, u32[]{:S(2)}, u32[]{:S(2)}) %collective-permute-start.20) | collective-permute-done | bytes 98336 | tf_op jit(solution)/shard_map/ppermute | solution.py:315
  45.2 0.9 %project.6 = (bf16[768,128]{1,0:T(8,128)(2,1)S(1)}, bf16[128,1536]{1,0:T(8,128)(2,1)S(1)}) custom-call(bf16[1040,128]{1,0:T(8,128)(2,1)S(1)} %concatenate.10.message_ref, bf16[1,2,768,1536]{3,2,1,0:T(8,128)(2,1)S(1)} %load_table.2.value_ref.refs_0_, bf16[1,2,768,1536]{3,2,1,0:T(8,128)(2,1)S(1)} %load_table.3.refs_1_, ...), custom_call_target="tpu_custom_call" | custom-call | flops 1 | bytes 1 | tf_op jit(solution)/shard_map/project/pallas_call | solution.py:83
  46.1 1.6 %collective-permute-start.24 = (bf16[768,128]{1,0:T(8,128)(2,1)S(1)}, bf16[768,128]{1,0:T(8,128)(2,1)S(1)}, u32[]{:S(2)}, u32[]{:S(2)}) collective-permute-start(bf16[768,128]{1,0:T(8,128)(2,1)S(1)} %get-tuple-element.79.mine_ref), channel_id=1, source_target_pairs={{0,4},{4,0},{1,5},{5,1},{2,6},{6,2},{3,7},{7,3},{8,12},{12,8},{9,1... | collective-permute-start | bytes 589832 | tf_op jit(solution)/shard_map/ppermute | solution.py:309
  47.6 0.9 %project.7 = (bf16[768,128]{1,0:T(8,128)(2,1)S(1)}, bf16[128,1536]{1,0:T(8,128)(2,1)S(1)}) custom-call(bf16[1040,128]{1,0:T(8,128)(2,1)S(1)} %collective-permute-done.2.message_ref, bf16[1,2,768,1536]{3,2,1,0:T(8,128)(2,1)S(1)} %load_table.2.value_ref.refs_0_, bf16[1,2,768,1536]{3,2,1,0:T(8,128)(2,1)S(1)} %load_table.3.refs_1_, ...), custom_call_target="tpu_custom_call" | custom-call | flops 1 | bytes 1 | tf_op jit(solution)/shard_map/project/pallas_call | solution.py:83
  49.1 4.7 %collective-permute-done.24.arrived_ref = bf16[768,128]{1,0:T(8,128)(2,1)S(1)} collective-permute-done((bf16[768,128]{1,0:T(8,128)(2,1)S(1)}, bf16[768,128]{1,0:T(8,128)(2,1)S(1)}, u32[]{:S(2)}, u32[]{:S(2)}) %collective-permute-start.24) | collective-permute-done | bytes 196640 | tf_op jit(solution)/shard_map/ppermute | solution.py:309
  54.8 2.9 %collective-permute-done.23.arrived_ref = bf16[768,128]{1,0:T(8,128)(2,1)S(1)} collective-permute-done((bf16[768,128]{1,0:T(8,128)(2,1)S(1)}, bf16[768,128]{1,0:T(8,128)(2,1)S(1)}, u32[]{:S(2)}, u32[]{:S(2)}) %collective-permute-start.23) | collective-permute-done | bytes 196640 | tf_op jit(solution)/shard_map/ppermute | solution.py:309
  57.6 0.9 %mix.6 = (bf16[768,128]{1,0:T(8,128)(2,1)S(1)}, bf16[2,32,1536]{2,1,0:T(8,128)(2,1)S(1)}, bf16[2,32,1536]{2,1,0:T(8,128)(2,1)S(1)}) custom-call(bf16[1040,128]{1,0:T(8,128)(2,1)S(1)} %concatenate.10.message_ref, bf16[1,2,768,1536]{3,2,1,0:T(8,128)(2,1)S(1)} %load_table.2.value_ref.refs_0_, bf16[768,128]{1,0:T(8,128)(2,1)S(1)} %get-tuple-element.79.mine_ref, ...), custom_call_target="tpu_custom_call" | custom-call | flops 1 | bytes 1 | tf_op jit(solution)/shard_map/mix/pallas_call | solution.py:141
  58.7 1.5 %collective-permute-start.28 = (bf16[32,1536]{1,0:T(8,128)(2,1)S(1)}, bf16[32,1536]{1,0:T(8,128)(2,1)S(1)}, u32[]{:S(2)}, u32[]{:S(2)}) collective-permute-start(bf16[32,1536]{1,0:T(8,128)(2,1)S(1)} %get-tuple-element.85), channel_id=1, source_target_pairs={{0,4},{1,5},{2,6},{3,7},{4,0},{5,1},{6,2},{7,3},{8,12},{9,13},{10,... | collective-permute-start | bytes 294920 | tf_op jit(solution)/shard_map/ppermute | solution.py:323
  61.0 1.4 %collective-permute-start.27 = (bf16[32,1536]{1,0:T(8,128)(2,1)S(1)}, bf16[32,1536]{1,0:T(8,128)(2,1)S(1)}, u32[]{:S(2)}, u32[]{:S(2)}) collective-permute-start(bf16[32,1536]{1,0:T(8,128)(2,1)S(1)} %get-tuple-element.90), channel_id=1, source_target_pairs={{0,2},{2,0},{1,3},{3,1},{4,6},{6,4},{5,7},{7,5},{8,10},{10,8},{9,1... | collective-permute-start | bytes 294920 | tf_op jit(solution)/shard_map/ppermute | solution.py:315
  62.4 3.5 %weight_grads.1 = (bf16[1,768,1536]{2,1,0:T(8,128)(2,1)}, bf16[1,768,1536]{2,1,0:T(8,128)(2,1)}) custom-call(bf16[768,128]{1,0:T(8,128)(2,1)S(1)} %get-tuple-element.91.a0, bf16[768,128]{1,0:T(8,128)(2,1)S(1)} %get-tuple-element.92.a1, bf16[768,128]{1,0:T(8,128)(2,1)S(1)} %get-tuple-element.95.b0, bf16[768,128]{1,0:T(8,128)(2,1)S(1)} %get-tuple-element.96.b1, ...), custom_call_target="tpu_custom_call" | custom-call | flops 1 | bytes 1 | tf_op jit(solution)/shard_map/weight_grads/pallas_call | solution.py:201
  66.4 0.9 %add_convert_fusion = bf16[32,1536]{1,0:T(8,128)(2,1)S(1)} fusion(bf16[32,1536]{1,0:T(8,128)(2,1)} %collective-permute-done.29, bf16[32,1536]{1,0:T(8,128)(2,1)S(1)} %collective-permute-done.28), kind=kLoop, calls=%fused_computation.3 | loop fusion | flops 196608 | bytes 294912 | tf_op jit(solution)/shard_map/convert_element_type | solution.py:415
  (62 shorter events, 13.0 us)
Async XLA Ops:
  1.7 5.8 %collective-permute-start = (bf16[32,1536]{1,0:T(8,128)(2,1)S(1)}, bf16[32,1536]{1,0:T(8,128)(2,1)S(1)}, u32[]{:S(2)}, u32[]{:S(2)}) collective-permute-start(bf16[32,1536]{1,0:T(8,128)(2,1)S(1)} %get-tuple-element.109), channel_id=1, source_target_pairs={{0,4},{4,0},{1,5},{5,1},{2,6},{6,2},{3,7},{7,3},{8,12},{12,8},{9,1... | collective-permute-start | bytes 294920 | tf_op jit(solution)/shard_map/ppermute | solution.py:309
  7.2 7.9 %collective-permute-start.2 = (bf16[1040,128]{1,0:T(8,128)(2,1)S(1)}, bf16[1040,128]{1,0:T(8,128)(2,1)S(1)}, u32[]{:S(2)}, u32[]{:S(2)}) collective-permute-start(bf16[1040,128]{1,0:T(8,128)(2,1)S(1)} %concatenate.10.message_ref), channel_id=1, source_target_pairs={{0,4},{4,0},{1,5},{5,1},{2,6},{6,2},{3,7},{7,3},{8,12},{12,8},{9,1... | collective-permute-start | bytes 798728 | tf_op jit(solution)/shard_map/ppermute | solution.py:309
  7.5 5.5 %collective-permute-start.3 = (bf16[32,1536]{1,0:T(8,128)(2,1)S(1)}, bf16[32,1536]{1,0:T(8,128)(2,1)S(1)}, u32[]{:S(2)}, u32[]{:S(2)}) collective-permute-start(bf16[32,1536]{1,0:T(8,128)(2,1)S(1)} %collective-permute-done.refs_1_.addend_ref), channel_id=1, source_target_pairs={{0,2},{2,0},{1,3},{3,1},{4,6},{6,4},{5,7},{7,5},{8,10},{10,8},{9,1... | collective-permute-start | bytes 294920 | tf_op jit(solution)/shard_map/ppermute | solution.py:315
  9.4 4.7 %collective-permute-start.1 = (bf16[32,1536]{1,0:T(8,128)(2,1)S(1)}, bf16[32,1536]{1,0:T(8,128)(2,1)S(1)}, u32[]{:S(2)}, u32[]{:S(2)}) collective-permute-start(bf16[32,1536]{1,0:T(8,128)(2,1)S(1)} %get-tuple-element.63.refs_1_.addend_ref), channel_id=1, source_target_pairs={{0,2},{2,0},{1,3},{3,1},{4,6},{6,4},{5,7},{7,5},{8,10},{10,8},{9,1... | collective-permute-start | bytes 294920 | tf_op jit(solution)/shard_map/ppermute | solution.py:315
  13.0 2.1 %collective-permute-start.4 = (bf16[32,1536]{1,0:T(8,128)(2,1)S(1)}, bf16[32,1536]{1,0:T(8,128)(2,1)S(1)}, u32[]{:S(2)}, u32[]{:S(2)}) collective-permute-start(bf16[32,1536]{1,0:T(8,128)(2,1)S(1)} %collective-permute-done.refs_1_.addend_ref), channel_id=1, source_target_pairs={{0,1},{1,0},{2,3},{3,2},{4,5},{5,4},{6,7},{7,6},{8,9},{9,8},{10,11... | collective-permute-start | bytes 294920 | tf_op jit(solution)/shard_map/ppermute | solution.py:312
  13.0 2.1 %collective-permute-start.5 = (bf16[32,1536]{1,0:T(8,128)(2,1)S(1)}, bf16[32,1536]{1,0:T(8,128)(2,1)S(1)}, u32[]{:S(2)}, u32[]{:S(2)}) collective-permute-start(bf16[32,1536]{1,0:T(8,128)(2,1)S(1)} %collective-permute-done.3.refs_2_), channel_id=1, source_target_pairs={{0,1},{1,0},{2,3},{3,2},{4,5},{5,4},{6,7},{7,6},{8,9},{9,8},{10,11... | collective-permute-start | bytes 294920 | tf_op jit(solution)/shard_map/ppermute | solution.py:312
  14.1 2.9 %collective-permute-start.6 = (bf16[32,1536]{1,0:T(8,128)(2,1)S(1)}, bf16[32,1536]{1,0:T(8,128)(2,1)S(1)}, u32[]{:S(2)}, u32[]{:S(2)}) collective-permute-start(bf16[32,1536]{1,0:T(8,128)(2,1)S(1)} %get-tuple-element.63.refs_1_.addend_ref), channel_id=1, source_target_pairs={{0,1},{1,0},{2,3},{3,2},{4,5},{5,4},{6,7},{7,6},{8,9},{9,8},{10,11... | collective-permute-start | bytes 294920 | tf_op jit(solution)/shard_map/ppermute | solution.py:312
  14.1 2.9 %collective-permute-start.7 = (bf16[32,1536]{1,0:T(8,128)(2,1)S(1)}, bf16[32,1536]{1,0:T(8,128)(2,1)S(1)}, u32[]{:S(2)}, u32[]{:S(2)}) collective-permute-start(bf16[32,1536]{1,0:T(8,128)(2,1)S(1)} %collective-permute-done.1.refs_2_), channel_id=1, source_target_pairs={{0,1},{1,0},{2,3},{3,2},{4,5},{5,4},{6,7},{7,6},{8,9},{9,8},{10,11... | collective-permute-start | bytes 294920 | tf_op jit(solution)/shard_map/ppermute | solution.py:312
  16.0 7.9 %collective-permute-start.8 = (bf16[768,128]{1,0:T(8,128)(2,1)S(1)}, bf16[768,128]{1,0:T(8,128)(2,1)S(1)}, u32[]{:S(2)}, u32[]{:S(2)}) collective-permute-start(bf16[768,128]{1,0:T(8,128)(2,1)S(1)} %get-tuple-element.59.mine_ref), channel_id=1, source_target_pairs={{0,4},{4,0},{1,5},{5,1},{2,6},{6,2},{3,7},{7,3},{8,12},{12,8},{9,1... | collective-permute-start | bytes 589832 | tf_op jit(solution)/shard_map/ppermute | solution.py:309
  17.9 8.9 %collective-permute-start.10 = (bf16[768,128]{1,0:T(8,128)(2,1)S(1)}, bf16[768,128]{1,0:T(8,128)(2,1)S(1)}, u32[]{:S(2)}, u32[]{:S(2)}) collective-permute-start(bf16[768,128]{1,0:T(8,128)(2,1)S(1)} %get-tuple-element.65.mine_ref), channel_id=1, source_target_pairs={{0,4},{4,0},{1,5},{5,1},{2,6},{6,2},{3,7},{7,3},{8,12},{12,8},{9,1... | collective-permute-start | bytes 589832 | tf_op jit(solution)/shard_map/ppermute | solution.py:309
  19.0 14.1 %slice-start = ((s8[4718592]{0:T(1024)(128)(4,1)}), s8[4194304]{0:T(1024)(128)(4,1)S(1)}, s32[]{:S(2)}) async-start(s8[4718592]{0:T(1024)(128)(4,1)} %bitcast.7), calls=%async_computation | async-start | bytes 8388608
  21.6 11.6 %slice-start.1 = ((s8[4718592]{0:T(1024)(128)(4,1)}), s8[524288]{0:T(1024)(128)(4,1)S(1)}, s32[]{:S(2)}) async-start(s8[4718592]{0:T(1024)(128)(4,1)} %bitcast.7), calls=%async_computation.1 | async-start | bytes 1048576
  24.9 3.0 %collective-permute-start.9 = (bf16[2,32,1536]{2,1,0:T(8,128)(2,1)S(1)}, bf16[2,32,1536]{2,1,0:T(8,128)(2,1)S(1)}, u32[]{:S(2)}, u32[]{:S(2)}) collective-permute-start(bf16[2,32,1536]{2,1,0:T(8,128)(2,1)S(1)} %get-tuple-element.68), channel_id=1, source_target_pairs={{0,1},{1,0},{2,3},{3,2},{4,5},{5,4},{6,7},{7,6},{8,9},{9,8},{10,11... | collective-permute-start | bytes 589832 | tf_op jit(solution)/shard_map/ppermute | solution.py:312
  27.8 3.0 %collective-permute-start.11 = (bf16[2,32,1536]{2,1,0:T(8,128)(2,1)S(1)}, bf16[2,32,1536]{2,1,0:T(8,128)(2,1)S(1)}, u32[]{:S(2)}, u32[]{:S(2)}) collective-permute-start(bf16[2,32,1536]{2,1,0:T(8,128)(2,1)S(1)} %get-tuple-element.73), channel_id=1, source_target_pairs={{0,1},{1,0},{2,3},{3,2},{4,5},{5,4},{6,7},{7,6},{8,9},{9,8},{10,11... | collective-permute-start | bytes 589832 | tf_op jit(solution)/shard_map/ppermute | solution.py:312
  28.0 7.8 %collective-permute-start.12 = (bf16[32,1536]{1,0:T(8,128)(2,1)S(1)}, bf16[32,1536]{1,0:T(8,128)(2,1)S(1)}, u32[]{:S(2)}, u32[]{:S(2)}) collective-permute-start(bf16[32,1536]{1,0:T(8,128)(2,1)S(1)} %get-tuple-element.69.refs_0_), channel_id=1, source_target_pairs={{0,8},{1,9},{2,10},{3,11},{8,0},{9,1},{10,2},{11,3},{16,24},{17,25... | collective-permute-start | bytes 294920 | tf_op jit(solution)/shard_map/ppermute | solution.py:331
  29.5 7.0 %collective-permute-start.13 = (bf16[32,1536]{1,0:T(8,128)(2,1)S(1)}, bf16[32,1536]{1,0:T(8,128)(2,1)S(1)}, u32[]{:S(2)}, u32[]{:S(2)}) collective-permute-start(bf16[32,1536]{1,0:T(8,128)(2,1)S(1)} %get-tuple-element.70.refs_1_), channel_id=1, source_target_pairs={{0,10},{1,11},{2,8},{3,9},{8,2},{9,3},{10,0},{11,1},{16,26},{17,27... | collective-permute-start | bytes 294920 | tf_op jit(solution)/shard_map/ppermute | solution.py:331
  30.9 7.1 %collective-permute-start.18 = (bf16[32,1536]{1,0:T(8,128)(2,1)S(1)}, bf16[32,1536]{1,0:T(8,128)(2,1)S(1)}, u32[]{:S(2)}, u32[]{:S(2)}) collective-permute-start(bf16[32,1536]{1,0:T(8,128)(2,1)S(1)} %get-tuple-element.74.refs_0_), channel_id=1, source_target_pairs={{0,8},{1,9},{2,10},{3,11},{8,0},{9,1},{10,2},{11,3},{16,24},{17,25... | collective-permute-start | bytes 294920 | tf_op jit(solution)/shard_map/ppermute | solution.py:331
  32.4 8.0 %collective-permute-start.19 = (bf16[32,1536]{1,0:T(8,128)(2,1)S(1)}, bf16[32,1536]{1,0:T(8,128)(2,1)S(1)}, u32[]{:S(2)}, u32[]{:S(2)}) collective-permute-start(bf16[32,1536]{1,0:T(8,128)(2,1)S(1)} %get-tuple-element.75.refs_1_), channel_id=1, source_target_pairs={{0,10},{1,11},{2,8},{3,9},{8,2},{9,3},{10,0},{11,1},{16,26},{17,27... | collective-permute-start | bytes 294920 | tf_op jit(solution)/shard_map/ppermute | solution.py:331
  34.2 6.2 %collective-permute-start.17 = (bf16[32,1536]{1,0:T(8,128)(2,1)S(1)}, bf16[32,1536]{1,0:T(8,128)(2,1)S(1)}, u32[]{:S(2)}, u32[]{:S(2)}) collective-permute-start(bf16[32,1536]{1,0:T(8,128)(2,1)S(1)} %get-tuple-element.80), channel_id=1, source_target_pairs={{0,4},{4,0},{1,5},{5,1},{2,6},{6,2},{3,7},{7,3},{8,12},{12,8},{9,1... | collective-permute-start | bytes 294920 | tf_op jit(solution)/shard_map/ppermute | solution.py:309
  36.6 5.8 %collective-permute-start.14 = (bf16[32,1536]{1,0:T(8,128)(2,1)S(1)}, bf16[32,1536]{1,0:T(8,128)(2,1)S(1)}, u32[]{:S(2)}, u32[]{:S(2)}) collective-permute-start(bf16[32,1536]{1,0:T(8,128)(2,1)S(1)} %fusion.refs_2_.addend_ref), channel_id=1, source_target_pairs={{0,2},{2,0},{1,3},{3,1},{4,6},{6,4},{5,7},{7,5},{8,10},{10,8},{9,1... | collective-permute-start | bytes 294920 | tf_op jit(solution)/shard_map/ppermute | solution.py:315
  40.5 4.7 %collective-permute-start.20 = (bf16[32,1536]{1,0:T(8,128)(2,1)S(1)}, bf16[32,1536]{1,0:T(8,128)(2,1)S(1)}, u32[]{:S(2)}, u32[]{:S(2)}) collective-permute-start(bf16[32,1536]{1,0:T(8,128)(2,1)S(1)} %fusion.1.refs_2_.addend_ref), channel_id=1, source_target_pairs={{0,2},{2,0},{1,3},{3,1},{4,6},{6,4},{5,7},{7,5},{8,10},{10,8},{9,1... | collective-permute-start | bytes 294920 | tf_op jit(solution)/shard_map/ppermute | solution.py:315
  41.2 3.9 %collective-permute-start.15 = (bf16[32,1536]{1,0:T(8,128)(2,1)S(1)}, bf16[32,1536]{1,0:T(8,128)(2,1)S(1)}, u32[]{:S(2)}, u32[]{:S(2)}) collective-permute-start(bf16[32,1536]{1,0:T(8,128)(2,1)S(1)} %fusion.refs_2_.addend_ref), channel_id=1, source_target_pairs={{0,1},{1,0},{2,3},{3,2},{4,5},{5,4},{6,7},{7,6},{8,9},{9,8},{10,11... | collective-permute-start | bytes 294920 | tf_op jit(solution)/shard_map/ppermute | solution.py:312
  42.4 2.8 %collective-permute-start.16 = (bf16[32,1536]{1,0:T(8,128)(2,1)S(1)}, bf16[32,1536]{1,0:T(8,128)(2,1)S(1)}, u32[]{:S(2)}, u32[]{:S(2)}) collective-permute-start(bf16[32,1536]{1,0:T(8,128)(2,1)S(1)} %collective-permute-done.14.refs_3_), channel_id=1, source_target_pairs={{0,1},{1,0},{2,3},{3,2},{4,5},{5,4},{6,7},{7,6},{8,9},{9,8},{10,11... | collective-permute-start | bytes 294920 | tf_op jit(solution)/shard_map/ppermute | solution.py:312
  42.4 5.3 %collective-permute-start.21 = (bf16[32,1536]{1,0:T(8,128)(2,1)S(1)}, bf16[32,1536]{1,0:T(8,128)(2,1)S(1)}, u32[]{:S(2)}, u32[]{:S(2)}) collective-permute-start(bf16[32,1536]{1,0:T(8,128)(2,1)S(1)} %fusion.1.refs_2_.addend_ref), channel_id=1, source_target_pairs={{0,1},{1,0},{2,3},{3,2},{4,5},{5,4},{6,7},{7,6},{8,9},{9,8},{10,11... | collective-permute-start | bytes 294920 | tf_op jit(solution)/shard_map/ppermute | solution.py:312
  45.2 2.5 %collective-permute-start.22 = (bf16[32,1536]{1,0:T(8,128)(2,1)S(1)}, bf16[32,1536]{1,0:T(8,128)(2,1)S(1)}, u32[]{:S(2)}, u32[]{:S(2)}) collective-permute-start(bf16[32,1536]{1,0:T(8,128)(2,1)S(1)} %collective-permute-done.20.refs_3_), channel_id=1, source_target_pairs={{0,1},{1,0},{2,3},{3,2},{4,5},{5,4},{6,7},{7,6},{8,9},{9,8},{10,11... | collective-permute-start | bytes 294920 | tf_op jit(solution)/shard_map/ppermute | solution.py:312
  46.1 7.8 %collective-permute-start.24 = (bf16[768,128]{1,0:T(8,128)(2,1)S(1)}, bf16[768,128]{1,0:T(8,128)(2,1)S(1)}, u32[]{:S(2)}, u32[]{:S(2)}) collective-permute-start(bf16[768,128]{1,0:T(8,128)(2,1)S(1)} %get-tuple-element.79.mine_ref), channel_id=1, source_target_pairs={{0,4},{4,0},{1,5},{5,1},{2,6},{6,2},{3,7},{7,3},{8,12},{12,8},{9,1... | collective-permute-start | bytes 589832 | tf_op jit(solution)/shard_map/ppermute | solution.py:309
  48.5 9.1 %collective-permute-start.23 = (bf16[768,128]{1,0:T(8,128)(2,1)S(1)}, bf16[768,128]{1,0:T(8,128)(2,1)S(1)}, u32[]{:S(2)}, u32[]{:S(2)}) collective-permute-start(bf16[768,128]{1,0:T(8,128)(2,1)S(1)} %get-tuple-element.81.mine_ref), channel_id=1, source_target_pairs={{0,4},{4,0},{1,5},{5,1},{2,6},{6,2},{3,7},{7,3},{8,12},{12,8},{9,1... | collective-permute-start | bytes 589832 | tf_op jit(solution)/shard_map/ppermute | solution.py:309
  54.7 3.9 %collective-permute-start.25 = (bf16[2,32,1536]{2,1,0:T(8,128)(2,1)S(1)}, bf16[2,32,1536]{2,1,0:T(8,128)(2,1)S(1)}, u32[]{:S(2)}, u32[]{:S(2)}) collective-permute-start(bf16[2,32,1536]{2,1,0:T(8,128)(2,1)S(1)} %get-tuple-element.84), channel_id=1, source_target_pairs={{0,1},{1,0},{2,3},{3,2},{4,5},{5,4},{6,7},{7,6},{8,9},{9,8},{10,11... | collective-permute-start | bytes 589832 | tf_op jit(solution)/shard_map/ppermute | solution.py:312
  58.6 2.4 %collective-permute-start.26 = (bf16[2,32,1536]{2,1,0:T(8,128)(2,1)S(1)}, bf16[2,32,1536]{2,1,0:T(8,128)(2,1)S(1)}, u32[]{:S(2)}, u32[]{:S(2)}) collective-permute-start(bf16[2,32,1536]{2,1,0:T(8,128)(2,1)S(1)} %get-tuple-element.88), channel_id=1, source_target_pairs={{0,1},{1,0},{2,3},{3,2},{4,5},{5,4},{6,7},{7,6},{8,9},{9,8},{10,11... | collective-permute-start | bytes 589832 | tf_op jit(solution)/shard_map/ppermute | solution.py:312
  58.7 7.2 %collective-permute-start.28 = (bf16[32,1536]{1,0:T(8,128)(2,1)S(1)}, bf16[32,1536]{1,0:T(8,128)(2,1)S(1)}, u32[]{:S(2)}, u32[]{:S(2)}) collective-permute-start(bf16[32,1536]{1,0:T(8,128)(2,1)S(1)} %get-tuple-element.85), channel_id=1, source_target_pairs={{0,4},{1,5},{2,6},{3,7},{4,0},{5,1},{6,2},{7,3},{8,12},{9,13},{10,... | collective-permute-start | bytes 294920 | tf_op jit(solution)/shard_map/ppermute | solution.py:323
  60.3 6.1 %collective-permute-start.29 = (bf16[32,1536]{1,0:T(8,128)(2,1)S(1)}, bf16[32,1536]{1,0:T(8,128)(2,1)}, u32[]{:S(2)}, u32[]{:S(2)}) collective-permute-start(bf16[32,1536]{1,0:T(8,128)(2,1)S(1)} %get-tuple-element.86), channel_id=1, source_target_pairs={{0,6},{1,7},{2,4},{3,5},{4,2},{5,3},{6,0},{7,1},{8,14},{9,15},{10,... | collective-permute-start | bytes 294920 | tf_op jit(solution)/shard_map/ppermute | solution.py:323
  61.0 6.8 %collective-permute-start.27 = (bf16[32,1536]{1,0:T(8,128)(2,1)S(1)}, bf16[32,1536]{1,0:T(8,128)(2,1)S(1)}, u32[]{:S(2)}, u32[]{:S(2)}) collective-permute-start(bf16[32,1536]{1,0:T(8,128)(2,1)S(1)} %get-tuple-element.90), channel_id=1, source_target_pairs={{0,2},{2,0},{1,3},{3,1},{4,6},{6,4},{5,7},{7,5},{8,10},{10,8},{9,1... | collective-permute-start | bytes 294920 | tf_op jit(solution)/shard_map/ppermute | solution.py:315
  (1 other events, 1.8 us)

commit v15 on v14

--- a/solution.py
+++ b/solution.py
@@ -311,8 +311,11 @@
     def swap_core(array):
         return lax.ppermute(array, "core", [(0, 1), (1, 0)])
 
-    def to_row(array, delta):
-        return lax.ppermute(array, "outer", [(i, i ^ delta) for i in range(outer)])
+    def to_row(array, delta, other_core=0):
+        pairs = [
+            (2 * i + c, 2 * (i ^ delta) + (c ^ other_core)) for i in range(outer) for c in range(2)
+        ]
+        return lax.ppermute(array, ("outer", "core"), pairs)
 
     def to_other_half(array, delta):
         pairs = [
@@ -393,7 +396,8 @@
         second_piece[m] = jnp.where(odd, input_piece[m], total(received).astype(jnp.bfloat16))
     for m in range(2):
         mine = spread_rows(second_piece[m])
-        theirs = [swap_core(piece) for piece in mine]
+        theirs = [swap_core(second_piece[m])]
+        theirs += [to_row(second_piece[m], delta, 1) for delta in range(1, outer)]
         partial[m], second_full[m] = project(
             shard, probs[m], (value_table, out_table), mine, theirs
         )

time: 68.8 us -> 67.7 us (0.984)
  waiting for transfers between devices: 22.2 us -> 18.6 us
  starting transfers between devices: 23.2 us -> 25.6 us
    ppermute x7, waiting for transfers between devices: 12.4 us -> 9.34 us  [swap_half(): return lax.ppermute(array, 'half', [(0, 1), (1, 0)])]
    ppermute x4, waiting for transfers between devices: 3.69 us -> 2.38 us  [swap_section(): return lax.ppermute(array, ('pair', 'outer', 'core'), pairs)]
    ppermute x12 -> x10, starting transfers between devices: 1.82 us -> 3.02 us  [swap_core(): return lax.ppermute(array, 'core', [(0, 1), (1, 0)])]
    ppermute x7, starting transfers between devices: 8.97 us -> 9.9 us  [swap_half(): return lax.ppermute(array, 'half', [(0, 1), (1, 0)])]
    ppermute x5 -> x7, waiting for transfers between devices: 5.52 us -> 6.35 us  [to_row(): return lax.ppermute(array, ('outer', 'core'), pairs)]
    ppermute x5 -> x7, starting transfers between devices: 5.08 us -> 5.4 us  [to_row(): return lax.ppermute(array, ('outer', 'core'), pairs)]
  transfers between devices with their start and end apart: 30 -> 30, of which waited for: 15 -> 16; matrix products, arithmetic and copies ran while one was open for 3% -> 3% of each run, Pallas kernels for 26% -> 26%
where the time goes in v15:
time: 67.7 us; the launch traced here: 67.5 us
  starting transfers between devices  25.6 us (38%)
  waiting for transfers between devices  18.6 us (27%)
  Pallas kernels  17.8 us (26%)
  other arithmetic  3.84 us (6%)
  between operations  1.55 us (2%)
    ppermute x7, starting transfers between devices, swap_half(): return lax.ppermute(array, 'half', [(0, 1), (1, 0)])  9.9 us
    ppermute x7, waiting for transfers between devices, swap_half(): return lax.ppermute(array, 'half', [(0, 1), (1, 0)])  9.34 us
    ppermute x7, waiting for transfers between devices, to_row(): return lax.ppermute(array, ('outer', 'core'), pairs)  6.35 us
    ppermute x7, starting transfers between devices, to_row(): return lax.ppermute(array, ('outer', 'core'), pairs)  5.4 us
    ppermute x4, starting transfers between devices, swap_section(): return lax.ppermute(array, ('pair', 'outer', 'core'), pairs)  5.08 us
    pallas_call x4, Pallas kernels, mix(): pl.pallas_call(functools.partial(mix_kernel, outer, odd_phase), out_shape...  3.82 us
    pallas_call x2, Pallas kernels, load_table(): pl.pallas_call(load_kernel, out_shape=jax.ShapeDtypeStruct(table.shape, j...  3.57 us
    pallas_call x4, Pallas kernels, project(): pl.pallas_call(functools.partial(project_kernel, outer, shard, len(tables...  3.5 us
  transfers between devices with their start and end apart: 30, of which 16 were waited for; matrix products, arithmetic and copies ran while one was open for 3% of the time, Pallas kernels for 26%

profile of v15, /device:TPU:0, one launch (start us, length us, event | category | flops | bytes accessed | tf_op | source)
XLA Modules:
  0.0 67.5 jit_solution(9661946206053332019)
XLA Ops:
  0.6 1.0 %bitcast_select_fusion = bf16[32,3072]{1,0:T(8,128)(2,1)S(1)} fusion(bf16[1,32,3072]{2,1,0:T(8,128)(2,1)} %param.10, pred[]{:T(512)S(6)} %eq.8, bf16[1,32,3072]{2,1,0:T(8,128)(2,1)} %param.7), kind=kLoop, calls=%fused_computation.2 | loop fusion | flops 98304 | bytes 589825 | tf_op jit(solution)/shard_map/jit(_where)/select_n | solution.py:351
  1.7 3.0 %collective-permute-start = (bf16[32,1536]{1,0:T(8,128)(2,1)S(1)}, bf16[32,1536]{1,0:T(8,128)(2,1)S(1)}, u32[]{:S(2)}, u32[]{:S(2)}) collective-permute-start(bf16[32,1536]{1,0:T(8,128)(2,1)S(1)} %get-tuple-element.109), channel_id=1, source_target_pairs={{0,4},{4,0},{1,5},{5,1},{2,6},{6,2},{3,7},{7,3},{8,12},{12,8},{9,1... | collective-permute-start | bytes 294920 | tf_op jit(solution)/shard_map/ppermute | solution.py:309
  4.7 1.1 %pad_maximum_fusion.stash_ref = bf16[2,768,128]{2,1,0:T(8,128)(2,1)S(1)} fusion(bf16[1,768,128]{2,1,0:T(8,128)(2,1)} %param.9, bf16[1,768,128]{2,1,0:T(8,128)(2,1)} %param.8), kind=kLoop, calls=%fused_computation | loop fusion | flops 196608 | bytes 786432 | tf_op jit(solution)/shard_map/concatenate | solution.py:357
  7.5 1.9 %collective-permute-start.3 = (bf16[32,1536]{1,0:T(8,128)(2,1)S(1)}, bf16[32,1536]{1,0:T(8,128)(2,1)S(1)}, u32[]{:S(2)}, u32[]{:S(2)}) collective-permute-start(bf16[32,1536]{1,0:T(8,128)(2,1)S(1)} %collective-permute-done.refs_1_.addend_ref), channel_id=1, source_target_pairs={{0,2},{1,3},{2,0},{3,1},{4,6},{5,7},{6,4},{7,5},{8,10},{9,11},{10,... | collective-permute-start | bytes 294920 | tf_op jit(solution)/shard_map/ppermute | solution.py:318
  9.5 2.4 %load_first.1.refs_0_ = bf16[1,2,768,1536]{3,2,1,0:T(8,128)(2,1)S(1)} custom-call(bf16[1,2,768,1536]{3,2,1,0:T(8,128)(2,1)} %source_ref, bf16[1,2,768,1536]{3,2,1,0:T(8,128)(2,1)} %source_ref.1), custom_call_target="tpu_custom_call" | custom-call | flops 1 | bytes 1 | tf_op jit(solution)/shard_map/load_first/pallas_call | solution.py:274
  11.9 1.1 %collective-permute-done.3.refs_2_ = bf16[32,1536]{1,0:T(8,128)(2,1)S(1)} collective-permute-done((bf16[32,1536]{1,0:T(8,128)(2,1)S(1)}, bf16[32,1536]{1,0:T(8,128)(2,1)S(1)}, u32[]{:S(2)}, u32[]{:S(2)}) %collective-permute-start.3) | collective-permute-done | bytes 98336 | tf_op jit(solution)/shard_map/ppermute | solution.py:318
  16.0 1.0 %collective-permute-start.8 = (bf16[768,128]{1,0:T(8,128)(2,1)S(1)}, bf16[768,128]{1,0:T(8,128)(2,1)S(1)}, u32[]{:S(2)}, u32[]{:S(2)}) collective-permute-start(bf16[768,128]{1,0:T(8,128)(2,1)S(1)} %get-tuple-element.59.mine_ref), channel_id=1, source_target_pairs={{0,4},{4,0},{1,5},{5,1},{2,6},{6,2},{3,7},{7,3},{8,12},{12,8},{9,1... | collective-permute-start | bytes 589832 | tf_op jit(solution)/shard_map/ppermute | solution.py:309
  17.9 1.1 %collective-permute-start.10 = (bf16[768,128]{1,0:T(8,128)(2,1)S(1)}, bf16[768,128]{1,0:T(8,128)(2,1)S(1)}, u32[]{:S(2)}, u32[]{:S(2)}) collective-permute-start(bf16[768,128]{1,0:T(8,128)(2,1)S(1)} %get-tuple-element.65.mine_ref), channel_id=1, source_target_pairs={{0,4},{4,0},{1,5},{5,1},{2,6},{6,2},{3,7},{7,3},{8,12},{12,8},{9,1... | collective-permute-start | bytes 589832 | tf_op jit(solution)/shard_map/ppermute | solution.py:309
  19.0 2.5 %load_table.2.value_ref.refs_0_ = bf16[1,2,768,1536]{3,2,1,0:T(8,128)(2,1)S(1)} custom-call(bf16[1,2,768,1536]{3,2,1,0:T(8,128)(2,1)} %source_ref), custom_call_target="tpu_custom_call" | custom-call | flops 1 | bytes 1 | tf_op jit(solution)/shard_map/load_table/pallas_call | solution.py:287
  21.6 2.3 %collective-permute-done.8.arrived_ref = bf16[768,128]{1,0:T(8,128)(2,1)S(1)} collective-permute-done((bf16[768,128]{1,0:T(8,128)(2,1)S(1)}, bf16[768,128]{1,0:T(8,128)(2,1)S(1)}, u32[]{:S(2)}, u32[]{:S(2)}) %collective-permute-start.8) | collective-permute-done | bytes 196640 | tf_op jit(solution)/shard_map/ppermute | solution.py:309
  23.9 1.0 %mix.4 = (bf16[768,128]{1,0:T(8,128)(2,1)S(1)}, bf16[2,32,1536]{2,1,0:T(8,128)(2,1)S(1)}, bf16[2,32,1536]{2,1,0:T(8,128)(2,1)S(1)}) custom-call(bf16[1040,128]{1,0:T(8,128)(2,1)S(1)} %concatenate.10.message_ref, bf16[1,2,768,1536]{3,2,1,0:T(8,128)(2,1)S(1)} %load_table.2.value_ref.refs_0_, bf16[768,128]{1,0:T(8,128)(2,1)S(1)} %get-tuple-element.65.mine_ref, ...), custom_call_target="tpu_custom_call" | custom-call | flops 1 | bytes 1 | tf_op jit(solution)/shard_map/mix/pallas_call | solution.py:141
  25.0 1.8 %collective-permute-done.10.arrived_ref = bf16[768,128]{1,0:T(8,128)(2,1)S(1)} collective-permute-done((bf16[768,128]{1,0:T(8,128)(2,1)S(1)}, bf16[768,128]{1,0:T(8,128)(2,1)S(1)}, u32[]{:S(2)}, u32[]{:S(2)}) %collective-permute-start.10) | collective-permute-done | bytes 196640 | tf_op jit(solution)/shard_map/ppermute | solution.py:309
  26.8 1.0 %mix.5 = (bf16[768,128]{1,0:T(8,128)(2,1)S(1)}, bf16[2,32,1536]{2,1,0:T(8,128)(2,1)S(1)}, bf16[2,32,1536]{2,1,0:T(8,128)(2,1)S(1)}) custom-call(bf16[1040,128]{1,0:T(8,128)(2,1)S(1)} %collective-permute-done.2.message_ref, bf16[1,2,768,1536]{3,2,1,0:T(8,128)(2,1)S(1)} %load_table.2.value_ref.refs_0_, bf16[768,128]{1,0:T(8,128)(2,1)S(1)} %get-tuple-element.59.mine_ref, ...), custom_call_target="tpu_custom_call" | custom-call | flops 1 | bytes 1 | tf_op jit(solution)/shard_map/mix/pallas_call | solution.py:141
  28.0 1.5 %collective-permute-start.12 = (bf16[32,1536]{1,0:T(8,128)(2,1)S(1)}, bf16[32,1536]{1,0:T(8,128)(2,1)S(1)}, u32[]{:S(2)}, u32[]{:S(2)}) collective-permute-start(bf16[32,1536]{1,0:T(8,128)(2,1)S(1)} %get-tuple-element.69.refs_0_), channel_id=1, source_target_pairs={{0,8},{1,9},{2,10},{3,11},{8,0},{9,1},{10,2},{11,3},{16,24},{17,25... | collective-permute-start | bytes 294920 | tf_op jit(solution)/shard_map/ppermute | solution.py:334
  29.5 1.4 %collective-permute-start.13 = (bf16[32,1536]{1,0:T(8,128)(2,1)S(1)}, bf16[32,1536]{1,0:T(8,128)(2,1)S(1)}, u32[]{:S(2)}, u32[]{:S(2)}) collective-permute-start(bf16[32,1536]{1,0:T(8,128)(2,1)S(1)} %get-tuple-element.70.refs_1_), channel_id=1, source_target_pairs={{0,10},{1,11},{2,8},{3,9},{8,2},{9,3},{10,0},{11,1},{16,26},{17,27... | collective-permute-start | bytes 294920 | tf_op jit(solution)/shard_map/ppermute | solution.py:334
  30.9 1.5 %collective-permute-start.18 = (bf16[32,1536]{1,0:T(8,128)(2,1)S(1)}, bf16[32,1536]{1,0:T(8,128)(2,1)S(1)}, u32[]{:S(2)}, u32[]{:S(2)}) collective-permute-start(bf16[32,1536]{1,0:T(8,128)(2,1)S(1)} %get-tuple-element.74.refs_0_), channel_id=1, source_target_pairs={{0,8},{1,9},{2,10},{3,11},{8,0},{9,1},{10,2},{11,3},{16,24},{17,25... | collective-permute-start | bytes 294920 | tf_op jit(solution)/shard_map/ppermute | solution.py:334
  33.2 1.0 %load_table.3.refs_1_ = bf16[1,2,768,1536]{3,2,1,0:T(8,128)(2,1)S(1)} custom-call(bf16[1,2,768,1536]{3,2,1,0:T(8,128)(2,1)S(1)} %bitcast.8), custom_call_target="tpu_custom_call" | custom-call | flops 1 | bytes 1 | tf_op jit(solution)/shard_map/load_table/pallas_call | solution.py:287
  34.2 1.6 %collective-permute-start.17 = (bf16[32,1536]{1,0:T(8,128)(2,1)S(1)}, bf16[32,1536]{1,0:T(8,128)(2,1)S(1)}, u32[]{:S(2)}, u32[]{:S(2)}) collective-permute-start(bf16[32,1536]{1,0:T(8,128)(2,1)S(1)} %get-tuple-element.80), channel_id=1, source_target_pairs={{0,4},{4,0},{1,5},{5,1},{2,6},{6,2},{3,7},{7,3},{8,12},{12,8},{9,1... | collective-permute-start | bytes 294920 | tf_op jit(solution)/shard_map/ppermute | solution.py:309
  36.6 0.9 %collective-permute-start.15 = (bf16[32,1536]{1,0:T(8,128)(2,1)S(1)}, bf16[32,1536]{1,0:T(8,128)(2,1)S(1)}, u32[]{:S(2)}, u32[]{:S(2)}) collective-permute-start(bf16[32,1536]{1,0:T(8,128)(2,1)S(1)} %fusion.refs_2_.addend_ref), channel_id=1, source_target_pairs={{0,1},{1,0},{2,3},{3,2},{4,5},{5,4},{6,7},{7,6},{8,9},{9,8},{10,11... | collective-permute-start | bytes 294920 | tf_op jit(solution)/shard_map/ppermute | solution.py:312
  38.0 1.2 %collective-permute-start.14 = (bf16[32,1536]{1,0:T(8,128)(2,1)S(1)}, bf16[32,1536]{1,0:T(8,128)(2,1)S(1)}, u32[]{:S(2)}, u32[]{:S(2)}) collective-permute-start(bf16[32,1536]{1,0:T(8,128)(2,1)S(1)} %fusion.refs_2_.addend_ref), channel_id=1, source_target_pairs={{0,2},{1,3},{2,0},{3,1},{4,6},{5,7},{6,4},{7,5},{8,10},{9,11},{10,... | collective-permute-start | bytes 294920 | tf_op jit(solution)/shard_map/ppermute | solution.py:318
  39.2 1.2 %collective-permute-done.19 = bf16[32,1536]{1,0:T(8,128)(2,1)S(1)} collective-permute-done((bf16[32,1536]{1,0:T(8,128)(2,1)S(1)}, bf16[32,1536]{1,0:T(8,128)(2,1)S(1)}, u32[]{:S(2)}, u32[]{:S(2)}) %collective-permute-start.19) | collective-permute-done | bytes 98336 | tf_op jit(solution)/shard_map/ppermute | solution.py:334
  41.3 1.1 %collective-permute-done.16.refs_5_ = bf16[32,1536]{1,0:T(8,128)(2,1)S(1)} collective-permute-done((bf16[32,1536]{1,0:T(8,128)(2,1)S(1)}, bf16[32,1536]{1,0:T(8,128)(2,1)S(1)}, u32[]{:S(2)}, u32[]{:S(2)}) %collective-permute-start.16) | collective-permute-done | bytes 98336 | tf_op jit(solution)/shard_map/ppermute | solution.py:318
  43.1 1.3 %collective-permute-done.14.refs_3_ = bf16[32,1536]{1,0:T(8,128)(2,1)S(1)} collective-permute-done((bf16[32,1536]{1,0:T(8,128)(2,1)S(1)}, bf16[32,1536]{1,0:T(8,128)(2,1)S(1)}, u32[]{:S(2)}, u32[]{:S(2)}) %collective-permute-start.14) | collective-permute-done | bytes 98336 | tf_op jit(solution)/shard_map/ppermute | solution.py:318
  45.4 1.6 %collective-permute-start.24 = (bf16[768,128]{1,0:T(8,128)(2,1)S(1)}, bf16[768,128]{1,0:T(8,128)(2,1)S(1)}, u32[]{:S(2)}, u32[]{:S(2)}) collective-permute-start(bf16[768,128]{1,0:T(8,128)(2,1)S(1)} %get-tuple-element.79.mine_ref), channel_id=1, source_target_pairs={{0,4},{4,0},{1,5},{5,1},{2,6},{6,2},{3,7},{7,3},{8,12},{12,8},{9,1... | collective-permute-start | bytes 589832 | tf_op jit(solution)/shard_map/ppermute | solution.py:309
  46.9 1.8 %collective-permute-done.20.refs_3_ = bf16[32,1536]{1,0:T(8,128)(2,1)S(1)} collective-permute-done((bf16[32,1536]{1,0:T(8,128)(2,1)S(1)}, bf16[32,1536]{1,0:T(8,128)(2,1)S(1)}, u32[]{:S(2)}, u32[]{:S(2)}) %collective-permute-start.20) | collective-permute-done | bytes 98336 | tf_op jit(solution)/shard_map/ppermute | solution.py:318
  49.6 1.6 %collective-permute-start.23 = (bf16[768,128]{1,0:T(8,128)(2,1)S(1)}, bf16[768,128]{1,0:T(8,128)(2,1)S(1)}, u32[]{:S(2)}, u32[]{:S(2)}) collective-permute-start(bf16[768,128]{1,0:T(8,128)(2,1)S(1)} %get-tuple-element.81.mine_ref), channel_id=1, source_target_pairs={{0,4},{4,0},{1,5},{5,1},{2,6},{6,2},{3,7},{7,3},{8,12},{12,8},{9,1... | collective-permute-start | bytes 589832 | tf_op jit(solution)/shard_map/ppermute | solution.py:309
  51.1 1.2 %collective-permute-done.24.arrived_ref = bf16[768,128]{1,0:T(8,128)(2,1)S(1)} collective-permute-done((bf16[768,128]{1,0:T(8,128)(2,1)S(1)}, bf16[768,128]{1,0:T(8,128)(2,1)S(1)}, u32[]{:S(2)}, u32[]{:S(2)}) %collective-permute-start.24) | collective-permute-done | bytes 196640 | tf_op jit(solution)/shard_map/ppermute | solution.py:309
  53.3 3.2 %collective-permute-done.23.arrived_ref = bf16[768,128]{1,0:T(8,128)(2,1)S(1)} collective-permute-done((bf16[768,128]{1,0:T(8,128)(2,1)S(1)}, bf16[768,128]{1,0:T(8,128)(2,1)S(1)}, u32[]{:S(2)}, u32[]{:S(2)}) %collective-permute-start.23) | collective-permute-done | bytes 196640 | tf_op jit(solution)/shard_map/ppermute | solution.py:309
  57.7 1.6 %collective-permute-start.28 = (bf16[32,1536]{1,0:T(8,128)(2,1)S(1)}, bf16[32,1536]{1,0:T(8,128)(2,1)S(1)}, u32[]{:S(2)}, u32[]{:S(2)}) collective-permute-start(bf16[32,1536]{1,0:T(8,128)(2,1)S(1)} %get-tuple-element.85), channel_id=1, source_target_pairs={{0,4},{1,5},{2,6},{3,7},{4,0},{5,1},{6,2},{7,3},{8,12},{9,13},{10,... | collective-permute-start | bytes 294920 | tf_op jit(solution)/shard_map/ppermute | solution.py:326
  60.0 1.4 %collective-permute-start.27 = (bf16[32,1536]{1,0:T(8,128)(2,1)S(1)}, bf16[32,1536]{1,0:T(8,128)(2,1)S(1)}, u32[]{:S(2)}, u32[]{:S(2)}) collective-permute-start(bf16[32,1536]{1,0:T(8,128)(2,1)S(1)} %get-tuple-element.90), channel_id=1, source_target_pairs={{0,2},{1,3},{2,0},{3,1},{4,6},{5,7},{6,4},{7,5},{8,10},{9,11},{10,... | collective-permute-start | bytes 294920 | tf_op jit(solution)/shard_map/ppermute | solution.py:318
  61.4 3.5 %weight_grads.1 = (bf16[1,768,1536]{2,1,0:T(8,128)(2,1)}, bf16[1,768,1536]{2,1,0:T(8,128)(2,1)}) custom-call(bf16[768,128]{1,0:T(8,128)(2,1)S(1)} %get-tuple-element.91.a0, bf16[768,128]{1,0:T(8,128)(2,1)S(1)} %get-tuple-element.92.a1, bf16[768,128]{1,0:T(8,128)(2,1)S(1)} %get-tuple-element.95.b0, bf16[768,128]{1,0:T(8,128)(2,1)S(1)} %get-tuple-element.96.b1, ...), custom_call_target="tpu_custom_call" | custom-call | flops 1 | bytes 1 | tf_op jit(solution)/shard_map/weight_grads/pallas_call | solution.py:201
  65.4 0.9 %add_convert_fusion = bf16[32,1536]{1,0:T(8,128)(2,1)S(1)} fusion(bf16[32,1536]{1,0:T(8,128)(2,1)} %collective-permute-done.29, bf16[32,1536]{1,0:T(8,128)(2,1)S(1)} %collective-permute-done.28), kind=kLoop, calls=%fused_computation.3 | loop fusion | flops 196608 | bytes 294912 | tf_op jit(solution)/shard_map/convert_element_type | solution.py:419
  (62 shorter events, 15.2 us)
Async XLA Ops:
  1.7 5.8 %collective-permute-start = (bf16[32,1536]{1,0:T(8,128)(2,1)S(1)}, bf16[32,1536]{1,0:T(8,128)(2,1)S(1)}, u32[]{:S(2)}, u32[]{:S(2)}) collective-permute-start(bf16[32,1536]{1,0:T(8,128)(2,1)S(1)} %get-tuple-element.109), channel_id=1, source_target_pairs={{0,4},{4,0},{1,5},{5,1},{2,6},{6,2},{3,7},{7,3},{8,12},{12,8},{9,1... | collective-permute-start | bytes 294920 | tf_op jit(solution)/shard_map/ppermute | solution.py:309
  7.2 7.9 %collective-permute-start.2 = (bf16[1040,128]{1,0:T(8,128)(2,1)S(1)}, bf16[1040,128]{1,0:T(8,128)(2,1)S(1)}, u32[]{:S(2)}, u32[]{:S(2)}) collective-permute-start(bf16[1040,128]{1,0:T(8,128)(2,1)S(1)} %concatenate.10.message_ref), channel_id=1, source_target_pairs={{0,4},{4,0},{1,5},{5,1},{2,6},{6,2},{3,7},{7,3},{8,12},{12,8},{9,1... | collective-permute-start | bytes 798728 | tf_op jit(solution)/shard_map/ppermute | solution.py:309
  7.5 5.5 %collective-permute-start.3 = (bf16[32,1536]{1,0:T(8,128)(2,1)S(1)}, bf16[32,1536]{1,0:T(8,128)(2,1)S(1)}, u32[]{:S(2)}, u32[]{:S(2)}) collective-permute-start(bf16[32,1536]{1,0:T(8,128)(2,1)S(1)} %collective-permute-done.refs_1_.addend_ref), channel_id=1, source_target_pairs={{0,2},{1,3},{2,0},{3,1},{4,6},{5,7},{6,4},{7,5},{8,10},{9,11},{10,... | collective-permute-start | bytes 294920 | tf_op jit(solution)/shard_map/ppermute | solution.py:318
  9.4 4.7 %collective-permute-start.1 = (bf16[32,1536]{1,0:T(8,128)(2,1)S(1)}, bf16[32,1536]{1,0:T(8,128)(2,1)S(1)}, u32[]{:S(2)}, u32[]{:S(2)}) collective-permute-start(bf16[32,1536]{1,0:T(8,128)(2,1)S(1)} %get-tuple-element.63.refs_1_.addend_ref), channel_id=1, source_target_pairs={{0,2},{1,3},{2,0},{3,1},{4,6},{5,7},{6,4},{7,5},{8,10},{9,11},{10,... | collective-permute-start | bytes 294920 | tf_op jit(solution)/shard_map/ppermute | solution.py:318
  13.0 2.1 %collective-permute-start.4 = (bf16[32,1536]{1,0:T(8,128)(2,1)S(1)}, bf16[32,1536]{1,0:T(8,128)(2,1)S(1)}, u32[]{:S(2)}, u32[]{:S(2)}) collective-permute-start(bf16[32,1536]{1,0:T(8,128)(2,1)S(1)} %collective-permute-done.refs_1_.addend_ref), channel_id=1, source_target_pairs={{0,1},{1,0},{2,3},{3,2},{4,5},{5,4},{6,7},{7,6},{8,9},{9,8},{10,11... | collective-permute-start | bytes 294920 | tf_op jit(solution)/shard_map/ppermute | solution.py:312
  13.0 2.1 %collective-permute-start.5 = (bf16[32,1536]{1,0:T(8,128)(2,1)S(1)}, bf16[32,1536]{1,0:T(8,128)(2,1)S(1)}, u32[]{:S(2)}, u32[]{:S(2)}) collective-permute-start(bf16[32,1536]{1,0:T(8,128)(2,1)S(1)} %collective-permute-done.3.refs_2_), channel_id=1, source_target_pairs={{0,1},{1,0},{2,3},{3,2},{4,5},{5,4},{6,7},{7,6},{8,9},{9,8},{10,11... | collective-permute-start | bytes 294920 | tf_op jit(solution)/shard_map/ppermute | solution.py:312
  14.1 2.9 %collective-permute-start.6 = (bf16[32,1536]{1,0:T(8,128)(2,1)S(1)}, bf16[32,1536]{1,0:T(8,128)(2,1)S(1)}, u32[]{:S(2)}, u32[]{:S(2)}) collective-permute-start(bf16[32,1536]{1,0:T(8,128)(2,1)S(1)} %get-tuple-element.63.refs_1_.addend_ref), channel_id=1, source_target_pairs={{0,1},{1,0},{2,3},{3,2},{4,5},{5,4},{6,7},{7,6},{8,9},{9,8},{10,11... | collective-permute-start | bytes 294920 | tf_op jit(solution)/shard_map/ppermute | solution.py:312
  14.1 2.9 %collective-permute-start.7 = (bf16[32,1536]{1,0:T(8,128)(2,1)S(1)}, bf16[32,1536]{1,0:T(8,128)(2,1)S(1)}, u32[]{:S(2)}, u32[]{:S(2)}) collective-permute-start(bf16[32,1536]{1,0:T(8,128)(2,1)S(1)} %collective-permute-done.1.refs_2_), channel_id=1, source_target_pairs={{0,1},{1,0},{2,3},{3,2},{4,5},{5,4},{6,7},{7,6},{8,9},{9,8},{10,11... | collective-permute-start | bytes 294920 | tf_op jit(solution)/shard_map/ppermute | solution.py:312
  16.0 7.9 %collective-permute-start.8 = (bf16[768,128]{1,0:T(8,128)(2,1)S(1)}, bf16[768,128]{1,0:T(8,128)(2,1)S(1)}, u32[]{:S(2)}, u32[]{:S(2)}) collective-permute-start(bf16[768,128]{1,0:T(8,128)(2,1)S(1)} %get-tuple-element.59.mine_ref), channel_id=1, source_target_pairs={{0,4},{4,0},{1,5},{5,1},{2,6},{6,2},{3,7},{7,3},{8,12},{12,8},{9,1... | collective-permute-start | bytes 589832 | tf_op jit(solution)/shard_map/ppermute | solution.py:309
  17.9 8.9 %collective-permute-start.10 = (bf16[768,128]{1,0:T(8,128)(2,1)S(1)}, bf16[768,128]{1,0:T(8,128)(2,1)S(1)}, u32[]{:S(2)}, u32[]{:S(2)}) collective-permute-start(bf16[768,128]{1,0:T(8,128)(2,1)S(1)} %get-tuple-element.65.mine_ref), channel_id=1, source_target_pairs={{0,4},{4,0},{1,5},{5,1},{2,6},{6,2},{3,7},{7,3},{8,12},{12,8},{9,1... | collective-permute-start | bytes 589832 | tf_op jit(solution)/shard_map/ppermute | solution.py:309
  19.0 14.1 %slice-start = ((s8[4718592]{0:T(1024)(128)(4,1)}), s8[4194304]{0:T(1024)(128)(4,1)S(1)}, s32[]{:S(2)}) async-start(s8[4718592]{0:T(1024)(128)(4,1)} %bitcast.7), calls=%async_computation | async-start | bytes 8388608
  21.6 11.6 %slice-start.1 = ((s8[4718592]{0:T(1024)(128)(4,1)}), s8[524288]{0:T(1024)(128)(4,1)S(1)}, s32[]{:S(2)}) async-start(s8[4718592]{0:T(1024)(128)(4,1)} %bitcast.7), calls=%async_computation.1 | async-start | bytes 1048576
  24.9 3.0 %collective-permute-start.9 = (bf16[2,32,1536]{2,1,0:T(8,128)(2,1)S(1)}, bf16[2,32,1536]{2,1,0:T(8,128)(2,1)S(1)}, u32[]{:S(2)}, u32[]{:S(2)}) collective-permute-start(bf16[2,32,1536]{2,1,0:T(8,128)(2,1)S(1)} %get-tuple-element.68), channel_id=1, source_target_pairs={{0,1},{1,0},{2,3},{3,2},{4,5},{5,4},{6,7},{7,6},{8,9},{9,8},{10,11... | collective-permute-start | bytes 589832 | tf_op jit(solution)/shard_map/ppermute | solution.py:312
  27.8 3.0 %collective-permute-start.11 = (bf16[2,32,1536]{2,1,0:T(8,128)(2,1)S(1)}, bf16[2,32,1536]{2,1,0:T(8,128)(2,1)S(1)}, u32[]{:S(2)}, u32[]{:S(2)}) collective-permute-start(bf16[2,32,1536]{2,1,0:T(8,128)(2,1)S(1)} %get-tuple-element.73), channel_id=1, source_target_pairs={{0,1},{1,0},{2,3},{3,2},{4,5},{5,4},{6,7},{7,6},{8,9},{9,8},{10,11... | collective-permute-start | bytes 589832 | tf_op jit(solution)/shard_map/ppermute | solution.py:312
  28.0 7.8 %collective-permute-start.12 = (bf16[32,1536]{1,0:T(8,128)(2,1)S(1)}, bf16[32,1536]{1,0:T(8,128)(2,1)S(1)}, u32[]{:S(2)}, u32[]{:S(2)}) collective-permute-start(bf16[32,1536]{1,0:T(8,128)(2,1)S(1)} %get-tuple-element.69.refs_0_), channel_id=1, source_target_pairs={{0,8},{1,9},{2,10},{3,11},{8,0},{9,1},{10,2},{11,3},{16,24},{17,25... | collective-permute-start | bytes 294920 | tf_op jit(solution)/shard_map/ppermute | solution.py:334
  29.5 7.0 %collective-permute-start.13 = (bf16[32,1536]{1,0:T(8,128)(2,1)S(1)}, bf16[32,1536]{1,0:T(8,128)(2,1)S(1)}, u32[]{:S(2)}, u32[]{:S(2)}) collective-permute-start(bf16[32,1536]{1,0:T(8,128)(2,1)S(1)} %get-tuple-element.70.refs_1_), channel_id=1, source_target_pairs={{0,10},{1,11},{2,8},{3,9},{8,2},{9,3},{10,0},{11,1},{16,26},{17,27... | collective-permute-start | bytes 294920 | tf_op jit(solution)/shard_map/ppermute | solution.py:334
  30.9 7.1 %collective-permute-start.18 = (bf16[32,1536]{1,0:T(8,128)(2,1)S(1)}, bf16[32,1536]{1,0:T(8,128)(2,1)S(1)}, u32[]{:S(2)}, u32[]{:S(2)}) collective-permute-start(bf16[32,1536]{1,0:T(8,128)(2,1)S(1)} %get-tuple-element.74.refs_0_), channel_id=1, source_target_pairs={{0,8},{1,9},{2,10},{3,11},{8,0},{9,1},{10,2},{11,3},{16,24},{17,25... | collective-permute-start | bytes 294920 | tf_op jit(solution)/shard_map/ppermute | solution.py:334
  32.4 8.0 %collective-permute-start.19 = (bf16[32,1536]{1,0:T(8,128)(2,1)S(1)}, bf16[32,1536]{1,0:T(8,128)(2,1)S(1)}, u32[]{:S(2)}, u32[]{:S(2)}) collective-permute-start(bf16[32,1536]{1,0:T(8,128)(2,1)S(1)} %get-tuple-element.75.refs_1_), channel_id=1, source_target_pairs={{0,10},{1,11},{2,8},{3,9},{8,2},{9,3},{10,0},{11,1},{16,26},{17,27... | collective-permute-start | bytes 294920 | tf_op jit(solution)/shard_map/ppermute | solution.py:334
  34.2 6.2 %collective-permute-start.17 = (bf16[32,1536]{1,0:T(8,128)(2,1)S(1)}, bf16[32,1536]{1,0:T(8,128)(2,1)S(1)}, u32[]{:S(2)}, u32[]{:S(2)}) collective-permute-start(bf16[32,1536]{1,0:T(8,128)(2,1)S(1)} %get-tuple-element.80), channel_id=1, source_target_pairs={{0,4},{4,0},{1,5},{5,1},{2,6},{6,2},{3,7},{7,3},{8,12},{12,8},{9,1... | collective-permute-start | bytes 294920 | tf_op jit(solution)/shard_map/ppermute | solution.py:309
  36.6 5.9 %collective-permute-start.16 = (bf16[32,1536]{1,0:T(8,128)(2,1)S(1)}, bf16[32,1536]{1,0:T(8,128)(2,1)S(1)}, u32[]{:S(2)}, u32[]{:S(2)}) collective-permute-start(bf16[32,1536]{1,0:T(8,128)(2,1)S(1)} %fusion.refs_2_.addend_ref), channel_id=1, source_target_pairs={{0,3},{1,2},{2,1},{3,0},{4,7},{5,6},{6,5},{7,4},{8,11},{9,10},{10,... | collective-permute-start | bytes 294920 | tf_op jit(solution)/shard_map/ppermute | solution.py:318
  36.6 6.5 %collective-permute-start.15 = (bf16[32,1536]{1,0:T(8,128)(2,1)S(1)}, bf16[32,1536]{1,0:T(8,128)(2,1)S(1)}, u32[]{:S(2)}, u32[]{:S(2)}) collective-permute-start(bf16[32,1536]{1,0:T(8,128)(2,1)S(1)} %fusion.refs_2_.addend_ref), channel_id=1, source_target_pairs={{0,1},{1,0},{2,3},{3,2},{4,5},{5,4},{6,7},{7,6},{8,9},{9,8},{10,11... | collective-permute-start | bytes 294920 | tf_op jit(solution)/shard_map/ppermute | solution.py:312
  38.0 6.5 %collective-permute-start.14 = (bf16[32,1536]{1,0:T(8,128)(2,1)S(1)}, bf16[32,1536]{1,0:T(8,128)(2,1)S(1)}, u32[]{:S(2)}, u32[]{:S(2)}) collective-permute-start(bf16[32,1536]{1,0:T(8,128)(2,1)S(1)} %fusion.refs_2_.addend_ref), channel_id=1, source_target_pairs={{0,2},{1,3},{2,0},{3,1},{4,6},{5,7},{6,4},{7,5},{8,10},{9,11},{10,... | collective-permute-start | bytes 294920 | tf_op jit(solution)/shard_map/ppermute | solution.py:318
  40.5 6.5 %collective-permute-start.22 = (bf16[32,1536]{1,0:T(8,128)(2,1)S(1)}, bf16[32,1536]{1,0:T(8,128)(2,1)S(1)}, u32[]{:S(2)}, u32[]{:S(2)}) collective-permute-start(bf16[32,1536]{1,0:T(8,128)(2,1)S(1)} %fusion.1.refs_2_.addend_ref), channel_id=1, source_target_pairs={{0,3},{1,2},{2,1},{3,0},{4,7},{5,6},{6,5},{7,4},{8,11},{9,10},{10,... | collective-permute-start | bytes 294920 | tf_op jit(solution)/shard_map/ppermute | solution.py:318
  40.6 6.4 %collective-permute-start.21 = (bf16[32,1536]{1,0:T(8,128)(2,1)S(1)}, bf16[32,1536]{1,0:T(8,128)(2,1)S(1)}, u32[]{:S(2)}, u32[]{:S(2)}) collective-permute-start(bf16[32,1536]{1,0:T(8,128)(2,1)S(1)} %fusion.1.refs_2_.addend_ref), channel_id=1, source_target_pairs={{0,1},{1,0},{2,3},{3,2},{4,5},{5,4},{6,7},{7,6},{8,9},{9,8},{10,11... | collective-permute-start | bytes 294920 | tf_op jit(solution)/shard_map/ppermute | solution.py:312
  42.5 6.2 %collective-permute-start.20 = (bf16[32,1536]{1,0:T(8,128)(2,1)S(1)}, bf16[32,1536]{1,0:T(8,128)(2,1)S(1)}, u32[]{:S(2)}, u32[]{:S(2)}) collective-permute-start(bf16[32,1536]{1,0:T(8,128)(2,1)S(1)} %fusion.1.refs_2_.addend_ref), channel_id=1, source_target_pairs={{0,2},{1,3},{2,0},{3,1},{4,6},{5,7},{6,4},{7,5},{8,10},{9,11},{10,... | collective-permute-start | bytes 294920 | tf_op jit(solution)/shard_map/ppermute | solution.py:318
  45.4 7.0 %collective-permute-start.24 = (bf16[768,128]{1,0:T(8,128)(2,1)S(1)}, bf16[768,128]{1,0:T(8,128)(2,1)S(1)}, u32[]{:S(2)}, u32[]{:S(2)}) collective-permute-start(bf16[768,128]{1,0:T(8,128)(2,1)S(1)} %get-tuple-element.79.mine_ref), channel_id=1, source_target_pairs={{0,4},{4,0},{1,5},{5,1},{2,6},{6,2},{3,7},{7,3},{8,12},{12,8},{9,1... | collective-permute-start | bytes 589832 | tf_op jit(solution)/shard_map/ppermute | solution.py:309
  49.6 7.0 %collective-permute-start.23 = (bf16[768,128]{1,0:T(8,128)(2,1)S(1)}, bf16[768,128]{1,0:T(8,128)(2,1)S(1)}, u32[]{:S(2)}, u32[]{:S(2)}) collective-permute-start(bf16[768,128]{1,0:T(8,128)(2,1)S(1)} %get-tuple-element.81.mine_ref), channel_id=1, source_target_pairs={{0,4},{4,0},{1,5},{5,1},{2,6},{6,2},{3,7},{7,3},{8,12},{12,8},{9,1... | collective-permute-start | bytes 589832 | tf_op jit(solution)/shard_map/ppermute | solution.py:309
  53.3 4.3 %collective-permute-start.25 = (bf16[2,32,1536]{2,1,0:T(8,128)(2,1)S(1)}, bf16[2,32,1536]{2,1,0:T(8,128)(2,1)S(1)}, u32[]{:S(2)}, u32[]{:S(2)}) collective-permute-start(bf16[2,32,1536]{2,1,0:T(8,128)(2,1)S(1)} %get-tuple-element.84), channel_id=1, source_target_pairs={{0,1},{1,0},{2,3},{3,2},{4,5},{5,4},{6,7},{7,6},{8,9},{9,8},{10,11... | collective-permute-start | bytes 589832 | tf_op jit(solution)/shard_map/ppermute | solution.py:312
  57.5 2.4 %collective-permute-start.26 = (bf16[2,32,1536]{2,1,0:T(8,128)(2,1)S(1)}, bf16[2,32,1536]{2,1,0:T(8,128)(2,1)S(1)}, u32[]{:S(2)}, u32[]{:S(2)}) collective-permute-start(bf16[2,32,1536]{2,1,0:T(8,128)(2,1)S(1)} %get-tuple-element.88), channel_id=1, source_target_pairs={{0,1},{1,0},{2,3},{3,2},{4,5},{5,4},{6,7},{7,6},{8,9},{9,8},{10,11... | collective-permute-start | bytes 589832 | tf_op jit(solution)/shard_map/ppermute | solution.py:312
  57.7 7.2 %collective-permute-start.28 = (bf16[32,1536]{1,0:T(8,128)(2,1)S(1)}, bf16[32,1536]{1,0:T(8,128)(2,1)S(1)}, u32[]{:S(2)}, u32[]{:S(2)}) collective-permute-start(bf16[32,1536]{1,0:T(8,128)(2,1)S(1)} %get-tuple-element.85), channel_id=1, source_target_pairs={{0,4},{1,5},{2,6},{3,7},{4,0},{5,1},{6,2},{7,3},{8,12},{9,13},{10,... | collective-permute-start | bytes 294920 | tf_op jit(solution)/shard_map/ppermute | solution.py:326
  59.2 6.2 %collective-permute-start.29 = (bf16[32,1536]{1,0:T(8,128)(2,1)S(1)}, bf16[32,1536]{1,0:T(8,128)(2,1)}, u32[]{:S(2)}, u32[]{:S(2)}) collective-permute-start(bf16[32,1536]{1,0:T(8,128)(2,1)S(1)} %get-tuple-element.86), channel_id=1, source_target_pairs={{0,6},{1,7},{2,4},{3,5},{4,2},{5,3},{6,0},{7,1},{8,14},{9,15},{10,... | collective-permute-start | bytes 294920 | tf_op jit(solution)/shard_map/ppermute | solution.py:326
  60.0 6.8 %collective-permute-start.27 = (bf16[32,1536]{1,0:T(8,128)(2,1)S(1)}, bf16[32,1536]{1,0:T(8,128)(2,1)S(1)}, u32[]{:S(2)}, u32[]{:S(2)}) collective-permute-start(bf16[32,1536]{1,0:T(8,128)(2,1)S(1)} %get-tuple-element.90), channel_id=1, source_target_pairs={{0,2},{1,3},{2,0},{3,1},{4,6},{5,7},{6,4},{7,5},{8,10},{9,11},{10,... | collective-permute-start | bytes 294920 | tf_op jit(solution)/shard_map/ppermute | solution.py:318
  (1 other events, 1.8 us)

commit v16 on v15

--- a/solution.py
+++ b/solution.py
@@ -393,10 +393,14 @@
     input_piece = [input_own, swap_half(input_sent)]
     for m in range(2):
         received = [swap_section(part, d) for d, part in enumerate(first_sent[m])]
+        last_received = received
         second_piece[m] = jnp.where(odd, input_piece[m], total(received).astype(jnp.bfloat16))
     for m in range(2):
         mine = spread_rows(second_piece[m])
-        theirs = [swap_core(second_piece[m])]
+        swapped = second_piece[m]
+        if m == 0:
+            swapped, _ = lax.optimization_barrier((swapped, last_received))
+        theirs = [swap_core(swapped)]
         theirs += [to_row(second_piece[m], delta, 1) for delta in range(1, outer)]
         partial[m], second_full[m] = project(
             shard, probs[m], (value_table, out_table), mine, theirs

time: 67.7 us -> 67.7 us (level)
  waiting for transfers between devices: 18.6 us -> 19.6 us
  starting transfers between devices: 25.6 us -> 24.7 us
    ppermute x10, starting transfers between devices: 3.02 us -> 1.31 us  [swap_core(): return lax.ppermute(array, 'core', [(0, 1), (1, 0)])]
    ppermute x4, waiting for transfers between devices: 2.38 us -> 3.61 us  [swap_section(): return lax.ppermute(array, ('pair', 'outer', 'core'), pairs)]
    ppermute x7, starting transfers between devices: 5.4 us -> 6.18 us  [to_row(): return lax.ppermute(array, ('outer', 'core'), pairs)]
    ppermute x7, waiting for transfers between devices: 6.35 us -> 5.66 us  [to_row(): return lax.ppermute(array, ('outer', 'core'), pairs)]
where the time goes in v16:
time: 67.7 us; the launch traced here: 67.5 us
  starting transfers between devices  24.7 us (36%)
  waiting for transfers between devices  19.6 us (29%)
  Pallas kernels  17.8 us (26%)
  other arithmetic  3.84 us (6%)
  between operations  1.54 us (2%)
    ppermute x7, starting transfers between devices, swap_half(): return lax.ppermute(array, 'half', [(0, 1), (1, 0)])  9.91 us
    ppermute x7, waiting for transfers between devices, swap_half(): return lax.ppermute(array, 'half', [(0, 1), (1, 0)])  9.34 us
    ppermute x7, starting transfers between devices, to_row(): return lax.ppermute(array, ('outer', 'core'), pairs)  6.18 us
    ppermute x7, waiting for transfers between devices, to_row(): return lax.ppermute(array, ('outer', 'core'), pairs)  5.66 us
    ppermute x4, starting transfers between devices, swap_section(): return lax.ppermute(array, ('pair', 'outer', 'core'), pairs)  5.08 us
    pallas_call x4, Pallas kernels, mix(): pl.pallas_call(functools.partial(mix_kernel, outer, odd_phase), out_shape...  3.82 us
    ppermute x4, waiting for transfers between devices, swap_section(): return lax.ppermute(array, ('pair', 'outer', 'core'), pairs)  3.61 us
    pallas_call x2, Pallas kernels, load_table(): pl.pallas_call(load_kernel, out_shape=jax.ShapeDtypeStruct(table.shape, j...  3.57 us
  transfers between devices with their start and end apart: 30, of which 16 were waited for; matrix products, arithmetic and copies ran while one was open for 3% of the time, Pallas kernels for 26%

profile of v16, /device:TPU:0, one launch (start us, length us, event | category | flops | bytes accessed | tf_op | source)
XLA Modules:
  0.0 67.5 jit_solution(10577678484601629691)
XLA Ops:
  0.6 1.0 %bitcast_select_fusion = bf16[32,3072]{1,0:T(8,128)(2,1)S(1)} fusion(bf16[1,32,3072]{2,1,0:T(8,128)(2,1)} %param.10, pred[]{:T(512)S(6)} %eq.8, bf16[1,32,3072]{2,1,0:T(8,128)(2,1)} %param.7), kind=kLoop, calls=%fused_computation.2 | loop fusion | flops 98304 | bytes 589825 | tf_op jit(solution)/shard_map/jit(_where)/select_n | solution.py:351
  1.7 3.0 %collective-permute-start = (bf16[32,1536]{1,0:T(8,128)(2,1)S(1)}, bf16[32,1536]{1,0:T(8,128)(2,1)S(1)}, u32[]{:S(2)}, u32[]{:S(2)}) collective-permute-start(bf16[32,1536]{1,0:T(8,128)(2,1)S(1)} %get-tuple-element.111), channel_id=1, source_target_pairs={{0,4},{4,0},{1,5},{5,1},{2,6},{6,2},{3,7},{7,3},{8,12},{12,8},{9,1... | collective-permute-start | bytes 294920 | tf_op jit(solution)/shard_map/ppermute | solution.py:309
  4.7 1.1 %pad_maximum_fusion.stash_ref = bf16[2,768,128]{2,1,0:T(8,128)(2,1)S(1)} fusion(bf16[1,768,128]{2,1,0:T(8,128)(2,1)} %param.9, bf16[1,768,128]{2,1,0:T(8,128)(2,1)} %param.8), kind=kLoop, calls=%fused_computation | loop fusion | flops 196608 | bytes 786432 | tf_op jit(solution)/shard_map/concatenate | solution.py:357
  7.5 1.9 %collective-permute-start.3 = (bf16[32,1536]{1,0:T(8,128)(2,1)S(1)}, bf16[32,1536]{1,0:T(8,128)(2,1)S(1)}, u32[]{:S(2)}, u32[]{:S(2)}) collective-permute-start(bf16[32,1536]{1,0:T(8,128)(2,1)S(1)} %collective-permute-done.refs_1_.addend_ref), channel_id=1, source_target_pairs={{0,2},{1,3},{2,0},{3,1},{4,6},{5,7},{6,4},{7,5},{8,10},{9,11},{10,... | collective-permute-start | bytes 294920 | tf_op jit(solution)/shard_map/ppermute | solution.py:318
  9.5 2.4 %load_first.1.refs_0_ = bf16[1,2,768,1536]{3,2,1,0:T(8,128)(2,1)S(1)} custom-call(bf16[1,2,768,1536]{3,2,1,0:T(8,128)(2,1)} %source_ref, bf16[1,2,768,1536]{3,2,1,0:T(8,128)(2,1)} %source_ref.1), custom_call_target="tpu_custom_call" | custom-call | flops 1 | bytes 1 | tf_op jit(solution)/shard_map/load_first/pallas_call | solution.py:274
  11.9 1.1 %collective-permute-done.3.refs_2_ = bf16[32,1536]{1,0:T(8,128)(2,1)S(1)} collective-permute-done((bf16[32,1536]{1,0:T(8,128)(2,1)S(1)}, bf16[32,1536]{1,0:T(8,128)(2,1)S(1)}, u32[]{:S(2)}, u32[]{:S(2)}) %collective-permute-start.3) | collective-permute-done | bytes 98336 | tf_op jit(solution)/shard_map/ppermute | solution.py:318
  16.0 1.0 %collective-permute-start.8 = (bf16[768,128]{1,0:T(8,128)(2,1)S(1)}, bf16[768,128]{1,0:T(8,128)(2,1)S(1)}, u32[]{:S(2)}, u32[]{:S(2)}) collective-permute-start(bf16[768,128]{1,0:T(8,128)(2,1)S(1)} %get-tuple-element.60.mine_ref), channel_id=1, source_target_pairs={{0,4},{4,0},{1,5},{5,1},{2,6},{6,2},{3,7},{7,3},{8,12},{12,8},{9,1... | collective-permute-start | bytes 589832 | tf_op jit(solution)/shard_map/ppermute | solution.py:309
  17.9 1.1 %collective-permute-start.10 = (bf16[768,128]{1,0:T(8,128)(2,1)S(1)}, bf16[768,128]{1,0:T(8,128)(2,1)S(1)}, u32[]{:S(2)}, u32[]{:S(2)}) collective-permute-start(bf16[768,128]{1,0:T(8,128)(2,1)S(1)} %get-tuple-element.66.mine_ref), channel_id=1, source_target_pairs={{0,4},{4,0},{1,5},{5,1},{2,6},{6,2},{3,7},{7,3},{8,12},{12,8},{9,1... | collective-permute-start | bytes 589832 | tf_op jit(solution)/shard_map/ppermute | solution.py:309
  19.0 2.5 %load_table.2.value_ref.refs_0_ = bf16[1,2,768,1536]{3,2,1,0:T(8,128)(2,1)S(1)} custom-call(bf16[1,2,768,1536]{3,2,1,0:T(8,128)(2,1)} %source_ref), custom_call_target="tpu_custom_call" | custom-call | flops 1 | bytes 1 | tf_op jit(solution)/shard_map/load_table/pallas_call | solution.py:287
  21.6 2.3 %collective-permute-done.8.arrived_ref = bf16[768,128]{1,0:T(8,128)(2,1)S(1)} collective-permute-done((bf16[768,128]{1,0:T(8,128)(2,1)S(1)}, bf16[768,128]{1,0:T(8,128)(2,1)S(1)}, u32[]{:S(2)}, u32[]{:S(2)}) %collective-permute-start.8) | collective-permute-done | bytes 196640 | tf_op jit(solution)/shard_map/ppermute | solution.py:309
  23.9 1.0 %mix.4 = (bf16[768,128]{1,0:T(8,128)(2,1)S(1)}, bf16[2,32,1536]{2,1,0:T(8,128)(2,1)S(1)}, bf16[2,32,1536]{2,1,0:T(8,128)(2,1)S(1)}) custom-call(bf16[1040,128]{1,0:T(8,128)(2,1)S(1)} %concatenate.10.message_ref, bf16[1,2,768,1536]{3,2,1,0:T(8,128)(2,1)S(1)} %load_table.2.value_ref.refs_0_, bf16[768,128]{1,0:T(8,128)(2,1)S(1)} %get-tuple-element.66.mine_ref, ...), custom_call_target="tpu_custom_call" | custom-call | flops 1 | bytes 1 | tf_op jit(solution)/shard_map/mix/pallas_call | solution.py:141
  25.0 1.8 %collective-permute-done.10.arrived_ref = bf16[768,128]{1,0:T(8,128)(2,1)S(1)} collective-permute-done((bf16[768,128]{1,0:T(8,128)(2,1)S(1)}, bf16[768,128]{1,0:T(8,128)(2,1)S(1)}, u32[]{:S(2)}, u32[]{:S(2)}) %collective-permute-start.10) | collective-permute-done | bytes 196640 | tf_op jit(solution)/shard_map/ppermute | solution.py:309
  26.8 1.0 %mix.5 = (bf16[768,128]{1,0:T(8,128)(2,1)S(1)}, bf16[2,32,1536]{2,1,0:T(8,128)(2,1)S(1)}, bf16[2,32,1536]{2,1,0:T(8,128)(2,1)S(1)}) custom-call(bf16[1040,128]{1,0:T(8,128)(2,1)S(1)} %collective-permute-done.2.message_ref, bf16[1,2,768,1536]{3,2,1,0:T(8,128)(2,1)S(1)} %load_table.2.value_ref.refs_0_, bf16[768,128]{1,0:T(8,128)(2,1)S(1)} %get-tuple-element.60.mine_ref, ...), custom_call_target="tpu_custom_call" | custom-call | flops 1 | bytes 1 | tf_op jit(solution)/shard_map/mix/pallas_call | solution.py:141
  28.0 1.5 %collective-permute-start.12 = (bf16[32,1536]{1,0:T(8,128)(2,1)S(1)}, bf16[32,1536]{1,0:T(8,128)(2,1)S(1)}, u32[]{:S(2)}, u32[]{:S(2)}) collective-permute-start(bf16[32,1536]{1,0:T(8,128)(2,1)S(1)} %get-tuple-element.70.refs_0_), channel_id=1, source_target_pairs={{0,8},{1,9},{2,10},{3,11},{8,0},{9,1},{10,2},{11,3},{16,24},{17,25... | collective-permute-start | bytes 294920 | tf_op jit(solution)/shard_map/ppermute | solution.py:334
  29.5 1.4 %collective-permute-start.13 = (bf16[32,1536]{1,0:T(8,128)(2,1)S(1)}, bf16[32,1536]{1,0:T(8,128)(2,1)S(1)}, u32[]{:S(2)}, u32[]{:S(2)}) collective-permute-start(bf16[32,1536]{1,0:T(8,128)(2,1)S(1)} %get-tuple-element.71.refs_1_), channel_id=1, source_target_pairs={{0,10},{1,11},{2,8},{3,9},{8,2},{9,3},{10,0},{11,1},{16,26},{17,27... | collective-permute-start | bytes 294920 | tf_op jit(solution)/shard_map/ppermute | solution.py:334
  30.9 1.5 %collective-permute-start.15 = (bf16[32,1536]{1,0:T(8,128)(2,1)S(1)}, bf16[32,1536]{1,0:T(8,128)(2,1)S(1)}, u32[]{:S(2)}, u32[]{:S(2)}) collective-permute-start(bf16[32,1536]{1,0:T(8,128)(2,1)S(1)} %get-tuple-element.75.refs_0_), channel_id=1, source_target_pairs={{0,8},{1,9},{2,10},{3,11},{8,0},{9,1},{10,2},{11,3},{16,24},{17,25... | collective-permute-start | bytes 294920 | tf_op jit(solution)/shard_map/ppermute | solution.py:334
  33.2 1.0 %load_table.3.refs_1_ = bf16[1,2,768,1536]{3,2,1,0:T(8,128)(2,1)S(1)} custom-call(bf16[1,2,768,1536]{3,2,1,0:T(8,128)(2,1)S(1)} %bitcast.8), custom_call_target="tpu_custom_call" | custom-call | flops 1 | bytes 1 | tf_op jit(solution)/shard_map/load_table/pallas_call | solution.py:287
  34.2 1.6 %collective-permute-start.19 = (bf16[32,1536]{1,0:T(8,128)(2,1)S(1)}, bf16[32,1536]{1,0:T(8,128)(2,1)S(1)}, u32[]{:S(2)}, u32[]{:S(2)}) collective-permute-start(bf16[32,1536]{1,0:T(8,128)(2,1)S(1)} %get-tuple-element.82), channel_id=1, source_target_pairs={{0,4},{4,0},{1,5},{5,1},{2,6},{6,2},{3,7},{7,3},{8,12},{12,8},{9,1... | collective-permute-start | bytes 294920 | tf_op jit(solution)/shard_map/ppermute | solution.py:309
  36.6 0.9 %collective-permute-start.14 = (bf16[32,1536]{1,0:T(8,128)(2,1)S(1)}, bf16[32,1536]{1,0:T(8,128)(2,1)S(1)}, u32[]{:S(2)}, u32[]{:S(2)}) collective-permute-start(bf16[32,1536]{1,0:T(8,128)(2,1)S(1)} %fusion.refs_2_.addend_ref), channel_id=1, source_target_pairs={{0,2},{1,3},{2,0},{3,1},{4,6},{5,7},{6,4},{7,5},{8,10},{9,11},{10,... | collective-permute-start | bytes 294920 | tf_op jit(solution)/shard_map/ppermute | solution.py:318
  38.0 2.4 %collective-permute-done.16 = bf16[32,1536]{1,0:T(8,128)(2,1)S(1)} collective-permute-done((bf16[32,1536]{1,0:T(8,128)(2,1)S(1)}, bf16[32,1536]{1,0:T(8,128)(2,1)S(1)}, u32[]{:S(2)}, u32[]{:S(2)}) %collective-permute-start.16) | collective-permute-done | bytes 98336 | tf_op jit(solution)/shard_map/ppermute | solution.py:334
  41.7 1.0 %collective-permute-start.20 = (bf16[32,1536]{1,0:T(8,128)(2,1)S(1)}, bf16[32,1536]{1,0:T(8,128)(2,1)S(1)}, u32[]{:S(2)}, u32[]{:S(2)}) collective-permute-start(bf16[32,1536]{1,0:T(8,128)(2,1)S(1)} %fusion.1.refs_2_.addend_ref), channel_id=1, source_target_pairs={{0,2},{1,3},{2,0},{3,1},{4,6},{5,7},{6,4},{7,5},{8,10},{9,11},{10,... | collective-permute-start | bytes 294920 | tf_op jit(solution)/shard_map/ppermute | solution.py:318
  42.7 1.8 %collective-permute-done.14.refs_3_ = bf16[32,1536]{1,0:T(8,128)(2,1)S(1)} collective-permute-done((bf16[32,1536]{1,0:T(8,128)(2,1)S(1)}, bf16[32,1536]{1,0:T(8,128)(2,1)S(1)}, u32[]{:S(2)}, u32[]{:S(2)}) %collective-permute-start.14) | collective-permute-done | bytes 98336 | tf_op jit(solution)/shard_map/ppermute | solution.py:318
  44.5 0.9 %project.6 = (bf16[768,128]{1,0:T(8,128)(2,1)S(1)}, bf16[128,1536]{1,0:T(8,128)(2,1)S(1)}) custom-call(bf16[1040,128]{1,0:T(8,128)(2,1)S(1)} %concatenate.10.message_ref, bf16[1,2,768,1536]{3,2,1,0:T(8,128)(2,1)S(1)} %load_table.2.value_ref.refs_0_, bf16[1,2,768,1536]{3,2,1,0:T(8,128)(2,1)S(1)} %load_table.3.refs_1_, ...), custom_call_target="tpu_custom_call" | custom-call | flops 1 | bytes 1 | tf_op jit(solution)/shard_map/project/pallas_call | solution.py:83
  45.4 1.6 %collective-permute-start.24 = (bf16[768,128]{1,0:T(8,128)(2,1)S(1)}, bf16[768,128]{1,0:T(8,128)(2,1)S(1)}, u32[]{:S(2)}, u32[]{:S(2)}) collective-permute-start(bf16[768,128]{1,0:T(8,128)(2,1)S(1)} %get-tuple-element.81.mine_ref), channel_id=1, source_target_pairs={{0,4},{4,0},{1,5},{5,1},{2,6},{6,2},{3,7},{7,3},{8,12},{12,8},{9,1... | collective-permute-start | bytes 589832 | tf_op jit(solution)/shard_map/ppermute | solution.py:309
  46.9 1.8 %collective-permute-done.20.refs_3_ = bf16[32,1536]{1,0:T(8,128)(2,1)S(1)} collective-permute-done((bf16[32,1536]{1,0:T(8,128)(2,1)S(1)}, bf16[32,1536]{1,0:T(8,128)(2,1)S(1)}, u32[]{:S(2)}, u32[]{:S(2)}) %collective-permute-start.20) | collective-permute-done | bytes 98336 | tf_op jit(solution)/shard_map/ppermute | solution.py:318
  49.6 1.6 %collective-permute-start.23 = (bf16[768,128]{1,0:T(8,128)(2,1)S(1)}, bf16[768,128]{1,0:T(8,128)(2,1)S(1)}, u32[]{:S(2)}, u32[]{:S(2)}) collective-permute-start(bf16[768,128]{1,0:T(8,128)(2,1)S(1)} %get-tuple-element.83.mine_ref), channel_id=1, source_target_pairs={{0,4},{4,0},{1,5},{5,1},{2,6},{6,2},{3,7},{7,3},{8,12},{12,8},{9,1... | collective-permute-start | bytes 589832 | tf_op jit(solution)/shard_map/ppermute | solution.py:309
  51.1 1.2 %collective-permute-done.24.arrived_ref = bf16[768,128]{1,0:T(8,128)(2,1)S(1)} collective-permute-done((bf16[768,128]{1,0:T(8,128)(2,1)S(1)}, bf16[768,128]{1,0:T(8,128)(2,1)S(1)}, u32[]{:S(2)}, u32[]{:S(2)}) %collective-permute-start.24) | collective-permute-done | bytes 196640 | tf_op jit(solution)/shard_map/ppermute | solution.py:309
  53.3 3.2 %collective-permute-done.23.arrived_ref = bf16[768,128]{1,0:T(8,128)(2,1)S(1)} collective-permute-done((bf16[768,128]{1,0:T(8,128)(2,1)S(1)}, bf16[768,128]{1,0:T(8,128)(2,1)S(1)}, u32[]{:S(2)}, u32[]{:S(2)}) %collective-permute-start.23) | collective-permute-done | bytes 196640 | tf_op jit(solution)/shard_map/ppermute | solution.py:309
  57.7 1.6 %collective-permute-start.28 = (bf16[32,1536]{1,0:T(8,128)(2,1)S(1)}, bf16[32,1536]{1,0:T(8,128)(2,1)S(1)}, u32[]{:S(2)}, u32[]{:S(2)}) collective-permute-start(bf16[32,1536]{1,0:T(8,128)(2,1)S(1)} %get-tuple-element.87), channel_id=1, source_target_pairs={{0,4},{1,5},{2,6},{3,7},{4,0},{5,1},{6,2},{7,3},{8,12},{9,13},{10,... | collective-permute-start | bytes 294920 | tf_op jit(solution)/shard_map/ppermute | solution.py:326
  60.0 1.4 %collective-permute-start.27 = (bf16[32,1536]{1,0:T(8,128)(2,1)S(1)}, bf16[32,1536]{1,0:T(8,128)(2,1)S(1)}, u32[]{:S(2)}, u32[]{:S(2)}) collective-permute-start(bf16[32,1536]{1,0:T(8,128)(2,1)S(1)} %get-tuple-element.92), channel_id=1, source_target_pairs={{0,2},{1,3},{2,0},{3,1},{4,6},{5,7},{6,4},{7,5},{8,10},{9,11},{10,... | collective-permute-start | bytes 294920 | tf_op jit(solution)/shard_map/ppermute | solution.py:318
  61.4 3.5 %weight_grads.1 = (bf16[1,768,1536]{2,1,0:T(8,128)(2,1)}, bf16[1,768,1536]{2,1,0:T(8,128)(2,1)}) custom-call(bf16[768,128]{1,0:T(8,128)(2,1)S(1)} %get-tuple-element.93.a0, bf16[768,128]{1,0:T(8,128)(2,1)S(1)} %get-tuple-element.94.a1, bf16[768,128]{1,0:T(8,128)(2,1)S(1)} %get-tuple-element.97.b0, bf16[768,128]{1,0:T(8,128)(2,1)S(1)} %get-tuple-element.98.b1, ...), custom_call_target="tpu_custom_call" | custom-call | flops 1 | bytes 1 | tf_op jit(solution)/shard_map/weight_grads/pallas_call | solution.py:201
  65.4 0.9 %add_convert_fusion = bf16[32,1536]{1,0:T(8,128)(2,1)S(1)} fusion(bf16[32,1536]{1,0:T(8,128)(2,1)} %collective-permute-done.29, bf16[32,1536]{1,0:T(8,128)(2,1)S(1)} %collective-permute-done.28), kind=kLoop, calls=%fused_computation.3 | loop fusion | flops 196608 | bytes 294912 | tf_op jit(solution)/shard_map/convert_element_type | solution.py:423
  (62 shorter events, 14.1 us)
Async XLA Ops:
  1.7 5.8 %collective-permute-start = (bf16[32,1536]{1,0:T(8,128)(2,1)S(1)}, bf16[32,1536]{1,0:T(8,128)(2,1)S(1)}, u32[]{:S(2)}, u32[]{:S(2)}) collective-permute-start(bf16[32,1536]{1,0:T(8,128)(2,1)S(1)} %get-tuple-element.111), channel_id=1, source_target_pairs={{0,4},{4,0},{1,5},{5,1},{2,6},{6,2},{3,7},{7,3},{8,12},{12,8},{9,1... | collective-permute-start | bytes 294920 | tf_op jit(solution)/shard_map/ppermute | solution.py:309
  7.2 7.9 %collective-permute-start.2 = (bf16[1040,128]{1,0:T(8,128)(2,1)S(1)}, bf16[1040,128]{1,0:T(8,128)(2,1)S(1)}, u32[]{:S(2)}, u32[]{:S(2)}) collective-permute-start(bf16[1040,128]{1,0:T(8,128)(2,1)S(1)} %concatenate.10.message_ref), channel_id=1, source_target_pairs={{0,4},{4,0},{1,5},{5,1},{2,6},{6,2},{3,7},{7,3},{8,12},{12,8},{9,1... | collective-permute-start | bytes 798728 | tf_op jit(solution)/shard_map/ppermute | solution.py:309
  7.5 5.5 %collective-permute-start.3 = (bf16[32,1536]{1,0:T(8,128)(2,1)S(1)}, bf16[32,1536]{1,0:T(8,128)(2,1)S(1)}, u32[]{:S(2)}, u32[]{:S(2)}) collective-permute-start(bf16[32,1536]{1,0:T(8,128)(2,1)S(1)} %collective-permute-done.refs_1_.addend_ref), channel_id=1, source_target_pairs={{0,2},{1,3},{2,0},{3,1},{4,6},{5,7},{6,4},{7,5},{8,10},{9,11},{10,... | collective-permute-start | bytes 294920 | tf_op jit(solution)/shard_map/ppermute | solution.py:318
  9.4 4.7 %collective-permute-start.1 = (bf16[32,1536]{1,0:T(8,128)(2,1)S(1)}, bf16[32,1536]{1,0:T(8,128)(2,1)S(1)}, u32[]{:S(2)}, u32[]{:S(2)}) collective-permute-start(bf16[32,1536]{1,0:T(8,128)(2,1)S(1)} %get-tuple-element.64.refs_1_.addend_ref), channel_id=1, source_target_pairs={{0,2},{1,3},{2,0},{3,1},{4,6},{5,7},{6,4},{7,5},{8,10},{9,11},{10,... | collective-permute-start | bytes 294920 | tf_op jit(solution)/shard_map/ppermute | solution.py:318
  13.0 2.1 %collective-permute-start.4 = (bf16[32,1536]{1,0:T(8,128)(2,1)S(1)}, bf16[32,1536]{1,0:T(8,128)(2,1)S(1)}, u32[]{:S(2)}, u32[]{:S(2)}) collective-permute-start(bf16[32,1536]{1,0:T(8,128)(2,1)S(1)} %collective-permute-done.refs_1_.addend_ref), channel_id=1, source_target_pairs={{0,1},{1,0},{2,3},{3,2},{4,5},{5,4},{6,7},{7,6},{8,9},{9,8},{10,11... | collective-permute-start | bytes 294920 | tf_op jit(solution)/shard_map/ppermute | solution.py:312
  13.0 2.1 %collective-permute-start.5 = (bf16[32,1536]{1,0:T(8,128)(2,1)S(1)}, bf16[32,1536]{1,0:T(8,128)(2,1)S(1)}, u32[]{:S(2)}, u32[]{:S(2)}) collective-permute-start(bf16[32,1536]{1,0:T(8,128)(2,1)S(1)} %collective-permute-done.3.refs_2_), channel_id=1, source_target_pairs={{0,1},{1,0},{2,3},{3,2},{4,5},{5,4},{6,7},{7,6},{8,9},{9,8},{10,11... | collective-permute-start | bytes 294920 | tf_op jit(solution)/shard_map/ppermute | solution.py:312
  14.1 2.9 %collective-permute-start.6 = (bf16[32,1536]{1,0:T(8,128)(2,1)S(1)}, bf16[32,1536]{1,0:T(8,128)(2,1)S(1)}, u32[]{:S(2)}, u32[]{:S(2)}) collective-permute-start(bf16[32,1536]{1,0:T(8,128)(2,1)S(1)} %get-tuple-element.64.refs_1_.addend_ref), channel_id=1, source_target_pairs={{0,1},{1,0},{2,3},{3,2},{4,5},{5,4},{6,7},{7,6},{8,9},{9,8},{10,11... | collective-permute-start | bytes 294920 | tf_op jit(solution)/shard_map/ppermute | solution.py:312
  14.1 2.9 %collective-permute-start.7 = (bf16[32,1536]{1,0:T(8,128)(2,1)S(1)}, bf16[32,1536]{1,0:T(8,128)(2,1)S(1)}, u32[]{:S(2)}, u32[]{:S(2)}) collective-permute-start(bf16[32,1536]{1,0:T(8,128)(2,1)S(1)} %collective-permute-done.1.refs_2_), channel_id=1, source_target_pairs={{0,1},{1,0},{2,3},{3,2},{4,5},{5,4},{6,7},{7,6},{8,9},{9,8},{10,11... | collective-permute-start | bytes 294920 | tf_op jit(solution)/shard_map/ppermute | solution.py:312
  16.0 7.9 %collective-permute-start.8 = (bf16[768,128]{1,0:T(8,128)(2,1)S(1)}, bf16[768,128]{1,0:T(8,128)(2,1)S(1)}, u32[]{:S(2)}, u32[]{:S(2)}) collective-permute-start(bf16[768,128]{1,0:T(8,128)(2,1)S(1)} %get-tuple-element.60.mine_ref), channel_id=1, source_target_pairs={{0,4},{4,0},{1,5},{5,1},{2,6},{6,2},{3,7},{7,3},{8,12},{12,8},{9,1... | collective-permute-start | bytes 589832 | tf_op jit(solution)/shard_map/ppermute | solution.py:309
  17.9 8.9 %collective-permute-start.10 = (bf16[768,128]{1,0:T(8,128)(2,1)S(1)}, bf16[768,128]{1,0:T(8,128)(2,1)S(1)}, u32[]{:S(2)}, u32[]{:S(2)}) collective-permute-start(bf16[768,128]{1,0:T(8,128)(2,1)S(1)} %get-tuple-element.66.mine_ref), channel_id=1, source_target_pairs={{0,4},{4,0},{1,5},{5,1},{2,6},{6,2},{3,7},{7,3},{8,12},{12,8},{9,1... | collective-permute-start | bytes 589832 | tf_op jit(solution)/shard_map/ppermute | solution.py:309
  19.0 14.1 %slice-start = ((s8[4718592]{0:T(1024)(128)(4,1)}), s8[4194304]{0:T(1024)(128)(4,1)S(1)}, s32[]{:S(2)}) async-start(s8[4718592]{0:T(1024)(128)(4,1)} %bitcast.7), calls=%async_computation | async-start | bytes 8388608
  21.6 11.6 %slice-start.1 = ((s8[4718592]{0:T(1024)(128)(4,1)}), s8[524288]{0:T(1024)(128)(4,1)S(1)}, s32[]{:S(2)}) async-start(s8[4718592]{0:T(1024)(128)(4,1)} %bitcast.7), calls=%async_computation.1 | async-start | bytes 1048576
  24.9 3.0 %collective-permute-start.9 = (bf16[2,32,1536]{2,1,0:T(8,128)(2,1)S(1)}, bf16[2,32,1536]{2,1,0:T(8,128)(2,1)S(1)}, u32[]{:S(2)}, u32[]{:S(2)}) collective-permute-start(bf16[2,32,1536]{2,1,0:T(8,128)(2,1)S(1)} %get-tuple-element.69), channel_id=1, source_target_pairs={{0,1},{1,0},{2,3},{3,2},{4,5},{5,4},{6,7},{7,6},{8,9},{9,8},{10,11... | collective-permute-start | bytes 589832 | tf_op jit(solution)/shard_map/ppermute | solution.py:312
  27.8 3.0 %collective-permute-start.11 = (bf16[2,32,1536]{2,1,0:T(8,128)(2,1)S(1)}, bf16[2,32,1536]{2,1,0:T(8,128)(2,1)S(1)}, u32[]{:S(2)}, u32[]{:S(2)}) collective-permute-start(bf16[2,32,1536]{2,1,0:T(8,128)(2,1)S(1)} %get-tuple-element.74), channel_id=1, source_target_pairs={{0,1},{1,0},{2,3},{3,2},{4,5},{5,4},{6,7},{7,6},{8,9},{9,8},{10,11... | collective-permute-start | bytes 589832 | tf_op jit(solution)/shard_map/ppermute | solution.py:312
  28.0 7.8 %collective-permute-start.12 = (bf16[32,1536]{1,0:T(8,128)(2,1)S(1)}, bf16[32,1536]{1,0:T(8,128)(2,1)S(1)}, u32[]{:S(2)}, u32[]{:S(2)}) collective-permute-start(bf16[32,1536]{1,0:T(8,128)(2,1)S(1)} %get-tuple-element.70.refs_0_), channel_id=1, source_target_pairs={{0,8},{1,9},{2,10},{3,11},{8,0},{9,1},{10,2},{11,3},{16,24},{17,25... | collective-permute-start | bytes 294920 | tf_op jit(solution)/shard_map/ppermute | solution.py:334
  29.5 7.0 %collective-permute-start.13 = (bf16[32,1536]{1,0:T(8,128)(2,1)S(1)}, bf16[32,1536]{1,0:T(8,128)(2,1)S(1)}, u32[]{:S(2)}, u32[]{:S(2)}) collective-permute-start(bf16[32,1536]{1,0:T(8,128)(2,1)S(1)} %get-tuple-element.71.refs_1_), channel_id=1, source_target_pairs={{0,10},{1,11},{2,8},{3,9},{8,2},{9,3},{10,0},{11,1},{16,26},{17,27... | collective-permute-start | bytes 294920 | tf_op jit(solution)/shard_map/ppermute | solution.py:334
  30.9 7.1 %collective-permute-start.15 = (bf16[32,1536]{1,0:T(8,128)(2,1)S(1)}, bf16[32,1536]{1,0:T(8,128)(2,1)S(1)}, u32[]{:S(2)}, u32[]{:S(2)}) collective-permute-start(bf16[32,1536]{1,0:T(8,128)(2,1)S(1)} %get-tuple-element.75.refs_0_), channel_id=1, source_target_pairs={{0,8},{1,9},{2,10},{3,11},{8,0},{9,1},{10,2},{11,3},{16,24},{17,25... | collective-permute-start | bytes 294920 | tf_op jit(solution)/shard_map/ppermute | solution.py:334
  32.4 8.0 %collective-permute-start.16 = (bf16[32,1536]{1,0:T(8,128)(2,1)S(1)}, bf16[32,1536]{1,0:T(8,128)(2,1)S(1)}, u32[]{:S(2)}, u32[]{:S(2)}) collective-permute-start(bf16[32,1536]{1,0:T(8,128)(2,1)S(1)} %get-tuple-element.76.refs_1_), channel_id=1, source_target_pairs={{0,10},{1,11},{2,8},{3,9},{8,2},{9,3},{10,0},{11,1},{16,26},{17,27... | collective-permute-start | bytes 294920 | tf_op jit(solution)/shard_map/ppermute | solution.py:334
  34.2 6.2 %collective-permute-start.19 = (bf16[32,1536]{1,0:T(8,128)(2,1)S(1)}, bf16[32,1536]{1,0:T(8,128)(2,1)S(1)}, u32[]{:S(2)}, u32[]{:S(2)}) collective-permute-start(bf16[32,1536]{1,0:T(8,128)(2,1)S(1)} %get-tuple-element.82), channel_id=1, source_target_pairs={{0,4},{4,0},{1,5},{5,1},{2,6},{6,2},{3,7},{7,3},{8,12},{12,8},{9,1... | collective-permute-start | bytes 294920 | tf_op jit(solution)/shard_map/ppermute | solution.py:309
  36.6 6.1 %collective-permute-start.18 = (bf16[32,1536]{1,0:T(8,128)(2,1)S(1)}, bf16[32,1536]{1,0:T(8,128)(2,1)S(1)}, u32[]{:S(2)}, u32[]{:S(2)}) collective-permute-start(bf16[32,1536]{1,0:T(8,128)(2,1)S(1)} %fusion.refs_2_.addend_ref), channel_id=1, source_target_pairs={{0,3},{1,2},{2,1},{3,0},{4,7},{5,6},{6,5},{7,4},{8,11},{9,10},{10,... | collective-permute-start | bytes 294920 | tf_op jit(solution)/shard_map/ppermute | solution.py:318
  36.6 7.8 %collective-permute-start.14 = (bf16[32,1536]{1,0:T(8,128)(2,1)S(1)}, bf16[32,1536]{1,0:T(8,128)(2,1)S(1)}, u32[]{:S(2)}, u32[]{:S(2)}) collective-permute-start(bf16[32,1536]{1,0:T(8,128)(2,1)S(1)} %fusion.refs_2_.addend_ref), channel_id=1, source_target_pairs={{0,2},{1,3},{2,0},{3,1},{4,6},{5,7},{6,4},{7,5},{8,10},{9,11},{10,... | collective-permute-start | bytes 294920 | tf_op jit(solution)/shard_map/ppermute | solution.py:318
  40.4 1.3 %collective-permute-start.17 = (bf16[32,1536]{1,0:T(8,128)(2,1)S(1)}, bf16[32,1536]{1,0:T(8,128)(2,1)S(1)}, u32[]{:S(2)}, u32[]{:S(2)}) collective-permute-start(bf16[32,1536]{1,0:T(8,128)(2,1)S(1)} %fusion.refs_2_.addend_ref), channel_id=1, source_target_pairs={{0,1},{1,0},{2,3},{3,2},{4,5},{5,4},{6,7},{7,6},{8,9},{9,8},{10,11... | collective-permute-start | bytes 294920 | tf_op jit(solution)/shard_map/ppermute | solution.py:312
  40.5 6.5 %collective-permute-start.22 = (bf16[32,1536]{1,0:T(8,128)(2,1)S(1)}, bf16[32,1536]{1,0:T(8,128)(2,1)S(1)}, u32[]{:S(2)}, u32[]{:S(2)}) collective-permute-start(bf16[32,1536]{1,0:T(8,128)(2,1)S(1)} %fusion.1.refs_2_.addend_ref), channel_id=1, source_target_pairs={{0,3},{1,2},{2,1},{3,0},{4,7},{5,6},{6,5},{7,4},{8,11},{9,10},{10,... | collective-permute-start | bytes 294920 | tf_op jit(solution)/shard_map/ppermute | solution.py:318
  41.3 5.6 %collective-permute-start.21 = (bf16[32,1536]{1,0:T(8,128)(2,1)S(1)}, bf16[32,1536]{1,0:T(8,128)(2,1)S(1)}, u32[]{:S(2)}, u32[]{:S(2)}) collective-permute-start(bf16[32,1536]{1,0:T(8,128)(2,1)S(1)} %fusion.1.refs_2_.addend_ref), channel_id=1, source_target_pairs={{0,1},{1,0},{2,3},{3,2},{4,5},{5,4},{6,7},{7,6},{8,9},{9,8},{10,11... | collective-permute-start | bytes 294920 | tf_op jit(solution)/shard_map/ppermute | solution.py:312
  41.7 7.0 %collective-permute-start.20 = (bf16[32,1536]{1,0:T(8,128)(2,1)S(1)}, bf16[32,1536]{1,0:T(8,128)(2,1)S(1)}, u32[]{:S(2)}, u32[]{:S(2)}) collective-permute-start(bf16[32,1536]{1,0:T(8,128)(2,1)S(1)} %fusion.1.refs_2_.addend_ref), channel_id=1, source_target_pairs={{0,2},{1,3},{2,0},{3,1},{4,6},{5,7},{6,4},{7,5},{8,10},{9,11},{10,... | collective-permute-start | bytes 294920 | tf_op jit(solution)/shard_map/ppermute | solution.py:318
  45.4 7.0 %collective-permute-start.24 = (bf16[768,128]{1,0:T(8,128)(2,1)S(1)}, bf16[768,128]{1,0:T(8,128)(2,1)S(1)}, u32[]{:S(2)}, u32[]{:S(2)}) collective-permute-start(bf16[768,128]{1,0:T(8,128)(2,1)S(1)} %get-tuple-element.81.mine_ref), channel_id=1, source_target_pairs={{0,4},{4,0},{1,5},{5,1},{2,6},{6,2},{3,7},{7,3},{8,12},{12,8},{9,1... | collective-permute-start | bytes 589832 | tf_op jit(solution)/shard_map/ppermute | solution.py:309
  49.6 7.0 %collective-permute-start.23 = (bf16[768,128]{1,0:T(8,128)(2,1)S(1)}, bf16[768,128]{1,0:T(8,128)(2,1)S(1)}, u32[]{:S(2)}, u32[]{:S(2)}) collective-permute-start(bf16[768,128]{1,0:T(8,128)(2,1)S(1)} %get-tuple-element.83.mine_ref), channel_id=1, source_target_pairs={{0,4},{4,0},{1,5},{5,1},{2,6},{6,2},{3,7},{7,3},{8,12},{12,8},{9,1... | collective-permute-start | bytes 589832 | tf_op jit(solution)/shard_map/ppermute | solution.py:309
  53.3 4.3 %collective-permute-start.25 = (bf16[2,32,1536]{2,1,0:T(8,128)(2,1)S(1)}, bf16[2,32,1536]{2,1,0:T(8,128)(2,1)S(1)}, u32[]{:S(2)}, u32[]{:S(2)}) collective-permute-start(bf16[2,32,1536]{2,1,0:T(8,128)(2,1)S(1)} %get-tuple-element.86), channel_id=1, source_target_pairs={{0,1},{1,0},{2,3},{3,2},{4,5},{5,4},{6,7},{7,6},{8,9},{9,8},{10,11... | collective-permute-start | bytes 589832 | tf_op jit(solution)/shard_map/ppermute | solution.py:312
  57.5 2.4 %collective-permute-start.26 = (bf16[2,32,1536]{2,1,0:T(8,128)(2,1)S(1)}, bf16[2,32,1536]{2,1,0:T(8,128)(2,1)S(1)}, u32[]{:S(2)}, u32[]{:S(2)}) collective-permute-start(bf16[2,32,1536]{2,1,0:T(8,128)(2,1)S(1)} %get-tuple-element.90), channel_id=1, source_target_pairs={{0,1},{1,0},{2,3},{3,2},{4,5},{5,4},{6,7},{7,6},{8,9},{9,8},{10,11... | collective-permute-start | bytes 589832 | tf_op jit(solution)/shard_map/ppermute | solution.py:312
  57.7 7.2 %collective-permute-start.28 = (bf16[32,1536]{1,0:T(8,128)(2,1)S(1)}, bf16[32,1536]{1,0:T(8,128)(2,1)S(1)}, u32[]{:S(2)}, u32[]{:S(2)}) collective-permute-start(bf16[32,1536]{1,0:T(8,128)(2,1)S(1)} %get-tuple-element.87), channel_id=1, source_target_pairs={{0,4},{1,5},{2,6},{3,7},{4,0},{5,1},{6,2},{7,3},{8,12},{9,13},{10,... | collective-permute-start | bytes 294920 | tf_op jit(solution)/shard_map/ppermute | solution.py:326
  59.2 6.2 %collective-permute-start.29 = (bf16[32,1536]{1,0:T(8,128)(2,1)S(1)}, bf16[32,1536]{1,0:T(8,128)(2,1)}, u32[]{:S(2)}, u32[]{:S(2)}) collective-permute-start(bf16[32,1536]{1,0:T(8,128)(2,1)S(1)} %get-tuple-element.88), channel_id=1, source_target_pairs={{0,6},{1,7},{2,4},{3,5},{4,2},{5,3},{6,0},{7,1},{8,14},{9,15},{10,... | collective-permute-start | bytes 294920 | tf_op jit(solution)/shard_map/ppermute | solution.py:326
  60.0 6.8 %collective-permute-start.27 = (bf16[32,1536]{1,0:T(8,128)(2,1)S(1)}, bf16[32,1536]{1,0:T(8,128)(2,1)S(1)}, u32[]{:S(2)}, u32[]{:S(2)}) collective-permute-start(bf16[32,1536]{1,0:T(8,128)(2,1)S(1)} %get-tuple-element.92), channel_id=1, source_target_pairs={{0,2},{1,3},{2,0},{3,1},{4,6},{5,7},{6,4},{7,5},{8,10},{9,11},{10,... | collective-permute-start | bytes 294920 | tf_op jit(solution)/shard_map/ppermute | solution.py:318
  (1 other events, 1.8 us)

commit v17 on v16

--- a/solution.py
+++ b/solution.py
@@ -401,7 +401,12 @@
         if m == 0:
             swapped, _ = lax.optimization_barrier((swapped, last_received))
         theirs = [swap_core(swapped)]
-        theirs += [to_row(second_piece[m], delta, 1) for delta in range(1, outer)]
+        for delta in range(1, outer):
+            if m == 0:
+                theirs.append(to_row(second_piece[m], delta, 1))
+            else:
+                late, _ = lax.optimization_barrier((mine[delta], partial[0]))
+                theirs.append(swap_core(late))
         partial[m], second_full[m] = project(
             shard, probs[m], (value_table, out_table), mine, theirs
         )
@@ -420,6 +425,7 @@
     grad_value, grad_out = weight_grads(
         first_result, second_result, first_full, second_full
     )
+    other_parts, _ = lax.optimization_barrier((other_parts, grad_value))
     other_grad = lax.optimization_barrier(total(other_parts).astype(jnp.bfloat16))
     own_parts, _ = lax.optimization_barrier((own_parts, grad_value))
     own_grad = total(own_parts).astype(jnp.bfloat16)

time: 67.7 us -> 69.3 us (1.024)
  waiting for transfers between devices: 19.6 us -> 22.2 us
  starting transfers between devices: 24.7 us -> 23.6 us
    ppermute x7, waiting for transfers between devices: 9.34 us -> 11.7 us  [swap_half(): return lax.ppermute(array, 'half', [(0, 1), (1, 0)])]
    ppermute x7 -> x6, starting transfers between devices: 6.18 us -> 5.11 us  [to_row(): return lax.ppermute(array, ('outer', 'core'), pairs)]
    ppermute x7 -> x6, waiting for transfers between devices: 5.66 us -> 6.08 us  [to_row(): return lax.ppermute(array, ('outer', 'core'), pairs)]
    ppermute x10 -> x11, starting transfers between devices: 1.31 us -> 1.65 us  [swap_core(): return lax.ppermute(array, 'core', [(0, 1), (1, 0)])]
  transfers between devices with their start and end apart: 30 -> 30, of which waited for: 16 -> 17; matrix products, arithmetic and copies ran while one was open for 3% -> 3% of each run, Pallas kernels for 26% -> 26%
where the time goes in v17:
time: 69.3 us; the launch traced here: 69.1 us
  starting transfers between devices  23.6 us (34%)
  waiting for transfers between devices  22.2 us (32%)
  Pallas kernels  17.8 us (26%)
  other arithmetic  3.84 us (6%)
  between operations  1.54 us (2%)
    ppermute x7, waiting for transfers between devices, swap_half(): return lax.ppermute(array, 'half', [(0, 1), (1, 0)])  11.7 us
    ppermute x7, starting transfers between devices, swap_half(): return lax.ppermute(array, 'half', [(0, 1), (1, 0)])  9.54 us
    ppermute x6, waiting for transfers between devices, to_row(): return lax.ppermute(array, ('outer', 'core'), pairs)  6.08 us
    ppermute x6, starting transfers between devices, to_row(): return lax.ppermute(array, ('outer', 'core'), pairs)  5.11 us
    ppermute x4, starting transfers between devices, swap_section(): return lax.ppermute(array, ('pair', 'outer', 'core'), pairs)  5.08 us
    pallas_call x4, Pallas kernels, mix(): pl.pallas_call(functools.partial(mix_kernel, outer, odd_phase), out_shape...  3.83 us
    ppermute x4, waiting for transfers between devices, swap_section(): return lax.ppermute(array, ('pair', 'outer', 'core'), pairs)  3.61 us
    pallas_call x2, Pallas kernels, load_table(): pl.pallas_call(load_kernel, out_shape=jax.ShapeDtypeStruct(table.shape, j...  3.57 us
  transfers between devices with their start and end apart: 30, of which 17 were waited for; matrix products, arithmetic and copies ran while one was open for 3% of the time, Pallas kernels for 26%

profile of v17, /device:TPU:0, one launch (start us, length us, event | category | flops | bytes accessed | tf_op | source)
XLA Modules:
  0.0 69.1 jit_solution(17130357877207555513)
XLA Ops:
  0.6 1.0 %bitcast_select_fusion = bf16[32,3072]{1,0:T(8,128)(2,1)S(1)} fusion(bf16[1,32,3072]{2,1,0:T(8,128)(2,1)} %param.10, pred[]{:T(512)S(6)} %eq.8, bf16[1,32,3072]{2,1,0:T(8,128)(2,1)} %param.7), kind=kLoop, calls=%fused_computation.2 | loop fusion | flops 98304 | bytes 589825 | tf_op jit(solution)/shard_map/jit(_where)/select_n | solution.py:351
  1.7 3.0 %collective-permute-start = (bf16[32,1536]{1,0:T(8,128)(2,1)S(1)}, bf16[32,1536]{1,0:T(8,128)(2,1)S(1)}, u32[]{:S(2)}, u32[]{:S(2)}) collective-permute-start(bf16[32,1536]{1,0:T(8,128)(2,1)S(1)} %get-tuple-element.117), channel_id=1, source_target_pairs={{0,4},{4,0},{1,5},{5,1},{2,6},{6,2},{3,7},{7,3},{8,12},{12,8},{9,1... | collective-permute-start | bytes 294920 | tf_op jit(solution)/shard_map/ppermute | solution.py:309
  4.7 1.1 %pad_maximum_fusion.stash_ref = bf16[2,768,128]{2,1,0:T(8,128)(2,1)S(1)} fusion(bf16[1,768,128]{2,1,0:T(8,128)(2,1)} %param.9, bf16[1,768,128]{2,1,0:T(8,128)(2,1)} %param.8), kind=kLoop, calls=%fused_computation | loop fusion | flops 196608 | bytes 786432 | tf_op jit(solution)/shard_map/concatenate | solution.py:357
  7.5 1.9 %collective-permute-start.3 = (bf16[32,1536]{1,0:T(8,128)(2,1)S(1)}, bf16[32,1536]{1,0:T(8,128)(2,1)S(1)}, u32[]{:S(2)}, u32[]{:S(2)}) collective-permute-start(bf16[32,1536]{1,0:T(8,128)(2,1)S(1)} %collective-permute-done.refs_1_.addend_ref), channel_id=1, source_target_pairs={{0,2},{1,3},{2,0},{3,1},{4,6},{5,7},{6,4},{7,5},{8,10},{9,11},{10,... | collective-permute-start | bytes 294920 | tf_op jit(solution)/shard_map/ppermute | solution.py:318
  9.5 2.4 %load_first.1.refs_0_ = bf16[1,2,768,1536]{3,2,1,0:T(8,128)(2,1)S(1)} custom-call(bf16[1,2,768,1536]{3,2,1,0:T(8,128)(2,1)} %source_ref, bf16[1,2,768,1536]{3,2,1,0:T(8,128)(2,1)} %source_ref.1), custom_call_target="tpu_custom_call" | custom-call | flops 1 | bytes 1 | tf_op jit(solution)/shard_map/load_first/pallas_call | solution.py:274
  11.9 1.1 %collective-permute-done.3.refs_2_ = bf16[32,1536]{1,0:T(8,128)(2,1)S(1)} collective-permute-done((bf16[32,1536]{1,0:T(8,128)(2,1)S(1)}, bf16[32,1536]{1,0:T(8,128)(2,1)S(1)}, u32[]{:S(2)}, u32[]{:S(2)}) %collective-permute-start.3) | collective-permute-done | bytes 98336 | tf_op jit(solution)/shard_map/ppermute | solution.py:318
  16.0 1.0 %collective-permute-start.8 = (bf16[768,128]{1,0:T(8,128)(2,1)S(1)}, bf16[768,128]{1,0:T(8,128)(2,1)S(1)}, u32[]{:S(2)}, u32[]{:S(2)}) collective-permute-start(bf16[768,128]{1,0:T(8,128)(2,1)S(1)} %get-tuple-element.63.mine_ref), channel_id=1, source_target_pairs={{0,4},{4,0},{1,5},{5,1},{2,6},{6,2},{3,7},{7,3},{8,12},{12,8},{9,1... | collective-permute-start | bytes 589832 | tf_op jit(solution)/shard_map/ppermute | solution.py:309
  17.9 1.1 %collective-permute-start.10 = (bf16[768,128]{1,0:T(8,128)(2,1)S(1)}, bf16[768,128]{1,0:T(8,128)(2,1)S(1)}, u32[]{:S(2)}, u32[]{:S(2)}) collective-permute-start(bf16[768,128]{1,0:T(8,128)(2,1)S(1)} %get-tuple-element.69.mine_ref), channel_id=1, source_target_pairs={{0,4},{4,0},{1,5},{5,1},{2,6},{6,2},{3,7},{7,3},{8,12},{12,8},{9,1... | collective-permute-start | bytes 589832 | tf_op jit(solution)/shard_map/ppermute | solution.py:309
  19.0 2.5 %load_table.2.value_ref.refs_0_ = bf16[1,2,768,1536]{3,2,1,0:T(8,128)(2,1)S(1)} custom-call(bf16[1,2,768,1536]{3,2,1,0:T(8,128)(2,1)} %source_ref), custom_call_target="tpu_custom_call" | custom-call | flops 1 | bytes 1 | tf_op jit(solution)/shard_map/load_table/pallas_call | solution.py:287
  21.6 2.3 %collective-permute-done.8.arrived_ref = bf16[768,128]{1,0:T(8,128)(2,1)S(1)} collective-permute-done((bf16[768,128]{1,0:T(8,128)(2,1)S(1)}, bf16[768,128]{1,0:T(8,128)(2,1)S(1)}, u32[]{:S(2)}, u32[]{:S(2)}) %collective-permute-start.8) | collective-permute-done | bytes 196640 | tf_op jit(solution)/shard_map/ppermute | solution.py:309
  23.9 1.0 %mix.4 = (bf16[768,128]{1,0:T(8,128)(2,1)S(1)}, bf16[2,32,1536]{2,1,0:T(8,128)(2,1)S(1)}, bf16[2,32,1536]{2,1,0:T(8,128)(2,1)S(1)}) custom-call(bf16[1040,128]{1,0:T(8,128)(2,1)S(1)} %concatenate.10.message_ref, bf16[1,2,768,1536]{3,2,1,0:T(8,128)(2,1)S(1)} %load_table.2.value_ref.refs_0_, bf16[768,128]{1,0:T(8,128)(2,1)S(1)} %get-tuple-element.69.mine_ref, ...), custom_call_target="tpu_custom_call" | custom-call | flops 1 | bytes 1 | tf_op jit(solution)/shard_map/mix/pallas_call | solution.py:141
  25.0 1.8 %collective-permute-done.10.arrived_ref = bf16[768,128]{1,0:T(8,128)(2,1)S(1)} collective-permute-done((bf16[768,128]{1,0:T(8,128)(2,1)S(1)}, bf16[768,128]{1,0:T(8,128)(2,1)S(1)}, u32[]{:S(2)}, u32[]{:S(2)}) %collective-permute-start.10) | collective-permute-done | bytes 196640 | tf_op jit(solution)/shard_map/ppermute | solution.py:309
  26.8 1.0 %mix.5 = (bf16[768,128]{1,0:T(8,128)(2,1)S(1)}, bf16[2,32,1536]{2,1,0:T(8,128)(2,1)S(1)}, bf16[2,32,1536]{2,1,0:T(8,128)(2,1)S(1)}) custom-call(bf16[1040,128]{1,0:T(8,128)(2,1)S(1)} %collective-permute-done.2.message_ref, bf16[1,2,768,1536]{3,2,1,0:T(8,128)(2,1)S(1)} %load_table.2.value_ref.refs_0_, bf16[768,128]{1,0:T(8,128)(2,1)S(1)} %get-tuple-element.63.mine_ref, ...), custom_call_target="tpu_custom_call" | custom-call | flops 1 | bytes 1 | tf_op jit(solution)/shard_map/mix/pallas_call | solution.py:141
  28.0 1.5 %collective-permute-start.12 = (bf16[32,1536]{1,0:T(8,128)(2,1)S(1)}, bf16[32,1536]{1,0:T(8,128)(2,1)S(1)}, u32[]{:S(2)}, u32[]{:S(2)}) collective-permute-start(bf16[32,1536]{1,0:T(8,128)(2,1)S(1)} %get-tuple-element.73.refs_0_), channel_id=1, source_target_pairs={{0,8},{1,9},{2,10},{3,11},{8,0},{9,1},{10,2},{11,3},{16,24},{17,25... | collective-permute-start | bytes 294920 | tf_op jit(solution)/shard_map/ppermute | solution.py:334
  29.5 1.4 %collective-permute-start.13 = (bf16[32,1536]{1,0:T(8,128)(2,1)S(1)}, bf16[32,1536]{1,0:T(8,128)(2,1)S(1)}, u32[]{:S(2)}, u32[]{:S(2)}) collective-permute-start(bf16[32,1536]{1,0:T(8,128)(2,1)S(1)} %get-tuple-element.74.refs_1_), channel_id=1, source_target_pairs={{0,10},{1,11},{2,8},{3,9},{8,2},{9,3},{10,0},{11,1},{16,26},{17,27... | collective-permute-start | bytes 294920 | tf_op jit(solution)/shard_map/ppermute | solution.py:334
  30.9 1.5 %collective-permute-start.15 = (bf16[32,1536]{1,0:T(8,128)(2,1)S(1)}, bf16[32,1536]{1,0:T(8,128)(2,1)S(1)}, u32[]{:S(2)}, u32[]{:S(2)}) collective-permute-start(bf16[32,1536]{1,0:T(8,128)(2,1)S(1)} %get-tuple-element.78.refs_0_), channel_id=1, source_target_pairs={{0,8},{1,9},{2,10},{3,11},{8,0},{9,1},{10,2},{11,3},{16,24},{17,25... | collective-permute-start | bytes 294920 | tf_op jit(solution)/shard_map/ppermute | solution.py:334
  33.2 1.0 %load_table.3.refs_1_ = bf16[1,2,768,1536]{3,2,1,0:T(8,128)(2,1)S(1)} custom-call(bf16[1,2,768,1536]{3,2,1,0:T(8,128)(2,1)S(1)} %bitcast.8), custom_call_target="tpu_custom_call" | custom-call | flops 1 | bytes 1 | tf_op jit(solution)/shard_map/load_table/pallas_call | solution.py:287
  34.2 1.6 %collective-permute-start.19 = (bf16[32,1536]{1,0:T(8,128)(2,1)S(1)}, bf16[32,1536]{1,0:T(8,128)(2,1)S(1)}, u32[]{:S(2)}, u32[]{:S(2)}) collective-permute-start(bf16[32,1536]{1,0:T(8,128)(2,1)S(1)} %get-tuple-element.85), channel_id=1, source_target_pairs={{0,4},{4,0},{1,5},{5,1},{2,6},{6,2},{3,7},{7,3},{8,12},{12,8},{9,1... | collective-permute-start | bytes 294920 | tf_op jit(solution)/shard_map/ppermute | solution.py:309
  36.6 0.9 %collective-permute-start.14 = (bf16[32,1536]{1,0:T(8,128)(2,1)S(1)}, bf16[32,1536]{1,0:T(8,128)(2,1)S(1)}, u32[]{:S(2)}, u32[]{:S(2)}) collective-permute-start(bf16[32,1536]{1,0:T(8,128)(2,1)S(1)} %fusion.refs_2_.addend_ref), channel_id=1, source_target_pairs={{0,2},{1,3},{2,0},{3,1},{4,6},{5,7},{6,4},{7,5},{8,10},{9,11},{10,... | collective-permute-start | bytes 294920 | tf_op jit(solution)/shard_map/ppermute | solution.py:318
  38.0 2.4 %collective-permute-done.16 = bf16[32,1536]{1,0:T(8,128)(2,1)S(1)} collective-permute-done((bf16[32,1536]{1,0:T(8,128)(2,1)S(1)}, bf16[32,1536]{1,0:T(8,128)(2,1)S(1)}, u32[]{:S(2)}, u32[]{:S(2)}) %collective-permute-start.16) | collective-permute-done | bytes 98336 | tf_op jit(solution)/shard_map/ppermute | solution.py:334
  42.5 2.0 %collective-permute-done.14.refs_3_ = bf16[32,1536]{1,0:T(8,128)(2,1)S(1)} collective-permute-done((bf16[32,1536]{1,0:T(8,128)(2,1)S(1)}, bf16[32,1536]{1,0:T(8,128)(2,1)S(1)}, u32[]{:S(2)}, u32[]{:S(2)}) %collective-permute-start.14) | collective-permute-done | bytes 98336 | tf_op jit(solution)/shard_map/ppermute | solution.py:318
  44.5 0.9 %project.6 = (bf16[768,128]{1,0:T(8,128)(2,1)S(1)}, bf16[128,1536]{1,0:T(8,128)(2,1)S(1)}) custom-call(bf16[1040,128]{1,0:T(8,128)(2,1)S(1)} %concatenate.10.message_ref, bf16[1,2,768,1536]{3,2,1,0:T(8,128)(2,1)S(1)} %load_table.2.value_ref.refs_0_, bf16[1,2,768,1536]{3,2,1,0:T(8,128)(2,1)S(1)} %load_table.3.refs_1_, ...), custom_call_target="tpu_custom_call" | custom-call | flops 1 | bytes 1 | tf_op jit(solution)/shard_map/project/pallas_call | solution.py:83
  45.4 1.2 %collective-permute-done.20.refs_3_ = bf16[32,1536]{1,0:T(8,128)(2,1)S(1)} collective-permute-done((bf16[32,1536]{1,0:T(8,128)(2,1)S(1)}, bf16[32,1536]{1,0:T(8,128)(2,1)S(1)}, u32[]{:S(2)}, u32[]{:S(2)}) %collective-permute-start.20) | collective-permute-done | bytes 98336 | tf_op jit(solution)/shard_map/ppermute | solution.py:318
  46.7 1.5 %collective-permute-start.24 = (bf16[768,128]{1,0:T(8,128)(2,1)S(1)}, bf16[768,128]{1,0:T(8,128)(2,1)S(1)}, u32[]{:S(2)}, u32[]{:S(2)}) collective-permute-start(bf16[768,128]{1,0:T(8,128)(2,1)S(1)} %get-tuple-element.84.mine_ref), channel_id=1, source_target_pairs={{0,4},{4,0},{1,5},{5,1},{2,6},{6,2},{3,7},{7,3},{8,12},{12,8},{9,1... | collective-permute-start | bytes 589832 | tf_op jit(solution)/shard_map/ppermute | solution.py:309
  49.1 1.2 %collective-permute-start.23 = (bf16[768,128]{1,0:T(8,128)(2,1)S(1)}, bf16[768,128]{1,0:T(8,128)(2,1)S(1)}, u32[]{:S(2)}, u32[]{:S(2)}) collective-permute-start(bf16[768,128]{1,0:T(8,128)(2,1)S(1)} %get-tuple-element.87.mine_ref), channel_id=1, source_target_pairs={{0,4},{4,0},{1,5},{5,1},{2,6},{6,2},{3,7},{7,3},{8,12},{12,8},{9,1... | collective-permute-start | bytes 589832 | tf_op jit(solution)/shard_map/ppermute | solution.py:309
  50.4 4.1 %collective-permute-done.24.arrived_ref = bf16[768,128]{1,0:T(8,128)(2,1)S(1)} collective-permute-done((bf16[768,128]{1,0:T(8,128)(2,1)S(1)}, bf16[768,128]{1,0:T(8,128)(2,1)S(1)}, u32[]{:S(2)}, u32[]{:S(2)}) %collective-permute-start.24) | collective-permute-done | bytes 196640 | tf_op jit(solution)/shard_map/ppermute | solution.py:309
  55.4 2.7 %collective-permute-done.23.arrived_ref = bf16[768,128]{1,0:T(8,128)(2,1)S(1)} collective-permute-done((bf16[768,128]{1,0:T(8,128)(2,1)S(1)}, bf16[768,128]{1,0:T(8,128)(2,1)S(1)}, u32[]{:S(2)}, u32[]{:S(2)}) %collective-permute-start.23) | collective-permute-done | bytes 196640 | tf_op jit(solution)/shard_map/ppermute | solution.py:309
  58.1 0.9 %mix.6 = (bf16[768,128]{1,0:T(8,128)(2,1)S(1)}, bf16[2,32,1536]{2,1,0:T(8,128)(2,1)S(1)}, bf16[2,32,1536]{2,1,0:T(8,128)(2,1)S(1)}) custom-call(bf16[1040,128]{1,0:T(8,128)(2,1)S(1)} %concatenate.10.message_ref, bf16[1,2,768,1536]{3,2,1,0:T(8,128)(2,1)S(1)} %load_table.2.value_ref.refs_0_, bf16[768,128]{1,0:T(8,128)(2,1)S(1)} %get-tuple-element.84.mine_ref, ...), custom_call_target="tpu_custom_call" | custom-call | flops 1 | bytes 1 | tf_op jit(solution)/shard_map/mix/pallas_call | solution.py:141
  59.2 1.6 %collective-permute-start.28 = (bf16[32,1536]{1,0:T(8,128)(2,1)S(1)}, bf16[32,1536]{1,0:T(8,128)(2,1)S(1)}, u32[]{:S(2)}, u32[]{:S(2)}) collective-permute-start(bf16[32,1536]{1,0:T(8,128)(2,1)S(1)} %get-tuple-element.91), channel_id=1, source_target_pairs={{0,4},{1,5},{2,6},{3,7},{4,0},{5,1},{6,2},{7,3},{8,12},{9,13},{10,... | collective-permute-start | bytes 294920 | tf_op jit(solution)/shard_map/ppermute | solution.py:326
  61.5 1.4 %collective-permute-start.27 = (bf16[32,1536]{1,0:T(8,128)(2,1)S(1)}, bf16[32,1536]{1,0:T(8,128)(2,1)S(1)}, u32[]{:S(2)}, u32[]{:S(2)}) collective-permute-start(bf16[32,1536]{1,0:T(8,128)(2,1)S(1)} %get-tuple-element.96), channel_id=1, source_target_pairs={{0,2},{1,3},{2,0},{3,1},{4,6},{5,7},{6,4},{7,5},{8,10},{9,11},{10,... | collective-permute-start | bytes 294920 | tf_op jit(solution)/shard_map/ppermute | solution.py:318
  62.9 3.5 %weight_grads.1 = (bf16[1,768,1536]{2,1,0:T(8,128)(2,1)}, bf16[1,768,1536]{2,1,0:T(8,128)(2,1)}) custom-call(bf16[768,128]{1,0:T(8,128)(2,1)S(1)} %get-tuple-element.97.a0, bf16[768,128]{1,0:T(8,128)(2,1)S(1)} %get-tuple-element.98.a1, bf16[768,128]{1,0:T(8,128)(2,1)S(1)} %get-tuple-element.101.b0, bf16[768,128]{1,0:T(8,128)(2,1)S(1)} %get-tuple-element.102.b1, ...), custom_call_target="tpu_custom_call" | custom-call | flops 1 | bytes 1 | tf_op jit(solution)/shard_map/weight_grads/pallas_call | solution.py:201
  66.9 0.9 %add_convert_fusion = bf16[32,1536]{1,0:T(8,128)(2,1)S(1)} fusion(bf16[32,1536]{1,0:T(8,128)(2,1)} %collective-permute-done.29, bf16[32,1536]{1,0:T(8,128)(2,1)S(1)} %collective-permute-done.28), kind=kLoop, calls=%fused_computation.3 | loop fusion | flops 196608 | bytes 294912 | tf_op jit(solution)/shard_map/convert_element_type | solution.py:429
  (62 shorter events, 14.1 us)
Async XLA Ops:
  1.7 5.8 %collective-permute-start = (bf16[32,1536]{1,0:T(8,128)(2,1)S(1)}, bf16[32,1536]{1,0:T(8,128)(2,1)S(1)}, u32[]{:S(2)}, u32[]{:S(2)}) collective-permute-start(bf16[32,1536]{1,0:T(8,128)(2,1)S(1)} %get-tuple-element.117), channel_id=1, source_target_pairs={{0,4},{4,0},{1,5},{5,1},{2,6},{6,2},{3,7},{7,3},{8,12},{12,8},{9,1... | collective-permute-start | bytes 294920 | tf_op jit(solution)/shard_map/ppermute | solution.py:309
  7.2 7.9 %collective-permute-start.2 = (bf16[1040,128]{1,0:T(8,128)(2,1)S(1)}, bf16[1040,128]{1,0:T(8,128)(2,1)S(1)}, u32[]{:S(2)}, u32[]{:S(2)}) collective-permute-start(bf16[1040,128]{1,0:T(8,128)(2,1)S(1)} %concatenate.10.message_ref), channel_id=1, source_target_pairs={{0,4},{4,0},{1,5},{5,1},{2,6},{6,2},{3,7},{7,3},{8,12},{12,8},{9,1... | collective-permute-start | bytes 798728 | tf_op jit(solution)/shard_map/ppermute | solution.py:309
  7.5 5.5 %collective-permute-start.3 = (bf16[32,1536]{1,0:T(8,128)(2,1)S(1)}, bf16[32,1536]{1,0:T(8,128)(2,1)S(1)}, u32[]{:S(2)}, u32[]{:S(2)}) collective-permute-start(bf16[32,1536]{1,0:T(8,128)(2,1)S(1)} %collective-permute-done.refs_1_.addend_ref), channel_id=1, source_target_pairs={{0,2},{1,3},{2,0},{3,1},{4,6},{5,7},{6,4},{7,5},{8,10},{9,11},{10,... | collective-permute-start | bytes 294920 | tf_op jit(solution)/shard_map/ppermute | solution.py:318
  9.4 4.7 %collective-permute-start.1 = (bf16[32,1536]{1,0:T(8,128)(2,1)S(1)}, bf16[32,1536]{1,0:T(8,128)(2,1)S(1)}, u32[]{:S(2)}, u32[]{:S(2)}) collective-permute-start(bf16[32,1536]{1,0:T(8,128)(2,1)S(1)} %get-tuple-element.67.refs_1_.addend_ref), channel_id=1, source_target_pairs={{0,2},{1,3},{2,0},{3,1},{4,6},{5,7},{6,4},{7,5},{8,10},{9,11},{10,... | collective-permute-start | bytes 294920 | tf_op jit(solution)/shard_map/ppermute | solution.py:318
  13.0 2.1 %collective-permute-start.4 = (bf16[32,1536]{1,0:T(8,128)(2,1)S(1)}, bf16[32,1536]{1,0:T(8,128)(2,1)S(1)}, u32[]{:S(2)}, u32[]{:S(2)}) collective-permute-start(bf16[32,1536]{1,0:T(8,128)(2,1)S(1)} %collective-permute-done.refs_1_.addend_ref), channel_id=1, source_target_pairs={{0,1},{1,0},{2,3},{3,2},{4,5},{5,4},{6,7},{7,6},{8,9},{9,8},{10,11... | collective-permute-start | bytes 294920 | tf_op jit(solution)/shard_map/ppermute | solution.py:312
  13.0 2.1 %collective-permute-start.5 = (bf16[32,1536]{1,0:T(8,128)(2,1)S(1)}, bf16[32,1536]{1,0:T(8,128)(2,1)S(1)}, u32[]{:S(2)}, u32[]{:S(2)}) collective-permute-start(bf16[32,1536]{1,0:T(8,128)(2,1)S(1)} %collective-permute-done.3.refs_2_), channel_id=1, source_target_pairs={{0,1},{1,0},{2,3},{3,2},{4,5},{5,4},{6,7},{7,6},{8,9},{9,8},{10,11... | collective-permute-start | bytes 294920 | tf_op jit(solution)/shard_map/ppermute | solution.py:312
  14.1 2.9 %collective-permute-start.6 = (bf16[32,1536]{1,0:T(8,128)(2,1)S(1)}, bf16[32,1536]{1,0:T(8,128)(2,1)S(1)}, u32[]{:S(2)}, u32[]{:S(2)}) collective-permute-start(bf16[32,1536]{1,0:T(8,128)(2,1)S(1)} %get-tuple-element.67.refs_1_.addend_ref), channel_id=1, source_target_pairs={{0,1},{1,0},{2,3},{3,2},{4,5},{5,4},{6,7},{7,6},{8,9},{9,8},{10,11... | collective-permute-start | bytes 294920 | tf_op jit(solution)/shard_map/ppermute | solution.py:312
  14.1 2.9 %collective-permute-start.7 = (bf16[32,1536]{1,0:T(8,128)(2,1)S(1)}, bf16[32,1536]{1,0:T(8,128)(2,1)S(1)}, u32[]{:S(2)}, u32[]{:S(2)}) collective-permute-start(bf16[32,1536]{1,0:T(8,128)(2,1)S(1)} %collective-permute-done.1.refs_2_), channel_id=1, source_target_pairs={{0,1},{1,0},{2,3},{3,2},{4,5},{5,4},{6,7},{7,6},{8,9},{9,8},{10,11... | collective-permute-start | bytes 294920 | tf_op jit(solution)/shard_map/ppermute | solution.py:312
  16.0 7.9 %collective-permute-start.8 = (bf16[768,128]{1,0:T(8,128)(2,1)S(1)}, bf16[768,128]{1,0:T(8,128)(2,1)S(1)}, u32[]{:S(2)}, u32[]{:S(2)}) collective-permute-start(bf16[768,128]{1,0:T(8,128)(2,1)S(1)} %get-tuple-element.63.mine_ref), channel_id=1, source_target_pairs={{0,4},{4,0},{1,5},{5,1},{2,6},{6,2},{3,7},{7,3},{8,12},{12,8},{9,1... | collective-permute-start | bytes 589832 | tf_op jit(solution)/shard_map/ppermute | solution.py:309
  17.9 8.9 %collective-permute-start.10 = (bf16[768,128]{1,0:T(8,128)(2,1)S(1)}, bf16[768,128]{1,0:T(8,128)(2,1)S(1)}, u32[]{:S(2)}, u32[]{:S(2)}) collective-permute-start(bf16[768,128]{1,0:T(8,128)(2,1)S(1)} %get-tuple-element.69.mine_ref), channel_id=1, source_target_pairs={{0,4},{4,0},{1,5},{5,1},{2,6},{6,2},{3,7},{7,3},{8,12},{12,8},{9,1... | collective-permute-start | bytes 589832 | tf_op jit(solution)/shard_map/ppermute | solution.py:309
  19.0 14.1 %slice-start = ((s8[4718592]{0:T(1024)(128)(4,1)}), s8[4194304]{0:T(1024)(128)(4,1)S(1)}, s32[]{:S(2)}) async-start(s8[4718592]{0:T(1024)(128)(4,1)} %bitcast.7), calls=%async_computation | async-start | bytes 8388608
  21.6 11.6 %slice-start.1 = ((s8[4718592]{0:T(1024)(128)(4,1)}), s8[524288]{0:T(1024)(128)(4,1)S(1)}, s32[]{:S(2)}) async-start(s8[4718592]{0:T(1024)(128)(4,1)} %bitcast.7), calls=%async_computation.1 | async-start | bytes 1048576
  24.9 3.0 %collective-permute-start.9 = (bf16[2,32,1536]{2,1,0:T(8,128)(2,1)S(1)}, bf16[2,32,1536]{2,1,0:T(8,128)(2,1)S(1)}, u32[]{:S(2)}, u32[]{:S(2)}) collective-permute-start(bf16[2,32,1536]{2,1,0:T(8,128)(2,1)S(1)} %get-tuple-element.72), channel_id=1, source_target_pairs={{0,1},{1,0},{2,3},{3,2},{4,5},{5,4},{6,7},{7,6},{8,9},{9,8},{10,11... | collective-permute-start | bytes 589832 | tf_op jit(solution)/shard_map/ppermute | solution.py:312
  27.8 3.0 %collective-permute-start.11 = (bf16[2,32,1536]{2,1,0:T(8,128)(2,1)S(1)}, bf16[2,32,1536]{2,1,0:T(8,128)(2,1)S(1)}, u32[]{:S(2)}, u32[]{:S(2)}) collective-permute-start(bf16[2,32,1536]{2,1,0:T(8,128)(2,1)S(1)} %get-tuple-element.77), channel_id=1, source_target_pairs={{0,1},{1,0},{2,3},{3,2},{4,5},{5,4},{6,7},{7,6},{8,9},{9,8},{10,11... | collective-permute-start | bytes 589832 | tf_op jit(solution)/shard_map/ppermute | solution.py:312
  28.0 7.8 %collective-permute-start.12 = (bf16[32,1536]{1,0:T(8,128)(2,1)S(1)}, bf16[32,1536]{1,0:T(8,128)(2,1)S(1)}, u32[]{:S(2)}, u32[]{:S(2)}) collective-permute-start(bf16[32,1536]{1,0:T(8,128)(2,1)S(1)} %get-tuple-element.73.refs_0_), channel_id=1, source_target_pairs={{0,8},{1,9},{2,10},{3,11},{8,0},{9,1},{10,2},{11,3},{16,24},{17,25... | collective-permute-start | bytes 294920 | tf_op jit(solution)/shard_map/ppermute | solution.py:334
  29.5 7.0 %collective-permute-start.13 = (bf16[32,1536]{1,0:T(8,128)(2,1)S(1)}, bf16[32,1536]{1,0:T(8,128)(2,1)S(1)}, u32[]{:S(2)}, u32[]{:S(2)}) collective-permute-start(bf16[32,1536]{1,0:T(8,128)(2,1)S(1)} %get-tuple-element.74.refs_1_), channel_id=1, source_target_pairs={{0,10},{1,11},{2,8},{3,9},{8,2},{9,3},{10,0},{11,1},{16,26},{17,27... | collective-permute-start | bytes 294920 | tf_op jit(solution)/shard_map/ppermute | solution.py:334
  30.9 7.1 %collective-permute-start.15 = (bf16[32,1536]{1,0:T(8,128)(2,1)S(1)}, bf16[32,1536]{1,0:T(8,128)(2,1)S(1)}, u32[]{:S(2)}, u32[]{:S(2)}) collective-permute-start(bf16[32,1536]{1,0:T(8,128)(2,1)S(1)} %get-tuple-element.78.refs_0_), channel_id=1, source_target_pairs={{0,8},{1,9},{2,10},{3,11},{8,0},{9,1},{10,2},{11,3},{16,24},{17,25... | collective-permute-start | bytes 294920 | tf_op jit(solution)/shard_map/ppermute | solution.py:334
  32.4 8.0 %collective-permute-start.16 = (bf16[32,1536]{1,0:T(8,128)(2,1)S(1)}, bf16[32,1536]{1,0:T(8,128)(2,1)S(1)}, u32[]{:S(2)}, u32[]{:S(2)}) collective-permute-start(bf16[32,1536]{1,0:T(8,128)(2,1)S(1)} %get-tuple-element.79.refs_1_), channel_id=1, source_target_pairs={{0,10},{1,11},{2,8},{3,9},{8,2},{9,3},{10,0},{11,1},{16,26},{17,27... | collective-permute-start | bytes 294920 | tf_op jit(solution)/shard_map/ppermute | solution.py:334
  34.2 6.2 %collective-permute-start.19 = (bf16[32,1536]{1,0:T(8,128)(2,1)S(1)}, bf16[32,1536]{1,0:T(8,128)(2,1)S(1)}, u32[]{:S(2)}, u32[]{:S(2)}) collective-permute-start(bf16[32,1536]{1,0:T(8,128)(2,1)S(1)} %get-tuple-element.85), channel_id=1, source_target_pairs={{0,4},{4,0},{1,5},{5,1},{2,6},{6,2},{3,7},{7,3},{8,12},{12,8},{9,1... | collective-permute-start | bytes 294920 | tf_op jit(solution)/shard_map/ppermute | solution.py:309
  36.6 5.9 %collective-permute-start.18 = (bf16[32,1536]{1,0:T(8,128)(2,1)S(1)}, bf16[32,1536]{1,0:T(8,128)(2,1)S(1)}, u32[]{:S(2)}, u32[]{:S(2)}) collective-permute-start(bf16[32,1536]{1,0:T(8,128)(2,1)S(1)} %fusion.refs_2_.addend_ref), channel_id=1, source_target_pairs={{0,3},{1,2},{2,1},{3,0},{4,7},{5,6},{6,5},{7,4},{8,11},{9,10},{10,... | collective-permute-start | bytes 294920 | tf_op jit(solution)/shard_map/ppermute | solution.py:318
  36.6 7.8 %collective-permute-start.14 = (bf16[32,1536]{1,0:T(8,128)(2,1)S(1)}, bf16[32,1536]{1,0:T(8,128)(2,1)S(1)}, u32[]{:S(2)}, u32[]{:S(2)}) collective-permute-start(bf16[32,1536]{1,0:T(8,128)(2,1)S(1)} %fusion.refs_2_.addend_ref), channel_id=1, source_target_pairs={{0,2},{1,3},{2,0},{3,1},{4,6},{5,7},{6,4},{7,5},{8,10},{9,11},{10,... | collective-permute-start | bytes 294920 | tf_op jit(solution)/shard_map/ppermute | solution.py:318
  40.4 1.3 %collective-permute-start.17 = (bf16[32,1536]{1,0:T(8,128)(2,1)S(1)}, bf16[32,1536]{1,0:T(8,128)(2,1)S(1)}, u32[]{:S(2)}, u32[]{:S(2)}) collective-permute-start(bf16[32,1536]{1,0:T(8,128)(2,1)S(1)} %fusion.refs_2_.addend_ref), channel_id=1, source_target_pairs={{0,1},{1,0},{2,3},{3,2},{4,5},{5,4},{6,7},{7,6},{8,9},{9,8},{10,11... | collective-permute-start | bytes 294920 | tf_op jit(solution)/shard_map/ppermute | solution.py:312
  40.5 6.1 %collective-permute-start.20 = (bf16[32,1536]{1,0:T(8,128)(2,1)S(1)}, bf16[32,1536]{1,0:T(8,128)(2,1)S(1)}, u32[]{:S(2)}, u32[]{:S(2)}) collective-permute-start(bf16[32,1536]{1,0:T(8,128)(2,1)S(1)} %fusion.1.refs_2_.addend_ref), channel_id=1, source_target_pairs={{0,2},{1,3},{2,0},{3,1},{4,6},{5,7},{6,4},{7,5},{8,10},{9,11},{10,... | collective-permute-start | bytes 294920 | tf_op jit(solution)/shard_map/ppermute | solution.py:318
  41.2 7.0 %collective-permute-start.21 = (bf16[32,1536]{1,0:T(8,128)(2,1)S(1)}, bf16[32,1536]{1,0:T(8,128)(2,1)S(1)}, u32[]{:S(2)}, u32[]{:S(2)}) collective-permute-start(bf16[32,1536]{1,0:T(8,128)(2,1)S(1)} %fusion.1.refs_2_.addend_ref), channel_id=1, source_target_pairs={{0,1},{1,0},{2,3},{3,2},{4,5},{5,4},{6,7},{7,6},{8,9},{9,8},{10,11... | collective-permute-start | bytes 294920 | tf_op jit(solution)/shard_map/ppermute | solution.py:312
  46.6 1.6 %collective-permute-start.22 = (bf16[32,1536]{1,0:T(8,128)(2,1)S(1)}, bf16[32,1536]{1,0:T(8,128)(2,1)S(1)}, u32[]{:S(2)}, u32[]{:S(2)}) collective-permute-start(bf16[32,1536]{1,0:T(8,128)(2,1)S(1)} %collective-permute-done.20.refs_3_), channel_id=1, source_target_pairs={{0,1},{1,0},{2,3},{3,2},{4,5},{5,4},{6,7},{7,6},{8,9},{9,8},{10,11... | collective-permute-start | bytes 294920 | tf_op jit(solution)/shard_map/ppermute | solution.py:312
  46.7 7.8 %collective-permute-start.24 = (bf16[768,128]{1,0:T(8,128)(2,1)S(1)}, bf16[768,128]{1,0:T(8,128)(2,1)S(1)}, u32[]{:S(2)}, u32[]{:S(2)}) collective-permute-start(bf16[768,128]{1,0:T(8,128)(2,1)S(1)} %get-tuple-element.84.mine_ref), channel_id=1, source_target_pairs={{0,4},{4,0},{1,5},{5,1},{2,6},{6,2},{3,7},{7,3},{8,12},{12,8},{9,1... | collective-permute-start | bytes 589832 | tf_op jit(solution)/shard_map/ppermute | solution.py:309
  49.1 9.0 %collective-permute-start.23 = (bf16[768,128]{1,0:T(8,128)(2,1)S(1)}, bf16[768,128]{1,0:T(8,128)(2,1)S(1)}, u32[]{:S(2)}, u32[]{:S(2)}) collective-permute-start(bf16[768,128]{1,0:T(8,128)(2,1)S(1)} %get-tuple-element.87.mine_ref), channel_id=1, source_target_pairs={{0,4},{4,0},{1,5},{5,1},{2,6},{6,2},{3,7},{7,3},{8,12},{12,8},{9,1... | collective-permute-start | bytes 589832 | tf_op jit(solution)/shard_map/ppermute | solution.py:309
  55.3 3.8 %collective-permute-start.25 = (bf16[2,32,1536]{2,1,0:T(8,128)(2,1)S(1)}, bf16[2,32,1536]{2,1,0:T(8,128)(2,1)S(1)}, u32[]{:S(2)}, u32[]{:S(2)}) collective-permute-start(bf16[2,32,1536]{2,1,0:T(8,128)(2,1)S(1)} %get-tuple-element.90), channel_id=1, source_target_pairs={{0,1},{1,0},{2,3},{3,2},{4,5},{5,4},{6,7},{7,6},{8,9},{9,8},{10,11... | collective-permute-start | bytes 589832 | tf_op jit(solution)/shard_map/ppermute | solution.py:312
  59.0 2.4 %collective-permute-start.26 = (bf16[2,32,1536]{2,1,0:T(8,128)(2,1)S(1)}, bf16[2,32,1536]{2,1,0:T(8,128)(2,1)S(1)}, u32[]{:S(2)}, u32[]{:S(2)}) collective-permute-start(bf16[2,32,1536]{2,1,0:T(8,128)(2,1)S(1)} %get-tuple-element.94), channel_id=1, source_target_pairs={{0,1},{1,0},{2,3},{3,2},{4,5},{5,4},{6,7},{7,6},{8,9},{9,8},{10,11... | collective-permute-start | bytes 589832 | tf_op jit(solution)/shard_map/ppermute | solution.py:312
  59.2 7.2 %collective-permute-start.28 = (bf16[32,1536]{1,0:T(8,128)(2,1)S(1)}, bf16[32,1536]{1,0:T(8,128)(2,1)S(1)}, u32[]{:S(2)}, u32[]{:S(2)}) collective-permute-start(bf16[32,1536]{1,0:T(8,128)(2,1)S(1)} %get-tuple-element.91), channel_id=1, source_target_pairs={{0,4},{1,5},{2,6},{3,7},{4,0},{5,1},{6,2},{7,3},{8,12},{9,13},{10,... | collective-permute-start | bytes 294920 | tf_op jit(solution)/shard_map/ppermute | solution.py:326
  60.8 6.2 %collective-permute-start.29 = (bf16[32,1536]{1,0:T(8,128)(2,1)S(1)}, bf16[32,1536]{1,0:T(8,128)(2,1)}, u32[]{:S(2)}, u32[]{:S(2)}) collective-permute-start(bf16[32,1536]{1,0:T(8,128)(2,1)S(1)} %get-tuple-element.92), channel_id=1, source_target_pairs={{0,6},{1,7},{2,4},{3,5},{4,2},{5,3},{6,0},{7,1},{8,14},{9,15},{10,... | collective-permute-start | bytes 294920 | tf_op jit(solution)/shard_map/ppermute | solution.py:326
  61.5 6.8 %collective-permute-start.27 = (bf16[32,1536]{1,0:T(8,128)(2,1)S(1)}, bf16[32,1536]{1,0:T(8,128)(2,1)S(1)}, u32[]{:S(2)}, u32[]{:S(2)}) collective-permute-start(bf16[32,1536]{1,0:T(8,128)(2,1)S(1)} %get-tuple-element.96), channel_id=1, source_target_pairs={{0,2},{1,3},{2,0},{3,1},{4,6},{5,7},{6,4},{7,5},{8,10},{9,11},{10,... | collective-permute-start | bytes 294920 | tf_op jit(solution)/shard_map/ppermute | solution.py:318
  (1 other events, 1.8 us)

commit v18 on v16

--- a/solution.py
+++ b/solution.py
@@ -393,7 +393,7 @@
     input_piece = [input_own, swap_half(input_sent)]
     for m in range(2):
         received = [swap_section(part, d) for d, part in enumerate(first_sent[m])]
-        last_received = received
+        last_received = received = received[:1] + lax.optimization_barrier(received[1:])
         second_piece[m] = jnp.where(odd, input_piece[m], total(received).astype(jnp.bfloat16))
     for m in range(2):
         mine = spread_rows(second_piece[m])
@@ -420,6 +420,7 @@
     grad_value, grad_out = weight_grads(
         first_result, second_result, first_full, second_full
     )
+    other_parts = other_parts[:1] + lax.optimization_barrier(other_parts[1:])
     other_grad = lax.optimization_barrier(total(other_parts).astype(jnp.bfloat16))
     own_parts, _ = lax.optimization_barrier((own_parts, grad_value))
     own_grad = total(own_parts).astype(jnp.bfloat16)

time: 67.7 us -> 67.2 us (level)
  transfers between devices with their start and end apart: 30 -> 30, of which waited for: 16 -> 14; matrix products, arithmetic and copies ran while one was open for 3% -> 3% of each run, Pallas kernels for 26% -> 27%
where the time goes in v18:
time: 67.2 us; the launch traced here: 67 us
  starting transfers between devices  24.7 us (37%)
  waiting for transfers between devices  19 us (28%)
  Pallas kernels  17.8 us (26%)
  other arithmetic  3.84 us (6%)
  between operations  1.56 us (2%)
    ppermute x7, starting transfers between devices, swap_half(): return lax.ppermute(array, 'half', [(0, 1), (1, 0)])  9.91 us
    ppermute x7, waiting for transfers between devices, swap_half(): return lax.ppermute(array, 'half', [(0, 1), (1, 0)])  9.34 us
    ppermute x7, starting transfers between devices, to_row(): return lax.ppermute(array, ('outer', 'core'), pairs)  6.18 us
    ppermute x7, waiting for transfers between devices, to_row(): return lax.ppermute(array, ('outer', 'core'), pairs)  5.18 us
    ppermute x4, starting transfers between devices, swap_section(): return lax.ppermute(array, ('pair', 'outer', 'core'), pairs)  5.08 us
    pallas_call x4, Pallas kernels, mix(): pl.pallas_call(functools.partial(mix_kernel, outer, odd_phase), out_shape...  3.82 us
    ppermute x4, waiting for transfers between devices, swap_section(): return lax.ppermute(array, ('pair', 'outer', 'core'), pairs)  3.61 us
    pallas_call x2, Pallas kernels, load_table(): pl.pallas_call(load_kernel, out_shape=jax.ShapeDtypeStruct(table.shape, j...  3.57 us
  transfers between devices with their start and end apart: 30, of which 14 were waited for; matrix products, arithmetic and copies ran while one was open for 3% of the time, Pallas kernels for 27%

profile of v18, /device:TPU:0, one launch (start us, length us, event | category | flops | bytes accessed | tf_op | source)
XLA Modules:
  0.0 67.0 jit_solution(17719422385153273734)
XLA Ops:
  0.6 1.0 %bitcast_select_fusion = bf16[32,3072]{1,0:T(8,128)(2,1)S(1)} fusion(bf16[1,32,3072]{2,1,0:T(8,128)(2,1)} %param.10, pred[]{:T(512)S(6)} %eq.8, bf16[1,32,3072]{2,1,0:T(8,128)(2,1)} %param.7), kind=kLoop, calls=%fused_computation.2 | loop fusion | flops 98304 | bytes 589825 | tf_op jit(solution)/shard_map/jit(_where)/select_n | solution.py:351
  1.7 3.0 %collective-permute-start = (bf16[32,1536]{1,0:T(8,128)(2,1)S(1)}, bf16[32,1536]{1,0:T(8,128)(2,1)S(1)}, u32[]{:S(2)}, u32[]{:S(2)}) collective-permute-start(bf16[32,1536]{1,0:T(8,128)(2,1)S(1)} %get-tuple-element.111), channel_id=1, source_target_pairs={{0,4},{4,0},{1,5},{5,1},{2,6},{6,2},{3,7},{7,3},{8,12},{12,8},{9,1... | collective-permute-start | bytes 294920 | tf_op jit(solution)/shard_map/ppermute | solution.py:309
  4.7 1.1 %pad_maximum_fusion.stash_ref = bf16[2,768,128]{2,1,0:T(8,128)(2,1)S(1)} fusion(bf16[1,768,128]{2,1,0:T(8,128)(2,1)} %param.9, bf16[1,768,128]{2,1,0:T(8,128)(2,1)} %param.8), kind=kLoop, calls=%fused_computation | loop fusion | flops 196608 | bytes 786432 | tf_op jit(solution)/shard_map/concatenate | solution.py:357
  7.5 1.9 %collective-permute-start.3 = (bf16[32,1536]{1,0:T(8,128)(2,1)S(1)}, bf16[32,1536]{1,0:T(8,128)(2,1)S(1)}, u32[]{:S(2)}, u32[]{:S(2)}) collective-permute-start(bf16[32,1536]{1,0:T(8,128)(2,1)S(1)} %collective-permute-done.refs_1_.addend_ref), channel_id=1, source_target_pairs={{0,2},{1,3},{2,0},{3,1},{4,6},{5,7},{6,4},{7,5},{8,10},{9,11},{10,... | collective-permute-start | bytes 294920 | tf_op jit(solution)/shard_map/ppermute | solution.py:318
  9.5 2.4 %load_first.1.refs_0_ = bf16[1,2,768,1536]{3,2,1,0:T(8,128)(2,1)S(1)} custom-call(bf16[1,2,768,1536]{3,2,1,0:T(8,128)(2,1)} %source_ref, bf16[1,2,768,1536]{3,2,1,0:T(8,128)(2,1)} %source_ref.1), custom_call_target="tpu_custom_call" | custom-call | flops 1 | bytes 1 | tf_op jit(solution)/shard_map/load_first/pallas_call | solution.py:274
  11.9 1.1 %collective-permute-done.3.refs_2_ = bf16[32,1536]{1,0:T(8,128)(2,1)S(1)} collective-permute-done((bf16[32,1536]{1,0:T(8,128)(2,1)S(1)}, bf16[32,1536]{1,0:T(8,128)(2,1)S(1)}, u32[]{:S(2)}, u32[]{:S(2)}) %collective-permute-start.3) | collective-permute-done | bytes 98336 | tf_op jit(solution)/shard_map/ppermute | solution.py:318
  16.0 1.0 %collective-permute-start.8 = (bf16[768,128]{1,0:T(8,128)(2,1)S(1)}, bf16[768,128]{1,0:T(8,128)(2,1)S(1)}, u32[]{:S(2)}, u32[]{:S(2)}) collective-permute-start(bf16[768,128]{1,0:T(8,128)(2,1)S(1)} %get-tuple-element.60.mine_ref), channel_id=1, source_target_pairs={{0,4},{4,0},{1,5},{5,1},{2,6},{6,2},{3,7},{7,3},{8,12},{12,8},{9,1... | collective-permute-start | bytes 589832 | tf_op jit(solution)/shard_map/ppermute | solution.py:309
  17.9 1.1 %collective-permute-start.10 = (bf16[768,128]{1,0:T(8,128)(2,1)S(1)}, bf16[768,128]{1,0:T(8,128)(2,1)S(1)}, u32[]{:S(2)}, u32[]{:S(2)}) collective-permute-start(bf16[768,128]{1,0:T(8,128)(2,1)S(1)} %get-tuple-element.66.mine_ref), channel_id=1, source_target_pairs={{0,4},{4,0},{1,5},{5,1},{2,6},{6,2},{3,7},{7,3},{8,12},{12,8},{9,1... | collective-permute-start | bytes 589832 | tf_op jit(solution)/shard_map/ppermute | solution.py:309
  19.0 2.5 %load_table.2.value_ref.refs_0_ = bf16[1,2,768,1536]{3,2,1,0:T(8,128)(2,1)S(1)} custom-call(bf16[1,2,768,1536]{3,2,1,0:T(8,128)(2,1)} %source_ref), custom_call_target="tpu_custom_call" | custom-call | flops 1 | bytes 1 | tf_op jit(solution)/shard_map/load_table/pallas_call | solution.py:287
  21.6 2.3 %collective-permute-done.8.arrived_ref = bf16[768,128]{1,0:T(8,128)(2,1)S(1)} collective-permute-done((bf16[768,128]{1,0:T(8,128)(2,1)S(1)}, bf16[768,128]{1,0:T(8,128)(2,1)S(1)}, u32[]{:S(2)}, u32[]{:S(2)}) %collective-permute-start.8) | collective-permute-done | bytes 196640 | tf_op jit(solution)/shard_map/ppermute | solution.py:309
  23.9 1.0 %mix.4 = (bf16[768,128]{1,0:T(8,128)(2,1)S(1)}, bf16[2,32,1536]{2,1,0:T(8,128)(2,1)S(1)}, bf16[2,32,1536]{2,1,0:T(8,128)(2,1)S(1)}) custom-call(bf16[1040,128]{1,0:T(8,128)(2,1)S(1)} %concatenate.10.message_ref, bf16[1,2,768,1536]{3,2,1,0:T(8,128)(2,1)S(1)} %load_table.2.value_ref.refs_0_, bf16[768,128]{1,0:T(8,128)(2,1)S(1)} %get-tuple-element.66.mine_ref, ...), custom_call_target="tpu_custom_call" | custom-call | flops 1 | bytes 1 | tf_op jit(solution)/shard_map/mix/pallas_call | solution.py:141
  25.0 1.8 %collective-permute-done.10.arrived_ref = bf16[768,128]{1,0:T(8,128)(2,1)S(1)} collective-permute-done((bf16[768,128]{1,0:T(8,128)(2,1)S(1)}, bf16[768,128]{1,0:T(8,128)(2,1)S(1)}, u32[]{:S(2)}, u32[]{:S(2)}) %collective-permute-start.10) | collective-permute-done | bytes 196640 | tf_op jit(solution)/shard_map/ppermute | solution.py:309
  26.8 1.0 %mix.5 = (bf16[768,128]{1,0:T(8,128)(2,1)S(1)}, bf16[2,32,1536]{2,1,0:T(8,128)(2,1)S(1)}, bf16[2,32,1536]{2,1,0:T(8,128)(2,1)S(1)}) custom-call(bf16[1040,128]{1,0:T(8,128)(2,1)S(1)} %collective-permute-done.2.message_ref, bf16[1,2,768,1536]{3,2,1,0:T(8,128)(2,1)S(1)} %load_table.2.value_ref.refs_0_, bf16[768,128]{1,0:T(8,128)(2,1)S(1)} %get-tuple-element.60.mine_ref, ...), custom_call_target="tpu_custom_call" | custom-call | flops 1 | bytes 1 | tf_op jit(solution)/shard_map/mix/pallas_call | solution.py:141
  28.0 1.5 %collective-permute-start.12 = (bf16[32,1536]{1,0:T(8,128)(2,1)S(1)}, bf16[32,1536]{1,0:T(8,128)(2,1)S(1)}, u32[]{:S(2)}, u32[]{:S(2)}) collective-permute-start(bf16[32,1536]{1,0:T(8,128)(2,1)S(1)} %get-tuple-element.70.refs_0_), channel_id=1, source_target_pairs={{0,8},{1,9},{2,10},{3,11},{8,0},{9,1},{10,2},{11,3},{16,24},{17,25... | collective-permute-start | bytes 294920 | tf_op jit(solution)/shard_map/ppermute | solution.py:334
  29.5 1.4 %collective-permute-start.13 = (bf16[32,1536]{1,0:T(8,128)(2,1)S(1)}, bf16[32,1536]{1,0:T(8,128)(2,1)S(1)}, u32[]{:S(2)}, u32[]{:S(2)}) collective-permute-start(bf16[32,1536]{1,0:T(8,128)(2,1)S(1)} %get-tuple-element.71.refs_1_), channel_id=1, source_target_pairs={{0,10},{1,11},{2,8},{3,9},{8,2},{9,3},{10,0},{11,1},{16,26},{17,27... | collective-permute-start | bytes 294920 | tf_op jit(solution)/shard_map/ppermute | solution.py:334
  30.9 1.5 %collective-permute-start.15 = (bf16[32,1536]{1,0:T(8,128)(2,1)S(1)}, bf16[32,1536]{1,0:T(8,128)(2,1)S(1)}, u32[]{:S(2)}, u32[]{:S(2)}) collective-permute-start(bf16[32,1536]{1,0:T(8,128)(2,1)S(1)} %get-tuple-element.75.refs_0_), channel_id=1, source_target_pairs={{0,8},{1,9},{2,10},{3,11},{8,0},{9,1},{10,2},{11,3},{16,24},{17,25... | collective-permute-start | bytes 294920 | tf_op jit(solution)/shard_map/ppermute | solution.py:334
  33.2 1.0 %load_table.3.refs_1_ = bf16[1,2,768,1536]{3,2,1,0:T(8,128)(2,1)S(1)} custom-call(bf16[1,2,768,1536]{3,2,1,0:T(8,128)(2,1)S(1)} %bitcast.8), custom_call_target="tpu_custom_call" | custom-call | flops 1 | bytes 1 | tf_op jit(solution)/shard_map/load_table/pallas_call | solution.py:287
  34.2 1.6 %collective-permute-start.19 = (bf16[32,1536]{1,0:T(8,128)(2,1)S(1)}, bf16[32,1536]{1,0:T(8,128)(2,1)S(1)}, u32[]{:S(2)}, u32[]{:S(2)}) collective-permute-start(bf16[32,1536]{1,0:T(8,128)(2,1)S(1)} %get-tuple-element.82), channel_id=1, source_target_pairs={{0,4},{4,0},{1,5},{5,1},{2,6},{6,2},{3,7},{7,3},{8,12},{12,8},{9,1... | collective-permute-start | bytes 294920 | tf_op jit(solution)/shard_map/ppermute | solution.py:309
  36.7 0.9 %collective-permute-start.14 = (bf16[32,1536]{1,0:T(8,128)(2,1)S(1)}, bf16[32,1536]{1,0:T(8,128)(2,1)S(1)}, u32[]{:S(2)}, u32[]{:S(2)}) collective-permute-start(bf16[32,1536]{1,0:T(8,128)(2,1)S(1)} %fusion.refs_2_.addend_ref), channel_id=1, source_target_pairs={{0,2},{1,3},{2,0},{3,1},{4,6},{5,7},{6,4},{7,5},{8,10},{9,11},{10,... | collective-permute-start | bytes 294920 | tf_op jit(solution)/shard_map/ppermute | solution.py:318
  37.5 2.9 %collective-permute-done.16 = bf16[32,1536]{1,0:T(8,128)(2,1)S(1)} collective-permute-done((bf16[32,1536]{1,0:T(8,128)(2,1)S(1)}, bf16[32,1536]{1,0:T(8,128)(2,1)S(1)}, u32[]{:S(2)}, u32[]{:S(2)}) %collective-permute-start.16) | collective-permute-done | bytes 98336 | tf_op jit(solution)/shard_map/ppermute | solution.py:334
  41.7 1.0 %collective-permute-start.20 = (bf16[32,1536]{1,0:T(8,128)(2,1)S(1)}, bf16[32,1536]{1,0:T(8,128)(2,1)S(1)}, u32[]{:S(2)}, u32[]{:S(2)}) collective-permute-start(bf16[32,1536]{1,0:T(8,128)(2,1)S(1)} %fusion.1.refs_2_.addend_ref), channel_id=1, source_target_pairs={{0,2},{1,3},{2,0},{3,1},{4,6},{5,7},{6,4},{7,5},{8,10},{9,11},{10,... | collective-permute-start | bytes 294920 | tf_op jit(solution)/shard_map/ppermute | solution.py:318
  42.7 1.8 %collective-permute-done.14.refs_3_ = bf16[32,1536]{1,0:T(8,128)(2,1)S(1)} collective-permute-done((bf16[32,1536]{1,0:T(8,128)(2,1)S(1)}, bf16[32,1536]{1,0:T(8,128)(2,1)S(1)}, u32[]{:S(2)}, u32[]{:S(2)}) %collective-permute-start.14) | collective-permute-done | bytes 98336 | tf_op jit(solution)/shard_map/ppermute | solution.py:318
  44.5 0.9 %project.6 = (bf16[768,128]{1,0:T(8,128)(2,1)S(1)}, bf16[128,1536]{1,0:T(8,128)(2,1)S(1)}) custom-call(bf16[1040,128]{1,0:T(8,128)(2,1)S(1)} %concatenate.10.message_ref, bf16[1,2,768,1536]{3,2,1,0:T(8,128)(2,1)S(1)} %load_table.2.value_ref.refs_0_, bf16[1,2,768,1536]{3,2,1,0:T(8,128)(2,1)S(1)} %load_table.3.refs_1_, ...), custom_call_target="tpu_custom_call" | custom-call | flops 1 | bytes 1 | tf_op jit(solution)/shard_map/project/pallas_call | solution.py:83
  45.4 1.6 %collective-permute-start.24 = (bf16[768,128]{1,0:T(8,128)(2,1)S(1)}, bf16[768,128]{1,0:T(8,128)(2,1)S(1)}, u32[]{:S(2)}, u32[]{:S(2)}) collective-permute-start(bf16[768,128]{1,0:T(8,128)(2,1)S(1)} %get-tuple-element.81.mine_ref), channel_id=1, source_target_pairs={{0,4},{4,0},{1,5},{5,1},{2,6},{6,2},{3,7},{7,3},{8,12},{12,8},{9,1... | collective-permute-start | bytes 589832 | tf_op jit(solution)/shard_map/ppermute | solution.py:309
  46.9 1.8 %collective-permute-done.20.refs_3_ = bf16[32,1536]{1,0:T(8,128)(2,1)S(1)} collective-permute-done((bf16[32,1536]{1,0:T(8,128)(2,1)S(1)}, bf16[32,1536]{1,0:T(8,128)(2,1)S(1)}, u32[]{:S(2)}, u32[]{:S(2)}) %collective-permute-start.20) | collective-permute-done | bytes 98336 | tf_op jit(solution)/shard_map/ppermute | solution.py:318
  49.6 1.6 %collective-permute-start.23 = (bf16[768,128]{1,0:T(8,128)(2,1)S(1)}, bf16[768,128]{1,0:T(8,128)(2,1)S(1)}, u32[]{:S(2)}, u32[]{:S(2)}) collective-permute-start(bf16[768,128]{1,0:T(8,128)(2,1)S(1)} %get-tuple-element.83.mine_ref), channel_id=1, source_target_pairs={{0,4},{4,0},{1,5},{5,1},{2,6},{6,2},{3,7},{7,3},{8,12},{12,8},{9,1... | collective-permute-start | bytes 589832 | tf_op jit(solution)/shard_map/ppermute | solution.py:309
  51.1 1.2 %collective-permute-done.24.arrived_ref = bf16[768,128]{1,0:T(8,128)(2,1)S(1)} collective-permute-done((bf16[768,128]{1,0:T(8,128)(2,1)S(1)}, bf16[768,128]{1,0:T(8,128)(2,1)S(1)}, u32[]{:S(2)}, u32[]{:S(2)}) %collective-permute-start.24) | collective-permute-done | bytes 196640 | tf_op jit(solution)/shard_map/ppermute | solution.py:309
  53.3 3.2 %collective-permute-done.23.arrived_ref = bf16[768,128]{1,0:T(8,128)(2,1)S(1)} collective-permute-done((bf16[768,128]{1,0:T(8,128)(2,1)S(1)}, bf16[768,128]{1,0:T(8,128)(2,1)S(1)}, u32[]{:S(2)}, u32[]{:S(2)}) %collective-permute-start.23) | collective-permute-done | bytes 196640 | tf_op jit(solution)/shard_map/ppermute | solution.py:309
  57.7 1.7 %collective-permute-start.29 = (bf16[32,1536]{1,0:T(8,128)(2,1)S(1)}, bf16[32,1536]{1,0:T(8,128)(2,1)S(1)}, u32[]{:S(2)}, u32[]{:S(2)}) collective-permute-start(bf16[32,1536]{1,0:T(8,128)(2,1)S(1)} %get-tuple-element.88), channel_id=1, source_target_pairs={{0,6},{1,7},{2,4},{3,5},{4,2},{5,3},{6,0},{7,1},{8,14},{9,15},{10,... | collective-permute-start | bytes 294920 | tf_op jit(solution)/shard_map/ppermute | solution.py:326
  60.0 1.4 %collective-permute-start.27 = (bf16[32,1536]{1,0:T(8,128)(2,1)S(1)}, bf16[32,1536]{1,0:T(8,128)(2,1)S(1)}, u32[]{:S(2)}, u32[]{:S(2)}) collective-permute-start(bf16[32,1536]{1,0:T(8,128)(2,1)S(1)} %get-tuple-element.92), channel_id=1, source_target_pairs={{0,2},{1,3},{2,0},{3,1},{4,6},{5,7},{6,4},{7,5},{8,10},{9,11},{10,... | collective-permute-start | bytes 294920 | tf_op jit(solution)/shard_map/ppermute | solution.py:318
  61.4 3.5 %weight_grads.1 = (bf16[1,768,1536]{2,1,0:T(8,128)(2,1)}, bf16[1,768,1536]{2,1,0:T(8,128)(2,1)}) custom-call(bf16[768,128]{1,0:T(8,128)(2,1)S(1)} %get-tuple-element.93.a0, bf16[768,128]{1,0:T(8,128)(2,1)S(1)} %get-tuple-element.94.a1, bf16[768,128]{1,0:T(8,128)(2,1)S(1)} %get-tuple-element.97.b0, bf16[768,128]{1,0:T(8,128)(2,1)S(1)} %get-tuple-element.98.b1, ...), custom_call_target="tpu_custom_call" | custom-call | flops 1 | bytes 1 | tf_op jit(solution)/shard_map/weight_grads/pallas_call | solution.py:201
  65.3 0.9 %add_convert_fusion = bf16[32,1536]{1,0:T(8,128)(2,1)S(1)} fusion(bf16[32,1536]{1,0:T(8,128)(2,1)S(1)} %collective-permute-done.29, bf16[32,1536]{1,0:T(8,128)(2,1)} %collective-permute-done.28), kind=kLoop, calls=%fused_computation.3 | loop fusion | flops 196608 | bytes 294912 | tf_op jit(solution)/shard_map/convert_element_type | solution.py:424
  (62 shorter events, 12.9 us)
Async XLA Ops:
  1.7 5.8 %collective-permute-start = (bf16[32,1536]{1,0:T(8,128)(2,1)S(1)}, bf16[32,1536]{1,0:T(8,128)(2,1)S(1)}, u32[]{:S(2)}, u32[]{:S(2)}) collective-permute-start(bf16[32,1536]{1,0:T(8,128)(2,1)S(1)} %get-tuple-element.111), channel_id=1, source_target_pairs={{0,4},{4,0},{1,5},{5,1},{2,6},{6,2},{3,7},{7,3},{8,12},{12,8},{9,1... | collective-permute-start | bytes 294920 | tf_op jit(solution)/shard_map/ppermute | solution.py:309
  7.2 7.9 %collective-permute-start.2 = (bf16[1040,128]{1,0:T(8,128)(2,1)S(1)}, bf16[1040,128]{1,0:T(8,128)(2,1)S(1)}, u32[]{:S(2)}, u32[]{:S(2)}) collective-permute-start(bf16[1040,128]{1,0:T(8,128)(2,1)S(1)} %concatenate.10.message_ref), channel_id=1, source_target_pairs={{0,4},{4,0},{1,5},{5,1},{2,6},{6,2},{3,7},{7,3},{8,12},{12,8},{9,1... | collective-permute-start | bytes 798728 | tf_op jit(solution)/shard_map/ppermute | solution.py:309
  7.5 5.5 %collective-permute-start.3 = (bf16[32,1536]{1,0:T(8,128)(2,1)S(1)}, bf16[32,1536]{1,0:T(8,128)(2,1)S(1)}, u32[]{:S(2)}, u32[]{:S(2)}) collective-permute-start(bf16[32,1536]{1,0:T(8,128)(2,1)S(1)} %collective-permute-done.refs_1_.addend_ref), channel_id=1, source_target_pairs={{0,2},{1,3},{2,0},{3,1},{4,6},{5,7},{6,4},{7,5},{8,10},{9,11},{10,... | collective-permute-start | bytes 294920 | tf_op jit(solution)/shard_map/ppermute | solution.py:318
  9.4 4.7 %collective-permute-start.1 = (bf16[32,1536]{1,0:T(8,128)(2,1)S(1)}, bf16[32,1536]{1,0:T(8,128)(2,1)S(1)}, u32[]{:S(2)}, u32[]{:S(2)}) collective-permute-start(bf16[32,1536]{1,0:T(8,128)(2,1)S(1)} %get-tuple-element.64.refs_1_.addend_ref), channel_id=1, source_target_pairs={{0,2},{1,3},{2,0},{3,1},{4,6},{5,7},{6,4},{7,5},{8,10},{9,11},{10,... | collective-permute-start | bytes 294920 | tf_op jit(solution)/shard_map/ppermute | solution.py:318
  13.0 2.1 %collective-permute-start.4 = (bf16[32,1536]{1,0:T(8,128)(2,1)S(1)}, bf16[32,1536]{1,0:T(8,128)(2,1)S(1)}, u32[]{:S(2)}, u32[]{:S(2)}) collective-permute-start(bf16[32,1536]{1,0:T(8,128)(2,1)S(1)} %collective-permute-done.refs_1_.addend_ref), channel_id=1, source_target_pairs={{0,1},{1,0},{2,3},{3,2},{4,5},{5,4},{6,7},{7,6},{8,9},{9,8},{10,11... | collective-permute-start | bytes 294920 | tf_op jit(solution)/shard_map/ppermute | solution.py:312
  13.0 2.1 %collective-permute-start.5 = (bf16[32,1536]{1,0:T(8,128)(2,1)S(1)}, bf16[32,1536]{1,0:T(8,128)(2,1)S(1)}, u32[]{:S(2)}, u32[]{:S(2)}) collective-permute-start(bf16[32,1536]{1,0:T(8,128)(2,1)S(1)} %collective-permute-done.3.refs_2_), channel_id=1, source_target_pairs={{0,1},{1,0},{2,3},{3,2},{4,5},{5,4},{6,7},{7,6},{8,9},{9,8},{10,11... | collective-permute-start | bytes 294920 | tf_op jit(solution)/shard_map/ppermute | solution.py:312
  14.1 2.9 %collective-permute-start.6 = (bf16[32,1536]{1,0:T(8,128)(2,1)S(1)}, bf16[32,1536]{1,0:T(8,128)(2,1)S(1)}, u32[]{:S(2)}, u32[]{:S(2)}) collective-permute-start(bf16[32,1536]{1,0:T(8,128)(2,1)S(1)} %get-tuple-element.64.refs_1_.addend_ref), channel_id=1, source_target_pairs={{0,1},{1,0},{2,3},{3,2},{4,5},{5,4},{6,7},{7,6},{8,9},{9,8},{10,11... | collective-permute-start | bytes 294920 | tf_op jit(solution)/shard_map/ppermute | solution.py:312
  14.1 2.9 %collective-permute-start.7 = (bf16[32,1536]{1,0:T(8,128)(2,1)S(1)}, bf16[32,1536]{1,0:T(8,128)(2,1)S(1)}, u32[]{:S(2)}, u32[]{:S(2)}) collective-permute-start(bf16[32,1536]{1,0:T(8,128)(2,1)S(1)} %collective-permute-done.1.refs_2_), channel_id=1, source_target_pairs={{0,1},{1,0},{2,3},{3,2},{4,5},{5,4},{6,7},{7,6},{8,9},{9,8},{10,11... | collective-permute-start | bytes 294920 | tf_op jit(solution)/shard_map/ppermute | solution.py:312
  16.0 7.9 %collective-permute-start.8 = (bf16[768,128]{1,0:T(8,128)(2,1)S(1)}, bf16[768,128]{1,0:T(8,128)(2,1)S(1)}, u32[]{:S(2)}, u32[]{:S(2)}) collective-permute-start(bf16[768,128]{1,0:T(8,128)(2,1)S(1)} %get-tuple-element.60.mine_ref), channel_id=1, source_target_pairs={{0,4},{4,0},{1,5},{5,1},{2,6},{6,2},{3,7},{7,3},{8,12},{12,8},{9,1... | collective-permute-start | bytes 589832 | tf_op jit(solution)/shard_map/ppermute | solution.py:309
  17.9 8.9 %collective-permute-start.10 = (bf16[768,128]{1,0:T(8,128)(2,1)S(1)}, bf16[768,128]{1,0:T(8,128)(2,1)S(1)}, u32[]{:S(2)}, u32[]{:S(2)}) collective-permute-start(bf16[768,128]{1,0:T(8,128)(2,1)S(1)} %get-tuple-element.66.mine_ref), channel_id=1, source_target_pairs={{0,4},{4,0},{1,5},{5,1},{2,6},{6,2},{3,7},{7,3},{8,12},{12,8},{9,1... | collective-permute-start | bytes 589832 | tf_op jit(solution)/shard_map/ppermute | solution.py:309
  19.0 14.1 %slice-start = ((s8[4718592]{0:T(1024)(128)(4,1)}), s8[4194304]{0:T(1024)(128)(4,1)S(1)}, s32[]{:S(2)}) async-start(s8[4718592]{0:T(1024)(128)(4,1)} %bitcast.7), calls=%async_computation | async-start | bytes 8388608
  21.6 11.6 %slice-start.1 = ((s8[4718592]{0:T(1024)(128)(4,1)}), s8[524288]{0:T(1024)(128)(4,1)S(1)}, s32[]{:S(2)}) async-start(s8[4718592]{0:T(1024)(128)(4,1)} %bitcast.7), calls=%async_computation.1 | async-start | bytes 1048576
  24.9 3.0 %collective-permute-start.9 = (bf16[2,32,1536]{2,1,0:T(8,128)(2,1)S(1)}, bf16[2,32,1536]{2,1,0:T(8,128)(2,1)S(1)}, u32[]{:S(2)}, u32[]{:S(2)}) collective-permute-start(bf16[2,32,1536]{2,1,0:T(8,128)(2,1)S(1)} %get-tuple-element.69), channel_id=1, source_target_pairs={{0,1},{1,0},{2,3},{3,2},{4,5},{5,4},{6,7},{7,6},{8,9},{9,8},{10,11... | collective-permute-start | bytes 589832 | tf_op jit(solution)/shard_map/ppermute | solution.py:312
  27.8 3.0 %collective-permute-start.11 = (bf16[2,32,1536]{2,1,0:T(8,128)(2,1)S(1)}, bf16[2,32,1536]{2,1,0:T(8,128)(2,1)S(1)}, u32[]{:S(2)}, u32[]{:S(2)}) collective-permute-start(bf16[2,32,1536]{2,1,0:T(8,128)(2,1)S(1)} %get-tuple-element.74), channel_id=1, source_target_pairs={{0,1},{1,0},{2,3},{3,2},{4,5},{5,4},{6,7},{7,6},{8,9},{9,8},{10,11... | collective-permute-start | bytes 589832 | tf_op jit(solution)/shard_map/ppermute | solution.py:312
  28.0 8.5 %collective-permute-start.12 = (bf16[32,1536]{1,0:T(8,128)(2,1)S(1)}, bf16[32,1536]{1,0:T(8,128)(2,1)S(1)}, u32[]{:S(2)}, u32[]{:S(2)}) collective-permute-start(bf16[32,1536]{1,0:T(8,128)(2,1)S(1)} %get-tuple-element.70.refs_0_), channel_id=1, source_target_pairs={{0,8},{1,9},{2,10},{3,11},{8,0},{9,1},{10,2},{11,3},{16,24},{17,25... | collective-permute-start | bytes 294920 | tf_op jit(solution)/shard_map/ppermute | solution.py:334
  29.5 7.0 %collective-permute-start.13 = (bf16[32,1536]{1,0:T(8,128)(2,1)S(1)}, bf16[32,1536]{1,0:T(8,128)(2,1)S(1)}, u32[]{:S(2)}, u32[]{:S(2)}) collective-permute-start(bf16[32,1536]{1,0:T(8,128)(2,1)S(1)} %get-tuple-element.71.refs_1_), channel_id=1, source_target_pairs={{0,10},{1,11},{2,8},{3,9},{8,2},{9,3},{10,0},{11,1},{16,26},{17,27... | collective-permute-start | bytes 294920 | tf_op jit(solution)/shard_map/ppermute | solution.py:334
  30.9 9.5 %collective-permute-start.15 = (bf16[32,1536]{1,0:T(8,128)(2,1)S(1)}, bf16[32,1536]{1,0:T(8,128)(2,1)S(1)}, u32[]{:S(2)}, u32[]{:S(2)}) collective-permute-start(bf16[32,1536]{1,0:T(8,128)(2,1)S(1)} %get-tuple-element.75.refs_0_), channel_id=1, source_target_pairs={{0,8},{1,9},{2,10},{3,11},{8,0},{9,1},{10,2},{11,3},{16,24},{17,25... | collective-permute-start | bytes 294920 | tf_op jit(solution)/shard_map/ppermute | solution.py:334
  32.4 8.0 %collective-permute-start.16 = (bf16[32,1536]{1,0:T(8,128)(2,1)S(1)}, bf16[32,1536]{1,0:T(8,128)(2,1)S(1)}, u32[]{:S(2)}, u32[]{:S(2)}) collective-permute-start(bf16[32,1536]{1,0:T(8,128)(2,1)S(1)} %get-tuple-element.76.refs_1_), channel_id=1, source_target_pairs={{0,10},{1,11},{2,8},{3,9},{8,2},{9,3},{10,0},{11,1},{16,26},{17,27... | collective-permute-start | bytes 294920 | tf_op jit(solution)/shard_map/ppermute | solution.py:334
  34.2 6.2 %collective-permute-start.19 = (bf16[32,1536]{1,0:T(8,128)(2,1)S(1)}, bf16[32,1536]{1,0:T(8,128)(2,1)S(1)}, u32[]{:S(2)}, u32[]{:S(2)}) collective-permute-start(bf16[32,1536]{1,0:T(8,128)(2,1)S(1)} %get-tuple-element.82), channel_id=1, source_target_pairs={{0,4},{4,0},{1,5},{5,1},{2,6},{6,2},{3,7},{7,3},{8,12},{12,8},{9,1... | collective-permute-start | bytes 294920 | tf_op jit(solution)/shard_map/ppermute | solution.py:309
  36.6 6.1 %collective-permute-start.18 = (bf16[32,1536]{1,0:T(8,128)(2,1)S(1)}, bf16[32,1536]{1,0:T(8,128)(2,1)S(1)}, u32[]{:S(2)}, u32[]{:S(2)}) collective-permute-start(bf16[32,1536]{1,0:T(8,128)(2,1)S(1)} %fusion.refs_2_.addend_ref), channel_id=1, source_target_pairs={{0,3},{1,2},{2,1},{3,0},{4,7},{5,6},{6,5},{7,4},{8,11},{9,10},{10,... | collective-permute-start | bytes 294920 | tf_op jit(solution)/shard_map/ppermute | solution.py:318
  36.7 7.8 %collective-permute-start.14 = (bf16[32,1536]{1,0:T(8,128)(2,1)S(1)}, bf16[32,1536]{1,0:T(8,128)(2,1)S(1)}, u32[]{:S(2)}, u32[]{:S(2)}) collective-permute-start(bf16[32,1536]{1,0:T(8,128)(2,1)S(1)} %fusion.refs_2_.addend_ref), channel_id=1, source_target_pairs={{0,2},{1,3},{2,0},{3,1},{4,6},{5,7},{6,4},{7,5},{8,10},{9,11},{10,... | collective-permute-start | bytes 294920 | tf_op jit(solution)/shard_map/ppermute | solution.py:318
  40.4 1.3 %collective-permute-start.17 = (bf16[32,1536]{1,0:T(8,128)(2,1)S(1)}, bf16[32,1536]{1,0:T(8,128)(2,1)S(1)}, u32[]{:S(2)}, u32[]{:S(2)}) collective-permute-start(bf16[32,1536]{1,0:T(8,128)(2,1)S(1)} %fusion.refs_2_.addend_ref), channel_id=1, source_target_pairs={{0,1},{1,0},{2,3},{3,2},{4,5},{5,4},{6,7},{7,6},{8,9},{9,8},{10,11... | collective-permute-start | bytes 294920 | tf_op jit(solution)/shard_map/ppermute | solution.py:312
  40.5 6.5 %collective-permute-start.22 = (bf16[32,1536]{1,0:T(8,128)(2,1)S(1)}, bf16[32,1536]{1,0:T(8,128)(2,1)S(1)}, u32[]{:S(2)}, u32[]{:S(2)}) collective-permute-start(bf16[32,1536]{1,0:T(8,128)(2,1)S(1)} %fusion.1.refs_2_.addend_ref), channel_id=1, source_target_pairs={{0,3},{1,2},{2,1},{3,0},{4,7},{5,6},{6,5},{7,4},{8,11},{9,10},{10,... | collective-permute-start | bytes 294920 | tf_op jit(solution)/shard_map/ppermute | solution.py:318
  41.3 5.6 %collective-permute-start.21 = (bf16[32,1536]{1,0:T(8,128)(2,1)S(1)}, bf16[32,1536]{1,0:T(8,128)(2,1)S(1)}, u32[]{:S(2)}, u32[]{:S(2)}) collective-permute-start(bf16[32,1536]{1,0:T(8,128)(2,1)S(1)} %fusion.1.refs_2_.addend_ref), channel_id=1, source_target_pairs={{0,1},{1,0},{2,3},{3,2},{4,5},{5,4},{6,7},{7,6},{8,9},{9,8},{10,11... | collective-permute-start | bytes 294920 | tf_op jit(solution)/shard_map/ppermute | solution.py:312
  41.7 7.0 %collective-permute-start.20 = (bf16[32,1536]{1,0:T(8,128)(2,1)S(1)}, bf16[32,1536]{1,0:T(8,128)(2,1)S(1)}, u32[]{:S(2)}, u32[]{:S(2)}) collective-permute-start(bf16[32,1536]{1,0:T(8,128)(2,1)S(1)} %fusion.1.refs_2_.addend_ref), channel_id=1, source_target_pairs={{0,2},{1,3},{2,0},{3,1},{4,6},{5,7},{6,4},{7,5},{8,10},{9,11},{10,... | collective-permute-start | bytes 294920 | tf_op jit(solution)/shard_map/ppermute | solution.py:318
  45.4 7.0 %collective-permute-start.24 = (bf16[768,128]{1,0:T(8,128)(2,1)S(1)}, bf16[768,128]{1,0:T(8,128)(2,1)S(1)}, u32[]{:S(2)}, u32[]{:S(2)}) collective-permute-start(bf16[768,128]{1,0:T(8,128)(2,1)S(1)} %get-tuple-element.81.mine_ref), channel_id=1, source_target_pairs={{0,4},{4,0},{1,5},{5,1},{2,6},{6,2},{3,7},{7,3},{8,12},{12,8},{9,1... | collective-permute-start | bytes 589832 | tf_op jit(solution)/shard_map/ppermute | solution.py:309
  49.6 7.0 %collective-permute-start.23 = (bf16[768,128]{1,0:T(8,128)(2,1)S(1)}, bf16[768,128]{1,0:T(8,128)(2,1)S(1)}, u32[]{:S(2)}, u32[]{:S(2)}) collective-permute-start(bf16[768,128]{1,0:T(8,128)(2,1)S(1)} %get-tuple-element.83.mine_ref), channel_id=1, source_target_pairs={{0,4},{4,0},{1,5},{5,1},{2,6},{6,2},{3,7},{7,3},{8,12},{12,8},{9,1... | collective-permute-start | bytes 589832 | tf_op jit(solution)/shard_map/ppermute | solution.py:309
  53.3 4.3 %collective-permute-start.25 = (bf16[2,32,1536]{2,1,0:T(8,128)(2,1)S(1)}, bf16[2,32,1536]{2,1,0:T(8,128)(2,1)S(1)}, u32[]{:S(2)}, u32[]{:S(2)}) collective-permute-start(bf16[2,32,1536]{2,1,0:T(8,128)(2,1)S(1)} %get-tuple-element.86), channel_id=1, source_target_pairs={{0,1},{1,0},{2,3},{3,2},{4,5},{5,4},{6,7},{7,6},{8,9},{9,8},{10,11... | collective-permute-start | bytes 589832 | tf_op jit(solution)/shard_map/ppermute | solution.py:312
  57.5 2.4 %collective-permute-start.26 = (bf16[2,32,1536]{2,1,0:T(8,128)(2,1)S(1)}, bf16[2,32,1536]{2,1,0:T(8,128)(2,1)S(1)}, u32[]{:S(2)}, u32[]{:S(2)}) collective-permute-start(bf16[2,32,1536]{2,1,0:T(8,128)(2,1)S(1)} %get-tuple-element.90), channel_id=1, source_target_pairs={{0,1},{1,0},{2,3},{3,2},{4,5},{5,4},{6,7},{7,6},{8,9},{9,8},{10,11... | collective-permute-start | bytes 589832 | tf_op jit(solution)/shard_map/ppermute | solution.py:312
  57.7 7.2 %collective-permute-start.29 = (bf16[32,1536]{1,0:T(8,128)(2,1)S(1)}, bf16[32,1536]{1,0:T(8,128)(2,1)S(1)}, u32[]{:S(2)}, u32[]{:S(2)}) collective-permute-start(bf16[32,1536]{1,0:T(8,128)(2,1)S(1)} %get-tuple-element.88), channel_id=1, source_target_pairs={{0,6},{1,7},{2,4},{3,5},{4,2},{5,3},{6,0},{7,1},{8,14},{9,15},{10,... | collective-permute-start | bytes 294920 | tf_op jit(solution)/shard_map/ppermute | solution.py:326
  59.4 5.9 %collective-permute-start.28 = (bf16[32,1536]{1,0:T(8,128)(2,1)S(1)}, bf16[32,1536]{1,0:T(8,128)(2,1)}, u32[]{:S(2)}, u32[]{:S(2)}) collective-permute-start(bf16[32,1536]{1,0:T(8,128)(2,1)S(1)} %get-tuple-element.87), channel_id=1, source_target_pairs={{0,4},{1,5},{2,6},{3,7},{4,0},{5,1},{6,2},{7,3},{8,12},{9,13},{10,... | collective-permute-start | bytes 294920 | tf_op jit(solution)/shard_map/ppermute | solution.py:326
  60.0 6.2 %collective-permute-start.27 = (bf16[32,1536]{1,0:T(8,128)(2,1)S(1)}, bf16[32,1536]{1,0:T(8,128)(2,1)S(1)}, u32[]{:S(2)}, u32[]{:S(2)}) collective-permute-start(bf16[32,1536]{1,0:T(8,128)(2,1)S(1)} %get-tuple-element.92), channel_id=1, source_target_pairs={{0,2},{1,3},{2,0},{3,1},{4,6},{5,7},{6,4},{7,5},{8,10},{9,11},{10,... | collective-permute-start | bytes 294920 | tf_op jit(solution)/shard_map/ppermute | solution.py:318
  (1 other events, 1.8 us)

commit v19 on v18

--- a/solution.py
+++ b/solution.py
@@ -420,8 +420,8 @@
     grad_value, grad_out = weight_grads(
         first_result, second_result, first_full, second_full
     )
-    other_parts = other_parts[:1] + lax.optimization_barrier(other_parts[1:])
-    other_grad = lax.optimization_barrier(total(other_parts).astype(jnp.bfloat16))
+    far_sum = lax.optimization_barrier(total(other_parts[1:]))
+    other_grad = total([other_parts[0], far_sum]).astype(jnp.bfloat16)
     own_parts, _ = lax.optimization_barrier((own_parts, grad_value))
     own_grad = total(own_parts).astype(jnp.bfloat16)
     input_grad = jnp.concatenate(

time: 67.2 us -> 66.9 us (level)
  other arithmetic: 3.84 us -> 2.95 us
    ppermute x7, waiting for transfers between devices: 5.18 us -> 6.21 us  [to_row(): return lax.ppermute(array, ('outer', 'core'), pairs)]
    convert_element_type x1, other arithmetic: 0.92 us -> 0.01 us  [total(): value = parts[0].astype(jnp.float32)]
  transfers between devices with their start and end apart: 30 -> 30, of which waited for: 14 -> 14; matrix products, arithmetic and copies ran while one was open for 3% -> 2% of each run, Pallas kernels for 27% -> 27%
where the time goes in v19:
time: 66.9 us; the launch traced here: 66.7 us
  starting transfers between devices  24.7 us (37%)
  waiting for transfers between devices  19.6 us (29%)
  Pallas kernels  17.8 us (27%)
  other arithmetic  2.95 us (4%)
  between operations  1.55 us (2%)
    ppermute x7, starting transfers between devices, swap_half(): return lax.ppermute(array, 'half', [(0, 1), (1, 0)])  9.91 us
    ppermute x7, waiting for transfers between devices, swap_half(): return lax.ppermute(array, 'half', [(0, 1), (1, 0)])  9.34 us
    ppermute x7, waiting for transfers between devices, to_row(): return lax.ppermute(array, ('outer', 'core'), pairs)  6.21 us
    ppermute x7, starting transfers between devices, to_row(): return lax.ppermute(array, ('outer', 'core'), pairs)  6.19 us
    ppermute x4, starting transfers between devices, swap_section(): return lax.ppermute(array, ('pair', 'outer', 'core'), pairs)  5.08 us
    pallas_call x4, Pallas kernels, mix(): pl.pallas_call(functools.partial(mix_kernel, outer, odd_phase), out_shape...  3.83 us
    ppermute x4, waiting for transfers between devices, swap_section(): return lax.ppermute(array, ('pair', 'outer', 'core'), pairs)  3.6 us
    pallas_call x2, Pallas kernels, load_table(): pl.pallas_call(load_kernel, out_shape=jax.ShapeDtypeStruct(table.shape, j...  3.57 us
  transfers between devices with their start and end apart: 30, of which 14 were waited for; matrix products, arithmetic and copies ran while one was open for 2% of the time, Pallas kernels for 27%

profile of v19, /device:TPU:0, one launch (start us, length us, event | category | flops | bytes accessed | tf_op | source)
XLA Modules:
  0.0 66.7 jit_solution(1977330216991583439)
XLA Ops:
  0.6 1.0 %bitcast_select_fusion = bf16[32,3072]{1,0:T(8,128)(2,1)S(1)} fusion(bf16[1,32,3072]{2,1,0:T(8,128)(2,1)} %param.10, pred[]{:T(512)S(6)} %eq.8, bf16[1,32,3072]{2,1,0:T(8,128)(2,1)} %param.7), kind=kLoop, calls=%fused_computation.2 | loop fusion | flops 98304 | bytes 589825 | tf_op jit(solution)/shard_map/jit(_where)/select_n | solution.py:351
  1.7 3.0 %collective-permute-start = (bf16[32,1536]{1,0:T(8,128)(2,1)S(1)}, bf16[32,1536]{1,0:T(8,128)(2,1)S(1)}, u32[]{:S(2)}, u32[]{:S(2)}) collective-permute-start(bf16[32,1536]{1,0:T(8,128)(2,1)S(1)} %get-tuple-element.111), channel_id=1, source_target_pairs={{0,4},{4,0},{1,5},{5,1},{2,6},{6,2},{3,7},{7,3},{8,12},{12,8},{9,1... | collective-permute-start | bytes 294920 | tf_op jit(solution)/shard_map/ppermute | solution.py:309
  4.7 1.1 %pad_maximum_fusion.stash_ref = bf16[2,768,128]{2,1,0:T(8,128)(2,1)S(1)} fusion(bf16[1,768,128]{2,1,0:T(8,128)(2,1)} %param.9, bf16[1,768,128]{2,1,0:T(8,128)(2,1)} %param.8), kind=kLoop, calls=%fused_computation | loop fusion | flops 196608 | bytes 786432 | tf_op jit(solution)/shard_map/concatenate | solution.py:357
  7.5 1.9 %collective-permute-start.3 = (bf16[32,1536]{1,0:T(8,128)(2,1)S(1)}, bf16[32,1536]{1,0:T(8,128)(2,1)S(1)}, u32[]{:S(2)}, u32[]{:S(2)}) collective-permute-start(bf16[32,1536]{1,0:T(8,128)(2,1)S(1)} %collective-permute-done.refs_1_.addend_ref), channel_id=1, source_target_pairs={{0,2},{1,3},{2,0},{3,1},{4,6},{5,7},{6,4},{7,5},{8,10},{9,11},{10,... | collective-permute-start | bytes 294920 | tf_op jit(solution)/shard_map/ppermute | solution.py:318
  9.5 2.4 %load_first.1.refs_0_ = bf16[1,2,768,1536]{3,2,1,0:T(8,128)(2,1)S(1)} custom-call(bf16[1,2,768,1536]{3,2,1,0:T(8,128)(2,1)} %source_ref, bf16[1,2,768,1536]{3,2,1,0:T(8,128)(2,1)} %source_ref.1), custom_call_target="tpu_custom_call" | custom-call | flops 1 | bytes 1 | tf_op jit(solution)/shard_map/load_first/pallas_call | solution.py:274
  11.9 1.1 %collective-permute-done.3.refs_2_ = bf16[32,1536]{1,0:T(8,128)(2,1)S(1)} collective-permute-done((bf16[32,1536]{1,0:T(8,128)(2,1)S(1)}, bf16[32,1536]{1,0:T(8,128)(2,1)S(1)}, u32[]{:S(2)}, u32[]{:S(2)}) %collective-permute-start.3) | collective-permute-done | bytes 98336 | tf_op jit(solution)/shard_map/ppermute | solution.py:318
  16.0 1.0 %collective-permute-start.8 = (bf16[768,128]{1,0:T(8,128)(2,1)S(1)}, bf16[768,128]{1,0:T(8,128)(2,1)S(1)}, u32[]{:S(2)}, u32[]{:S(2)}) collective-permute-start(bf16[768,128]{1,0:T(8,128)(2,1)S(1)} %get-tuple-element.60.mine_ref), channel_id=1, source_target_pairs={{0,4},{4,0},{1,5},{5,1},{2,6},{6,2},{3,7},{7,3},{8,12},{12,8},{9,1... | collective-permute-start | bytes 589832 | tf_op jit(solution)/shard_map/ppermute | solution.py:309
  17.9 1.1 %collective-permute-start.10 = (bf16[768,128]{1,0:T(8,128)(2,1)S(1)}, bf16[768,128]{1,0:T(8,128)(2,1)S(1)}, u32[]{:S(2)}, u32[]{:S(2)}) collective-permute-start(bf16[768,128]{1,0:T(8,128)(2,1)S(1)} %get-tuple-element.66.mine_ref), channel_id=1, source_target_pairs={{0,4},{4,0},{1,5},{5,1},{2,6},{6,2},{3,7},{7,3},{8,12},{12,8},{9,1... | collective-permute-start | bytes 589832 | tf_op jit(solution)/shard_map/ppermute | solution.py:309
  19.0 2.5 %load_table.2.value_ref.refs_0_ = bf16[1,2,768,1536]{3,2,1,0:T(8,128)(2,1)S(1)} custom-call(bf16[1,2,768,1536]{3,2,1,0:T(8,128)(2,1)} %source_ref), custom_call_target="tpu_custom_call" | custom-call | flops 1 | bytes 1 | tf_op jit(solution)/shard_map/load_table/pallas_call | solution.py:287
  21.6 2.3 %collective-permute-done.8.arrived_ref = bf16[768,128]{1,0:T(8,128)(2,1)S(1)} collective-permute-done((bf16[768,128]{1,0:T(8,128)(2,1)S(1)}, bf16[768,128]{1,0:T(8,128)(2,1)S(1)}, u32[]{:S(2)}, u32[]{:S(2)}) %collective-permute-start.8) | collective-permute-done | bytes 196640 | tf_op jit(solution)/shard_map/ppermute | solution.py:309
  23.9 1.0 %mix.4 = (bf16[768,128]{1,0:T(8,128)(2,1)S(1)}, bf16[2,32,1536]{2,1,0:T(8,128)(2,1)S(1)}, bf16[2,32,1536]{2,1,0:T(8,128)(2,1)S(1)}) custom-call(bf16[1040,128]{1,0:T(8,128)(2,1)S(1)} %concatenate.10.message_ref, bf16[1,2,768,1536]{3,2,1,0:T(8,128)(2,1)S(1)} %load_table.2.value_ref.refs_0_, bf16[768,128]{1,0:T(8,128)(2,1)S(1)} %get-tuple-element.66.mine_ref, ...), custom_call_target="tpu_custom_call" | custom-call | flops 1 | bytes 1 | tf_op jit(solution)/shard_map/mix/pallas_call | solution.py:141
  25.0 1.8 %collective-permute-done.10.arrived_ref = bf16[768,128]{1,0:T(8,128)(2,1)S(1)} collective-permute-done((bf16[768,128]{1,0:T(8,128)(2,1)S(1)}, bf16[768,128]{1,0:T(8,128)(2,1)S(1)}, u32[]{:S(2)}, u32[]{:S(2)}) %collective-permute-start.10) | collective-permute-done | bytes 196640 | tf_op jit(solution)/shard_map/ppermute | solution.py:309
  26.8 1.0 %mix.5 = (bf16[768,128]{1,0:T(8,128)(2,1)S(1)}, bf16[2,32,1536]{2,1,0:T(8,128)(2,1)S(1)}, bf16[2,32,1536]{2,1,0:T(8,128)(2,1)S(1)}) custom-call(bf16[1040,128]{1,0:T(8,128)(2,1)S(1)} %collective-permute-done.2.message_ref, bf16[1,2,768,1536]{3,2,1,0:T(8,128)(2,1)S(1)} %load_table.2.value_ref.refs_0_, bf16[768,128]{1,0:T(8,128)(2,1)S(1)} %get-tuple-element.60.mine_ref, ...), custom_call_target="tpu_custom_call" | custom-call | flops 1 | bytes 1 | tf_op jit(solution)/shard_map/mix/pallas_call | solution.py:141
  28.0 1.5 %collective-permute-start.12 = (bf16[32,1536]{1,0:T(8,128)(2,1)S(1)}, bf16[32,1536]{1,0:T(8,128)(2,1)S(1)}, u32[]{:S(2)}, u32[]{:S(2)}) collective-permute-start(bf16[32,1536]{1,0:T(8,128)(2,1)S(1)} %get-tuple-element.70.refs_0_), channel_id=1, source_target_pairs={{0,8},{1,9},{2,10},{3,11},{8,0},{9,1},{10,2},{11,3},{16,24},{17,25... | collective-permute-start | bytes 294920 | tf_op jit(solution)/shard_map/ppermute | solution.py:334
  29.5 1.4 %collective-permute-start.13 = (bf16[32,1536]{1,0:T(8,128)(2,1)S(1)}, bf16[32,1536]{1,0:T(8,128)(2,1)S(1)}, u32[]{:S(2)}, u32[]{:S(2)}) collective-permute-start(bf16[32,1536]{1,0:T(8,128)(2,1)S(1)} %get-tuple-element.71.refs_1_), channel_id=1, source_target_pairs={{0,10},{1,11},{2,8},{3,9},{8,2},{9,3},{10,0},{11,1},{16,26},{17,27... | collective-permute-start | bytes 294920 | tf_op jit(solution)/shard_map/ppermute | solution.py:334
  30.9 1.5 %collective-permute-start.15 = (bf16[32,1536]{1,0:T(8,128)(2,1)S(1)}, bf16[32,1536]{1,0:T(8,128)(2,1)S(1)}, u32[]{:S(2)}, u32[]{:S(2)}) collective-permute-start(bf16[32,1536]{1,0:T(8,128)(2,1)S(1)} %get-tuple-element.75.refs_0_), channel_id=1, source_target_pairs={{0,8},{1,9},{2,10},{3,11},{8,0},{9,1},{10,2},{11,3},{16,24},{17,25... | collective-permute-start | bytes 294920 | tf_op jit(solution)/shard_map/ppermute | solution.py:334
  33.2 1.0 %load_table.3.refs_1_ = bf16[1,2,768,1536]{3,2,1,0:T(8,128)(2,1)S(1)} custom-call(bf16[1,2,768,1536]{3,2,1,0:T(8,128)(2,1)S(1)} %bitcast.8), custom_call_target="tpu_custom_call" | custom-call | flops 1 | bytes 1 | tf_op jit(solution)/shard_map/load_table/pallas_call | solution.py:287
  34.2 1.6 %collective-permute-start.19 = (bf16[32,1536]{1,0:T(8,128)(2,1)S(1)}, bf16[32,1536]{1,0:T(8,128)(2,1)S(1)}, u32[]{:S(2)}, u32[]{:S(2)}) collective-permute-start(bf16[32,1536]{1,0:T(8,128)(2,1)S(1)} %get-tuple-element.82), channel_id=1, source_target_pairs={{0,4},{4,0},{1,5},{5,1},{2,6},{6,2},{3,7},{7,3},{8,12},{12,8},{9,1... | collective-permute-start | bytes 294920 | tf_op jit(solution)/shard_map/ppermute | solution.py:309
  36.7 0.9 %collective-permute-start.14 = (bf16[32,1536]{1,0:T(8,128)(2,1)S(1)}, bf16[32,1536]{1,0:T(8,128)(2,1)S(1)}, u32[]{:S(2)}, u32[]{:S(2)}) collective-permute-start(bf16[32,1536]{1,0:T(8,128)(2,1)S(1)} %fusion.refs_2_.addend_ref), channel_id=1, source_target_pairs={{0,2},{1,3},{2,0},{3,1},{4,6},{5,7},{6,4},{7,5},{8,10},{9,11},{10,... | collective-permute-start | bytes 294920 | tf_op jit(solution)/shard_map/ppermute | solution.py:318
  37.6 2.9 %collective-permute-done.16 = bf16[32,1536]{1,0:T(8,128)(2,1)S(1)} collective-permute-done((bf16[32,1536]{1,0:T(8,128)(2,1)S(1)}, bf16[32,1536]{1,0:T(8,128)(2,1)S(1)}, u32[]{:S(2)}, u32[]{:S(2)}) %collective-permute-start.16) | collective-permute-done | bytes 98336 | tf_op jit(solution)/shard_map/ppermute | solution.py:334
  41.7 1.0 %collective-permute-start.20 = (bf16[32,1536]{1,0:T(8,128)(2,1)S(1)}, bf16[32,1536]{1,0:T(8,128)(2,1)S(1)}, u32[]{:S(2)}, u32[]{:S(2)}) collective-permute-start(bf16[32,1536]{1,0:T(8,128)(2,1)S(1)} %fusion.1.refs_2_.addend_ref), channel_id=1, source_target_pairs={{0,2},{1,3},{2,0},{3,1},{4,6},{5,7},{6,4},{7,5},{8,10},{9,11},{10,... | collective-permute-start | bytes 294920 | tf_op jit(solution)/shard_map/ppermute | solution.py:318
  42.7 1.8 %collective-permute-done.14.refs_3_ = bf16[32,1536]{1,0:T(8,128)(2,1)S(1)} collective-permute-done((bf16[32,1536]{1,0:T(8,128)(2,1)S(1)}, bf16[32,1536]{1,0:T(8,128)(2,1)S(1)}, u32[]{:S(2)}, u32[]{:S(2)}) %collective-permute-start.14) | collective-permute-done | bytes 98336 | tf_op jit(solution)/shard_map/ppermute | solution.py:318
  44.5 0.9 %project.6 = (bf16[768,128]{1,0:T(8,128)(2,1)S(1)}, bf16[128,1536]{1,0:T(8,128)(2,1)S(1)}) custom-call(bf16[1040,128]{1,0:T(8,128)(2,1)S(1)} %concatenate.10.message_ref, bf16[1,2,768,1536]{3,2,1,0:T(8,128)(2,1)S(1)} %load_table.2.value_ref.refs_0_, bf16[1,2,768,1536]{3,2,1,0:T(8,128)(2,1)S(1)} %load_table.3.refs_1_, ...), custom_call_target="tpu_custom_call" | custom-call | flops 1 | bytes 1 | tf_op jit(solution)/shard_map/project/pallas_call | solution.py:83
  45.4 1.6 %collective-permute-start.24 = (bf16[768,128]{1,0:T(8,128)(2,1)S(1)}, bf16[768,128]{1,0:T(8,128)(2,1)S(1)}, u32[]{:S(2)}, u32[]{:S(2)}) collective-permute-start(bf16[768,128]{1,0:T(8,128)(2,1)S(1)} %get-tuple-element.81.mine_ref), channel_id=1, source_target_pairs={{0,4},{4,0},{1,5},{5,1},{2,6},{6,2},{3,7},{7,3},{8,12},{12,8},{9,1... | collective-permute-start | bytes 589832 | tf_op jit(solution)/shard_map/ppermute | solution.py:309
  46.9 1.8 %collective-permute-done.20.refs_3_ = bf16[32,1536]{1,0:T(8,128)(2,1)S(1)} collective-permute-done((bf16[32,1536]{1,0:T(8,128)(2,1)S(1)}, bf16[32,1536]{1,0:T(8,128)(2,1)S(1)}, u32[]{:S(2)}, u32[]{:S(2)}) %collective-permute-start.20) | collective-permute-done | bytes 98336 | tf_op jit(solution)/shard_map/ppermute | solution.py:318
  49.6 1.6 %collective-permute-start.23 = (bf16[768,128]{1,0:T(8,128)(2,1)S(1)}, bf16[768,128]{1,0:T(8,128)(2,1)S(1)}, u32[]{:S(2)}, u32[]{:S(2)}) collective-permute-start(bf16[768,128]{1,0:T(8,128)(2,1)S(1)} %get-tuple-element.83.mine_ref), channel_id=1, source_target_pairs={{0,4},{4,0},{1,5},{5,1},{2,6},{6,2},{3,7},{7,3},{8,12},{12,8},{9,1... | collective-permute-start | bytes 589832 | tf_op jit(solution)/shard_map/ppermute | solution.py:309
  51.1 1.2 %collective-permute-done.24.arrived_ref = bf16[768,128]{1,0:T(8,128)(2,1)S(1)} collective-permute-done((bf16[768,128]{1,0:T(8,128)(2,1)S(1)}, bf16[768,128]{1,0:T(8,128)(2,1)S(1)}, u32[]{:S(2)}, u32[]{:S(2)}) %collective-permute-start.24) | collective-permute-done | bytes 196640 | tf_op jit(solution)/shard_map/ppermute | solution.py:309
  53.3 3.2 %collective-permute-done.23.arrived_ref = bf16[768,128]{1,0:T(8,128)(2,1)S(1)} collective-permute-done((bf16[768,128]{1,0:T(8,128)(2,1)S(1)}, bf16[768,128]{1,0:T(8,128)(2,1)S(1)}, u32[]{:S(2)}, u32[]{:S(2)}) %collective-permute-start.23) | collective-permute-done | bytes 196640 | tf_op jit(solution)/shard_map/ppermute | solution.py:309
  57.7 1.7 %collective-permute-start.29 = (bf16[32,1536]{1,0:T(8,128)(2,1)S(1)}, bf16[32,1536]{1,0:T(8,128)(2,1)S(1)}, u32[]{:S(2)}, u32[]{:S(2)}) collective-permute-start(bf16[32,1536]{1,0:T(8,128)(2,1)S(1)} %get-tuple-element.88), channel_id=1, source_target_pairs={{0,6},{1,7},{2,4},{3,5},{4,2},{5,3},{6,0},{7,1},{8,14},{9,15},{10,... | collective-permute-start | bytes 294920 | tf_op jit(solution)/shard_map/ppermute | solution.py:326
  59.5 1.4 %collective-permute-start.27 = (bf16[32,1536]{1,0:T(8,128)(2,1)S(1)}, bf16[32,1536]{1,0:T(8,128)(2,1)S(1)}, u32[]{:S(2)}, u32[]{:S(2)}) collective-permute-start(bf16[32,1536]{1,0:T(8,128)(2,1)S(1)} %get-tuple-element.92), channel_id=1, source_target_pairs={{0,2},{1,3},{2,0},{3,1},{4,6},{5,7},{6,4},{7,5},{8,10},{9,11},{10,... | collective-permute-start | bytes 294920 | tf_op jit(solution)/shard_map/ppermute | solution.py:318
  61.4 3.5 %weight_grads.1 = (bf16[1,768,1536]{2,1,0:T(8,128)(2,1)}, bf16[1,768,1536]{2,1,0:T(8,128)(2,1)}) custom-call(bf16[768,128]{1,0:T(8,128)(2,1)S(1)} %get-tuple-element.93.a0, bf16[768,128]{1,0:T(8,128)(2,1)S(1)} %get-tuple-element.94.a1, bf16[768,128]{1,0:T(8,128)(2,1)S(1)} %get-tuple-element.97.b0, bf16[768,128]{1,0:T(8,128)(2,1)S(1)} %get-tuple-element.98.b1, ...), custom_call_target="tpu_custom_call" | custom-call | flops 1 | bytes 1 | tf_op jit(solution)/shard_map/weight_grads/pallas_call | solution.py:201
  64.9 1.0 %collective-permute-done.27 = bf16[32,1536]{1,0:T(8,128)(2,1)S(1)} collective-permute-done((bf16[32,1536]{1,0:T(8,128)(2,1)S(1)}, bf16[32,1536]{1,0:T(8,128)(2,1)S(1)}, u32[]{:S(2)}, u32[]{:S(2)}) %collective-permute-start.27) | collective-permute-done | bytes 98336 | tf_op jit(solution)/shard_map/ppermute | solution.py:318
  (62 shorter events, 12.5 us)
Async XLA Ops:
  1.7 5.8 %collective-permute-start = (bf16[32,1536]{1,0:T(8,128)(2,1)S(1)}, bf16[32,1536]{1,0:T(8,128)(2,1)S(1)}, u32[]{:S(2)}, u32[]{:S(2)}) collective-permute-start(bf16[32,1536]{1,0:T(8,128)(2,1)S(1)} %get-tuple-element.111), channel_id=1, source_target_pairs={{0,4},{4,0},{1,5},{5,1},{2,6},{6,2},{3,7},{7,3},{8,12},{12,8},{9,1... | collective-permute-start | bytes 294920 | tf_op jit(solution)/shard_map/ppermute | solution.py:309
  7.2 7.9 %collective-permute-start.2 = (bf16[1040,128]{1,0:T(8,128)(2,1)S(1)}, bf16[1040,128]{1,0:T(8,128)(2,1)S(1)}, u32[]{:S(2)}, u32[]{:S(2)}) collective-permute-start(bf16[1040,128]{1,0:T(8,128)(2,1)S(1)} %concatenate.10.message_ref), channel_id=1, source_target_pairs={{0,4},{4,0},{1,5},{5,1},{2,6},{6,2},{3,7},{7,3},{8,12},{12,8},{9,1... | collective-permute-start | bytes 798728 | tf_op jit(solution)/shard_map/ppermute | solution.py:309
  7.5 5.5 %collective-permute-start.3 = (bf16[32,1536]{1,0:T(8,128)(2,1)S(1)}, bf16[32,1536]{1,0:T(8,128)(2,1)S(1)}, u32[]{:S(2)}, u32[]{:S(2)}) collective-permute-start(bf16[32,1536]{1,0:T(8,128)(2,1)S(1)} %collective-permute-done.refs_1_.addend_ref), channel_id=1, source_target_pairs={{0,2},{1,3},{2,0},{3,1},{4,6},{5,7},{6,4},{7,5},{8,10},{9,11},{10,... | collective-permute-start | bytes 294920 | tf_op jit(solution)/shard_map/ppermute | solution.py:318
  9.4 4.7 %collective-permute-start.1 = (bf16[32,1536]{1,0:T(8,128)(2,1)S(1)}, bf16[32,1536]{1,0:T(8,128)(2,1)S(1)}, u32[]{:S(2)}, u32[]{:S(2)}) collective-permute-start(bf16[32,1536]{1,0:T(8,128)(2,1)S(1)} %get-tuple-element.64.refs_1_.addend_ref), channel_id=1, source_target_pairs={{0,2},{1,3},{2,0},{3,1},{4,6},{5,7},{6,4},{7,5},{8,10},{9,11},{10,... | collective-permute-start | bytes 294920 | tf_op jit(solution)/shard_map/ppermute | solution.py:318
  13.0 2.1 %collective-permute-start.4 = (bf16[32,1536]{1,0:T(8,128)(2,1)S(1)}, bf16[32,1536]{1,0:T(8,128)(2,1)S(1)}, u32[]{:S(2)}, u32[]{:S(2)}) collective-permute-start(bf16[32,1536]{1,0:T(8,128)(2,1)S(1)} %collective-permute-done.refs_1_.addend_ref), channel_id=1, source_target_pairs={{0,1},{1,0},{2,3},{3,2},{4,5},{5,4},{6,7},{7,6},{8,9},{9,8},{10,11... | collective-permute-start | bytes 294920 | tf_op jit(solution)/shard_map/ppermute | solution.py:312
  13.0 2.1 %collective-permute-start.5 = (bf16[32,1536]{1,0:T(8,128)(2,1)S(1)}, bf16[32,1536]{1,0:T(8,128)(2,1)S(1)}, u32[]{:S(2)}, u32[]{:S(2)}) collective-permute-start(bf16[32,1536]{1,0:T(8,128)(2,1)S(1)} %collective-permute-done.3.refs_2_), channel_id=1, source_target_pairs={{0,1},{1,0},{2,3},{3,2},{4,5},{5,4},{6,7},{7,6},{8,9},{9,8},{10,11... | collective-permute-start | bytes 294920 | tf_op jit(solution)/shard_map/ppermute | solution.py:312
  14.1 2.9 %collective-permute-start.6 = (bf16[32,1536]{1,0:T(8,128)(2,1)S(1)}, bf16[32,1536]{1,0:T(8,128)(2,1)S(1)}, u32[]{:S(2)}, u32[]{:S(2)}) collective-permute-start(bf16[32,1536]{1,0:T(8,128)(2,1)S(1)} %get-tuple-element.64.refs_1_.addend_ref), channel_id=1, source_target_pairs={{0,1},{1,0},{2,3},{3,2},{4,5},{5,4},{6,7},{7,6},{8,9},{9,8},{10,11... | collective-permute-start | bytes 294920 | tf_op jit(solution)/shard_map/ppermute | solution.py:312
  14.1 2.9 %collective-permute-start.7 = (bf16[32,1536]{1,0:T(8,128)(2,1)S(1)}, bf16[32,1536]{1,0:T(8,128)(2,1)S(1)}, u32[]{:S(2)}, u32[]{:S(2)}) collective-permute-start(bf16[32,1536]{1,0:T(8,128)(2,1)S(1)} %collective-permute-done.1.refs_2_), channel_id=1, source_target_pairs={{0,1},{1,0},{2,3},{3,2},{4,5},{5,4},{6,7},{7,6},{8,9},{9,8},{10,11... | collective-permute-start | bytes 294920 | tf_op jit(solution)/shard_map/ppermute | solution.py:312
  16.0 7.9 %collective-permute-start.8 = (bf16[768,128]{1,0:T(8,128)(2,1)S(1)}, bf16[768,128]{1,0:T(8,128)(2,1)S(1)}, u32[]{:S(2)}, u32[]{:S(2)}) collective-permute-start(bf16[768,128]{1,0:T(8,128)(2,1)S(1)} %get-tuple-element.60.mine_ref), channel_id=1, source_target_pairs={{0,4},{4,0},{1,5},{5,1},{2,6},{6,2},{3,7},{7,3},{8,12},{12,8},{9,1... | collective-permute-start | bytes 589832 | tf_op jit(solution)/shard_map/ppermute | solution.py:309
  17.9 8.9 %collective-permute-start.10 = (bf16[768,128]{1,0:T(8,128)(2,1)S(1)}, bf16[768,128]{1,0:T(8,128)(2,1)S(1)}, u32[]{:S(2)}, u32[]{:S(2)}) collective-permute-start(bf16[768,128]{1,0:T(8,128)(2,1)S(1)} %get-tuple-element.66.mine_ref), channel_id=1, source_target_pairs={{0,4},{4,0},{1,5},{5,1},{2,6},{6,2},{3,7},{7,3},{8,12},{12,8},{9,1... | collective-permute-start | bytes 589832 | tf_op jit(solution)/shard_map/ppermute | solution.py:309
  19.0 14.1 %slice-start = ((s8[4718592]{0:T(1024)(128)(4,1)}), s8[4194304]{0:T(1024)(128)(4,1)S(1)}, s32[]{:S(2)}) async-start(s8[4718592]{0:T(1024)(128)(4,1)} %bitcast.7), calls=%async_computation | async-start | bytes 8388608
  21.6 11.6 %slice-start.1 = ((s8[4718592]{0:T(1024)(128)(4,1)}), s8[524288]{0:T(1024)(128)(4,1)S(1)}, s32[]{:S(2)}) async-start(s8[4718592]{0:T(1024)(128)(4,1)} %bitcast.7), calls=%async_computation.1 | async-start | bytes 1048576
  24.9 3.0 %collective-permute-start.9 = (bf16[2,32,1536]{2,1,0:T(8,128)(2,1)S(1)}, bf16[2,32,1536]{2,1,0:T(8,128)(2,1)S(1)}, u32[]{:S(2)}, u32[]{:S(2)}) collective-permute-start(bf16[2,32,1536]{2,1,0:T(8,128)(2,1)S(1)} %get-tuple-element.69), channel_id=1, source_target_pairs={{0,1},{1,0},{2,3},{3,2},{4,5},{5,4},{6,7},{7,6},{8,9},{9,8},{10,11... | collective-permute-start | bytes 589832 | tf_op jit(solution)/shard_map/ppermute | solution.py:312
  27.8 3.0 %collective-permute-start.11 = (bf16[2,32,1536]{2,1,0:T(8,128)(2,1)S(1)}, bf16[2,32,1536]{2,1,0:T(8,128)(2,1)S(1)}, u32[]{:S(2)}, u32[]{:S(2)}) collective-permute-start(bf16[2,32,1536]{2,1,0:T(8,128)(2,1)S(1)} %get-tuple-element.74), channel_id=1, source_target_pairs={{0,1},{1,0},{2,3},{3,2},{4,5},{5,4},{6,7},{7,6},{8,9},{9,8},{10,11... | collective-permute-start | bytes 589832 | tf_op jit(solution)/shard_map/ppermute | solution.py:312
  28.0 8.5 %collective-permute-start.12 = (bf16[32,1536]{1,0:T(8,128)(2,1)S(1)}, bf16[32,1536]{1,0:T(8,128)(2,1)S(1)}, u32[]{:S(2)}, u32[]{:S(2)}) collective-permute-start(bf16[32,1536]{1,0:T(8,128)(2,1)S(1)} %get-tuple-element.70.refs_0_), channel_id=1, source_target_pairs={{0,8},{1,9},{2,10},{3,11},{8,0},{9,1},{10,2},{11,3},{16,24},{17,25... | collective-permute-start | bytes 294920 | tf_op jit(solution)/shard_map/ppermute | solution.py:334
  29.5 7.0 %collective-permute-start.13 = (bf16[32,1536]{1,0:T(8,128)(2,1)S(1)}, bf16[32,1536]{1,0:T(8,128)(2,1)S(1)}, u32[]{:S(2)}, u32[]{:S(2)}) collective-permute-start(bf16[32,1536]{1,0:T(8,128)(2,1)S(1)} %get-tuple-element.71.refs_1_), channel_id=1, source_target_pairs={{0,10},{1,11},{2,8},{3,9},{8,2},{9,3},{10,0},{11,1},{16,26},{17,27... | collective-permute-start | bytes 294920 | tf_op jit(solution)/shard_map/ppermute | solution.py:334
  30.9 9.5 %collective-permute-start.15 = (bf16[32,1536]{1,0:T(8,128)(2,1)S(1)}, bf16[32,1536]{1,0:T(8,128)(2,1)S(1)}, u32[]{:S(2)}, u32[]{:S(2)}) collective-permute-start(bf16[32,1536]{1,0:T(8,128)(2,1)S(1)} %get-tuple-element.75.refs_0_), channel_id=1, source_target_pairs={{0,8},{1,9},{2,10},{3,11},{8,0},{9,1},{10,2},{11,3},{16,24},{17,25... | collective-permute-start | bytes 294920 | tf_op jit(solution)/shard_map/ppermute | solution.py:334
  32.4 8.0 %collective-permute-start.16 = (bf16[32,1536]{1,0:T(8,128)(2,1)S(1)}, bf16[32,1536]{1,0:T(8,128)(2,1)S(1)}, u32[]{:S(2)}, u32[]{:S(2)}) collective-permute-start(bf16[32,1536]{1,0:T(8,128)(2,1)S(1)} %get-tuple-element.76.refs_1_), channel_id=1, source_target_pairs={{0,10},{1,11},{2,8},{3,9},{8,2},{9,3},{10,0},{11,1},{16,26},{17,27... | collective-permute-start | bytes 294920 | tf_op jit(solution)/shard_map/ppermute | solution.py:334
  34.2 6.2 %collective-permute-start.19 = (bf16[32,1536]{1,0:T(8,128)(2,1)S(1)}, bf16[32,1536]{1,0:T(8,128)(2,1)S(1)}, u32[]{:S(2)}, u32[]{:S(2)}) collective-permute-start(bf16[32,1536]{1,0:T(8,128)(2,1)S(1)} %get-tuple-element.82), channel_id=1, source_target_pairs={{0,4},{4,0},{1,5},{5,1},{2,6},{6,2},{3,7},{7,3},{8,12},{12,8},{9,1... | collective-permute-start | bytes 294920 | tf_op jit(solution)/shard_map/ppermute | solution.py:309
  36.6 6.1 %collective-permute-start.18 = (bf16[32,1536]{1,0:T(8,128)(2,1)S(1)}, bf16[32,1536]{1,0:T(8,128)(2,1)S(1)}, u32[]{:S(2)}, u32[]{:S(2)}) collective-permute-start(bf16[32,1536]{1,0:T(8,128)(2,1)S(1)} %fusion.refs_2_.addend_ref), channel_id=1, source_target_pairs={{0,3},{1,2},{2,1},{3,0},{4,7},{5,6},{6,5},{7,4},{8,11},{9,10},{10,... | collective-permute-start | bytes 294920 | tf_op jit(solution)/shard_map/ppermute | solution.py:318
  36.7 7.8 %collective-permute-start.14 = (bf16[32,1536]{1,0:T(8,128)(2,1)S(1)}, bf16[32,1536]{1,0:T(8,128)(2,1)S(1)}, u32[]{:S(2)}, u32[]{:S(2)}) collective-permute-start(bf16[32,1536]{1,0:T(8,128)(2,1)S(1)} %fusion.refs_2_.addend_ref), channel_id=1, source_target_pairs={{0,2},{1,3},{2,0},{3,1},{4,6},{5,7},{6,4},{7,5},{8,10},{9,11},{10,... | collective-permute-start | bytes 294920 | tf_op jit(solution)/shard_map/ppermute | solution.py:318
  40.4 1.3 %collective-permute-start.17 = (bf16[32,1536]{1,0:T(8,128)(2,1)S(1)}, bf16[32,1536]{1,0:T(8,128)(2,1)S(1)}, u32[]{:S(2)}, u32[]{:S(2)}) collective-permute-start(bf16[32,1536]{1,0:T(8,128)(2,1)S(1)} %fusion.refs_2_.addend_ref), channel_id=1, source_target_pairs={{0,1},{1,0},{2,3},{3,2},{4,5},{5,4},{6,7},{7,6},{8,9},{9,8},{10,11... | collective-permute-start | bytes 294920 | tf_op jit(solution)/shard_map/ppermute | solution.py:312
  40.5 6.5 %collective-permute-start.22 = (bf16[32,1536]{1,0:T(8,128)(2,1)S(1)}, bf16[32,1536]{1,0:T(8,128)(2,1)S(1)}, u32[]{:S(2)}, u32[]{:S(2)}) collective-permute-start(bf16[32,1536]{1,0:T(8,128)(2,1)S(1)} %fusion.1.refs_2_.addend_ref), channel_id=1, source_target_pairs={{0,3},{1,2},{2,1},{3,0},{4,7},{5,6},{6,5},{7,4},{8,11},{9,10},{10,... | collective-permute-start | bytes 294920 | tf_op jit(solution)/shard_map/ppermute | solution.py:318
  41.3 5.6 %collective-permute-start.21 = (bf16[32,1536]{1,0:T(8,128)(2,1)S(1)}, bf16[32,1536]{1,0:T(8,128)(2,1)S(1)}, u32[]{:S(2)}, u32[]{:S(2)}) collective-permute-start(bf16[32,1536]{1,0:T(8,128)(2,1)S(1)} %fusion.1.refs_2_.addend_ref), channel_id=1, source_target_pairs={{0,1},{1,0},{2,3},{3,2},{4,5},{5,4},{6,7},{7,6},{8,9},{9,8},{10,11... | collective-permute-start | bytes 294920 | tf_op jit(solution)/shard_map/ppermute | solution.py:312
  41.7 7.0 %collective-permute-start.20 = (bf16[32,1536]{1,0:T(8,128)(2,1)S(1)}, bf16[32,1536]{1,0:T(8,128)(2,1)S(1)}, u32[]{:S(2)}, u32[]{:S(2)}) collective-permute-start(bf16[32,1536]{1,0:T(8,128)(2,1)S(1)} %fusion.1.refs_2_.addend_ref), channel_id=1, source_target_pairs={{0,2},{1,3},{2,0},{3,1},{4,6},{5,7},{6,4},{7,5},{8,10},{9,11},{10,... | collective-permute-start | bytes 294920 | tf_op jit(solution)/shard_map/ppermute | solution.py:318
  45.4 7.0 %collective-permute-start.24 = (bf16[768,128]{1,0:T(8,128)(2,1)S(1)}, bf16[768,128]{1,0:T(8,128)(2,1)S(1)}, u32[]{:S(2)}, u32[]{:S(2)}) collective-permute-start(bf16[768,128]{1,0:T(8,128)(2,1)S(1)} %get-tuple-element.81.mine_ref), channel_id=1, source_target_pairs={{0,4},{4,0},{1,5},{5,1},{2,6},{6,2},{3,7},{7,3},{8,12},{12,8},{9,1... | collective-permute-start | bytes 589832 | tf_op jit(solution)/shard_map/ppermute | solution.py:309
  49.6 7.0 %collective-permute-start.23 = (bf16[768,128]{1,0:T(8,128)(2,1)S(1)}, bf16[768,128]{1,0:T(8,128)(2,1)S(1)}, u32[]{:S(2)}, u32[]{:S(2)}) collective-permute-start(bf16[768,128]{1,0:T(8,128)(2,1)S(1)} %get-tuple-element.83.mine_ref), channel_id=1, source_target_pairs={{0,4},{4,0},{1,5},{5,1},{2,6},{6,2},{3,7},{7,3},{8,12},{12,8},{9,1... | collective-permute-start | bytes 589832 | tf_op jit(solution)/shard_map/ppermute | solution.py:309
  53.3 4.3 %collective-permute-start.25 = (bf16[2,32,1536]{2,1,0:T(8,128)(2,1)S(1)}, bf16[2,32,1536]{2,1,0:T(8,128)(2,1)S(1)}, u32[]{:S(2)}, u32[]{:S(2)}) collective-permute-start(bf16[2,32,1536]{2,1,0:T(8,128)(2,1)S(1)} %get-tuple-element.86), channel_id=1, source_target_pairs={{0,1},{1,0},{2,3},{3,2},{4,5},{5,4},{6,7},{7,6},{8,9},{9,8},{10,11... | collective-permute-start | bytes 589832 | tf_op jit(solution)/shard_map/ppermute | solution.py:312
  57.5 1.9 %collective-permute-start.26 = (bf16[2,32,1536]{2,1,0:T(8,128)(2,1)S(1)}, bf16[2,32,1536]{2,1,0:T(8,128)(2,1)S(1)}, u32[]{:S(2)}, u32[]{:S(2)}) collective-permute-start(bf16[2,32,1536]{2,1,0:T(8,128)(2,1)S(1)} %get-tuple-element.90), channel_id=1, source_target_pairs={{0,1},{1,0},{2,3},{3,2},{4,5},{5,4},{6,7},{7,6},{8,9},{9,8},{10,11... | collective-permute-start | bytes 589832 | tf_op jit(solution)/shard_map/ppermute | solution.py:312
  57.7 7.2 %collective-permute-start.29 = (bf16[32,1536]{1,0:T(8,128)(2,1)S(1)}, bf16[32,1536]{1,0:T(8,128)(2,1)S(1)}, u32[]{:S(2)}, u32[]{:S(2)}) collective-permute-start(bf16[32,1536]{1,0:T(8,128)(2,1)S(1)} %get-tuple-element.88), channel_id=1, source_target_pairs={{0,6},{1,7},{2,4},{3,5},{4,2},{5,3},{6,0},{7,1},{8,14},{9,15},{10,... | collective-permute-start | bytes 294920 | tf_op jit(solution)/shard_map/ppermute | solution.py:326
  59.5 6.5 %collective-permute-start.27 = (bf16[32,1536]{1,0:T(8,128)(2,1)S(1)}, bf16[32,1536]{1,0:T(8,128)(2,1)S(1)}, u32[]{:S(2)}, u32[]{:S(2)}) collective-permute-start(bf16[32,1536]{1,0:T(8,128)(2,1)S(1)} %get-tuple-element.92), channel_id=1, source_target_pairs={{0,2},{1,3},{2,0},{3,1},{4,6},{5,7},{6,4},{7,5},{8,10},{9,11},{10,... | collective-permute-start | bytes 294920 | tf_op jit(solution)/shard_map/ppermute | solution.py:318
  60.8 5.1 %collective-permute-start.28 = (bf16[32,1536]{1,0:T(8,128)(2,1)S(1)}, bf16[32,1536]{1,0:T(8,128)(2,1)S(1)}, u32[]{:S(2)}, u32[]{:S(2)}) collective-permute-start(bf16[32,1536]{1,0:T(8,128)(2,1)S(1)} %get-tuple-element.87), channel_id=1, source_target_pairs={{0,4},{1,5},{2,6},{3,7},{4,0},{5,1},{6,2},{7,3},{8,12},{9,13},{10,... | collective-permute-start | bytes 294920 | tf_op jit(solution)/shard_map/ppermute | solution.py:326
  (1 other events, 1.8 us)
